TPU v7x, 32 devices: a whole 2x2x4 slice. The times are simulated.
32 devices in a mesh: groups: 2 (over x), seq: 16 (over z, y, core).
Axes of the slice: x: 2, y: 2, z: 4, core: 2. Of those that a mesh axis runs over, the one named last changes fastest.
Arguments:
- queries: bfloat16 [4096, 2048], P(('groups', 'seq')), parts along dimension 0, may hold values from -2.5 to 2.5
- keys: bfloat16 [4096, 2048], P(('groups', 'seq')), parts along dimension 0, may hold values from -2.5 to 2.5
- values: bfloat16 [4096, 2048], P(('groups', 'seq')), parts along dimension 0, may hold values from -6 to 6
- grad_out: bfloat16 [4096, 2048], P(('groups', 'seq')), parts along dimension 0, may hold values from -6 to 6
- doc_lengths: int32 [16], P('groups'), parts along dimension 0, may hold values from 1 to 896, 2048 in all
Outputs:
- attn_out: bfloat16 [4096, 2048], P(('groups', 'seq')), parts along dimension 0
- grad_queries: bfloat16 [4096, 2048], P(('groups', 'seq')), parts along dimension 0
- grad_keys: bfloat16 [4096, 2048], P(('groups', 'seq')), parts along dimension 0
- grad_values: bfloat16 [4096, 2048], P(('groups', 'seq')), parts along dimension 0
There are 2 independent parts, one for each index of `groups`. A program takes and returns all parts, laid end to end along the dimension named above; each array names one. Nothing has to cross between parts.
Inputs may be any that keep to these rules, and one draw needn't show every extreme that they name: `doc_lengths`: lengths of the documents in order; they sum to 2048 and the longest has exactly 896 tokens.
All inputs are finite; a program needn't handle non-finite values.
Results may differ from a plain program's by a relative error of at most 0.0058.
Values may be sent and summed in bfloat16 or wider, within the bound.
No kernel may reach another device: no remote copies, remote signals or barrier semaphores. Data moves between devices by JAX's collectives and lax.ppermute only.
A program may use at most 256 MiB of HBM per device.

v0:
```python
import jax
import jax.numpy as jnp
from jax import lax
from jax.sharding import PartitionSpec as P

HEADS = 16
HD = 128


def from_behind(shard, axis, by):
    length = lax.axis_size(axis)
    pairs = [(i, i + by) for i in range(length) if 0 <= i + by < length]
    return lax.ppermute(shard, axis, pairs)


def starts_within(starts, lower, upper):
    return jnp.any((starts >= lower) & (starts < upper)).astype(jnp.float32)


def prefix_states(starts, tail_state, block_index, rows_here):
    window_state = tail_state
    for level_bit in range(3):
        shifted = from_behind(window_state, "seq", 2**level_bit)
        window_flag = starts_within(
            starts, (block_index - 2**level_bit + 1) * rows_here, (block_index + 1) * rows_here
        )
        window_state = jnp.where(window_flag > 0.5, window_state, shifted + window_state)
    return from_behind(window_state.astype(jnp.bfloat16), "seq", 1)


def suffix_states(starts, head_state, block_index, rows_here):
    window_state = head_state
    for level_bit in range(3):
        shifted = from_behind(window_state, "seq", -(2**level_bit))
        window_flag = starts_within(
            starts, block_index * rows_here + 1, (block_index + 2**level_bit) * rows_here + 1
        )
        window_state = jnp.where(window_flag > 0.5, window_state, shifted + window_state)
    return from_behind(window_state.astype(jnp.bfloat16), "seq", -1)


def forward_terms(query_heads, key_heads, value_heads, same_doc, use_prefix, inv_root, carried):
    scores = jnp.einsum("thd,shd->hts", query_heads, key_heads, preferred_element_type=jnp.float32)
    weights = jnp.where(same_doc[None], scores, 0.0).astype(jnp.bfloat16)
    attended = jnp.einsum("hts,she->the", weights, value_heads, preferred_element_type=jnp.float32)
    from_before = jnp.einsum(
        "thd,hde->the", query_heads, carried, preferred_element_type=jnp.float32
    )
    attended = attended + jnp.where(use_prefix, from_before, 0.0)
    attn_rows = (attended * inv_root[:, None, None]).astype(jnp.bfloat16)
    return (attn_rows, weights, carried)


def backward_terms(
    query_heads,
    key_heads,
    value_heads,
    scaled_grad,
    weights,
    same_doc,
    use_prefix,
    use_suffix,
    carried_low,
    returned,
):
    dscores = jnp.einsum(
        "the,she->hts", scaled_grad, value_heads, preferred_element_type=jnp.float32
    )
    dweights = jnp.where(same_doc[None], dscores, 0.0).astype(jnp.bfloat16)
    grad_query = jnp.einsum("hts,shd->thd", dweights, key_heads, preferred_element_type=jnp.float32)
    grad_query = grad_query + jnp.where(
        use_prefix,
        jnp.einsum("the,hde->thd", scaled_grad, carried_low, preferred_element_type=jnp.float32),
        0.0,
    )
    grad_key = jnp.einsum("hts,thd->shd", dweights, query_heads, preferred_element_type=jnp.float32)
    grad_key = grad_key + jnp.where(
        use_suffix,
        jnp.einsum("she,hde->shd", value_heads, returned, preferred_element_type=jnp.float32),
        0.0,
    )
    grad_value = jnp.einsum(
        "hts,the->she", weights, scaled_grad, preferred_element_type=jnp.float32
    )
    grad_value = grad_value + jnp.where(
        use_suffix,
        jnp.einsum("shd,hde->she", key_heads, returned, preferred_element_type=jnp.float32),
        0.0,
    )
    return (
        grad_query.astype(jnp.bfloat16),
        grad_key.astype(jnp.bfloat16),
        grad_value.astype(jnp.bfloat16),
    )


def per_device(queries, keys, values, grad_out, doc_lengths):
    rows_here = queries.shape[0]
    block_index = lax.axis_index("seq")
    seq_total = rows_here * lax.axis_size("seq")
    first_row = block_index * rows_here
    starts = jnp.cumsum(doc_lengths) - doc_lengths
    local_rows = jnp.arange(rows_here, dtype=jnp.int32)
    positions = first_row + local_rows
    before = starts[None, :] <= positions[:, None]
    doc_begin = jnp.max(jnp.where(before, starts[None, :], 0), axis=1)
    finish = jnp.min(jnp.where(before, seq_total, starts[None, :]), axis=1)
    inv_root = 1.0 / jnp.sqrt((positions - doc_begin + 1).astype(jnp.float32))
    same_doc = (doc_begin[:, None] == doc_begin[None, :]) & (
        local_rows[None, :] <= local_rows[:, None]
    )
    use_prefix = (doc_begin < first_row)[:, None, None]
    use_suffix = (finish > first_row + rows_here)[:, None, None]
    query_heads = queries.reshape(rows_here, HEADS, HD)
    key_heads = keys.reshape(rows_here, HEADS, HD)
    value_heads = values.reshape(rows_here, HEADS, HD)
    scaled_grad = (
        grad_out.reshape(rows_here, HEADS, HD).astype(jnp.float32) * inv_root[:, None, None]
    ).astype(jnp.bfloat16)
    tail_keys = jnp.where(
        (finish >= first_row + rows_here)[:, None, None], key_heads, jnp.zeros((), jnp.bfloat16)
    )
    tail_state = jnp.einsum(
        "shd,she->hde", tail_keys, value_heads, preferred_element_type=jnp.float32
    )
    head_queries = jnp.where(
        (doc_begin <= first_row)[:, None, None], query_heads, jnp.zeros((), jnp.bfloat16)
    )
    head_state = jnp.einsum(
        "thd,the->hde", head_queries, scaled_grad, preferred_element_type=jnp.float32
    )
    carried = prefix_states(starts, tail_state, block_index, rows_here)
    attn_rows, weights, carried_low = forward_terms(
        query_heads, key_heads, value_heads, same_doc, use_prefix, inv_root, carried
    )
    returned = suffix_states(starts, head_state, block_index, rows_here)
    grad_query, grad_key, grad_value = backward_terms(
        query_heads,
        key_heads,
        value_heads,
        scaled_grad,
        weights,
        same_doc,
        use_prefix,
        use_suffix,
        carried_low,
        returned,
    )
    width = HEADS * HD
    return (
        attn_rows.reshape(rows_here, width),
        grad_query.reshape(rows_here, width),
        grad_key.reshape(rows_here, width),
        grad_value.reshape(rows_here, width),
    )


def solution(mesh):
    placed = (
        P(("groups", "seq"), None),
        P(("groups", "seq"), None),
        P(("groups", "seq"), None),
        P(("groups", "seq"), None),
        P("groups"),
    )
    return jax.shard_map(
        per_device,
        mesh=mesh,
        in_specs=placed,
        out_specs=(
            P(("groups", "seq"), None),
            P(("groups", "seq"), None),
            P(("groups", "seq"), None),
            P(("groups", "seq"), None),
        ),
        check_vma=False,
    )
```

profile of v0, /device:TPU:20, one launch (start us, length us, event | category | flops | bytes accessed | tf_op | source)
XLA Modules:
  0.0 129.8 jit_solution(9055956385832950792)
XLA Ops:
  0.7 1.2 copy.61
  2.4 0.6 copy-done.8
  3.2 0.7 and_reduce_fusion.2
  4.3 1.9 %collective-permute-start = (f32[16,128,128]{2,1,0:T(8,128)S(1)}, f32[16,128,128]{2,1,0:T(8,128)}, u32[]{:S(2)}, u32[]{:S(2)}) collective-permute-start(f32[16,128,128]{2,1,0:T(8,128)S(1)} %fusion.19), channel_id=1, source_target_pairs={{0,1},{1,2},{2,3},{3,4},{4,5},{5,6},{6,7},{7,8},{8,9},{9,10},{10,1... | collective-permute-start | bytes 3145736 | tf_op jit(solution)/shard_map/ppermute | solution.py:13
  6.3 1.4 %copy.58 = bf16[128,2048]{0,1:T(8,128)(2,1)S(1)} copy(bf16[128,2048]{1,0:T(8,128)(2,1)} %param.5) | data formatting | bytes 1048576 | tf_op jit(solution)/shard_map/reshape | solution.py:114
  7.7 1.2 copy.38
  8.9 1.3 %multiply_convert_fusion = bf16[128,16,128]{0,2,1:T(8,128)(2,1)S(1)} fusion(f32[128,16,128]{0,2,1:T(8,128)} %bitcast.94, f32[128]{0:T(128)S(1)} %convert_rsqrt_fusion), kind=kLoop, calls=%fused_computation.31 | loop fusion | flops 524288 | bytes 1573376 | tf_op jit(solution)/shard_map/convert_element_type | solution.py:119
  10.3 1.5 %fusion.23 = f32[16,128,128]{2,1,0:T(8,128)} fusion(bf16[128,16,128]{0,2,1:T(8,128)(2,1)S(1)} %multiply_convert_fusion, bf16[128,16,128]{0,2,1:T(8,128)(2,1)S(1)} %bitcast.90, pred[128]{0:T(512)(128)(4,1)S(1)} %get-tuple-element.23), kind=kOutput, calls=%fused_computation.39 | convolution fusion | flops 67371008 | bytes 2097280 | tf_op jit(solution)/shard_map/thd,the->hde/dot_general | solution.py:129
  11.8 3.6 %collective-permute-start.4 = (f32[16,128,128]{2,1,0:T(8,128)}, f32[16,128,128]{2,1,0:T(8,128)}, u32[]{:S(2)}, u32[]{:S(2)}) collective-permute-start(f32[16,128,128]{2,1,0:T(8,128)} %fusion.23), channel_id=1, source_target_pairs={{1,0},{2,1},{3,2},{4,3},{5,4},{6,5},{7,6},{8,7},{9,8},{10,9},{11,1... | collective-permute-start | bytes 3145736 | tf_op jit(solution)/shard_map/ppermute | solution.py:13
  19.2 12.6 %collective-permute-done = f32[16,128,128]{2,1,0:T(8,128)} collective-permute-done((f32[16,128,128]{2,1,0:T(8,128)S(1)}, f32[16,128,128]{2,1,0:T(8,128)}, u32[]{:S(2)}, u32[]{:S(2)}) %collective-permute-start) | collective-permute-done | bytes 1048608 | tf_op jit(solution)/shard_map/ppermute | solution.py:13
  31.8 1.3 %add_select_fusion.5 = f32[16,128,128]{2,1,0:T(8,128)S(1)} fusion(f32[16,128,128]{2,1,0:T(8,128)S(1)} %fusion.19, f32[16,128,128]{2,1,0:T(8,128)} %collective-permute-done, pred[]{:T(512)S(6)} %gt.28), kind=kLoop, calls=%fused_computation.5 | loop fusion | flops 524288 | bytes 3145729 | tf_op jit(solution)/shard_map/jit(_where)/select_n | solution.py:27
  33.1 1.9 %collective-permute-start.1 = (f32[16,128,128]{2,1,0:T(8,128)S(1)}, f32[16,128,128]{2,1,0:T(8,128)S(1)}, u32[]{:S(2)}, u32[]{:S(2)}) collective-permute-start(f32[16,128,128]{2,1,0:T(8,128)S(1)} %add_select_fusion.5), channel_id=1, source_target_pairs={{0,2},{1,3},{2,4},{3,5},{4,6},{5,7},{6,8},{7,9},{8,10},{9,11},{10,... | collective-permute-start | bytes 3145736 | tf_op jit(solution)/shard_map/ppermute | solution.py:13
  35.1 1.7 %add_select_fusion.2 = f32[16,128,128]{2,1,0:T(8,128)S(1)} fusion(f32[16,128,128]{2,1,0:T(8,128)} %fusion.23, f32[16,128,128]{2,1,0:T(8,128)} %collective-permute-done.4, pred[]{:T(512)S(6)} %gt.32), kind=kLoop, calls=%fused_computation.2 | loop fusion | flops 524288 | bytes 3145729 | tf_op jit(solution)/shard_map/jit(_where)/select_n | solution.py:38
  36.8 3.9 %collective-permute-start.5 = (f32[16,128,128]{2,1,0:T(8,128)S(1)}, f32[16,128,128]{2,1,0:T(8,128)S(1)}, u32[]{:S(2)}, u32[]{:S(2)}) collective-permute-start(f32[16,128,128]{2,1,0:T(8,128)S(1)} %add_select_fusion.2), channel_id=1, source_target_pairs={{2,0},{3,1},{4,2},{5,3},{6,4},{7,5},{8,6},{9,7},{10,8},{11,9},{12,... | collective-permute-start | bytes 3145736 | tf_op jit(solution)/shard_map/ppermute | solution.py:13
  40.7 0.5 fusion.13
  41.7 38.6 %collective-permute-done.1 = f32[16,128,128]{2,1,0:T(8,128)S(1)} collective-permute-done((f32[16,128,128]{2,1,0:T(8,128)S(1)}, f32[16,128,128]{2,1,0:T(8,128)S(1)}, u32[]{:S(2)}, u32[]{:S(2)}) %collective-permute-start.1) | collective-permute-done | bytes 1048608 | tf_op jit(solution)/shard_map/ppermute | solution.py:13
  80.5 1.9 %collective-permute-start.2 = (f32[16,128,128]{2,1,0:T(8,128)S(1)}, f32[16,128,128]{2,1,0:T(8,128)S(1)}, u32[]{:S(2)}, u32[]{:S(2)}) collective-permute-start(f32[16,128,128]{2,1,0:T(8,128)S(1)} %add_select_fusion.4), channel_id=1, source_target_pairs={{0,4},{1,5},{2,6},{3,7},{4,8},{5,9},{6,10},{7,11},{8,12},{9,13},{1... | collective-permute-start | bytes 3145736 | tf_op jit(solution)/shard_map/ppermute | solution.py:13
  82.4 1.3 convolution_bitcast_fusion
  83.9 4.1 %collective-permute-start.6 = (f32[16,128,128]{2,1,0:T(8,128)S(1)}, f32[16,128,128]{2,1,0:T(8,128)S(1)}, u32[]{:S(2)}, u32[]{:S(2)}) collective-permute-start(f32[16,128,128]{2,1,0:T(8,128)S(1)} %add_select_fusion.1), channel_id=1, source_target_pairs={{4,0},{5,1},{6,2},{7,3},{8,4},{9,5},{10,6},{11,7},{12,8},{13,9},{1... | collective-permute-start | bytes 3145736 | tf_op jit(solution)/shard_map/ppermute | solution.py:13
  87.9 0.5 fusion.12
  89.0 15.4 %collective-permute-done.2 = f32[16,128,128]{2,1,0:T(8,128)S(1)} collective-permute-done((f32[16,128,128]{2,1,0:T(8,128)S(1)}, f32[16,128,128]{2,1,0:T(8,128)S(1)}, u32[]{:S(2)}, u32[]{:S(2)}) %collective-permute-start.2) | collective-permute-done | bytes 1048608 | tf_op jit(solution)/shard_map/ppermute | solution.py:13
  104.5 1.9 %collective-permute-start.3 = (bf16[16,128,128]{2,1,0:T(8,128)(2,1)S(1)}, bf16[16,128,128]{2,1,0:T(8,128)(2,1)S(1)}, u32[]{:S(2)}, u32[]{:S(2)}) collective-permute-start(bf16[16,128,128]{2,1,0:T(8,128)(2,1)S(1)} %fusion.14), channel_id=1, source_target_pairs={{0,1},{1,2},{2,3},{3,4},{4,5},{5,6},{6,7},{7,8},{8,9},{9,10},{10,1... | collective-permute-start | bytes 1572872 | tf_op jit(solution)/shard_map/ppermute | solution.py:13
  106.4 1.3 %fusion.41 = f32[16,128,128]{2,1,0:T(8,128)} fusion(bf16[128,16,128]{0,2,1:T(8,128)(2,1)S(1)} %multiply_convert_fusion, bf16[16,128,128]{2,1,0:T(8,128)(2,1)S(1)} %fusion.12), kind=kOutput, calls=%fused_computation.75 | convolution fusion | flops 67108864 | bytes 2097152 | tf_op jit(solution)/shard_map/hts,the->she/dot_general | solution.py:82
  107.8 0.9 fusion.15
  108.8 3.6 %collective-permute-start.7 = (bf16[16,128,128]{2,1,0:T(8,128)(2,1)}, bf16[16,128,128]{2,1,0:T(8,128)(2,1)}, u32[]{:S(2)}, u32[]{:S(2)}) collective-permute-start(bf16[16,128,128]{2,1,0:T(8,128)(2,1)} %fusion.15), channel_id=1, source_target_pairs={{1,0},{2,1},{3,2},{4,3},{5,4},{6,5},{7,6},{8,7},{9,8},{10,9},{11,1... | collective-permute-start | bytes 1572872 | tf_op jit(solution)/shard_map/ppermute | solution.py:13
  112.3 8.3 %collective-permute-done.3 = bf16[16,128,128]{2,1,0:T(8,128)(2,1)S(1)} collective-permute-done((bf16[16,128,128]{2,1,0:T(8,128)(2,1)S(1)}, bf16[16,128,128]{2,1,0:T(8,128)(2,1)S(1)}, u32[]{:S(2)}, u32[]{:S(2)}) %collective-permute-start.3) | collective-permute-done | bytes 524320 | tf_op jit(solution)/shard_map/ppermute | solution.py:13
  121.4 1.0 copy.49
  122.8 1.0 copy.50
  124.2 1.6 %fusion.9 = bf16[128,16,128]{0,2,1:T(8,128)(2,1)S(1)} fusion(f32[128,16,128]{0,2,1:T(8,128)S(1)} %copy-done.1, bf16[16,128,128]{2,1,0:T(8,128)(2,1)} %collective-permute-done.7, pred[128]{0:T(512)(128)(4,1)S(1)} %get-tuple-element.21, bf16[128,2048]{1,0:T(8,128)(2,1)S(1)} %copy-done), kind=kOutput, calls=%fused_computation.24 | convolution fusion | flops 67895296 | bytes 2621568 | tf_op jit(solution)/shard_map/she,hde->shd/dot_general | solution.py:79
  125.8 1.0 copy.51
  127.2 1.6 %fusion.8 = bf16[16,128,128]{2,1,0:T(8,128)(2,1)S(1)} fusion(f32[16,128,128]{2,1,0:T(8,128)S(1)} %copy-done.2, bf16[16,128,128]{2,1,0:T(8,128)(2,1)} %collective-permute-done.7, pred[128]{0:T(512)(128)(4,1)S(1)} %get-tuple-element.21, bf16[128,2048]{1,0:T(8,128)(2,1)S(1)} %copy-done.6), kind=kOutput, calls=%fused_computation.23 | convolution fusion | flops 67895296 | bytes 2621568 | tf_op jit(solution)/shard_map/shd,hde->she/dot_general | solution.py:87
  128.7 1.0 copy.52
  (37 shorter events, 4.6 us)
Async XLA Ops:
  0.6 3.4 %copy-start = (bf16[128,2048]{1,0:T(8,128)(2,1)S(1)}, bf16[128,2048]{1,0:T(8,128)(2,1)}, u32[]{:S(2)}) copy-start(bf16[128,2048]{1,0:T(8,128)(2,1)} %param.7) | copy-start | bytes 1572868
  2.3 0.7 copy-start.8
  4.3 27.5 %collective-permute-start = (f32[16,128,128]{2,1,0:T(8,128)S(1)}, f32[16,128,128]{2,1,0:T(8,128)}, u32[]{:S(2)}, u32[]{:S(2)}) collective-permute-start(f32[16,128,128]{2,1,0:T(8,128)S(1)} %fusion.19), channel_id=1, source_target_pairs={{0,1},{1,2},{2,3},{3,4},{4,5},{5,6},{6,7},{7,8},{8,9},{9,10},{10,1... | collective-permute-start | bytes 3145736 | tf_op jit(solution)/shard_map/ppermute | solution.py:13
  6.3 1.4 %copy-start.7 = (bf16[128,2048]{1,0:T(8,128)(2,1)S(1)}, bf16[128,2048]{1,0:T(8,128)(2,1)}, u32[]{:S(2)}) copy-start(bf16[128,2048]{1,0:T(8,128)(2,1)} %param.8) | copy-start | bytes 1572868
  11.8 23.4 %collective-permute-start.4 = (f32[16,128,128]{2,1,0:T(8,128)}, f32[16,128,128]{2,1,0:T(8,128)}, u32[]{:S(2)}, u32[]{:S(2)}) collective-permute-start(f32[16,128,128]{2,1,0:T(8,128)} %fusion.23), channel_id=1, source_target_pairs={{1,0},{2,1},{3,2},{4,3},{5,4},{6,5},{7,6},{8,7},{9,8},{10,9},{11,1... | collective-permute-start | bytes 3145736 | tf_op jit(solution)/shard_map/ppermute | solution.py:13
  33.1 47.2 %collective-permute-start.1 = (f32[16,128,128]{2,1,0:T(8,128)S(1)}, f32[16,128,128]{2,1,0:T(8,128)S(1)}, u32[]{:S(2)}, u32[]{:S(2)}) collective-permute-start(f32[16,128,128]{2,1,0:T(8,128)S(1)} %add_select_fusion.5), channel_id=1, source_target_pairs={{0,2},{1,3},{2,4},{3,5},{4,6},{5,7},{6,8},{7,9},{8,10},{9,11},{10,... | collective-permute-start | bytes 3145736 | tf_op jit(solution)/shard_map/ppermute | solution.py:13
  36.8 46.9 %collective-permute-start.5 = (f32[16,128,128]{2,1,0:T(8,128)S(1)}, f32[16,128,128]{2,1,0:T(8,128)S(1)}, u32[]{:S(2)}, u32[]{:S(2)}) collective-permute-start(f32[16,128,128]{2,1,0:T(8,128)S(1)} %add_select_fusion.2), channel_id=1, source_target_pairs={{2,0},{3,1},{4,2},{5,3},{6,4},{7,5},{8,6},{9,7},{10,8},{11,9},{12,... | collective-permute-start | bytes 3145736 | tf_op jit(solution)/shard_map/ppermute | solution.py:13
  80.5 23.9 %collective-permute-start.2 = (f32[16,128,128]{2,1,0:T(8,128)S(1)}, f32[16,128,128]{2,1,0:T(8,128)S(1)}, u32[]{:S(2)}, u32[]{:S(2)}) collective-permute-start(f32[16,128,128]{2,1,0:T(8,128)S(1)} %add_select_fusion.4), channel_id=1, source_target_pairs={{0,4},{1,5},{2,6},{3,7},{4,8},{5,9},{6,10},{7,11},{8,12},{9,13},{1... | collective-permute-start | bytes 3145736 | tf_op jit(solution)/shard_map/ppermute | solution.py:13
  83.7 4.2 %copy-start.5 = (bf16[128,2048]{1,0:T(8,128)(2,1)S(1)}, bf16[128,2048]{1,0:T(8,128)(2,1)}, u32[]{:S(2)}) copy-start(bf16[128,2048]{1,0:T(8,128)(2,1)} %param.6) | copy-start | bytes 1572868
  83.9 24.0 %collective-permute-start.6 = (f32[16,128,128]{2,1,0:T(8,128)S(1)}, f32[16,128,128]{2,1,0:T(8,128)S(1)}, u32[]{:S(2)}, u32[]{:S(2)}) collective-permute-start(f32[16,128,128]{2,1,0:T(8,128)S(1)} %add_select_fusion.1), channel_id=1, source_target_pairs={{4,0},{5,1},{6,2},{7,3},{8,4},{9,5},{10,6},{11,7},{12,8},{13,9},{1... | collective-permute-start | bytes 3145736 | tf_op jit(solution)/shard_map/ppermute | solution.py:13
  104.5 16.1 %collective-permute-start.3 = (bf16[16,128,128]{2,1,0:T(8,128)(2,1)S(1)}, bf16[16,128,128]{2,1,0:T(8,128)(2,1)S(1)}, u32[]{:S(2)}, u32[]{:S(2)}) collective-permute-start(bf16[16,128,128]{2,1,0:T(8,128)(2,1)S(1)} %fusion.14), channel_id=1, source_target_pairs={{0,1},{1,2},{2,3},{3,4},{4,5},{5,6},{6,7},{7,8},{8,9},{9,10},{10,1... | collective-permute-start | bytes 1572872 | tf_op jit(solution)/shard_map/ppermute | solution.py:13
  108.8 15.0 %collective-permute-start.7 = (bf16[16,128,128]{2,1,0:T(8,128)(2,1)}, bf16[16,128,128]{2,1,0:T(8,128)(2,1)}, u32[]{:S(2)}, u32[]{:S(2)}) collective-permute-start(bf16[16,128,128]{2,1,0:T(8,128)(2,1)} %fusion.15), channel_id=1, source_target_pairs={{1,0},{2,1},{3,2},{4,3},{5,4},{6,5},{7,6},{8,7},{9,8},{10,9},{11,1... | collective-permute-start | bytes 1572872 | tf_op jit(solution)/shard_map/ppermute | solution.py:13
  120.6 0.8 copy-start.3
  121.4 1.0 copy-start.4
  122.8 1.4 %copy-start.1 = (f32[128,16,128]{0,2,1:T(8,128)S(1)}, f32[128,16,128]{0,2,1:T(8,128)}, u32[]{:S(2)}) copy-start(f32[128,16,128]{0,2,1:T(8,128)} %convolution_bitcast_fusion) | copy-start | bytes 3145732
  124.2 2.6 %copy-start.6 = (bf16[128,2048]{1,0:T(8,128)(2,1)S(1)}, bf16[128,2048]{1,0:T(8,128)(2,1)}, u32[]{:S(2)}) copy-start(bf16[128,2048]{1,0:T(8,128)(2,1)} %param.6) | copy-start | bytes 1572868
  125.8 1.4 %copy-start.2 = (f32[16,128,128]{2,1,0:T(8,128)S(1)}, f32[16,128,128]{2,1,0:T(8,128)}, u32[]{:S(2)}) copy-start(f32[16,128,128]{2,1,0:T(8,128)} %fusion.41) | copy-start | bytes 3145732
where the time goes:
time: 130 us
  waiting for transfers between devices  75 us (58%)
  starting transfers between devices  22.8 us (18%)
  local copies, waits for them, and re-layouts  10.2 us (8%)
  matrix products  10.2 us (8%)
  other arithmetic  6.77 us (5%)
  between operations  4.66 us (4%)
    ppermute x8, waiting for transfers between devices, from_behind(): return lax.ppermute(shard, axis, pairs)  75 us
    ppermute x8, starting transfers between devices, from_behind(): return lax.ppermute(shard, axis, pairs)  22.8 us
    unnamed x23, local copies, waits for them, and re-layouts  7.17 us
  transfers between devices with their start and end apart: 8, of which 5 were waited for; matrix products, arithmetic and copies ran while one was open for 13% of the time, Pallas kernels for 0%

commit v1 on v0

v1 whole, which is shorter than its diff:
```python
import functools

import jax
import jax.numpy as jnp
from jax import lax
from jax.experimental import pallas as pl
from jax.experimental.pallas import tpu as pltpu
from jax.sharding import PartitionSpec as P

HD = 128
TEAM = 8
F32 = jnp.float32
BF16 = jnp.bfloat16


def doc_starts(len_ref):
    starts, at = [], jnp.int32(0)
    for j in range(len_ref.shape[0]):
        starts.append(at)
        at = at + len_ref[j]
    return starts


def any_start(starts, low, high):
    found = jnp.int32(0)
    for s in starts:
        found = found | ((s >= low) & (s < high)).astype(jnp.int32)
    return found > 0


def row_facts(starts, first, rows):
    pos = first + lax.broadcasted_iota(jnp.int32, (rows, HD), 0)
    begin = jnp.zeros((rows, HD), jnp.int32)
    for s in starts:
        begin = jnp.where(pos >= s, s, begin)
    inv_root = 1.0 / jnp.sqrt((pos - begin + 1).astype(F32))
    return pos, begin, inv_root


def min_start(starts, low, otherwise):
    out = jnp.int32(otherwise)
    for s in starts:
        out = jnp.where(s >= low, jnp.minimum(out, s), out)
    return out


def max_start(starts, high):
    out = jnp.int32(0)
    for s in starts:
        out = jnp.where(s < high, jnp.maximum(out, s), out)
    return out


def dot(a, b, contract):
    return lax.dot_general(a, b, ((contract[:1], contract[1:]), ((), ())), preferred_element_type=F32)


def states_kernel(total, len_ref, q_ref, k_ref, v_ref, g_ref, out_ref):
    rows, width = q_ref.shape
    first = lax.axis_index("seq") * rows
    starts = doc_starts(len_ref)
    pos, _, inv_root = row_facts(starts, first, rows)
    tail_rows = pos >= max_start(starts, first + rows)
    head_rows = pos < min_start(starts, first + 1, total)
    zero = jnp.zeros((), BF16)
    per = out_ref.shape[2]
    for h in range(width // HD):
        cols = pl.ds(h * HD, HD)
        k = jnp.where(tail_rows, k_ref[:, cols], zero)
        q = jnp.where(head_rows, q_ref[:, cols], zero)
        g = (g_ref[:, cols].astype(F32) * inv_root).astype(BF16)
        out_ref[h // per, 0, h % per] = dot(k, v_ref[:, cols], (0, 0)).astype(BF16)
        out_ref[h // per, 1, h % per] = dot(q, g, (0, 0)).astype(BF16)


def local_kernel(len_ref, q_ref, k_ref, v_ref, g_ref, w_ref, dw_ref):
    rows, width = q_ref.shape
    first = lax.axis_index("seq") * rows
    starts = doc_starts(len_ref)
    pos, begin, inv_root = row_facts(starts, first, rows)
    col = first + lax.broadcasted_iota(jnp.int32, (rows, HD), 1)
    same = (col <= pos) & (col >= begin)
    for h in range(width // HD):
        cols = pl.ds(h * HD, HD)
        g = (g_ref[:, cols].astype(F32) * inv_root).astype(BF16)
        w_ref[h] = jnp.where(same, dot(q_ref[:, cols], k_ref[:, cols], (1, 1)), 0.0).astype(BF16)
        dw_ref[h] = jnp.where(same, dot(g, v_ref[:, cols], (1, 1)), 0.0).astype(BF16)


def team_flags(len_ref, rows):
    starts = doc_starts(len_ref)
    base = lax.axis_index("seq") // TEAM * TEAM
    flags = []
    for b in range(TEAM):
        first = (base + b) * rows
        flags.append(
            (any_start(starts, first, first + rows), any_start(starts, first + 1, first + rows + 1))
        )
    return flags


def totals_kernel(rows, len_ref, got_ref, out_ref):
    flags = team_flags(len_ref, rows)
    for h in range(got_ref.shape[2]):
        fwd = jnp.zeros((HD, HD), F32)
        bwd = jnp.zeros((HD, HD), F32)
        for b in range(TEAM):
            fwd = got_ref[b, 0, h].astype(F32) + jnp.where(flags[b][0], 0.0, fwd)
        for b in reversed(range(TEAM)):
            bwd = got_ref[b, 1, h].astype(F32) + jnp.where(flags[b][1], 0.0, bwd)
        if out_ref.shape[0] == 1:
            lower = lax.axis_index("seq") < TEAM
            out_ref[0, h] = jnp.where(lower, fwd, bwd).astype(BF16)
        else:
            out_ref[0, h] = fwd.astype(BF16)
            out_ref[1, h] = bwd.astype(BF16)


def scan_kernel(rows, len_ref, got_ref, enter_ref, out_ref):
    flags = team_flags(len_ref, rows)
    for h in range(got_ref.shape[2]):
        if enter_ref.shape[0] == 1:
            enter = enter_ref[0, h].astype(F32)
            lower = lax.axis_index("seq") < TEAM
            fwd = jnp.where(lower, 0.0, enter)
            bwd = jnp.where(lower, enter, 0.0)
        else:
            fwd = enter_ref[0, h].astype(F32)
            bwd = enter_ref[1, h].astype(F32)
        for b in range(TEAM):
            out_ref[b, 0, h] = fwd.astype(BF16)
            fwd = got_ref[b, 0, h].astype(F32) + jnp.where(flags[b][0], 0.0, fwd)
        for b in reversed(range(TEAM)):
            out_ref[b, 1, h] = bwd.astype(BF16)
            bwd = got_ref[b, 1, h].astype(F32) + jnp.where(flags[b][1], 0.0, bwd)


def finish_kernel(
    total, len_ref, q_ref, k_ref, v_ref, g_ref, w_ref, dw_ref, s_ref, o_ref, dq_ref, dk_ref, dv_ref
):
    rows, width = q_ref.shape
    first = lax.axis_index("seq") * rows
    starts = doc_starts(len_ref)
    pos, _, inv_root = row_facts(starts, first, rows)
    use_prefix = pos < min_start(starts, first, total)
    use_suffix = pos >= max_start(starts + [jnp.int32(total)], first + rows + 1)
    zero = jnp.zeros((), BF16)
    per = s_ref.shape[2]
    for h in range(width // HD):
        cols = pl.ds(h * HD, HD)
        q, k, v = q_ref[:, cols], k_ref[:, cols], v_ref[:, cols]
        g = (g_ref[:, cols].astype(F32) * inv_root).astype(BF16)
        w, dw = w_ref[h], dw_ref[h]
        carried, returned = s_ref[h // per, 0, h % per], s_ref[h // per, 1, h % per]
        o = dot(w, v, (1, 0)) + dot(jnp.where(use_prefix, q, zero), carried, (1, 0))
        o_ref[:, cols] = (o * inv_root).astype(BF16)
        dq = dot(dw, k, (1, 0)) + dot(jnp.where(use_prefix, g, zero), carried, (1, 1))
        dq_ref[:, cols] = dq.astype(BF16)
        dk = dot(dw, q, (0, 0)) + dot(jnp.where(use_suffix, v, zero), returned, (1, 1))
        dk_ref[:, cols] = dk.astype(BF16)
        dv = dot(w, g, (0, 0)) + dot(jnp.where(use_suffix, k, zero), returned, (1, 0))
        dv_ref[:, cols] = dv.astype(BF16)


def per_device(queries, keys, values, grad_out, doc_lengths):
    rows, width = queries.shape
    n = lax.axis_size("seq")
    heads = width // HD
    total = rows * n
    teams = n // TEAM
    per = heads // TEAM
    steps = 4
    hs = heads // steps
    smem = pl.BlockSpec(memory_space=pltpu.SMEM)
    vmem = pl.BlockSpec(memory_space=pltpu.VMEM)
    tok = pl.BlockSpec((rows, hs * HD), lambda i: (0, i))
    mat = pl.BlockSpec((hs, rows, rows), lambda i: (i, 0, 0))
    state = pl.BlockSpec((hs // per, 2, per, HD, HD), lambda i: (i, 0, 0, 0, 0))
    state_shape = jax.ShapeDtypeStruct((TEAM, 2, per, HD, HD), BF16)
    mat_shape = jax.ShapeDtypeStruct((heads, rows, rows), BF16)

    states = pl.pallas_call(
        functools.partial(states_kernel, total),
        grid=(steps,),
        in_specs=[smem] + [tok] * 4,
        out_specs=state,
        out_shape=state_shape,
        name="states",
    )(doc_lengths, queries, keys, values, grad_out)
    members = [[t * TEAM + i for i in range(TEAM)] for t in range(teams)]
    got = lax.all_to_all(states, "seq", 0, 0, axis_index_groups=members, tiled=True)
    weights, dweights = pl.pallas_call(
        local_kernel,
        grid=(steps,),
        in_specs=[smem] + [tok] * 4,
        out_specs=[mat] * 2,
        out_shape=[mat_shape] * 2,
        name="local",
    )(doc_lengths, queries, keys, values, grad_out)
    kinds = 1 if teams == 2 else 2
    edge = pl.pallas_call(
        functools.partial(totals_kernel, rows),
        in_specs=[smem, vmem],
        out_specs=vmem,
        out_shape=jax.ShapeDtypeStruct((kinds, per, HD, HD), BF16),
        name="totals",
    )(doc_lengths, got)
    up = [(i, i + TEAM) for i in range(n - TEAM)]
    down = [(j, i) for i, j in up]
    if kinds == 1:
        enter = lax.ppermute(edge, "seq", up + down)
    else:
        enter = jnp.stack([lax.ppermute(edge[0], "seq", up), lax.ppermute(edge[1], "seq", down)])
    entering = pl.pallas_call(
        functools.partial(scan_kernel, rows),
        in_specs=[smem, vmem, vmem],
        out_specs=vmem,
        out_shape=state_shape,
        name="scan",
    )(doc_lengths, got, enter)
    mine = lax.all_to_all(entering, "seq", 0, 0, axis_index_groups=members, tiled=True)
    return pl.pallas_call(
        functools.partial(finish_kernel, total),
        grid=(steps,),
        in_specs=[smem] + [tok] * 4 + [mat] * 2 + [state],
        out_specs=[tok] * 4,
        out_shape=[jax.ShapeDtypeStruct((rows, width), BF16)] * 4,
        name="finish",
    )(doc_lengths, queries, keys, values, grad_out, weights, dweights, mine)


def solution(mesh):
    placed = P(("groups", "seq"), None)
    return jax.shard_map(
        per_device,
        mesh=mesh,
        in_specs=(placed,) * 4 + (P("groups"),),
        out_specs=(placed,) * 4,
        check_vma=False,
    )
```

time: 130 us -> 61.4 us (0.47)
  the two profiles are of different devices: /device:TPU:20 before, /device:TPU:0 now
where the time goes in v1:
time: 61.4 us; the launch traced here: 60.9 us
  blocking collectives  20 us (33%)
  Pallas kernels  18.4 us (30%)
  waiting for transfers between devices  13.9 us (23%)
  starting transfers between devices  6.45 us (11%)
  local copies, waits for them, and re-layouts  1.6 us (3%)
  between operations  0.64 us (1%)
    all_to_all x1, blocking collectives, per_device(): lax.all_to_all(states, 'seq', 0, 0, axis_index_groups=members, tiled=True)  20 us
    all_to_all x1, waiting for transfers between devices, per_device(): lax.all_to_all(entering, 'seq', 0, 0, axis_index_groups=members, tiled=True)  10.2 us
    pallas_call x1, Pallas kernels, per_device(): pl.pallas_call(functools.partial(finish_kernel, total), grid=(steps,), in...  5.19 us
    pallas_call x1, Pallas kernels, per_device(): pl.pallas_call(functools.partial(states_kernel, total), grid=(steps,), in...  4.23 us
    pallas_call x1, Pallas kernels, per_device(): pl.pallas_call(local_kernel, grid=(steps,), in_specs=[smem] + [tok] * 4,...  4.19 us
    ppermute x1, waiting for transfers between devices, per_device(): enter = lax.ppermute(edge, 'seq', up + down)  3.68 us
    all_to_all x1, starting transfers between devices, per_device(): lax.all_to_all(entering, 'seq', 0, 0, axis_index_groups=members, tiled=True)  3.56 us
    ppermute x1, starting transfers between devices, per_device(): enter = lax.ppermute(edge, 'seq', up + down)  2.9 us
  transfers between devices with their start and end apart: 2, of which 2 were waited for; matrix products, arithmetic and copies ran while one was open for 0% of the time, Pallas kernels for 7%

profile of v1, /device:TPU:0, one launch (start us, length us, event | category | flops | bytes accessed | tf_op | source)
XLA Modules:
  0.0 60.9 jit_solution(14482032519379569869)
XLA Ops:
  0.6 4.2 %states.1 = bf16[8,2,2,128,128]{4,3,2,1,0:T(8,128)(2,1)} custom-call(s32[8]{0:T(128)} %len_ref.9, bf16[128,2048]{1,0:T(8,128)(2,1)} %q_ref.5, bf16[128,2048]{1,0:T(8,128)(2,1)} %k_ref.5, bf16[128,2048]{1,0:T(8,128)(2,1)} %v_ref.5, bf16[128,2048]{1,0:T(8,128)(2,1)} %g_ref.5), custom_call_target="tpu_custom_call" | custom-call | tf_op jit(solution)/shard_map/states/pallas_call | solution.py:182
  4.9 20.0 %all_to_all.10.got_ref = bf16[8,2,2,128,128]{4,3,2,1,0:T(8,128)(2,1)} all-to-all(bf16[8,2,2,128,128]{4,3,2,1,0:T(8,128)(2,1)} %states.1), channel_id=1, replica_groups={{0,1,2,3,4,5,6,7},{8,9,10,11,12,13,14,15},{16,17,18,19,20,21,22,23},{24..., dimensions={0} | all-to-all | bytes 2097152 | tf_op jit(solution)/shard_map/all_to_all | solution.py:191
  24.8 2.2 %totals.1 = bf16[1,2,128,128]{3,2,1,0:T(8,128)(2,1)} custom-call(s32[8]{0:T(128)} %len_ref.9, bf16[8,2,2,128,128]{4,3,2,1,0:T(8,128)(2,1)} %all_to_all.10.got_ref), custom_call_target="tpu_custom_call" | custom-call | tf_op jit(solution)/shard_map/totals/pallas_call | solution.py:201
  27.1 2.9 %collective-permute-start = (bf16[1,2,128,128]{3,2,1,0:T(8,128)(2,1)}, bf16[1,2,128,128]{3,2,1,0:T(8,128)(2,1)S(1)}, u32[]{:S(2)}, u32[]{:S(2)}) collective-permute-start(bf16[1,2,128,128]{3,2,1,0:T(8,128)(2,1)} %totals.1), channel_id=1, source_target_pairs={{0,8},{1,9},{2,10},{3,11},{4,12},{5,13},{6,14},{7,15},{8,0},{9,1},... | collective-permute-start | bytes 196616 | tf_op jit(solution)/shard_map/ppermute | solution.py:211
  30.0 3.7 %collective-permute-done.enter_ref = bf16[1,2,128,128]{3,2,1,0:T(8,128)(2,1)S(1)} collective-permute-done((bf16[1,2,128,128]{3,2,1,0:T(8,128)(2,1)}, bf16[1,2,128,128]{3,2,1,0:T(8,128)(2,1)S(1)}, u32[]{:S(2)}, u32[]{:S(2)}) %collective-permute-start) | collective-permute-done | bytes 65568 | tf_op jit(solution)/shard_map/ppermute | solution.py:211
  33.6 0.0 copy-start.1
  33.6 0.6 %copy-done.1 = bf16[1,2,128,128]{3,2,1,0:T(8,128)(2,1)} copy-done((bf16[1,2,128,128]{3,2,1,0:T(8,128)(2,1)}, bf16[1,2,128,128]{3,2,1,0:T(8,128)(2,1)S(1)}, u32[]{:S(2)}) %copy-start.1) | copy-done | bytes 65560
  34.3 2.5 %scan.1 = bf16[8,2,2,128,128]{4,3,2,1,0:T(8,128)(2,1)} custom-call(s32[8]{0:T(128)} %len_ref.9, bf16[8,2,2,128,128]{4,3,2,1,0:T(8,128)(2,1)} %all_to_all.10.got_ref, bf16[1,2,128,128]{3,2,1,0:T(8,128)(2,1)} %copy-done.1), custom_call_target="tpu_custom_call" | custom-call | tf_op jit(solution)/shard_map/scan/pallas_call | solution.py:214
  36.8 3.6 %all-to-all-start.1 = ((bf16[8,2,2,128,128]{4,3,2,1,0:T(8,128)(2,1)}), bf16[8,2,2,128,128]{4,3,2,1,0:T(8,128)(2,1)S(1)}, u32[]{:S(2)}, u32[]{:S(2)}) async-start(bf16[8,2,2,128,128]{4,3,2,1,0:T(8,128)(2,1)} %scan.1), calls=%async_computation.1 | async-start | bytes 2097152 | tf_op jit(solution)/shard_map/all_to_all | solution.py:221
  40.3 4.2 %local.1 = (bf16[16,128,128]{2,1,0:T(8,128)(2,1)}, bf16[16,128,128]{2,1,0:T(8,128)(2,1)}) custom-call(s32[8]{0:T(128)} %len_ref.9, bf16[128,2048]{1,0:T(8,128)(2,1)} %q_ref.5, bf16[128,2048]{1,0:T(8,128)(2,1)} %k_ref.5, bf16[128,2048]{1,0:T(8,128)(2,1)} %v_ref.5, bf16[128,2048]{1,0:T(8,128)(2,1)} %g_ref.5), custom_call_target="tpu_custom_call" | custom-call | tf_op jit(solution)/shard_map/local/pallas_call | solution.py:192
  44.5 10.2 %all-to-all-done.1.s_ref = bf16[8,2,2,128,128]{4,3,2,1,0:T(8,128)(2,1)S(1)} async-done(((bf16[8,2,2,128,128]{4,3,2,1,0:T(8,128)(2,1)}), bf16[8,2,2,128,128]{4,3,2,1,0:T(8,128)(2,1)S(1)}, u32[]{:S(2)}, u32[]{:S(2)}) %all-to-all-start.1) | async-done | bytes 1048608 | tf_op jit(solution)/shard_map/all_to_all | solution.py:221
  54.7 0.0 copy-start
  54.7 1.0 %copy-done = bf16[8,2,2,128,128]{4,3,2,1,0:T(8,128)(2,1)} copy-done((bf16[8,2,2,128,128]{4,3,2,1,0:T(8,128)(2,1)}, bf16[8,2,2,128,128]{4,3,2,1,0:T(8,128)(2,1)S(1)}, u32[]{:S(2)}) %copy-start) | copy-done | bytes 1048600
  55.7 5.2 %finish.1 = (bf16[128,2048]{1,0:T(8,128)(2,1)}, bf16[128,2048]{1,0:T(8,128)(2,1)}, bf16[128,2048]{1,0:T(8,128)(2,1)}, bf16[128,2048]{1,0:T(8,128)(2,1)}) custom-call(s32[8]{0:T(128)} %len_ref.9, bf16[128,2048]{1,0:T(8,128)(2,1)} %q_ref.5, bf16[128,2048]{1,0:T(8,128)(2,1)} %k_ref.5, bf16[128,2048]{1,0:T(8,128)(2,1)} %v_ref.5, bf16[128,2048]{1,0:T(8,128)(2,1)} %g_ref.5, ...), custom_call_target="tpu_custom_call" | custom-call | tf_op jit(solution)/shard_map/finish/pallas_call | solution.py:222
Async XLA Ops:
  27.1 6.6 %collective-permute-start = (bf16[1,2,128,128]{3,2,1,0:T(8,128)(2,1)}, bf16[1,2,128,128]{3,2,1,0:T(8,128)(2,1)S(1)}, u32[]{:S(2)}, u32[]{:S(2)}) collective-permute-start(bf16[1,2,128,128]{3,2,1,0:T(8,128)(2,1)} %totals.1), channel_id=1, source_target_pairs={{0,8},{1,9},{2,10},{3,11},{4,12},{5,13},{6,14},{7,15},{8,0},{9,1},... | collective-permute-start | bytes 196616 | tf_op jit(solution)/shard_map/ppermute | solution.py:211
  33.6 0.6 %copy-start.1 = (bf16[1,2,128,128]{3,2,1,0:T(8,128)(2,1)}, bf16[1,2,128,128]{3,2,1,0:T(8,128)(2,1)S(1)}, u32[]{:S(2)}) copy-start(bf16[1,2,128,128]{3,2,1,0:T(8,128)(2,1)S(1)} %collective-permute-done.enter_ref) | copy-start | bytes 196612
  36.8 17.9 %all-to-all-start.1 = ((bf16[8,2,2,128,128]{4,3,2,1,0:T(8,128)(2,1)}), bf16[8,2,2,128,128]{4,3,2,1,0:T(8,128)(2,1)S(1)}, u32[]{:S(2)}, u32[]{:S(2)}) async-start(bf16[8,2,2,128,128]{4,3,2,1,0:T(8,128)(2,1)} %scan.1), calls=%async_computation.1 | async-start | bytes 2097152 | tf_op jit(solution)/shard_map/all_to_all | solution.py:221
  54.7 1.0 %copy-start = (bf16[8,2,2,128,128]{4,3,2,1,0:T(8,128)(2,1)}, bf16[8,2,2,128,128]{4,3,2,1,0:T(8,128)(2,1)S(1)}, u32[]{:S(2)}) copy-start(bf16[8,2,2,128,128]{4,3,2,1,0:T(8,128)(2,1)S(1)} %all-to-all-done.1.s_ref) | copy-start | bytes 3145732

commit v2 on v1

v2 whole, which is shorter than its diff:
```python
import functools

import jax
import jax.numpy as jnp
from jax import lax
from jax.experimental import pallas as pl
from jax.experimental.pallas import tpu as pltpu
from jax.sharding import PartitionSpec as P

HD = 128
PAIRS = 4
TEAM = 2 * PAIRS
F32 = jnp.float32
BF16 = jnp.bfloat16

KEEP_F, GOT_F, KEEP_B, GOT_B = 0, 1, 2, 3
TOT_F, TOT_B = 4, 8
MIX_F, MIX_B = 12, 28
ENTER_F, ENTER_B = 44, 48
MINE_F, MINE_B, THEIRS_F, THEIRS_B = 52, 54, 56, 58
COEFS = 64


def doc_starts(len_ref):
    starts, at = [], jnp.int32(0)
    for j in range(len_ref.shape[0]):
        starts.append(at)
        at = at + len_ref[j]
    return starts


def starts_before(starts, limit):
    count = jnp.int32(0)
    for s in starts:
        count = count + (s < limit).astype(jnp.int32)
    return count


def min_start(starts, low, otherwise):
    out = jnp.int32(otherwise)
    for s in starts:
        out = jnp.where(s >= low, jnp.minimum(out, s), out)
    return out


def max_start(starts, high):
    out = jnp.int32(0)
    for s in starts:
        out = jnp.where(s < high, jnp.maximum(out, s), out)
    return out


def row_facts(starts, first, rows):
    pos = first + lax.broadcasted_iota(jnp.int32, (rows, HD), 0)
    begin = jnp.zeros((rows, HD), jnp.int32)
    for s in starts:
        begin = jnp.where(pos >= s, s, begin)
    inv_root = 1.0 / jnp.sqrt((pos - begin + 1).astype(F32))
    return pos, begin, inv_root


def dot(a, b, contract):
    return lax.dot_general(a, b, ((contract[:1], contract[1:]), ((), ())), preferred_element_type=F32)


def state_pair(total, starts, first, rows):
    pos, _, inv_root = row_facts(starts, first, rows)
    tail_rows = pos >= max_start(starts, first + rows)
    head_rows = pos < min_start(starts, first + 1, total)
    zero = jnp.zeros((), BF16)

    def of(q, k, v, g):
        scaled = (g.astype(F32) * inv_root).astype(BF16)
        tail = dot(jnp.where(tail_rows, k, zero), v, (0, 0))
        head = dot(jnp.where(head_rows, q, zero), scaled, (0, 0))
        return tail.astype(BF16), head.astype(BF16)

    return of


def send_kernel(total, chunks, len_ref, q_ref, k_ref, v_ref, g_ref, out_ref, buf, sems):
    rows = q_ref.shape[0]
    half = out_ref.shape[1] * HD
    me = lax.axis_index("seq")
    offset = (1 - lax.rem(me, 2)) * half
    size = half // chunks
    copies = []
    for c in range(chunks):
        at = pl.ds(pl.multiple_of(offset + c * size, HD), size)
        for i, ref in enumerate((q_ref, k_ref, v_ref, g_ref)):
            copy = pltpu.make_async_copy(
                ref.at[:, at], buf.at[i, :, pl.ds(c * size, size)], sems.at[i, c]
            )
            copy.start()
            copies.append(copy)
    of = state_pair(total, doc_starts(len_ref), me * rows, rows)
    for c in range(chunks):
        for copy in copies[4 * c : 4 * c + 4]:
            copy.wait()
        for h in range(c * size // HD, (c + 1) * size // HD):
            cols = pl.ds(h * HD, HD)
            tail, head = of(*(buf[i, :, cols] for i in range(4)))
            out_ref[0, h] = tail
            out_ref[1, h] = head


def coefficients(starts, rows, n, coef_ref):
    me = lax.axis_index("seq")
    core = lax.rem(me, 2)
    pair = lax.rem(me, TEAM) // 2
    base = me - lax.rem(me, TEAM)
    teams = n // TEAM
    one, zero = jnp.int32(1), jnp.int32(0)

    def put(row, flag):
        coef_ref[pl.ds(row, 1), :] = jnp.full((1, HD), flag.astype(F32), F32)

    def both(block):
        return starts_before(starts, block * rows), starts_before(starts, block * rows + 1)

    def same(a, b):
        return (a == b).astype(jnp.int32)

    team_low, team_high = both(base), both(base + TEAM)
    pairs = [pair ^ d for d in range(PAIRS)]
    low = [both(base + 2 * p) for p in pairs]
    high = [both(base + 2 * p + 2) for p in pairs]
    middle = both(me - core + 1)
    open_0 = same(low[0][0], middle[0])
    open_1 = same(middle[0], high[0][0])
    close_0 = same(low[0][1], middle[1])
    close_1 = same(middle[1], high[0][1])
    odd = core
    even = one - core
    put(KEEP_F, jnp.where(odd == 1, one, open_1))
    put(GOT_F, jnp.where(odd == 1, open_1, one))
    put(KEEP_B, jnp.where(odd == 1, close_0, one))
    put(GOT_B, jnp.where(odd == 1, one, close_0))
    is_low = (base == 0).astype(jnp.int32)
    is_high = (base == n - TEAM).astype(jnp.int32)
    for d in range(PAIRS):
        tot_f = same(high[d][0], team_high[0])
        tot_b = same(team_low[1], low[d][1])
        put(TOT_F + d, tot_f * is_low if teams == 2 else tot_f)
        put(TOT_B + d, tot_b * is_high if teams == 2 else tot_b)
        put(ENTER_F + d, same(team_low[0], low[d][0]) * (one - is_low))
        put(ENTER_B + d, same(high[d][1], team_high[1]) * (one - is_high))
        for s in range(PAIRS):
            before = (pairs[s] < pairs[d]).astype(jnp.int32)
            after = (pairs[s] > pairs[d]).astype(jnp.int32)
            put(MIX_F + d * PAIRS + s, before * same(high[s][0], low[d][0]))
            put(MIX_B + d * PAIRS + s, after * same(high[d][1], low[s][1]))
    put(MINE_F, jnp.where(odd == 1, open_0, one))
    put(MINE_F + 1, odd)
    put(MINE_B, jnp.where(odd == 1, one, close_1))
    put(MINE_B + 1, even)
    put(THEIRS_F, jnp.where(odd == 1, one, open_0))
    put(THEIRS_F + 1, even)
    put(THEIRS_B, jnp.where(odd == 1, close_1, one))
    put(THEIRS_B + 1, odd)


def keep_kernel(total, len_ref, q_ref, k_ref, v_ref, g_ref, out_ref, coef_ref):
    rows = q_ref.shape[0]
    half = out_ref.shape[1] * HD
    me = lax.axis_index("seq")
    offset = lax.rem(me, 2) * half
    starts = doc_starts(len_ref)
    coefficients(starts, rows, total // rows, coef_ref)
    of = state_pair(total, starts, me * rows, rows)
    for h in range(out_ref.shape[1]):
        cols = pl.ds(pl.multiple_of(offset + h * HD, HD), HD)
        tail, head = of(q_ref[:, cols], k_ref[:, cols], v_ref[:, cols], g_ref[:, cols])
        out_ref[0, h] = tail
        out_ref[1, h] = head


def local_kernel(
    total,
    len_ref,
    q_ref,
    k_ref,
    v_ref,
    g_ref,
    w_ref,
    wt_ref,
    dw_ref,
    dwt_ref,
    kt_ref,
    qt_ref,
    sg_ref,
    mask_ref,
    root_ref,
):
    rows, width = q_ref.shape
    first = lax.axis_index("seq") * rows
    starts = doc_starts(len_ref)
    pos, begin, inv_root = row_facts(starts, first, rows)
    root_ref[...] = inv_root
    one, none = jnp.ones((), F32), jnp.zeros((), F32)
    mask_ref[0] = jnp.where(pos < min_start(starts, first, total), one, none).astype(BF16)
    suffix = pos >= max_start(starts + [jnp.int32(total)], first + rows + 1)
    mask_ref[1] = jnp.where(suffix, one, none).astype(BF16)
    col = first + lax.broadcasted_iota(jnp.int32, (rows, HD), 1)
    same = (col <= pos) & (col >= begin)
    same_t = jnp.where(same, one, none).T > 0.5
    for h in range(width // HD):
        cols = pl.ds(h * HD, HD)
        q, k, v = q_ref[:, cols], k_ref[:, cols], v_ref[:, cols]
        g = (g_ref[:, cols].astype(F32) * inv_root).astype(BF16)
        sg_ref[:, cols] = g
        w_ref[h] = jnp.where(same, dot(q, k, (1, 1)), 0.0).astype(BF16)
        wt_ref[h] = jnp.where(same_t, dot(k, q, (1, 1)), 0.0).astype(BF16)
        dw_ref[h] = jnp.where(same, dot(g, v, (1, 1)), 0.0).astype(BF16)
        dwt_ref[h] = jnp.where(same_t, dot(v, g, (1, 1)), 0.0).astype(BF16)
        kt_ref[h] = k.T
        qt_ref[h] = q.T


def coef(coef_ref, row):
    return coef_ref[pl.ds(row, 1), :]


def pair_kernel(coef_ref, keep_ref, got_ref, *out_refs):
    per = out_refs[0].shape[1]
    pair = lax.rem(lax.axis_index("seq"), TEAM) // 2
    for kind, (a, b) in enumerate(((KEEP_F, GOT_F), (KEEP_B, GOT_B))):
        ca, cb = coef(coef_ref, a), coef(coef_ref, b)
        for d, out_ref in enumerate(out_refs):
            for i in range(per):
                h = (pair ^ d) * per + i
                both = keep_ref[kind, h].astype(F32) * ca + got_ref[kind, h].astype(F32) * cb
                out_ref[kind, i] = both.astype(BF16)


def totals_kernel(coef_ref, s0, s1, s2, s3, out_ref):
    sums = (s0, s1, s2, s3)
    for i in range(out_ref.shape[1]):
        fwd, bwd = (
            sum(sums[d][kind, i].astype(F32) * coef(coef_ref, row + d) for d in range(PAIRS))
            for kind, row in enumerate((TOT_F, TOT_B))
        )
        if out_ref.shape[0] == 1:
            out_ref[0, i] = (fwd + bwd).astype(BF16)
        else:
            out_ref[0, i] = fwd.astype(BF16)
            out_ref[1, i] = bwd.astype(BF16)


def scan_kernel(coef_ref, s0, s1, s2, s3, enter_ref, *out_refs):
    sums = (s0, s1, s2, s3)
    last = enter_ref.shape[0] - 1
    for kind, (mix, enter) in enumerate(((MIX_F, ENTER_F), (MIX_B, ENTER_B))):
        for i in range(out_refs[0].shape[1]):
            came = enter_ref[min(kind, last), i].astype(F32)
            parts = [s[kind, i].astype(F32) for s in sums]
            for d, out_ref in enumerate(out_refs):
                total = came * coef(coef_ref, enter + d)
                for s in range(PAIRS):
                    if s != d:
                        total = total + parts[s] * coef(coef_ref, mix + d * PAIRS + s)
                out_ref[kind, i] = total.astype(BF16)


def post_kernel(coef_ref, c0, c1, c2, c3, keep_ref, got_ref, mine_ref, theirs_ref):
    per = c0.shape[1]
    pair = lax.rem(lax.axis_index("seq"), TEAM) // 2
    for kind in range(2):
        m, t = (MINE_F, THEIRS_F) if kind == 0 else (MINE_B, THEIRS_B)
        m0, m1 = coef(coef_ref, m), coef(coef_ref, m + 1)
        t0, t1 = coef(coef_ref, t), coef(coef_ref, t + 1)
        for d, c_ref in enumerate((c0, c1, c2, c3)):
            for i in range(per):
                h = (pair ^ d) * per + i
                came = c_ref[kind, i].astype(F32)
                theirs_ref[kind, h] = (came * t0 + keep_ref[kind, h].astype(F32) * t1).astype(BF16)
                mine_ref[kind, h] = (came * m0 + got_ref[kind, h].astype(F32) * m1).astype(BF16)


def finish_kernel(other, chunks, *refs):
    (q_ref, k_ref, v_ref, g_ref, w_ref, wt_ref, dw_ref, dwt_ref, kt_ref, qt_ref, mask_ref, root_ref, s_ref) = (
        refs[:13]
    )
    out_refs, (buf, sems) = refs[-6:-2], refs[-2:]
    heads = s_ref.shape[1]
    core = lax.rem(lax.axis_index("seq"), 2)
    half = 1 - core if other else core
    prefix, suffix, root = mask_ref[0], mask_ref[1], root_ref[...]
    size = heads * HD // chunks
    copies = []

    def wide(a, b):
        return jnp.concatenate([a, b], axis=1)

    for c in range(chunks):
        for i in range(c * heads // chunks, (c + 1) * heads // chunks):
            h = half * heads + i
            cols = pl.ds(pl.multiple_of(h * HD, HD), HD)
            at = pl.ds(i * HD, HD)
            q, k, v, g = q_ref[:, cols], k_ref[:, cols], v_ref[:, cols], g_ref[:, cols]
            carried, returned = s_ref[0, i], s_ref[1, i]
            o = dot(wide(w_ref[h], q * prefix), jnp.concatenate([v, carried], axis=0), (1, 0))
            buf[0, :, at] = (o * root).astype(BF16)
            dq = dot(wide(dw_ref[h], g * prefix), wide(kt_ref[h], carried), (1, 1))
            buf[1, :, at] = dq.astype(BF16)
            dk = dot(wide(dwt_ref[h], v * suffix), wide(qt_ref[h], returned), (1, 1))
            buf[2, :, at] = dk.astype(BF16)
            dv = dot(wide(wt_ref[h], k * suffix), jnp.concatenate([g, returned], axis=0), (1, 0))
            buf[3, :, at] = dv.astype(BF16)
        to = pl.ds(pl.multiple_of(half * heads * HD + c * size, HD), size)
        for i, ref in enumerate(out_refs):
            copy = pltpu.make_async_copy(buf.at[i, :, pl.ds(c * size, size)], ref.at[:, to], sems.at[i, c])
            copy.start()
            copies.append(copy)
    for copy in copies:
        copy.wait()


def per_device(queries, keys, values, grad_out, doc_lengths):
    rows, width = queries.shape
    n = lax.axis_size("seq")
    heads = width // HD
    total = rows * n
    teams = n // TEAM
    half = heads // 2
    per = half // PAIRS
    smem = pl.BlockSpec(memory_space=pltpu.SMEM)
    vmem = pl.BlockSpec(memory_space=pltpu.VMEM)
    hbm = pl.BlockSpec(memory_space=pl.ANY)

    def shape(*dims, dtype=BF16):
        return jax.ShapeDtypeStruct(dims, dtype)

    def call(kernel, name, outs, args, specs, out_specs=None, flops=0, scratch=(), aliases=None):
        moved = sum(a.size * a.dtype.itemsize for a in list(args) + list(outs))
        return pl.pallas_call(
            kernel,
            in_specs=specs,
            out_specs=out_specs or [vmem] * len(outs),
            out_shape=list(outs),
            scratch_shapes=list(scratch),
            input_output_aliases=aliases or {},
            compiler_params=pltpu.CompilerParams(vmem_limit_bytes=8 * 1024 * 1024),
            cost_estimate=pl.CostEstimate(flops=flops, bytes_accessed=moved, transcendentals=0),
            name=name,
        )(*args)

    product = 2 * rows * HD * HD
    inputs = (doc_lengths, queries, keys, values, grad_out)
    states = shape(2, half, HD, HD)
    chunks = 2
    (send,) = call(
        functools.partial(send_kernel, total, chunks),
        "send",
        [states],
        inputs,
        [smem] + [hbm] * 4,
        flops=2 * half * product,
        scratch=[pltpu.VMEM((4, rows, half * HD), BF16), pltpu.SemaphoreType.DMA((4, chunks))],
    )
    swap = [(i, i ^ 1) for i in range(n)]
    got = lax.ppermute(send, "seq", swap)
    keep, table = call(
        functools.partial(keep_kernel, total),
        "keep",
        [states, shape(COEFS, HD, dtype=F32)],
        inputs,
        [smem] + [vmem] * 4,
        flops=2 * half * product,
    )
    mats = shape(heads, rows, HD)
    local = call(
        functools.partial(local_kernel, total),
        "local",
        [mats] * 6 + [shape(rows, width), shape(2, rows, HD), shape(rows, HD, dtype=F32)],
        inputs,
        [smem] + [vmem] * 4,
        flops=4 * heads * product,
    )
    owned = shape(2, per, HD, HD)
    sums = call(pair_kernel, "pair", [owned] * PAIRS, (table, keep, got), [vmem] * 3)

    def trade(parts):
        return [parts[0]] + [
            lax.ppermute(parts[d], "seq", [(i, i ^ (2 * d)) for i in range(n)]) for d in range(1, PAIRS)
        ]

    sums = trade(sums)
    kinds = 1 if teams == 2 else 2
    (edge,) = call(
        totals_kernel, "totals", [shape(kinds, per, HD, HD)], (table, *sums), [vmem] * 5
    )
    up = [(i, i + TEAM) for i in range(n - TEAM)]
    down = [(j, i) for i, j in up]
    if kinds == 1:
        enter = lax.ppermute(edge, "seq", up + down)
    else:
        enter = jnp.stack([lax.ppermute(edge[0], "seq", up), lax.ppermute(edge[1], "seq", down)])
    entering = trade(call(scan_kernel, "scan", [owned] * PAIRS, (table, *sums, enter), [vmem] * 6))
    mine, theirs = call(
        post_kernel, "post", [states] * 2, (table, *entering, keep, got), [vmem] * 7
    )
    other = lax.ppermute(theirs, "seq", swap)
    w, wt, dw, dwt, kt, qt, scaled, masks, root = local
    fixed = (queries, keys, values, scaled, w, wt, dw, dwt, kt, qt, masks, root)
    chunks = 4
    outs = [shape(rows, width)] * 4

    def finish(name, other, state, before):
        return call(
            functools.partial(finish_kernel, other, chunks),
            name,
            outs,
            (*fixed, state, *before),
            [vmem] * 13 + [hbm] * len(before),
            [hbm] * 4,
            flops=8 * half * product,
            scratch=[pltpu.VMEM((4, rows, half * HD), BF16), pltpu.SemaphoreType.DMA((4, chunks))],
            aliases={13 + i: i for i in range(len(before))},
        )

    return tuple(finish("finish_other", True, other, finish("finish_mine", False, mine, ())))


def solution(mesh):
    placed = P(("groups", "seq"), None)
    return jax.shard_map(
        per_device,
        mesh=mesh,
        in_specs=(placed,) * 4 + (P("groups"),),
        out_specs=(placed,) * 4,
        check_vma=False,
    )
```

time: 61.4 us -> 41.6 us (0.68)
  blocking collectives: 20 us -> 0 us
  Pallas kernels: 18.4 us -> 8.79 us
  starting transfers between devices: 6.45 us -> 11.5 us
  local copies, waits for them, and re-layouts: 1.6 us -> 5.72 us
  waiting for transfers between devices: 13.9 us -> 14.6 us
    all_to_all x1 -> x0, blocking collectives: 20 us -> none  [per_device(): lax.all_to_all(states, 'seq', 0, 0, axis_index_groups=members, tiled=True)]
    ppermute x0 -> x8, waiting for transfers between devices: none -> 12.2 us  [the longest x6 11.9 us: trade(): lax.ppermute(parts[d], 'seq', [(i, i ^ 2 * d) for i in range(n)])]
    all_to_all x1 -> x0, waiting for transfers between devices: 10.2 us -> none  [per_device(): lax.all_to_all(entering, 'seq', 0, 0, axis_index_groups=members, tiled=True)]
    pallas_call x5 -> x9, Pallas kernels: 18.4 us -> 8.79 us  [call(): pl.pallas_call(kernel, in_specs=specs, out_specs=out_specs or [vmem] * le...]
    ppermute x0 -> x8, starting transfers between devices: none -> 8.67 us  [the longest x6 8.08 us: trade(): lax.ppermute(parts[d], 'seq', [(i, i ^ 2 * d) for i in range(n)])]
    unnamed x4 -> x20, local copies, waits for them, and re-layouts: 1.6 us -> 5.72 us
    all_to_all x1 -> x0, starting transfers between devices: 3.56 us -> none  [per_device(): lax.all_to_all(entering, 'seq', 0, 0, axis_index_groups=members, tiled=True)]
    ppermute x1, waiting for transfers between devices: 3.68 us -> 2.43 us  [per_device(): enter = lax.ppermute(edge, 'seq', up + down)]
  transfers between devices with their start and end apart: 2 -> 9, of which waited for: 2 -> 8; matrix products, arithmetic and copies ran while one was open for 0% -> 0% of each run, Pallas kernels for 7% -> 12%
where the time goes in v2:
time: 41.6 us; the launch traced here: 41.3 us
  waiting for transfers between devices  14.6 us (35%)
  starting transfers between devices  11.5 us (28%)
  Pallas kernels  8.79 us (21%)
  local copies, waits for them, and re-layouts  5.72 us (14%)
  between operations  0.72 us (2%)
    ppermute x6, waiting for transfers between devices, trade(): lax.ppermute(parts[d], 'seq', [(i, i ^ 2 * d) for i in range(n)])  11.9 us
    pallas_call x9, Pallas kernels, call(): pl.pallas_call(kernel, in_specs=specs, out_specs=out_specs or [vmem] * le...  8.79 us
    ppermute x6, starting transfers between devices, trade(): lax.ppermute(parts[d], 'seq', [(i, i ^ 2 * d) for i in range(n)])  8.08 us
    unnamed x20, local copies, waits for them, and re-layouts  5.72 us
    ppermute x1, starting transfers between devices, per_device(): enter = lax.ppermute(edge, 'seq', up + down)  2.8 us
    ppermute x1, waiting for transfers between devices, per_device(): enter = lax.ppermute(edge, 'seq', up + down)  2.43 us
  transfers between devices with their start and end apart: 9, of which 8 were waited for; matrix products, arithmetic and copies ran while one was open for 0% of the time, Pallas kernels for 12%

profile of v2, /device:TPU:0, one launch (start us, length us, event | category | flops | bytes accessed | tf_op | source)
XLA Modules:
  0.0 41.3 jit_solution(4269407929185308009)
XLA Ops:
  0.6 1.0 %copy-done = bf16[128,2048]{1,0:T(8,128)(2,1)S(1)} copy-done((bf16[128,2048]{1,0:T(8,128)(2,1)S(1)}, bf16[128,2048]{1,0:T(8,128)(2,1)}, u32[]{:S(2)}) %copy-start) | copy-done | bytes 524312
  1.7 1.0 %copy-done.2 = bf16[128,2048]{1,0:T(8,128)(2,1)S(1)} copy-done((bf16[128,2048]{1,0:T(8,128)(2,1)S(1)}, bf16[128,2048]{1,0:T(8,128)(2,1)}, u32[]{:S(2)}) %copy-start.2) | copy-done | bytes 524312
  2.7 1.0 %copy-done.4 = bf16[128,2048]{1,0:T(8,128)(2,1)S(1)} copy-done((bf16[128,2048]{1,0:T(8,128)(2,1)S(1)}, bf16[128,2048]{1,0:T(8,128)(2,1)}, u32[]{:S(2)}) %copy-start.4) | copy-done | bytes 524312
  3.8 1.0 %copy-done.6 = bf16[128,2048]{1,0:T(8,128)(2,1)S(1)} copy-done((bf16[128,2048]{1,0:T(8,128)(2,1)S(1)}, bf16[128,2048]{1,0:T(8,128)(2,1)}, u32[]{:S(2)}) %copy-start.6) | copy-done | bytes 524312
  4.8 0.7 %copy-done.8 = s32[8]{0:T(128)S(1)} copy-done((s32[8]{0:T(128)S(1)}, s32[8]{0:T(128)}, u32[]{:S(2)}) %copy-start.8) | copy-done | bytes 56
  5.5 1.4 %send.1 = bf16[2,8,128,128]{3,2,1,0:T(8,128)(2,1)S(1)} custom-call(s32[8]{0:T(128)S(1)} %copy-done.8, bf16[128,2048]{1,0:T(8,128)(2,1)S(1)} %copy-done, bf16[128,2048]{1,0:T(8,128)(2,1)S(1)} %copy-done.2, bf16[128,2048]{1,0:T(8,128)(2,1)S(1)} %copy-done.4, bf16[128,2048]{1,0:T(8,128)(2,1)S(1)} %copy-done.6), custom_call_target="tpu_custom_call" | custom-call | flops 67108864 | bytes 2621472 | tf_op jit(solution)/shard_map/send/pallas_call | solution.py:336
  6.9 0.5 %collective-permute-start = (bf16[2,8,128,128]{3,2,1,0:T(8,128)(2,1)S(1)}, bf16[2,8,128,128]{3,2,1,0:T(8,128)(2,1)S(1)}, u32[]{:S(2)}, u32[]{:S(2)}) collective-permute-start(bf16[2,8,128,128]{3,2,1,0:T(8,128)(2,1)S(1)} %send.1), channel_id=1, source_target_pairs={{0,1},{1,0},{2,3},{3,2},{4,5},{5,4},{6,7},{7,6},{8,9},{9,8},{10,11... | collective-permute-start | bytes 1572872 | tf_op jit(solution)/shard_map/ppermute | solution.py:362
  7.4 1.3 %keep.1 = (bf16[2,8,128,128]{3,2,1,0:T(8,128)(2,1)S(1)}, f32[64,128]{1,0:T(8,128)S(1)}) custom-call(s32[8]{0:T(128)S(1)} %copy-done.8, bf16[128,2048]{1,0:T(8,128)(2,1)S(1)} %copy-done, bf16[128,2048]{1,0:T(8,128)(2,1)S(1)} %copy-done.2, bf16[128,2048]{1,0:T(8,128)(2,1)S(1)} %copy-done.4, bf16[128,2048]{1,0:T(8,128)(2,1)S(1)} %copy-done.6), custom_call_target="tpu_custom_call" | custom-call | flops 67108864 | bytes 2654240 | tf_op jit(solution)/shard_map/keep/pallas_call | solution.py:336
  8.7 0.3 collective-permute-done.got_ref
  9.0 0.2 pair.1
  9.1 3.0 %collective-permute-start.1 = (bf16[2,2,128,128]{3,2,1,0:T(8,128)(2,1)S(1)}, bf16[2,2,128,128]{3,2,1,0:T(8,128)(2,1)S(1)}, u32[]{:S(2)}, u32[]{:S(2)}) collective-permute-start(bf16[2,2,128,128]{3,2,1,0:T(8,128)(2,1)S(1)} %get-tuple-element.41), channel_id=1, source_target_pairs={{0,2},{1,3},{2,0},{3,1},{4,6},{5,7},{6,4},{7,5},{8,10},{9,11},{10,... | collective-permute-start | bytes 393224 | tf_op jit(solution)/shard_map/ppermute | solution.py:385
  12.1 1.6 %collective-permute-start.2 = (bf16[2,2,128,128]{3,2,1,0:T(8,128)(2,1)S(1)}, bf16[2,2,128,128]{3,2,1,0:T(8,128)(2,1)S(1)}, u32[]{:S(2)}, u32[]{:S(2)}) collective-permute-start(bf16[2,2,128,128]{3,2,1,0:T(8,128)(2,1)S(1)} %get-tuple-element.42), channel_id=1, source_target_pairs={{0,4},{1,5},{2,6},{3,7},{4,0},{5,1},{6,2},{7,3},{8,12},{9,13},{10,... | collective-permute-start | bytes 393224 | tf_op jit(solution)/shard_map/ppermute | solution.py:385
  13.7 2.2 %collective-permute-done.1.s1 = bf16[2,2,128,128]{3,2,1,0:T(8,128)(2,1)S(1)} collective-permute-done((bf16[2,2,128,128]{3,2,1,0:T(8,128)(2,1)S(1)}, bf16[2,2,128,128]{3,2,1,0:T(8,128)(2,1)S(1)}, u32[]{:S(2)}, u32[]{:S(2)}) %collective-permute-start.1) | collective-permute-done | bytes 131104 | tf_op jit(solution)/shard_map/ppermute | solution.py:385
  15.9 2.6 %collective-permute-done.2.s2 = bf16[2,2,128,128]{3,2,1,0:T(8,128)(2,1)S(1)} collective-permute-done((bf16[2,2,128,128]{3,2,1,0:T(8,128)(2,1)S(1)}, bf16[2,2,128,128]{3,2,1,0:T(8,128)(2,1)S(1)}, u32[]{:S(2)}, u32[]{:S(2)}) %collective-permute-start.2) | collective-permute-done | bytes 131104 | tf_op jit(solution)/shard_map/ppermute | solution.py:385
  18.5 1.5 %collective-permute-done.3.s3 = bf16[2,2,128,128]{3,2,1,0:T(8,128)(2,1)S(1)} collective-permute-done((bf16[2,2,128,128]{3,2,1,0:T(8,128)(2,1)S(1)}, bf16[2,2,128,128]{3,2,1,0:T(8,128)(2,1)S(1)}, u32[]{:S(2)}, u32[]{:S(2)}) %collective-permute-start.3) | collective-permute-done | bytes 131104 | tf_op jit(solution)/shard_map/ppermute | solution.py:385
  20.0 0.1 totals.1
  20.1 2.8 %collective-permute-start.4 = (bf16[1,2,128,128]{3,2,1,0:T(8,128)(2,1)S(1)}, bf16[1,2,128,128]{3,2,1,0:T(8,128)(2,1)S(1)}, u32[]{:S(2)}, u32[]{:S(2)}) collective-permute-start(bf16[1,2,128,128]{3,2,1,0:T(8,128)(2,1)S(1)} %totals.1), channel_id=1, source_target_pairs={{0,8},{1,9},{2,10},{3,11},{4,12},{5,13},{6,14},{7,15},{8,0},{9,1},... | collective-permute-start | bytes 196616 | tf_op jit(solution)/shard_map/ppermute | solution.py:396
  22.9 2.4 %collective-permute-done.4.enter_ref = bf16[1,2,128,128]{3,2,1,0:T(8,128)(2,1)S(1)} collective-permute-done((bf16[1,2,128,128]{3,2,1,0:T(8,128)(2,1)S(1)}, bf16[1,2,128,128]{3,2,1,0:T(8,128)(2,1)S(1)}, u32[]{:S(2)}, u32[]{:S(2)}) %collective-permute-start.4) | collective-permute-done | bytes 65568 | tf_op jit(solution)/shard_map/ppermute | solution.py:396
  25.3 0.3 scan.1
  25.6 1.7 %collective-permute-start.5 = (bf16[2,2,128,128]{3,2,1,0:T(8,128)(2,1)S(1)}, bf16[2,2,128,128]{3,2,1,0:T(8,128)(2,1)S(1)}, u32[]{:S(2)}, u32[]{:S(2)}) collective-permute-start(bf16[2,2,128,128]{3,2,1,0:T(8,128)(2,1)S(1)} %get-tuple-element.45), channel_id=1, source_target_pairs={{0,2},{1,3},{2,0},{3,1},{4,6},{5,7},{6,4},{7,5},{8,10},{9,11},{10,... | collective-permute-start | bytes 393224 | tf_op jit(solution)/shard_map/ppermute | solution.py:385
  27.3 1.6 %collective-permute-start.6 = (bf16[2,2,128,128]{3,2,1,0:T(8,128)(2,1)S(1)}, bf16[2,2,128,128]{3,2,1,0:T(8,128)(2,1)S(1)}, u32[]{:S(2)}, u32[]{:S(2)}) collective-permute-start(bf16[2,2,128,128]{3,2,1,0:T(8,128)(2,1)S(1)} %get-tuple-element.46), channel_id=1, source_target_pairs={{0,4},{1,5},{2,6},{3,7},{4,0},{5,1},{6,2},{7,3},{8,12},{9,13},{10,... | collective-permute-start | bytes 393224 | tf_op jit(solution)/shard_map/ppermute | solution.py:385
  28.9 0.2 collective-permute-start.7
  29.2 2.9 %collective-permute-done.5.c1 = bf16[2,2,128,128]{3,2,1,0:T(8,128)(2,1)S(1)} collective-permute-done((bf16[2,2,128,128]{3,2,1,0:T(8,128)(2,1)S(1)}, bf16[2,2,128,128]{3,2,1,0:T(8,128)(2,1)S(1)}, u32[]{:S(2)}, u32[]{:S(2)}) %collective-permute-start.5) | collective-permute-done | bytes 131104 | tf_op jit(solution)/shard_map/ppermute | solution.py:385
  32.1 0.3 collective-permute-done.6.c2
  32.3 2.5 %collective-permute-done.7.c3 = bf16[2,2,128,128]{3,2,1,0:T(8,128)(2,1)S(1)} collective-permute-done((bf16[2,2,128,128]{3,2,1,0:T(8,128)(2,1)S(1)}, bf16[2,2,128,128]{3,2,1,0:T(8,128)(2,1)S(1)}, u32[]{:S(2)}, u32[]{:S(2)}) %collective-permute-start.7) | collective-permute-done | bytes 131104 | tf_op jit(solution)/shard_map/ppermute | solution.py:385
  34.8 0.4 post.1
  35.3 0.6 %copy-done.1 = bf16[128,2048]{1,0:T(8,128)(2,1)S(1)} copy-done((bf16[128,2048]{1,0:T(8,128)(2,1)S(1)}, bf16[128,2048]{1,0:T(8,128)(2,1)}, u32[]{:S(2)}) %copy-start.1) | copy-done | bytes 524312
  35.8 0.2 copy-done.3
  36.0 0.2 copy-done.5
  36.2 1.9 %local.1 = (bf16[16,128,128]{2,1,0:T(8,128)(2,1)S(1)}, bf16[16,128,128]{2,1,0:T(8,128)(2,1)S(1)}, bf16[16,128,128]{2,1,0:T(8,128)(2,1)S(1)}, bf16[16,128,128]{2,...) custom-call(s32[8]{0:T(128)S(1)} %copy-done.9, ...), custom_call_target="tpu_custom_call" | custom-call | flops 268435456 | bytes 5898272 | tf_op jit(solution)/shard_map/local/pallas_call | solution.py:336
  38.1 1.6 %finish_mine.1 = (bf16[128,2048]{1,0:T(8,128)(2,1)}, bf16[128,2048]{1,0:T(8,128)(2,1)}, bf16[128,2048]{1,0:T(8,128)(2,1)}, bf16[128,2048]{1,0:T(8,128)(2,1)}) custom-call(bf16[128,2048]{1,0:T(8,128)(2,1)S(1)} %copy-done.1, bf16[128,2048]{1,0:T(8,128)(2,1)S(1)} %copy-done.3, bf16[128,2048]{1,0:T(8,128)(2,1)S(1)} %copy-done.5, ...), custom_call_target="tpu_custom_call" | custom-call | flops 268435456 | bytes 7995392 | tf_op jit(solution)/shard_map/finish_mine/pallas_call | solution.py:336
  39.7 1.6 %finish_other.1 = (bf16[128,2048]{1,0:T(8,128)(2,1)}, bf16[128,2048]{1,0:T(8,128)(2,1)}, bf16[128,2048]{1,0:T(8,128)(2,1)}, bf16[128,2048]{1,0:T(8,128)(2,1)}) custom-call(bf16[128,2048]{1,0:T(8,128)(2,1)S(1)} %copy-done.1, bf16[128,2048]{1,0:T(8,128)(2,1)S(1)} %copy-done.3, ...), custom_call_target="tpu_custom_call", output_to_operand_aliasing={{0}: (13, {}), {1}: (14, {}), {2}: (15, {}), {3}: (16, {})} | custom-call | flops 268435456 | bytes 10092544 | tf_op jit(solution)/shard_map/finish_other/pallas_call | solution.py:336
  (15 shorter events, 0.1 us)
Async XLA Ops:
  0.6 1.0 %copy-start = (bf16[128,2048]{1,0:T(8,128)(2,1)S(1)}, bf16[128,2048]{1,0:T(8,128)(2,1)}, u32[]{:S(2)}) copy-start(bf16[128,2048]{1,0:T(8,128)(2,1)} %refs_0_.3) | copy-start | bytes 1572868
  1.7 1.0 %copy-start.2 = (bf16[128,2048]{1,0:T(8,128)(2,1)S(1)}, bf16[128,2048]{1,0:T(8,128)(2,1)}, u32[]{:S(2)}) copy-start(bf16[128,2048]{1,0:T(8,128)(2,1)} %refs_1_.3) | copy-start | bytes 1572868
  2.7 1.0 %copy-start.4 = (bf16[128,2048]{1,0:T(8,128)(2,1)S(1)}, bf16[128,2048]{1,0:T(8,128)(2,1)}, u32[]{:S(2)}) copy-start(bf16[128,2048]{1,0:T(8,128)(2,1)} %refs_2_.3) | copy-start | bytes 1572868
  3.8 1.0 %copy-start.6 = (bf16[128,2048]{1,0:T(8,128)(2,1)S(1)}, bf16[128,2048]{1,0:T(8,128)(2,1)}, u32[]{:S(2)}) copy-start(bf16[128,2048]{1,0:T(8,128)(2,1)} %g_ref.5) | copy-start | bytes 1572868
  4.8 0.7 %copy-start.8 = (s32[8]{0:T(128)S(1)}, s32[8]{0:T(128)}, u32[]{:S(2)}) copy-start(s32[8]{0:T(128)} %len_ref.5) | copy-start | bytes 100
  6.9 2.1 %collective-permute-start = (bf16[2,8,128,128]{3,2,1,0:T(8,128)(2,1)S(1)}, bf16[2,8,128,128]{3,2,1,0:T(8,128)(2,1)S(1)}, u32[]{:S(2)}, u32[]{:S(2)}) collective-permute-start(bf16[2,8,128,128]{3,2,1,0:T(8,128)(2,1)S(1)} %send.1), channel_id=1, source_target_pairs={{0,1},{1,0},{2,3},{3,2},{4,5},{5,4},{6,7},{7,6},{8,9},{9,8},{10,11... | collective-permute-start | bytes 1572872 | tf_op jit(solution)/shard_map/ppermute | solution.py:362
  9.1 6.8 %collective-permute-start.1 = (bf16[2,2,128,128]{3,2,1,0:T(8,128)(2,1)S(1)}, bf16[2,2,128,128]{3,2,1,0:T(8,128)(2,1)S(1)}, u32[]{:S(2)}, u32[]{:S(2)}) collective-permute-start(bf16[2,2,128,128]{3,2,1,0:T(8,128)(2,1)S(1)} %get-tuple-element.41), channel_id=1, source_target_pairs={{0,2},{1,3},{2,0},{3,1},{4,6},{5,7},{6,4},{7,5},{8,10},{9,11},{10,... | collective-permute-start | bytes 393224 | tf_op jit(solution)/shard_map/ppermute | solution.py:385
  12.1 6.4 %collective-permute-start.2 = (bf16[2,2,128,128]{3,2,1,0:T(8,128)(2,1)S(1)}, bf16[2,2,128,128]{3,2,1,0:T(8,128)(2,1)S(1)}, u32[]{:S(2)}, u32[]{:S(2)}) collective-permute-start(bf16[2,2,128,128]{3,2,1,0:T(8,128)(2,1)S(1)} %get-tuple-element.42), channel_id=1, source_target_pairs={{0,4},{1,5},{2,6},{3,7},{4,0},{5,1},{6,2},{7,3},{8,12},{9,13},{10,... | collective-permute-start | bytes 393224 | tf_op jit(solution)/shard_map/ppermute | solution.py:385
  13.7 6.3 %collective-permute-start.3 = (bf16[2,2,128,128]{3,2,1,0:T(8,128)(2,1)S(1)}, bf16[2,2,128,128]{3,2,1,0:T(8,128)(2,1)S(1)}, u32[]{:S(2)}, u32[]{:S(2)}) collective-permute-start(bf16[2,2,128,128]{3,2,1,0:T(8,128)(2,1)S(1)} %get-tuple-element.43), channel_id=1, source_target_pairs={{0,6},{1,7},{2,4},{3,5},{4,2},{5,3},{6,0},{7,1},{8,14},{9,15},{10,... | collective-permute-start | bytes 393224 | tf_op jit(solution)/shard_map/ppermute | solution.py:385
  20.1 5.2 %collective-permute-start.4 = (bf16[1,2,128,128]{3,2,1,0:T(8,128)(2,1)S(1)}, bf16[1,2,128,128]{3,2,1,0:T(8,128)(2,1)S(1)}, u32[]{:S(2)}, u32[]{:S(2)}) collective-permute-start(bf16[1,2,128,128]{3,2,1,0:T(8,128)(2,1)S(1)} %totals.1), channel_id=1, source_target_pairs={{0,8},{1,9},{2,10},{3,11},{4,12},{5,13},{6,14},{7,15},{8,0},{9,1},... | collective-permute-start | bytes 196616 | tf_op jit(solution)/shard_map/ppermute | solution.py:396
  25.3 9.9 %copy-start.7 = (bf16[128,2048]{1,0:T(8,128)(2,1)S(1)}, bf16[128,2048]{1,0:T(8,128)(2,1)}, u32[]{:S(2)}) copy-start(bf16[128,2048]{1,0:T(8,128)(2,1)} %g_ref.5) | copy-start | bytes 1572868
  25.6 6.4 %collective-permute-start.5 = (bf16[2,2,128,128]{3,2,1,0:T(8,128)(2,1)S(1)}, bf16[2,2,128,128]{3,2,1,0:T(8,128)(2,1)S(1)}, u32[]{:S(2)}, u32[]{:S(2)}) collective-permute-start(bf16[2,2,128,128]{3,2,1,0:T(8,128)(2,1)S(1)} %get-tuple-element.45), channel_id=1, source_target_pairs={{0,2},{1,3},{2,0},{3,1},{4,6},{5,7},{6,4},{7,5},{8,10},{9,11},{10,... | collective-permute-start | bytes 393224 | tf_op jit(solution)/shard_map/ppermute | solution.py:385
  27.3 5.0 %collective-permute-start.6 = (bf16[2,2,128,128]{3,2,1,0:T(8,128)(2,1)S(1)}, bf16[2,2,128,128]{3,2,1,0:T(8,128)(2,1)S(1)}, u32[]{:S(2)}, u32[]{:S(2)}) collective-permute-start(bf16[2,2,128,128]{3,2,1,0:T(8,128)(2,1)S(1)} %get-tuple-element.46), channel_id=1, source_target_pairs={{0,4},{1,5},{2,6},{3,7},{4,0},{5,1},{6,2},{7,3},{8,12},{9,13},{10,... | collective-permute-start | bytes 393224 | tf_op jit(solution)/shard_map/ppermute | solution.py:385
  28.9 5.9 %collective-permute-start.7 = (bf16[2,2,128,128]{3,2,1,0:T(8,128)(2,1)S(1)}, bf16[2,2,128,128]{3,2,1,0:T(8,128)(2,1)S(1)}, u32[]{:S(2)}, u32[]{:S(2)}) collective-permute-start(bf16[2,2,128,128]{3,2,1,0:T(8,128)(2,1)S(1)} %get-tuple-element.47), channel_id=1, source_target_pairs={{0,6},{1,7},{2,4},{3,5},{4,2},{5,3},{6,0},{7,1},{8,14},{9,15},{10,... | collective-permute-start | bytes 393224 | tf_op jit(solution)/shard_map/ppermute | solution.py:385
  34.8 1.0 %copy-start.1 = (bf16[128,2048]{1,0:T(8,128)(2,1)S(1)}, bf16[128,2048]{1,0:T(8,128)(2,1)}, u32[]{:S(2)}) copy-start(bf16[128,2048]{1,0:T(8,128)(2,1)} %refs_0_.3) | copy-start | bytes 1572868
  34.8 1.2 %copy-start.3 = (bf16[128,2048]{1,0:T(8,128)(2,1)S(1)}, bf16[128,2048]{1,0:T(8,128)(2,1)}, u32[]{:S(2)}) copy-start(bf16[128,2048]{1,0:T(8,128)(2,1)} %refs_1_.3) | copy-start | bytes 1572868
  34.8 1.4 %copy-start.5 = (bf16[128,2048]{1,0:T(8,128)(2,1)S(1)}, bf16[128,2048]{1,0:T(8,128)(2,1)}, u32[]{:S(2)}) copy-start(bf16[128,2048]{1,0:T(8,128)(2,1)} %refs_2_.3) | copy-start | bytes 1572868
  35.2 1.0 %copy-start.9 = (s32[8]{0:T(128)S(1)}, s32[8]{0:T(128)}, u32[]{:S(2)}) copy-start(s32[8]{0:T(128)} %len_ref.5) | copy-start | bytes 100
  35.2 4.5 %collective-permute-start.8 = (bf16[2,8,128,128]{3,2,1,0:T(8,128)(2,1)S(1)}, bf16[2,8,128,128]{3,2,1,0:T(8,128)(2,1)S(1)}, u32[]{:S(2)}, u32[]{:S(2)}) collective-permute-start(bf16[2,8,128,128]{3,2,1,0:T(8,128)(2,1)S(1)} %get-tuple-element.48), channel_id=1, source_target_pairs={{0,1},{1,0},{2,3},{3,2},{4,5},{5,4},{6,7},{7,6},{8,9},{9,8},{10,11... | collective-permute-start | bytes 1572872 | tf_op jit(solution)/shard_map/ppermute | solution.py:403

commit v3 on v2

--- a/solution.py
+++ b/solution.py
@@ -9,6 +9,7 @@
 
 HD = 128
 PAIRS = 4
+PARTNERS = (0, 3, 1, 2)
 TEAM = 2 * PAIRS
 F32 = jnp.float32
 BF16 = jnp.bfloat16
@@ -63,45 +64,75 @@
     return lax.dot_general(a, b, ((contract[:1], contract[1:]), ((), ())), preferred_element_type=F32)
 
 
-def state_pair(total, starts, first, rows):
-    pos, _, inv_root = row_facts(starts, first, rows)
-    tail_rows = pos >= max_start(starts, first + rows)
-    head_rows = pos < min_start(starts, first + 1, total)
-    zero = jnp.zeros((), BF16)
-
-    def of(q, k, v, g):
-        scaled = (g.astype(F32) * inv_root).astype(BF16)
-        tail = dot(jnp.where(tail_rows, k, zero), v, (0, 0))
-        head = dot(jnp.where(head_rows, q, zero), scaled, (0, 0))
-        return tail.astype(BF16), head.astype(BF16)
-
-    return of
-
-
-def send_kernel(total, chunks, len_ref, q_ref, k_ref, v_ref, g_ref, out_ref, buf, sems):
+def states_of(q, k, v, g, tail_rows, head_rows, inv_root):
+    scaled = (g.astype(F32) * inv_root).astype(BF16)
+    tail = dot(k * tail_rows, v, (0, 0))
+    head = dot(q * head_rows, scaled, (0, 0))
+    return tail.astype(BF16), head.astype(BF16)
+
+
+def send_kernel(
+    total,
+    chunks,
+    len_hbm,
+    q_hbm,
+    k_hbm,
+    v_hbm,
+    g_hbm,
+    len_out,
+    out_ref,
+    q_ref,
+    k_ref,
+    v_ref,
+    g_ref,
+    rows_ref,
+    root_ref,
+    len_ref,
+    sems,
+    len_sems,
+):
     rows = q_ref.shape[0]
     half = out_ref.shape[1] * HD
     me = lax.axis_index("seq")
-    offset = (1 - lax.rem(me, 2)) * half
+    other = (1 - lax.rem(me, 2)) * half
+    mine = lax.rem(me, 2) * half
     size = half // chunks
+    len_copy = pltpu.make_async_copy(len_hbm, len_ref, len_sems.at[0])
+    len_copy.start()
+    len_pass = pltpu.make_async_copy(len_hbm, len_out, len_sems.at[1])
+    len_pass.start()
+    pairs = ((q_hbm, q_ref), (k_hbm, k_ref), (v_hbm, v_ref), (g_hbm, g_ref))
     copies = []
-    for c in range(chunks):
-        at = pl.ds(pl.multiple_of(offset + c * size, HD), size)
-        for i, ref in enumerate((q_ref, k_ref, v_ref, g_ref)):
-            copy = pltpu.make_async_copy(
-                ref.at[:, at], buf.at[i, :, pl.ds(c * size, size)], sems.at[i, c]
-            )
+    for c in range(2 * chunks):
+        begin = other + c * size if c < chunks else mine + (c - chunks) * size
+        at = pl.ds(pl.multiple_of(begin, HD), size)
+        for i, (src, dst) in enumerate(pairs):
+            copy = pltpu.make_async_copy(src.at[:, at], dst.at[:, at], sems.at[i, c])
             copy.start()
             copies.append(copy)
-    of = state_pair(total, doc_starts(len_ref), me * rows, rows)
+    len_copy.wait()
+    starts = doc_starts(len_ref)
+    first = me * rows
+    pos, _, inv_root = row_facts(starts, first, rows)
+    one, none = jnp.ones((), F32), jnp.zeros((), F32)
+    tail_rows = jnp.where(pos >= max_start(starts, first + rows), one, none).astype(BF16)
+    head_rows = jnp.where(pos < min_start(starts, first + 1, total), one, none).astype(BF16)
+    rows_ref[0] = tail_rows
+    rows_ref[1] = head_rows
+    root_ref[...] = inv_root
     for c in range(chunks):
         for copy in copies[4 * c : 4 * c + 4]:
             copy.wait()
         for h in range(c * size // HD, (c + 1) * size // HD):
-            cols = pl.ds(h * HD, HD)
-            tail, head = of(*(buf[i, :, cols] for i in range(4)))
+            cols = pl.ds(pl.multiple_of(other + h * HD, HD), HD)
+            tail, head = states_of(
+                q_ref[:, cols], k_ref[:, cols], v_ref[:, cols], g_ref[:, cols], tail_rows, head_rows, inv_root
+            )
             out_ref[0, h] = tail
             out_ref[1, h] = head
+    for copy in copies[4 * chunks :]:
+        copy.wait()
+    len_pass.wait()
 
 
 def coefficients(starts, rows, n, coef_ref):
@@ -122,7 +153,7 @@
         return (a == b).astype(jnp.int32)
 
     team_low, team_high = both(base), both(base + TEAM)
-    pairs = [pair ^ d for d in range(PAIRS)]
+    pairs = [pair ^ d for d in PARTNERS]
     low = [both(base + 2 * p) for p in pairs]
     high = [both(base + 2 * p + 2) for p in pairs]
     middle = both(me - core + 1)
@@ -160,24 +191,27 @@
     put(THEIRS_B + 1, odd)
 
 
-def keep_kernel(total, len_ref, q_ref, k_ref, v_ref, g_ref, out_ref, coef_ref):
+def keep_kernel(total, len_hbm, q_ref, k_ref, v_ref, g_ref, rows_ref, root_ref, out_ref, coef_ref, len_ref, len_sem):
     rows = q_ref.shape[0]
     half = out_ref.shape[1] * HD
-    me = lax.axis_index("seq")
-    offset = lax.rem(me, 2) * half
-    starts = doc_starts(len_ref)
-    coefficients(starts, rows, total // rows, coef_ref)
-    of = state_pair(total, starts, me * rows, rows)
+    offset = lax.rem(lax.axis_index("seq"), 2) * half
+    len_copy = pltpu.make_async_copy(len_hbm, len_ref, len_sem)
+    len_copy.start()
+    tail_rows, head_rows, inv_root = rows_ref[0], rows_ref[1], root_ref[...]
     for h in range(out_ref.shape[1]):
         cols = pl.ds(pl.multiple_of(offset + h * HD, HD), HD)
-        tail, head = of(q_ref[:, cols], k_ref[:, cols], v_ref[:, cols], g_ref[:, cols])
+        tail, head = states_of(
+            q_ref[:, cols], k_ref[:, cols], v_ref[:, cols], g_ref[:, cols], tail_rows, head_rows, inv_root
+        )
         out_ref[0, h] = tail
         out_ref[1, h] = head
+    len_copy.wait()
+    coefficients(doc_starts(len_ref), rows, total // rows, coef_ref)
 
 
 def local_kernel(
     total,
-    len_ref,
+    len_hbm,
     q_ref,
     k_ref,
     v_ref,
@@ -190,13 +224,16 @@
     qt_ref,
     sg_ref,
     mask_ref,
-    root_ref,
+    len_ref,
+    len_sem,
 ):
+    len_copy = pltpu.make_async_copy(len_hbm, len_ref, len_sem)
+    len_copy.start()
+    len_copy.wait()
     rows, width = q_ref.shape
     first = lax.axis_index("seq") * rows
     starts = doc_starts(len_ref)
     pos, begin, inv_root = row_facts(starts, first, rows)
-    root_ref[...] = inv_root
     one, none = jnp.ones((), F32), jnp.zeros((), F32)
     mask_ref[0] = jnp.where(pos < min_start(starts, first, total), one, none).astype(BF16)
     suffix = pos >= max_start(starts + [jnp.int32(total)], first + rows + 1)
@@ -228,12 +265,13 @@
         ca, cb = coef(coef_ref, a), coef(coef_ref, b)
         for d, out_ref in enumerate(out_refs):
             for i in range(per):
-                h = (pair ^ d) * per + i
+                h = (pair ^ PARTNERS[d]) * per + i
                 both = keep_ref[kind, h].astype(F32) * ca + got_ref[kind, h].astype(F32) * cb
                 out_ref[kind, i] = both.astype(BF16)
 
 
-def totals_kernel(coef_ref, s0, s1, s2, s3, out_ref):
+def totals_kernel(coef_ref, s0, s1, s2, s3, after_ref, out_ref):
+    del after_ref
     sums = (s0, s1, s2, s3)
     for i in range(out_ref.shape[1]):
         fwd, bwd = (
@@ -271,7 +309,7 @@
         t0, t1 = coef(coef_ref, t), coef(coef_ref, t + 1)
         for d, c_ref in enumerate((c0, c1, c2, c3)):
             for i in range(per):
-                h = (pair ^ d) * per + i
+                h = (pair ^ PARTNERS[d]) * per + i
                 came = c_ref[kind, i].astype(F32)
                 theirs_ref[kind, h] = (came * t0 + keep_ref[kind, h].astype(F32) * t1).astype(BF16)
                 mine_ref[kind, h] = (came * m0 + got_ref[kind, h].astype(F32) * m1).astype(BF16)
@@ -281,13 +319,21 @@
     (q_ref, k_ref, v_ref, g_ref, w_ref, wt_ref, dw_ref, dwt_ref, kt_ref, qt_ref, mask_ref, root_ref, s_ref) = (
         refs[:13]
     )
-    out_refs, (buf, sems) = refs[-6:-2], refs[-2:]
     heads = s_ref.shape[1]
     core = lax.rem(lax.axis_index("seq"), 2)
     half = 1 - core if other else core
     prefix, suffix, root = mask_ref[0], mask_ref[1], root_ref[...]
     size = heads * HD // chunks
     copies = []
+    if other:
+        done_refs, out_refs, bufs, sems = refs[13:17], refs[17:21], refs[21:25], refs[25]
+        to = pl.ds(pl.multiple_of(core * heads * HD, HD), heads * HD)
+        for i, ref in enumerate(out_refs):
+            copy = pltpu.make_async_copy(done_refs[i], ref.at[:, to], sems.at[i, chunks])
+            copy.start()
+            copies.append(copy)
+    else:
+        bufs = refs[13:17]
 
     def wide(a, b):
         return jnp.concatenate([a, b], axis=1)
@@ -300,18 +346,19 @@
             q, k, v, g = q_ref[:, cols], k_ref[:, cols], v_ref[:, cols], g_ref[:, cols]
             carried, returned = s_ref[0, i], s_ref[1, i]
             o = dot(wide(w_ref[h], q * prefix), jnp.concatenate([v, carried], axis=0), (1, 0))
-            buf[0, :, at] = (o * root).astype(BF16)
+            bufs[0][:, at] = (o * root).astype(BF16)
             dq = dot(wide(dw_ref[h], g * prefix), wide(kt_ref[h], carried), (1, 1))
-            buf[1, :, at] = dq.astype(BF16)
+            bufs[1][:, at] = dq.astype(BF16)
             dk = dot(wide(dwt_ref[h], v * suffix), wide(qt_ref[h], returned), (1, 1))
-            buf[2, :, at] = dk.astype(BF16)
+            bufs[2][:, at] = dk.astype(BF16)
             dv = dot(wide(wt_ref[h], k * suffix), jnp.concatenate([g, returned], axis=0), (1, 0))
-            buf[3, :, at] = dv.astype(BF16)
-        to = pl.ds(pl.multiple_of(half * heads * HD + c * size, HD), size)
-        for i, ref in enumerate(out_refs):
-            copy = pltpu.make_async_copy(buf.at[i, :, pl.ds(c * size, size)], ref.at[:, to], sems.at[i, c])
-            copy.start()
-            copies.append(copy)
+            bufs[3][:, at] = dv.astype(BF16)
+        if other:
+            to = pl.ds(pl.multiple_of(half * heads * HD + c * size, HD), size)
+            for i, ref in enumerate(out_refs):
+                copy = pltpu.make_async_copy(bufs[i].at[:, pl.ds(c * size, size)], ref.at[:, to], sems.at[i, c])
+                copy.start()
+                copies.append(copy)
     for copy in copies:
         copy.wait()
 
@@ -324,14 +371,13 @@
     teams = n // TEAM
     half = heads // 2
     per = half // PAIRS
-    smem = pl.BlockSpec(memory_space=pltpu.SMEM)
     vmem = pl.BlockSpec(memory_space=pltpu.VMEM)
-    hbm = pl.BlockSpec(memory_space=pl.ANY)
+    hbm = pl.BlockSpec(memory_space=pltpu.HBM)
 
     def shape(*dims, dtype=BF16):
         return jax.ShapeDtypeStruct(dims, dtype)
 
-    def call(kernel, name, outs, args, specs, out_specs=None, flops=0, scratch=(), aliases=None):
+    def call(kernel, name, outs, args, specs, out_specs=None, flops=0, scratch=(), room=8):
         moved = sum(a.size * a.dtype.itemsize for a in list(args) + list(outs))
         return pl.pallas_call(
             kernel,
@@ -339,8 +385,7 @@
             out_specs=out_specs or [vmem] * len(outs),
             out_shape=list(outs),
             scratch_shapes=list(scratch),
-            input_output_aliases=aliases or {},
-            compiler_params=pltpu.CompilerParams(vmem_limit_bytes=8 * 1024 * 1024),
+            compiler_params=pltpu.CompilerParams(vmem_limit_bytes=room * 1024 * 1024),
             cost_estimate=pl.CostEstimate(flops=flops, bytes_accessed=moved, transcendentals=0),
             name=name,
         )(*args)
@@ -349,46 +394,57 @@
     inputs = (doc_lengths, queries, keys, values, grad_out)
     states = shape(2, half, HD, HD)
     chunks = 2
-    (send,) = call(
+    tokens = shape(rows, width)
+    lengths = [pltpu.SMEM(doc_lengths.shape, jnp.int32)]
+    doc_lengths, send, *ready = call(
         functools.partial(send_kernel, total, chunks),
         "send",
-        [states],
+        [shape(*doc_lengths.shape, dtype=jnp.int32), states]
+        + [tokens] * 4
+        + [shape(2, rows, HD), shape(rows, HD, dtype=F32)],
         inputs,
-        [smem] + [hbm] * 4,
+        [hbm] * 5,
+        [hbm] + [vmem] * 7,
         flops=2 * half * product,
-        scratch=[pltpu.VMEM((4, rows, half * HD), BF16), pltpu.SemaphoreType.DMA((4, chunks))],
-    )
+        scratch=lengths + [pltpu.SemaphoreType.DMA((4, 2 * chunks)), pltpu.SemaphoreType.DMA((2,))],
+        room=51,
+    )
+    queries, keys, values, grad_out, row_masks, root = ready
+    lengths = lengths + [pltpu.SemaphoreType.DMA(())]
     swap = [(i, i ^ 1) for i in range(n)]
     got = lax.ppermute(send, "seq", swap)
     keep, table = call(
         functools.partial(keep_kernel, total),
         "keep",
         [states, shape(COEFS, HD, dtype=F32)],
-        inputs,
-        [smem] + [vmem] * 4,
+        (doc_lengths, queries, keys, values, grad_out, row_masks, root),
+        [hbm] + [vmem] * 6,
         flops=2 * half * product,
+        scratch=lengths,
     )
     mats = shape(heads, rows, HD)
-    local = call(
+    *local, masks = call(
         functools.partial(local_kernel, total),
         "local",
-        [mats] * 6 + [shape(rows, width), shape(2, rows, HD), shape(rows, HD, dtype=F32)],
-        inputs,
-        [smem] + [vmem] * 4,
+        [mats] * 6 + [tokens, shape(2, rows, HD)],
+        (doc_lengths, queries, keys, values, grad_out),
+        [hbm] + [vmem] * 4,
         flops=4 * heads * product,
+        scratch=lengths,
     )
     owned = shape(2, per, HD, HD)
     sums = call(pair_kernel, "pair", [owned] * PAIRS, (table, keep, got), [vmem] * 3)
 
     def trade(parts):
         return [parts[0]] + [
-            lax.ppermute(parts[d], "seq", [(i, i ^ (2 * d)) for i in range(n)]) for d in range(1, PAIRS)
+            lax.ppermute(parts[d], "seq", [(i, i ^ (2 * PARTNERS[d])) for i in range(n)])
+            for d in range(1, PAIRS)
         ]
 
     sums = trade(sums)
     kinds = 1 if teams == 2 else 2
     (edge,) = call(
-        totals_kernel, "totals", [shape(kinds, per, HD, HD)], (table, *sums), [vmem] * 5
+        totals_kernel, "totals", [shape(kinds, per, HD, HD)], (table, *sums, masks), [vmem] * 6
     )
     up = [(i, i + TEAM) for i in range(n - TEAM)]
     down = [(j, i) for i, j in up]
@@ -401,25 +457,30 @@
         post_kernel, "post", [states] * 2, (table, *entering, keep, got), [vmem] * 7
     )
     other = lax.ppermute(theirs, "seq", swap)
-    w, wt, dw, dwt, kt, qt, scaled, masks, root = local
+    w, wt, dw, dwt, kt, qt, scaled = local
     fixed = (queries, keys, values, scaled, w, wt, dw, dwt, kt, qt, masks, root)
     chunks = 4
-    outs = [shape(rows, width)] * 4
-
-    def finish(name, other, state, before):
-        return call(
-            functools.partial(finish_kernel, other, chunks),
-            name,
-            outs,
-            (*fixed, state, *before),
-            [vmem] * 13 + [hbm] * len(before),
+    part = shape(rows, half * HD)
+    done = call(
+        functools.partial(finish_kernel, False, chunks),
+        "finish_mine",
+        [part] * 4,
+        (*fixed, mine),
+        [vmem] * 13,
+        flops=8 * half * product,
+    )
+    return tuple(
+        call(
+            functools.partial(finish_kernel, True, chunks),
+            "finish_other",
+            [tokens] * 4,
+            (*fixed, other, *done),
+            [vmem] * 17,
             [hbm] * 4,
             flops=8 * half * product,
-            scratch=[pltpu.VMEM((4, rows, half * HD), BF16), pltpu.SemaphoreType.DMA((4, chunks))],
-            aliases={13 + i: i for i in range(len(before))},
+            scratch=[pltpu.VMEM(part.shape, BF16)] * 4 + [pltpu.SemaphoreType.DMA((4, chunks + 1))],
         )
-
-    return tuple(finish("finish_other", True, other, finish("finish_mine", False, mine, ())))
+    )
 
 
 def solution(mesh):

time: 41.6 us -> 35.2 us (0.85)
  local copies, waits for them, and re-layouts: 5.72 us -> 0.65 us
  waiting for transfers between devices: 14.6 us -> 14 us
  Pallas kernels: 8.79 us -> 8.2 us
    unnamed x20 -> x2, local copies, waits for them, and re-layouts: 5.72 us -> 0.65 us
    ppermute x6, waiting for transfers between devices: 11.9 us -> 8.48 us  [trade(): lax.ppermute(parts[d], 'seq', [(i, i ^ 2 * PARTNERS[d]) for i in range(n)])]
    ppermute x1, waiting for transfers between devices: 2.43 us -> 3.97 us  [per_device(): enter = lax.ppermute(edge, 'seq', up + down)]
    ppermute x1, waiting for transfers between devices: 0.01 us -> 1.13 us  [per_device(): other = lax.ppermute(theirs, 'seq', swap)]
    pallas_call x9, Pallas kernels: 8.79 us -> 8.2 us  [call(): pl.pallas_call(kernel, in_specs=specs, out_specs=out_specs or [vmem] * le...]
  transfers between devices with their start and end apart: 9 -> 9, of which waited for: 8 -> 9; matrix products, arithmetic and copies ran while one was open for 0% -> 0% of each run, Pallas kernels for 12% -> 11%
where the time goes in v3:
time: 35.2 us; the launch traced here: 35 us
  waiting for transfers between devices  14 us (40%)
  starting transfers between devices  11.4 us (32%)
  Pallas kernels  8.2 us (23%)
  between operations  0.7 us (2%)
  local copies, waits for them, and re-layouts  0.65 us (2%)
    ppermute x6, waiting for transfers between devices, trade(): lax.ppermute(parts[d], 'seq', [(i, i ^ 2 * PARTNERS[d]) for i in range(n)])  8.48 us
    pallas_call x9, Pallas kernels, call(): pl.pallas_call(kernel, in_specs=specs, out_specs=out_specs or [vmem] * le...  8.2 us
    ppermute x6, starting transfers between devices, trade(): lax.ppermute(parts[d], 'seq', [(i, i ^ 2 * PARTNERS[d]) for i in range(n)])  8.16 us
    ppermute x1, waiting for transfers between devices, per_device(): enter = lax.ppermute(edge, 'seq', up + down)  3.97 us
    ppermute x1, starting transfers between devices, per_device(): enter = lax.ppermute(edge, 'seq', up + down)  2.66 us
    ppermute x1, waiting for transfers between devices, per_device(): other = lax.ppermute(theirs, 'seq', swap)  1.13 us
  transfers between devices with their start and end apart: 9, of which 9 were waited for; matrix products, arithmetic and copies ran while one was open for 0% of the time, Pallas kernels for 11%

profile of v3, /device:TPU:0, one launch (start us, length us, event | category | flops | bytes accessed | tf_op | source)
XLA Modules:
  0.0 35.0 jit_solution(16077203080223690351)
XLA Ops:
  0.6 0.0 copy-start
  0.6 0.6 %copy-done = s32[8]{0:T(128)S(1)} copy-done((s32[8]{0:T(128)S(1)}, s32[8]{0:T(128)}, u32[]{:S(2)}) %copy-start) | copy-done | bytes 56
  1.3 1.9 %send.1 = (s32[8]{0:T(128)S(1)}, bf16[2,8,128,128]{3,2,1,0:T(8,128)(2,1)S(1)}, bf16[128,2048]{1,0:T(8,128)(2,1)S(1)}, bf16[128,2048]{1,0:T(8,128)(2,1)S(1)}, bf1...) custom-call(s32[8]{0:T(128)S(1)} %copy-done, ...), custom_call_target="tpu_custom_call" | custom-call | flops 67108864 | bytes 4849728 | tf_op jit(solution)/shard_map/send/pallas_call | solution.py:382
  3.2 0.5 %collective-permute-start = (bf16[2,8,128,128]{3,2,1,0:T(8,128)(2,1)S(1)}, bf16[2,8,128,128]{3,2,1,0:T(8,128)(2,1)S(1)}, u32[]{:S(2)}, u32[]{:S(2)}) collective-permute-start(bf16[2,8,128,128]{3,2,1,0:T(8,128)(2,1)S(1)} %get-tuple-element.53), channel_id=1, source_target_pairs={{0,1},{1,0},{2,3},{3,2},{4,5},{5,4},{6,7},{7,6},{8,9},{9,8},{10,11... | collective-permute-start | bytes 1572872 | tf_op jit(solution)/shard_map/ppermute | solution.py:415
  3.7 1.1 %keep.1 = (bf16[2,8,128,128]{3,2,1,0:T(8,128)(2,1)S(1)}, f32[64,128]{1,0:T(8,128)S(1)}) custom-call(s32[8]{0:T(128)S(1)} %get-tuple-element.39.len_hbm, bf16[128,2048]{1,0:T(8,128)(2,1)S(1)} %get-tuple-element.36.q_ref.refs_0_, bf16[128,2048]{1,0:T(8,128)(2,1)S(1)} %get-tuple-element.37.k_ref.refs_1_, bf16[128,2048]{1,0:T(8,128)(2,1)S(1)} %get-tuple-element.38.v_ref.refs_2_, ...), custom_call_target="tpu_custom_call" | custom-call | flops 67108864 | bytes 2785312 | tf_op jit(solution)/shard_map/keep/pallas_call | solution.py:382
  4.8 0.5 %collective-permute-done.got_ref = bf16[2,8,128,128]{3,2,1,0:T(8,128)(2,1)S(1)} collective-permute-done((bf16[2,8,128,128]{3,2,1,0:T(8,128)(2,1)S(1)}, bf16[2,8,128,128]{3,2,1,0:T(8,128)(2,1)S(1)}, u32[]{:S(2)}, u32[]{:S(2)}) %collective-permute-start) | collective-permute-done | bytes 524320 | tf_op jit(solution)/shard_map/ppermute | solution.py:415
  5.2 0.2 pair.1
  5.4 4.0 %collective-permute-start.1 = (bf16[2,2,128,128]{3,2,1,0:T(8,128)(2,1)S(1)}, bf16[2,2,128,128]{3,2,1,0:T(8,128)(2,1)S(1)}, u32[]{:S(2)}, u32[]{:S(2)}) collective-permute-start(bf16[2,2,128,128]{3,2,1,0:T(8,128)(2,1)S(1)} %get-tuple-element.55), channel_id=1, source_target_pairs={{0,6},{1,7},{2,4},{3,5},{4,2},{5,3},{6,0},{7,1},{8,14},{9,15},{10,... | collective-permute-start | bytes 393224 | tf_op jit(solution)/shard_map/ppermute | solution.py:440
  9.4 0.5 %collective-permute-start.2 = (bf16[2,2,128,128]{3,2,1,0:T(8,128)(2,1)S(1)}, bf16[2,2,128,128]{3,2,1,0:T(8,128)(2,1)S(1)}, u32[]{:S(2)}, u32[]{:S(2)}) collective-permute-start(bf16[2,2,128,128]{3,2,1,0:T(8,128)(2,1)S(1)} %get-tuple-element.56), channel_id=1, source_target_pairs={{0,2},{1,3},{2,0},{3,1},{4,6},{5,7},{6,4},{7,5},{8,10},{9,11},{10,... | collective-permute-start | bytes 393224 | tf_op jit(solution)/shard_map/ppermute | solution.py:440
  9.9 0.1 collective-permute-start.3
  10.0 1.9 %local.1 = (bf16[16,128,128]{2,1,0:T(8,128)(2,1)S(1)}, bf16[16,128,128]{2,1,0:T(8,128)(2,1)S(1)}, bf16[16,128,128]{2,1,0:T(8,128)(2,1)S(1)}, bf16[16,128,128]{2,...) custom-call(s32[8]{0:T(128)S(1)} %get-tuple-element.39.len_hbm, ...), custom_call_target="tpu_custom_call" | custom-call | flops 268435456 | bytes 5832736 | tf_op jit(solution)/shard_map/local/pallas_call | solution.py:382
  11.9 1.4 %collective-permute-done.1.s1 = bf16[2,2,128,128]{3,2,1,0:T(8,128)(2,1)S(1)} collective-permute-done((bf16[2,2,128,128]{3,2,1,0:T(8,128)(2,1)S(1)}, bf16[2,2,128,128]{3,2,1,0:T(8,128)(2,1)S(1)}, u32[]{:S(2)}, u32[]{:S(2)}) %collective-permute-start.1) | collective-permute-done | bytes 131104 | tf_op jit(solution)/shard_map/ppermute | solution.py:440
  13.3 2.7 %collective-permute-done.2.s2 = bf16[2,2,128,128]{3,2,1,0:T(8,128)(2,1)S(1)} collective-permute-done((bf16[2,2,128,128]{3,2,1,0:T(8,128)(2,1)S(1)}, bf16[2,2,128,128]{3,2,1,0:T(8,128)(2,1)S(1)}, u32[]{:S(2)}, u32[]{:S(2)}) %collective-permute-start.2) | collective-permute-done | bytes 131104 | tf_op jit(solution)/shard_map/ppermute | solution.py:440
  16.0 0.2 collective-permute-done.3.s3
  16.2 0.1 totals.1
  16.3 2.7 %collective-permute-start.4 = (bf16[1,2,128,128]{3,2,1,0:T(8,128)(2,1)S(1)}, bf16[1,2,128,128]{3,2,1,0:T(8,128)(2,1)S(1)}, u32[]{:S(2)}, u32[]{:S(2)}) collective-permute-start(bf16[1,2,128,128]{3,2,1,0:T(8,128)(2,1)S(1)} %totals.1), channel_id=1, source_target_pairs={{0,8},{1,9},{2,10},{3,11},{4,12},{5,13},{6,14},{7,15},{8,0},{9,1},... | collective-permute-start | bytes 196616 | tf_op jit(solution)/shard_map/ppermute | solution.py:452
  18.9 4.0 %collective-permute-done.4.enter_ref = bf16[1,2,128,128]{3,2,1,0:T(8,128)(2,1)S(1)} collective-permute-done((bf16[1,2,128,128]{3,2,1,0:T(8,128)(2,1)S(1)}, bf16[1,2,128,128]{3,2,1,0:T(8,128)(2,1)S(1)}, u32[]{:S(2)}, u32[]{:S(2)}) %collective-permute-start.4) | collective-permute-done | bytes 65568 | tf_op jit(solution)/shard_map/ppermute | solution.py:452
  22.9 0.3 scan.1
  23.2 0.7 %collective-permute-start.5 = (bf16[2,2,128,128]{3,2,1,0:T(8,128)(2,1)S(1)}, bf16[2,2,128,128]{3,2,1,0:T(8,128)(2,1)S(1)}, u32[]{:S(2)}, u32[]{:S(2)}) collective-permute-start(bf16[2,2,128,128]{3,2,1,0:T(8,128)(2,1)S(1)} %get-tuple-element.59), channel_id=1, source_target_pairs={{0,6},{1,7},{2,4},{3,5},{4,2},{5,3},{6,0},{7,1},{8,14},{9,15},{10,... | collective-permute-start | bytes 393224 | tf_op jit(solution)/shard_map/ppermute | solution.py:440
  23.9 1.2 %collective-permute-start.6 = (bf16[2,2,128,128]{3,2,1,0:T(8,128)(2,1)S(1)}, bf16[2,2,128,128]{3,2,1,0:T(8,128)(2,1)S(1)}, u32[]{:S(2)}, u32[]{:S(2)}) collective-permute-start(bf16[2,2,128,128]{3,2,1,0:T(8,128)(2,1)S(1)} %get-tuple-element.60), channel_id=1, source_target_pairs={{0,2},{1,3},{2,0},{3,1},{4,6},{5,7},{6,4},{7,5},{8,10},{9,11},{10,... | collective-permute-start | bytes 393224 | tf_op jit(solution)/shard_map/ppermute | solution.py:440
  25.1 1.7 %collective-permute-start.7 = (bf16[2,2,128,128]{3,2,1,0:T(8,128)(2,1)S(1)}, bf16[2,2,128,128]{3,2,1,0:T(8,128)(2,1)S(1)}, u32[]{:S(2)}, u32[]{:S(2)}) collective-permute-start(bf16[2,2,128,128]{3,2,1,0:T(8,128)(2,1)S(1)} %get-tuple-element.61), channel_id=1, source_target_pairs={{0,4},{1,5},{2,6},{3,7},{4,0},{5,1},{6,2},{7,3},{8,12},{9,13},{10,... | collective-permute-start | bytes 393224 | tf_op jit(solution)/shard_map/ppermute | solution.py:440
  26.8 2.6 %collective-permute-done.5.c1 = bf16[2,2,128,128]{3,2,1,0:T(8,128)(2,1)S(1)} collective-permute-done((bf16[2,2,128,128]{3,2,1,0:T(8,128)(2,1)S(1)}, bf16[2,2,128,128]{3,2,1,0:T(8,128)(2,1)S(1)}, u32[]{:S(2)}, u32[]{:S(2)}) %collective-permute-start.5) | collective-permute-done | bytes 131104 | tf_op jit(solution)/shard_map/ppermute | solution.py:440
  29.4 0.9 %collective-permute-done.6.c2 = bf16[2,2,128,128]{3,2,1,0:T(8,128)(2,1)S(1)} collective-permute-done((bf16[2,2,128,128]{3,2,1,0:T(8,128)(2,1)S(1)}, bf16[2,2,128,128]{3,2,1,0:T(8,128)(2,1)S(1)}, u32[]{:S(2)}, u32[]{:S(2)}) %collective-permute-start.6) | collective-permute-done | bytes 131104 | tf_op jit(solution)/shard_map/ppermute | solution.py:440
  30.3 0.7 %collective-permute-done.7.c3 = bf16[2,2,128,128]{3,2,1,0:T(8,128)(2,1)S(1)} collective-permute-done((bf16[2,2,128,128]{3,2,1,0:T(8,128)(2,1)S(1)}, bf16[2,2,128,128]{3,2,1,0:T(8,128)(2,1)S(1)}, u32[]{:S(2)}, u32[]{:S(2)}) %collective-permute-start.7) | collective-permute-done | bytes 131104 | tf_op jit(solution)/shard_map/ppermute | solution.py:440
  31.0 0.4 %post.1 = (bf16[2,8,128,128]{3,2,1,0:T(8,128)(2,1)S(1)}, bf16[2,8,128,128]{3,2,1,0:T(8,128)(2,1)S(1)}) custom-call(f32[64,128]{1,0:T(8,128)S(1)} %get-tuple-element.51.coef_ref, bf16[2,2,128,128]{3,2,1,0:T(8,128)(2,1)S(1)} %get-tuple-element.58.c0, bf16[2,2,128,128]{3,2,1,0:T(8,128)(2,1)S(1)} %collective-permute-done.5.c1, ...), custom_call_target="tpu_custom_call" | custom-call | bytes 2654208 | tf_op jit(solution)/shard_map/post/pallas_call | solution.py:382
  31.4 0.1 collective-permute-start.8
  31.4 0.8 %finish_mine.1 = (bf16[128,1024]{1,0:T(8,128)(2,1)S(1)}, bf16[128,1024]{1,0:T(8,128)(2,1)S(1)}, bf16[128,1024]{1,0:T(8,128)(2,1)S(1)}, bf16[128,1024]{1,0:T(8,128)(2,1)S(1)}) custom-call(bf16[128,2048]{1,0:T(8,128)(2,1)S(1)} %get-tuple-element.36.q_ref.refs_0_, bf16[128,2048]{1,0:T(8,128)(2,1)S(1)} %get-tuple-element.37.k_ref.refs_1_, ...), custom_call_target="tpu_custom_call" | custom-call | flops 268435456 | bytes 6946816 | tf_op jit(solution)/shard_map/finish_mine/pallas_call | solution.py:382
  32.2 1.1 %collective-permute-done.8.refs_12_ = bf16[2,8,128,128]{3,2,1,0:T(8,128)(2,1)S(1)} collective-permute-done((bf16[2,8,128,128]{3,2,1,0:T(8,128)(2,1)S(1)}, bf16[2,8,128,128]{3,2,1,0:T(8,128)(2,1)S(1)}, u32[]{:S(2)}, u32[]{:S(2)}) %collective-permute-start.8) | collective-permute-done | bytes 524320 | tf_op jit(solution)/shard_map/ppermute | solution.py:459
  33.3 1.7 %finish_other.1 = (bf16[128,2048]{1,0:T(8,128)(2,1)}, bf16[128,2048]{1,0:T(8,128)(2,1)}, bf16[128,2048]{1,0:T(8,128)(2,1)}, bf16[128,2048]{1,0:T(8,128)(2,1)}) custom-call(bf16[128,2048]{1,0:T(8,128)(2,1)S(1)} %get-tuple-element.36.q_ref.refs_0_, bf16[128,2048]{1,0:T(8,128)(2,1)S(1)} %get-tuple-element.37.k_ref.refs_1_, ...), custom_call_target="tpu_custom_call" | custom-call | flops 268435456 | bytes 9043968 | tf_op jit(solution)/shard_map/finish_other/pallas_call | solution.py:382
Async XLA Ops:
  0.6 0.7 %copy-start = (s32[8]{0:T(128)S(1)}, s32[8]{0:T(128)}, u32[]{:S(2)}) copy-start(s32[8]{0:T(128)} %len_hbm.1) | copy-start | bytes 100
  3.2 2.1 %collective-permute-start = (bf16[2,8,128,128]{3,2,1,0:T(8,128)(2,1)S(1)}, bf16[2,8,128,128]{3,2,1,0:T(8,128)(2,1)S(1)}, u32[]{:S(2)}, u32[]{:S(2)}) collective-permute-start(bf16[2,8,128,128]{3,2,1,0:T(8,128)(2,1)S(1)} %get-tuple-element.53), channel_id=1, source_target_pairs={{0,1},{1,0},{2,3},{3,2},{4,5},{5,4},{6,7},{7,6},{8,9},{9,8},{10,11... | collective-permute-start | bytes 1572872 | tf_op jit(solution)/shard_map/ppermute | solution.py:415
  5.4 7.9 %collective-permute-start.1 = (bf16[2,2,128,128]{3,2,1,0:T(8,128)(2,1)S(1)}, bf16[2,2,128,128]{3,2,1,0:T(8,128)(2,1)S(1)}, u32[]{:S(2)}, u32[]{:S(2)}) collective-permute-start(bf16[2,2,128,128]{3,2,1,0:T(8,128)(2,1)S(1)} %get-tuple-element.55), channel_id=1, source_target_pairs={{0,6},{1,7},{2,4},{3,5},{4,2},{5,3},{6,0},{7,1},{8,14},{9,15},{10,... | collective-permute-start | bytes 393224 | tf_op jit(solution)/shard_map/ppermute | solution.py:440
  9.4 6.6 %collective-permute-start.2 = (bf16[2,2,128,128]{3,2,1,0:T(8,128)(2,1)S(1)}, bf16[2,2,128,128]{3,2,1,0:T(8,128)(2,1)S(1)}, u32[]{:S(2)}, u32[]{:S(2)}) collective-permute-start(bf16[2,2,128,128]{3,2,1,0:T(8,128)(2,1)S(1)} %get-tuple-element.56), channel_id=1, source_target_pairs={{0,2},{1,3},{2,0},{3,1},{4,6},{5,7},{6,4},{7,5},{8,10},{9,11},{10,... | collective-permute-start | bytes 393224 | tf_op jit(solution)/shard_map/ppermute | solution.py:440
  9.9 6.3 %collective-permute-start.3 = (bf16[2,2,128,128]{3,2,1,0:T(8,128)(2,1)S(1)}, bf16[2,2,128,128]{3,2,1,0:T(8,128)(2,1)S(1)}, u32[]{:S(2)}, u32[]{:S(2)}) collective-permute-start(bf16[2,2,128,128]{3,2,1,0:T(8,128)(2,1)S(1)} %get-tuple-element.57), channel_id=1, source_target_pairs={{0,4},{1,5},{2,6},{3,7},{4,0},{5,1},{6,2},{7,3},{8,12},{9,13},{10,... | collective-permute-start | bytes 393224 | tf_op jit(solution)/shard_map/ppermute | solution.py:440
  16.3 6.6 %collective-permute-start.4 = (bf16[1,2,128,128]{3,2,1,0:T(8,128)(2,1)S(1)}, bf16[1,2,128,128]{3,2,1,0:T(8,128)(2,1)S(1)}, u32[]{:S(2)}, u32[]{:S(2)}) collective-permute-start(bf16[1,2,128,128]{3,2,1,0:T(8,128)(2,1)S(1)} %totals.1), channel_id=1, source_target_pairs={{0,8},{1,9},{2,10},{3,11},{4,12},{5,13},{6,14},{7,15},{8,0},{9,1},... | collective-permute-start | bytes 196616 | tf_op jit(solution)/shard_map/ppermute | solution.py:452
  23.2 6.2 %collective-permute-start.5 = (bf16[2,2,128,128]{3,2,1,0:T(8,128)(2,1)S(1)}, bf16[2,2,128,128]{3,2,1,0:T(8,128)(2,1)S(1)}, u32[]{:S(2)}, u32[]{:S(2)}) collective-permute-start(bf16[2,2,128,128]{3,2,1,0:T(8,128)(2,1)S(1)} %get-tuple-element.59), channel_id=1, source_target_pairs={{0,6},{1,7},{2,4},{3,5},{4,2},{5,3},{6,0},{7,1},{8,14},{9,15},{10,... | collective-permute-start | bytes 393224 | tf_op jit(solution)/shard_map/ppermute | solution.py:440
  23.9 6.4 %collective-permute-start.6 = (bf16[2,2,128,128]{3,2,1,0:T(8,128)(2,1)S(1)}, bf16[2,2,128,128]{3,2,1,0:T(8,128)(2,1)S(1)}, u32[]{:S(2)}, u32[]{:S(2)}) collective-permute-start(bf16[2,2,128,128]{3,2,1,0:T(8,128)(2,1)S(1)} %get-tuple-element.60), channel_id=1, source_target_pairs={{0,2},{1,3},{2,0},{3,1},{4,6},{5,7},{6,4},{7,5},{8,10},{9,11},{10,... | collective-permute-start | bytes 393224 | tf_op jit(solution)/shard_map/ppermute | solution.py:440
  25.1 5.9 %collective-permute-start.7 = (bf16[2,2,128,128]{3,2,1,0:T(8,128)(2,1)S(1)}, bf16[2,2,128,128]{3,2,1,0:T(8,128)(2,1)S(1)}, u32[]{:S(2)}, u32[]{:S(2)}) collective-permute-start(bf16[2,2,128,128]{3,2,1,0:T(8,128)(2,1)S(1)} %get-tuple-element.61), channel_id=1, source_target_pairs={{0,4},{1,5},{2,6},{3,7},{4,0},{5,1},{6,2},{7,3},{8,12},{9,13},{10,... | collective-permute-start | bytes 393224 | tf_op jit(solution)/shard_map/ppermute | solution.py:440
  31.4 2.0 %collective-permute-start.8 = (bf16[2,8,128,128]{3,2,1,0:T(8,128)(2,1)S(1)}, bf16[2,8,128,128]{3,2,1,0:T(8,128)(2,1)S(1)}, u32[]{:S(2)}, u32[]{:S(2)}) collective-permute-start(bf16[2,8,128,128]{3,2,1,0:T(8,128)(2,1)S(1)} %get-tuple-element.62), channel_id=1, source_target_pairs={{0,1},{1,0},{2,3},{3,2},{4,5},{5,4},{6,7},{7,6},{8,9},{9,8},{10,11... | collective-permute-start | bytes 1572872 | tf_op jit(solution)/shard_map/ppermute | solution.py:459

commit v4 on v3

--- a/solution.py
+++ b/solution.py
@@ -8,18 +8,13 @@
 from jax.sharding import PartitionSpec as P
 
 HD = 128
-PAIRS = 4
-PARTNERS = (0, 3, 1, 2)
-TEAM = 2 * PAIRS
 F32 = jnp.float32
 BF16 = jnp.bfloat16
 
 KEEP_F, GOT_F, KEEP_B, GOT_B = 0, 1, 2, 3
-TOT_F, TOT_B = 4, 8
-MIX_F, MIX_B = 12, 28
-ENTER_F, ENTER_B = 44, 48
-MINE_F, MINE_B, THEIRS_F, THEIRS_B = 52, 54, 56, 58
-COEFS = 64
+FAR_F, FAR_B, NEXT_F, NEXT_B = 4, 5, 6, 7
+MINE_F, MINE_B, THEIRS_F, THEIRS_B = 8, 10, 12, 14
+COEFS = 16
 
 
 def doc_starts(len_ref):
@@ -135,63 +130,46 @@
     len_pass.wait()
 
 
-def coefficients(starts, rows, n, coef_ref):
+def coefficients(starts, rows, coef_ref):
     me = lax.axis_index("seq")
-    core = lax.rem(me, 2)
-    pair = lax.rem(me, TEAM) // 2
-    base = me - lax.rem(me, TEAM)
-    teams = n // TEAM
-    one, zero = jnp.int32(1), jnp.int32(0)
+    odd = lax.rem(me, 2)
+    even = 1 - odd
+    low = (me - odd) * rows
 
     def put(row, flag):
         coef_ref[pl.ds(row, 1), :] = jnp.full((1, HD), flag.astype(F32), F32)
 
-    def both(block):
-        return starts_before(starts, block * rows), starts_before(starts, block * rows + 1)
-
-    def same(a, b):
+    def none(begin, end):
+        a, b = starts_before(starts, low + begin * rows), starts_before(starts, low + end * rows)
         return (a == b).astype(jnp.int32)
 
-    team_low, team_high = both(base), both(base + TEAM)
-    pairs = [pair ^ d for d in PARTNERS]
-    low = [both(base + 2 * p) for p in pairs]
-    high = [both(base + 2 * p + 2) for p in pairs]
-    middle = both(me - core + 1)
-    open_0 = same(low[0][0], middle[0])
-    open_1 = same(middle[0], high[0][0])
-    close_0 = same(low[0][1], middle[1])
-    close_1 = same(middle[1], high[0][1])
-    odd = core
-    even = one - core
-    put(KEEP_F, jnp.where(odd == 1, one, open_1))
-    put(GOT_F, jnp.where(odd == 1, open_1, one))
-    put(KEEP_B, jnp.where(odd == 1, close_0, one))
-    put(GOT_B, jnp.where(odd == 1, one, close_0))
-    is_low = (base == 0).astype(jnp.int32)
-    is_high = (base == n - TEAM).astype(jnp.int32)
-    for d in range(PAIRS):
-        tot_f = same(high[d][0], team_high[0])
-        tot_b = same(team_low[1], low[d][1])
-        put(TOT_F + d, tot_f * is_low if teams == 2 else tot_f)
-        put(TOT_B + d, tot_b * is_high if teams == 2 else tot_b)
-        put(ENTER_F + d, same(team_low[0], low[d][0]) * (one - is_low))
-        put(ENTER_B + d, same(high[d][1], team_high[1]) * (one - is_high))
-        for s in range(PAIRS):
-            before = (pairs[s] < pairs[d]).astype(jnp.int32)
-            after = (pairs[s] > pairs[d]).astype(jnp.int32)
-            put(MIX_F + d * PAIRS + s, before * same(high[s][0], low[d][0]))
-            put(MIX_B + d * PAIRS + s, after * same(high[d][1], low[s][1]))
-    put(MINE_F, jnp.where(odd == 1, open_0, one))
+    def none_after(begin, end):
+        a, b = starts_before(starts, low + begin * rows + 1), starts_before(starts, low + end * rows + 1)
+        return (a == b).astype(jnp.int32)
+
+    def either(if_odd, if_even):
+        return jnp.where(odd == 1, if_odd, if_even)
+
+    one = jnp.int32(1)
+    put(KEEP_F, either(one, none(1, 2)))
+    put(GOT_F, either(none(1, 2), one))
+    put(KEEP_B, either(none_after(0, 1), one))
+    put(GOT_B, either(one, none_after(0, 1)))
+    put(FAR_F, none(-2, 2))
+    put(FAR_B, none_after(0, 4))
+    put(NEXT_F, none(-2, 0))
+    put(NEXT_B, none_after(2, 4))
+    put(MINE_F, either(none(0, 1), one))
     put(MINE_F + 1, odd)
-    put(MINE_B, jnp.where(odd == 1, one, close_1))
+    put(MINE_B, either(one, none_after(1, 2)))
     put(MINE_B + 1, even)
-    put(THEIRS_F, jnp.where(odd == 1, one, open_0))
+    put(THEIRS_F, either(one, none(0, 1)))
     put(THEIRS_F + 1, even)
-    put(THEIRS_B, jnp.where(odd == 1, close_1, one))
+    put(THEIRS_B, either(none_after(1, 2), one))
     put(THEIRS_B + 1, odd)
 
 
-def keep_kernel(total, len_hbm, q_ref, k_ref, v_ref, g_ref, rows_ref, root_ref, out_ref, coef_ref, len_ref, len_sem):
+def keep_kernel(len_hbm, q_ref, k_ref, v_ref, g_ref, rows_ref, root_ref, out_ref, coef_ref, len_ref, len_sem):
     rows = q_ref.shape[0]
     half = out_ref.shape[1] * HD
     offset = lax.rem(lax.axis_index("seq"), 2) * half
@@ -206,7 +184,7 @@
         out_ref[0, h] = tail
         out_ref[1, h] = head
     len_copy.wait()
-    coefficients(doc_starts(len_ref), rows, total // rows, coef_ref)
+    coefficients(doc_starts(len_ref), rows, coef_ref)
 
 
 def local_kernel(
@@ -259,60 +237,46 @@
 
 
 def pair_kernel(coef_ref, keep_ref, got_ref, *out_refs):
-    per = out_refs[0].shape[1]
-    pair = lax.rem(lax.axis_index("seq"), TEAM) // 2
+    chunks = len(out_refs) // 2
     for kind, (a, b) in enumerate(((KEEP_F, GOT_F), (KEEP_B, GOT_B))):
         ca, cb = coef(coef_ref, a), coef(coef_ref, b)
-        for d, out_ref in enumerate(out_refs):
+        for c in range(chunks):
+            out_ref = out_refs[kind * chunks + c]
+            per = out_ref.shape[0]
             for i in range(per):
-                h = (pair ^ PARTNERS[d]) * per + i
+                h = c * per + i
                 both = keep_ref[kind, h].astype(F32) * ca + got_ref[kind, h].astype(F32) * cb
-                out_ref[kind, i] = both.astype(BF16)
-
-
-def totals_kernel(coef_ref, s0, s1, s2, s3, after_ref, out_ref):
+                out_ref[i] = both.astype(BF16)
+
+
+def far_kernel(row, chunks, coef_ref, own_ref, far_ref, *refs):
+    before, out_ref, all_ref = refs[:chunks], refs[chunks], refs[-1]
+    factor = coef(coef_ref, row)
+    per = out_ref.shape[0]
+    for i in range(per):
+        both = (own_ref[i].astype(F32) + far_ref[i].astype(F32) * factor).astype(BF16)
+        out_ref[i] = both
+        if before:
+            all_ref[chunks * per + i] = both
+    for c, ref in enumerate(before):
+        for i in range(per):
+            all_ref[c * per + i] = ref[i]
+
+
+def post_kernel(coef_ref, keep_ref, got_ref, after_ref, *refs):
     del after_ref
-    sums = (s0, s1, s2, s3)
-    for i in range(out_ref.shape[1]):
-        fwd, bwd = (
-            sum(sums[d][kind, i].astype(F32) * coef(coef_ref, row + d) for d in range(PAIRS))
-            for kind, row in enumerate((TOT_F, TOT_B))
-        )
-        if out_ref.shape[0] == 1:
-            out_ref[0, i] = (fwd + bwd).astype(BF16)
-        else:
-            out_ref[0, i] = fwd.astype(BF16)
-            out_ref[1, i] = bwd.astype(BF16)
-
-
-def scan_kernel(coef_ref, s0, s1, s2, s3, enter_ref, *out_refs):
-    sums = (s0, s1, s2, s3)
-    last = enter_ref.shape[0] - 1
-    for kind, (mix, enter) in enumerate(((MIX_F, ENTER_F), (MIX_B, ENTER_B))):
-        for i in range(out_refs[0].shape[1]):
-            came = enter_ref[min(kind, last), i].astype(F32)
-            parts = [s[kind, i].astype(F32) for s in sums]
-            for d, out_ref in enumerate(out_refs):
-                total = came * coef(coef_ref, enter + d)
-                for s in range(PAIRS):
-                    if s != d:
-                        total = total + parts[s] * coef(coef_ref, mix + d * PAIRS + s)
-                out_ref[kind, i] = total.astype(BF16)
-
-
-def post_kernel(coef_ref, c0, c1, c2, c3, keep_ref, got_ref, mine_ref, theirs_ref):
-    per = c0.shape[1]
-    pair = lax.rem(lax.axis_index("seq"), TEAM) // 2
-    for kind in range(2):
-        m, t = (MINE_F, THEIRS_F) if kind == 0 else (MINE_B, THEIRS_B)
+    ins, (mine_ref, theirs_ref) = refs[:-2], refs[-2:]
+    chunks = len(ins) // 2 - 1
+    for kind, (far, m, t) in enumerate(((NEXT_F, MINE_F, THEIRS_F), (NEXT_B, MINE_B, THEIRS_B))):
+        near_refs, far_ref = ins[kind * (chunks + 1) :][:chunks], ins[kind * (chunks + 1) + chunks]
+        factor = coef(coef_ref, far)
         m0, m1 = coef(coef_ref, m), coef(coef_ref, m + 1)
         t0, t1 = coef(coef_ref, t), coef(coef_ref, t + 1)
-        for d, c_ref in enumerate((c0, c1, c2, c3)):
-            for i in range(per):
-                h = (pair ^ PARTNERS[d]) * per + i
-                came = c_ref[kind, i].astype(F32)
-                theirs_ref[kind, h] = (came * t0 + keep_ref[kind, h].astype(F32) * t1).astype(BF16)
-                mine_ref[kind, h] = (came * m0 + got_ref[kind, h].astype(F32) * m1).astype(BF16)
+        per = near_refs[0].shape[0]
+        for h in range(chunks * per):
+            came = near_refs[h // per][h % per].astype(F32) + far_ref[h].astype(F32) * factor
+            theirs_ref[kind, h] = (came * t0 + keep_ref[kind, h].astype(F32) * t1).astype(BF16)
+            mine_ref[kind, h] = (came * m0 + got_ref[kind, h].astype(F32) * m1).astype(BF16)
 
 
 def finish_kernel(other, chunks, *refs):
@@ -368,9 +332,7 @@
     n = lax.axis_size("seq")
     heads = width // HD
     total = rows * n
-    teams = n // TEAM
     half = heads // 2
-    per = half // PAIRS
     vmem = pl.BlockSpec(memory_space=pltpu.VMEM)
     hbm = pl.BlockSpec(memory_space=pltpu.HBM)
 
@@ -414,7 +376,7 @@
     swap = [(i, i ^ 1) for i in range(n)]
     got = lax.ppermute(send, "seq", swap)
     keep, table = call(
-        functools.partial(keep_kernel, total),
+        keep_kernel,
         "keep",
         [states, shape(COEFS, HD, dtype=F32)],
         (doc_lengths, queries, keys, values, grad_out, row_masks, root),
@@ -432,29 +394,38 @@
         flops=4 * heads * product,
         scratch=lengths,
     )
-    owned = shape(2, per, HD, HD)
-    sums = call(pair_kernel, "pair", [owned] * PAIRS, (table, keep, got), [vmem] * 3)
-
-    def trade(parts):
-        return [parts[0]] + [
-            lax.ppermute(parts[d], "seq", [(i, i ^ (2 * PARTNERS[d])) for i in range(n)])
-            for d in range(1, PAIRS)
-        ]
-
-    sums = trade(sums)
-    kinds = 1 if teams == 2 else 2
-    (edge,) = call(
-        totals_kernel, "totals", [shape(kinds, per, HD, HD)], (table, *sums, masks), [vmem] * 6
-    )
-    up = [(i, i + TEAM) for i in range(n - TEAM)]
-    down = [(j, i) for i, j in up]
-    if kinds == 1:
-        enter = lax.ppermute(edge, "seq", up + down)
-    else:
-        enter = jnp.stack([lax.ppermute(edge[0], "seq", up), lax.ppermute(edge[1], "seq", down)])
-    entering = trade(call(scan_kernel, "scan", [owned] * PAIRS, (table, *sums, enter), [vmem] * 6))
+    parts = 2
+    some = shape(half // parts, HD, HD)
+    sums = call(pair_kernel, "pair", [some] * (2 * parts), (table, keep, got), [vmem] * 3)
+
+    def pass_on(x, chips):
+        step = 2 * chips
+        return lax.ppermute(x, "seq", [(i, i + step) for i in range(n) if 0 <= i + step < n])
+
+    far = [[pass_on(sums[kind * parts + c], 2 - 4 * kind) for kind in range(2)] for c in range(parts)]
+    near, whole = [[], []], [None, None]
+    for c in range(parts):
+        for kind, row in enumerate((FAR_F, FAR_B)):
+            last = c == parts - 1
+            before = near[kind] if last else []
+            added = call(
+                functools.partial(far_kernel, row, len(before)),
+                "far",
+                [some] + [shape(half, HD, HD)] * len(before[:1]),
+                (table, sums[kind * parts + c], far[c][kind], *before),
+                [vmem] * (3 + len(before)),
+            )
+            near[kind].append(added[0])
+            whole[kind] = added[-1]
+    came = [[pass_on(x, 1 - 2 * kind) for x in near[kind]] for kind in range(2)]
+    for kind in range(2):
+        came[kind].append(pass_on(whole[kind], 2 - 4 * kind))
     mine, theirs = call(
-        post_kernel, "post", [states] * 2, (table, *entering, keep, got), [vmem] * 7
+        post_kernel,
+        "post",
+        [states] * 2,
+        (table, keep, got, masks, *came[0], *came[1]),
+        [vmem] * (4 + 2 * (parts + 1)),
     )
     other = lax.ppermute(theirs, "seq", swap)
     w, wt, dw, dwt, kt, qt, scaled = local

time: 35.2 us -> 45.9 us (1.30)
  starting transfers between devices: 11.4 us -> 29.6 us
  waiting for transfers between devices: 14 us -> 6.28 us
    ppermute x7 -> x10, starting transfers between devices: 10.8 us -> 29 us  [pass_on(): lax.ppermute(x, 'seq', [(i, i + step) for i in range(n) if 0 <= i + step...]
    ppermute x7 -> x10, waiting for transfers between devices: 12.4 us -> 4.5 us  [pass_on(): lax.ppermute(x, 'seq', [(i, i + step) for i in range(n) if 0 <= i + step...]
    pallas_call x9 -> x11, Pallas kernels: 8.2 us -> 7.89 us  [call(): pl.pallas_call(kernel, in_specs=specs, out_specs=out_specs or [vmem] * le...]
  transfers between devices with their start and end apart: 9 -> 12, of which waited for: 9 -> 3; matrix products, arithmetic and copies ran while one was open for 0% -> 0% of each run, Pallas kernels for 11% -> 8%
where the time goes in v4:
time: 45.9 us; the launch traced here: 45.3 us
  starting transfers between devices  29.6 us (64%)
  Pallas kernels  7.89 us (17%)
  waiting for transfers between devices  6.28 us (14%)
  between operations  0.85 us (2%)
  local copies, waits for them, and re-layouts  0.65 us (1%)
    ppermute x10, starting transfers between devices, pass_on(): lax.ppermute(x, 'seq', [(i, i + step) for i in range(n) if 0 <= i + step...  29 us
    pallas_call x11, Pallas kernels, call(): pl.pallas_call(kernel, in_specs=specs, out_specs=out_specs or [vmem] * le...  7.89 us
    ppermute x10, waiting for transfers between devices, pass_on(): lax.ppermute(x, 'seq', [(i, i + step) for i in range(n) if 0 <= i + step...  4.5 us
    ppermute x1, waiting for transfers between devices, per_device(): other = lax.ppermute(theirs, 'seq', swap)  1.14 us
  transfers between devices with their start and end apart: 12, of which 3 were waited for; matrix products, arithmetic and copies ran while one was open for 0% of the time, Pallas kernels for 8%

profile of v4, /device:TPU:0, one launch (start us, length us, event | category | flops | bytes accessed | tf_op | source)
XLA Modules:
  0.0 45.3 jit_solution(17028154221259923653)
XLA Ops:
  0.6 0.6 %copy-done = s32[8]{0:T(128)S(1)} copy-done((s32[8]{0:T(128)S(1)}, s32[8]{0:T(128)}, u32[]{:S(2)}) %copy-start) | copy-done | bytes 56
  1.3 1.9 %send.1 = (s32[8]{0:T(128)S(1)}, bf16[2,8,128,128]{3,2,1,0:T(8,128)(2,1)S(1)}, bf16[128,2048]{1,0:T(8,128)(2,1)S(1)}, bf16[128,2048]{1,0:T(8,128)(2,1)S(1)}, bf1...) custom-call(s32[8]{0:T(128)S(1)} %copy-done, ...), custom_call_target="tpu_custom_call" | custom-call | flops 67108864 | bytes 4849728 | tf_op jit(solution)/shard_map/send/pallas_call | solution.py:344
  3.2 0.5 %collective-permute-start = (bf16[2,8,128,128]{3,2,1,0:T(8,128)(2,1)S(1)}, bf16[2,8,128,128]{3,2,1,0:T(8,128)(2,1)S(1)}, u32[]{:S(2)}, u32[]{:S(2)}) collective-permute-start(bf16[2,8,128,128]{3,2,1,0:T(8,128)(2,1)S(1)} %get-tuple-element.53), channel_id=1, source_target_pairs={{0,1},{1,0},{2,3},{3,2},{4,5},{5,4},{6,7},{7,6},{8,9},{9,8},{10,11... | collective-permute-start | bytes 1572872 | tf_op jit(solution)/shard_map/ppermute | solution.py:377
  3.7 0.9 %keep.1 = (bf16[2,8,128,128]{3,2,1,0:T(8,128)(2,1)S(1)}, f32[16,128]{1,0:T(8,128)S(1)}) custom-call(s32[8]{0:T(128)S(1)} %get-tuple-element.39.len_hbm, bf16[128,2048]{1,0:T(8,128)(2,1)S(1)} %get-tuple-element.36.q_ref.refs_0_, bf16[128,2048]{1,0:T(8,128)(2,1)S(1)} %get-tuple-element.37.k_ref.refs_1_, bf16[128,2048]{1,0:T(8,128)(2,1)S(1)} %get-tuple-element.38.v_ref.refs_2_, ...), custom_call_target="tpu_custom_call" | custom-call | flops 67108864 | bytes 2760736 | tf_op jit(solution)/shard_map/keep/pallas_call | solution.py:344
  4.6 0.6 %collective-permute-done.got_ref = bf16[2,8,128,128]{3,2,1,0:T(8,128)(2,1)S(1)} collective-permute-done((bf16[2,8,128,128]{3,2,1,0:T(8,128)(2,1)S(1)}, bf16[2,8,128,128]{3,2,1,0:T(8,128)(2,1)S(1)}, u32[]{:S(2)}, u32[]{:S(2)}) %collective-permute-start) | collective-permute-done | bytes 524320 | tf_op jit(solution)/shard_map/ppermute | solution.py:377
  5.2 0.2 pair.1
  5.4 4.9 %collective-permute-start.1 = (bf16[4,128,128]{2,1,0:T(8,128)(2,1)S(1)}, bf16[4,128,128]{2,1,0:T(8,128)(2,1)S(1)}, u32[]{:S(2)}, u32[]{:S(2)}) collective-permute-start(bf16[4,128,128]{2,1,0:T(8,128)(2,1)S(1)} %get-tuple-element.54.own_ref), channel_id=1, source_target_pairs={{0,4},{1,5},{2,6},{3,7},{4,8},{5,9},{6,10},{7,11},{8,12},{9,13},{1... | collective-permute-start | bytes 393224 | tf_op jit(solution)/shard_map/ppermute | solution.py:403
  10.3 1.3 %collective-permute-start.6 = (bf16[4,128,128]{2,1,0:T(8,128)(2,1)S(1)}, bf16[4,128,128]{2,1,0:T(8,128)(2,1)S(1)}, u32[]{:S(2)}, u32[]{:S(2)}) collective-permute-start(bf16[4,128,128]{2,1,0:T(8,128)(2,1)S(1)} %get-tuple-element.58.own_ref), channel_id=1, source_target_pairs={{4,0},{5,1},{6,2},{7,3},{8,4},{9,5},{10,6},{11,7},{12,8},{13,9},{1... | collective-permute-start | bytes 393224 | tf_op jit(solution)/shard_map/ppermute | solution.py:403
  11.6 1.3 %collective-permute-start.8 = (bf16[4,128,128]{2,1,0:T(8,128)(2,1)S(1)}, bf16[4,128,128]{2,1,0:T(8,128)(2,1)S(1)}, u32[]{:S(2)}, u32[]{:S(2)}) collective-permute-start(bf16[4,128,128]{2,1,0:T(8,128)(2,1)S(1)} %get-tuple-element.59.own_ref), channel_id=1, source_target_pairs={{4,0},{5,1},{6,2},{7,3},{8,4},{9,5},{10,6},{11,7},{12,8},{13,9},{1... | collective-permute-start | bytes 393224 | tf_op jit(solution)/shard_map/ppermute | solution.py:403
  12.9 5.2 %collective-permute-start.3 = (bf16[4,128,128]{2,1,0:T(8,128)(2,1)S(1)}, bf16[4,128,128]{2,1,0:T(8,128)(2,1)S(1)}, u32[]{:S(2)}, u32[]{:S(2)}) collective-permute-start(bf16[4,128,128]{2,1,0:T(8,128)(2,1)S(1)} %get-tuple-element.55.own_ref), channel_id=1, source_target_pairs={{0,4},{1,5},{2,6},{3,7},{4,8},{5,9},{6,10},{7,11},{8,12},{9,13},{1... | collective-permute-start | bytes 393224 | tf_op jit(solution)/shard_map/ppermute | solution.py:403
  18.1 0.0 collective-permute-done.1.far_ref
  18.1 3.4 %collective-permute-start.2 = (bf16[4,128,128]{2,1,0:T(8,128)(2,1)S(1)}, bf16[4,128,128]{2,1,0:T(8,128)(2,1)S(1)}, u32[]{:S(2)}, u32[]{:S(2)}) collective-permute-start(bf16[4,128,128]{2,1,0:T(8,128)(2,1)S(1)} %far.4.refs_0_), channel_id=1, source_target_pairs={{0,2},{1,3},{2,4},{3,5},{4,6},{5,7},{6,8},{7,9},{8,10},{9,11},{10,... | collective-permute-start | bytes 393224 | tf_op jit(solution)/shard_map/ppermute | solution.py:403
  21.6 0.0 collective-permute-done.6.far_ref
  21.6 0.0 collective-permute-done.8.far_ref
  21.7 1.3 %collective-permute-start.10 = (bf16[8,128,128]{2,1,0:T(8,128)(2,1)S(1)}, bf16[8,128,128]{2,1,0:T(8,128)(2,1)S(1)}, u32[]{:S(2)}, u32[]{:S(2)}) collective-permute-start(bf16[8,128,128]{2,1,0:T(8,128)(2,1)S(1)} %get-tuple-element.61), channel_id=1, source_target_pairs={{4,0},{5,1},{6,2},{7,3},{8,4},{9,5},{10,6},{11,7},{12,8},{13,9},{1... | collective-permute-start | bytes 786440 | tf_op jit(solution)/shard_map/ppermute | solution.py:403
  23.0 0.0 collective-permute-done.3.far_ref
  23.1 4.6 %collective-permute-start.5 = (bf16[8,128,128]{2,1,0:T(8,128)(2,1)S(1)}, bf16[8,128,128]{2,1,0:T(8,128)(2,1)S(1)}, u32[]{:S(2)}, u32[]{:S(2)}) collective-permute-start(bf16[8,128,128]{2,1,0:T(8,128)(2,1)S(1)} %get-tuple-element.57), channel_id=1, source_target_pairs={{0,4},{1,5},{2,6},{3,7},{4,8},{5,9},{6,10},{7,11},{8,12},{9,13},{1... | collective-permute-start | bytes 786440 | tf_op jit(solution)/shard_map/ppermute | solution.py:403
  27.6 1.3 %collective-permute-start.7 = (bf16[4,128,128]{2,1,0:T(8,128)(2,1)S(1)}, bf16[4,128,128]{2,1,0:T(8,128)(2,1)S(1)}, u32[]{:S(2)}, u32[]{:S(2)}) collective-permute-start(bf16[4,128,128]{2,1,0:T(8,128)(2,1)S(1)} %far.6.refs_0_), channel_id=1, source_target_pairs={{2,0},{3,1},{4,2},{5,3},{6,4},{7,5},{8,6},{9,7},{10,8},{11,9},{12,... | collective-permute-start | bytes 393224 | tf_op jit(solution)/shard_map/ppermute | solution.py:403
  28.9 4.6 %collective-permute-start.4 = (bf16[4,128,128]{2,1,0:T(8,128)(2,1)S(1)}, bf16[4,128,128]{2,1,0:T(8,128)(2,1)S(1)}, u32[]{:S(2)}, u32[]{:S(2)}) collective-permute-start(bf16[4,128,128]{2,1,0:T(8,128)(2,1)S(1)} %get-tuple-element.56), channel_id=1, source_target_pairs={{0,2},{1,3},{2,4},{3,5},{4,6},{5,7},{6,8},{7,9},{8,10},{9,11},{10,... | collective-permute-start | bytes 393224 | tf_op jit(solution)/shard_map/ppermute | solution.py:403
  33.5 0.0 collective-permute-done.2.refs_0_
  33.5 1.3 %collective-permute-start.9 = (bf16[4,128,128]{2,1,0:T(8,128)(2,1)S(1)}, bf16[4,128,128]{2,1,0:T(8,128)(2,1)S(1)}, u32[]{:S(2)}, u32[]{:S(2)}) collective-permute-start(bf16[4,128,128]{2,1,0:T(8,128)(2,1)S(1)} %get-tuple-element.60), channel_id=1, source_target_pairs={{2,0},{3,1},{4,2},{5,3},{6,4},{7,5},{8,6},{9,7},{10,8},{11,9},{12,... | collective-permute-start | bytes 393224 | tf_op jit(solution)/shard_map/ppermute | solution.py:403
  34.8 1.9 %local.1 = (bf16[16,128,128]{2,1,0:T(8,128)(2,1)S(1)}, bf16[16,128,128]{2,1,0:T(8,128)(2,1)S(1)}, bf16[16,128,128]{2,1,0:T(8,128)(2,1)S(1)}, bf16[16,128,128]{2,...) custom-call(s32[8]{0:T(128)S(1)} %get-tuple-element.39.len_hbm, ...), custom_call_target="tpu_custom_call" | custom-call | flops 268435456 | bytes 5832736 | tf_op jit(solution)/shard_map/local/pallas_call | solution.py:344
  36.7 0.0 collective-permute-done.4.refs_1_
  36.7 0.0 collective-permute-done.7.refs_3_
  36.7 4.5 %collective-permute-done.9.refs_4_ = bf16[4,128,128]{2,1,0:T(8,128)(2,1)S(1)} collective-permute-done((bf16[4,128,128]{2,1,0:T(8,128)(2,1)S(1)}, bf16[4,128,128]{2,1,0:T(8,128)(2,1)S(1)}, u32[]{:S(2)}, u32[]{:S(2)}) %collective-permute-start.9) | collective-permute-done | bytes 131104 | tf_op jit(solution)/shard_map/ppermute | solution.py:403
  41.2 0.0 collective-permute-done.10.refs_5_
  41.2 0.0 collective-permute-done.5.refs_2_
  41.2 0.5 %post.1 = (bf16[2,8,128,128]{3,2,1,0:T(8,128)(2,1)S(1)}, bf16[2,8,128,128]{3,2,1,0:T(8,128)(2,1)S(1)}) custom-call(f32[16,128]{1,0:T(8,128)S(1)} %get-tuple-element.51.coef_ref, bf16[2,8,128,128]{3,2,1,0:T(8,128)(2,1)S(1)} %get-tuple-element.52.keep_ref, bf16[2,8,128,128]{3,2,1,0:T(8,128)(2,1)S(1)} %collective-permute-done.got_ref, ...), custom_call_target="tpu_custom_call" | custom-call | bytes 3219456 | tf_op jit(solution)/shard_map/post/pallas_call | solution.py:344
  41.7 0.1 collective-permute-start.11
  41.7 0.8 %finish_mine.1 = (bf16[128,1024]{1,0:T(8,128)(2,1)S(1)}, bf16[128,1024]{1,0:T(8,128)(2,1)S(1)}, bf16[128,1024]{1,0:T(8,128)(2,1)S(1)}, bf16[128,1024]{1,0:T(8,128)(2,1)S(1)}) custom-call(bf16[128,2048]{1,0:T(8,128)(2,1)S(1)} %get-tuple-element.36.q_ref.refs_0_, bf16[128,2048]{1,0:T(8,128)(2,1)S(1)} %get-tuple-element.37.k_ref.refs_1_, ...), custom_call_target="tpu_custom_call" | custom-call | flops 268435456 | bytes 6946816 | tf_op jit(solution)/shard_map/finish_mine/pallas_call | solution.py:344
  42.5 1.1 %collective-permute-done.11.refs_12_ = bf16[2,8,128,128]{3,2,1,0:T(8,128)(2,1)S(1)} collective-permute-done((bf16[2,8,128,128]{3,2,1,0:T(8,128)(2,1)S(1)}, bf16[2,8,128,128]{3,2,1,0:T(8,128)(2,1)S(1)}, u32[]{:S(2)}, u32[]{:S(2)}) %collective-permute-start.11) | collective-permute-done | bytes 524320 | tf_op jit(solution)/shard_map/ppermute | solution.py:430
  43.6 1.7 %finish_other.1 = (bf16[128,2048]{1,0:T(8,128)(2,1)}, bf16[128,2048]{1,0:T(8,128)(2,1)}, bf16[128,2048]{1,0:T(8,128)(2,1)}, bf16[128,2048]{1,0:T(8,128)(2,1)}) custom-call(bf16[128,2048]{1,0:T(8,128)(2,1)S(1)} %get-tuple-element.36.q_ref.refs_0_, bf16[128,2048]{1,0:T(8,128)(2,1)S(1)} %get-tuple-element.37.k_ref.refs_1_, ...), custom_call_target="tpu_custom_call" | custom-call | flops 268435456 | bytes 9043968 | tf_op jit(solution)/shard_map/finish_other/pallas_call | solution.py:344
  (5 shorter events, 0.2 us)
Async XLA Ops:
  0.6 0.7 %copy-start = (s32[8]{0:T(128)S(1)}, s32[8]{0:T(128)}, u32[]{:S(2)}) copy-start(s32[8]{0:T(128)} %len_hbm.1) | copy-start | bytes 100
  3.2 2.1 %collective-permute-start = (bf16[2,8,128,128]{3,2,1,0:T(8,128)(2,1)S(1)}, bf16[2,8,128,128]{3,2,1,0:T(8,128)(2,1)S(1)}, u32[]{:S(2)}, u32[]{:S(2)}) collective-permute-start(bf16[2,8,128,128]{3,2,1,0:T(8,128)(2,1)S(1)} %get-tuple-element.53), channel_id=1, source_target_pairs={{0,1},{1,0},{2,3},{3,2},{4,5},{5,4},{6,7},{7,6},{8,9},{9,8},{10,11... | collective-permute-start | bytes 1572872 | tf_op jit(solution)/shard_map/ppermute | solution.py:377
  5.4 12.7 %collective-permute-start.1 = (bf16[4,128,128]{2,1,0:T(8,128)(2,1)S(1)}, bf16[4,128,128]{2,1,0:T(8,128)(2,1)S(1)}, u32[]{:S(2)}, u32[]{:S(2)}) collective-permute-start(bf16[4,128,128]{2,1,0:T(8,128)(2,1)S(1)} %get-tuple-element.54.own_ref), channel_id=1, source_target_pairs={{0,4},{1,5},{2,6},{3,7},{4,8},{5,9},{6,10},{7,11},{8,12},{9,13},{1... | collective-permute-start | bytes 393224 | tf_op jit(solution)/shard_map/ppermute | solution.py:403
  10.3 11.3 %collective-permute-start.6 = (bf16[4,128,128]{2,1,0:T(8,128)(2,1)S(1)}, bf16[4,128,128]{2,1,0:T(8,128)(2,1)S(1)}, u32[]{:S(2)}, u32[]{:S(2)}) collective-permute-start(bf16[4,128,128]{2,1,0:T(8,128)(2,1)S(1)} %get-tuple-element.58.own_ref), channel_id=1, source_target_pairs={{4,0},{5,1},{6,2},{7,3},{8,4},{9,5},{10,6},{11,7},{12,8},{13,9},{1... | collective-permute-start | bytes 393224 | tf_op jit(solution)/shard_map/ppermute | solution.py:403
  11.6 10.1 %collective-permute-start.8 = (bf16[4,128,128]{2,1,0:T(8,128)(2,1)S(1)}, bf16[4,128,128]{2,1,0:T(8,128)(2,1)S(1)}, u32[]{:S(2)}, u32[]{:S(2)}) collective-permute-start(bf16[4,128,128]{2,1,0:T(8,128)(2,1)S(1)} %get-tuple-element.59.own_ref), channel_id=1, source_target_pairs={{4,0},{5,1},{6,2},{7,3},{8,4},{9,5},{10,6},{11,7},{12,8},{13,9},{1... | collective-permute-start | bytes 393224 | tf_op jit(solution)/shard_map/ppermute | solution.py:403
  12.9 10.1 %collective-permute-start.3 = (bf16[4,128,128]{2,1,0:T(8,128)(2,1)S(1)}, bf16[4,128,128]{2,1,0:T(8,128)(2,1)S(1)}, u32[]{:S(2)}, u32[]{:S(2)}) collective-permute-start(bf16[4,128,128]{2,1,0:T(8,128)(2,1)S(1)} %get-tuple-element.55.own_ref), channel_id=1, source_target_pairs={{0,4},{1,5},{2,6},{3,7},{4,8},{5,9},{6,10},{7,11},{8,12},{9,13},{1... | collective-permute-start | bytes 393224 | tf_op jit(solution)/shard_map/ppermute | solution.py:403
  18.1 15.4 %collective-permute-start.2 = (bf16[4,128,128]{2,1,0:T(8,128)(2,1)S(1)}, bf16[4,128,128]{2,1,0:T(8,128)(2,1)S(1)}, u32[]{:S(2)}, u32[]{:S(2)}) collective-permute-start(bf16[4,128,128]{2,1,0:T(8,128)(2,1)S(1)} %far.4.refs_0_), channel_id=1, source_target_pairs={{0,2},{1,3},{2,4},{3,5},{4,6},{5,7},{6,8},{7,9},{8,10},{9,11},{10,... | collective-permute-start | bytes 393224 | tf_op jit(solution)/shard_map/ppermute | solution.py:403
  21.7 19.5 %collective-permute-start.10 = (bf16[8,128,128]{2,1,0:T(8,128)(2,1)S(1)}, bf16[8,128,128]{2,1,0:T(8,128)(2,1)S(1)}, u32[]{:S(2)}, u32[]{:S(2)}) collective-permute-start(bf16[8,128,128]{2,1,0:T(8,128)(2,1)S(1)} %get-tuple-element.61), channel_id=1, source_target_pairs={{4,0},{5,1},{6,2},{7,3},{8,4},{9,5},{10,6},{11,7},{12,8},{13,9},{1... | collective-permute-start | bytes 786440 | tf_op jit(solution)/shard_map/ppermute | solution.py:403
  23.1 18.1 %collective-permute-start.5 = (bf16[8,128,128]{2,1,0:T(8,128)(2,1)S(1)}, bf16[8,128,128]{2,1,0:T(8,128)(2,1)S(1)}, u32[]{:S(2)}, u32[]{:S(2)}) collective-permute-start(bf16[8,128,128]{2,1,0:T(8,128)(2,1)S(1)} %get-tuple-element.57), channel_id=1, source_target_pairs={{0,4},{1,5},{2,6},{3,7},{4,8},{5,9},{6,10},{7,11},{8,12},{9,13},{1... | collective-permute-start | bytes 786440 | tf_op jit(solution)/shard_map/ppermute | solution.py:403
  27.6 9.1 %collective-permute-start.7 = (bf16[4,128,128]{2,1,0:T(8,128)(2,1)S(1)}, bf16[4,128,128]{2,1,0:T(8,128)(2,1)S(1)}, u32[]{:S(2)}, u32[]{:S(2)}) collective-permute-start(bf16[4,128,128]{2,1,0:T(8,128)(2,1)S(1)} %far.6.refs_0_), channel_id=1, source_target_pairs={{2,0},{3,1},{4,2},{5,3},{6,4},{7,5},{8,6},{9,7},{10,8},{11,9},{12,... | collective-permute-start | bytes 393224 | tf_op jit(solution)/shard_map/ppermute | solution.py:403
  28.9 7.8 %collective-permute-start.4 = (bf16[4,128,128]{2,1,0:T(8,128)(2,1)S(1)}, bf16[4,128,128]{2,1,0:T(8,128)(2,1)S(1)}, u32[]{:S(2)}, u32[]{:S(2)}) collective-permute-start(bf16[4,128,128]{2,1,0:T(8,128)(2,1)S(1)} %get-tuple-element.56), channel_id=1, source_target_pairs={{0,2},{1,3},{2,4},{3,5},{4,6},{5,7},{6,8},{7,9},{8,10},{9,11},{10,... | collective-permute-start | bytes 393224 | tf_op jit(solution)/shard_map/ppermute | solution.py:403
  33.5 7.7 %collective-permute-start.9 = (bf16[4,128,128]{2,1,0:T(8,128)(2,1)S(1)}, bf16[4,128,128]{2,1,0:T(8,128)(2,1)S(1)}, u32[]{:S(2)}, u32[]{:S(2)}) collective-permute-start(bf16[4,128,128]{2,1,0:T(8,128)(2,1)S(1)} %get-tuple-element.60), channel_id=1, source_target_pairs={{2,0},{3,1},{4,2},{5,3},{6,4},{7,5},{8,6},{9,7},{10,8},{11,9},{12,... | collective-permute-start | bytes 393224 | tf_op jit(solution)/shard_map/ppermute | solution.py:403
  41.7 2.0 %collective-permute-start.11 = (bf16[2,8,128,128]{3,2,1,0:T(8,128)(2,1)S(1)}, bf16[2,8,128,128]{3,2,1,0:T(8,128)(2,1)S(1)}, u32[]{:S(2)}, u32[]{:S(2)}) collective-permute-start(bf16[2,8,128,128]{3,2,1,0:T(8,128)(2,1)S(1)} %get-tuple-element.62), channel_id=1, source_target_pairs={{0,1},{1,0},{2,3},{3,2},{4,5},{5,4},{6,7},{7,6},{8,9},{9,8},{10,11... | collective-permute-start | bytes 1572872 | tf_op jit(solution)/shard_map/ppermute | solution.py:430

commit v5 on v3

--- a/solution.py
+++ b/solution.py
@@ -140,8 +140,7 @@
     core = lax.rem(me, 2)
     pair = lax.rem(me, TEAM) // 2
     base = me - lax.rem(me, TEAM)
-    teams = n // TEAM
-    one, zero = jnp.int32(1), jnp.int32(0)
+    one = jnp.int32(1)
 
     def put(row, flag):
         coef_ref[pl.ds(row, 1), :] = jnp.full((1, HD), flag.astype(F32), F32)
@@ -172,8 +171,8 @@
     for d in range(PAIRS):
         tot_f = same(high[d][0], team_high[0])
         tot_b = same(team_low[1], low[d][1])
-        put(TOT_F + d, tot_f * is_low if teams == 2 else tot_f)
-        put(TOT_B + d, tot_b * is_high if teams == 2 else tot_b)
+        put(TOT_F + d, tot_f)
+        put(TOT_B + d, tot_b)
         put(ENTER_F + d, same(team_low[0], low[d][0]) * (one - is_low))
         put(ENTER_B + d, same(high[d][1], team_high[1]) * (one - is_high))
         for s in range(PAIRS):
@@ -258,59 +257,61 @@
     return coef_ref[pl.ds(row, 1), :]
 
 
-def pair_kernel(coef_ref, keep_ref, got_ref, *out_refs):
-    per = out_refs[0].shape[1]
+def kind_of(which, split):
+    if not split:
+        return which
+    upper = (lax.axis_index("seq") >= TEAM).astype(jnp.int32)
+    return upper if which == 0 else 1 - upper
+
+
+def pair_kernel(split, coef_ref, keep_ref, got_ref, *out_refs):
+    per = out_refs[0].shape[0]
     pair = lax.rem(lax.axis_index("seq"), TEAM) // 2
-    for kind, (a, b) in enumerate(((KEEP_F, GOT_F), (KEEP_B, GOT_B))):
-        ca, cb = coef(coef_ref, a), coef(coef_ref, b)
-        for d, out_ref in enumerate(out_refs):
+    for which in range(2):
+        kind = kind_of(which, split)
+        ca, cb = coef(coef_ref, KEEP_F + 2 * kind), coef(coef_ref, GOT_F + 2 * kind)
+        for d in range(PAIRS):
             for i in range(per):
                 h = (pair ^ PARTNERS[d]) * per + i
                 both = keep_ref[kind, h].astype(F32) * ca + got_ref[kind, h].astype(F32) * cb
-                out_ref[kind, i] = both.astype(BF16)
-
-
-def totals_kernel(coef_ref, s0, s1, s2, s3, after_ref, out_ref):
+                out_refs[which * PAIRS + d][i] = both.astype(BF16)
+
+
+def totals_kernel(which, split, coef_ref, s0, s1, s2, s3, out_ref):
+    row = TOT_F + PAIRS * kind_of(which, split)
+    for i in range(out_ref.shape[0]):
+        parts = [s[i].astype(F32) * coef(coef_ref, row + d) for d, s in enumerate((s0, s1, s2, s3))]
+        out_ref[i] = sum(parts).astype(BF16)
+
+
+def scan_kernel(which, split, enters, coef_ref, *refs):
+    sums, out_refs = refs[:PAIRS], refs[-PAIRS:]
+    kind = kind_of(which, split)
+    mix, enter = MIX_F + PAIRS * PAIRS * kind, ENTER_F + PAIRS * kind
+    for i in range(out_refs[0].shape[0]):
+        parts = [s[i].astype(F32) for s in sums]
+        for d, out_ref in enumerate(out_refs):
+            terms = [
+                parts[s] * coef(coef_ref, mix + d * PAIRS + s) for s in range(PAIRS) if s != d
+            ]
+            if enters:
+                terms.append(refs[PAIRS][i].astype(F32) * coef(coef_ref, enter + d))
+            out_ref[i] = sum(terms).astype(BF16)
+
+
+def post_kernel(split, coef_ref, keep_ref, got_ref, after_ref, *refs):
     del after_ref
-    sums = (s0, s1, s2, s3)
-    for i in range(out_ref.shape[1]):
-        fwd, bwd = (
-            sum(sums[d][kind, i].astype(F32) * coef(coef_ref, row + d) for d in range(PAIRS))
-            for kind, row in enumerate((TOT_F, TOT_B))
-        )
-        if out_ref.shape[0] == 1:
-            out_ref[0, i] = (fwd + bwd).astype(BF16)
-        else:
-            out_ref[0, i] = fwd.astype(BF16)
-            out_ref[1, i] = bwd.astype(BF16)
-
-
-def scan_kernel(coef_ref, s0, s1, s2, s3, enter_ref, *out_refs):
-    sums = (s0, s1, s2, s3)
-    last = enter_ref.shape[0] - 1
-    for kind, (mix, enter) in enumerate(((MIX_F, ENTER_F), (MIX_B, ENTER_B))):
-        for i in range(out_refs[0].shape[1]):
-            came = enter_ref[min(kind, last), i].astype(F32)
-            parts = [s[kind, i].astype(F32) for s in sums]
-            for d, out_ref in enumerate(out_refs):
-                total = came * coef(coef_ref, enter + d)
-                for s in range(PAIRS):
-                    if s != d:
-                        total = total + parts[s] * coef(coef_ref, mix + d * PAIRS + s)
-                out_ref[kind, i] = total.astype(BF16)
-
-
-def post_kernel(coef_ref, c0, c1, c2, c3, keep_ref, got_ref, mine_ref, theirs_ref):
-    per = c0.shape[1]
+    mine_ref, theirs_ref = refs[-2:]
+    per = refs[0].shape[0]
     pair = lax.rem(lax.axis_index("seq"), TEAM) // 2
-    for kind in range(2):
-        m, t = (MINE_F, THEIRS_F) if kind == 0 else (MINE_B, THEIRS_B)
-        m0, m1 = coef(coef_ref, m), coef(coef_ref, m + 1)
-        t0, t1 = coef(coef_ref, t), coef(coef_ref, t + 1)
-        for d, c_ref in enumerate((c0, c1, c2, c3)):
+    for which in range(2):
+        kind = kind_of(which, split)
+        m0, m1 = coef(coef_ref, MINE_F + 2 * kind), coef(coef_ref, MINE_F + 2 * kind + 1)
+        t0, t1 = coef(coef_ref, THEIRS_F + 2 * kind), coef(coef_ref, THEIRS_F + 2 * kind + 1)
+        for d in range(PAIRS):
             for i in range(per):
                 h = (pair ^ PARTNERS[d]) * per + i
-                came = c_ref[kind, i].astype(F32)
+                came = refs[which * PAIRS + d][i].astype(F32)
                 theirs_ref[kind, h] = (came * t0 + keep_ref[kind, h].astype(F32) * t1).astype(BF16)
                 mine_ref[kind, h] = (came * m0 + got_ref[kind, h].astype(F32) * m1).astype(BF16)
 
@@ -432,8 +433,15 @@
         flops=4 * heads * product,
         scratch=lengths,
     )
-    owned = shape(2, per, HD, HD)
-    sums = call(pair_kernel, "pair", [owned] * PAIRS, (table, keep, got), [vmem] * 3)
+    owned = shape(per, HD, HD)
+    split = teams == 2
+    parts = call(
+        functools.partial(pair_kernel, split),
+        "pair",
+        [owned] * (2 * PAIRS),
+        (table, keep, got),
+        [vmem] * 3,
+    )
 
     def trade(parts):
         return [parts[0]] + [
@@ -441,20 +449,36 @@
             for d in range(1, PAIRS)
         ]
 
-    sums = trade(sums)
-    kinds = 1 if teams == 2 else 2
-    (edge,) = call(
-        totals_kernel, "totals", [shape(kinds, per, HD, HD)], (table, *sums, masks), [vmem] * 6
-    )
+    sums = [trade(parts[:PAIRS]), trade(parts[PAIRS:])]
+
+    def edge(which):
+        kernel = functools.partial(totals_kernel, which, split)
+        return call(kernel, "totals", [owned], (table, *sums[which]), [vmem] * 5)[0]
+
+    def scan(which, *enter):
+        return trade(
+            call(
+                functools.partial(scan_kernel, which, split, bool(enter)),
+                "scan",
+                [owned] * PAIRS,
+                (table, *sums[which], *enter),
+                [vmem] * (5 + len(enter)),
+            )
+        )
+
     up = [(i, i + TEAM) for i in range(n - TEAM)]
     down = [(j, i) for i, j in up]
-    if kinds == 1:
-        enter = lax.ppermute(edge, "seq", up + down)
+    if split:
+        enter = lax.ppermute(edge(0), "seq", up + down)
+        entering = scan(0) + scan(1, enter)
     else:
-        enter = jnp.stack([lax.ppermute(edge[0], "seq", up), lax.ppermute(edge[1], "seq", down)])
-    entering = trade(call(scan_kernel, "scan", [owned] * PAIRS, (table, *sums, enter), [vmem] * 6))
+        entering = scan(0, lax.ppermute(edge(0), "seq", up)) + scan(1, lax.ppermute(edge(1), "seq", down))
     mine, theirs = call(
-        post_kernel, "post", [states] * 2, (table, *entering, keep, got), [vmem] * 7
+        functools.partial(post_kernel, split),
+        "post",
+        [states] * 2,
+        (table, keep, got, masks, *entering),
+        [vmem] * (4 + 2 * PAIRS),
     )
     other = lax.ppermute(theirs, "seq", swap)
     w, wt, dw, dwt, kt, qt, scaled = local

time: 35.2 us -> 32.1 us (0.912)
  waiting for transfers between devices: 14 us -> 3.7 us
  starting transfers between devices: 11.4 us -> 18.7 us
    ppermute x6 -> x12, starting transfers between devices: 8.16 us -> 15.5 us  [trade(): lax.ppermute(parts[d], 'seq', [(i, i ^ 2 * PARTNERS[d]) for i in range(n)])]
    ppermute x6 -> x12, waiting for transfers between devices: 8.48 us -> 2.08 us  [trade(): lax.ppermute(parts[d], 'seq', [(i, i ^ 2 * PARTNERS[d]) for i in range(n)])]
    ppermute x1, waiting for transfers between devices: 3.97 us -> 0.01 us  [per_device(): enter = lax.ppermute(edge(0), 'seq', up + down)]
    pallas_call x9 -> x10, Pallas kernels: 8.2 us -> 8.2 us  [call(): pl.pallas_call(kernel, in_specs=specs, out_specs=out_specs or [vmem] * le...]
  transfers between devices with their start and end apart: 9 -> 15, of which waited for: 9 -> 5; matrix products, arithmetic and copies ran while one was open for 0% -> 0% of each run, Pallas kernels for 11% -> 13%
where the time goes in v5:
time: 32.1 us; the launch traced here: 32 us
  starting transfers between devices  18.7 us (58%)
  Pallas kernels  8.2 us (26%)
  waiting for transfers between devices  3.7 us (12%)
  between operations  0.73 us (2%)
  local copies, waits for them, and re-layouts  0.65 us (2%)
    ppermute x12, starting transfers between devices, trade(): lax.ppermute(parts[d], 'seq', [(i, i ^ 2 * PARTNERS[d]) for i in range(n)])  15.5 us
    pallas_call x10, Pallas kernels, call(): pl.pallas_call(kernel, in_specs=specs, out_specs=out_specs or [vmem] * le...  8.2 us
    ppermute x1, starting transfers between devices, per_device(): enter = lax.ppermute(edge(0), 'seq', up + down)  2.66 us
    ppermute x12, waiting for transfers between devices, trade(): lax.ppermute(parts[d], 'seq', [(i, i ^ 2 * PARTNERS[d]) for i in range(n)])  2.08 us
    ppermute x1, waiting for transfers between devices, per_device(): other = lax.ppermute(theirs, 'seq', swap)  1.13 us
    unnamed x2, local copies, waits for them, and re-layouts  0.65 us
  transfers between devices with their start and end apart: 15, of which 5 were waited for; matrix products, arithmetic and copies ran while one was open for 0% of the time, Pallas kernels for 13%

profile of v5, /device:TPU:0, one launch (start us, length us, event | category | flops | bytes accessed | tf_op | source)
XLA Modules:
  0.0 32.0 jit_solution(12719558761753877331)
XLA Ops:
  0.6 0.6 %copy-done = s32[8]{0:T(128)S(1)} copy-done((s32[8]{0:T(128)S(1)}, s32[8]{0:T(128)}, u32[]{:S(2)}) %copy-start) | copy-done | bytes 56
  1.3 1.9 %send.1 = (s32[8]{0:T(128)S(1)}, bf16[2,8,128,128]{3,2,1,0:T(8,128)(2,1)S(1)}, bf16[128,2048]{1,0:T(8,128)(2,1)S(1)}, bf16[128,2048]{1,0:T(8,128)(2,1)S(1)}, bf1...) custom-call(s32[8]{0:T(128)S(1)} %copy-done, ...), custom_call_target="tpu_custom_call" | custom-call | flops 67108864 | bytes 4849728 | tf_op jit(solution)/shard_map/send/pallas_call | solution.py:383
  3.2 0.5 %collective-permute-start = (bf16[2,8,128,128]{3,2,1,0:T(8,128)(2,1)S(1)}, bf16[2,8,128,128]{3,2,1,0:T(8,128)(2,1)S(1)}, u32[]{:S(2)}, u32[]{:S(2)}) collective-permute-start(bf16[2,8,128,128]{3,2,1,0:T(8,128)(2,1)S(1)} %get-tuple-element.61), channel_id=1, source_target_pairs={{0,1},{1,0},{2,3},{3,2},{4,5},{5,4},{6,7},{7,6},{8,9},{9,8},{10,11... | collective-permute-start | bytes 1572872 | tf_op jit(solution)/shard_map/ppermute | solution.py:416
  3.7 1.0 %keep.1 = (bf16[2,8,128,128]{3,2,1,0:T(8,128)(2,1)S(1)}, f32[64,128]{1,0:T(8,128)S(1)}) custom-call(s32[8]{0:T(128)S(1)} %get-tuple-element.47.len_hbm, bf16[128,2048]{1,0:T(8,128)(2,1)S(1)} %get-tuple-element.44.q_ref.refs_0_, bf16[128,2048]{1,0:T(8,128)(2,1)S(1)} %get-tuple-element.45.k_ref.refs_1_, bf16[128,2048]{1,0:T(8,128)(2,1)S(1)} %get-tuple-element.46.v_ref.refs_2_, ...), custom_call_target="tpu_custom_call" | custom-call | flops 67108864 | bytes 2785312 | tf_op jit(solution)/shard_map/keep/pallas_call | solution.py:383
  4.7 0.5 %collective-permute-done.got_ref = bf16[2,8,128,128]{3,2,1,0:T(8,128)(2,1)S(1)} collective-permute-done((bf16[2,8,128,128]{3,2,1,0:T(8,128)(2,1)S(1)}, bf16[2,8,128,128]{3,2,1,0:T(8,128)(2,1)S(1)}, u32[]{:S(2)}, u32[]{:S(2)}) %collective-permute-start) | collective-permute-done | bytes 524320 | tf_op jit(solution)/shard_map/ppermute | solution.py:416
  5.2 0.2 pair.1
  5.4 4.0 %collective-permute-start.1 = (bf16[2,128,128]{2,1,0:T(8,128)(2,1)S(1)}, bf16[2,128,128]{2,1,0:T(8,128)(2,1)S(1)}, u32[]{:S(2)}, u32[]{:S(2)}) collective-permute-start(bf16[2,128,128]{2,1,0:T(8,128)(2,1)S(1)} %get-tuple-element.63), channel_id=1, source_target_pairs={{0,6},{1,7},{2,4},{3,5},{4,2},{5,3},{6,0},{7,1},{8,14},{9,15},{10,... | collective-permute-start | bytes 196616 | tf_op jit(solution)/shard_map/ppermute | solution.py:448
  9.4 0.5 %collective-permute-start.2 = (bf16[2,128,128]{2,1,0:T(8,128)(2,1)S(1)}, bf16[2,128,128]{2,1,0:T(8,128)(2,1)S(1)}, u32[]{:S(2)}, u32[]{:S(2)}) collective-permute-start(bf16[2,128,128]{2,1,0:T(8,128)(2,1)S(1)} %get-tuple-element.64), channel_id=1, source_target_pairs={{0,2},{1,3},{2,0},{3,1},{4,6},{5,7},{6,4},{7,5},{8,10},{9,11},{10,... | collective-permute-start | bytes 196616 | tf_op jit(solution)/shard_map/ppermute | solution.py:448
  9.9 0.1 collective-permute-start.3
  10.0 2.8 %collective-permute-start.7 = (bf16[2,128,128]{2,1,0:T(8,128)(2,1)S(1)}, bf16[2,128,128]{2,1,0:T(8,128)(2,1)S(1)}, u32[]{:S(2)}, u32[]{:S(2)}) collective-permute-start(bf16[2,128,128]{2,1,0:T(8,128)(2,1)S(1)} %get-tuple-element.71), channel_id=1, source_target_pairs={{0,6},{1,7},{2,4},{3,5},{4,2},{5,3},{6,0},{7,1},{8,14},{9,15},{10,... | collective-permute-start | bytes 196616 | tf_op jit(solution)/shard_map/ppermute | solution.py:448
  12.9 0.5 %collective-permute-start.8 = (bf16[2,128,128]{2,1,0:T(8,128)(2,1)S(1)}, bf16[2,128,128]{2,1,0:T(8,128)(2,1)S(1)}, u32[]{:S(2)}, u32[]{:S(2)}) collective-permute-start(bf16[2,128,128]{2,1,0:T(8,128)(2,1)S(1)} %get-tuple-element.72), channel_id=1, source_target_pairs={{0,2},{1,3},{2,0},{3,1},{4,6},{5,7},{6,4},{7,5},{8,10},{9,11},{10,... | collective-permute-start | bytes 196616 | tf_op jit(solution)/shard_map/ppermute | solution.py:448
  13.4 0.0 collective-permute-done.1.refs_1_.s1
  13.4 0.4 %collective-permute-start.9 = (bf16[2,128,128]{2,1,0:T(8,128)(2,1)S(1)}, bf16[2,128,128]{2,1,0:T(8,128)(2,1)S(1)}, u32[]{:S(2)}, u32[]{:S(2)}) collective-permute-start(bf16[2,128,128]{2,1,0:T(8,128)(2,1)S(1)} %get-tuple-element.73), channel_id=1, source_target_pairs={{0,4},{1,5},{2,6},{3,7},{4,0},{5,1},{6,2},{7,3},{8,12},{9,13},{10,... | collective-permute-start | bytes 196616 | tf_op jit(solution)/shard_map/ppermute | solution.py:448
  13.8 0.8 %collective-permute-done.3.refs_3_.s3 = bf16[2,128,128]{2,1,0:T(8,128)(2,1)S(1)} collective-permute-done((bf16[2,128,128]{2,1,0:T(8,128)(2,1)S(1)}, bf16[2,128,128]{2,1,0:T(8,128)(2,1)S(1)}, u32[]{:S(2)}, u32[]{:S(2)}) %collective-permute-start.3) | collective-permute-done | bytes 65568 | tf_op jit(solution)/shard_map/ppermute | solution.py:448
  14.6 0.1 totals.1
  14.7 2.7 %collective-permute-start.10 = (bf16[2,128,128]{2,1,0:T(8,128)(2,1)S(1)}, bf16[2,128,128]{2,1,0:T(8,128)(2,1)S(1)}, u32[]{:S(2)}, u32[]{:S(2)}) collective-permute-start(bf16[2,128,128]{2,1,0:T(8,128)(2,1)S(1)} %totals.1), channel_id=1, source_target_pairs={{0,8},{1,9},{2,10},{3,11},{4,12},{5,13},{6,14},{7,15},{8,0},{9,1},... | collective-permute-start | bytes 196616 | tf_op jit(solution)/shard_map/ppermute | solution.py:472
  17.3 0.1 scan.2
  17.4 1.8 %collective-permute-start.4 = (bf16[2,128,128]{2,1,0:T(8,128)(2,1)S(1)}, bf16[2,128,128]{2,1,0:T(8,128)(2,1)S(1)}, u32[]{:S(2)}, u32[]{:S(2)}) collective-permute-start(bf16[2,128,128]{2,1,0:T(8,128)(2,1)S(1)} %get-tuple-element.67), channel_id=1, source_target_pairs={{0,6},{1,7},{2,4},{3,5},{4,2},{5,3},{6,0},{7,1},{8,14},{9,15},{10,... | collective-permute-start | bytes 196616 | tf_op jit(solution)/shard_map/ppermute | solution.py:448
  19.3 0.5 %collective-permute-start.5 = (bf16[2,128,128]{2,1,0:T(8,128)(2,1)S(1)}, bf16[2,128,128]{2,1,0:T(8,128)(2,1)S(1)}, u32[]{:S(2)}, u32[]{:S(2)}) collective-permute-start(bf16[2,128,128]{2,1,0:T(8,128)(2,1)S(1)} %get-tuple-element.68), channel_id=1, source_target_pairs={{0,2},{1,3},{2,0},{3,1},{4,6},{5,7},{6,4},{7,5},{8,10},{9,11},{10,... | collective-permute-start | bytes 196616 | tf_op jit(solution)/shard_map/ppermute | solution.py:448
  19.8 1.2 %collective-permute-start.6 = (bf16[2,128,128]{2,1,0:T(8,128)(2,1)S(1)}, bf16[2,128,128]{2,1,0:T(8,128)(2,1)S(1)}, u32[]{:S(2)}, u32[]{:S(2)}) collective-permute-start(bf16[2,128,128]{2,1,0:T(8,128)(2,1)S(1)} %get-tuple-element.69), channel_id=1, source_target_pairs={{0,4},{1,5},{2,6},{3,7},{4,0},{5,1},{6,2},{7,3},{8,12},{9,13},{10,... | collective-permute-start | bytes 196616 | tf_op jit(solution)/shard_map/ppermute | solution.py:448
  21.0 0.2 scan.3
  21.2 1.8 %collective-permute-start.11 = (bf16[2,128,128]{2,1,0:T(8,128)(2,1)S(1)}, bf16[2,128,128]{2,1,0:T(8,128)(2,1)S(1)}, u32[]{:S(2)}, u32[]{:S(2)}) collective-permute-start(bf16[2,128,128]{2,1,0:T(8,128)(2,1)S(1)} %get-tuple-element.75), channel_id=1, source_target_pairs={{0,6},{1,7},{2,4},{3,5},{4,2},{5,3},{6,0},{7,1},{8,14},{9,15},{10,... | collective-permute-start | bytes 196616 | tf_op jit(solution)/shard_map/ppermute | solution.py:448
  23.0 0.6 %collective-permute-start.12 = (bf16[2,128,128]{2,1,0:T(8,128)(2,1)S(1)}, bf16[2,128,128]{2,1,0:T(8,128)(2,1)S(1)}, u32[]{:S(2)}, u32[]{:S(2)}) collective-permute-start(bf16[2,128,128]{2,1,0:T(8,128)(2,1)S(1)} %get-tuple-element.76), channel_id=1, source_target_pairs={{0,2},{1,3},{2,0},{3,1},{4,6},{5,7},{6,4},{7,5},{8,10},{9,11},{10,... | collective-permute-start | bytes 196616 | tf_op jit(solution)/shard_map/ppermute | solution.py:448
  23.6 1.1 %collective-permute-start.13 = (bf16[2,128,128]{2,1,0:T(8,128)(2,1)S(1)}, bf16[2,128,128]{2,1,0:T(8,128)(2,1)S(1)}, u32[]{:S(2)}, u32[]{:S(2)}) collective-permute-start(bf16[2,128,128]{2,1,0:T(8,128)(2,1)S(1)} %get-tuple-element.77), channel_id=1, source_target_pairs={{0,4},{1,5},{2,6},{3,7},{4,0},{5,1},{6,2},{7,3},{8,12},{9,13},{10,... | collective-permute-start | bytes 196616 | tf_op jit(solution)/shard_map/ppermute | solution.py:448
  24.7 1.9 %local.1 = (bf16[16,128,128]{2,1,0:T(8,128)(2,1)S(1)}, bf16[16,128,128]{2,1,0:T(8,128)(2,1)S(1)}, bf16[16,128,128]{2,1,0:T(8,128)(2,1)S(1)}, bf16[16,128,128]{2,...) custom-call(s32[8]{0:T(128)S(1)} %get-tuple-element.47.len_hbm, ...), custom_call_target="tpu_custom_call" | custom-call | flops 268435456 | bytes 5832736 | tf_op jit(solution)/shard_map/local/pallas_call | solution.py:383
  26.7 0.6 %collective-permute-done.12.refs_6_ = bf16[2,128,128]{2,1,0:T(8,128)(2,1)S(1)} collective-permute-done((bf16[2,128,128]{2,1,0:T(8,128)(2,1)S(1)}, bf16[2,128,128]{2,1,0:T(8,128)(2,1)S(1)}, u32[]{:S(2)}, u32[]{:S(2)}) %collective-permute-start.12) | collective-permute-done | bytes 65568 | tf_op jit(solution)/shard_map/ppermute | solution.py:448
  27.3 0.6 %collective-permute-done.13.refs_7_ = bf16[2,128,128]{2,1,0:T(8,128)(2,1)S(1)} collective-permute-done((bf16[2,128,128]{2,1,0:T(8,128)(2,1)S(1)}, bf16[2,128,128]{2,1,0:T(8,128)(2,1)S(1)}, u32[]{:S(2)}, u32[]{:S(2)}) %collective-permute-start.13) | collective-permute-done | bytes 65568 | tf_op jit(solution)/shard_map/ppermute | solution.py:448
  27.9 0.4 %post.1 = (bf16[2,8,128,128]{3,2,1,0:T(8,128)(2,1)S(1)}, bf16[2,8,128,128]{3,2,1,0:T(8,128)(2,1)S(1)}) custom-call(f32[64,128]{1,0:T(8,128)S(1)} %get-tuple-element.59.coef_ref, bf16[2,8,128,128]{3,2,1,0:T(8,128)(2,1)S(1)} %get-tuple-element.60.keep_ref, bf16[2,8,128,128]{3,2,1,0:T(8,128)(2,1)S(1)} %collective-permute-done.got_ref, ...), custom_call_target="tpu_custom_call" | custom-call | bytes 2719744 | tf_op jit(solution)/shard_map/post/pallas_call | solution.py:383
  28.3 0.1 collective-permute-start.14
  28.4 0.8 %finish_mine.1 = (bf16[128,1024]{1,0:T(8,128)(2,1)S(1)}, bf16[128,1024]{1,0:T(8,128)(2,1)S(1)}, bf16[128,1024]{1,0:T(8,128)(2,1)S(1)}, bf16[128,1024]{1,0:T(8,128)(2,1)S(1)}) custom-call(bf16[128,2048]{1,0:T(8,128)(2,1)S(1)} %get-tuple-element.44.q_ref.refs_0_, bf16[128,2048]{1,0:T(8,128)(2,1)S(1)} %get-tuple-element.45.k_ref.refs_1_, ...), custom_call_target="tpu_custom_call" | custom-call | flops 268435456 | bytes 6946816 | tf_op jit(solution)/shard_map/finish_mine/pallas_call | solution.py:383
  29.2 1.1 %collective-permute-done.14.refs_12_ = bf16[2,8,128,128]{3,2,1,0:T(8,128)(2,1)S(1)} collective-permute-done((bf16[2,8,128,128]{3,2,1,0:T(8,128)(2,1)S(1)}, bf16[2,8,128,128]{3,2,1,0:T(8,128)(2,1)S(1)}, u32[]{:S(2)}, u32[]{:S(2)}) %collective-permute-start.14) | collective-permute-done | bytes 524320 | tf_op jit(solution)/shard_map/ppermute | solution.py:483
  30.3 1.7 %finish_other.1 = (bf16[128,2048]{1,0:T(8,128)(2,1)}, bf16[128,2048]{1,0:T(8,128)(2,1)}, bf16[128,2048]{1,0:T(8,128)(2,1)}, bf16[128,2048]{1,0:T(8,128)(2,1)}) custom-call(bf16[128,2048]{1,0:T(8,128)(2,1)S(1)} %get-tuple-element.44.q_ref.refs_0_, bf16[128,2048]{1,0:T(8,128)(2,1)S(1)} %get-tuple-element.45.k_ref.refs_1_, ...), custom_call_target="tpu_custom_call" | custom-call | flops 268435456 | bytes 9043968 | tf_op jit(solution)/shard_map/finish_other/pallas_call | solution.py:383
  (10 shorter events, 0.0 us)
Async XLA Ops:
  0.6 0.7 %copy-start = (s32[8]{0:T(128)S(1)}, s32[8]{0:T(128)}, u32[]{:S(2)}) copy-start(s32[8]{0:T(128)} %len_hbm.1) | copy-start | bytes 100
  3.2 2.1 %collective-permute-start = (bf16[2,8,128,128]{3,2,1,0:T(8,128)(2,1)S(1)}, bf16[2,8,128,128]{3,2,1,0:T(8,128)(2,1)S(1)}, u32[]{:S(2)}, u32[]{:S(2)}) collective-permute-start(bf16[2,8,128,128]{3,2,1,0:T(8,128)(2,1)S(1)} %get-tuple-element.61), channel_id=1, source_target_pairs={{0,1},{1,0},{2,3},{3,2},{4,5},{5,4},{6,7},{7,6},{8,9},{9,8},{10,11... | collective-permute-start | bytes 1572872 | tf_op jit(solution)/shard_map/ppermute | solution.py:416
  5.4 8.0 %collective-permute-start.1 = (bf16[2,128,128]{2,1,0:T(8,128)(2,1)S(1)}, bf16[2,128,128]{2,1,0:T(8,128)(2,1)S(1)}, u32[]{:S(2)}, u32[]{:S(2)}) collective-permute-start(bf16[2,128,128]{2,1,0:T(8,128)(2,1)S(1)} %get-tuple-element.63), channel_id=1, source_target_pairs={{0,6},{1,7},{2,4},{3,5},{4,2},{5,3},{6,0},{7,1},{8,14},{9,15},{10,... | collective-permute-start | bytes 196616 | tf_op jit(solution)/shard_map/ppermute | solution.py:448
  9.4 4.4 %collective-permute-start.2 = (bf16[2,128,128]{2,1,0:T(8,128)(2,1)S(1)}, bf16[2,128,128]{2,1,0:T(8,128)(2,1)S(1)}, u32[]{:S(2)}, u32[]{:S(2)}) collective-permute-start(bf16[2,128,128]{2,1,0:T(8,128)(2,1)S(1)} %get-tuple-element.64), channel_id=1, source_target_pairs={{0,2},{1,3},{2,0},{3,1},{4,6},{5,7},{6,4},{7,5},{8,10},{9,11},{10,... | collective-permute-start | bytes 196616 | tf_op jit(solution)/shard_map/ppermute | solution.py:448
  9.9 4.7 %collective-permute-start.3 = (bf16[2,128,128]{2,1,0:T(8,128)(2,1)S(1)}, bf16[2,128,128]{2,1,0:T(8,128)(2,1)S(1)}, u32[]{:S(2)}, u32[]{:S(2)}) collective-permute-start(bf16[2,128,128]{2,1,0:T(8,128)(2,1)S(1)} %get-tuple-element.65), channel_id=1, source_target_pairs={{0,4},{1,5},{2,6},{3,7},{4,0},{5,1},{6,2},{7,3},{8,12},{9,13},{10,... | collective-permute-start | bytes 196616 | tf_op jit(solution)/shard_map/ppermute | solution.py:448
  10.0 9.3 %collective-permute-start.7 = (bf16[2,128,128]{2,1,0:T(8,128)(2,1)S(1)}, bf16[2,128,128]{2,1,0:T(8,128)(2,1)S(1)}, u32[]{:S(2)}, u32[]{:S(2)}) collective-permute-start(bf16[2,128,128]{2,1,0:T(8,128)(2,1)S(1)} %get-tuple-element.71), channel_id=1, source_target_pairs={{0,6},{1,7},{2,4},{3,5},{4,2},{5,3},{6,0},{7,1},{8,14},{9,15},{10,... | collective-permute-start | bytes 196616 | tf_op jit(solution)/shard_map/ppermute | solution.py:448
  12.9 6.9 %collective-permute-start.8 = (bf16[2,128,128]{2,1,0:T(8,128)(2,1)S(1)}, bf16[2,128,128]{2,1,0:T(8,128)(2,1)S(1)}, u32[]{:S(2)}, u32[]{:S(2)}) collective-permute-start(bf16[2,128,128]{2,1,0:T(8,128)(2,1)S(1)} %get-tuple-element.72), channel_id=1, source_target_pairs={{0,2},{1,3},{2,0},{3,1},{4,6},{5,7},{6,4},{7,5},{8,10},{9,11},{10,... | collective-permute-start | bytes 196616 | tf_op jit(solution)/shard_map/ppermute | solution.py:448
  13.4 7.6 %collective-permute-start.9 = (bf16[2,128,128]{2,1,0:T(8,128)(2,1)S(1)}, bf16[2,128,128]{2,1,0:T(8,128)(2,1)S(1)}, u32[]{:S(2)}, u32[]{:S(2)}) collective-permute-start(bf16[2,128,128]{2,1,0:T(8,128)(2,1)S(1)} %get-tuple-element.73), channel_id=1, source_target_pairs={{0,4},{1,5},{2,6},{3,7},{4,0},{5,1},{6,2},{7,3},{8,12},{9,13},{10,... | collective-permute-start | bytes 196616 | tf_op jit(solution)/shard_map/ppermute | solution.py:448
  14.7 6.3 %collective-permute-start.10 = (bf16[2,128,128]{2,1,0:T(8,128)(2,1)S(1)}, bf16[2,128,128]{2,1,0:T(8,128)(2,1)S(1)}, u32[]{:S(2)}, u32[]{:S(2)}) collective-permute-start(bf16[2,128,128]{2,1,0:T(8,128)(2,1)S(1)} %totals.1), channel_id=1, source_target_pairs={{0,8},{1,9},{2,10},{3,11},{4,12},{5,13},{6,14},{7,15},{8,0},{9,1},... | collective-permute-start | bytes 196616 | tf_op jit(solution)/shard_map/ppermute | solution.py:472
  17.4 6.2 %collective-permute-start.4 = (bf16[2,128,128]{2,1,0:T(8,128)(2,1)S(1)}, bf16[2,128,128]{2,1,0:T(8,128)(2,1)S(1)}, u32[]{:S(2)}, u32[]{:S(2)}) collective-permute-start(bf16[2,128,128]{2,1,0:T(8,128)(2,1)S(1)} %get-tuple-element.67), channel_id=1, source_target_pairs={{0,6},{1,7},{2,4},{3,5},{4,2},{5,3},{6,0},{7,1},{8,14},{9,15},{10,... | collective-permute-start | bytes 196616 | tf_op jit(solution)/shard_map/ppermute | solution.py:448
  19.3 7.3 %collective-permute-start.5 = (bf16[2,128,128]{2,1,0:T(8,128)(2,1)S(1)}, bf16[2,128,128]{2,1,0:T(8,128)(2,1)S(1)}, u32[]{:S(2)}, u32[]{:S(2)}) collective-permute-start(bf16[2,128,128]{2,1,0:T(8,128)(2,1)S(1)} %get-tuple-element.68), channel_id=1, source_target_pairs={{0,2},{1,3},{2,0},{3,1},{4,6},{5,7},{6,4},{7,5},{8,10},{9,11},{10,... | collective-permute-start | bytes 196616 | tf_op jit(solution)/shard_map/ppermute | solution.py:448
  19.8 6.8 %collective-permute-start.6 = (bf16[2,128,128]{2,1,0:T(8,128)(2,1)S(1)}, bf16[2,128,128]{2,1,0:T(8,128)(2,1)S(1)}, u32[]{:S(2)}, u32[]{:S(2)}) collective-permute-start(bf16[2,128,128]{2,1,0:T(8,128)(2,1)S(1)} %get-tuple-element.69), channel_id=1, source_target_pairs={{0,4},{1,5},{2,6},{3,7},{4,0},{5,1},{6,2},{7,3},{8,12},{9,13},{10,... | collective-permute-start | bytes 196616 | tf_op jit(solution)/shard_map/ppermute | solution.py:448
  21.2 5.5 %collective-permute-start.11 = (bf16[2,128,128]{2,1,0:T(8,128)(2,1)S(1)}, bf16[2,128,128]{2,1,0:T(8,128)(2,1)S(1)}, u32[]{:S(2)}, u32[]{:S(2)}) collective-permute-start(bf16[2,128,128]{2,1,0:T(8,128)(2,1)S(1)} %get-tuple-element.75), channel_id=1, source_target_pairs={{0,6},{1,7},{2,4},{3,5},{4,2},{5,3},{6,0},{7,1},{8,14},{9,15},{10,... | collective-permute-start | bytes 196616 | tf_op jit(solution)/shard_map/ppermute | solution.py:448
  23.0 4.3 %collective-permute-start.12 = (bf16[2,128,128]{2,1,0:T(8,128)(2,1)S(1)}, bf16[2,128,128]{2,1,0:T(8,128)(2,1)S(1)}, u32[]{:S(2)}, u32[]{:S(2)}) collective-permute-start(bf16[2,128,128]{2,1,0:T(8,128)(2,1)S(1)} %get-tuple-element.76), channel_id=1, source_target_pairs={{0,2},{1,3},{2,0},{3,1},{4,6},{5,7},{6,4},{7,5},{8,10},{9,11},{10,... | collective-permute-start | bytes 196616 | tf_op jit(solution)/shard_map/ppermute | solution.py:448
  23.6 4.3 %collective-permute-start.13 = (bf16[2,128,128]{2,1,0:T(8,128)(2,1)S(1)}, bf16[2,128,128]{2,1,0:T(8,128)(2,1)S(1)}, u32[]{:S(2)}, u32[]{:S(2)}) collective-permute-start(bf16[2,128,128]{2,1,0:T(8,128)(2,1)S(1)} %get-tuple-element.77), channel_id=1, source_target_pairs={{0,4},{1,5},{2,6},{3,7},{4,0},{5,1},{6,2},{7,3},{8,12},{9,13},{10,... | collective-permute-start | bytes 196616 | tf_op jit(solution)/shard_map/ppermute | solution.py:448
  28.3 2.0 %collective-permute-start.14 = (bf16[2,8,128,128]{3,2,1,0:T(8,128)(2,1)S(1)}, bf16[2,8,128,128]{3,2,1,0:T(8,128)(2,1)S(1)}, u32[]{:S(2)}, u32[]{:S(2)}) collective-permute-start(bf16[2,8,128,128]{3,2,1,0:T(8,128)(2,1)S(1)} %get-tuple-element.78), channel_id=1, source_target_pairs={{0,1},{1,0},{2,3},{3,2},{4,5},{5,4},{6,7},{7,6},{8,9},{9,8},{10,11... | collective-permute-start | bytes 1572872 | tf_op jit(solution)/shard_map/ppermute | solution.py:483

commit v6 on v5

--- a/solution.py
+++ b/solution.py
@@ -9,7 +9,6 @@
 
 HD = 128
 PAIRS = 4
-PARTNERS = (0, 3, 1, 2)
 TEAM = 2 * PAIRS
 F32 = jnp.float32
 BF16 = jnp.bfloat16
@@ -138,7 +137,6 @@
 def coefficients(starts, rows, n, coef_ref):
     me = lax.axis_index("seq")
     core = lax.rem(me, 2)
-    pair = lax.rem(me, TEAM) // 2
     base = me - lax.rem(me, TEAM)
     one = jnp.int32(1)
 
@@ -152,14 +150,14 @@
         return (a == b).astype(jnp.int32)
 
     team_low, team_high = both(base), both(base + TEAM)
-    pairs = [pair ^ d for d in PARTNERS]
+    pairs = [jnp.int32(d) for d in range(PAIRS)]
     low = [both(base + 2 * p) for p in pairs]
     high = [both(base + 2 * p + 2) for p in pairs]
-    middle = both(me - core + 1)
-    open_0 = same(low[0][0], middle[0])
-    open_1 = same(middle[0], high[0][0])
-    close_0 = same(low[0][1], middle[1])
-    close_1 = same(middle[1], high[0][1])
+    first, middle, last = both(me - core), both(me - core + 1), both(me - core + 2)
+    open_0 = same(first[0], middle[0])
+    open_1 = same(middle[0], last[0])
+    close_0 = same(first[1], middle[1])
+    close_1 = same(middle[1], last[1])
     odd = core
     even = one - core
     put(KEEP_F, jnp.where(odd == 1, one, open_1))
@@ -265,53 +263,51 @@
 
 
 def pair_kernel(split, coef_ref, keep_ref, got_ref, *out_refs):
-    per = out_refs[0].shape[0]
-    pair = lax.rem(lax.axis_index("seq"), TEAM) // 2
+    per = out_refs[0].shape[1]
     for which in range(2):
         kind = kind_of(which, split)
         ca, cb = coef(coef_ref, KEEP_F + 2 * kind), coef(coef_ref, GOT_F + 2 * kind)
         for d in range(PAIRS):
             for i in range(per):
-                h = (pair ^ PARTNERS[d]) * per + i
+                h = d * per + i
                 both = keep_ref[kind, h].astype(F32) * ca + got_ref[kind, h].astype(F32) * cb
-                out_refs[which * PAIRS + d][i] = both.astype(BF16)
-
-
-def totals_kernel(which, split, coef_ref, s0, s1, s2, s3, out_ref):
+                out_refs[which][d, i] = both.astype(BF16)
+
+
+def totals_kernel(which, split, coef_ref, sums_ref, out_ref):
     row = TOT_F + PAIRS * kind_of(which, split)
     for i in range(out_ref.shape[0]):
-        parts = [s[i].astype(F32) * coef(coef_ref, row + d) for d, s in enumerate((s0, s1, s2, s3))]
+        parts = [sums_ref[d, i].astype(F32) * coef(coef_ref, row + d) for d in range(PAIRS)]
         out_ref[i] = sum(parts).astype(BF16)
 
 
-def scan_kernel(which, split, enters, coef_ref, *refs):
-    sums, out_refs = refs[:PAIRS], refs[-PAIRS:]
+def scan_kernel(which, split, coef_ref, sums_ref, *refs):
+    out_ref = refs[-1]
     kind = kind_of(which, split)
     mix, enter = MIX_F + PAIRS * PAIRS * kind, ENTER_F + PAIRS * kind
-    for i in range(out_refs[0].shape[0]):
-        parts = [s[i].astype(F32) for s in sums]
-        for d, out_ref in enumerate(out_refs):
+    for i in range(out_ref.shape[1]):
+        parts = [sums_ref[s, i].astype(F32) for s in range(PAIRS)]
+        for d in range(PAIRS):
             terms = [
                 parts[s] * coef(coef_ref, mix + d * PAIRS + s) for s in range(PAIRS) if s != d
             ]
-            if enters:
-                terms.append(refs[PAIRS][i].astype(F32) * coef(coef_ref, enter + d))
-            out_ref[i] = sum(terms).astype(BF16)
+            if len(refs) > 1:
+                terms.append(refs[0][i].astype(F32) * coef(coef_ref, enter + d))
+            out_ref[d, i] = sum(terms).astype(BF16)
 
 
 def post_kernel(split, coef_ref, keep_ref, got_ref, after_ref, *refs):
     del after_ref
     mine_ref, theirs_ref = refs[-2:]
-    per = refs[0].shape[0]
-    pair = lax.rem(lax.axis_index("seq"), TEAM) // 2
+    per = refs[0].shape[1]
     for which in range(2):
         kind = kind_of(which, split)
         m0, m1 = coef(coef_ref, MINE_F + 2 * kind), coef(coef_ref, MINE_F + 2 * kind + 1)
         t0, t1 = coef(coef_ref, THEIRS_F + 2 * kind), coef(coef_ref, THEIRS_F + 2 * kind + 1)
         for d in range(PAIRS):
             for i in range(per):
-                h = (pair ^ PARTNERS[d]) * per + i
-                came = refs[which * PAIRS + d][i].astype(F32)
+                h = d * per + i
+                came = refs[which][d, i].astype(F32)
                 theirs_ref[kind, h] = (came * t0 + keep_ref[kind, h].astype(F32) * t1).astype(BF16)
                 mine_ref[kind, h] = (came * m0 + got_ref[kind, h].astype(F32) * m1).astype(BF16)
 
@@ -433,52 +429,46 @@
         flops=4 * heads * product,
         scratch=lengths,
     )
-    owned = shape(per, HD, HD)
+    owned, spread = shape(per, HD, HD), shape(PAIRS, per, HD, HD)
     split = teams == 2
-    parts = call(
-        functools.partial(pair_kernel, split),
-        "pair",
-        [owned] * (2 * PAIRS),
-        (table, keep, got),
-        [vmem] * 3,
-    )
-
-    def trade(parts):
-        return [parts[0]] + [
-            lax.ppermute(parts[d], "seq", [(i, i ^ (2 * PARTNERS[d])) for i in range(n)])
-            for d in range(1, PAIRS)
-        ]
-
-    sums = [trade(parts[:PAIRS]), trade(parts[PAIRS:])]
+    members = [
+        [t * TEAM + 2 * p + core for p in range(PAIRS)] for t in range(teams) for core in range(2)
+    ]
+
+    def trade(x):
+        return lax.all_to_all(x, "seq", 0, 0, axis_index_groups=members, tiled=True)
+
+    sums = [
+        trade(x)
+        for x in call(
+            functools.partial(pair_kernel, split), "pair", [spread] * 2, (table, keep, got), [vmem] * 3
+        )
+    ]
 
     def edge(which):
         kernel = functools.partial(totals_kernel, which, split)
-        return call(kernel, "totals", [owned], (table, *sums[which]), [vmem] * 5)[0]
+        return call(kernel, "totals", [owned], (table, sums[which]), [vmem] * 2)[0]
 
     def scan(which, *enter):
+        kernel = functools.partial(scan_kernel, which, split)
         return trade(
-            call(
-                functools.partial(scan_kernel, which, split, bool(enter)),
-                "scan",
-                [owned] * PAIRS,
-                (table, *sums[which], *enter),
-                [vmem] * (5 + len(enter)),
-            )
+            call(kernel, "scan", [spread], (table, sums[which], *enter), [vmem] * (2 + len(enter)))[0]
         )
 
     up = [(i, i + TEAM) for i in range(n - TEAM)]
     down = [(j, i) for i, j in up]
     if split:
         enter = lax.ppermute(edge(0), "seq", up + down)
-        entering = scan(0) + scan(1, enter)
+        entering = scan(0), scan(1, enter)
     else:
-        entering = scan(0, lax.ppermute(edge(0), "seq", up)) + scan(1, lax.ppermute(edge(1), "seq", down))
+        forward, backward = lax.ppermute(edge(0), "seq", up), lax.ppermute(edge(1), "seq", down)
+        entering = scan(0, forward), scan(1, backward)
     mine, theirs = call(
         functools.partial(post_kernel, split),
         "post",
         [states] * 2,
         (table, keep, got, masks, *entering),
-        [vmem] * (4 + 2 * PAIRS),
+        [vmem] * 6,
     )
     other = lax.ppermute(theirs, "seq", swap)
     w, wt, dw, dwt, kt, qt, scaled = local

time: 32.1 us -> 61.8 us (1.93); the launches traced: 32 us -> 61.1 us
  local copies, waits for them, and re-layouts: 0.65 us -> 14.9 us
  blocking collectives: 0 us -> 11 us
  waiting for transfers between devices: 3.7 us -> 7.89 us
  starting transfers between devices: 18.7 us -> 16.5 us
  Pallas kernels: 8.2 us -> 9.98 us
    ppermute x12 -> x0, starting transfers between devices: 15.5 us -> none  [trade(): lax.ppermute(parts[d], 'seq', [(i, i ^ 2 * PARTNERS[d]) for i in range(n)])]
    unnamed x2 -> x44, local copies, waits for them, and re-layouts: 0.65 us -> 14.9 us
    all_to_all x0 -> x3, starting transfers between devices: none -> 13.3 us  [trade(): return lax.all_to_all(x, 'seq', 0, 0, axis_index_groups=members, tiled=True)]
    all_to_all x0 -> x1, blocking collectives: none -> 11 us  [trade(): return lax.all_to_all(x, 'seq', 0, 0, axis_index_groups=members, tiled=True)]
    all_to_all x0 -> x3, waiting for transfers between devices: none -> 4.61 us  [trade(): return lax.all_to_all(x, 'seq', 0, 0, axis_index_groups=members, tiled=True)]
    ppermute x1, waiting for transfers between devices: 0.01 us -> 2.68 us  [per_device(): enter = lax.ppermute(edge(0), 'seq', up + down)]
    ppermute x12 -> x0, waiting for transfers between devices: 2.08 us -> none  [trade(): lax.ppermute(parts[d], 'seq', [(i, i ^ 2 * PARTNERS[d]) for i in range(n)])]
    pallas_call x10, Pallas kernels: 8.2 us -> 9.98 us  [call(): pl.pallas_call(kernel, in_specs=specs, out_specs=out_specs or [vmem] * le...]
  transfers between devices with their start and end apart: 15 -> 6, of which waited for: 5 -> 3; matrix products, arithmetic and copies ran while one was open for 0% -> 0% of each run, Pallas kernels for 13% -> 8%
where the time goes in v6:
time: 61.8 us; the launch traced here: 61.1 us
  starting transfers between devices  16.5 us (27%)
  local copies, waits for them, and re-layouts  14.9 us (24%)
  blocking collectives  11 us (18%)
  Pallas kernels  9.98 us (16%)
  waiting for transfers between devices  7.89 us (13%)
  between operations  0.81 us (1%)
    unnamed x44, local copies, waits for them, and re-layouts  14.9 us
    all_to_all x3, starting transfers between devices, trade(): return lax.all_to_all(x, 'seq', 0, 0, axis_index_groups=members, tiled=True)  13.3 us
    all_to_all x1, blocking collectives, trade(): return lax.all_to_all(x, 'seq', 0, 0, axis_index_groups=members, tiled=True)  11 us
    pallas_call x10, Pallas kernels, call(): pl.pallas_call(kernel, in_specs=specs, out_specs=out_specs or [vmem] * le...  9.98 us
    all_to_all x3, waiting for transfers between devices, trade(): return lax.all_to_all(x, 'seq', 0, 0, axis_index_groups=members, tiled=True)  4.61 us
    ppermute x1, waiting for transfers between devices, per_device(): enter = lax.ppermute(edge(0), 'seq', up + down)  2.68 us
    ppermute x1, starting transfers between devices, per_device(): enter = lax.ppermute(edge(0), 'seq', up + down)  2.65 us
  transfers between devices with their start and end apart: 6, of which 3 were waited for; matrix products, arithmetic and copies ran while one was open for 0% of the time, Pallas kernels for 8%

profile of v6, /device:TPU:0, one launch (start us, length us, event | category | flops | bytes accessed | tf_op | source)
XLA Modules:
  0.0 61.1 jit_solution(10190687791335954846)
XLA Ops:
  0.6 0.6 %copy-done.21 = s32[8]{0:T(128)S(1)} copy-done((s32[8]{0:T(128)S(1)}, s32[8]{0:T(128)}, u32[]{:S(2)}) %copy-start.21) | copy-done | bytes 56
  1.3 1.9 %send.1 = (s32[8]{0:T(128)S(1)}, bf16[2,8,128,128]{3,2,1,0:T(8,128)(2,1)S(1)}, bf16[128,2048]{1,0:T(8,128)(2,1)S(1)}, bf16[128,2048]{1,0:T(8,128)(2,1)S(1)}, bf1...) custom-call(s32[8]{0:T(128)S(1)} %copy-done.21, ...), custom_call_target="tpu_custom_call" | custom-call | flops 67108864 | bytes 4849728 | tf_op jit(solution)/shard_map/send/pallas_call | solution.py:379
  3.7 0.9 %keep.1 = (bf16[2,8,128,128]{3,2,1,0:T(8,128)(2,1)S(1)}, f32[64,128]{1,0:T(8,128)S(1)}) custom-call(s32[8]{0:T(128)S(1)} %get-tuple-element.33.len_hbm, bf16[128,2048]{1,0:T(8,128)(2,1)S(1)} %get-tuple-element.30.q_ref.refs_0_, bf16[128,2048]{1,0:T(8,128)(2,1)S(1)} %get-tuple-element.31.k_ref.refs_1_, bf16[128,2048]{1,0:T(8,128)(2,1)S(1)} %get-tuple-element.32.v_ref.refs_2_, ...), custom_call_target="tpu_custom_call" | custom-call | flops 67108864 | bytes 2785312 | tf_op jit(solution)/shard_map/keep/pallas_call | solution.py:379
  5.4 11.0 %all_to_all.20.sums_ref = bf16[4,2,128,128]{3,2,1,0:T(8,128)(2,1)S(1)} all-to-all(bf16[4,2,128,128]{3,2,1,0:T(8,128)(2,1)S(1)} %get-tuple-element.48), channel_id=1, replica_groups={{0,2,4,6},{1,3,5,7},{8,10,12,14},{9,11,13,15},{16,18,20,22},{17,19,21,2..., dimensions={0} | all-to-all | bytes 524288 | tf_op jit(solution)/shard_map/all_to_all | solution.py:439
  16.4 4.1 %all-to-all-start.2 = ((bf16[4,2,128,128]{3,2,1,0:T(8,128)(2,1)}), bf16[4,2,128,128]{3,2,1,0:T(8,128)(2,1)}, u32[]{:S(2)}, u32[]{:S(2)}) async-start(bf16[4,2,128,128]{3,2,1,0:T(8,128)(2,1)} %copy-done.20), calls=%async_computation.2 | async-start | bytes 524288 | tf_op jit(solution)/shard_map/all_to_all | solution.py:439
  20.6 0.7 %copy-done.16 = bf16[4,2,128,128]{3,2,1,0:T(8,128)(2,1)} copy-done((bf16[4,2,128,128]{3,2,1,0:T(8,128)(2,1)}, bf16[4,2,128,128]{3,2,1,0:T(8,128)(2,1)S(1)}, u32[]{:S(2)}) %copy-start.16) | copy-done | bytes 262168
  21.3 4.6 %all-to-all-done.2.sums_ref = bf16[4,2,128,128]{3,2,1,0:T(8,128)(2,1)} async-done(((bf16[4,2,128,128]{3,2,1,0:T(8,128)(2,1)}), bf16[4,2,128,128]{3,2,1,0:T(8,128)(2,1)}, u32[]{:S(2)}, u32[]{:S(2)}) %all-to-all-start.2) | async-done | bytes 262176 | tf_op jit(solution)/shard_map/all_to_all | solution.py:439
  25.9 4.1 %all-to-all-start.1 = ((bf16[4,2,128,128]{3,2,1,0:T(8,128)(2,1)}), bf16[4,2,128,128]{3,2,1,0:T(8,128)(2,1)}, u32[]{:S(2)}, u32[]{:S(2)}) async-start(bf16[4,2,128,128]{3,2,1,0:T(8,128)(2,1)} %copy-done.16), calls=%async_computation.1 | async-start | bytes 524288 | tf_op jit(solution)/shard_map/all_to_all | solution.py:439
  30.0 2.7 %collective-permute-start.1 = (bf16[2,128,128]{2,1,0:T(8,128)(2,1)S(1)}, bf16[2,128,128]{2,1,0:T(8,128)(2,1)S(1)}, u32[]{:S(2)}, u32[]{:S(2)}) collective-permute-start(bf16[2,128,128]{2,1,0:T(8,128)(2,1)S(1)} %totals.1), channel_id=1, source_target_pairs={{0,8},{1,9},{2,10},{3,11},{4,12},{5,13},{6,14},{7,15},{8,0},{9,1},... | collective-permute-start | bytes 196616 | tf_op jit(solution)/shard_map/ppermute | solution.py:461
  32.7 2.7 %collective-permute-done.1.refs_0_ = bf16[2,128,128]{2,1,0:T(8,128)(2,1)S(1)} collective-permute-done((bf16[2,128,128]{2,1,0:T(8,128)(2,1)S(1)}, bf16[2,128,128]{2,1,0:T(8,128)(2,1)S(1)}, u32[]{:S(2)}, u32[]{:S(2)}) %collective-permute-start.1) | collective-permute-done | bytes 65568 | tf_op jit(solution)/shard_map/ppermute | solution.py:461
  35.4 1.1 %scan.3 = bf16[4,2,128,128]{3,2,1,0:T(8,128)(2,1)S(1)} custom-call(f32[64,128]{1,0:T(8,128)S(1)} %get-tuple-element.45.coef_ref, bf16[4,2,128,128]{3,2,1,0:T(8,128)(2,1)} %all-to-all-done.2.sums_ref, bf16[2,128,128]{2,1,0:T(8,128)(2,1)S(1)} %collective-permute-done.1.refs_0_), custom_call_target="tpu_custom_call" | custom-call | bytes 622592 | tf_op jit(solution)/shard_map/scan/pallas_call | solution.py:379
  36.5 0.7 %copy-done.17 = bf16[4,2,128,128]{3,2,1,0:T(8,128)(2,1)} copy-done((bf16[4,2,128,128]{3,2,1,0:T(8,128)(2,1)}, bf16[4,2,128,128]{3,2,1,0:T(8,128)(2,1)S(1)}, u32[]{:S(2)}) %copy-start.17) | copy-done | bytes 262168
  37.2 5.2 %all-to-all-start.3 = ((bf16[4,2,128,128]{3,2,1,0:T(8,128)(2,1)}), bf16[4,2,128,128]{3,2,1,0:T(8,128)(2,1)S(1)}, u32[]{:S(2)}, u32[]{:S(2)}) async-start(bf16[4,2,128,128]{3,2,1,0:T(8,128)(2,1)} %copy-done.17), calls=%async_computation.3 | async-start | bytes 524288 | tf_op jit(solution)/shard_map/all_to_all | solution.py:439
  42.4 1.9 %local.1 = (bf16[16,128,128]{2,1,0:T(8,128)(2,1)S(1)}, bf16[16,128,128]{2,1,0:T(8,128)(2,1)S(1)}, bf16[16,128,128]{2,1,0:T(8,128)(2,1)S(1)}, bf16[16,128,128]{2,...) custom-call(s32[8]{0:T(128)S(1)} %get-tuple-element.33.len_hbm, ...), custom_call_target="tpu_custom_call" | custom-call | flops 268435456 | bytes 5832736 | tf_op jit(solution)/shard_map/local/pallas_call | solution.py:379
  44.3 0.8 %copy-done = bf16[16,128,128]{2,1,0:T(8,128)(2,1)} copy-done((bf16[16,128,128]{2,1,0:T(8,128)(2,1)}, bf16[16,128,128]{2,1,0:T(8,128)(2,1)S(1)}, u32[]{:S(2)}) %copy-start) | copy-done | bytes 524312
  45.1 0.8 %copy-done.2 = bf16[16,128,128]{2,1,0:T(8,128)(2,1)} copy-done((bf16[16,128,128]{2,1,0:T(8,128)(2,1)}, bf16[16,128,128]{2,1,0:T(8,128)(2,1)S(1)}, u32[]{:S(2)}) %copy-start.2) | copy-done | bytes 524312
  45.8 0.8 %copy-done.4 = bf16[16,128,128]{2,1,0:T(8,128)(2,1)} copy-done((bf16[16,128,128]{2,1,0:T(8,128)(2,1)}, bf16[16,128,128]{2,1,0:T(8,128)(2,1)S(1)}, u32[]{:S(2)}) %copy-start.4) | copy-done | bytes 524312
  46.6 0.8 %copy-done.6 = bf16[16,128,128]{2,1,0:T(8,128)(2,1)} copy-done((bf16[16,128,128]{2,1,0:T(8,128)(2,1)}, bf16[16,128,128]{2,1,0:T(8,128)(2,1)S(1)}, u32[]{:S(2)}) %copy-start.6) | copy-done | bytes 524312
  47.4 0.8 %copy-done.8 = bf16[16,128,128]{2,1,0:T(8,128)(2,1)} copy-done((bf16[16,128,128]{2,1,0:T(8,128)(2,1)}, bf16[16,128,128]{2,1,0:T(8,128)(2,1)S(1)}, u32[]{:S(2)}) %copy-start.8) | copy-done | bytes 524312
  48.2 0.8 %copy-done.10 = bf16[16,128,128]{2,1,0:T(8,128)(2,1)} copy-done((bf16[16,128,128]{2,1,0:T(8,128)(2,1)}, bf16[16,128,128]{2,1,0:T(8,128)(2,1)S(1)}, u32[]{:S(2)}) %copy-start.10) | copy-done | bytes 524312
  49.0 0.8 %copy-done.12 = bf16[128,2048]{1,0:T(8,128)(2,1)} copy-done((bf16[128,2048]{1,0:T(8,128)(2,1)}, bf16[128,2048]{1,0:T(8,128)(2,1)S(1)}, u32[]{:S(2)}) %copy-start.12) | copy-done | bytes 524312
  49.8 0.6 %copy-done.18 = bf16[2,128,128]{2,1,0:T(8,128)(2,1)} copy-done((bf16[2,128,128]{2,1,0:T(8,128)(2,1)}, bf16[2,128,128]{2,1,0:T(8,128)(2,1)S(1)}, u32[]{:S(2)}) %copy-start.18) | copy-done | bytes 65560
  50.4 0.7 %copy-done.14 = bf16[4,2,128,128]{3,2,1,0:T(8,128)(2,1)} copy-done((bf16[4,2,128,128]{3,2,1,0:T(8,128)(2,1)}, bf16[4,2,128,128]{3,2,1,0:T(8,128)(2,1)S(1)}, u32[]{:S(2)}) %copy-start.14) | copy-done | bytes 262168
  51.1 0.9 %copy-done.15 = bf16[4,2,128,128]{3,2,1,0:T(8,128)(2,1)S(1)} copy-done((bf16[4,2,128,128]{3,2,1,0:T(8,128)(2,1)S(1)}, bf16[4,2,128,128]{3,2,1,0:T(8,128)(2,1)}, u32[]{:S(2)}) %copy-start.15) | copy-done | bytes 262168
  52.1 0.8 %copy-done.19 = bf16[2,128,128]{2,1,0:T(8,128)(2,1)S(1)} copy-done((bf16[2,128,128]{2,1,0:T(8,128)(2,1)S(1)}, bf16[2,128,128]{2,1,0:T(8,128)(2,1)}, u32[]{:S(2)}) %copy-start.19) | copy-done | bytes 65560
  52.9 1.4 %post.1 = (bf16[2,8,128,128]{3,2,1,0:T(8,128)(2,1)S(1)}, bf16[2,8,128,128]{3,2,1,0:T(8,128)(2,1)S(1)}) custom-call(f32[64,128]{1,0:T(8,128)S(1)} %get-tuple-element.45.coef_ref, bf16[2,8,128,128]{3,2,1,0:T(8,128)(2,1)S(1)} %get-tuple-element.46.keep_ref, bf16[2,8,128,128]{3,2,1,0:T(8,128)(2,1)S(1)} %collective-permute-done.got_ref, ...), custom_call_target="tpu_custom_call" | custom-call | bytes 2719744 | tf_op jit(solution)/shard_map/post/pallas_call | solution.py:379
  54.5 1.0 %copy-done.7 = bf16[16,128,128]{2,1,0:T(8,128)(2,1)S(1)} copy-done((bf16[16,128,128]{2,1,0:T(8,128)(2,1)S(1)}, bf16[16,128,128]{2,1,0:T(8,128)(2,1)}, u32[]{:S(2)}) %copy-start.7) | copy-done | bytes 524312
  55.5 1.0 %copy-done.9 = bf16[16,128,128]{2,1,0:T(8,128)(2,1)S(1)} copy-done((bf16[16,128,128]{2,1,0:T(8,128)(2,1)S(1)}, bf16[16,128,128]{2,1,0:T(8,128)(2,1)}, u32[]{:S(2)}) %copy-start.9) | copy-done | bytes 524312
  56.6 1.0 %copy-done.11 = bf16[16,128,128]{2,1,0:T(8,128)(2,1)S(1)} copy-done((bf16[16,128,128]{2,1,0:T(8,128)(2,1)S(1)}, bf16[16,128,128]{2,1,0:T(8,128)(2,1)}, u32[]{:S(2)}) %copy-start.11) | copy-done | bytes 524312
  57.6 1.0 %copy-done.13 = bf16[128,2048]{1,0:T(8,128)(2,1)S(1)} copy-done((bf16[128,2048]{1,0:T(8,128)(2,1)S(1)}, bf16[128,2048]{1,0:T(8,128)(2,1)}, u32[]{:S(2)}) %copy-start.13) | copy-done | bytes 524312
  58.6 0.7 %finish_mine.1 = (bf16[128,1024]{1,0:T(8,128)(2,1)S(1)}, bf16[128,1024]{1,0:T(8,128)(2,1)S(1)}, bf16[128,1024]{1,0:T(8,128)(2,1)S(1)}, bf16[128,1024]{1,0:T(8,128)(2,1)S(1)}) custom-call(bf16[128,2048]{1,0:T(8,128)(2,1)S(1)} %get-tuple-element.30.q_ref.refs_0_, bf16[128,2048]{1,0:T(8,128)(2,1)S(1)} %get-tuple-element.31.k_ref.refs_1_, ...), custom_call_target="tpu_custom_call" | custom-call | flops 268435456 | bytes 6946816 | tf_op jit(solution)/shard_map/finish_mine/pallas_call | solution.py:379
  59.4 1.7 %finish_other.1 = (bf16[128,2048]{1,0:T(8,128)(2,1)}, bf16[128,2048]{1,0:T(8,128)(2,1)}, bf16[128,2048]{1,0:T(8,128)(2,1)}, bf16[128,2048]{1,0:T(8,128)(2,1)}) custom-call(bf16[128,2048]{1,0:T(8,128)(2,1)S(1)} %get-tuple-element.30.q_ref.refs_0_, bf16[128,2048]{1,0:T(8,128)(2,1)S(1)} %get-tuple-element.31.k_ref.refs_1_, ...), custom_call_target="tpu_custom_call" | custom-call | flops 268435456 | bytes 9043968 | tf_op jit(solution)/shard_map/finish_other/pallas_call | solution.py:379
  (35 shorter events, 1.6 us)
Async XLA Ops:
  0.6 0.7 %copy-start.21 = (s32[8]{0:T(128)S(1)}, s32[8]{0:T(128)}, u32[]{:S(2)}) copy-start(s32[8]{0:T(128)} %len_hbm.1) | copy-start | bytes 100
  3.2 2.1 %collective-permute-start = (bf16[2,8,128,128]{3,2,1,0:T(8,128)(2,1)S(1)}, bf16[2,8,128,128]{3,2,1,0:T(8,128)(2,1)S(1)}, u32[]{:S(2)}, u32[]{:S(2)}) collective-permute-start(bf16[2,8,128,128]{3,2,1,0:T(8,128)(2,1)S(1)} %get-tuple-element.47), channel_id=1, source_target_pairs={{0,1},{1,0},{2,3},{3,2},{4,5},{5,4},{6,7},{7,6},{8,9},{9,8},{10,11... | collective-permute-start | bytes 1572872 | tf_op jit(solution)/shard_map/ppermute | solution.py:412
  5.4 11.0 %copy-start.20 = (bf16[4,2,128,128]{3,2,1,0:T(8,128)(2,1)}, bf16[4,2,128,128]{3,2,1,0:T(8,128)(2,1)S(1)}, u32[]{:S(2)}) copy-start(bf16[4,2,128,128]{3,2,1,0:T(8,128)(2,1)S(1)} %get-tuple-element.49) | copy-start | bytes 786436
  16.4 9.5 %all-to-all-start.2 = ((bf16[4,2,128,128]{3,2,1,0:T(8,128)(2,1)}), bf16[4,2,128,128]{3,2,1,0:T(8,128)(2,1)}, u32[]{:S(2)}, u32[]{:S(2)}) async-start(bf16[4,2,128,128]{3,2,1,0:T(8,128)(2,1)} %copy-done.20), calls=%async_computation.2 | async-start | bytes 524288 | tf_op jit(solution)/shard_map/all_to_all | solution.py:439
  20.6 0.7 %copy-start.16 = (bf16[4,2,128,128]{3,2,1,0:T(8,128)(2,1)}, bf16[4,2,128,128]{3,2,1,0:T(8,128)(2,1)S(1)}, u32[]{:S(2)}) copy-start(bf16[4,2,128,128]{3,2,1,0:T(8,128)(2,1)S(1)} %scan.2) | copy-start | bytes 786436
  25.9 11.3 %all-to-all-start.1 = ((bf16[4,2,128,128]{3,2,1,0:T(8,128)(2,1)}), bf16[4,2,128,128]{3,2,1,0:T(8,128)(2,1)}, u32[]{:S(2)}, u32[]{:S(2)}) async-start(bf16[4,2,128,128]{3,2,1,0:T(8,128)(2,1)} %copy-done.16), calls=%async_computation.1 | async-start | bytes 524288 | tf_op jit(solution)/shard_map/all_to_all | solution.py:439
  30.0 5.3 %collective-permute-start.1 = (bf16[2,128,128]{2,1,0:T(8,128)(2,1)S(1)}, bf16[2,128,128]{2,1,0:T(8,128)(2,1)S(1)}, u32[]{:S(2)}, u32[]{:S(2)}) collective-permute-start(bf16[2,128,128]{2,1,0:T(8,128)(2,1)S(1)} %totals.1), channel_id=1, source_target_pairs={{0,8},{1,9},{2,10},{3,11},{4,12},{5,13},{6,14},{7,15},{8,0},{9,1},... | collective-permute-start | bytes 196616 | tf_op jit(solution)/shard_map/ppermute | solution.py:461
  36.5 0.7 %copy-start.17 = (bf16[4,2,128,128]{3,2,1,0:T(8,128)(2,1)}, bf16[4,2,128,128]{3,2,1,0:T(8,128)(2,1)S(1)}, u32[]{:S(2)}) copy-start(bf16[4,2,128,128]{3,2,1,0:T(8,128)(2,1)S(1)} %scan.3) | copy-start | bytes 786436
  37.2 13.3 %all-to-all-start.3 = ((bf16[4,2,128,128]{3,2,1,0:T(8,128)(2,1)}), bf16[4,2,128,128]{3,2,1,0:T(8,128)(2,1)S(1)}, u32[]{:S(2)}, u32[]{:S(2)}) async-start(bf16[4,2,128,128]{3,2,1,0:T(8,128)(2,1)} %copy-done.17), calls=%async_computation.3 | async-start | bytes 524288 | tf_op jit(solution)/shard_map/all_to_all | solution.py:439
  44.3 0.8 %copy-start = (bf16[16,128,128]{2,1,0:T(8,128)(2,1)}, bf16[16,128,128]{2,1,0:T(8,128)(2,1)S(1)}, u32[]{:S(2)}) copy-start(bf16[16,128,128]{2,1,0:T(8,128)(2,1)S(1)} %get-tuple-element.36.refs_4_) | copy-start | bytes 1572868
  45.0 0.8 %copy-start.2 = (bf16[16,128,128]{2,1,0:T(8,128)(2,1)}, bf16[16,128,128]{2,1,0:T(8,128)(2,1)S(1)}, u32[]{:S(2)}) copy-start(bf16[16,128,128]{2,1,0:T(8,128)(2,1)S(1)} %get-tuple-element.37.refs_5_) | copy-start | bytes 1572868
  45.8 0.8 %copy-start.4 = (bf16[16,128,128]{2,1,0:T(8,128)(2,1)}, bf16[16,128,128]{2,1,0:T(8,128)(2,1)S(1)}, u32[]{:S(2)}) copy-start(bf16[16,128,128]{2,1,0:T(8,128)(2,1)S(1)} %get-tuple-element.38.refs_6_) | copy-start | bytes 1572868
  46.6 0.8 %copy-start.6 = (bf16[16,128,128]{2,1,0:T(8,128)(2,1)}, bf16[16,128,128]{2,1,0:T(8,128)(2,1)S(1)}, u32[]{:S(2)}) copy-start(bf16[16,128,128]{2,1,0:T(8,128)(2,1)S(1)} %get-tuple-element.39.refs_7_) | copy-start | bytes 1572868
  47.4 0.8 %copy-start.8 = (bf16[16,128,128]{2,1,0:T(8,128)(2,1)}, bf16[16,128,128]{2,1,0:T(8,128)(2,1)S(1)}, u32[]{:S(2)}) copy-start(bf16[16,128,128]{2,1,0:T(8,128)(2,1)S(1)} %get-tuple-element.40.refs_8_) | copy-start | bytes 1572868
  48.2 0.8 %copy-start.10 = (bf16[16,128,128]{2,1,0:T(8,128)(2,1)}, bf16[16,128,128]{2,1,0:T(8,128)(2,1)S(1)}, u32[]{:S(2)}) copy-start(bf16[16,128,128]{2,1,0:T(8,128)(2,1)S(1)} %get-tuple-element.41.refs_9_) | copy-start | bytes 1572868
  49.0 0.8 %copy-start.12 = (bf16[128,2048]{1,0:T(8,128)(2,1)}, bf16[128,2048]{1,0:T(8,128)(2,1)S(1)}, u32[]{:S(2)}) copy-start(bf16[128,2048]{1,0:T(8,128)(2,1)S(1)} %get-tuple-element.35.refs_3_) | copy-start | bytes 1572868
  49.8 0.6 %copy-start.18 = (bf16[2,128,128]{2,1,0:T(8,128)(2,1)}, bf16[2,128,128]{2,1,0:T(8,128)(2,1)S(1)}, u32[]{:S(2)}) copy-start(bf16[2,128,128]{2,1,0:T(8,128)(2,1)S(1)} %get-tuple-element.42.after_ref.refs_10_) | copy-start | bytes 196612
  50.4 0.7 %copy-start.14 = (bf16[4,2,128,128]{3,2,1,0:T(8,128)(2,1)}, bf16[4,2,128,128]{3,2,1,0:T(8,128)(2,1)S(1)}, u32[]{:S(2)}) copy-start(bf16[4,2,128,128]{3,2,1,0:T(8,128)(2,1)S(1)} %all-to-all-done.3.refs_1_) | copy-start | bytes 786436
  51.1 0.9 %copy-start.15 = (bf16[4,2,128,128]{3,2,1,0:T(8,128)(2,1)S(1)}, bf16[4,2,128,128]{3,2,1,0:T(8,128)(2,1)}, u32[]{:S(2)}) copy-start(bf16[4,2,128,128]{3,2,1,0:T(8,128)(2,1)} %copy-done.14) | copy-start | bytes 786436
  52.1 0.8 %copy-start.19 = (bf16[2,128,128]{2,1,0:T(8,128)(2,1)S(1)}, bf16[2,128,128]{2,1,0:T(8,128)(2,1)}, u32[]{:S(2)}) copy-start(bf16[2,128,128]{2,1,0:T(8,128)(2,1)} %copy-done.18) | copy-start | bytes 196612
  52.9 1.5 %copy-start.1 = (bf16[16,128,128]{2,1,0:T(8,128)(2,1)S(1)}, bf16[16,128,128]{2,1,0:T(8,128)(2,1)}, u32[]{:S(2)}) copy-start(bf16[16,128,128]{2,1,0:T(8,128)(2,1)} %copy-done) | copy-start | bytes 1572868
  52.9 1.5 %copy-start.3 = (bf16[16,128,128]{2,1,0:T(8,128)(2,1)S(1)}, bf16[16,128,128]{2,1,0:T(8,128)(2,1)}, u32[]{:S(2)}) copy-start(bf16[16,128,128]{2,1,0:T(8,128)(2,1)} %copy-done.2) | copy-start | bytes 1572868
  52.9 1.5 %copy-start.5 = (bf16[16,128,128]{2,1,0:T(8,128)(2,1)S(1)}, bf16[16,128,128]{2,1,0:T(8,128)(2,1)}, u32[]{:S(2)}) copy-start(bf16[16,128,128]{2,1,0:T(8,128)(2,1)} %copy-done.4) | copy-start | bytes 1572868
  54.4 5.0 %collective-permute-start.2 = (bf16[2,8,128,128]{3,2,1,0:T(8,128)(2,1)S(1)}, bf16[2,8,128,128]{3,2,1,0:T(8,128)(2,1)S(1)}, u32[]{:S(2)}, u32[]{:S(2)}) collective-permute-start(bf16[2,8,128,128]{3,2,1,0:T(8,128)(2,1)S(1)} %get-tuple-element.50), channel_id=1, source_target_pairs={{0,1},{1,0},{2,3},{3,2},{4,5},{5,4},{6,7},{7,6},{8,9},{9,8},{10,11... | collective-permute-start | bytes 1572872 | tf_op jit(solution)/shard_map/ppermute | solution.py:473
  54.5 1.0 %copy-start.7 = (bf16[16,128,128]{2,1,0:T(8,128)(2,1)S(1)}, bf16[16,128,128]{2,1,0:T(8,128)(2,1)}, u32[]{:S(2)}) copy-start(bf16[16,128,128]{2,1,0:T(8,128)(2,1)} %copy-done.6) | copy-start | bytes 1572868
  55.5 1.0 %copy-start.9 = (bf16[16,128,128]{2,1,0:T(8,128)(2,1)S(1)}, bf16[16,128,128]{2,1,0:T(8,128)(2,1)}, u32[]{:S(2)}) copy-start(bf16[16,128,128]{2,1,0:T(8,128)(2,1)} %copy-done.8) | copy-start | bytes 1572868
  56.6 1.0 %copy-start.11 = (bf16[16,128,128]{2,1,0:T(8,128)(2,1)S(1)}, bf16[16,128,128]{2,1,0:T(8,128)(2,1)}, u32[]{:S(2)}) copy-start(bf16[16,128,128]{2,1,0:T(8,128)(2,1)} %copy-done.10) | copy-start | bytes 1572868
  57.6 1.0 %copy-start.13 = (bf16[128,2048]{1,0:T(8,128)(2,1)S(1)}, bf16[128,2048]{1,0:T(8,128)(2,1)}, u32[]{:S(2)}) copy-start(bf16[128,2048]{1,0:T(8,128)(2,1)} %copy-done.12) | copy-start | bytes 1572868

commit v7 on v5

--- a/solution.py
+++ b/solution.py
@@ -64,10 +64,10 @@
     return lax.dot_general(a, b, ((contract[:1], contract[1:]), ((), ())), preferred_element_type=F32)
 
 
-def states_of(q, k, v, g, tail_rows, head_rows, inv_root):
+def states_of(kt, qt, v, g, tail_rows, head_rows, inv_root):
     scaled = (g.astype(F32) * inv_root).astype(BF16)
-    tail = dot(k * tail_rows, v, (0, 0))
-    head = dot(q * head_rows, scaled, (0, 0))
+    tail = dot(kt, v * tail_rows, (1, 0))
+    head = dot(qt, scaled * head_rows, (1, 0))
     return tail.astype(BF16), head.astype(BF16)
 
 
@@ -85,6 +85,8 @@
     k_ref,
     v_ref,
     g_ref,
+    kt_ref,
+    qt_ref,
     rows_ref,
     root_ref,
     len_ref,
@@ -92,20 +94,20 @@
     len_sems,
 ):
     rows = q_ref.shape[0]
-    half = out_ref.shape[1] * HD
+    heads = out_ref.shape[1]
     me = lax.axis_index("seq")
-    other = (1 - lax.rem(me, 2)) * half
-    mine = lax.rem(me, 2) * half
-    size = half // chunks
+    other = (1 - lax.rem(me, 2)) * heads
+    mine = lax.rem(me, 2) * heads
     len_copy = pltpu.make_async_copy(len_hbm, len_ref, len_sems.at[0])
     len_copy.start()
     len_pass = pltpu.make_async_copy(len_hbm, len_out, len_sems.at[1])
     len_pass.start()
-    pairs = ((q_hbm, q_ref), (k_hbm, k_ref), (v_hbm, v_ref), (g_hbm, g_ref))
+    pairs = ((k_hbm, k_ref), (q_hbm, q_ref), (v_hbm, v_ref), (g_hbm, g_ref))
+    per = heads // chunks
     copies = []
     for c in range(2 * chunks):
-        begin = other + c * size if c < chunks else mine + (c - chunks) * size
-        at = pl.ds(pl.multiple_of(begin, HD), size)
+        begin = other + c * per if c < chunks else mine + (c - chunks) * per
+        at = pl.ds(pl.multiple_of(begin * HD, HD), per * HD)
         for i, (src, dst) in enumerate(pairs):
             copy = pltpu.make_async_copy(src.at[:, at], dst.at[:, at], sems.at[i, c])
             copy.start()
@@ -121,12 +123,16 @@
     rows_ref[1] = head_rows
     root_ref[...] = inv_root
     for c in range(chunks):
-        for copy in copies[4 * c : 4 * c + 4]:
+        for i, (ref, t_ref) in enumerate(((k_ref, kt_ref), (q_ref, qt_ref))):
+            copies[4 * c + i].wait()
+            for h in range(c * per, (c + 1) * per):
+                t_ref[h] = ref[:, pl.ds(pl.multiple_of((other + h) * HD, HD), HD)].T
+        for copy in copies[4 * c + 2 : 4 * c + 4]:
             copy.wait()
-        for h in range(c * size // HD, (c + 1) * size // HD):
-            cols = pl.ds(pl.multiple_of(other + h * HD, HD), HD)
+        for h in range(c * per, (c + 1) * per):
+            cols = pl.ds(pl.multiple_of((other + h) * HD, HD), HD)
             tail, head = states_of(
-                q_ref[:, cols], k_ref[:, cols], v_ref[:, cols], g_ref[:, cols], tail_rows, head_rows, inv_root
+                kt_ref[h], qt_ref[h], v_ref[:, cols], g_ref[:, cols], tail_rows, head_rows, inv_root
             )
             out_ref[0, h] = tail
             out_ref[1, h] = head
@@ -190,18 +196,21 @@
     put(THEIRS_B + 1, odd)
 
 
-def keep_kernel(total, len_hbm, q_ref, k_ref, v_ref, g_ref, rows_ref, root_ref, out_ref, coef_ref, len_ref, len_sem):
+def keep_kernel(
+    total, len_hbm, q_ref, k_ref, v_ref, g_ref, rows_ref, root_ref, out_ref, kt_ref, qt_ref, coef_ref, len_ref, len_sem
+):
     rows = q_ref.shape[0]
-    half = out_ref.shape[1] * HD
-    offset = lax.rem(lax.axis_index("seq"), 2) * half
+    heads = out_ref.shape[1]
+    core = lax.rem(lax.axis_index("seq"), 2)
     len_copy = pltpu.make_async_copy(len_hbm, len_ref, len_sem)
     len_copy.start()
     tail_rows, head_rows, inv_root = rows_ref[0], rows_ref[1], root_ref[...]
-    for h in range(out_ref.shape[1]):
-        cols = pl.ds(pl.multiple_of(offset + h * HD, HD), HD)
-        tail, head = states_of(
-            q_ref[:, cols], k_ref[:, cols], v_ref[:, cols], g_ref[:, cols], tail_rows, head_rows, inv_root
-        )
+    for h in range(heads):
+        cols = pl.ds(pl.multiple_of((core * heads + h) * HD, HD), HD)
+        kt, qt = k_ref[:, cols].T, q_ref[:, cols].T
+        kt_ref[h] = kt
+        qt_ref[h] = qt
+        tail, head = states_of(kt, qt, v_ref[:, cols], g_ref[:, cols], tail_rows, head_rows, inv_root)
         out_ref[0, h] = tail
         out_ref[1, h] = head
     len_copy.wait()
@@ -219,8 +228,6 @@
     wt_ref,
     dw_ref,
     dwt_ref,
-    kt_ref,
-    qt_ref,
     sg_ref,
     mask_ref,
     len_ref,
@@ -249,8 +256,6 @@
         wt_ref[h] = jnp.where(same_t, dot(k, q, (1, 1)), 0.0).astype(BF16)
         dw_ref[h] = jnp.where(same, dot(g, v, (1, 1)), 0.0).astype(BF16)
         dwt_ref[h] = jnp.where(same_t, dot(v, g, (1, 1)), 0.0).astype(BF16)
-        kt_ref[h] = k.T
-        qt_ref[h] = q.T
 
 
 def coef(coef_ref, row):
@@ -299,42 +304,40 @@
             out_ref[i] = sum(terms).astype(BF16)
 
 
-def post_kernel(split, coef_ref, keep_ref, got_ref, after_ref, *refs):
-    del after_ref
+def post_kernel(which, split, coef_ref, keep_ref, got_ref, *refs):
     mine_ref, theirs_ref = refs[-2:]
     per = refs[0].shape[0]
     pair = lax.rem(lax.axis_index("seq"), TEAM) // 2
-    for which in range(2):
-        kind = kind_of(which, split)
-        m0, m1 = coef(coef_ref, MINE_F + 2 * kind), coef(coef_ref, MINE_F + 2 * kind + 1)
-        t0, t1 = coef(coef_ref, THEIRS_F + 2 * kind), coef(coef_ref, THEIRS_F + 2 * kind + 1)
-        for d in range(PAIRS):
-            for i in range(per):
-                h = (pair ^ PARTNERS[d]) * per + i
-                came = refs[which * PAIRS + d][i].astype(F32)
-                theirs_ref[kind, h] = (came * t0 + keep_ref[kind, h].astype(F32) * t1).astype(BF16)
-                mine_ref[kind, h] = (came * m0 + got_ref[kind, h].astype(F32) * m1).astype(BF16)
-
-
-def finish_kernel(other, chunks, *refs):
-    (q_ref, k_ref, v_ref, g_ref, w_ref, wt_ref, dw_ref, dwt_ref, kt_ref, qt_ref, mask_ref, root_ref, s_ref) = (
-        refs[:13]
-    )
-    heads = s_ref.shape[1]
+    kind = kind_of(which, split)
+    m0, m1 = coef(coef_ref, MINE_F + 2 * kind), coef(coef_ref, MINE_F + 2 * kind + 1)
+    t0, t1 = coef(coef_ref, THEIRS_F + 2 * kind), coef(coef_ref, THEIRS_F + 2 * kind + 1)
+    for d in range(PAIRS):
+        for i in range(per):
+            h = (pair ^ PARTNERS[d]) * per + i
+            came = refs[d][i].astype(F32)
+            theirs_ref[h] = (came * t0 + keep_ref[kind, h].astype(F32) * t1).astype(BF16)
+            mine_ref[h] = (came * m0 + got_ref[kind, h].astype(F32) * m1).astype(BF16)
+
+
+def finish_kernel(other, split, chunks, *refs):
+    q_ref, k_ref, v_ref, g_ref, w_ref, wt_ref, dw_ref, dwt_ref, mask_ref, root_ref = refs[:10]
+    kt_ref, qt_ref, early_ref, late_ref = refs[10:14]
+    heads = early_ref.shape[0]
+    forward_is_late = kind_of(0, split) == 1
     core = lax.rem(lax.axis_index("seq"), 2)
     half = 1 - core if other else core
     prefix, suffix, root = mask_ref[0], mask_ref[1], root_ref[...]
     size = heads * HD // chunks
     copies = []
     if other:
-        done_refs, out_refs, bufs, sems = refs[13:17], refs[17:21], refs[21:25], refs[25]
+        done_refs, out_refs, bufs, sems = refs[14:18], refs[18:22], refs[22:26], refs[26]
         to = pl.ds(pl.multiple_of(core * heads * HD, HD), heads * HD)
         for i, ref in enumerate(out_refs):
             copy = pltpu.make_async_copy(done_refs[i], ref.at[:, to], sems.at[i, chunks])
             copy.start()
             copies.append(copy)
     else:
-        bufs = refs[13:17]
+        bufs = refs[14:18]
 
     def wide(a, b):
         return jnp.concatenate([a, b], axis=1)
@@ -345,12 +348,14 @@
             cols = pl.ds(pl.multiple_of(h * HD, HD), HD)
             at = pl.ds(i * HD, HD)
             q, k, v, g = q_ref[:, cols], k_ref[:, cols], v_ref[:, cols], g_ref[:, cols]
-            carried, returned = s_ref[0, i], s_ref[1, i]
+            early, late = early_ref[i], late_ref[i]
+            carried = jnp.where(forward_is_late, late, early)
+            returned = jnp.where(forward_is_late, early, late)
             o = dot(wide(w_ref[h], q * prefix), jnp.concatenate([v, carried], axis=0), (1, 0))
             bufs[0][:, at] = (o * root).astype(BF16)
-            dq = dot(wide(dw_ref[h], g * prefix), wide(kt_ref[h], carried), (1, 1))
+            dq = dot(wide(dw_ref[h], g * prefix), wide(kt_ref[i], carried), (1, 1))
             bufs[1][:, at] = dq.astype(BF16)
-            dk = dot(wide(dwt_ref[h], v * suffix), wide(qt_ref[h], returned), (1, 1))
+            dk = dot(wide(dwt_ref[h], v * suffix), wide(qt_ref[i], returned), (1, 1))
             bufs[2][:, at] = dk.astype(BF16)
             dv = dot(wide(wt_ref[h], k * suffix), jnp.concatenate([g, returned], axis=0), (1, 0))
             bufs[3][:, at] = dv.astype(BF16)
@@ -386,38 +391,35 @@
             out_specs=out_specs or [vmem] * len(outs),
             out_shape=list(outs),
             scratch_shapes=list(scratch),
-            compiler_params=pltpu.CompilerParams(vmem_limit_bytes=room * 1024 * 1024),
+            compiler_params=pltpu.CompilerParams(vmem_limit_bytes=int(room * 1024 * 1024)),
             cost_estimate=pl.CostEstimate(flops=flops, bytes_accessed=moved, transcendentals=0),
             name=name,
         )(*args)
 
     product = 2 * rows * HD * HD
-    inputs = (doc_lengths, queries, keys, values, grad_out)
-    states = shape(2, half, HD, HD)
+    states, halves, tokens = shape(2, half, HD, HD), shape(half, HD, HD), shape(rows, width)
+    lengths = [pltpu.SMEM(doc_lengths.shape, jnp.int32), pltpu.SemaphoreType.DMA(())]
     chunks = 2
-    tokens = shape(rows, width)
-    lengths = [pltpu.SMEM(doc_lengths.shape, jnp.int32)]
-    doc_lengths, send, *ready = call(
+    doc_lengths, send, queries, keys, values, grad_out, kt_other, qt_other, row_masks, root = call(
         functools.partial(send_kernel, total, chunks),
         "send",
         [shape(*doc_lengths.shape, dtype=jnp.int32), states]
         + [tokens] * 4
+        + [halves] * 2
         + [shape(2, rows, HD), shape(rows, HD, dtype=F32)],
-        inputs,
+        (doc_lengths, queries, keys, values, grad_out),
         [hbm] * 5,
-        [hbm] + [vmem] * 7,
+        [hbm] + [vmem] * 9,
         flops=2 * half * product,
-        scratch=lengths + [pltpu.SemaphoreType.DMA((4, 2 * chunks)), pltpu.SemaphoreType.DMA((2,))],
-        room=51,
-    )
-    queries, keys, values, grad_out, row_masks, root = ready
-    lengths = lengths + [pltpu.SemaphoreType.DMA(())]
+        scratch=lengths[:1] + [pltpu.SemaphoreType.DMA((4, 2 * chunks)), pltpu.SemaphoreType.DMA((2,))],
+        room=50.5,
+    )
     swap = [(i, i ^ 1) for i in range(n)]
     got = lax.ppermute(send, "seq", swap)
-    keep, table = call(
+    keep, kt_mine, qt_mine, table = call(
         functools.partial(keep_kernel, total),
         "keep",
-        [states, shape(COEFS, HD, dtype=F32)],
+        [states, halves, halves, shape(COEFS, HD, dtype=F32)],
         (doc_lengths, queries, keys, values, grad_out, row_masks, root),
         [hbm] + [vmem] * 6,
         flops=2 * half * product,
@@ -427,7 +429,7 @@
     *local, masks = call(
         functools.partial(local_kernel, total),
         "local",
-        [mats] * 6 + [tokens, shape(2, rows, HD)],
+        [mats] * 4 + [tokens, shape(2, rows, HD)],
         (doc_lengths, queries, keys, values, grad_out),
         [hbm] + [vmem] * 4,
         flops=4 * heads * product,
@@ -473,33 +475,36 @@
         entering = scan(0) + scan(1, enter)
     else:
         entering = scan(0, lax.ppermute(edge(0), "seq", up)) + scan(1, lax.ppermute(edge(1), "seq", down))
-    mine, theirs = call(
-        functools.partial(post_kernel, split),
-        "post",
-        [states] * 2,
-        (table, keep, got, masks, *entering),
-        [vmem] * (4 + 2 * PAIRS),
-    )
-    other = lax.ppermute(theirs, "seq", swap)
-    w, wt, dw, dwt, kt, qt, scaled = local
-    fixed = (queries, keys, values, scaled, w, wt, dw, dwt, kt, qt, masks, root)
+    mine, other = [], []
+    for which in range(2):
+        own, theirs = call(
+            functools.partial(post_kernel, which, split),
+            "post",
+            [halves] * 2,
+            (table, keep, got, *entering[which * PAIRS :][:PAIRS], *[masks][:which]),
+            [vmem] * (3 + PAIRS + which),
+        )
+        mine.append(own)
+        other.append(lax.ppermute(theirs, "seq", swap))
+    w, wt, dw, dwt, scaled = local
+    fixed = (queries, keys, values, scaled, w, wt, dw, dwt, masks, root)
     chunks = 4
     part = shape(rows, half * HD)
     done = call(
-        functools.partial(finish_kernel, False, chunks),
+        functools.partial(finish_kernel, False, split, chunks),
         "finish_mine",
         [part] * 4,
-        (*fixed, mine),
-        [vmem] * 13,
+        (*fixed, kt_mine, qt_mine, *mine),
+        [vmem] * 14,
         flops=8 * half * product,
     )
     return tuple(
         call(
-            functools.partial(finish_kernel, True, chunks),
+            functools.partial(finish_kernel, True, split, chunks),
             "finish_other",
             [tokens] * 4,
-            (*fixed, other, *done),
-            [vmem] * 17,
+            (*fixed, kt_other, qt_other, *other, *done),
+            [vmem] * 18,
             [hbm] * 4,
             flops=8 * half * product,
             scratch=[pltpu.VMEM(part.shape, BF16)] * 4 + [pltpu.SemaphoreType.DMA((4, chunks + 1))],

time: 32.1 us -> 31.6 us (0.984)
  waiting for transfers between devices: 3.7 us -> 2.94 us
    ppermute x1 -> x2, waiting for transfers between devices: 1.13 us -> 0.76 us  [per_device(): other.append(lax.ppermute(theirs, 'seq', swap))]
    pallas_call x10 -> x11, Pallas kernels: 8.2 us -> 8.37 us  [call(): pl.pallas_call(kernel, in_specs=specs, out_specs=out_specs or [vmem] * le...]
  transfers between devices with their start and end apart: 15 -> 16, of which waited for: 5 -> 5; matrix products, arithmetic and copies ran while one was open for 0% -> 0% of each run, Pallas kernels for 13% -> 15%
where the time goes in v7:
time: 31.6 us; the launch traced here: 31.5 us
  starting transfers between devices  18.8 us (59%)
  Pallas kernels  8.37 us (26%)
  waiting for transfers between devices  2.94 us (9%)
  between operations  0.75 us (2%)
  local copies, waits for them, and re-layouts  0.65 us (2%)
    ppermute x12, starting transfers between devices, trade(): lax.ppermute(parts[d], 'seq', [(i, i ^ 2 * PARTNERS[d]) for i in range(n)])  15.5 us
    pallas_call x11, Pallas kernels, call(): pl.pallas_call(kernel, in_specs=specs, out_specs=out_specs or [vmem] * le...  8.37 us
    ppermute x1, starting transfers between devices, per_device(): enter = lax.ppermute(edge(0), 'seq', up + down)  2.65 us
    ppermute x12, waiting for transfers between devices, trade(): lax.ppermute(parts[d], 'seq', [(i, i ^ 2 * PARTNERS[d]) for i in range(n)])  1.81 us
    ppermute x2, waiting for transfers between devices, per_device(): other.append(lax.ppermute(theirs, 'seq', swap))  0.76 us
    unnamed x2, local copies, waits for them, and re-layouts  0.65 us
  transfers between devices with their start and end apart: 16, of which 5 were waited for; matrix products, arithmetic and copies ran while one was open for 0% of the time, Pallas kernels for 15%

profile of v7, /device:TPU:0, one launch (start us, length us, event | category | flops | bytes accessed | tf_op | source)
XLA Modules:
  0.0 31.5 jit_solution(17484110045161617664)
XLA Ops:
  0.6 0.6 %copy-done = s32[8]{0:T(128)S(1)} copy-done((s32[8]{0:T(128)S(1)}, s32[8]{0:T(128)}, u32[]{:S(2)}) %copy-start) | copy-done | bytes 56
  1.3 1.9 %send.1 = (s32[8]{0:T(128)S(1)}, bf16[2,8,128,128]{3,2,1,0:T(8,128)(2,1)S(1)}, bf16[128,2048]{1,0:T(8,128)(2,1)S(1)}, bf16[128,2048]{1,0:T(8,128)(2,1)S(1)}, bf1...) custom-call(s32[8]{0:T(128)S(1)} %copy-done, ...), custom_call_target="tpu_custom_call" | custom-call | flops 67108864 | bytes 5374016 | tf_op jit(solution)/shard_map/send/pallas_call | solution.py:388
  3.2 0.5 %collective-permute-start = (bf16[2,8,128,128]{3,2,1,0:T(8,128)(2,1)S(1)}, bf16[2,8,128,128]{3,2,1,0:T(8,128)(2,1)S(1)}, u32[]{:S(2)}, u32[]{:S(2)}) collective-permute-start(bf16[2,8,128,128]{3,2,1,0:T(8,128)(2,1)S(1)} %get-tuple-element.65), channel_id=1, source_target_pairs={{0,1},{1,0},{2,3},{3,2},{4,5},{5,4},{6,7},{7,6},{8,9},{9,8},{10,11... | collective-permute-start | bytes 1572872 | tf_op jit(solution)/shard_map/ppermute | solution.py:418
  3.7 1.2 %keep.1 = (bf16[2,8,128,128]{3,2,1,0:T(8,128)(2,1)S(1)}, bf16[8,128,128]{2,1,0:T(8,128)(2,1)S(1)}, bf16[8,128,128]{2,1,0:T(8,128)(2,1)S(1)}, f32[64,128]{1,0:T(8,128)S(1)}) custom-call(s32[8]{0:T(128)S(1)} %get-tuple-element.51.len_hbm, bf16[128,2048]{1,0:T(8,128)(2,1)S(1)} %get-tuple-element.48.q_ref.refs_0_, ...), custom_call_target="tpu_custom_call" | custom-call | flops 67108864 | bytes 3309600 | tf_op jit(solution)/shard_map/keep/pallas_call | solution.py:388
  4.9 0.4 %collective-permute-done.got_ref = bf16[2,8,128,128]{3,2,1,0:T(8,128)(2,1)S(1)} collective-permute-done((bf16[2,8,128,128]{3,2,1,0:T(8,128)(2,1)S(1)}, bf16[2,8,128,128]{3,2,1,0:T(8,128)(2,1)S(1)}, u32[]{:S(2)}, u32[]{:S(2)}) %collective-permute-start) | collective-permute-done | bytes 524320 | tf_op jit(solution)/shard_map/ppermute | solution.py:418
  5.3 0.2 pair.1
  5.5 4.0 %collective-permute-start.1 = (bf16[2,128,128]{2,1,0:T(8,128)(2,1)S(1)}, bf16[2,128,128]{2,1,0:T(8,128)(2,1)S(1)}, u32[]{:S(2)}, u32[]{:S(2)}) collective-permute-start(bf16[2,128,128]{2,1,0:T(8,128)(2,1)S(1)} %get-tuple-element.67), channel_id=1, source_target_pairs={{0,6},{1,7},{2,4},{3,5},{4,2},{5,3},{6,0},{7,1},{8,14},{9,15},{10,... | collective-permute-start | bytes 196616 | tf_op jit(solution)/shard_map/ppermute | solution.py:450
  9.4 0.5 %collective-permute-start.2 = (bf16[2,128,128]{2,1,0:T(8,128)(2,1)S(1)}, bf16[2,128,128]{2,1,0:T(8,128)(2,1)S(1)}, u32[]{:S(2)}, u32[]{:S(2)}) collective-permute-start(bf16[2,128,128]{2,1,0:T(8,128)(2,1)S(1)} %get-tuple-element.68), channel_id=1, source_target_pairs={{0,2},{1,3},{2,0},{3,1},{4,6},{5,7},{6,4},{7,5},{8,10},{9,11},{10,... | collective-permute-start | bytes 196616 | tf_op jit(solution)/shard_map/ppermute | solution.py:450
  9.9 0.1 collective-permute-start.3
  10.1 2.8 %collective-permute-start.8 = (bf16[2,128,128]{2,1,0:T(8,128)(2,1)S(1)}, bf16[2,128,128]{2,1,0:T(8,128)(2,1)S(1)}, u32[]{:S(2)}, u32[]{:S(2)}) collective-permute-start(bf16[2,128,128]{2,1,0:T(8,128)(2,1)S(1)} %get-tuple-element.76), channel_id=1, source_target_pairs={{0,6},{1,7},{2,4},{3,5},{4,2},{5,3},{6,0},{7,1},{8,14},{9,15},{10,... | collective-permute-start | bytes 196616 | tf_op jit(solution)/shard_map/ppermute | solution.py:450
  12.9 0.5 %collective-permute-start.9 = (bf16[2,128,128]{2,1,0:T(8,128)(2,1)S(1)}, bf16[2,128,128]{2,1,0:T(8,128)(2,1)S(1)}, u32[]{:S(2)}, u32[]{:S(2)}) collective-permute-start(bf16[2,128,128]{2,1,0:T(8,128)(2,1)S(1)} %get-tuple-element.77), channel_id=1, source_target_pairs={{0,2},{1,3},{2,0},{3,1},{4,6},{5,7},{6,4},{7,5},{8,10},{9,11},{10,... | collective-permute-start | bytes 196616 | tf_op jit(solution)/shard_map/ppermute | solution.py:450
  13.4 0.4 %collective-permute-start.10 = (bf16[2,128,128]{2,1,0:T(8,128)(2,1)S(1)}, bf16[2,128,128]{2,1,0:T(8,128)(2,1)S(1)}, u32[]{:S(2)}, u32[]{:S(2)}) collective-permute-start(bf16[2,128,128]{2,1,0:T(8,128)(2,1)S(1)} %get-tuple-element.78), channel_id=1, source_target_pairs={{0,4},{1,5},{2,6},{3,7},{4,0},{5,1},{6,2},{7,3},{8,12},{9,13},{10,... | collective-permute-start | bytes 196616 | tf_op jit(solution)/shard_map/ppermute | solution.py:450
  13.8 0.8 %collective-permute-done.3.refs_3_.s3 = bf16[2,128,128]{2,1,0:T(8,128)(2,1)S(1)} collective-permute-done((bf16[2,128,128]{2,1,0:T(8,128)(2,1)S(1)}, bf16[2,128,128]{2,1,0:T(8,128)(2,1)S(1)}, u32[]{:S(2)}, u32[]{:S(2)}) %collective-permute-start.3) | collective-permute-done | bytes 65568 | tf_op jit(solution)/shard_map/ppermute | solution.py:450
  14.7 2.6 %collective-permute-start.11 = (bf16[2,128,128]{2,1,0:T(8,128)(2,1)S(1)}, bf16[2,128,128]{2,1,0:T(8,128)(2,1)S(1)}, u32[]{:S(2)}, u32[]{:S(2)}) collective-permute-start(bf16[2,128,128]{2,1,0:T(8,128)(2,1)S(1)} %totals.1), channel_id=1, source_target_pairs={{0,8},{1,9},{2,10},{3,11},{4,12},{5,13},{6,14},{7,15},{8,0},{9,1},... | collective-permute-start | bytes 196616 | tf_op jit(solution)/shard_map/ppermute | solution.py:474
  17.4 0.1 scan.2
  17.5 1.8 %collective-permute-start.4 = (bf16[2,128,128]{2,1,0:T(8,128)(2,1)S(1)}, bf16[2,128,128]{2,1,0:T(8,128)(2,1)S(1)}, u32[]{:S(2)}, u32[]{:S(2)}) collective-permute-start(bf16[2,128,128]{2,1,0:T(8,128)(2,1)S(1)} %get-tuple-element.71), channel_id=1, source_target_pairs={{0,6},{1,7},{2,4},{3,5},{4,2},{5,3},{6,0},{7,1},{8,14},{9,15},{10,... | collective-permute-start | bytes 196616 | tf_op jit(solution)/shard_map/ppermute | solution.py:450
  19.3 0.5 %collective-permute-start.5 = (bf16[2,128,128]{2,1,0:T(8,128)(2,1)S(1)}, bf16[2,128,128]{2,1,0:T(8,128)(2,1)S(1)}, u32[]{:S(2)}, u32[]{:S(2)}) collective-permute-start(bf16[2,128,128]{2,1,0:T(8,128)(2,1)S(1)} %get-tuple-element.72), channel_id=1, source_target_pairs={{0,2},{1,3},{2,0},{3,1},{4,6},{5,7},{6,4},{7,5},{8,10},{9,11},{10,... | collective-permute-start | bytes 196616 | tf_op jit(solution)/shard_map/ppermute | solution.py:450
  19.8 1.2 %collective-permute-start.6 = (bf16[2,128,128]{2,1,0:T(8,128)(2,1)S(1)}, bf16[2,128,128]{2,1,0:T(8,128)(2,1)S(1)}, u32[]{:S(2)}, u32[]{:S(2)}) collective-permute-start(bf16[2,128,128]{2,1,0:T(8,128)(2,1)S(1)} %get-tuple-element.73), channel_id=1, source_target_pairs={{0,4},{1,5},{2,6},{3,7},{4,0},{5,1},{6,2},{7,3},{8,12},{9,13},{10,... | collective-permute-start | bytes 196616 | tf_op jit(solution)/shard_map/ppermute | solution.py:450
  21.1 0.2 scan.3
  21.2 1.8 %collective-permute-start.12 = (bf16[2,128,128]{2,1,0:T(8,128)(2,1)S(1)}, bf16[2,128,128]{2,1,0:T(8,128)(2,1)S(1)}, u32[]{:S(2)}, u32[]{:S(2)}) collective-permute-start(bf16[2,128,128]{2,1,0:T(8,128)(2,1)S(1)} %get-tuple-element.80), channel_id=1, source_target_pairs={{0,6},{1,7},{2,4},{3,5},{4,2},{5,3},{6,0},{7,1},{8,14},{9,15},{10,... | collective-permute-start | bytes 196616 | tf_op jit(solution)/shard_map/ppermute | solution.py:450
  23.1 0.6 %collective-permute-start.13 = (bf16[2,128,128]{2,1,0:T(8,128)(2,1)S(1)}, bf16[2,128,128]{2,1,0:T(8,128)(2,1)S(1)}, u32[]{:S(2)}, u32[]{:S(2)}) collective-permute-start(bf16[2,128,128]{2,1,0:T(8,128)(2,1)S(1)} %get-tuple-element.81), channel_id=1, source_target_pairs={{0,2},{1,3},{2,0},{3,1},{4,6},{5,7},{6,4},{7,5},{8,10},{9,11},{10,... | collective-permute-start | bytes 196616 | tf_op jit(solution)/shard_map/ppermute | solution.py:450
  23.7 1.1 %collective-permute-start.14 = (bf16[2,128,128]{2,1,0:T(8,128)(2,1)S(1)}, bf16[2,128,128]{2,1,0:T(8,128)(2,1)S(1)}, u32[]{:S(2)}, u32[]{:S(2)}) collective-permute-start(bf16[2,128,128]{2,1,0:T(8,128)(2,1)S(1)} %get-tuple-element.82), channel_id=1, source_target_pairs={{0,4},{1,5},{2,6},{3,7},{4,0},{5,1},{6,2},{7,3},{8,12},{9,13},{10,... | collective-permute-start | bytes 196616 | tf_op jit(solution)/shard_map/ppermute | solution.py:450
  24.8 1.9 %local.1 = (bf16[16,128,128]{2,1,0:T(8,128)(2,1)S(1)}, bf16[16,128,128]{2,1,0:T(8,128)(2,1)S(1)}, bf16[16,128,128]{2,1,0:T(8,128)(2,1)S(1)}, bf16[16,128,128]{2,...) custom-call(s32[8]{0:T(128)S(1)} %get-tuple-element.51.len_hbm, ...), custom_call_target="tpu_custom_call" | custom-call | flops 268435456 | bytes 4784160 | tf_op jit(solution)/shard_map/local/pallas_call | solution.py:388
  26.7 0.2 post.2
  26.9 0.1 collective-permute-start.7
  27.0 0.3 %collective-permute-done.13.refs_2_ = bf16[2,128,128]{2,1,0:T(8,128)(2,1)S(1)} collective-permute-done((bf16[2,128,128]{2,1,0:T(8,128)(2,1)S(1)}, bf16[2,128,128]{2,1,0:T(8,128)(2,1)S(1)}, u32[]{:S(2)}, u32[]{:S(2)}) %collective-permute-start.13) | collective-permute-done | bytes 65568 | tf_op jit(solution)/shard_map/ppermute | solution.py:450
  27.3 0.6 %collective-permute-done.14.refs_3_ = bf16[2,128,128]{2,1,0:T(8,128)(2,1)S(1)} collective-permute-done((bf16[2,128,128]{2,1,0:T(8,128)(2,1)S(1)}, bf16[2,128,128]{2,1,0:T(8,128)(2,1)S(1)}, u32[]{:S(2)}, u32[]{:S(2)}) %collective-permute-start.14) | collective-permute-done | bytes 65568 | tf_op jit(solution)/shard_map/ppermute | solution.py:450
  28.0 0.2 post.3
  28.2 0.1 collective-permute-start.15
  28.3 0.8 %finish_mine.1 = (bf16[128,1024]{1,0:T(8,128)(2,1)S(1)}, bf16[128,1024]{1,0:T(8,128)(2,1)S(1)}, bf16[128,1024]{1,0:T(8,128)(2,1)S(1)}, bf16[128,1024]{1,0:T(8,128)(2,1)S(1)}) custom-call(bf16[128,2048]{1,0:T(8,128)(2,1)S(1)} %get-tuple-element.48.q_ref.refs_0_, bf16[128,2048]{1,0:T(8,128)(2,1)S(1)} %get-tuple-element.49.k_ref.refs_1_, ...), custom_call_target="tpu_custom_call" | custom-call | flops 268435456 | bytes 6422528 | tf_op jit(solution)/shard_map/finish_mine/pallas_call | solution.py:388
  29.0 0.8 %collective-permute-done.15.refs_13_ = bf16[8,128,128]{2,1,0:T(8,128)(2,1)S(1)} collective-permute-done((bf16[8,128,128]{2,1,0:T(8,128)(2,1)S(1)}, bf16[8,128,128]{2,1,0:T(8,128)(2,1)S(1)}, u32[]{:S(2)}, u32[]{:S(2)}) %collective-permute-start.15) | collective-permute-done | bytes 262176 | tf_op jit(solution)/shard_map/ppermute | solution.py:488
  29.8 1.7 %finish_other.1 = (bf16[128,2048]{1,0:T(8,128)(2,1)}, bf16[128,2048]{1,0:T(8,128)(2,1)}, bf16[128,2048]{1,0:T(8,128)(2,1)}, bf16[128,2048]{1,0:T(8,128)(2,1)}) custom-call(bf16[128,2048]{1,0:T(8,128)(2,1)S(1)} %get-tuple-element.48.q_ref.refs_0_, bf16[128,2048]{1,0:T(8,128)(2,1)S(1)} %get-tuple-element.49.k_ref.refs_1_, ...), custom_call_target="tpu_custom_call" | custom-call | flops 268435456 | bytes 8519680 | tf_op jit(solution)/shard_map/finish_other/pallas_call | solution.py:388
  (13 shorter events, 0.1 us)
Async XLA Ops:
  0.6 0.7 %copy-start = (s32[8]{0:T(128)S(1)}, s32[8]{0:T(128)}, u32[]{:S(2)}) copy-start(s32[8]{0:T(128)} %len_hbm.1) | copy-start | bytes 100
  3.2 2.1 %collective-permute-start = (bf16[2,8,128,128]{3,2,1,0:T(8,128)(2,1)S(1)}, bf16[2,8,128,128]{3,2,1,0:T(8,128)(2,1)S(1)}, u32[]{:S(2)}, u32[]{:S(2)}) collective-permute-start(bf16[2,8,128,128]{3,2,1,0:T(8,128)(2,1)S(1)} %get-tuple-element.65), channel_id=1, source_target_pairs={{0,1},{1,0},{2,3},{3,2},{4,5},{5,4},{6,7},{7,6},{8,9},{9,8},{10,11... | collective-permute-start | bytes 1572872 | tf_op jit(solution)/shard_map/ppermute | solution.py:418
  5.5 8.0 %collective-permute-start.1 = (bf16[2,128,128]{2,1,0:T(8,128)(2,1)S(1)}, bf16[2,128,128]{2,1,0:T(8,128)(2,1)S(1)}, u32[]{:S(2)}, u32[]{:S(2)}) collective-permute-start(bf16[2,128,128]{2,1,0:T(8,128)(2,1)S(1)} %get-tuple-element.67), channel_id=1, source_target_pairs={{0,6},{1,7},{2,4},{3,5},{4,2},{5,3},{6,0},{7,1},{8,14},{9,15},{10,... | collective-permute-start | bytes 196616 | tf_op jit(solution)/shard_map/ppermute | solution.py:450
  9.4 4.4 %collective-permute-start.2 = (bf16[2,128,128]{2,1,0:T(8,128)(2,1)S(1)}, bf16[2,128,128]{2,1,0:T(8,128)(2,1)S(1)}, u32[]{:S(2)}, u32[]{:S(2)}) collective-permute-start(bf16[2,128,128]{2,1,0:T(8,128)(2,1)S(1)} %get-tuple-element.68), channel_id=1, source_target_pairs={{0,2},{1,3},{2,0},{3,1},{4,6},{5,7},{6,4},{7,5},{8,10},{9,11},{10,... | collective-permute-start | bytes 196616 | tf_op jit(solution)/shard_map/ppermute | solution.py:450
  9.9 4.7 %collective-permute-start.3 = (bf16[2,128,128]{2,1,0:T(8,128)(2,1)S(1)}, bf16[2,128,128]{2,1,0:T(8,128)(2,1)S(1)}, u32[]{:S(2)}, u32[]{:S(2)}) collective-permute-start(bf16[2,128,128]{2,1,0:T(8,128)(2,1)S(1)} %get-tuple-element.69), channel_id=1, source_target_pairs={{0,4},{1,5},{2,6},{3,7},{4,0},{5,1},{6,2},{7,3},{8,12},{9,13},{10,... | collective-permute-start | bytes 196616 | tf_op jit(solution)/shard_map/ppermute | solution.py:450
  10.1 9.3 %collective-permute-start.8 = (bf16[2,128,128]{2,1,0:T(8,128)(2,1)S(1)}, bf16[2,128,128]{2,1,0:T(8,128)(2,1)S(1)}, u32[]{:S(2)}, u32[]{:S(2)}) collective-permute-start(bf16[2,128,128]{2,1,0:T(8,128)(2,1)S(1)} %get-tuple-element.76), channel_id=1, source_target_pairs={{0,6},{1,7},{2,4},{3,5},{4,2},{5,3},{6,0},{7,1},{8,14},{9,15},{10,... | collective-permute-start | bytes 196616 | tf_op jit(solution)/shard_map/ppermute | solution.py:450
  12.9 6.9 %collective-permute-start.9 = (bf16[2,128,128]{2,1,0:T(8,128)(2,1)S(1)}, bf16[2,128,128]{2,1,0:T(8,128)(2,1)S(1)}, u32[]{:S(2)}, u32[]{:S(2)}) collective-permute-start(bf16[2,128,128]{2,1,0:T(8,128)(2,1)S(1)} %get-tuple-element.77), channel_id=1, source_target_pairs={{0,2},{1,3},{2,0},{3,1},{4,6},{5,7},{6,4},{7,5},{8,10},{9,11},{10,... | collective-permute-start | bytes 196616 | tf_op jit(solution)/shard_map/ppermute | solution.py:450
  13.4 7.6 %collective-permute-start.10 = (bf16[2,128,128]{2,1,0:T(8,128)(2,1)S(1)}, bf16[2,128,128]{2,1,0:T(8,128)(2,1)S(1)}, u32[]{:S(2)}, u32[]{:S(2)}) collective-permute-start(bf16[2,128,128]{2,1,0:T(8,128)(2,1)S(1)} %get-tuple-element.78), channel_id=1, source_target_pairs={{0,4},{1,5},{2,6},{3,7},{4,0},{5,1},{6,2},{7,3},{8,12},{9,13},{10,... | collective-permute-start | bytes 196616 | tf_op jit(solution)/shard_map/ppermute | solution.py:450
  14.7 6.3 %collective-permute-start.11 = (bf16[2,128,128]{2,1,0:T(8,128)(2,1)S(1)}, bf16[2,128,128]{2,1,0:T(8,128)(2,1)S(1)}, u32[]{:S(2)}, u32[]{:S(2)}) collective-permute-start(bf16[2,128,128]{2,1,0:T(8,128)(2,1)S(1)} %totals.1), channel_id=1, source_target_pairs={{0,8},{1,9},{2,10},{3,11},{4,12},{5,13},{6,14},{7,15},{8,0},{9,1},... | collective-permute-start | bytes 196616 | tf_op jit(solution)/shard_map/ppermute | solution.py:474
  17.5 6.2 %collective-permute-start.4 = (bf16[2,128,128]{2,1,0:T(8,128)(2,1)S(1)}, bf16[2,128,128]{2,1,0:T(8,128)(2,1)S(1)}, u32[]{:S(2)}, u32[]{:S(2)}) collective-permute-start(bf16[2,128,128]{2,1,0:T(8,128)(2,1)S(1)} %get-tuple-element.71), channel_id=1, source_target_pairs={{0,6},{1,7},{2,4},{3,5},{4,2},{5,3},{6,0},{7,1},{8,14},{9,15},{10,... | collective-permute-start | bytes 196616 | tf_op jit(solution)/shard_map/ppermute | solution.py:450
  19.3 7.3 %collective-permute-start.5 = (bf16[2,128,128]{2,1,0:T(8,128)(2,1)S(1)}, bf16[2,128,128]{2,1,0:T(8,128)(2,1)S(1)}, u32[]{:S(2)}, u32[]{:S(2)}) collective-permute-start(bf16[2,128,128]{2,1,0:T(8,128)(2,1)S(1)} %get-tuple-element.72), channel_id=1, source_target_pairs={{0,2},{1,3},{2,0},{3,1},{4,6},{5,7},{6,4},{7,5},{8,10},{9,11},{10,... | collective-permute-start | bytes 196616 | tf_op jit(solution)/shard_map/ppermute | solution.py:450
  19.8 6.8 %collective-permute-start.6 = (bf16[2,128,128]{2,1,0:T(8,128)(2,1)S(1)}, bf16[2,128,128]{2,1,0:T(8,128)(2,1)S(1)}, u32[]{:S(2)}, u32[]{:S(2)}) collective-permute-start(bf16[2,128,128]{2,1,0:T(8,128)(2,1)S(1)} %get-tuple-element.73), channel_id=1, source_target_pairs={{0,4},{1,5},{2,6},{3,7},{4,0},{5,1},{6,2},{7,3},{8,12},{9,13},{10,... | collective-permute-start | bytes 196616 | tf_op jit(solution)/shard_map/ppermute | solution.py:450
  21.2 5.8 %collective-permute-start.12 = (bf16[2,128,128]{2,1,0:T(8,128)(2,1)S(1)}, bf16[2,128,128]{2,1,0:T(8,128)(2,1)S(1)}, u32[]{:S(2)}, u32[]{:S(2)}) collective-permute-start(bf16[2,128,128]{2,1,0:T(8,128)(2,1)S(1)} %get-tuple-element.80), channel_id=1, source_target_pairs={{0,6},{1,7},{2,4},{3,5},{4,2},{5,3},{6,0},{7,1},{8,14},{9,15},{10,... | collective-permute-start | bytes 196616 | tf_op jit(solution)/shard_map/ppermute | solution.py:450
  23.1 4.3 %collective-permute-start.13 = (bf16[2,128,128]{2,1,0:T(8,128)(2,1)S(1)}, bf16[2,128,128]{2,1,0:T(8,128)(2,1)S(1)}, u32[]{:S(2)}, u32[]{:S(2)}) collective-permute-start(bf16[2,128,128]{2,1,0:T(8,128)(2,1)S(1)} %get-tuple-element.81), channel_id=1, source_target_pairs={{0,2},{1,3},{2,0},{3,1},{4,6},{5,7},{6,4},{7,5},{8,10},{9,11},{10,... | collective-permute-start | bytes 196616 | tf_op jit(solution)/shard_map/ppermute | solution.py:450
  23.7 4.3 %collective-permute-start.14 = (bf16[2,128,128]{2,1,0:T(8,128)(2,1)S(1)}, bf16[2,128,128]{2,1,0:T(8,128)(2,1)S(1)}, u32[]{:S(2)}, u32[]{:S(2)}) collective-permute-start(bf16[2,128,128]{2,1,0:T(8,128)(2,1)S(1)} %get-tuple-element.82), channel_id=1, source_target_pairs={{0,4},{1,5},{2,6},{3,7},{4,0},{5,1},{6,2},{7,3},{8,12},{9,13},{10,... | collective-permute-start | bytes 196616 | tf_op jit(solution)/shard_map/ppermute | solution.py:450
  26.9 2.1 %collective-permute-start.7 = (bf16[8,128,128]{2,1,0:T(8,128)(2,1)S(1)}, bf16[8,128,128]{2,1,0:T(8,128)(2,1)S(1)}, u32[]{:S(2)}, u32[]{:S(2)}) collective-permute-start(bf16[8,128,128]{2,1,0:T(8,128)(2,1)S(1)} %get-tuple-element.74), channel_id=1, source_target_pairs={{0,1},{1,0},{2,3},{3,2},{4,5},{5,4},{6,7},{7,6},{8,9},{9,8},{10,11... | collective-permute-start | bytes 786440 | tf_op jit(solution)/shard_map/ppermute | solution.py:488
  28.2 1.6 %collective-permute-start.15 = (bf16[8,128,128]{2,1,0:T(8,128)(2,1)S(1)}, bf16[8,128,128]{2,1,0:T(8,128)(2,1)S(1)}, u32[]{:S(2)}, u32[]{:S(2)}) collective-permute-start(bf16[8,128,128]{2,1,0:T(8,128)(2,1)S(1)} %get-tuple-element.83), channel_id=1, source_target_pairs={{0,1},{1,0},{2,3},{3,2},{4,5},{5,4},{6,7},{7,6},{8,9},{9,8},{10,11... | collective-permute-start | bytes 786440 | tf_op jit(solution)/shard_map/ppermute | solution.py:488

commit v8 on v7

--- a/solution.py
+++ b/solution.py
@@ -9,7 +9,7 @@
 
 HD = 128
 PAIRS = 4
-PARTNERS = (0, 3, 1, 2)
+PARTNERS = ((0, 3, 1, 2), (0, 3, 2, 1))
 TEAM = 2 * PAIRS
 F32 = jnp.float32
 BF16 = jnp.bfloat16
@@ -141,10 +141,15 @@
     len_pass.wait()
 
 
+def slots():
+    me = lax.axis_index("seq")
+    pair, odd = lax.rem(me, TEAM) // 2, lax.rem(me, 2) == 1
+    return [pair ^ jnp.where(odd, b, a) for a, b in zip(*PARTNERS)]
+
+
 def coefficients(starts, rows, n, coef_ref):
     me = lax.axis_index("seq")
     core = lax.rem(me, 2)
-    pair = lax.rem(me, TEAM) // 2
     base = me - lax.rem(me, TEAM)
     one = jnp.int32(1)
 
@@ -158,7 +163,7 @@
         return (a == b).astype(jnp.int32)
 
     team_low, team_high = both(base), both(base + TEAM)
-    pairs = [pair ^ d for d in PARTNERS]
+    pairs = slots()
     low = [both(base + 2 * p) for p in pairs]
     high = [both(base + 2 * p + 2) for p in pairs]
     middle = both(me - core + 1)
@@ -246,16 +251,17 @@
     mask_ref[1] = jnp.where(suffix, one, none).astype(BF16)
     col = first + lax.broadcasted_iota(jnp.int32, (rows, HD), 1)
     same = (col <= pos) & (col >= begin)
-    same_t = jnp.where(same, one, none).T > 0.5
     for h in range(width // HD):
         cols = pl.ds(h * HD, HD)
         q, k, v = q_ref[:, cols], k_ref[:, cols], v_ref[:, cols]
         g = (g_ref[:, cols].astype(F32) * inv_root).astype(BF16)
         sg_ref[:, cols] = g
-        w_ref[h] = jnp.where(same, dot(q, k, (1, 1)), 0.0).astype(BF16)
-        wt_ref[h] = jnp.where(same_t, dot(k, q, (1, 1)), 0.0).astype(BF16)
-        dw_ref[h] = jnp.where(same, dot(g, v, (1, 1)), 0.0).astype(BF16)
-        dwt_ref[h] = jnp.where(same_t, dot(v, g, (1, 1)), 0.0).astype(BF16)
+        w = jnp.where(same, dot(q, k, (1, 1)), 0.0).astype(BF16)
+        w_ref[h] = w
+        wt_ref[h] = w.T
+        dw = jnp.where(same, dot(g, v, (1, 1)), 0.0).astype(BF16)
+        dw_ref[h] = dw
+        dwt_ref[h] = dw.T
 
 
 def coef(coef_ref, row):
@@ -271,13 +277,13 @@
 
 def pair_kernel(split, coef_ref, keep_ref, got_ref, *out_refs):
     per = out_refs[0].shape[0]
-    pair = lax.rem(lax.axis_index("seq"), TEAM) // 2
+    pairs = slots()
     for which in range(2):
         kind = kind_of(which, split)
         ca, cb = coef(coef_ref, KEEP_F + 2 * kind), coef(coef_ref, GOT_F + 2 * kind)
         for d in range(PAIRS):
             for i in range(per):
-                h = (pair ^ PARTNERS[d]) * per + i
+                h = pairs[d] * per + i
                 both = keep_ref[kind, h].astype(F32) * ca + got_ref[kind, h].astype(F32) * cb
                 out_refs[which * PAIRS + d][i] = both.astype(BF16)
 
@@ -307,13 +313,13 @@
 def post_kernel(which, split, coef_ref, keep_ref, got_ref, *refs):
     mine_ref, theirs_ref = refs[-2:]
     per = refs[0].shape[0]
-    pair = lax.rem(lax.axis_index("seq"), TEAM) // 2
+    pairs = slots()
     kind = kind_of(which, split)
     m0, m1 = coef(coef_ref, MINE_F + 2 * kind), coef(coef_ref, MINE_F + 2 * kind + 1)
     t0, t1 = coef(coef_ref, THEIRS_F + 2 * kind), coef(coef_ref, THEIRS_F + 2 * kind + 1)
     for d in range(PAIRS):
         for i in range(per):
-            h = (pair ^ PARTNERS[d]) * per + i
+            h = pairs[d] * per + i
             came = refs[d][i].astype(F32)
             theirs_ref[h] = (came * t0 + keep_ref[kind, h].astype(F32) * t1).astype(BF16)
             mine_ref[h] = (came * m0 + got_ref[kind, h].astype(F32) * m1).astype(BF16)
@@ -432,7 +438,7 @@
         [mats] * 4 + [tokens, shape(2, rows, HD)],
         (doc_lengths, queries, keys, values, grad_out),
         [hbm] + [vmem] * 4,
-        flops=4 * heads * product,
+        flops=2 * heads * product,
         scratch=lengths,
     )
     owned = shape(per, HD, HD)
@@ -447,7 +453,7 @@
 
     def trade(parts):
         return [parts[0]] + [
-            lax.ppermute(parts[d], "seq", [(i, i ^ (2 * PARTNERS[d])) for i in range(n)])
+            lax.ppermute(parts[d], "seq", [(i, i ^ (2 * PARTNERS[i % 2][d])) for i in range(n)])
             for d in range(1, PAIRS)
         ]
 

time: 31.6 us -> 32 us (1.013)
  Pallas kernels: 8.37 us -> 7.85 us
  starting transfers between devices: 18.8 us -> 19.3 us
  waiting for transfers between devices: 2.94 us -> 3.32 us
    ppermute x12, starting transfers between devices: 15.5 us -> 16 us  [trade(): lax.ppermute(parts[d], 'seq', [(i, i ^ 2 * PARTNERS[i % 2][d]) for i in r...]
    pallas_call x11, Pallas kernels: 8.37 us -> 7.85 us  [call(): pl.pallas_call(kernel, in_specs=specs, out_specs=out_specs or [vmem] * le...]
    ppermute x12, waiting for transfers between devices: 1.81 us -> 2.2 us  [trade(): lax.ppermute(parts[d], 'seq', [(i, i ^ 2 * PARTNERS[i % 2][d]) for i in r...]
  transfers between devices with their start and end apart: 16 -> 16, of which waited for: 5 -> 6; matrix products, arithmetic and copies ran while one was open for 0% -> 0% of each run, Pallas kernels for 15% -> 13%
where the time goes in v8:
time: 32 us; the launch traced here: 31.9 us
  starting transfers between devices  19.3 us (60%)
  Pallas kernels  7.85 us (25%)
  waiting for transfers between devices  3.32 us (10%)
  between operations  0.75 us (2%)
  local copies, waits for them, and re-layouts  0.65 us (2%)
    ppermute x12, starting transfers between devices, trade(): lax.ppermute(parts[d], 'seq', [(i, i ^ 2 * PARTNERS[i % 2][d]) for i in r...  16 us
    pallas_call x11, Pallas kernels, call(): pl.pallas_call(kernel, in_specs=specs, out_specs=out_specs or [vmem] * le...  7.85 us
    ppermute x1, starting transfers between devices, per_device(): enter = lax.ppermute(edge(0), 'seq', up + down)  2.64 us
    ppermute x12, waiting for transfers between devices, trade(): lax.ppermute(parts[d], 'seq', [(i, i ^ 2 * PARTNERS[i % 2][d]) for i in r...  2.2 us
    ppermute x2, waiting for transfers between devices, per_device(): other.append(lax.ppermute(theirs, 'seq', swap))  0.76 us
    unnamed x2, local copies, waits for them, and re-layouts  0.65 us
  transfers between devices with their start and end apart: 16, of which 6 were waited for; matrix products, arithmetic and copies ran while one was open for 0% of the time, Pallas kernels for 13%

profile of v8, /device:TPU:0, one launch (start us, length us, event | category | flops | bytes accessed | tf_op | source)
XLA Modules:
  0.0 31.9 jit_solution(11131868594508658243)
XLA Ops:
  0.6 0.6 %copy-done = s32[8]{0:T(128)S(1)} copy-done((s32[8]{0:T(128)S(1)}, s32[8]{0:T(128)}, u32[]{:S(2)}) %copy-start) | copy-done | bytes 56
  1.3 1.9 %send.1 = (s32[8]{0:T(128)S(1)}, bf16[2,8,128,128]{3,2,1,0:T(8,128)(2,1)S(1)}, bf16[128,2048]{1,0:T(8,128)(2,1)S(1)}, bf16[128,2048]{1,0:T(8,128)(2,1)S(1)}, bf1...) custom-call(s32[8]{0:T(128)S(1)} %copy-done, ...), custom_call_target="tpu_custom_call" | custom-call | flops 67108864 | bytes 5374016 | tf_op jit(solution)/shard_map/send/pallas_call | solution.py:394
  3.2 0.5 %collective-permute-start = (bf16[2,8,128,128]{3,2,1,0:T(8,128)(2,1)S(1)}, bf16[2,8,128,128]{3,2,1,0:T(8,128)(2,1)S(1)}, u32[]{:S(2)}, u32[]{:S(2)}) collective-permute-start(bf16[2,8,128,128]{3,2,1,0:T(8,128)(2,1)S(1)} %get-tuple-element.65), channel_id=1, source_target_pairs={{0,1},{1,0},{2,3},{3,2},{4,5},{5,4},{6,7},{7,6},{8,9},{9,8},{10,11... | collective-permute-start | bytes 1572872 | tf_op jit(solution)/shard_map/ppermute | solution.py:424
  3.7 1.2 %keep.1 = (bf16[2,8,128,128]{3,2,1,0:T(8,128)(2,1)S(1)}, bf16[8,128,128]{2,1,0:T(8,128)(2,1)S(1)}, bf16[8,128,128]{2,1,0:T(8,128)(2,1)S(1)}, f32[64,128]{1,0:T(8,128)S(1)}) custom-call(s32[8]{0:T(128)S(1)} %get-tuple-element.51.len_hbm, bf16[128,2048]{1,0:T(8,128)(2,1)S(1)} %get-tuple-element.48.q_ref.refs_0_, ...), custom_call_target="tpu_custom_call" | custom-call | flops 67108864 | bytes 3309600 | tf_op jit(solution)/shard_map/keep/pallas_call | solution.py:394
  4.9 0.4 %collective-permute-done.got_ref = bf16[2,8,128,128]{3,2,1,0:T(8,128)(2,1)S(1)} collective-permute-done((bf16[2,8,128,128]{3,2,1,0:T(8,128)(2,1)S(1)}, bf16[2,8,128,128]{3,2,1,0:T(8,128)(2,1)S(1)}, u32[]{:S(2)}, u32[]{:S(2)}) %collective-permute-start) | collective-permute-done | bytes 524320 | tf_op jit(solution)/shard_map/ppermute | solution.py:424
  5.3 0.2 pair.1
  5.5 4.0 %collective-permute-start.1 = (bf16[2,128,128]{2,1,0:T(8,128)(2,1)S(1)}, bf16[2,128,128]{2,1,0:T(8,128)(2,1)S(1)}, u32[]{:S(2)}, u32[]{:S(2)}) collective-permute-start(bf16[2,128,128]{2,1,0:T(8,128)(2,1)S(1)} %get-tuple-element.67), channel_id=1, source_target_pairs={{0,6},{1,7},{2,4},{3,5},{4,2},{5,3},{6,0},{7,1},{8,14},{9,15},{10,... | collective-permute-start | bytes 196616 | tf_op jit(solution)/shard_map/ppermute | solution.py:456
  9.4 0.5 %collective-permute-start.2 = (bf16[2,128,128]{2,1,0:T(8,128)(2,1)S(1)}, bf16[2,128,128]{2,1,0:T(8,128)(2,1)S(1)}, u32[]{:S(2)}, u32[]{:S(2)}) collective-permute-start(bf16[2,128,128]{2,1,0:T(8,128)(2,1)S(1)} %get-tuple-element.68), channel_id=1, source_target_pairs={{0,2},{1,5},{2,0},{3,7},{4,6},{5,1},{6,4},{7,3},{8,10},{9,13},{10,... | collective-permute-start | bytes 196616 | tf_op jit(solution)/shard_map/ppermute | solution.py:456
  9.9 0.1 collective-permute-start.3
  10.1 2.8 %collective-permute-start.8 = (bf16[2,128,128]{2,1,0:T(8,128)(2,1)S(1)}, bf16[2,128,128]{2,1,0:T(8,128)(2,1)S(1)}, u32[]{:S(2)}, u32[]{:S(2)}) collective-permute-start(bf16[2,128,128]{2,1,0:T(8,128)(2,1)S(1)} %get-tuple-element.76), channel_id=1, source_target_pairs={{0,6},{1,7},{2,4},{3,5},{4,2},{5,3},{6,0},{7,1},{8,14},{9,15},{10,... | collective-permute-start | bytes 196616 | tf_op jit(solution)/shard_map/ppermute | solution.py:456
  12.9 0.5 %collective-permute-start.9 = (bf16[2,128,128]{2,1,0:T(8,128)(2,1)S(1)}, bf16[2,128,128]{2,1,0:T(8,128)(2,1)S(1)}, u32[]{:S(2)}, u32[]{:S(2)}) collective-permute-start(bf16[2,128,128]{2,1,0:T(8,128)(2,1)S(1)} %get-tuple-element.77), channel_id=1, source_target_pairs={{0,2},{1,5},{2,0},{3,7},{4,6},{5,1},{6,4},{7,3},{8,10},{9,13},{10,... | collective-permute-start | bytes 196616 | tf_op jit(solution)/shard_map/ppermute | solution.py:456
  13.4 0.9 %collective-permute-start.10 = (bf16[2,128,128]{2,1,0:T(8,128)(2,1)S(1)}, bf16[2,128,128]{2,1,0:T(8,128)(2,1)S(1)}, u32[]{:S(2)}, u32[]{:S(2)}) collective-permute-start(bf16[2,128,128]{2,1,0:T(8,128)(2,1)S(1)} %get-tuple-element.78), channel_id=1, source_target_pairs={{0,4},{1,3},{2,6},{3,1},{4,0},{5,7},{6,2},{7,5},{8,12},{9,11},{10,... | collective-permute-start | bytes 196616 | tf_op jit(solution)/shard_map/ppermute | solution.py:456
  14.3 0.1 collective-permute-done.2.refs_2_.s2
  14.4 0.4 %collective-permute-done.3.refs_3_.s3 = bf16[2,128,128]{2,1,0:T(8,128)(2,1)S(1)} collective-permute-done((bf16[2,128,128]{2,1,0:T(8,128)(2,1)S(1)}, bf16[2,128,128]{2,1,0:T(8,128)(2,1)S(1)}, u32[]{:S(2)}, u32[]{:S(2)}) %collective-permute-start.3) | collective-permute-done | bytes 65568 | tf_op jit(solution)/shard_map/ppermute | solution.py:456
  14.8 2.6 %collective-permute-start.11 = (bf16[2,128,128]{2,1,0:T(8,128)(2,1)S(1)}, bf16[2,128,128]{2,1,0:T(8,128)(2,1)S(1)}, u32[]{:S(2)}, u32[]{:S(2)}) collective-permute-start(bf16[2,128,128]{2,1,0:T(8,128)(2,1)S(1)} %totals.1), channel_id=1, source_target_pairs={{0,8},{1,9},{2,10},{3,11},{4,12},{5,13},{6,14},{7,15},{8,0},{9,1},... | collective-permute-start | bytes 196616 | tf_op jit(solution)/shard_map/ppermute | solution.py:480
  17.5 0.1 scan.2
  17.6 1.7 %collective-permute-start.4 = (bf16[2,128,128]{2,1,0:T(8,128)(2,1)S(1)}, bf16[2,128,128]{2,1,0:T(8,128)(2,1)S(1)}, u32[]{:S(2)}, u32[]{:S(2)}) collective-permute-start(bf16[2,128,128]{2,1,0:T(8,128)(2,1)S(1)} %get-tuple-element.71), channel_id=1, source_target_pairs={{0,6},{1,7},{2,4},{3,5},{4,2},{5,3},{6,0},{7,1},{8,14},{9,15},{10,... | collective-permute-start | bytes 196616 | tf_op jit(solution)/shard_map/ppermute | solution.py:456
  19.3 0.8 %collective-permute-start.5 = (bf16[2,128,128]{2,1,0:T(8,128)(2,1)S(1)}, bf16[2,128,128]{2,1,0:T(8,128)(2,1)S(1)}, u32[]{:S(2)}, u32[]{:S(2)}) collective-permute-start(bf16[2,128,128]{2,1,0:T(8,128)(2,1)S(1)} %get-tuple-element.72), channel_id=1, source_target_pairs={{0,2},{1,5},{2,0},{3,7},{4,6},{5,1},{6,4},{7,3},{8,10},{9,13},{10,... | collective-permute-start | bytes 196616 | tf_op jit(solution)/shard_map/ppermute | solution.py:456
  20.2 1.0 %collective-permute-start.6 = (bf16[2,128,128]{2,1,0:T(8,128)(2,1)S(1)}, bf16[2,128,128]{2,1,0:T(8,128)(2,1)S(1)}, u32[]{:S(2)}, u32[]{:S(2)}) collective-permute-start(bf16[2,128,128]{2,1,0:T(8,128)(2,1)S(1)} %get-tuple-element.73), channel_id=1, source_target_pairs={{0,4},{1,3},{2,6},{3,1},{4,0},{5,7},{6,2},{7,5},{8,12},{9,11},{10,... | collective-permute-start | bytes 196616 | tf_op jit(solution)/shard_map/ppermute | solution.py:456
  21.2 0.2 scan.3
  21.3 1.8 %collective-permute-start.12 = (bf16[2,128,128]{2,1,0:T(8,128)(2,1)S(1)}, bf16[2,128,128]{2,1,0:T(8,128)(2,1)S(1)}, u32[]{:S(2)}, u32[]{:S(2)}) collective-permute-start(bf16[2,128,128]{2,1,0:T(8,128)(2,1)S(1)} %get-tuple-element.80), channel_id=1, source_target_pairs={{0,6},{1,7},{2,4},{3,5},{4,2},{5,3},{6,0},{7,1},{8,14},{9,15},{10,... | collective-permute-start | bytes 196616 | tf_op jit(solution)/shard_map/ppermute | solution.py:456
  23.1 1.0 %collective-permute-start.13 = (bf16[2,128,128]{2,1,0:T(8,128)(2,1)S(1)}, bf16[2,128,128]{2,1,0:T(8,128)(2,1)S(1)}, u32[]{:S(2)}, u32[]{:S(2)}) collective-permute-start(bf16[2,128,128]{2,1,0:T(8,128)(2,1)S(1)} %get-tuple-element.81), channel_id=1, source_target_pairs={{0,2},{1,5},{2,0},{3,7},{4,6},{5,1},{6,4},{7,3},{8,10},{9,13},{10,... | collective-permute-start | bytes 196616 | tf_op jit(solution)/shard_map/ppermute | solution.py:456
  24.1 0.8 %collective-permute-start.14 = (bf16[2,128,128]{2,1,0:T(8,128)(2,1)S(1)}, bf16[2,128,128]{2,1,0:T(8,128)(2,1)S(1)}, u32[]{:S(2)}, u32[]{:S(2)}) collective-permute-start(bf16[2,128,128]{2,1,0:T(8,128)(2,1)S(1)} %get-tuple-element.82), channel_id=1, source_target_pairs={{0,4},{1,3},{2,6},{3,1},{4,0},{5,7},{6,2},{7,5},{8,12},{9,11},{10,... | collective-permute-start | bytes 196616 | tf_op jit(solution)/shard_map/ppermute | solution.py:456
  24.9 1.3 %local.1 = (bf16[16,128,128]{2,1,0:T(8,128)(2,1)S(1)}, bf16[16,128,128]{2,1,0:T(8,128)(2,1)S(1)}, bf16[16,128,128]{2,1,0:T(8,128)(2,1)S(1)}, bf16[16,128,128]{2,...) custom-call(s32[8]{0:T(128)S(1)} %get-tuple-element.51.len_hbm, ...), custom_call_target="tpu_custom_call" | custom-call | flops 134217728 | bytes 4784160 | tf_op jit(solution)/shard_map/local/pallas_call | solution.py:394
  26.3 0.2 post.2
  26.6 0.7 %collective-permute-done.13.refs_2_ = bf16[2,128,128]{2,1,0:T(8,128)(2,1)S(1)} collective-permute-done((bf16[2,128,128]{2,1,0:T(8,128)(2,1)S(1)}, bf16[2,128,128]{2,1,0:T(8,128)(2,1)S(1)}, u32[]{:S(2)}, u32[]{:S(2)}) %collective-permute-start.13) | collective-permute-done | bytes 65568 | tf_op jit(solution)/shard_map/ppermute | solution.py:456
  27.4 1.0 %collective-permute-done.14.refs_3_ = bf16[2,128,128]{2,1,0:T(8,128)(2,1)S(1)} collective-permute-done((bf16[2,128,128]{2,1,0:T(8,128)(2,1)S(1)}, bf16[2,128,128]{2,1,0:T(8,128)(2,1)S(1)}, u32[]{:S(2)}, u32[]{:S(2)}) %collective-permute-start.14) | collective-permute-done | bytes 65568 | tf_op jit(solution)/shard_map/ppermute | solution.py:456
  28.4 0.2 post.3
  28.6 0.1 collective-permute-start.15
  28.7 0.8 %finish_mine.1 = (bf16[128,1024]{1,0:T(8,128)(2,1)S(1)}, bf16[128,1024]{1,0:T(8,128)(2,1)S(1)}, bf16[128,1024]{1,0:T(8,128)(2,1)S(1)}, bf16[128,1024]{1,0:T(8,128)(2,1)S(1)}) custom-call(bf16[128,2048]{1,0:T(8,128)(2,1)S(1)} %get-tuple-element.48.q_ref.refs_0_, bf16[128,2048]{1,0:T(8,128)(2,1)S(1)} %get-tuple-element.49.k_ref.refs_1_, ...), custom_call_target="tpu_custom_call" | custom-call | flops 268435456 | bytes 6422528 | tf_op jit(solution)/shard_map/finish_mine/pallas_call | solution.py:394
  29.4 0.8 %collective-permute-done.15.refs_13_ = bf16[8,128,128]{2,1,0:T(8,128)(2,1)S(1)} collective-permute-done((bf16[8,128,128]{2,1,0:T(8,128)(2,1)S(1)}, bf16[8,128,128]{2,1,0:T(8,128)(2,1)S(1)}, u32[]{:S(2)}, u32[]{:S(2)}) %collective-permute-start.15) | collective-permute-done | bytes 262176 | tf_op jit(solution)/shard_map/ppermute | solution.py:494
  30.2 1.7 %finish_other.1 = (bf16[128,2048]{1,0:T(8,128)(2,1)}, bf16[128,2048]{1,0:T(8,128)(2,1)}, bf16[128,2048]{1,0:T(8,128)(2,1)}, bf16[128,2048]{1,0:T(8,128)(2,1)}) custom-call(bf16[128,2048]{1,0:T(8,128)(2,1)S(1)} %get-tuple-element.48.q_ref.refs_0_, bf16[128,2048]{1,0:T(8,128)(2,1)S(1)} %get-tuple-element.49.k_ref.refs_1_, ...), custom_call_target="tpu_custom_call" | custom-call | flops 268435456 | bytes 8519680 | tf_op jit(solution)/shard_map/finish_other/pallas_call | solution.py:394
  (13 shorter events, 0.2 us)
Async XLA Ops:
  0.6 0.7 %copy-start = (s32[8]{0:T(128)S(1)}, s32[8]{0:T(128)}, u32[]{:S(2)}) copy-start(s32[8]{0:T(128)} %len_hbm.1) | copy-start | bytes 100
  3.2 2.1 %collective-permute-start = (bf16[2,8,128,128]{3,2,1,0:T(8,128)(2,1)S(1)}, bf16[2,8,128,128]{3,2,1,0:T(8,128)(2,1)S(1)}, u32[]{:S(2)}, u32[]{:S(2)}) collective-permute-start(bf16[2,8,128,128]{3,2,1,0:T(8,128)(2,1)S(1)} %get-tuple-element.65), channel_id=1, source_target_pairs={{0,1},{1,0},{2,3},{3,2},{4,5},{5,4},{6,7},{7,6},{8,9},{9,8},{10,11... | collective-permute-start | bytes 1572872 | tf_op jit(solution)/shard_map/ppermute | solution.py:424
  5.5 8.0 %collective-permute-start.1 = (bf16[2,128,128]{2,1,0:T(8,128)(2,1)S(1)}, bf16[2,128,128]{2,1,0:T(8,128)(2,1)S(1)}, u32[]{:S(2)}, u32[]{:S(2)}) collective-permute-start(bf16[2,128,128]{2,1,0:T(8,128)(2,1)S(1)} %get-tuple-element.67), channel_id=1, source_target_pairs={{0,6},{1,7},{2,4},{3,5},{4,2},{5,3},{6,0},{7,1},{8,14},{9,15},{10,... | collective-permute-start | bytes 196616 | tf_op jit(solution)/shard_map/ppermute | solution.py:456
  9.4 5.0 %collective-permute-start.2 = (bf16[2,128,128]{2,1,0:T(8,128)(2,1)S(1)}, bf16[2,128,128]{2,1,0:T(8,128)(2,1)S(1)}, u32[]{:S(2)}, u32[]{:S(2)}) collective-permute-start(bf16[2,128,128]{2,1,0:T(8,128)(2,1)S(1)} %get-tuple-element.68), channel_id=1, source_target_pairs={{0,2},{1,5},{2,0},{3,7},{4,6},{5,1},{6,4},{7,3},{8,10},{9,13},{10,... | collective-permute-start | bytes 196616 | tf_op jit(solution)/shard_map/ppermute | solution.py:456
  9.9 4.8 %collective-permute-start.3 = (bf16[2,128,128]{2,1,0:T(8,128)(2,1)S(1)}, bf16[2,128,128]{2,1,0:T(8,128)(2,1)S(1)}, u32[]{:S(2)}, u32[]{:S(2)}) collective-permute-start(bf16[2,128,128]{2,1,0:T(8,128)(2,1)S(1)} %get-tuple-element.69), channel_id=1, source_target_pairs={{0,4},{1,3},{2,6},{3,1},{4,0},{5,7},{6,2},{7,5},{8,12},{9,11},{10,... | collective-permute-start | bytes 196616 | tf_op jit(solution)/shard_map/ppermute | solution.py:456
  10.1 9.3 %collective-permute-start.8 = (bf16[2,128,128]{2,1,0:T(8,128)(2,1)S(1)}, bf16[2,128,128]{2,1,0:T(8,128)(2,1)S(1)}, u32[]{:S(2)}, u32[]{:S(2)}) collective-permute-start(bf16[2,128,128]{2,1,0:T(8,128)(2,1)S(1)} %get-tuple-element.76), channel_id=1, source_target_pairs={{0,6},{1,7},{2,4},{3,5},{4,2},{5,3},{6,0},{7,1},{8,14},{9,15},{10,... | collective-permute-start | bytes 196616 | tf_op jit(solution)/shard_map/ppermute | solution.py:456
  12.9 7.2 %collective-permute-start.9 = (bf16[2,128,128]{2,1,0:T(8,128)(2,1)S(1)}, bf16[2,128,128]{2,1,0:T(8,128)(2,1)S(1)}, u32[]{:S(2)}, u32[]{:S(2)}) collective-permute-start(bf16[2,128,128]{2,1,0:T(8,128)(2,1)S(1)} %get-tuple-element.77), channel_id=1, source_target_pairs={{0,2},{1,5},{2,0},{3,7},{4,6},{5,1},{6,4},{7,3},{8,10},{9,13},{10,... | collective-permute-start | bytes 196616 | tf_op jit(solution)/shard_map/ppermute | solution.py:456
  13.4 7.7 %collective-permute-start.10 = (bf16[2,128,128]{2,1,0:T(8,128)(2,1)S(1)}, bf16[2,128,128]{2,1,0:T(8,128)(2,1)S(1)}, u32[]{:S(2)}, u32[]{:S(2)}) collective-permute-start(bf16[2,128,128]{2,1,0:T(8,128)(2,1)S(1)} %get-tuple-element.78), channel_id=1, source_target_pairs={{0,4},{1,3},{2,6},{3,1},{4,0},{5,7},{6,2},{7,5},{8,12},{9,11},{10,... | collective-permute-start | bytes 196616 | tf_op jit(solution)/shard_map/ppermute | solution.py:456
  14.8 6.3 %collective-permute-start.11 = (bf16[2,128,128]{2,1,0:T(8,128)(2,1)S(1)}, bf16[2,128,128]{2,1,0:T(8,128)(2,1)S(1)}, u32[]{:S(2)}, u32[]{:S(2)}) collective-permute-start(bf16[2,128,128]{2,1,0:T(8,128)(2,1)S(1)} %totals.1), channel_id=1, source_target_pairs={{0,8},{1,9},{2,10},{3,11},{4,12},{5,13},{6,14},{7,15},{8,0},{9,1},... | collective-permute-start | bytes 196616 | tf_op jit(solution)/shard_map/ppermute | solution.py:480
  17.6 6.5 %collective-permute-start.4 = (bf16[2,128,128]{2,1,0:T(8,128)(2,1)S(1)}, bf16[2,128,128]{2,1,0:T(8,128)(2,1)S(1)}, u32[]{:S(2)}, u32[]{:S(2)}) collective-permute-start(bf16[2,128,128]{2,1,0:T(8,128)(2,1)S(1)} %get-tuple-element.71), channel_id=1, source_target_pairs={{0,6},{1,7},{2,4},{3,5},{4,2},{5,3},{6,0},{7,1},{8,14},{9,15},{10,... | collective-permute-start | bytes 196616 | tf_op jit(solution)/shard_map/ppermute | solution.py:456
  19.3 6.9 %collective-permute-start.5 = (bf16[2,128,128]{2,1,0:T(8,128)(2,1)S(1)}, bf16[2,128,128]{2,1,0:T(8,128)(2,1)S(1)}, u32[]{:S(2)}, u32[]{:S(2)}) collective-permute-start(bf16[2,128,128]{2,1,0:T(8,128)(2,1)S(1)} %get-tuple-element.72), channel_id=1, source_target_pairs={{0,2},{1,5},{2,0},{3,7},{4,6},{5,1},{6,4},{7,3},{8,10},{9,13},{10,... | collective-permute-start | bytes 196616 | tf_op jit(solution)/shard_map/ppermute | solution.py:456
  20.2 6.1 %collective-permute-start.6 = (bf16[2,128,128]{2,1,0:T(8,128)(2,1)S(1)}, bf16[2,128,128]{2,1,0:T(8,128)(2,1)S(1)}, u32[]{:S(2)}, u32[]{:S(2)}) collective-permute-start(bf16[2,128,128]{2,1,0:T(8,128)(2,1)S(1)} %get-tuple-element.73), channel_id=1, source_target_pairs={{0,4},{1,3},{2,6},{3,1},{4,0},{5,7},{6,2},{7,5},{8,12},{9,11},{10,... | collective-permute-start | bytes 196616 | tf_op jit(solution)/shard_map/ppermute | solution.py:456
  21.3 5.3 %collective-permute-start.12 = (bf16[2,128,128]{2,1,0:T(8,128)(2,1)S(1)}, bf16[2,128,128]{2,1,0:T(8,128)(2,1)S(1)}, u32[]{:S(2)}, u32[]{:S(2)}) collective-permute-start(bf16[2,128,128]{2,1,0:T(8,128)(2,1)S(1)} %get-tuple-element.80), channel_id=1, source_target_pairs={{0,6},{1,7},{2,4},{3,5},{4,2},{5,3},{6,0},{7,1},{8,14},{9,15},{10,... | collective-permute-start | bytes 196616 | tf_op jit(solution)/shard_map/ppermute | solution.py:456
  23.1 4.3 %collective-permute-start.13 = (bf16[2,128,128]{2,1,0:T(8,128)(2,1)S(1)}, bf16[2,128,128]{2,1,0:T(8,128)(2,1)S(1)}, u32[]{:S(2)}, u32[]{:S(2)}) collective-permute-start(bf16[2,128,128]{2,1,0:T(8,128)(2,1)S(1)} %get-tuple-element.81), channel_id=1, source_target_pairs={{0,2},{1,5},{2,0},{3,7},{4,6},{5,1},{6,4},{7,3},{8,10},{9,13},{10,... | collective-permute-start | bytes 196616 | tf_op jit(solution)/shard_map/ppermute | solution.py:456
  24.1 4.3 %collective-permute-start.14 = (bf16[2,128,128]{2,1,0:T(8,128)(2,1)S(1)}, bf16[2,128,128]{2,1,0:T(8,128)(2,1)S(1)}, u32[]{:S(2)}, u32[]{:S(2)}) collective-permute-start(bf16[2,128,128]{2,1,0:T(8,128)(2,1)S(1)} %get-tuple-element.82), channel_id=1, source_target_pairs={{0,4},{1,3},{2,6},{3,1},{4,0},{5,7},{6,2},{7,5},{8,12},{9,11},{10,... | collective-permute-start | bytes 196616 | tf_op jit(solution)/shard_map/ppermute | solution.py:456
  26.5 2.9 %collective-permute-start.7 = (bf16[8,128,128]{2,1,0:T(8,128)(2,1)S(1)}, bf16[8,128,128]{2,1,0:T(8,128)(2,1)S(1)}, u32[]{:S(2)}, u32[]{:S(2)}) collective-permute-start(bf16[8,128,128]{2,1,0:T(8,128)(2,1)S(1)} %get-tuple-element.74), channel_id=1, source_target_pairs={{0,1},{1,0},{2,3},{3,2},{4,5},{5,4},{6,7},{7,6},{8,9},{9,8},{10,11... | collective-permute-start | bytes 786440 | tf_op jit(solution)/shard_map/ppermute | solution.py:494
  28.6 1.6 %collective-permute-start.15 = (bf16[8,128,128]{2,1,0:T(8,128)(2,1)S(1)}, bf16[8,128,128]{2,1,0:T(8,128)(2,1)S(1)}, u32[]{:S(2)}, u32[]{:S(2)}) collective-permute-start(bf16[8,128,128]{2,1,0:T(8,128)(2,1)S(1)} %get-tuple-element.83), channel_id=1, source_target_pairs={{0,1},{1,0},{2,3},{3,2},{4,5},{5,4},{6,7},{7,6},{8,9},{9,8},{10,11... | collective-permute-start | bytes 786440 | tf_op jit(solution)/shard_map/ppermute | solution.py:494

commit v9 on v7

--- a/solution.py
+++ b/solution.py
@@ -246,16 +246,17 @@
     mask_ref[1] = jnp.where(suffix, one, none).astype(BF16)
     col = first + lax.broadcasted_iota(jnp.int32, (rows, HD), 1)
     same = (col <= pos) & (col >= begin)
-    same_t = jnp.where(same, one, none).T > 0.5
     for h in range(width // HD):
         cols = pl.ds(h * HD, HD)
         q, k, v = q_ref[:, cols], k_ref[:, cols], v_ref[:, cols]
         g = (g_ref[:, cols].astype(F32) * inv_root).astype(BF16)
         sg_ref[:, cols] = g
-        w_ref[h] = jnp.where(same, dot(q, k, (1, 1)), 0.0).astype(BF16)
-        wt_ref[h] = jnp.where(same_t, dot(k, q, (1, 1)), 0.0).astype(BF16)
-        dw_ref[h] = jnp.where(same, dot(g, v, (1, 1)), 0.0).astype(BF16)
-        dwt_ref[h] = jnp.where(same_t, dot(v, g, (1, 1)), 0.0).astype(BF16)
+        w = jnp.where(same, dot(q, k, (1, 1)), 0.0).astype(BF16)
+        w_ref[h] = w
+        wt_ref[h] = w.T
+        dw = jnp.where(same, dot(g, v, (1, 1)), 0.0).astype(BF16)
+        dw_ref[h] = dw
+        dwt_ref[h] = dw.T
 
 
 def coef(coef_ref, row):
@@ -319,54 +320,101 @@
             mine_ref[h] = (came * m0 + got_ref[kind, h].astype(F32) * m1).astype(BF16)
 
 
-def finish_kernel(other, split, chunks, *refs):
-    q_ref, k_ref, v_ref, g_ref, w_ref, wt_ref, dw_ref, dwt_ref, mask_ref, root_ref = refs[:10]
-    kt_ref, qt_ref, early_ref, late_ref = refs[10:14]
-    heads = early_ref.shape[0]
-    forward_is_late = kind_of(0, split) == 1
-    core = lax.rem(lax.axis_index("seq"), 2)
-    half = 1 - core if other else core
-    prefix, suffix, root = mask_ref[0], mask_ref[1], root_ref[...]
-    size = heads * HD // chunks
-    copies = []
-    if other:
-        done_refs, out_refs, bufs, sems = refs[14:18], refs[18:22], refs[22:26], refs[26]
-        to = pl.ds(pl.multiple_of(core * heads * HD, HD), heads * HD)
-        for i, ref in enumerate(out_refs):
-            copy = pltpu.make_async_copy(done_refs[i], ref.at[:, to], sems.at[i, chunks])
-            copy.start()
-            copies.append(copy)
-    else:
-        bufs = refs[14:18]
+def on_kind(which, split, run):
+    kind = kind_of(which, split)
+    if not split:
+        run(kind)
+        return
+    for choice in range(2):
+        pl.when(kind == choice)(functools.partial(run, choice))
+
+
+def outputs_of(kind, fixed_refs, h, state, kt_ref, qt_ref, i):
+    q_ref, k_ref, v_ref, g_ref, w_ref, wt_ref, dw_ref, dwt_ref, mask_ref, root_ref = fixed_refs
+    cols = pl.ds(pl.multiple_of(h * HD, HD), HD)
+    q, k, v, g = q_ref[:, cols], k_ref[:, cols], v_ref[:, cols], g_ref[:, cols]
 
     def wide(a, b):
         return jnp.concatenate([a, b], axis=1)
 
-    for c in range(chunks):
-        for i in range(c * heads // chunks, (c + 1) * heads // chunks):
-            h = half * heads + i
-            cols = pl.ds(pl.multiple_of(h * HD, HD), HD)
+    if kind == 0:
+        prefix = mask_ref[0]
+        o = dot(wide(w_ref[h], q * prefix), jnp.concatenate([v, state], axis=0), (1, 0))
+        dq = dot(wide(dw_ref[h], g * prefix), wide(kt_ref[i], state), (1, 1))
+        return (o * root_ref[...]).astype(BF16), dq.astype(BF16)
+    suffix = mask_ref[1]
+    dk = dot(wide(dwt_ref[h], v * suffix), wide(qt_ref[i], state), (1, 1))
+    dv = dot(wide(wt_ref[h], k * suffix), jnp.concatenate([g, state], axis=0), (1, 0))
+    return dk.astype(BF16), dv.astype(BF16)
+
+
+def early_kernel(split, *refs):
+    fixed, (kt_mine, qt_mine, mine_ref, kt_other, qt_other, other_ref), outs = refs[:10], refs[10:16], refs[16:]
+    heads = mine_ref.shape[0]
+    core = lax.rem(lax.axis_index("seq"), 2)
+
+    def run(kind):
+        for half, kt_ref, qt_ref, s_ref in (
+            (core, kt_mine, qt_mine, mine_ref),
+            (1 - core, kt_other, qt_other, other_ref),
+        ):
+            for i in range(heads):
+                h = half * heads + i
+                cols = pl.ds(pl.multiple_of(h * HD, HD), HD)
+                outs[0][:, cols], outs[1][:, cols] = outputs_of(kind, fixed, h, s_ref[i], kt_ref, qt_ref, i)
+
+    on_kind(0, split, run)
+
+
+def late_kernel(split, *refs):
+    fixed, (kt_ref, qt_ref, s_ref), outs = refs[:10], refs[10:13], refs[13:]
+    heads = s_ref.shape[0]
+    half = lax.rem(lax.axis_index("seq"), 2)
+
+    def run(kind):
+        for i in range(heads):
             at = pl.ds(i * HD, HD)
-            q, k, v, g = q_ref[:, cols], k_ref[:, cols], v_ref[:, cols], g_ref[:, cols]
-            early, late = early_ref[i], late_ref[i]
-            carried = jnp.where(forward_is_late, late, early)
-            returned = jnp.where(forward_is_late, early, late)
-            o = dot(wide(w_ref[h], q * prefix), jnp.concatenate([v, carried], axis=0), (1, 0))
-            bufs[0][:, at] = (o * root).astype(BF16)
-            dq = dot(wide(dw_ref[h], g * prefix), wide(kt_ref[i], carried), (1, 1))
-            bufs[1][:, at] = dq.astype(BF16)
-            dk = dot(wide(dwt_ref[h], v * suffix), wide(qt_ref[i], returned), (1, 1))
-            bufs[2][:, at] = dk.astype(BF16)
-            dv = dot(wide(wt_ref[h], k * suffix), jnp.concatenate([g, returned], axis=0), (1, 0))
-            bufs[3][:, at] = dv.astype(BF16)
-        if other:
-            to = pl.ds(pl.multiple_of(half * heads * HD + c * size, HD), size)
-            for i, ref in enumerate(out_refs):
-                copy = pltpu.make_async_copy(bufs[i].at[:, pl.ds(c * size, size)], ref.at[:, to], sems.at[i, c])
+            outs[0][:, at], outs[1][:, at] = outputs_of(
+                kind, fixed, half * heads + i, s_ref[i], kt_ref, qt_ref, i
+            )
+
+    on_kind(1, split, run)
+
+
+def last_kernel(split, chunks, *refs):
+    early, fixed, (kt_ref, qt_ref, s_ref), late = refs[:2], refs[2:12], refs[12:15], refs[15:17]
+    outs, bufs, (sems, early_sems, late_sems) = refs[17:21], refs[21:23], refs[23:]
+    heads = s_ref.shape[0]
+    width = heads * HD
+    core = lax.rem(lax.axis_index("seq"), 2)
+    size = width // chunks
+
+    def run(kind):
+        early_outs, late_outs = (outs[2:], outs[:2]) if kind == 0 else (outs[:2], outs[2:])
+        copies = []
+        to = pl.ds(pl.multiple_of(core * width, HD), width)
+        for i in range(2):
+            copies.append(pltpu.make_async_copy(early[i], early_outs[i], early_sems.at[i]))
+            copies.append(pltpu.make_async_copy(late[i], late_outs[i].at[:, to], late_sems.at[i]))
+        for copy in copies:
+            copy.start()
+        for c in range(chunks):
+            for i in range(c * heads // chunks, (c + 1) * heads // chunks):
+                at = pl.ds(i * HD, HD)
+                bufs[0][:, at], bufs[1][:, at] = outputs_of(
+                    kind, fixed, (1 - core) * heads + i, s_ref[i], kt_ref, qt_ref, i
+                )
+            to = pl.ds(pl.multiple_of((1 - core) * width + c * size, HD), size)
+            for i in range(2):
+                copy = pltpu.make_async_copy(
+                    bufs[i].at[:, pl.ds(c * size, size)], late_outs[i].at[:, to], sems.at[i, c]
+                )
                 copy.start()
                 copies.append(copy)
-    for copy in copies:
-        copy.wait()
+        for copy in copies:
+            copy.wait()
+
+    on_kind(1, split, run)
 
 
 def per_device(queries, keys, values, grad_out, doc_lengths):
@@ -432,7 +480,7 @@
         [mats] * 4 + [tokens, shape(2, rows, HD)],
         (doc_lengths, queries, keys, values, grad_out),
         [hbm] + [vmem] * 4,
-        flops=4 * heads * product,
+        flops=2 * heads * product,
         scratch=lengths,
     )
     owned = shape(per, HD, HD)
@@ -488,26 +536,35 @@
         other.append(lax.ppermute(theirs, "seq", swap))
     w, wt, dw, dwt, scaled = local
     fixed = (queries, keys, values, scaled, w, wt, dw, dwt, masks, root)
+    part = shape(rows, half * HD)
+    early = call(
+        functools.partial(early_kernel, split),
+        "early",
+        [tokens] * 2,
+        (*fixed, kt_mine, qt_mine, mine[0], kt_other, qt_other, other[0]),
+        [vmem] * 16,
+        flops=8 * half * product,
+    )
+    late = call(
+        functools.partial(late_kernel, split),
+        "late",
+        [part] * 2,
+        (*fixed, kt_mine, qt_mine, mine[1]),
+        [vmem] * 13,
+        flops=4 * half * product,
+    )
     chunks = 4
-    part = shape(rows, half * HD)
-    done = call(
-        functools.partial(finish_kernel, False, split, chunks),
-        "finish_mine",
-        [part] * 4,
-        (*fixed, kt_mine, qt_mine, *mine),
-        [vmem] * 14,
-        flops=8 * half * product,
-    )
     return tuple(
         call(
-            functools.partial(finish_kernel, True, split, chunks),
-            "finish_other",
+            functools.partial(last_kernel, split, chunks),
+            "last",
             [tokens] * 4,
-            (*fixed, kt_other, qt_other, *other, *done),
-            [vmem] * 18,
+            (*early, *fixed, kt_other, qt_other, other[1], *late),
+            [vmem] * 17,
             [hbm] * 4,
-            flops=8 * half * product,
-            scratch=[pltpu.VMEM(part.shape, BF16)] * 4 + [pltpu.SemaphoreType.DMA((4, chunks + 1))],
+            flops=4 * half * product,
+            scratch=[pltpu.VMEM(part.shape, BF16)] * 2
+            + [pltpu.SemaphoreType.DMA((2, chunks)), pltpu.SemaphoreType.DMA((2,)), pltpu.SemaphoreType.DMA((2,))],
         )
     )
 

time: 31.6 us -> 31.5 us (level)
    ppermute x12, waiting for transfers between devices: 1.81 us -> 2.35 us  [trade(): lax.ppermute(parts[d], 'seq', [(i, i ^ 2 * PARTNERS[d]) for i in range(n)])]
    ppermute x2, waiting for transfers between devices: 0.76 us -> 0.28 us  [per_device(): other.append(lax.ppermute(theirs, 'seq', swap))]
    pallas_call x11 -> x12, Pallas kernels: 8.37 us -> 8.21 us  [call(): pl.pallas_call(kernel, in_specs=specs, out_specs=out_specs or [vmem] * le...]
  transfers between devices with their start and end apart: 16 -> 16, of which waited for: 5 -> 5; matrix products, arithmetic and copies ran while one was open for 0% -> 0% of each run, Pallas kernels for 15% -> 14%
where the time goes in v9:
time: 31.5 us; the launch traced here: 31.4 us
  starting transfers between devices  18.8 us (60%)
  Pallas kernels  8.21 us (26%)
  waiting for transfers between devices  3 us (10%)
  between operations  0.75 us (2%)
  local copies, waits for them, and re-layouts  0.65 us (2%)
    ppermute x12, starting transfers between devices, trade(): lax.ppermute(parts[d], 'seq', [(i, i ^ 2 * PARTNERS[d]) for i in range(n)])  15.5 us
    pallas_call x12, Pallas kernels, call(): pl.pallas_call(kernel, in_specs=specs, out_specs=out_specs or [vmem] * le...  8.21 us
    ppermute x1, starting transfers between devices, per_device(): enter = lax.ppermute(edge(0), 'seq', up + down)  2.65 us
    ppermute x12, waiting for transfers between devices, trade(): lax.ppermute(parts[d], 'seq', [(i, i ^ 2 * PARTNERS[d]) for i in range(n)])  2.35 us
    unnamed x2, local copies, waits for them, and re-layouts  0.65 us
  transfers between devices with their start and end apart: 16, of which 5 were waited for; matrix products, arithmetic and copies ran while one was open for 0% of the time, Pallas kernels for 14%

profile of v9, /device:TPU:0, one launch (start us, length us, event | category | flops | bytes accessed | tf_op | source)
XLA Modules:
  0.0 31.4 jit_solution(11168200521274056506)
XLA Ops:
  0.6 0.6 %copy-done = s32[8]{0:T(128)S(1)} copy-done((s32[8]{0:T(128)S(1)}, s32[8]{0:T(128)}, u32[]{:S(2)}) %copy-start) | copy-done | bytes 56
  1.3 1.9 %send.1 = (s32[8]{0:T(128)S(1)}, bf16[2,8,128,128]{3,2,1,0:T(8,128)(2,1)S(1)}, bf16[128,2048]{1,0:T(8,128)(2,1)S(1)}, bf16[128,2048]{1,0:T(8,128)(2,1)S(1)}, bf1...) custom-call(s32[8]{0:T(128)S(1)} %copy-done, ...), custom_call_target="tpu_custom_call" | custom-call | flops 67108864 | bytes 5374016 | tf_op jit(solution)/shard_map/send/pallas_call | solution.py:436
  3.2 0.5 %collective-permute-start = (bf16[2,8,128,128]{3,2,1,0:T(8,128)(2,1)S(1)}, bf16[2,8,128,128]{3,2,1,0:T(8,128)(2,1)S(1)}, u32[]{:S(2)}, u32[]{:S(2)}) collective-permute-start(bf16[2,8,128,128]{3,2,1,0:T(8,128)(2,1)S(1)} %get-tuple-element.65), channel_id=1, source_target_pairs={{0,1},{1,0},{2,3},{3,2},{4,5},{5,4},{6,7},{7,6},{8,9},{9,8},{10,11... | collective-permute-start | bytes 1572872 | tf_op jit(solution)/shard_map/ppermute | solution.py:466
  3.7 1.2 %keep.1 = (bf16[2,8,128,128]{3,2,1,0:T(8,128)(2,1)S(1)}, bf16[8,128,128]{2,1,0:T(8,128)(2,1)S(1)}, bf16[8,128,128]{2,1,0:T(8,128)(2,1)S(1)}, f32[64,128]{1,0:T(8,128)S(1)}) custom-call(s32[8]{0:T(128)S(1)} %get-tuple-element.51.len_hbm, bf16[128,2048]{1,0:T(8,128)(2,1)S(1)} %get-tuple-element.48.q_ref.refs_0_.refs_2_, ...), custom_call_target="tpu_custom_call" | custom-call | flops 67108864 | bytes 3309600 | tf_op jit(solution)/shard_map/keep/pallas_call | solution.py:436
  4.9 0.4 %collective-permute-done.got_ref = bf16[2,8,128,128]{3,2,1,0:T(8,128)(2,1)S(1)} collective-permute-done((bf16[2,8,128,128]{3,2,1,0:T(8,128)(2,1)S(1)}, bf16[2,8,128,128]{3,2,1,0:T(8,128)(2,1)S(1)}, u32[]{:S(2)}, u32[]{:S(2)}) %collective-permute-start) | collective-permute-done | bytes 524320 | tf_op jit(solution)/shard_map/ppermute | solution.py:466
  5.3 0.2 pair.1
  5.5 4.0 %collective-permute-start.1 = (bf16[2,128,128]{2,1,0:T(8,128)(2,1)S(1)}, bf16[2,128,128]{2,1,0:T(8,128)(2,1)S(1)}, u32[]{:S(2)}, u32[]{:S(2)}) collective-permute-start(bf16[2,128,128]{2,1,0:T(8,128)(2,1)S(1)} %get-tuple-element.67), channel_id=1, source_target_pairs={{0,6},{1,7},{2,4},{3,5},{4,2},{5,3},{6,0},{7,1},{8,14},{9,15},{10,... | collective-permute-start | bytes 196616 | tf_op jit(solution)/shard_map/ppermute | solution.py:498
  9.4 0.5 %collective-permute-start.2 = (bf16[2,128,128]{2,1,0:T(8,128)(2,1)S(1)}, bf16[2,128,128]{2,1,0:T(8,128)(2,1)S(1)}, u32[]{:S(2)}, u32[]{:S(2)}) collective-permute-start(bf16[2,128,128]{2,1,0:T(8,128)(2,1)S(1)} %get-tuple-element.68), channel_id=1, source_target_pairs={{0,2},{1,3},{2,0},{3,1},{4,6},{5,7},{6,4},{7,5},{8,10},{9,11},{10,... | collective-permute-start | bytes 196616 | tf_op jit(solution)/shard_map/ppermute | solution.py:498
  9.9 0.1 collective-permute-start.3
  10.1 2.8 %collective-permute-start.8 = (bf16[2,128,128]{2,1,0:T(8,128)(2,1)S(1)}, bf16[2,128,128]{2,1,0:T(8,128)(2,1)S(1)}, u32[]{:S(2)}, u32[]{:S(2)}) collective-permute-start(bf16[2,128,128]{2,1,0:T(8,128)(2,1)S(1)} %get-tuple-element.81), channel_id=1, source_target_pairs={{0,6},{1,7},{2,4},{3,5},{4,2},{5,3},{6,0},{7,1},{8,14},{9,15},{10,... | collective-permute-start | bytes 196616 | tf_op jit(solution)/shard_map/ppermute | solution.py:498
  12.9 0.5 %collective-permute-start.9 = (bf16[2,128,128]{2,1,0:T(8,128)(2,1)S(1)}, bf16[2,128,128]{2,1,0:T(8,128)(2,1)S(1)}, u32[]{:S(2)}, u32[]{:S(2)}) collective-permute-start(bf16[2,128,128]{2,1,0:T(8,128)(2,1)S(1)} %get-tuple-element.82), channel_id=1, source_target_pairs={{0,2},{1,3},{2,0},{3,1},{4,6},{5,7},{6,4},{7,5},{8,10},{9,11},{10,... | collective-permute-start | bytes 196616 | tf_op jit(solution)/shard_map/ppermute | solution.py:498
  13.4 0.4 %collective-permute-start.10 = (bf16[2,128,128]{2,1,0:T(8,128)(2,1)S(1)}, bf16[2,128,128]{2,1,0:T(8,128)(2,1)S(1)}, u32[]{:S(2)}, u32[]{:S(2)}) collective-permute-start(bf16[2,128,128]{2,1,0:T(8,128)(2,1)S(1)} %get-tuple-element.83), channel_id=1, source_target_pairs={{0,4},{1,5},{2,6},{3,7},{4,0},{5,1},{6,2},{7,3},{8,12},{9,13},{10,... | collective-permute-start | bytes 196616 | tf_op jit(solution)/shard_map/ppermute | solution.py:498
  13.8 0.8 %collective-permute-done.3.refs_3_.s3 = bf16[2,128,128]{2,1,0:T(8,128)(2,1)S(1)} collective-permute-done((bf16[2,128,128]{2,1,0:T(8,128)(2,1)S(1)}, bf16[2,128,128]{2,1,0:T(8,128)(2,1)S(1)}, u32[]{:S(2)}, u32[]{:S(2)}) %collective-permute-start.3) | collective-permute-done | bytes 65568 | tf_op jit(solution)/shard_map/ppermute | solution.py:498
  14.7 2.6 %collective-permute-start.11 = (bf16[2,128,128]{2,1,0:T(8,128)(2,1)S(1)}, bf16[2,128,128]{2,1,0:T(8,128)(2,1)S(1)}, u32[]{:S(2)}, u32[]{:S(2)}) collective-permute-start(bf16[2,128,128]{2,1,0:T(8,128)(2,1)S(1)} %totals.1), channel_id=1, source_target_pairs={{0,8},{1,9},{2,10},{3,11},{4,12},{5,13},{6,14},{7,15},{8,0},{9,1},... | collective-permute-start | bytes 196616 | tf_op jit(solution)/shard_map/ppermute | solution.py:522
  17.4 0.1 scan.2
  17.5 1.8 %collective-permute-start.4 = (bf16[2,128,128]{2,1,0:T(8,128)(2,1)S(1)}, bf16[2,128,128]{2,1,0:T(8,128)(2,1)S(1)}, u32[]{:S(2)}, u32[]{:S(2)}) collective-permute-start(bf16[2,128,128]{2,1,0:T(8,128)(2,1)S(1)} %get-tuple-element.71), channel_id=1, source_target_pairs={{0,6},{1,7},{2,4},{3,5},{4,2},{5,3},{6,0},{7,1},{8,14},{9,15},{10,... | collective-permute-start | bytes 196616 | tf_op jit(solution)/shard_map/ppermute | solution.py:498
  19.3 0.5 %collective-permute-start.5 = (bf16[2,128,128]{2,1,0:T(8,128)(2,1)S(1)}, bf16[2,128,128]{2,1,0:T(8,128)(2,1)S(1)}, u32[]{:S(2)}, u32[]{:S(2)}) collective-permute-start(bf16[2,128,128]{2,1,0:T(8,128)(2,1)S(1)} %get-tuple-element.72), channel_id=1, source_target_pairs={{0,2},{1,3},{2,0},{3,1},{4,6},{5,7},{6,4},{7,5},{8,10},{9,11},{10,... | collective-permute-start | bytes 196616 | tf_op jit(solution)/shard_map/ppermute | solution.py:498
  19.8 1.2 %collective-permute-start.6 = (bf16[2,128,128]{2,1,0:T(8,128)(2,1)S(1)}, bf16[2,128,128]{2,1,0:T(8,128)(2,1)S(1)}, u32[]{:S(2)}, u32[]{:S(2)}) collective-permute-start(bf16[2,128,128]{2,1,0:T(8,128)(2,1)S(1)} %get-tuple-element.73), channel_id=1, source_target_pairs={{0,4},{1,5},{2,6},{3,7},{4,0},{5,1},{6,2},{7,3},{8,12},{9,13},{10,... | collective-permute-start | bytes 196616 | tf_op jit(solution)/shard_map/ppermute | solution.py:498
  21.1 0.2 scan.3
  21.2 1.8 %collective-permute-start.12 = (bf16[2,128,128]{2,1,0:T(8,128)(2,1)S(1)}, bf16[2,128,128]{2,1,0:T(8,128)(2,1)S(1)}, u32[]{:S(2)}, u32[]{:S(2)}) collective-permute-start(bf16[2,128,128]{2,1,0:T(8,128)(2,1)S(1)} %get-tuple-element.85), channel_id=1, source_target_pairs={{0,6},{1,7},{2,4},{3,5},{4,2},{5,3},{6,0},{7,1},{8,14},{9,15},{10,... | collective-permute-start | bytes 196616 | tf_op jit(solution)/shard_map/ppermute | solution.py:498
  23.1 0.6 %collective-permute-start.13 = (bf16[2,128,128]{2,1,0:T(8,128)(2,1)S(1)}, bf16[2,128,128]{2,1,0:T(8,128)(2,1)S(1)}, u32[]{:S(2)}, u32[]{:S(2)}) collective-permute-start(bf16[2,128,128]{2,1,0:T(8,128)(2,1)S(1)} %get-tuple-element.86), channel_id=1, source_target_pairs={{0,2},{1,3},{2,0},{3,1},{4,6},{5,7},{6,4},{7,5},{8,10},{9,11},{10,... | collective-permute-start | bytes 196616 | tf_op jit(solution)/shard_map/ppermute | solution.py:498
  23.7 1.1 %collective-permute-start.14 = (bf16[2,128,128]{2,1,0:T(8,128)(2,1)S(1)}, bf16[2,128,128]{2,1,0:T(8,128)(2,1)S(1)}, u32[]{:S(2)}, u32[]{:S(2)}) collective-permute-start(bf16[2,128,128]{2,1,0:T(8,128)(2,1)S(1)} %get-tuple-element.87), channel_id=1, source_target_pairs={{0,4},{1,5},{2,6},{3,7},{4,0},{5,1},{6,2},{7,3},{8,12},{9,13},{10,... | collective-permute-start | bytes 196616 | tf_op jit(solution)/shard_map/ppermute | solution.py:498
  24.8 0.2 post.2
  25.1 0.1 collective-permute-start.7
  25.1 1.3 %local.1 = (bf16[16,128,128]{2,1,0:T(8,128)(2,1)S(1)}, bf16[16,128,128]{2,1,0:T(8,128)(2,1)S(1)}, bf16[16,128,128]{2,1,0:T(8,128)(2,1)S(1)}, bf16[16,128,128]{2,...) custom-call(s32[8]{0:T(128)S(1)} %get-tuple-element.51.len_hbm, ...), custom_call_target="tpu_custom_call" | custom-call | flops 134217728 | bytes 4784160 | tf_op jit(solution)/shard_map/local/pallas_call | solution.py:436
  26.5 0.8 %collective-permute-done.13.refs_2_ = bf16[2,128,128]{2,1,0:T(8,128)(2,1)S(1)} collective-permute-done((bf16[2,128,128]{2,1,0:T(8,128)(2,1)S(1)}, bf16[2,128,128]{2,1,0:T(8,128)(2,1)S(1)}, u32[]{:S(2)}, u32[]{:S(2)}) %collective-permute-start.13) | collective-permute-done | bytes 65568 | tf_op jit(solution)/shard_map/ppermute | solution.py:498
  27.3 0.6 %collective-permute-done.14.refs_3_ = bf16[2,128,128]{2,1,0:T(8,128)(2,1)S(1)} collective-permute-done((bf16[2,128,128]{2,1,0:T(8,128)(2,1)S(1)}, bf16[2,128,128]{2,1,0:T(8,128)(2,1)S(1)}, u32[]{:S(2)}, u32[]{:S(2)}) %collective-permute-start.14) | collective-permute-done | bytes 65568 | tf_op jit(solution)/shard_map/ppermute | solution.py:498
  28.0 0.2 post.3
  28.3 0.5 %late.1 = (bf16[128,1024]{1,0:T(8,128)(2,1)S(1)}, bf16[128,1024]{1,0:T(8,128)(2,1)S(1)}) custom-call(bf16[128,2048]{1,0:T(8,128)(2,1)S(1)} %get-tuple-element.48.q_ref.refs_0_.refs_2_, bf16[128,2048]{1,0:T(8,128)(2,1)S(1)} %get-tuple-element.49.k_ref.refs_1_.refs_3_, bf16[128,2048]{1,0:T(8,128)(2,1)S(1)} %get-tuple-element.50.v_ref.refs_2_.refs_4_, ...), custom_call_target="tpu_custom_call" | custom-call | flops 134217728 | bytes 5636096 | tf_op jit(solution)/shard_map/late/pallas_call | solution.py:436
  28.8 0.8 %early.1 = (bf16[128,2048]{1,0:T(8,128)(2,1)S(1)}, bf16[128,2048]{1,0:T(8,128)(2,1)S(1)}) custom-call(bf16[128,2048]{1,0:T(8,128)(2,1)S(1)} %get-tuple-element.48.q_ref.refs_0_.refs_2_, bf16[128,2048]{1,0:T(8,128)(2,1)S(1)} %get-tuple-element.49.k_ref.refs_1_.refs_3_, bf16[128,2048]{1,0:T(8,128)(2,1)S(1)} %get-tuple-element.50.v_ref.refs_2_.refs_4_, ...), custom_call_target="tpu_custom_call" | custom-call | flops 268435456 | bytes 6946816 | tf_op jit(solution)/shard_map/early/pallas_call | solution.py:436
  29.5 0.3 collective-permute-done.15.refs_14_
  29.8 1.6 %last.1 = (bf16[128,2048]{1,0:T(8,128)(2,1)}, bf16[128,2048]{1,0:T(8,128)(2,1)}, bf16[128,2048]{1,0:T(8,128)(2,1)}, bf16[128,2048]{1,0:T(8,128)(2,1)}) custom-call(bf16[128,2048]{1,0:T(8,128)(2,1)S(1)} %get-tuple-element.78.refs_0_, bf16[128,2048]{1,0:T(8,128)(2,1)S(1)} %get-tuple-element.79.refs_1_, ...), custom_call_target="tpu_custom_call" | custom-call | flops 134217728 | bytes 8781824 | tf_op jit(solution)/shard_map/last/pallas_call | solution.py:436
  (14 shorter events, 0.2 us)
Async XLA Ops:
  0.6 0.7 %copy-start = (s32[8]{0:T(128)S(1)}, s32[8]{0:T(128)}, u32[]{:S(2)}) copy-start(s32[8]{0:T(128)} %len_hbm.1) | copy-start | bytes 100
  3.2 2.1 %collective-permute-start = (bf16[2,8,128,128]{3,2,1,0:T(8,128)(2,1)S(1)}, bf16[2,8,128,128]{3,2,1,0:T(8,128)(2,1)S(1)}, u32[]{:S(2)}, u32[]{:S(2)}) collective-permute-start(bf16[2,8,128,128]{3,2,1,0:T(8,128)(2,1)S(1)} %get-tuple-element.65), channel_id=1, source_target_pairs={{0,1},{1,0},{2,3},{3,2},{4,5},{5,4},{6,7},{7,6},{8,9},{9,8},{10,11... | collective-permute-start | bytes 1572872 | tf_op jit(solution)/shard_map/ppermute | solution.py:466
  5.5 8.0 %collective-permute-start.1 = (bf16[2,128,128]{2,1,0:T(8,128)(2,1)S(1)}, bf16[2,128,128]{2,1,0:T(8,128)(2,1)S(1)}, u32[]{:S(2)}, u32[]{:S(2)}) collective-permute-start(bf16[2,128,128]{2,1,0:T(8,128)(2,1)S(1)} %get-tuple-element.67), channel_id=1, source_target_pairs={{0,6},{1,7},{2,4},{3,5},{4,2},{5,3},{6,0},{7,1},{8,14},{9,15},{10,... | collective-permute-start | bytes 196616 | tf_op jit(solution)/shard_map/ppermute | solution.py:498
  9.4 4.4 %collective-permute-start.2 = (bf16[2,128,128]{2,1,0:T(8,128)(2,1)S(1)}, bf16[2,128,128]{2,1,0:T(8,128)(2,1)S(1)}, u32[]{:S(2)}, u32[]{:S(2)}) collective-permute-start(bf16[2,128,128]{2,1,0:T(8,128)(2,1)S(1)} %get-tuple-element.68), channel_id=1, source_target_pairs={{0,2},{1,3},{2,0},{3,1},{4,6},{5,7},{6,4},{7,5},{8,10},{9,11},{10,... | collective-permute-start | bytes 196616 | tf_op jit(solution)/shard_map/ppermute | solution.py:498
  9.9 4.7 %collective-permute-start.3 = (bf16[2,128,128]{2,1,0:T(8,128)(2,1)S(1)}, bf16[2,128,128]{2,1,0:T(8,128)(2,1)S(1)}, u32[]{:S(2)}, u32[]{:S(2)}) collective-permute-start(bf16[2,128,128]{2,1,0:T(8,128)(2,1)S(1)} %get-tuple-element.69), channel_id=1, source_target_pairs={{0,4},{1,5},{2,6},{3,7},{4,0},{5,1},{6,2},{7,3},{8,12},{9,13},{10,... | collective-permute-start | bytes 196616 | tf_op jit(solution)/shard_map/ppermute | solution.py:498
  10.1 9.3 %collective-permute-start.8 = (bf16[2,128,128]{2,1,0:T(8,128)(2,1)S(1)}, bf16[2,128,128]{2,1,0:T(8,128)(2,1)S(1)}, u32[]{:S(2)}, u32[]{:S(2)}) collective-permute-start(bf16[2,128,128]{2,1,0:T(8,128)(2,1)S(1)} %get-tuple-element.81), channel_id=1, source_target_pairs={{0,6},{1,7},{2,4},{3,5},{4,2},{5,3},{6,0},{7,1},{8,14},{9,15},{10,... | collective-permute-start | bytes 196616 | tf_op jit(solution)/shard_map/ppermute | solution.py:498
  12.9 6.9 %collective-permute-start.9 = (bf16[2,128,128]{2,1,0:T(8,128)(2,1)S(1)}, bf16[2,128,128]{2,1,0:T(8,128)(2,1)S(1)}, u32[]{:S(2)}, u32[]{:S(2)}) collective-permute-start(bf16[2,128,128]{2,1,0:T(8,128)(2,1)S(1)} %get-tuple-element.82), channel_id=1, source_target_pairs={{0,2},{1,3},{2,0},{3,1},{4,6},{5,7},{6,4},{7,5},{8,10},{9,11},{10,... | collective-permute-start | bytes 196616 | tf_op jit(solution)/shard_map/ppermute | solution.py:498
  13.4 7.6 %collective-permute-start.10 = (bf16[2,128,128]{2,1,0:T(8,128)(2,1)S(1)}, bf16[2,128,128]{2,1,0:T(8,128)(2,1)S(1)}, u32[]{:S(2)}, u32[]{:S(2)}) collective-permute-start(bf16[2,128,128]{2,1,0:T(8,128)(2,1)S(1)} %get-tuple-element.83), channel_id=1, source_target_pairs={{0,4},{1,5},{2,6},{3,7},{4,0},{5,1},{6,2},{7,3},{8,12},{9,13},{10,... | collective-permute-start | bytes 196616 | tf_op jit(solution)/shard_map/ppermute | solution.py:498
  14.7 6.3 %collective-permute-start.11 = (bf16[2,128,128]{2,1,0:T(8,128)(2,1)S(1)}, bf16[2,128,128]{2,1,0:T(8,128)(2,1)S(1)}, u32[]{:S(2)}, u32[]{:S(2)}) collective-permute-start(bf16[2,128,128]{2,1,0:T(8,128)(2,1)S(1)} %totals.1), channel_id=1, source_target_pairs={{0,8},{1,9},{2,10},{3,11},{4,12},{5,13},{6,14},{7,15},{8,0},{9,1},... | collective-permute-start | bytes 196616 | tf_op jit(solution)/shard_map/ppermute | solution.py:522
  17.5 6.2 %collective-permute-start.4 = (bf16[2,128,128]{2,1,0:T(8,128)(2,1)S(1)}, bf16[2,128,128]{2,1,0:T(8,128)(2,1)S(1)}, u32[]{:S(2)}, u32[]{:S(2)}) collective-permute-start(bf16[2,128,128]{2,1,0:T(8,128)(2,1)S(1)} %get-tuple-element.71), channel_id=1, source_target_pairs={{0,6},{1,7},{2,4},{3,5},{4,2},{5,3},{6,0},{7,1},{8,14},{9,15},{10,... | collective-permute-start | bytes 196616 | tf_op jit(solution)/shard_map/ppermute | solution.py:498
  19.3 5.5 %collective-permute-start.5 = (bf16[2,128,128]{2,1,0:T(8,128)(2,1)S(1)}, bf16[2,128,128]{2,1,0:T(8,128)(2,1)S(1)}, u32[]{:S(2)}, u32[]{:S(2)}) collective-permute-start(bf16[2,128,128]{2,1,0:T(8,128)(2,1)S(1)} %get-tuple-element.72), channel_id=1, source_target_pairs={{0,2},{1,3},{2,0},{3,1},{4,6},{5,7},{6,4},{7,5},{8,10},{9,11},{10,... | collective-permute-start | bytes 196616 | tf_op jit(solution)/shard_map/ppermute | solution.py:498
  19.8 5.0 %collective-permute-start.6 = (bf16[2,128,128]{2,1,0:T(8,128)(2,1)S(1)}, bf16[2,128,128]{2,1,0:T(8,128)(2,1)S(1)}, u32[]{:S(2)}, u32[]{:S(2)}) collective-permute-start(bf16[2,128,128]{2,1,0:T(8,128)(2,1)S(1)} %get-tuple-element.73), channel_id=1, source_target_pairs={{0,4},{1,5},{2,6},{3,7},{4,0},{5,1},{6,2},{7,3},{8,12},{9,13},{10,... | collective-permute-start | bytes 196616 | tf_op jit(solution)/shard_map/ppermute | solution.py:498
  21.2 5.3 %collective-permute-start.12 = (bf16[2,128,128]{2,1,0:T(8,128)(2,1)S(1)}, bf16[2,128,128]{2,1,0:T(8,128)(2,1)S(1)}, u32[]{:S(2)}, u32[]{:S(2)}) collective-permute-start(bf16[2,128,128]{2,1,0:T(8,128)(2,1)S(1)} %get-tuple-element.85), channel_id=1, source_target_pairs={{0,6},{1,7},{2,4},{3,5},{4,2},{5,3},{6,0},{7,1},{8,14},{9,15},{10,... | collective-permute-start | bytes 196616 | tf_op jit(solution)/shard_map/ppermute | solution.py:498
  23.1 4.3 %collective-permute-start.13 = (bf16[2,128,128]{2,1,0:T(8,128)(2,1)S(1)}, bf16[2,128,128]{2,1,0:T(8,128)(2,1)S(1)}, u32[]{:S(2)}, u32[]{:S(2)}) collective-permute-start(bf16[2,128,128]{2,1,0:T(8,128)(2,1)S(1)} %get-tuple-element.86), channel_id=1, source_target_pairs={{0,2},{1,3},{2,0},{3,1},{4,6},{5,7},{6,4},{7,5},{8,10},{9,11},{10,... | collective-permute-start | bytes 196616 | tf_op jit(solution)/shard_map/ppermute | solution.py:498
  23.7 4.3 %collective-permute-start.14 = (bf16[2,128,128]{2,1,0:T(8,128)(2,1)S(1)}, bf16[2,128,128]{2,1,0:T(8,128)(2,1)S(1)}, u32[]{:S(2)}, u32[]{:S(2)}) collective-permute-start(bf16[2,128,128]{2,1,0:T(8,128)(2,1)S(1)} %get-tuple-element.87), channel_id=1, source_target_pairs={{0,4},{1,5},{2,6},{3,7},{4,0},{5,1},{6,2},{7,3},{8,12},{9,13},{10,... | collective-permute-start | bytes 196616 | tf_op jit(solution)/shard_map/ppermute | solution.py:498
  25.1 3.7 %collective-permute-start.7 = (bf16[8,128,128]{2,1,0:T(8,128)(2,1)S(1)}, bf16[8,128,128]{2,1,0:T(8,128)(2,1)S(1)}, u32[]{:S(2)}, u32[]{:S(2)}) collective-permute-start(bf16[8,128,128]{2,1,0:T(8,128)(2,1)S(1)} %get-tuple-element.77), channel_id=1, source_target_pairs={{0,1},{1,0},{2,3},{3,2},{4,5},{5,4},{6,7},{7,6},{8,9},{9,8},{10,11... | collective-permute-start | bytes 786440 | tf_op jit(solution)/shard_map/ppermute | solution.py:536
  28.2 1.6 %collective-permute-start.15 = (bf16[8,128,128]{2,1,0:T(8,128)(2,1)S(1)}, bf16[8,128,128]{2,1,0:T(8,128)(2,1)S(1)}, u32[]{:S(2)}, u32[]{:S(2)}) collective-permute-start(bf16[8,128,128]{2,1,0:T(8,128)(2,1)S(1)} %get-tuple-element.88), channel_id=1, source_target_pairs={{0,1},{1,0},{2,3},{3,2},{4,5},{5,4},{6,7},{7,6},{8,9},{9,8},{10,11... | collective-permute-start | bytes 786440 | tf_op jit(solution)/shard_map/ppermute | solution.py:536

commit v10 on v8

v10 whole, which is shorter than its diff:
```python
import functools

import jax
import jax.numpy as jnp
from jax import lax
from jax.experimental import pallas as pl
from jax.experimental.pallas import tpu as pltpu
from jax.sharding import PartitionSpec as P

HD = 128
PAIRS = 4
PARTNERS = (0, 3, 1, 2)
TEAM = 2 * PAIRS
F32 = jnp.float32
BF16 = jnp.bfloat16

KEEP_F, GOT_F, KEEP_B, GOT_B = 0, 1, 2, 3
TOT_F, TOT_B = 4, 8
MIX_F, MIX_B = 12, 28
ENTER_F, ENTER_B = 44, 48
MINE_F, MINE_B, THEIRS_F, THEIRS_B = 52, 54, 56, 58
COEFS = 64


def doc_starts(len_ref):
    starts, at = [], jnp.int32(0)
    for j in range(len_ref.shape[0]):
        starts.append(at)
        at = at + len_ref[j]
    return starts


def starts_before(starts, limit):
    count = jnp.int32(0)
    for s in starts:
        count = count + (s < limit).astype(jnp.int32)
    return count


def min_start(starts, low, otherwise):
    out = jnp.int32(otherwise)
    for s in starts:
        out = jnp.where(s >= low, jnp.minimum(out, s), out)
    return out


def max_start(starts, high):
    out = jnp.int32(0)
    for s in starts:
        out = jnp.where(s < high, jnp.maximum(out, s), out)
    return out


def row_facts(starts, first, rows):
    pos = first + lax.broadcasted_iota(jnp.int32, (rows, HD), 0)
    begin = jnp.zeros((rows, HD), jnp.int32)
    for s in starts:
        begin = jnp.where(pos >= s, s, begin)
    inv_root = 1.0 / jnp.sqrt((pos - begin + 1).astype(F32))
    return pos, begin, inv_root


def dot(a, b, contract):
    return lax.dot_general(a, b, ((contract[:1], contract[1:]), ((), ())), preferred_element_type=F32)


def early_kind(split):
    return (lax.axis_index("seq") >= TEAM).astype(jnp.int32) if split else 0


def is_odd():
    return lax.rem(lax.axis_index("seq"), 2) == 1


def my_kind(split):
    early = early_kind(split)
    return jnp.where(is_odd(), early, 1 - early)


def on_kind(kind, run):
    if isinstance(kind, int):
        run(kind)
        return
    for choice in range(2):
        pl.when(kind == choice)(functools.partial(run, choice))


def state_of(kind, t, x, row_mask, inv_root):
    if kind == 1:
        x = (x.astype(F32) * inv_root).astype(BF16)
    return dot(t, x * row_mask, (1, 0)).astype(BF16)


def send_kernel(
    total,
    split,
    chunks,
    len_hbm,
    q_hbm,
    k_hbm,
    v_hbm,
    g_hbm,
    len_out,
    out_ref,
    q_ref,
    k_ref,
    v_ref,
    g_ref,
    t_ref,
    rows_ref,
    root_ref,
    len_ref,
    sems,
    rest_sems,
    len_sems,
):
    rows, width = q_ref.shape
    first = lax.axis_index("seq") * rows
    size = width // chunks
    len_copy = pltpu.make_async_copy(len_hbm, len_ref, len_sems.at[0])
    len_copy.start()
    len_pass = pltpu.make_async_copy(len_hbm, len_out, len_sems.at[1])
    len_pass.start()
    of_kind = (((k_hbm, k_ref), (v_hbm, v_ref)), ((q_hbm, q_ref), (g_hbm, g_ref)))

    def run(kind):
        copies = []
        for c in range(chunks):
            at = pl.ds(c * size, size)
            for i, (src, dst) in enumerate(of_kind[kind]):
                copies.append(pltpu.make_async_copy(src.at[:, at], dst.at[:, at], sems.at[i, c]))
        for i, (src, dst) in enumerate(of_kind[1 - kind]):
            copies.append(pltpu.make_async_copy(src, dst, rest_sems.at[i]))
        for copy in copies:
            copy.start()
        len_copy.wait()
        starts = doc_starts(len_ref)
        pos, _, inv_root = row_facts(starts, first, rows)
        one, none = jnp.ones((), F32), jnp.zeros((), F32)
        tail_rows = jnp.where(pos >= max_start(starts, first + rows), one, none).astype(BF16)
        head_rows = jnp.where(pos < min_start(starts, first + 1, total), one, none).astype(BF16)
        rows_ref[0] = tail_rows
        rows_ref[1] = head_rows
        root_ref[...] = inv_root
        (_, t_from), (_, x_ref) = of_kind[kind]
        per = size // HD
        for c in range(chunks):
            copies[2 * c].wait()
            for h in range(c * per, (c + 1) * per):
                t_ref[h] = t_from[:, pl.ds(h * HD, HD)].T
            copies[2 * c + 1].wait()
            for h in range(c * per, (c + 1) * per):
                mask = head_rows if kind else tail_rows
                out_ref[h] = state_of(kind, t_ref[h], x_ref[:, pl.ds(h * HD, HD)], mask, inv_root)
        for copy in copies[2 * chunks :]:
            copy.wait()
        len_pass.wait()

    on_kind(1 - my_kind(split), run)


def slots():
    pair = lax.rem(lax.axis_index("seq"), TEAM) // 2
    return [pair ^ d for d in PARTNERS]


def coefficients(starts, rows, n, coef_ref):
    me = lax.axis_index("seq")
    core = lax.rem(me, 2)
    pair = lax.rem(me, TEAM) // 2
    base = me - lax.rem(me, TEAM)
    one = jnp.int32(1)

    def put(row, flag):
        coef_ref[pl.ds(row, 1), :] = jnp.full((1, HD), flag.astype(F32), F32)

    def both(block):
        return starts_before(starts, block * rows), starts_before(starts, block * rows + 1)

    def same(a, b):
        return (a == b).astype(jnp.int32)

    team_low, team_high = both(base), both(base + TEAM)
    pairs = [pair ^ d for d in PARTNERS]
    low = [both(base + 2 * p) for p in pairs]
    high = [both(base + 2 * p + 2) for p in pairs]
    middle = both(me - core + 1)
    open_0 = same(low[0][0], middle[0])
    open_1 = same(middle[0], high[0][0])
    close_0 = same(low[0][1], middle[1])
    close_1 = same(middle[1], high[0][1])
    odd = core
    even = one - core
    put(KEEP_F, jnp.where(odd == 1, one, open_1))
    put(GOT_F, jnp.where(odd == 1, open_1, one))
    put(KEEP_B, jnp.where(odd == 1, close_0, one))
    put(GOT_B, jnp.where(odd == 1, one, close_0))
    is_low = (base == 0).astype(jnp.int32)
    is_high = (base == n - TEAM).astype(jnp.int32)
    for d in range(PAIRS):
        tot_f = same(high[d][0], team_high[0])
        tot_b = same(team_low[1], low[d][1])
        put(TOT_F + d, tot_f)
        put(TOT_B + d, tot_b)
        put(ENTER_F + d, same(team_low[0], low[d][0]) * (one - is_low))
        put(ENTER_B + d, same(high[d][1], team_high[1]) * (one - is_high))
        for s in range(PAIRS):
            before = (pairs[s] < pairs[d]).astype(jnp.int32)
            after = (pairs[s] > pairs[d]).astype(jnp.int32)
            put(MIX_F + d * PAIRS + s, before * same(high[s][0], low[d][0]))
            put(MIX_B + d * PAIRS + s, after * same(high[d][1], low[s][1]))
    put(MINE_F, jnp.where(odd == 1, open_0, one))
    put(MINE_F + 1, odd)
    put(MINE_B, jnp.where(odd == 1, one, close_1))
    put(MINE_B + 1, even)
    put(THEIRS_F, jnp.where(odd == 1, one, open_0))
    put(THEIRS_F + 1, even)
    put(THEIRS_B, jnp.where(odd == 1, close_1, one))
    put(THEIRS_B + 1, odd)


def keep_kernel(
    total, split, len_hbm, q_ref, k_ref, v_ref, g_ref, rows_ref, root_ref, out_ref, t_ref, coef_ref, len_ref, len_sem
):
    rows = q_ref.shape[0]
    len_copy = pltpu.make_async_copy(len_hbm, len_ref, len_sem)
    len_copy.start()

    def run(kind):
        t_from, x_ref = (q_ref, g_ref) if kind else (k_ref, v_ref)
        for h in range(out_ref.shape[0]):
            cols = pl.ds(h * HD, HD)
            t = t_from[:, cols].T
            t_ref[h] = t
            out_ref[h] = state_of(kind, t, x_ref[:, cols], rows_ref[kind], root_ref[...])

    on_kind(my_kind(split), run)
    len_copy.wait()
    coefficients(doc_starts(len_ref), rows, total // rows, coef_ref)


def local_kernel(
    total,
    len_hbm,
    q_ref,
    k_ref,
    v_ref,
    g_ref,
    w_ref,
    wt_ref,
    dw_ref,
    dwt_ref,
    sg_ref,
    mask_ref,
    len_ref,
    len_sem,
):
    len_copy = pltpu.make_async_copy(len_hbm, len_ref, len_sem)
    len_copy.start()
    len_copy.wait()
    rows, width = q_ref.shape
    first = lax.axis_index("seq") * rows
    starts = doc_starts(len_ref)
    pos, begin, inv_root = row_facts(starts, first, rows)
    one, none = jnp.ones((), F32), jnp.zeros((), F32)
    mask_ref[0] = jnp.where(pos < min_start(starts, first, total), one, none).astype(BF16)
    suffix = pos >= max_start(starts + [jnp.int32(total)], first + rows + 1)
    mask_ref[1] = jnp.where(suffix, one, none).astype(BF16)
    col = first + lax.broadcasted_iota(jnp.int32, (rows, HD), 1)
    same = (col <= pos) & (col >= begin)
    for h in range(width // HD):
        cols = pl.ds(h * HD, HD)
        q, k, v = q_ref[:, cols], k_ref[:, cols], v_ref[:, cols]
        g = (g_ref[:, cols].astype(F32) * inv_root).astype(BF16)
        sg_ref[:, cols] = g
        w = jnp.where(same, dot(q, k, (1, 1)), 0.0).astype(BF16)
        w_ref[h] = w
        wt_ref[h] = w.T
        dw = jnp.where(same, dot(g, v, (1, 1)), 0.0).astype(BF16)
        dw_ref[h] = dw
        dwt_ref[h] = dw.T


def coef(coef_ref, row):
    return coef_ref[pl.ds(row, 1), :]


def pair_kernel(split, coef_ref, keep_ref, got_ref, *refs):
    out_refs = refs[-PAIRS:]
    per = out_refs[0].shape[0]
    kind = my_kind(split)
    ca, cb = coef(coef_ref, KEEP_F + 2 * kind), coef(coef_ref, GOT_F + 2 * kind)
    for pair, out_ref in zip(slots(), out_refs):
        for i in range(per):
            h = pair * per + i
            out_ref[i] = (keep_ref[h].astype(F32) * ca + got_ref[h].astype(F32) * cb).astype(BF16)


def totals_kernel(split, coef_ref, s0, s1, s2, s3, out_ref):
    row = TOT_F + PAIRS * my_kind(split)
    for i in range(out_ref.shape[0]):
        parts = [s[i].astype(F32) * coef(coef_ref, row + d) for d, s in enumerate((s0, s1, s2, s3))]
        out_ref[i] = sum(parts).astype(BF16)


def scan_kernel(split, enters, coef_ref, *refs):
    sums, out_refs = refs[:PAIRS], refs[-PAIRS:]
    kind = my_kind(split)
    mix, enter = MIX_F + PAIRS * PAIRS * kind, ENTER_F + PAIRS * kind
    for i in range(out_refs[0].shape[0]):
        parts = [s[i].astype(F32) for s in sums]
        for d, out_ref in enumerate(out_refs):
            terms = [
                parts[s] * coef(coef_ref, mix + d * PAIRS + s) for s in range(PAIRS) if s != d
            ]
            if enters:
                terms.append(refs[PAIRS][i].astype(F32) * coef(coef_ref, enter + d))
            out_ref[i] = sum(terms).astype(BF16)


def post_kernel(split, coef_ref, keep_ref, got_ref, *refs):
    mine_ref, theirs_ref = refs[-2:]
    per = refs[0].shape[0]
    kind = my_kind(split)
    m0, m1 = coef(coef_ref, MINE_F + 2 * kind), coef(coef_ref, MINE_F + 2 * kind + 1)
    t0, t1 = coef(coef_ref, THEIRS_F + 2 * kind), coef(coef_ref, THEIRS_F + 2 * kind + 1)
    for d, pair in enumerate(slots()):
        for i in range(per):
            h = pair * per + i
            came = refs[d][i].astype(F32)
            theirs_ref[h] = (came * t0 + keep_ref[h].astype(F32) * t1).astype(BF16)
            mine_ref[h] = (came * m0 + got_ref[h].astype(F32) * m1).astype(BF16)


def outputs_of(kind, fixed_refs, h, state, t):
    q_ref, k_ref, v_ref, g_ref, w_ref, wt_ref, dw_ref, dwt_ref, mask_ref, root_ref = fixed_refs
    cols = pl.ds(h * HD, HD)
    q, k, v, g = q_ref[:, cols], k_ref[:, cols], v_ref[:, cols], g_ref[:, cols]

    def wide(a, b):
        return jnp.concatenate([a, b], axis=1)

    if kind == 0:
        prefix = mask_ref[0]
        o = dot(wide(w_ref[h], q * prefix), jnp.concatenate([v, state], axis=0), (1, 0))
        dq = dot(wide(dw_ref[h], g * prefix), wide(t, state), (1, 1))
        return (o * root_ref[...]).astype(BF16), dq.astype(BF16)
    suffix = mask_ref[1]
    dk = dot(wide(dwt_ref[h], v * suffix), wide(t, state), (1, 1))
    dv = dot(wide(wt_ref[h], k * suffix), jnp.concatenate([g, state], axis=0), (1, 0))
    return dk.astype(BF16), dv.astype(BF16)


def finish_kernel(late, split, chunks, *refs):
    fixed, (t_mine, t_other, odd_ref, even_ref) = refs[:10], refs[10:14]
    outs, bufs, sems = refs[-7:-3], refs[-3:-1], refs[-1]
    if not late:
        outs, done_ref = refs[-8:-4], refs[-4]
        done_ref[...] = jnp.zeros(done_ref.shape, done_ref.dtype)
    heads = odd_ref.shape[0]
    odd = is_odd()
    own = jnp.logical_not(odd) if late else odd
    size = heads * HD // chunks

    def run(kind):
        copies = []
        for c in range(chunks):
            for h in range(c * heads // chunks, (c + 1) * heads // chunks):
                at = pl.ds(h * HD, HD)
                state = jnp.where(odd, odd_ref[h], even_ref[h])
                t = jnp.where(own, t_mine[h], t_other[h])
                bufs[0][:, at], bufs[1][:, at] = outputs_of(kind, fixed, h, state, t)
            at = pl.ds(c * size, size)
            for i in range(2):
                copy = pltpu.make_async_copy(bufs[i].at[:, at], outs[2 * kind + i].at[:, at], sems.at[i, c])
                copy.start()
                copies.append(copy)
        for copy in copies:
            copy.wait()

    early = early_kind(split)
    on_kind(1 - early if late else early, run)


def per_device(queries, keys, values, grad_out, doc_lengths):
    rows, width = queries.shape
    n = lax.axis_size("seq")
    heads = width // HD
    total = rows * n
    split = n == 2 * TEAM
    vmem = pl.BlockSpec(memory_space=pltpu.VMEM)
    hbm = pl.BlockSpec(memory_space=pltpu.HBM)

    def shape(*dims, dtype=BF16):
        return jax.ShapeDtypeStruct(dims, dtype)

    def call(kernel, name, outs, args, specs, out_specs=None, flops=0, scratch=(), room=8, aliases=None):
        moved = sum(a.size * a.dtype.itemsize for a in list(args) + list(outs))
        return pl.pallas_call(
            kernel,
            in_specs=specs,
            out_specs=out_specs or [vmem] * len(outs),
            out_shape=list(outs),
            scratch_shapes=list(scratch),
            input_output_aliases=aliases or {},
            compiler_params=pltpu.CompilerParams(vmem_limit_bytes=int(room * 1024 * 1024)),
            cost_estimate=pl.CostEstimate(flops=flops, bytes_accessed=moved, transcendentals=0),
            name=name,
        )(*args)

    product = 2 * rows * HD * HD
    tokens, mats = shape(rows, width), shape(heads, rows, HD)
    lengths = [pltpu.SMEM(doc_lengths.shape, jnp.int32), pltpu.SemaphoreType.DMA(())]
    chunks = 4
    doc_lengths, send, queries, keys, values, grad_out, t_other, row_masks, root = call(
        functools.partial(send_kernel, total, split, chunks),
        "send",
        [shape(*doc_lengths.shape, dtype=jnp.int32), mats]
        + [tokens] * 4
        + [mats, shape(2, rows, HD), shape(rows, HD, dtype=F32)],
        (doc_lengths, queries, keys, values, grad_out),
        [hbm] * 5,
        [hbm] + [vmem] * 8,
        flops=heads * product,
        scratch=lengths[:1]
        + [pltpu.SemaphoreType.DMA((2, chunks)), pltpu.SemaphoreType.DMA((2,)), pltpu.SemaphoreType.DMA((2,))],
        room=50.5,
    )
    got = lax.ppermute(send, "seq", [(i, i ^ 1) for i in range(n)])
    keep, t_mine, table = call(
        functools.partial(keep_kernel, total, split),
        "keep",
        [mats, mats, shape(COEFS, HD, dtype=F32)],
        (doc_lengths, queries, keys, values, grad_out, row_masks, root),
        [hbm] + [vmem] * 6,
        flops=heads * product,
        scratch=lengths,
    )
    *local, masks = call(
        functools.partial(local_kernel, total),
        "local",
        [mats] * 4 + [tokens, shape(2, rows, HD)],
        (doc_lengths, queries, keys, values, grad_out),
        [hbm] + [vmem] * 4,
        flops=2 * heads * product,
        scratch=lengths,
    )
    w, wt, dw, dwt, scaled = local
    fixed = (queries, keys, values, scaled, w, wt, dw, dwt, masks, root)
    owned = shape(heads // PAIRS, HD, HD)

    def pair(*after):
        kernel = functools.partial(pair_kernel, split)
        return call(kernel, "pair", [owned] * PAIRS, (table, keep, got, *after), [vmem] * (3 + len(after)))

    def trade(parts, devices):
        return [parts[0]] + [
            lax.ppermute(parts[d], "seq", [(i, i ^ (2 * PARTNERS[d])) for i in devices])
            for d in range(1, PAIRS)
        ]

    def edge(sums):
        return call(functools.partial(totals_kernel, split), "totals", [owned], (table, *sums), [vmem] * 5)[0]

    def scan(sums, *enter):
        kernel = functools.partial(scan_kernel, split, bool(enter))
        return call(kernel, "scan", [owned] * PAIRS, (table, *sums, *enter), [vmem] * (5 + len(enter)))

    def post(entering, *after):
        kernel = functools.partial(post_kernel, split)
        args = (table, keep, got, *entering, *after)
        return call(kernel, "post", [mats] * 2, args, [vmem] * len(args))

    def finish(late, states, before):
        kernel = functools.partial(finish_kernel, late, split, chunks)
        args = (*fixed, t_mine, t_other, *states, *before)
        done = [] if late else [shape(8, HD, dtype=F32)]
        return call(
            kernel,
            "late" if late else "early",
            [tokens] * 4 + done,
            args,
            [vmem] * 14 + [hbm] * len(before),
            [hbm] * 4 + [vmem] * len(done),
            flops=4 * heads * product,
            scratch=[pltpu.VMEM((rows, width), BF16)] * 2 + [pltpu.SemaphoreType.DMA((2, chunks))],
            aliases={14 + i: i for i in range(len(before))},
        )

    odds, evens = range(1, n, 2), range(0, n, 2)
    if split:
        sums = trade(pair(), odds)
        late_sums = trade(pair(masks), evens)
        enter = lax.ppermute(edge(sums), "seq", [(i, (i ^ TEAM) - 1) for i in odds])
        mine, theirs = post(trade(scan(sums), odds))
        early_states = (mine, lax.ppermute(theirs, "seq", [(i, i - 1) for i in odds]))
        *outs, _ = finish(False, early_states, ())
        mine, theirs = post(trade(scan(late_sums, enter), evens))
        late_states = (lax.ppermute(theirs, "seq", [(i, i + 1) for i in evens]), mine)
    else:
        sums = trade(pair(), range(n))
        ups = [(i, i + TEAM) for i in odds if i + TEAM < n]
        enter = lax.ppermute(edge(sums), "seq", ups + [(i, i - TEAM) for i in evens if i >= TEAM])
        mine, theirs = post(trade(scan(sums, enter), range(n)))
        other = lax.ppermute(theirs, "seq", [(i, i ^ 1) for i in range(n)])
        early_states, late_states = (mine, other), (other, mine)
        *outs, _ = finish(False, early_states, ())
    return tuple(finish(True, late_states, outs))


def solution(mesh):
    placed = P(("groups", "seq"), None)
    return jax.shard_map(
        per_device,
        mesh=mesh,
        in_specs=(placed,) * 4 + (P("groups"),),
        out_specs=(placed,) * 4,
        check_vma=False,
    )
```

time: 32 us -> 47.1 us (1.47)
  starting transfers between devices: 19.3 us -> 29.1 us
  waiting for transfers between devices: 3.32 us -> 6.21 us
  Pallas kernels: 7.85 us -> 9.81 us
    ppermute x16, starting transfers between devices: 19.3 us -> 29.1 us  [the longest x12 24.7 us: trade(): lax.ppermute(parts[d], 'seq', [(i, i ^ 2 * PARTNERS[d]) for i in devices])]
    ppermute x16, waiting for transfers between devices: 3.32 us -> 6.21 us  [the longest x12 3.06 us: trade(): lax.ppermute(parts[d], 'seq', [(i, i ^ 2 * PARTNERS[d]) for i in devices])]
    pallas_call x11 -> x12, Pallas kernels: 7.85 us -> 9.81 us  [call(): pl.pallas_call(kernel, in_specs=specs, out_specs=out_specs or [vmem] * le...]
  transfers between devices with their start and end apart: 16 -> 16, of which waited for: 6 -> 4; matrix products, arithmetic and copies ran while one was open for 0% -> 0% of each run, Pallas kernels for 13% -> 13%
where the time goes in v10:
time: 47.1 us; the launch traced here: 46.7 us
  starting transfers between devices  29.1 us (62%)
  Pallas kernels  9.81 us (21%)
  waiting for transfers between devices  6.21 us (13%)
  between operations  0.92 us (2%)
  local copies, waits for them, and re-layouts  0.65 us (1%)
    ppermute x12, starting transfers between devices, trade(): lax.ppermute(parts[d], 'seq', [(i, i ^ 2 * PARTNERS[d]) for i in devices])  24.7 us
    pallas_call x12, Pallas kernels, call(): pl.pallas_call(kernel, in_specs=specs, out_specs=out_specs or [vmem] * le...  9.81 us
    ppermute x12, waiting for transfers between devices, trade(): lax.ppermute(parts[d], 'seq', [(i, i ^ 2 * PARTNERS[d]) for i in devices])  3.06 us
    ppermute x1, waiting for transfers between devices, per_device(): enter = lax.ppermute(edge(sums), 'seq', [(i, (i ^ TEAM) - 1) for i in odds])  2.46 us
    ppermute x1, starting transfers between devices, per_device(): lax.ppermute(theirs, 'seq', [(i, i + 1) for i in evens])  1.32 us
    ppermute x1, starting transfers between devices, per_device(): enter = lax.ppermute(edge(sums), 'seq', [(i, (i ^ TEAM) - 1) for i in odds])  1.29 us
    ppermute x1, starting transfers between devices, per_device(): lax.ppermute(theirs, 'seq', [(i, i - 1) for i in odds])  1.29 us
  transfers between devices with their start and end apart: 16, of which 4 were waited for; matrix products, arithmetic and copies ran while one was open for 0% of the time, Pallas kernels for 13%

profile of v10, /device:TPU:0, one launch (start us, length us, event | category | flops | bytes accessed | tf_op | source)
XLA Modules:
  0.0 46.7 jit_solution(7697917188353277091)
XLA Ops:
  0.6 0.6 %copy-done = s32[8]{0:T(128)S(1)} copy-done((s32[8]{0:T(128)S(1)}, s32[8]{0:T(128)}, u32[]{:S(2)}) %copy-start) | copy-done | bytes 56
  1.3 2.1 %send.1 = (s32[8]{0:T(128)S(1)}, bf16[16,128,128]{2,1,0:T(8,128)(2,1)S(1)}, bf16[128,2048]{1,0:T(8,128)(2,1)S(1)}, bf16[128,2048]{1,0:T(8,128)(2,1)S(1)}, bf16[1...) custom-call(s32[8]{0:T(128)S(1)} %copy-done, ...), custom_call_target="tpu_custom_call" | custom-call | flops 67108864 | bytes 5374016 | tf_op jit(solution)/shard_map/send/pallas_call | solution.py:399
  3.4 0.5 %collective-permute-start = (bf16[16,128,128]{2,1,0:T(8,128)(2,1)S(1)}, bf16[16,128,128]{2,1,0:T(8,128)(2,1)S(1)}, u32[]{:S(2)}, u32[]{:S(2)}) collective-permute-start(bf16[16,128,128]{2,1,0:T(8,128)(2,1)S(1)} %get-tuple-element.63), channel_id=1, source_target_pairs={{0,1},{1,0},{2,3},{3,2},{4,5},{5,4},{6,7},{7,6},{8,9},{9,8},{10,11... | collective-permute-start | bytes 1572872 | tf_op jit(solution)/shard_map/ppermute | solution.py:429
  3.9 0.8 %keep.1 = (bf16[16,128,128]{2,1,0:T(8,128)(2,1)S(1)}, bf16[16,128,128]{2,1,0:T(8,128)(2,1)S(1)}, f32[64,128]{1,0:T(8,128)S(1)}) custom-call(s32[8]{0:T(128)S(1)} %get-tuple-element.49.len_hbm, bf16[128,2048]{1,0:T(8,128)(2,1)S(1)} %get-tuple-element.46.q_ref.refs_0_, bf16[128,2048]{1,0:T(8,128)(2,1)S(1)} %get-tuple-element.47.k_ref.refs_1_, ...), custom_call_target="tpu_custom_call" | custom-call | flops 67108864 | bytes 3309600 | tf_op jit(solution)/shard_map/keep/pallas_call | solution.py:399
  4.8 0.7 %collective-permute-done.got_ref = bf16[16,128,128]{2,1,0:T(8,128)(2,1)S(1)} collective-permute-done((bf16[16,128,128]{2,1,0:T(8,128)(2,1)S(1)}, bf16[16,128,128]{2,1,0:T(8,128)(2,1)S(1)}, u32[]{:S(2)}, u32[]{:S(2)}) %collective-permute-start) | collective-permute-done | bytes 524320 | tf_op jit(solution)/shard_map/ppermute | solution.py:429
  5.5 0.2 pair.3
  5.6 0.7 %collective-permute-start.4 = (bf16[4,128,128]{2,1,0:T(8,128)(2,1)S(1)}, bf16[4,128,128]{2,1,0:T(8,128)(2,1)S(1)}, u32[]{:S(2)}, u32[]{:S(2)}) collective-permute-start(bf16[4,128,128]{2,1,0:T(8,128)(2,1)S(1)} %get-tuple-element.69), channel_id=1, source_target_pairs={{1,7},{3,5},{5,3},{7,1},{9,15},{11,13},{13,11},{15,9},{17,23},{19,... | collective-permute-start | bytes 393224 | tf_op jit(solution)/shard_map/ppermute | solution.py:458
  6.3 0.7 %collective-permute-start.5 = (bf16[4,128,128]{2,1,0:T(8,128)(2,1)S(1)}, bf16[4,128,128]{2,1,0:T(8,128)(2,1)S(1)}, u32[]{:S(2)}, u32[]{:S(2)}) collective-permute-start(bf16[4,128,128]{2,1,0:T(8,128)(2,1)S(1)} %get-tuple-element.70), channel_id=1, source_target_pairs={{1,3},{3,1},{5,7},{7,5},{9,11},{11,9},{13,15},{15,13},{17,19},{19,... | collective-permute-start | bytes 393224 | tf_op jit(solution)/shard_map/ppermute | solution.py:458
  7.0 0.7 %collective-permute-start.6 = (bf16[4,128,128]{2,1,0:T(8,128)(2,1)S(1)}, bf16[4,128,128]{2,1,0:T(8,128)(2,1)S(1)}, u32[]{:S(2)}, u32[]{:S(2)}) collective-permute-start(bf16[4,128,128]{2,1,0:T(8,128)(2,1)S(1)} %get-tuple-element.71), channel_id=1, source_target_pairs={{1,5},{3,7},{5,1},{7,3},{9,13},{11,15},{13,9},{15,11},{17,21},{19,... | collective-permute-start | bytes 393224 | tf_op jit(solution)/shard_map/ppermute | solution.py:458
  7.7 1.3 %local.1 = (bf16[16,128,128]{2,1,0:T(8,128)(2,1)S(1)}, bf16[16,128,128]{2,1,0:T(8,128)(2,1)S(1)}, bf16[16,128,128]{2,1,0:T(8,128)(2,1)S(1)}, bf16[16,128,128]{2,...) custom-call(s32[8]{0:T(128)S(1)} %get-tuple-element.49.len_hbm, ...), custom_call_target="tpu_custom_call" | custom-call | flops 134217728 | bytes 4784160 | tf_op jit(solution)/shard_map/local/pallas_call | solution.py:399
  9.0 0.2 pair.2
  9.2 5.8 %collective-permute-start.1 = (bf16[4,128,128]{2,1,0:T(8,128)(2,1)S(1)}, bf16[4,128,128]{2,1,0:T(8,128)(2,1)S(1)}, u32[]{:S(2)}, u32[]{:S(2)}) collective-permute-start(bf16[4,128,128]{2,1,0:T(8,128)(2,1)S(1)} %get-tuple-element.65), channel_id=1, source_target_pairs={{0,6},{2,4},{4,2},{6,0},{8,14},{10,12},{12,10},{14,8},{16,22},{18,... | collective-permute-start | bytes 393224 | tf_op jit(solution)/shard_map/ppermute | solution.py:458
  15.1 2.4 %collective-permute-start.2 = (bf16[4,128,128]{2,1,0:T(8,128)(2,1)S(1)}, bf16[4,128,128]{2,1,0:T(8,128)(2,1)S(1)}, u32[]{:S(2)}, u32[]{:S(2)}) collective-permute-start(bf16[4,128,128]{2,1,0:T(8,128)(2,1)S(1)} %get-tuple-element.66), channel_id=1, source_target_pairs={{0,2},{2,0},{4,6},{6,4},{8,10},{10,8},{12,14},{14,12},{16,18},{18,... | collective-permute-start | bytes 393224 | tf_op jit(solution)/shard_map/ppermute | solution.py:458
  17.5 2.0 %collective-permute-start.3 = (bf16[4,128,128]{2,1,0:T(8,128)(2,1)S(1)}, bf16[4,128,128]{2,1,0:T(8,128)(2,1)S(1)}, u32[]{:S(2)}, u32[]{:S(2)}) collective-permute-start(bf16[4,128,128]{2,1,0:T(8,128)(2,1)S(1)} %get-tuple-element.67), channel_id=1, source_target_pairs={{0,4},{2,6},{4,0},{6,2},{8,12},{10,14},{12,8},{14,10},{16,20},{18,... | collective-permute-start | bytes 393224 | tf_op jit(solution)/shard_map/ppermute | solution.py:458
  19.6 1.3 %collective-permute-start.7 = (bf16[4,128,128]{2,1,0:T(8,128)(2,1)S(1)}, bf16[4,128,128]{2,1,0:T(8,128)(2,1)S(1)}, u32[]{:S(2)}, u32[]{:S(2)}) collective-permute-start(bf16[4,128,128]{2,1,0:T(8,128)(2,1)S(1)} %totals.1), channel_id=1, source_target_pairs={{1,8},{3,10},{5,12},{7,14},{9,0},{11,2},{13,4},{15,6},{17,24},{19,... | collective-permute-start | bytes 393224 | tf_op jit(solution)/shard_map/ppermute | solution.py:494
  20.9 0.2 scan.3
  21.2 0.7 %collective-permute-start.12 = (bf16[4,128,128]{2,1,0:T(8,128)(2,1)S(1)}, bf16[4,128,128]{2,1,0:T(8,128)(2,1)S(1)}, u32[]{:S(2)}, u32[]{:S(2)}) collective-permute-start(bf16[4,128,128]{2,1,0:T(8,128)(2,1)S(1)} %get-tuple-element.79), channel_id=1, source_target_pairs={{1,7},{3,5},{5,3},{7,1},{9,15},{11,13},{13,11},{15,9},{17,23},{19,... | collective-permute-start | bytes 393224 | tf_op jit(solution)/shard_map/ppermute | solution.py:458
  21.8 0.7 %collective-permute-start.13 = (bf16[4,128,128]{2,1,0:T(8,128)(2,1)S(1)}, bf16[4,128,128]{2,1,0:T(8,128)(2,1)S(1)}, u32[]{:S(2)}, u32[]{:S(2)}) collective-permute-start(bf16[4,128,128]{2,1,0:T(8,128)(2,1)S(1)} %get-tuple-element.80), channel_id=1, source_target_pairs={{1,3},{3,1},{5,7},{7,5},{9,11},{11,9},{13,15},{15,13},{17,19},{19,... | collective-permute-start | bytes 393224 | tf_op jit(solution)/shard_map/ppermute | solution.py:458
  22.5 0.7 %collective-permute-start.14 = (bf16[4,128,128]{2,1,0:T(8,128)(2,1)S(1)}, bf16[4,128,128]{2,1,0:T(8,128)(2,1)S(1)}, u32[]{:S(2)}, u32[]{:S(2)}) collective-permute-start(bf16[4,128,128]{2,1,0:T(8,128)(2,1)S(1)} %get-tuple-element.81), channel_id=1, source_target_pairs={{1,5},{3,7},{5,1},{7,3},{9,13},{11,15},{13,9},{15,11},{17,21},{19,... | collective-permute-start | bytes 393224 | tf_op jit(solution)/shard_map/ppermute | solution.py:458
  23.2 1.1 %collective-permute-done.3.refs_3_ = bf16[4,128,128]{2,1,0:T(8,128)(2,1)S(1)} collective-permute-done((bf16[4,128,128]{2,1,0:T(8,128)(2,1)S(1)}, bf16[4,128,128]{2,1,0:T(8,128)(2,1)S(1)}, u32[]{:S(2)}, u32[]{:S(2)}) %collective-permute-start.3) | collective-permute-done | bytes 131104 | tf_op jit(solution)/shard_map/ppermute | solution.py:458
  24.4 2.5 %collective-permute-done.7.refs_4_ = bf16[4,128,128]{2,1,0:T(8,128)(2,1)S(1)} collective-permute-done((bf16[4,128,128]{2,1,0:T(8,128)(2,1)S(1)}, bf16[4,128,128]{2,1,0:T(8,128)(2,1)S(1)}, u32[]{:S(2)}, u32[]{:S(2)}) %collective-permute-start.7) | collective-permute-done | bytes 131104 | tf_op jit(solution)/shard_map/ppermute | solution.py:494
  26.8 0.3 scan.2
  27.1 4.9 %collective-permute-start.8 = (bf16[4,128,128]{2,1,0:T(8,128)(2,1)S(1)}, bf16[4,128,128]{2,1,0:T(8,128)(2,1)S(1)}, u32[]{:S(2)}, u32[]{:S(2)}) collective-permute-start(bf16[4,128,128]{2,1,0:T(8,128)(2,1)S(1)} %get-tuple-element.73), channel_id=1, source_target_pairs={{0,6},{2,4},{4,2},{6,0},{8,14},{10,12},{12,10},{14,8},{16,22},{18,... | collective-permute-start | bytes 393224 | tf_op jit(solution)/shard_map/ppermute | solution.py:458
  32.1 2.3 %collective-permute-start.9 = (bf16[4,128,128]{2,1,0:T(8,128)(2,1)S(1)}, bf16[4,128,128]{2,1,0:T(8,128)(2,1)S(1)}, u32[]{:S(2)}, u32[]{:S(2)}) collective-permute-start(bf16[4,128,128]{2,1,0:T(8,128)(2,1)S(1)} %get-tuple-element.74), channel_id=1, source_target_pairs={{0,2},{2,0},{4,6},{6,4},{8,10},{10,8},{12,14},{14,12},{16,18},{18,... | collective-permute-start | bytes 393224 | tf_op jit(solution)/shard_map/ppermute | solution.py:458
  34.4 3.3 %collective-permute-start.10 = (bf16[4,128,128]{2,1,0:T(8,128)(2,1)S(1)}, bf16[4,128,128]{2,1,0:T(8,128)(2,1)S(1)}, u32[]{:S(2)}, u32[]{:S(2)}) collective-permute-start(bf16[4,128,128]{2,1,0:T(8,128)(2,1)S(1)} %get-tuple-element.75), channel_id=1, source_target_pairs={{0,4},{2,6},{4,0},{6,2},{8,12},{10,14},{12,8},{14,10},{16,20},{18,... | collective-permute-start | bytes 393224 | tf_op jit(solution)/shard_map/ppermute | solution.py:458
  37.7 0.4 post.3
  38.1 1.3 %collective-permute-start.15 = (bf16[16,128,128]{2,1,0:T(8,128)(2,1)S(1)}, bf16[16,128,128]{2,1,0:T(8,128)(2,1)S(1)}, u32[]{:S(2)}, u32[]{:S(2)}) collective-permute-start(bf16[16,128,128]{2,1,0:T(8,128)(2,1)S(1)} %get-tuple-element.83), channel_id=1, source_target_pairs={{1,0},{3,2},{5,4},{7,6},{9,8},{11,10},{13,12},{15,14},{17,16},{19,... | collective-permute-start | bytes 1572872 | tf_op jit(solution)/shard_map/ppermute | solution.py:496
  39.4 1.9 %collective-permute-done.10.refs_3_ = bf16[4,128,128]{2,1,0:T(8,128)(2,1)S(1)} collective-permute-done((bf16[4,128,128]{2,1,0:T(8,128)(2,1)S(1)}, bf16[4,128,128]{2,1,0:T(8,128)(2,1)S(1)}, u32[]{:S(2)}, u32[]{:S(2)}) %collective-permute-start.10) | collective-permute-done | bytes 131104 | tf_op jit(solution)/shard_map/ppermute | solution.py:458
  41.3 0.4 post.2
  41.6 1.3 %collective-permute-start.11 = (bf16[16,128,128]{2,1,0:T(8,128)(2,1)S(1)}, bf16[16,128,128]{2,1,0:T(8,128)(2,1)S(1)}, u32[]{:S(2)}, u32[]{:S(2)}) collective-permute-start(bf16[16,128,128]{2,1,0:T(8,128)(2,1)S(1)} %get-tuple-element.76), channel_id=1, source_target_pairs={{0,1},{2,3},{4,5},{6,7},{8,9},{10,11},{12,13},{14,15},{16,17},{18,... | collective-permute-start | bytes 1572872 | tf_op jit(solution)/shard_map/ppermute | solution.py:499
  43.0 2.2 %early.1 = (bf16[128,2048]{1,0:T(8,128)(2,1)}, bf16[128,2048]{1,0:T(8,128)(2,1)}, bf16[128,2048]{1,0:T(8,128)(2,1)}, bf16[128,2048]{1,0:T(8,128)(2,1)}, f32[8,128]{1,0:T(8,128)}) custom-call(bf16[128,2048]{1,0:T(8,128)(2,1)S(1)} %get-tuple-element.46.q_ref.refs_0_, bf16[128,2048]{1,0:T(8,128)(2,1)S(1)} %get-tuple-element.47.k_ref.refs_1_, ...), custom_call_target="tpu_custom_call" | custom-call | flops 268435456 | bytes 8523776 | tf_op jit(solution)/shard_map/early/pallas_call | solution.py:399
  45.2 1.6 %late.1 = (bf16[128,2048]{1,0:T(8,128)(2,1)}, bf16[128,2048]{1,0:T(8,128)(2,1)}, bf16[128,2048]{1,0:T(8,128)(2,1)}, bf16[128,2048]{1,0:T(8,128)(2,1)}) custom-call(bf16[128,2048]{1,0:T(8,128)(2,1)S(1)} %get-tuple-element.46.q_ref.refs_0_, ...), custom_call_target="tpu_custom_call", output_to_operand_aliasing={{0}: (14, {}), {1}: (15, {}), {2}: (16, {}), {3}: (17, {})} | custom-call | flops 268435456 | bytes 10616832 | tf_op jit(solution)/shard_map/late/pallas_call | solution.py:399
  (14 shorter events, 0.2 us)
Async XLA Ops:
  0.6 0.7 %copy-start = (s32[8]{0:T(128)S(1)}, s32[8]{0:T(128)}, u32[]{:S(2)}) copy-start(s32[8]{0:T(128)} %len_hbm.1) | copy-start | bytes 100
  3.4 2.1 %collective-permute-start = (bf16[16,128,128]{2,1,0:T(8,128)(2,1)S(1)}, bf16[16,128,128]{2,1,0:T(8,128)(2,1)S(1)}, u32[]{:S(2)}, u32[]{:S(2)}) collective-permute-start(bf16[16,128,128]{2,1,0:T(8,128)(2,1)S(1)} %get-tuple-element.63), channel_id=1, source_target_pairs={{0,1},{1,0},{2,3},{3,2},{4,5},{5,4},{6,7},{7,6},{8,9},{9,8},{10,11... | collective-permute-start | bytes 1572872 | tf_op jit(solution)/shard_map/ppermute | solution.py:429
  5.6 11.8 %collective-permute-start.4 = (bf16[4,128,128]{2,1,0:T(8,128)(2,1)S(1)}, bf16[4,128,128]{2,1,0:T(8,128)(2,1)S(1)}, u32[]{:S(2)}, u32[]{:S(2)}) collective-permute-start(bf16[4,128,128]{2,1,0:T(8,128)(2,1)S(1)} %get-tuple-element.69), channel_id=1, source_target_pairs={{1,7},{3,5},{5,3},{7,1},{9,15},{11,13},{13,11},{15,9},{17,23},{19,... | collective-permute-start | bytes 393224 | tf_op jit(solution)/shard_map/ppermute | solution.py:458
  6.3 13.2 %collective-permute-start.5 = (bf16[4,128,128]{2,1,0:T(8,128)(2,1)S(1)}, bf16[4,128,128]{2,1,0:T(8,128)(2,1)S(1)}, u32[]{:S(2)}, u32[]{:S(2)}) collective-permute-start(bf16[4,128,128]{2,1,0:T(8,128)(2,1)S(1)} %get-tuple-element.70), channel_id=1, source_target_pairs={{1,3},{3,1},{5,7},{7,5},{9,11},{11,9},{13,15},{15,13},{17,19},{19,... | collective-permute-start | bytes 393224 | tf_op jit(solution)/shard_map/ppermute | solution.py:458
  7.0 12.5 %collective-permute-start.6 = (bf16[4,128,128]{2,1,0:T(8,128)(2,1)S(1)}, bf16[4,128,128]{2,1,0:T(8,128)(2,1)S(1)}, u32[]{:S(2)}, u32[]{:S(2)}) collective-permute-start(bf16[4,128,128]{2,1,0:T(8,128)(2,1)S(1)} %get-tuple-element.71), channel_id=1, source_target_pairs={{1,5},{3,7},{5,1},{7,3},{9,13},{11,15},{13,9},{15,11},{17,21},{19,... | collective-permute-start | bytes 393224 | tf_op jit(solution)/shard_map/ppermute | solution.py:458
  9.2 12.6 %collective-permute-start.1 = (bf16[4,128,128]{2,1,0:T(8,128)(2,1)S(1)}, bf16[4,128,128]{2,1,0:T(8,128)(2,1)S(1)}, u32[]{:S(2)}, u32[]{:S(2)}) collective-permute-start(bf16[4,128,128]{2,1,0:T(8,128)(2,1)S(1)} %get-tuple-element.65), channel_id=1, source_target_pairs={{0,6},{2,4},{4,2},{6,0},{8,14},{10,12},{12,10},{14,8},{16,22},{18,... | collective-permute-start | bytes 393224 | tf_op jit(solution)/shard_map/ppermute | solution.py:458
  15.1 7.5 %collective-permute-start.2 = (bf16[4,128,128]{2,1,0:T(8,128)(2,1)S(1)}, bf16[4,128,128]{2,1,0:T(8,128)(2,1)S(1)}, u32[]{:S(2)}, u32[]{:S(2)}) collective-permute-start(bf16[4,128,128]{2,1,0:T(8,128)(2,1)S(1)} %get-tuple-element.66), channel_id=1, source_target_pairs={{0,2},{2,0},{4,6},{6,4},{8,10},{10,8},{12,14},{14,12},{16,18},{18,... | collective-permute-start | bytes 393224 | tf_op jit(solution)/shard_map/ppermute | solution.py:458
  17.5 6.9 %collective-permute-start.3 = (bf16[4,128,128]{2,1,0:T(8,128)(2,1)S(1)}, bf16[4,128,128]{2,1,0:T(8,128)(2,1)S(1)}, u32[]{:S(2)}, u32[]{:S(2)}) collective-permute-start(bf16[4,128,128]{2,1,0:T(8,128)(2,1)S(1)} %get-tuple-element.67), channel_id=1, source_target_pairs={{0,4},{2,6},{4,0},{6,2},{8,12},{10,14},{12,8},{14,10},{16,20},{18,... | collective-permute-start | bytes 393224 | tf_op jit(solution)/shard_map/ppermute | solution.py:458
  19.6 7.2 %collective-permute-start.7 = (bf16[4,128,128]{2,1,0:T(8,128)(2,1)S(1)}, bf16[4,128,128]{2,1,0:T(8,128)(2,1)S(1)}, u32[]{:S(2)}, u32[]{:S(2)}) collective-permute-start(bf16[4,128,128]{2,1,0:T(8,128)(2,1)S(1)} %totals.1), channel_id=1, source_target_pairs={{1,8},{3,10},{5,12},{7,14},{9,0},{11,2},{13,4},{15,6},{17,24},{19,... | collective-permute-start | bytes 393224 | tf_op jit(solution)/shard_map/ppermute | solution.py:494
  21.2 13.2 %collective-permute-start.12 = (bf16[4,128,128]{2,1,0:T(8,128)(2,1)S(1)}, bf16[4,128,128]{2,1,0:T(8,128)(2,1)S(1)}, u32[]{:S(2)}, u32[]{:S(2)}) collective-permute-start(bf16[4,128,128]{2,1,0:T(8,128)(2,1)S(1)} %get-tuple-element.79), channel_id=1, source_target_pairs={{1,7},{3,5},{5,3},{7,1},{9,15},{11,13},{13,11},{15,9},{17,23},{19,... | collective-permute-start | bytes 393224 | tf_op jit(solution)/shard_map/ppermute | solution.py:458
  21.8 15.8 %collective-permute-start.13 = (bf16[4,128,128]{2,1,0:T(8,128)(2,1)S(1)}, bf16[4,128,128]{2,1,0:T(8,128)(2,1)S(1)}, u32[]{:S(2)}, u32[]{:S(2)}) collective-permute-start(bf16[4,128,128]{2,1,0:T(8,128)(2,1)S(1)} %get-tuple-element.80), channel_id=1, source_target_pairs={{1,3},{3,1},{5,7},{7,5},{9,11},{11,9},{13,15},{15,13},{17,19},{19,... | collective-permute-start | bytes 393224 | tf_op jit(solution)/shard_map/ppermute | solution.py:458
  22.5 15.1 %collective-permute-start.14 = (bf16[4,128,128]{2,1,0:T(8,128)(2,1)S(1)}, bf16[4,128,128]{2,1,0:T(8,128)(2,1)S(1)}, u32[]{:S(2)}, u32[]{:S(2)}) collective-permute-start(bf16[4,128,128]{2,1,0:T(8,128)(2,1)S(1)} %get-tuple-element.81), channel_id=1, source_target_pairs={{1,5},{3,7},{5,1},{7,3},{9,13},{11,15},{13,9},{15,11},{17,21},{19,... | collective-permute-start | bytes 393224 | tf_op jit(solution)/shard_map/ppermute | solution.py:458
  27.1 12.2 %collective-permute-start.8 = (bf16[4,128,128]{2,1,0:T(8,128)(2,1)S(1)}, bf16[4,128,128]{2,1,0:T(8,128)(2,1)S(1)}, u32[]{:S(2)}, u32[]{:S(2)}) collective-permute-start(bf16[4,128,128]{2,1,0:T(8,128)(2,1)S(1)} %get-tuple-element.73), channel_id=1, source_target_pairs={{0,6},{2,4},{4,2},{6,0},{8,14},{10,12},{12,10},{14,8},{16,22},{18,... | collective-permute-start | bytes 393224 | tf_op jit(solution)/shard_map/ppermute | solution.py:458
  32.1 7.3 %collective-permute-start.9 = (bf16[4,128,128]{2,1,0:T(8,128)(2,1)S(1)}, bf16[4,128,128]{2,1,0:T(8,128)(2,1)S(1)}, u32[]{:S(2)}, u32[]{:S(2)}) collective-permute-start(bf16[4,128,128]{2,1,0:T(8,128)(2,1)S(1)} %get-tuple-element.74), channel_id=1, source_target_pairs={{0,2},{2,0},{4,6},{6,4},{8,10},{10,8},{12,14},{14,12},{16,18},{18,... | collective-permute-start | bytes 393224 | tf_op jit(solution)/shard_map/ppermute | solution.py:458
  34.4 6.9 %collective-permute-start.10 = (bf16[4,128,128]{2,1,0:T(8,128)(2,1)S(1)}, bf16[4,128,128]{2,1,0:T(8,128)(2,1)S(1)}, u32[]{:S(2)}, u32[]{:S(2)}) collective-permute-start(bf16[4,128,128]{2,1,0:T(8,128)(2,1)S(1)} %get-tuple-element.75), channel_id=1, source_target_pairs={{0,4},{2,6},{4,0},{6,2},{8,12},{10,14},{12,8},{14,10},{16,20},{18,... | collective-permute-start | bytes 393224 | tf_op jit(solution)/shard_map/ppermute | solution.py:458
  38.1 4.9 %collective-permute-start.15 = (bf16[16,128,128]{2,1,0:T(8,128)(2,1)S(1)}, bf16[16,128,128]{2,1,0:T(8,128)(2,1)S(1)}, u32[]{:S(2)}, u32[]{:S(2)}) collective-permute-start(bf16[16,128,128]{2,1,0:T(8,128)(2,1)S(1)} %get-tuple-element.83), channel_id=1, source_target_pairs={{1,0},{3,2},{5,4},{7,6},{9,8},{11,10},{13,12},{15,14},{17,16},{19,... | collective-permute-start | bytes 1572872 | tf_op jit(solution)/shard_map/ppermute | solution.py:496
  41.6 3.5 %collective-permute-start.11 = (bf16[16,128,128]{2,1,0:T(8,128)(2,1)S(1)}, bf16[16,128,128]{2,1,0:T(8,128)(2,1)S(1)}, u32[]{:S(2)}, u32[]{:S(2)}) collective-permute-start(bf16[16,128,128]{2,1,0:T(8,128)(2,1)S(1)} %get-tuple-element.76), channel_id=1, source_target_pairs={{0,1},{2,3},{4,5},{6,7},{8,9},{10,11},{12,13},{14,15},{16,17},{18,... | collective-permute-start | bytes 1572872 | tf_op jit(solution)/shard_map/ppermute | solution.py:499

commit v11 on v9

--- a/solution.py
+++ b/solution.py
@@ -69,6 +69,35 @@
     tail = dot(kt, v * tail_rows, (1, 0))
     head = dot(qt, scaled * head_rows, (1, 0))
     return tail.astype(BF16), head.astype(BF16)
+
+
+def bring(pairs, begin, chunks, sems):
+    width = pairs[0][1].shape[1]
+    size = width // chunks
+    copies = []
+    for c in range(chunks):
+        at = pl.ds(pl.multiple_of(begin * HD + c * size, HD), size)
+        for i, (src, dst) in enumerate(pairs):
+            copy = pltpu.make_async_copy(src.at[:, at], dst.at[:, pl.ds(c * size, size)], sems.at[i, c])
+            copy.start()
+            copies.append(copy)
+    return copies
+
+
+def states_by_chunk(copies, chunks, q_ref, k_ref, v_ref, g_ref, kt_ref, qt_ref, out_ref, masks):
+    per = out_ref.shape[1] // chunks
+    for c in range(chunks):
+        for i, (ref, t_ref) in enumerate(((k_ref, kt_ref), (q_ref, qt_ref))):
+            copies[4 * c + i].wait()
+            for h in range(c * per, (c + 1) * per):
+                t_ref[h] = ref[:, pl.ds(h * HD, HD)].T
+        for copy in copies[4 * c + 2 : 4 * c + 4]:
+            copy.wait()
+        for h in range(c * per, (c + 1) * per):
+            cols = pl.ds(h * HD, HD)
+            tail, head = states_of(kt_ref[h], qt_ref[h], v_ref[:, cols], g_ref[:, cols], *masks)
+            out_ref[0, h] = tail
+            out_ref[1, h] = head
 
 
 def send_kernel(
@@ -94,24 +123,13 @@
     len_sems,
 ):
     rows = q_ref.shape[0]
-    heads = out_ref.shape[1]
     me = lax.axis_index("seq")
-    other = (1 - lax.rem(me, 2)) * heads
-    mine = lax.rem(me, 2) * heads
     len_copy = pltpu.make_async_copy(len_hbm, len_ref, len_sems.at[0])
     len_copy.start()
     len_pass = pltpu.make_async_copy(len_hbm, len_out, len_sems.at[1])
     len_pass.start()
     pairs = ((k_hbm, k_ref), (q_hbm, q_ref), (v_hbm, v_ref), (g_hbm, g_ref))
-    per = heads // chunks
-    copies = []
-    for c in range(2 * chunks):
-        begin = other + c * per if c < chunks else mine + (c - chunks) * per
-        at = pl.ds(pl.multiple_of(begin * HD, HD), per * HD)
-        for i, (src, dst) in enumerate(pairs):
-            copy = pltpu.make_async_copy(src.at[:, at], dst.at[:, at], sems.at[i, c])
-            copy.start()
-            copies.append(copy)
+    copies = bring(pairs, (1 - lax.rem(me, 2)) * out_ref.shape[1], chunks, sems)
     len_copy.wait()
     starts = doc_starts(len_ref)
     first = me * rows
@@ -122,22 +140,9 @@
     rows_ref[0] = tail_rows
     rows_ref[1] = head_rows
     root_ref[...] = inv_root
-    for c in range(chunks):
-        for i, (ref, t_ref) in enumerate(((k_ref, kt_ref), (q_ref, qt_ref))):
-            copies[4 * c + i].wait()
-            for h in range(c * per, (c + 1) * per):
-                t_ref[h] = ref[:, pl.ds(pl.multiple_of((other + h) * HD, HD), HD)].T
-        for copy in copies[4 * c + 2 : 4 * c + 4]:
-            copy.wait()
-        for h in range(c * per, (c + 1) * per):
-            cols = pl.ds(pl.multiple_of((other + h) * HD, HD), HD)
-            tail, head = states_of(
-                kt_ref[h], qt_ref[h], v_ref[:, cols], g_ref[:, cols], tail_rows, head_rows, inv_root
-            )
-            out_ref[0, h] = tail
-            out_ref[1, h] = head
-    for copy in copies[4 * chunks :]:
-        copy.wait()
+    states_by_chunk(
+        copies, chunks, q_ref, k_ref, v_ref, g_ref, kt_ref, qt_ref, out_ref, (tail_rows, head_rows, inv_root)
+    )
     len_pass.wait()
 
 
@@ -197,46 +202,44 @@
 
 
 def keep_kernel(
-    total, len_hbm, q_ref, k_ref, v_ref, g_ref, rows_ref, root_ref, out_ref, kt_ref, qt_ref, coef_ref, len_ref, len_sem
-):
-    rows = q_ref.shape[0]
-    heads = out_ref.shape[1]
-    core = lax.rem(lax.axis_index("seq"), 2)
-    len_copy = pltpu.make_async_copy(len_hbm, len_ref, len_sem)
-    len_copy.start()
-    tail_rows, head_rows, inv_root = rows_ref[0], rows_ref[1], root_ref[...]
-    for h in range(heads):
-        cols = pl.ds(pl.multiple_of((core * heads + h) * HD, HD), HD)
-        kt, qt = k_ref[:, cols].T, q_ref[:, cols].T
-        kt_ref[h] = kt
-        qt_ref[h] = qt
-        tail, head = states_of(kt, qt, v_ref[:, cols], g_ref[:, cols], tail_rows, head_rows, inv_root)
-        out_ref[0, h] = tail
-        out_ref[1, h] = head
-    len_copy.wait()
-    coefficients(doc_starts(len_ref), rows, total // rows, coef_ref)
-
-
-def local_kernel(
     total,
+    chunks,
     len_hbm,
+    q_hbm,
+    k_hbm,
+    v_hbm,
+    g_hbm,
+    rows_ref,
+    root_ref,
+    out_ref,
     q_ref,
     k_ref,
     v_ref,
     g_ref,
-    w_ref,
-    wt_ref,
-    dw_ref,
-    dwt_ref,
-    sg_ref,
-    mask_ref,
+    kt_ref,
+    qt_ref,
+    coef_ref,
     len_ref,
+    sems,
     len_sem,
 ):
+    rows = q_ref.shape[0]
+    len_copy = pltpu.make_async_copy(len_hbm, len_ref, len_sem)
+    len_copy.start()
+    pairs = ((k_hbm, k_ref), (q_hbm, q_ref), (v_hbm, v_ref), (g_hbm, g_ref))
+    copies = bring(pairs, lax.rem(lax.axis_index("seq"), 2) * out_ref.shape[1], chunks, sems)
+    len_copy.wait()
+    coefficients(doc_starts(len_ref), rows, total // rows, coef_ref)
+    masks = rows_ref[0], rows_ref[1], root_ref[...]
+    states_by_chunk(copies, chunks, q_ref, k_ref, v_ref, g_ref, kt_ref, qt_ref, out_ref, masks)
+
+
+def local_kernel(total, len_hbm, *refs):
+    halves, (w_ref, wt_ref, dw_ref, dwt_ref, sg_ref, mask_ref, len_ref, len_sem) = refs[:8], refs[8:]
     len_copy = pltpu.make_async_copy(len_hbm, len_ref, len_sem)
     len_copy.start()
     len_copy.wait()
-    rows, width = q_ref.shape
+    rows, half = halves[0].shape
     first = lax.axis_index("seq") * rows
     starts = doc_starts(len_ref)
     pos, begin, inv_root = row_facts(starts, first, rows)
@@ -246,15 +249,16 @@
     mask_ref[1] = jnp.where(suffix, one, none).astype(BF16)
     col = first + lax.broadcasted_iota(jnp.int32, (rows, HD), 1)
     same = (col <= pos) & (col >= begin)
-    for h in range(width // HD):
-        cols = pl.ds(h * HD, HD)
-        q, k, v = q_ref[:, cols], k_ref[:, cols], v_ref[:, cols]
+    heads = half // HD
+    for h in range(2 * heads):
+        q_ref, k_ref, v_ref, g_ref = halves[h // heads * 4 :][:4]
+        cols = pl.ds(h % heads * HD, HD)
         g = (g_ref[:, cols].astype(F32) * inv_root).astype(BF16)
-        sg_ref[:, cols] = g
-        w = jnp.where(same, dot(q, k, (1, 1)), 0.0).astype(BF16)
+        sg_ref[:, pl.ds(h * HD, HD)] = g
+        w = jnp.where(same, dot(q_ref[:, cols], k_ref[:, cols], (1, 1)), 0.0).astype(BF16)
         w_ref[h] = w
         wt_ref[h] = w.T
-        dw = jnp.where(same, dot(g, v, (1, 1)), 0.0).astype(BF16)
+        dw = jnp.where(same, dot(g, v_ref[:, cols], (1, 1)), 0.0).astype(BF16)
         dw_ref[h] = dw
         dwt_ref[h] = dw.T
 
@@ -329,10 +333,16 @@
         pl.when(kind == choice)(functools.partial(run, choice))
 
 
-def outputs_of(kind, fixed_refs, h, state, kt_ref, qt_ref, i):
-    q_ref, k_ref, v_ref, g_ref, w_ref, wt_ref, dw_ref, dwt_ref, mask_ref, root_ref = fixed_refs
-    cols = pl.ds(pl.multiple_of(h * HD, HD), HD)
-    q, k, v, g = q_ref[:, cols], k_ref[:, cols], v_ref[:, cols], g_ref[:, cols]
+FIXED = 13
+
+
+def outputs_of(kind, fixed_refs, other, state, kt_ref, qt_ref, i):
+    q_ref, k_ref, v_ref = fixed_refs[3 * other :][:3]
+    g_ref, w_ref, wt_ref, dw_ref, dwt_ref, mask_ref, root_ref = fixed_refs[6:]
+    cols = pl.ds(i * HD, HD)
+    q, k, v = q_ref[:, cols], k_ref[:, cols], v_ref[:, cols]
+    h = other * (q_ref.shape[1] // HD) + i
+    g = g_ref[:, pl.ds(h * HD, HD)]
 
     def wide(a, b):
         return jnp.concatenate([a, b], axis=1)
@@ -349,61 +359,58 @@
 
 
 def early_kernel(split, *refs):
-    fixed, (kt_mine, qt_mine, mine_ref, kt_other, qt_other, other_ref), outs = refs[:10], refs[10:16], refs[16:]
-    heads = mine_ref.shape[0]
-    core = lax.rem(lax.axis_index("seq"), 2)
+    fixed, sides, outs = refs[:FIXED], refs[FIXED : FIXED + 6], refs[FIXED + 6 :]
+    heads = sides[2].shape[0]
 
     def run(kind):
-        for half, kt_ref, qt_ref, s_ref in (
-            (core, kt_mine, qt_mine, mine_ref),
-            (1 - core, kt_other, qt_other, other_ref),
-        ):
-            for i in range(heads):
-                h = half * heads + i
-                cols = pl.ds(pl.multiple_of(h * HD, HD), HD)
-                outs[0][:, cols], outs[1][:, cols] = outputs_of(kind, fixed, h, s_ref[i], kt_ref, qt_ref, i)
+        for h in range(2 * heads):
+            kt_ref, qt_ref, s_ref = sides[h // heads * 3 :][:3]
+            at = pl.ds(h * HD, HD)
+            i = h % heads
+            outs[0][:, at], outs[1][:, at] = outputs_of(
+                kind, fixed, h // heads, s_ref[i], kt_ref, qt_ref, i
+            )
 
     on_kind(0, split, run)
 
 
 def late_kernel(split, *refs):
-    fixed, (kt_ref, qt_ref, s_ref), outs = refs[:10], refs[10:13], refs[13:]
-    heads = s_ref.shape[0]
-    half = lax.rem(lax.axis_index("seq"), 2)
+    fixed, (kt_ref, qt_ref, s_ref), outs = refs[:FIXED], refs[FIXED : FIXED + 3], refs[FIXED + 3 :]
 
     def run(kind):
-        for i in range(heads):
+        for i in range(s_ref.shape[0]):
             at = pl.ds(i * HD, HD)
-            outs[0][:, at], outs[1][:, at] = outputs_of(
-                kind, fixed, half * heads + i, s_ref[i], kt_ref, qt_ref, i
-            )
+            outs[0][:, at], outs[1][:, at] = outputs_of(kind, fixed, 0, s_ref[i], kt_ref, qt_ref, i)
 
     on_kind(1, split, run)
 
 
 def last_kernel(split, chunks, *refs):
-    early, fixed, (kt_ref, qt_ref, s_ref), late = refs[:2], refs[2:12], refs[12:15], refs[15:17]
-    outs, bufs, (sems, early_sems, late_sems) = refs[17:21], refs[21:23], refs[23:]
+    early, fixed, (kt_ref, qt_ref, s_ref), late = refs[:2], refs[2 : FIXED + 2], refs[FIXED + 2 :][:3], refs[FIXED + 5 :][:2]
+    outs, bufs, (sems, early_sems, late_sems) = refs[-9:-5], refs[-5:-3], refs[-3:]
     heads = s_ref.shape[0]
     width = heads * HD
     core = lax.rem(lax.axis_index("seq"), 2)
+    mine, other = (pl.ds(pl.multiple_of(x * width, HD), width) for x in (core, 1 - core))
     size = width // chunks
 
     def run(kind):
         early_outs, late_outs = (outs[2:], outs[:2]) if kind == 0 else (outs[:2], outs[2:])
         copies = []
-        to = pl.ds(pl.multiple_of(core * width, HD), width)
         for i in range(2):
-            copies.append(pltpu.make_async_copy(early[i], early_outs[i], early_sems.at[i]))
-            copies.append(pltpu.make_async_copy(late[i], late_outs[i].at[:, to], late_sems.at[i]))
+            for j, to in enumerate((mine, other)):
+                copies.append(
+                    pltpu.make_async_copy(
+                        early[i].at[:, pl.ds(j * width, width)], early_outs[i].at[:, to], early_sems.at[i, j]
+                    )
+                )
+            copies.append(pltpu.make_async_copy(late[i], late_outs[i].at[:, mine], late_sems.at[i]))
         for copy in copies:
             copy.start()
         for c in range(chunks):
             for i in range(c * heads // chunks, (c + 1) * heads // chunks):
                 at = pl.ds(i * HD, HD)
-                bufs[0][:, at], bufs[1][:, at] = outputs_of(
-                    kind, fixed, (1 - core) * heads + i, s_ref[i], kt_ref, qt_ref, i
-                )
+                bufs[0][:, at], bufs[1][:, at] = outputs_of(kind, fixed, 1, s_ref[i], kt_ref, qt_ref, i)
             to = pl.ds(pl.multiple_of((1 - core) * width + c * size, HD), size)
             for i in range(2):
                 copy = pltpu.make_async_copy(
@@ -446,40 +453,45 @@
 
     product = 2 * rows * HD * HD
     states, halves, tokens = shape(2, half, HD, HD), shape(half, HD, HD), shape(rows, width)
+    part = shape(rows, half * HD)
     lengths = [pltpu.SMEM(doc_lengths.shape, jnp.int32), pltpu.SemaphoreType.DMA(())]
+    arrays = (queries, keys, values, grad_out)
     chunks = 2
-    doc_lengths, send, queries, keys, values, grad_out, kt_other, qt_other, row_masks, root = call(
+    doc_lengths, send, *others = call(
         functools.partial(send_kernel, total, chunks),
         "send",
         [shape(*doc_lengths.shape, dtype=jnp.int32), states]
-        + [tokens] * 4
+        + [part] * 4
         + [halves] * 2
         + [shape(2, rows, HD), shape(rows, HD, dtype=F32)],
-        (doc_lengths, queries, keys, values, grad_out),
+        (doc_lengths, *arrays),
         [hbm] * 5,
         [hbm] + [vmem] * 9,
         flops=2 * half * product,
-        scratch=lengths[:1] + [pltpu.SemaphoreType.DMA((4, 2 * chunks)), pltpu.SemaphoreType.DMA((2,))],
-        room=50.5,
-    )
+        scratch=lengths[:1] + [pltpu.SemaphoreType.DMA((4, chunks)), pltpu.SemaphoreType.DMA((2,))],
+        room=51.5,
+    )
+    q_other, k_other, v_other, g_other, kt_other, qt_other, row_masks, root = others
     swap = [(i, i ^ 1) for i in range(n)]
     got = lax.ppermute(send, "seq", swap)
-    keep, kt_mine, qt_mine, table = call(
-        functools.partial(keep_kernel, total),
+    keep, *mines, table = call(
+        functools.partial(keep_kernel, total, chunks),
         "keep",
-        [states, halves, halves, shape(COEFS, HD, dtype=F32)],
-        (doc_lengths, queries, keys, values, grad_out, row_masks, root),
-        [hbm] + [vmem] * 6,
+        [states] + [part] * 4 + [halves] * 2 + [shape(COEFS, HD, dtype=F32)],
+        (doc_lengths, *arrays, row_masks, root),
+        [hbm] * 5 + [vmem] * 2,
         flops=2 * half * product,
-        scratch=lengths,
-    )
+        scratch=lengths[:1] + [pltpu.SemaphoreType.DMA((4, chunks))] + lengths[1:],
+        room=51.5,
+    )
+    q_mine, k_mine, v_mine, g_mine, kt_mine, qt_mine = mines
     mats = shape(heads, rows, HD)
     *local, masks = call(
         functools.partial(local_kernel, total),
         "local",
         [mats] * 4 + [tokens, shape(2, rows, HD)],
-        (doc_lengths, queries, keys, values, grad_out),
-        [hbm] + [vmem] * 4,
+        (doc_lengths, *mines[:4], *others[:4]),
+        [hbm] + [vmem] * 8,
         flops=2 * heads * product,
         scratch=lengths,
     )
@@ -535,14 +547,13 @@
         mine.append(own)
         other.append(lax.ppermute(theirs, "seq", swap))
     w, wt, dw, dwt, scaled = local
-    fixed = (queries, keys, values, scaled, w, wt, dw, dwt, masks, root)
-    part = shape(rows, half * HD)
+    fixed = (*mines[:3], *others[:3], scaled, w, wt, dw, dwt, masks, root)
     early = call(
         functools.partial(early_kernel, split),
         "early",
         [tokens] * 2,
         (*fixed, kt_mine, qt_mine, mine[0], kt_other, qt_other, other[0]),
-        [vmem] * 16,
+        [vmem] * (FIXED + 6),
         flops=8 * half * product,
     )
     late = call(
@@ -550,7 +561,7 @@
         "late",
         [part] * 2,
         (*fixed, kt_mine, qt_mine, mine[1]),
-        [vmem] * 13,
+        [vmem] * (FIXED + 3),
         flops=4 * half * product,
     )
     chunks = 4
@@ -560,11 +571,11 @@
             "last",
             [tokens] * 4,
             (*early, *fixed, kt_other, qt_other, other[1], *late),
-            [vmem] * 17,
+            [vmem] * (FIXED + 7),
             [hbm] * 4,
             flops=4 * half * product,
             scratch=[pltpu.VMEM(part.shape, BF16)] * 2
-            + [pltpu.SemaphoreType.DMA((2, chunks)), pltpu.SemaphoreType.DMA((2,)), pltpu.SemaphoreType.DMA((2,))],
+            + [pltpu.SemaphoreType.DMA((2, chunks)), pltpu.SemaphoreType.DMA((2, 2)), pltpu.SemaphoreType.DMA((2,))],
         )
     )
 

time: 31.5 us -> 31.3 us (level)
  waiting for transfers between devices: 3 us -> 2.42 us
  Pallas kernels: 8.21 us -> 8.71 us
    pallas_call x12, Pallas kernels: 8.21 us -> 8.71 us  [call(): pl.pallas_call(kernel, in_specs=specs, out_specs=out_specs or [vmem] * le...]
    ppermute x1, waiting for transfers between devices: 0.37 us -> 0.01 us  [per_device(): got = lax.ppermute(send, 'seq', swap)]
  transfers between devices with their start and end apart: 16 -> 16, of which waited for: 5 -> 4; matrix products, arithmetic and copies ran while one was open for 0% -> 0% of each run, Pallas kernels for 14% -> 17%
where the time goes in v11:
time: 31.3 us; the launch traced here: 31.1 us
  starting transfers between devices  18.6 us (59%)
  Pallas kernels  8.71 us (28%)
  waiting for transfers between devices  2.42 us (8%)
  between operations  0.76 us (2%)
  local copies, waits for them, and re-layouts  0.65 us (2%)
    ppermute x12, starting transfers between devices, trade(): lax.ppermute(parts[d], 'seq', [(i, i ^ 2 * PARTNERS[d]) for i in range(n)])  15.2 us
    pallas_call x12, Pallas kernels, call(): pl.pallas_call(kernel, in_specs=specs, out_specs=out_specs or [vmem] * le...  8.71 us
    ppermute x1, starting transfers between devices, per_device(): enter = lax.ppermute(edge(0), 'seq', up + down)  2.66 us
    ppermute x12, waiting for transfers between devices, trade(): lax.ppermute(parts[d], 'seq', [(i, i ^ 2 * PARTNERS[d]) for i in range(n)])  2.12 us
    unnamed x2, local copies, waits for them, and re-layouts  0.65 us
  transfers between devices with their start and end apart: 16, of which 4 were waited for; matrix products, arithmetic and copies ran while one was open for 0% of the time, Pallas kernels for 17%

profile of v11, /device:TPU:0, one launch (start us, length us, event | category | flops | bytes accessed | tf_op | source)
XLA Modules:
  0.0 31.1 jit_solution(9411650313573027808)
XLA Ops:
  0.6 0.6 %copy-done = s32[8]{0:T(128)S(1)} copy-done((s32[8]{0:T(128)S(1)}, s32[8]{0:T(128)}, u32[]{:S(2)}) %copy-start) | copy-done | bytes 56
  1.3 1.8 %send.1 = (s32[8]{0:T(128)S(1)}, bf16[2,8,128,128]{3,2,1,0:T(8,128)(2,1)S(1)}, bf16[128,1024]{1,0:T(8,128)(2,1)S(1)}, bf16[128,1024]{1,0:T(8,128)(2,1)S(1)}, bf1...) custom-call(s32[8]{0:T(128)S(1)} %copy-done, ...), custom_call_target="tpu_custom_call" | custom-call | flops 67108864 | bytes 4325440 | tf_op jit(solution)/shard_map/send/pallas_call | solution.py:443
  3.1 0.5 %collective-permute-start = (bf16[2,8,128,128]{3,2,1,0:T(8,128)(2,1)S(1)}, bf16[2,8,128,128]{3,2,1,0:T(8,128)(2,1)S(1)}, u32[]{:S(2)}, u32[]{:S(2)}) collective-permute-start(bf16[2,8,128,128]{3,2,1,0:T(8,128)(2,1)S(1)} %get-tuple-element.73), channel_id=1, source_target_pairs={{0,1},{1,0},{2,3},{3,2},{4,5},{5,4},{6,7},{7,6},{8,9},{9,8},{10,11... | collective-permute-start | bytes 1572872 | tf_op jit(solution)/shard_map/ppermute | solution.py:476
  3.7 1.8 %keep.1 = (bf16[2,8,128,128]{3,2,1,0:T(8,128)(2,1)S(1)}, bf16[128,1024]{1,0:T(8,128)(2,1)S(1)}, bf16[128,1024]{1,0:T(8,128)(2,1)S(1)}, bf16[128,1024]{1,0:T(8,12...) custom-call(s32[8]{0:T(128)S(1)} %get-tuple-element.52.len_hbm, ...), custom_call_target="tpu_custom_call" | custom-call | flops 67108864 | bytes 4358176 | tf_op jit(solution)/shard_map/keep/pallas_call | solution.py:443
  5.5 0.2 pair.1
  5.7 3.6 %collective-permute-start.1 = (bf16[2,128,128]{2,1,0:T(8,128)(2,1)S(1)}, bf16[2,128,128]{2,1,0:T(8,128)(2,1)S(1)}, u32[]{:S(2)}, u32[]{:S(2)}) collective-permute-start(bf16[2,128,128]{2,1,0:T(8,128)(2,1)S(1)} %get-tuple-element.75), channel_id=1, source_target_pairs={{0,6},{1,7},{2,4},{3,5},{4,2},{5,3},{6,0},{7,1},{8,14},{9,15},{10,... | collective-permute-start | bytes 196616 | tf_op jit(solution)/shard_map/ppermute | solution.py:510
  9.3 0.5 %collective-permute-start.2 = (bf16[2,128,128]{2,1,0:T(8,128)(2,1)S(1)}, bf16[2,128,128]{2,1,0:T(8,128)(2,1)S(1)}, u32[]{:S(2)}, u32[]{:S(2)}) collective-permute-start(bf16[2,128,128]{2,1,0:T(8,128)(2,1)S(1)} %get-tuple-element.76), channel_id=1, source_target_pairs={{0,2},{1,3},{2,0},{3,1},{4,6},{5,7},{6,4},{7,5},{8,10},{9,11},{10,... | collective-permute-start | bytes 196616 | tf_op jit(solution)/shard_map/ppermute | solution.py:510
  9.9 0.1 collective-permute-start.3
  10.0 2.8 %collective-permute-start.8 = (bf16[2,128,128]{2,1,0:T(8,128)(2,1)S(1)}, bf16[2,128,128]{2,1,0:T(8,128)(2,1)S(1)}, u32[]{:S(2)}, u32[]{:S(2)}) collective-permute-start(bf16[2,128,128]{2,1,0:T(8,128)(2,1)S(1)} %get-tuple-element.89), channel_id=1, source_target_pairs={{0,6},{1,7},{2,4},{3,5},{4,2},{5,3},{6,0},{7,1},{8,14},{9,15},{10,... | collective-permute-start | bytes 196616 | tf_op jit(solution)/shard_map/ppermute | solution.py:510
  12.8 0.5 %collective-permute-start.9 = (bf16[2,128,128]{2,1,0:T(8,128)(2,1)S(1)}, bf16[2,128,128]{2,1,0:T(8,128)(2,1)S(1)}, u32[]{:S(2)}, u32[]{:S(2)}) collective-permute-start(bf16[2,128,128]{2,1,0:T(8,128)(2,1)S(1)} %get-tuple-element.90), channel_id=1, source_target_pairs={{0,2},{1,3},{2,0},{3,1},{4,6},{5,7},{6,4},{7,5},{8,10},{9,11},{10,... | collective-permute-start | bytes 196616 | tf_op jit(solution)/shard_map/ppermute | solution.py:510
  13.3 0.5 %collective-permute-start.10 = (bf16[2,128,128]{2,1,0:T(8,128)(2,1)S(1)}, bf16[2,128,128]{2,1,0:T(8,128)(2,1)S(1)}, u32[]{:S(2)}, u32[]{:S(2)}) collective-permute-start(bf16[2,128,128]{2,1,0:T(8,128)(2,1)S(1)} %get-tuple-element.91), channel_id=1, source_target_pairs={{0,4},{1,5},{2,6},{3,7},{4,0},{5,1},{6,2},{7,3},{8,12},{9,13},{10,... | collective-permute-start | bytes 196616 | tf_op jit(solution)/shard_map/ppermute | solution.py:510
  13.9 0.9 %collective-permute-done.3.refs_3_.s3 = bf16[2,128,128]{2,1,0:T(8,128)(2,1)S(1)} collective-permute-done((bf16[2,128,128]{2,1,0:T(8,128)(2,1)S(1)}, bf16[2,128,128]{2,1,0:T(8,128)(2,1)S(1)}, u32[]{:S(2)}, u32[]{:S(2)}) %collective-permute-start.3) | collective-permute-done | bytes 65568 | tf_op jit(solution)/shard_map/ppermute | solution.py:510
  14.8 2.7 %collective-permute-start.11 = (bf16[2,128,128]{2,1,0:T(8,128)(2,1)S(1)}, bf16[2,128,128]{2,1,0:T(8,128)(2,1)S(1)}, u32[]{:S(2)}, u32[]{:S(2)}) collective-permute-start(bf16[2,128,128]{2,1,0:T(8,128)(2,1)S(1)} %totals.1), channel_id=1, source_target_pairs={{0,8},{1,9},{2,10},{3,11},{4,12},{5,13},{6,14},{7,15},{8,0},{9,1},... | collective-permute-start | bytes 196616 | tf_op jit(solution)/shard_map/ppermute | solution.py:534
  17.5 0.1 scan.2
  17.6 1.7 %collective-permute-start.4 = (bf16[2,128,128]{2,1,0:T(8,128)(2,1)S(1)}, bf16[2,128,128]{2,1,0:T(8,128)(2,1)S(1)}, u32[]{:S(2)}, u32[]{:S(2)}) collective-permute-start(bf16[2,128,128]{2,1,0:T(8,128)(2,1)S(1)} %get-tuple-element.79), channel_id=1, source_target_pairs={{0,6},{1,7},{2,4},{3,5},{4,2},{5,3},{6,0},{7,1},{8,14},{9,15},{10,... | collective-permute-start | bytes 196616 | tf_op jit(solution)/shard_map/ppermute | solution.py:510
  19.2 0.5 %collective-permute-start.5 = (bf16[2,128,128]{2,1,0:T(8,128)(2,1)S(1)}, bf16[2,128,128]{2,1,0:T(8,128)(2,1)S(1)}, u32[]{:S(2)}, u32[]{:S(2)}) collective-permute-start(bf16[2,128,128]{2,1,0:T(8,128)(2,1)S(1)} %get-tuple-element.80), channel_id=1, source_target_pairs={{0,2},{1,3},{2,0},{3,1},{4,6},{5,7},{6,4},{7,5},{8,10},{9,11},{10,... | collective-permute-start | bytes 196616 | tf_op jit(solution)/shard_map/ppermute | solution.py:510
  19.8 1.4 %collective-permute-start.6 = (bf16[2,128,128]{2,1,0:T(8,128)(2,1)S(1)}, bf16[2,128,128]{2,1,0:T(8,128)(2,1)S(1)}, u32[]{:S(2)}, u32[]{:S(2)}) collective-permute-start(bf16[2,128,128]{2,1,0:T(8,128)(2,1)S(1)} %get-tuple-element.81), channel_id=1, source_target_pairs={{0,4},{1,5},{2,6},{3,7},{4,0},{5,1},{6,2},{7,3},{8,12},{9,13},{10,... | collective-permute-start | bytes 196616 | tf_op jit(solution)/shard_map/ppermute | solution.py:510
  21.2 0.2 scan.3
  21.3 1.7 %collective-permute-start.12 = (bf16[2,128,128]{2,1,0:T(8,128)(2,1)S(1)}, bf16[2,128,128]{2,1,0:T(8,128)(2,1)S(1)}, u32[]{:S(2)}, u32[]{:S(2)}) collective-permute-start(bf16[2,128,128]{2,1,0:T(8,128)(2,1)S(1)} %get-tuple-element.93), channel_id=1, source_target_pairs={{0,6},{1,7},{2,4},{3,5},{4,2},{5,3},{6,0},{7,1},{8,14},{9,15},{10,... | collective-permute-start | bytes 196616 | tf_op jit(solution)/shard_map/ppermute | solution.py:510
  23.0 0.5 %collective-permute-start.13 = (bf16[2,128,128]{2,1,0:T(8,128)(2,1)S(1)}, bf16[2,128,128]{2,1,0:T(8,128)(2,1)S(1)}, u32[]{:S(2)}, u32[]{:S(2)}) collective-permute-start(bf16[2,128,128]{2,1,0:T(8,128)(2,1)S(1)} %get-tuple-element.94), channel_id=1, source_target_pairs={{0,2},{1,3},{2,0},{3,1},{4,6},{5,7},{6,4},{7,5},{8,10},{9,11},{10,... | collective-permute-start | bytes 196616 | tf_op jit(solution)/shard_map/ppermute | solution.py:510
  23.5 1.4 %collective-permute-start.14 = (bf16[2,128,128]{2,1,0:T(8,128)(2,1)S(1)}, bf16[2,128,128]{2,1,0:T(8,128)(2,1)S(1)}, u32[]{:S(2)}, u32[]{:S(2)}) collective-permute-start(bf16[2,128,128]{2,1,0:T(8,128)(2,1)S(1)} %get-tuple-element.95), channel_id=1, source_target_pairs={{0,4},{1,5},{2,6},{3,7},{4,0},{5,1},{6,2},{7,3},{8,12},{9,13},{10,... | collective-permute-start | bytes 196616 | tf_op jit(solution)/shard_map/ppermute | solution.py:510
  24.9 0.2 post.2
  25.1 0.1 collective-permute-start.7
  25.2 1.3 %local.1 = (bf16[16,128,128]{2,1,0:T(8,128)(2,1)S(1)}, bf16[16,128,128]{2,1,0:T(8,128)(2,1)S(1)}, bf16[16,128,128]{2,1,0:T(8,128)(2,1)S(1)}, bf16[16,128,128]{2,...) custom-call(s32[8]{0:T(128)S(1)} %get-tuple-element.52.len_hbm, ...), custom_call_target="tpu_custom_call" | custom-call | flops 134217728 | bytes 4784160 | tf_op jit(solution)/shard_map/local/pallas_call | solution.py:443
  26.6 0.7 %collective-permute-done.13.refs_2_ = bf16[2,128,128]{2,1,0:T(8,128)(2,1)S(1)} collective-permute-done((bf16[2,128,128]{2,1,0:T(8,128)(2,1)S(1)}, bf16[2,128,128]{2,1,0:T(8,128)(2,1)S(1)}, u32[]{:S(2)}, u32[]{:S(2)}) %collective-permute-start.13) | collective-permute-done | bytes 65568 | tf_op jit(solution)/shard_map/ppermute | solution.py:510
  27.3 0.5 %collective-permute-done.14.refs_3_ = bf16[2,128,128]{2,1,0:T(8,128)(2,1)S(1)} collective-permute-done((bf16[2,128,128]{2,1,0:T(8,128)(2,1)S(1)}, bf16[2,128,128]{2,1,0:T(8,128)(2,1)S(1)}, u32[]{:S(2)}, u32[]{:S(2)}) %collective-permute-start.14) | collective-permute-done | bytes 65568 | tf_op jit(solution)/shard_map/ppermute | solution.py:510
  27.8 0.2 post.3
  28.0 0.1 collective-permute-start.15
  28.1 0.5 %late.1 = (bf16[128,1024]{1,0:T(8,128)(2,1)S(1)}, bf16[128,1024]{1,0:T(8,128)(2,1)S(1)}) custom-call(bf16[128,1024]{1,0:T(8,128)(2,1)S(1)} %get-tuple-element.55.refs_0_.refs_2_, bf16[128,1024]{1,0:T(8,128)(2,1)S(1)} %get-tuple-element.56.refs_1_.refs_3_, bf16[128,1024]{1,0:T(8,128)(2,1)S(1)} %get-tuple-element.57.refs_2_.refs_4_, ...), custom_call_target="tpu_custom_call" | custom-call | flops 134217728 | bytes 5636096 | tf_op jit(solution)/shard_map/late/pallas_call | solution.py:443
  28.6 0.8 %early.1 = (bf16[128,2048]{1,0:T(8,128)(2,1)S(1)}, bf16[128,2048]{1,0:T(8,128)(2,1)S(1)}) custom-call(bf16[128,1024]{1,0:T(8,128)(2,1)S(1)} %get-tuple-element.55.refs_0_.refs_2_, bf16[128,1024]{1,0:T(8,128)(2,1)S(1)} %get-tuple-element.56.refs_1_.refs_3_, bf16[128,1024]{1,0:T(8,128)(2,1)S(1)} %get-tuple-element.57.refs_2_.refs_4_, ...), custom_call_target="tpu_custom_call" | custom-call | flops 268435456 | bytes 6946816 | tf_op jit(solution)/shard_map/early/pallas_call | solution.py:443
  29.3 0.3 collective-permute-done.15.refs_17_
  29.6 1.5 %last.1 = (bf16[128,2048]{1,0:T(8,128)(2,1)}, bf16[128,2048]{1,0:T(8,128)(2,1)}, bf16[128,2048]{1,0:T(8,128)(2,1)}, bf16[128,2048]{1,0:T(8,128)(2,1)}) custom-call(bf16[128,2048]{1,0:T(8,128)(2,1)S(1)} %get-tuple-element.86.refs_0_, bf16[128,2048]{1,0:T(8,128)(2,1)S(1)} %get-tuple-element.87.refs_1_, ...), custom_call_target="tpu_custom_call" | custom-call | flops 134217728 | bytes 8781824 | tf_op jit(solution)/shard_map/last/pallas_call | solution.py:443
  (14 shorter events, 0.1 us)
Async XLA Ops:
  0.6 0.7 %copy-start = (s32[8]{0:T(128)S(1)}, s32[8]{0:T(128)}, u32[]{:S(2)}) copy-start(s32[8]{0:T(128)} %len_hbm.1) | copy-start | bytes 100
  3.1 2.4 %collective-permute-start = (bf16[2,8,128,128]{3,2,1,0:T(8,128)(2,1)S(1)}, bf16[2,8,128,128]{3,2,1,0:T(8,128)(2,1)S(1)}, u32[]{:S(2)}, u32[]{:S(2)}) collective-permute-start(bf16[2,8,128,128]{3,2,1,0:T(8,128)(2,1)S(1)} %get-tuple-element.73), channel_id=1, source_target_pairs={{0,1},{1,0},{2,3},{3,2},{4,5},{5,4},{6,7},{7,6},{8,9},{9,8},{10,11... | collective-permute-start | bytes 1572872 | tf_op jit(solution)/shard_map/ppermute | solution.py:476
  5.7 7.6 %collective-permute-start.1 = (bf16[2,128,128]{2,1,0:T(8,128)(2,1)S(1)}, bf16[2,128,128]{2,1,0:T(8,128)(2,1)S(1)}, u32[]{:S(2)}, u32[]{:S(2)}) collective-permute-start(bf16[2,128,128]{2,1,0:T(8,128)(2,1)S(1)} %get-tuple-element.75), channel_id=1, source_target_pairs={{0,6},{1,7},{2,4},{3,5},{4,2},{5,3},{6,0},{7,1},{8,14},{9,15},{10,... | collective-permute-start | bytes 196616 | tf_op jit(solution)/shard_map/ppermute | solution.py:510
  9.3 4.5 %collective-permute-start.2 = (bf16[2,128,128]{2,1,0:T(8,128)(2,1)S(1)}, bf16[2,128,128]{2,1,0:T(8,128)(2,1)S(1)}, u32[]{:S(2)}, u32[]{:S(2)}) collective-permute-start(bf16[2,128,128]{2,1,0:T(8,128)(2,1)S(1)} %get-tuple-element.76), channel_id=1, source_target_pairs={{0,2},{1,3},{2,0},{3,1},{4,6},{5,7},{6,4},{7,5},{8,10},{9,11},{10,... | collective-permute-start | bytes 196616 | tf_op jit(solution)/shard_map/ppermute | solution.py:510
  9.9 4.9 %collective-permute-start.3 = (bf16[2,128,128]{2,1,0:T(8,128)(2,1)S(1)}, bf16[2,128,128]{2,1,0:T(8,128)(2,1)S(1)}, u32[]{:S(2)}, u32[]{:S(2)}) collective-permute-start(bf16[2,128,128]{2,1,0:T(8,128)(2,1)S(1)} %get-tuple-element.77), channel_id=1, source_target_pairs={{0,4},{1,5},{2,6},{3,7},{4,0},{5,1},{6,2},{7,3},{8,12},{9,13},{10,... | collective-permute-start | bytes 196616 | tf_op jit(solution)/shard_map/ppermute | solution.py:510
  10.0 9.3 %collective-permute-start.8 = (bf16[2,128,128]{2,1,0:T(8,128)(2,1)S(1)}, bf16[2,128,128]{2,1,0:T(8,128)(2,1)S(1)}, u32[]{:S(2)}, u32[]{:S(2)}) collective-permute-start(bf16[2,128,128]{2,1,0:T(8,128)(2,1)S(1)} %get-tuple-element.89), channel_id=1, source_target_pairs={{0,6},{1,7},{2,4},{3,5},{4,2},{5,3},{6,0},{7,1},{8,14},{9,15},{10,... | collective-permute-start | bytes 196616 | tf_op jit(solution)/shard_map/ppermute | solution.py:510
  12.8 6.9 %collective-permute-start.9 = (bf16[2,128,128]{2,1,0:T(8,128)(2,1)S(1)}, bf16[2,128,128]{2,1,0:T(8,128)(2,1)S(1)}, u32[]{:S(2)}, u32[]{:S(2)}) collective-permute-start(bf16[2,128,128]{2,1,0:T(8,128)(2,1)S(1)} %get-tuple-element.90), channel_id=1, source_target_pairs={{0,2},{1,3},{2,0},{3,1},{4,6},{5,7},{6,4},{7,5},{8,10},{9,11},{10,... | collective-permute-start | bytes 196616 | tf_op jit(solution)/shard_map/ppermute | solution.py:510
  13.3 7.8 %collective-permute-start.10 = (bf16[2,128,128]{2,1,0:T(8,128)(2,1)S(1)}, bf16[2,128,128]{2,1,0:T(8,128)(2,1)S(1)}, u32[]{:S(2)}, u32[]{:S(2)}) collective-permute-start(bf16[2,128,128]{2,1,0:T(8,128)(2,1)S(1)} %get-tuple-element.91), channel_id=1, source_target_pairs={{0,4},{1,5},{2,6},{3,7},{4,0},{5,1},{6,2},{7,3},{8,12},{9,13},{10,... | collective-permute-start | bytes 196616 | tf_op jit(solution)/shard_map/ppermute | solution.py:510
  14.8 6.3 %collective-permute-start.11 = (bf16[2,128,128]{2,1,0:T(8,128)(2,1)S(1)}, bf16[2,128,128]{2,1,0:T(8,128)(2,1)S(1)}, u32[]{:S(2)}, u32[]{:S(2)}) collective-permute-start(bf16[2,128,128]{2,1,0:T(8,128)(2,1)S(1)} %totals.1), channel_id=1, source_target_pairs={{0,8},{1,9},{2,10},{3,11},{4,12},{5,13},{6,14},{7,15},{8,0},{9,1},... | collective-permute-start | bytes 196616 | tf_op jit(solution)/shard_map/ppermute | solution.py:534
  17.6 5.9 %collective-permute-start.4 = (bf16[2,128,128]{2,1,0:T(8,128)(2,1)S(1)}, bf16[2,128,128]{2,1,0:T(8,128)(2,1)S(1)}, u32[]{:S(2)}, u32[]{:S(2)}) collective-permute-start(bf16[2,128,128]{2,1,0:T(8,128)(2,1)S(1)} %get-tuple-element.79), channel_id=1, source_target_pairs={{0,6},{1,7},{2,4},{3,5},{4,2},{5,3},{6,0},{7,1},{8,14},{9,15},{10,... | collective-permute-start | bytes 196616 | tf_op jit(solution)/shard_map/ppermute | solution.py:510
  19.2 5.7 %collective-permute-start.5 = (bf16[2,128,128]{2,1,0:T(8,128)(2,1)S(1)}, bf16[2,128,128]{2,1,0:T(8,128)(2,1)S(1)}, u32[]{:S(2)}, u32[]{:S(2)}) collective-permute-start(bf16[2,128,128]{2,1,0:T(8,128)(2,1)S(1)} %get-tuple-element.80), channel_id=1, source_target_pairs={{0,2},{1,3},{2,0},{3,1},{4,6},{5,7},{6,4},{7,5},{8,10},{9,11},{10,... | collective-permute-start | bytes 196616 | tf_op jit(solution)/shard_map/ppermute | solution.py:510
  19.8 5.1 %collective-permute-start.6 = (bf16[2,128,128]{2,1,0:T(8,128)(2,1)S(1)}, bf16[2,128,128]{2,1,0:T(8,128)(2,1)S(1)}, u32[]{:S(2)}, u32[]{:S(2)}) collective-permute-start(bf16[2,128,128]{2,1,0:T(8,128)(2,1)S(1)} %get-tuple-element.81), channel_id=1, source_target_pairs={{0,4},{1,5},{2,6},{3,7},{4,0},{5,1},{6,2},{7,3},{8,12},{9,13},{10,... | collective-permute-start | bytes 196616 | tf_op jit(solution)/shard_map/ppermute | solution.py:510
  21.3 5.3 %collective-permute-start.12 = (bf16[2,128,128]{2,1,0:T(8,128)(2,1)S(1)}, bf16[2,128,128]{2,1,0:T(8,128)(2,1)S(1)}, u32[]{:S(2)}, u32[]{:S(2)}) collective-permute-start(bf16[2,128,128]{2,1,0:T(8,128)(2,1)S(1)} %get-tuple-element.93), channel_id=1, source_target_pairs={{0,6},{1,7},{2,4},{3,5},{4,2},{5,3},{6,0},{7,1},{8,14},{9,15},{10,... | collective-permute-start | bytes 196616 | tf_op jit(solution)/shard_map/ppermute | solution.py:510
  23.0 4.3 %collective-permute-start.13 = (bf16[2,128,128]{2,1,0:T(8,128)(2,1)S(1)}, bf16[2,128,128]{2,1,0:T(8,128)(2,1)S(1)}, u32[]{:S(2)}, u32[]{:S(2)}) collective-permute-start(bf16[2,128,128]{2,1,0:T(8,128)(2,1)S(1)} %get-tuple-element.94), channel_id=1, source_target_pairs={{0,2},{1,3},{2,0},{3,1},{4,6},{5,7},{6,4},{7,5},{8,10},{9,11},{10,... | collective-permute-start | bytes 196616 | tf_op jit(solution)/shard_map/ppermute | solution.py:510
  23.5 4.3 %collective-permute-start.14 = (bf16[2,128,128]{2,1,0:T(8,128)(2,1)S(1)}, bf16[2,128,128]{2,1,0:T(8,128)(2,1)S(1)}, u32[]{:S(2)}, u32[]{:S(2)}) collective-permute-start(bf16[2,128,128]{2,1,0:T(8,128)(2,1)S(1)} %get-tuple-element.95), channel_id=1, source_target_pairs={{0,4},{1,5},{2,6},{3,7},{4,0},{5,1},{6,2},{7,3},{8,12},{9,13},{10,... | collective-permute-start | bytes 196616 | tf_op jit(solution)/shard_map/ppermute | solution.py:510
  25.1 3.4 %collective-permute-start.7 = (bf16[8,128,128]{2,1,0:T(8,128)(2,1)S(1)}, bf16[8,128,128]{2,1,0:T(8,128)(2,1)S(1)}, u32[]{:S(2)}, u32[]{:S(2)}) collective-permute-start(bf16[8,128,128]{2,1,0:T(8,128)(2,1)S(1)} %get-tuple-element.85), channel_id=1, source_target_pairs={{0,1},{1,0},{2,3},{3,2},{4,5},{5,4},{6,7},{7,6},{8,9},{9,8},{10,11... | collective-permute-start | bytes 786440 | tf_op jit(solution)/shard_map/ppermute | solution.py:548
  28.0 1.6 %collective-permute-start.15 = (bf16[8,128,128]{2,1,0:T(8,128)(2,1)S(1)}, bf16[8,128,128]{2,1,0:T(8,128)(2,1)S(1)}, u32[]{:S(2)}, u32[]{:S(2)}) collective-permute-start(bf16[8,128,128]{2,1,0:T(8,128)(2,1)S(1)} %get-tuple-element.96), channel_id=1, source_target_pairs={{0,1},{1,0},{2,3},{3,2},{4,5},{5,4},{6,7},{7,6},{8,9},{9,8},{10,11... | collective-permute-start | bytes 786440 | tf_op jit(solution)/shard_map/ppermute | solution.py:548

commit v12 on v11

--- a/solution.py
+++ b/solution.py
@@ -438,7 +438,7 @@
     def shape(*dims, dtype=BF16):
         return jax.ShapeDtypeStruct(dims, dtype)
 
-    def call(kernel, name, outs, args, specs, out_specs=None, flops=0, scratch=(), room=8):
+    def call(kernel, name, outs, args, specs, out_specs=None, flops=0, scratch=()):
         moved = sum(a.size * a.dtype.itemsize for a in list(args) + list(outs))
         return pl.pallas_call(
             kernel,
@@ -446,7 +446,7 @@
             out_specs=out_specs or [vmem] * len(outs),
             out_shape=list(outs),
             scratch_shapes=list(scratch),
-            compiler_params=pltpu.CompilerParams(vmem_limit_bytes=int(room * 1024 * 1024)),
+            compiler_params=pltpu.CompilerParams(vmem_limit_bytes=8 * 1024 * 1024),
             cost_estimate=pl.CostEstimate(flops=flops, bytes_accessed=moved, transcendentals=0),
             name=name,
         )(*args)
@@ -455,7 +455,10 @@
     states, halves, tokens = shape(2, half, HD, HD), shape(half, HD, HD), shape(rows, width)
     part = shape(rows, half * HD)
     lengths = [pltpu.SMEM(doc_lengths.shape, jnp.int32), pltpu.SemaphoreType.DMA(())]
-    arrays = (queries, keys, values, grad_out)
+    doc_lengths, *arrays = (
+        pltpu.with_memory_space_constraint(x, pltpu.HBM)
+        for x in (doc_lengths, queries, keys, values, grad_out)
+    )
     chunks = 2
     doc_lengths, send, *others = call(
         functools.partial(send_kernel, total, chunks),
@@ -469,7 +472,6 @@
         [hbm] + [vmem] * 9,
         flops=2 * half * product,
         scratch=lengths[:1] + [pltpu.SemaphoreType.DMA((4, chunks)), pltpu.SemaphoreType.DMA((2,))],
-        room=51.5,
     )
     q_other, k_other, v_other, g_other, kt_other, qt_other, row_masks, root = others
     swap = [(i, i ^ 1) for i in range(n)]
@@ -482,7 +484,6 @@
         [hbm] * 5 + [vmem] * 2,
         flops=2 * half * product,
         scratch=lengths[:1] + [pltpu.SemaphoreType.DMA((4, chunks))] + lengths[1:],
-        room=51.5,
     )
     q_mine, k_mine, v_mine, g_mine, kt_mine, qt_mine = mines
     mats = shape(heads, rows, HD)

time: 31.3 us -> 30.6 us (0.978)
  local copies, waits for them, and re-layouts: 0.65 us -> 0 us
    unnamed x2 -> x0, local copies, waits for them, and re-layouts: 0.65 us -> none
where the time goes in v12:
time: 30.6 us; the launch traced here: 30.4 us
  starting transfers between devices  18.6 us (61%)
  Pallas kernels  8.66 us (28%)
  waiting for transfers between devices  2.45 us (8%)
  between operations  0.75 us (2%)
    ppermute x12, starting transfers between devices, trade(): lax.ppermute(parts[d], 'seq', [(i, i ^ 2 * PARTNERS[d]) for i in range(n)])  15.2 us
    pallas_call x12, Pallas kernels, call(): pl.pallas_call(kernel, in_specs=specs, out_specs=out_specs or [vmem] * le...  8.66 us
    ppermute x1, starting transfers between devices, per_device(): enter = lax.ppermute(edge(0), 'seq', up + down)  2.66 us
    ppermute x12, waiting for transfers between devices, trade(): lax.ppermute(parts[d], 'seq', [(i, i ^ 2 * PARTNERS[d]) for i in range(n)])  2.11 us
  transfers between devices with their start and end apart: 16, of which 4 were waited for; matrix products, arithmetic and copies ran while one was open for 0% of the time, Pallas kernels for 17%

profile of v12, /device:TPU:0, one launch (start us, length us, event | category | flops | bytes accessed | tf_op | source)
XLA Modules:
  0.0 30.4 jit_solution(16131866173844131459)
XLA Ops:
  0.6 1.9 %send.1 = (s32[8]{0:T(128)S(1)}, bf16[2,8,128,128]{3,2,1,0:T(8,128)(2,1)S(1)}, bf16[128,1024]{1,0:T(8,128)(2,1)S(1)}, bf16[128,1024]{1,0:T(8,128)(2,1)S(1)}, bf1...) custom-call(s32[8]{0:T(128)} %len_hbm.1, ...), custom_call_target="tpu_custom_call" | custom-call | flops 67108864 | bytes 4325440 | tf_op jit(solution)/shard_map/send/pallas_call | solution.py:443
  2.5 0.5 %collective-permute-start = (bf16[2,8,128,128]{3,2,1,0:T(8,128)(2,1)S(1)}, bf16[2,8,128,128]{3,2,1,0:T(8,128)(2,1)S(1)}, u32[]{:S(2)}, u32[]{:S(2)}) collective-permute-start(bf16[2,8,128,128]{3,2,1,0:T(8,128)(2,1)S(1)} %get-tuple-element.73), channel_id=1, source_target_pairs={{0,1},{1,0},{2,3},{3,2},{4,5},{5,4},{6,7},{7,6},{8,9},{9,8},{10,11... | collective-permute-start | bytes 1572872 | tf_op jit(solution)/shard_map/ppermute | solution.py:478
  3.0 1.8 %keep.1 = (bf16[2,8,128,128]{3,2,1,0:T(8,128)(2,1)S(1)}, bf16[128,1024]{1,0:T(8,128)(2,1)S(1)}, bf16[128,1024]{1,0:T(8,128)(2,1)S(1)}, bf16[128,1024]{1,0:T(8,12...) custom-call(s32[8]{0:T(128)S(1)} %get-tuple-element.52.len_hbm, ...), custom_call_target="tpu_custom_call" | custom-call | flops 67108864 | bytes 4358176 | tf_op jit(solution)/shard_map/keep/pallas_call | solution.py:443
  4.9 0.2 pair.1
  5.1 3.6 %collective-permute-start.1 = (bf16[2,128,128]{2,1,0:T(8,128)(2,1)S(1)}, bf16[2,128,128]{2,1,0:T(8,128)(2,1)S(1)}, u32[]{:S(2)}, u32[]{:S(2)}) collective-permute-start(bf16[2,128,128]{2,1,0:T(8,128)(2,1)S(1)} %get-tuple-element.75), channel_id=1, source_target_pairs={{0,6},{1,7},{2,4},{3,5},{4,2},{5,3},{6,0},{7,1},{8,14},{9,15},{10,... | collective-permute-start | bytes 196616 | tf_op jit(solution)/shard_map/ppermute | solution.py:511
  8.7 0.5 %collective-permute-start.2 = (bf16[2,128,128]{2,1,0:T(8,128)(2,1)S(1)}, bf16[2,128,128]{2,1,0:T(8,128)(2,1)S(1)}, u32[]{:S(2)}, u32[]{:S(2)}) collective-permute-start(bf16[2,128,128]{2,1,0:T(8,128)(2,1)S(1)} %get-tuple-element.76), channel_id=1, source_target_pairs={{0,2},{1,3},{2,0},{3,1},{4,6},{5,7},{6,4},{7,5},{8,10},{9,11},{10,... | collective-permute-start | bytes 196616 | tf_op jit(solution)/shard_map/ppermute | solution.py:511
  9.2 0.1 collective-permute-start.3
  9.3 2.8 %collective-permute-start.8 = (bf16[2,128,128]{2,1,0:T(8,128)(2,1)S(1)}, bf16[2,128,128]{2,1,0:T(8,128)(2,1)S(1)}, u32[]{:S(2)}, u32[]{:S(2)}) collective-permute-start(bf16[2,128,128]{2,1,0:T(8,128)(2,1)S(1)} %get-tuple-element.89), channel_id=1, source_target_pairs={{0,6},{1,7},{2,4},{3,5},{4,2},{5,3},{6,0},{7,1},{8,14},{9,15},{10,... | collective-permute-start | bytes 196616 | tf_op jit(solution)/shard_map/ppermute | solution.py:511
  12.2 0.5 %collective-permute-start.9 = (bf16[2,128,128]{2,1,0:T(8,128)(2,1)S(1)}, bf16[2,128,128]{2,1,0:T(8,128)(2,1)S(1)}, u32[]{:S(2)}, u32[]{:S(2)}) collective-permute-start(bf16[2,128,128]{2,1,0:T(8,128)(2,1)S(1)} %get-tuple-element.90), channel_id=1, source_target_pairs={{0,2},{1,3},{2,0},{3,1},{4,6},{5,7},{6,4},{7,5},{8,10},{9,11},{10,... | collective-permute-start | bytes 196616 | tf_op jit(solution)/shard_map/ppermute | solution.py:511
  12.7 0.5 %collective-permute-start.10 = (bf16[2,128,128]{2,1,0:T(8,128)(2,1)S(1)}, bf16[2,128,128]{2,1,0:T(8,128)(2,1)S(1)}, u32[]{:S(2)}, u32[]{:S(2)}) collective-permute-start(bf16[2,128,128]{2,1,0:T(8,128)(2,1)S(1)} %get-tuple-element.91), channel_id=1, source_target_pairs={{0,4},{1,5},{2,6},{3,7},{4,0},{5,1},{6,2},{7,3},{8,12},{9,13},{10,... | collective-permute-start | bytes 196616 | tf_op jit(solution)/shard_map/ppermute | solution.py:511
  13.2 0.9 %collective-permute-done.3.refs_3_.s3 = bf16[2,128,128]{2,1,0:T(8,128)(2,1)S(1)} collective-permute-done((bf16[2,128,128]{2,1,0:T(8,128)(2,1)S(1)}, bf16[2,128,128]{2,1,0:T(8,128)(2,1)S(1)}, u32[]{:S(2)}, u32[]{:S(2)}) %collective-permute-start.3) | collective-permute-done | bytes 65568 | tf_op jit(solution)/shard_map/ppermute | solution.py:511
  14.1 0.1 totals.1
  14.2 2.7 %collective-permute-start.11 = (bf16[2,128,128]{2,1,0:T(8,128)(2,1)S(1)}, bf16[2,128,128]{2,1,0:T(8,128)(2,1)S(1)}, u32[]{:S(2)}, u32[]{:S(2)}) collective-permute-start(bf16[2,128,128]{2,1,0:T(8,128)(2,1)S(1)} %totals.1), channel_id=1, source_target_pairs={{0,8},{1,9},{2,10},{3,11},{4,12},{5,13},{6,14},{7,15},{8,0},{9,1},... | collective-permute-start | bytes 196616 | tf_op jit(solution)/shard_map/ppermute | solution.py:535
  16.8 0.1 scan.2
  16.9 1.6 %collective-permute-start.4 = (bf16[2,128,128]{2,1,0:T(8,128)(2,1)S(1)}, bf16[2,128,128]{2,1,0:T(8,128)(2,1)S(1)}, u32[]{:S(2)}, u32[]{:S(2)}) collective-permute-start(bf16[2,128,128]{2,1,0:T(8,128)(2,1)S(1)} %get-tuple-element.79), channel_id=1, source_target_pairs={{0,6},{1,7},{2,4},{3,5},{4,2},{5,3},{6,0},{7,1},{8,14},{9,15},{10,... | collective-permute-start | bytes 196616 | tf_op jit(solution)/shard_map/ppermute | solution.py:511
  18.6 0.5 %collective-permute-start.5 = (bf16[2,128,128]{2,1,0:T(8,128)(2,1)S(1)}, bf16[2,128,128]{2,1,0:T(8,128)(2,1)S(1)}, u32[]{:S(2)}, u32[]{:S(2)}) collective-permute-start(bf16[2,128,128]{2,1,0:T(8,128)(2,1)S(1)} %get-tuple-element.80), channel_id=1, source_target_pairs={{0,2},{1,3},{2,0},{3,1},{4,6},{5,7},{6,4},{7,5},{8,10},{9,11},{10,... | collective-permute-start | bytes 196616 | tf_op jit(solution)/shard_map/ppermute | solution.py:511
  19.1 1.4 %collective-permute-start.6 = (bf16[2,128,128]{2,1,0:T(8,128)(2,1)S(1)}, bf16[2,128,128]{2,1,0:T(8,128)(2,1)S(1)}, u32[]{:S(2)}, u32[]{:S(2)}) collective-permute-start(bf16[2,128,128]{2,1,0:T(8,128)(2,1)S(1)} %get-tuple-element.81), channel_id=1, source_target_pairs={{0,4},{1,5},{2,6},{3,7},{4,0},{5,1},{6,2},{7,3},{8,12},{9,13},{10,... | collective-permute-start | bytes 196616 | tf_op jit(solution)/shard_map/ppermute | solution.py:511
  20.5 0.2 scan.3
  20.7 1.6 %collective-permute-start.12 = (bf16[2,128,128]{2,1,0:T(8,128)(2,1)S(1)}, bf16[2,128,128]{2,1,0:T(8,128)(2,1)S(1)}, u32[]{:S(2)}, u32[]{:S(2)}) collective-permute-start(bf16[2,128,128]{2,1,0:T(8,128)(2,1)S(1)} %get-tuple-element.93), channel_id=1, source_target_pairs={{0,6},{1,7},{2,4},{3,5},{4,2},{5,3},{6,0},{7,1},{8,14},{9,15},{10,... | collective-permute-start | bytes 196616 | tf_op jit(solution)/shard_map/ppermute | solution.py:511
  22.3 0.5 %collective-permute-start.13 = (bf16[2,128,128]{2,1,0:T(8,128)(2,1)S(1)}, bf16[2,128,128]{2,1,0:T(8,128)(2,1)S(1)}, u32[]{:S(2)}, u32[]{:S(2)}) collective-permute-start(bf16[2,128,128]{2,1,0:T(8,128)(2,1)S(1)} %get-tuple-element.94), channel_id=1, source_target_pairs={{0,2},{1,3},{2,0},{3,1},{4,6},{5,7},{6,4},{7,5},{8,10},{9,11},{10,... | collective-permute-start | bytes 196616 | tf_op jit(solution)/shard_map/ppermute | solution.py:511
  22.8 1.4 %collective-permute-start.14 = (bf16[2,128,128]{2,1,0:T(8,128)(2,1)S(1)}, bf16[2,128,128]{2,1,0:T(8,128)(2,1)S(1)}, u32[]{:S(2)}, u32[]{:S(2)}) collective-permute-start(bf16[2,128,128]{2,1,0:T(8,128)(2,1)S(1)} %get-tuple-element.95), channel_id=1, source_target_pairs={{0,4},{1,5},{2,6},{3,7},{4,0},{5,1},{6,2},{7,3},{8,12},{9,13},{10,... | collective-permute-start | bytes 196616 | tf_op jit(solution)/shard_map/ppermute | solution.py:511
  24.3 0.2 post.2
  24.5 0.1 collective-permute-start.7
  24.6 1.3 %local.1 = (bf16[16,128,128]{2,1,0:T(8,128)(2,1)S(1)}, bf16[16,128,128]{2,1,0:T(8,128)(2,1)S(1)}, bf16[16,128,128]{2,1,0:T(8,128)(2,1)S(1)}, bf16[16,128,128]{2,...) custom-call(s32[8]{0:T(128)S(1)} %get-tuple-element.52.len_hbm, ...), custom_call_target="tpu_custom_call" | custom-call | flops 134217728 | bytes 4784160 | tf_op jit(solution)/shard_map/local/pallas_call | solution.py:443
  25.9 0.7 %collective-permute-done.13.refs_2_ = bf16[2,128,128]{2,1,0:T(8,128)(2,1)S(1)} collective-permute-done((bf16[2,128,128]{2,1,0:T(8,128)(2,1)S(1)}, bf16[2,128,128]{2,1,0:T(8,128)(2,1)S(1)}, u32[]{:S(2)}, u32[]{:S(2)}) %collective-permute-start.13) | collective-permute-done | bytes 65568 | tf_op jit(solution)/shard_map/ppermute | solution.py:511
  26.6 0.5 %collective-permute-done.14.refs_3_ = bf16[2,128,128]{2,1,0:T(8,128)(2,1)S(1)} collective-permute-done((bf16[2,128,128]{2,1,0:T(8,128)(2,1)S(1)}, bf16[2,128,128]{2,1,0:T(8,128)(2,1)S(1)}, u32[]{:S(2)}, u32[]{:S(2)}) %collective-permute-start.14) | collective-permute-done | bytes 65568 | tf_op jit(solution)/shard_map/ppermute | solution.py:511
  27.1 0.2 post.3
  27.3 0.1 collective-permute-start.15
  27.4 0.4 %late.1 = (bf16[128,1024]{1,0:T(8,128)(2,1)S(1)}, bf16[128,1024]{1,0:T(8,128)(2,1)S(1)}) custom-call(bf16[128,1024]{1,0:T(8,128)(2,1)S(1)} %get-tuple-element.55.refs_0_.refs_2_, bf16[128,1024]{1,0:T(8,128)(2,1)S(1)} %get-tuple-element.56.refs_1_.refs_3_, bf16[128,1024]{1,0:T(8,128)(2,1)S(1)} %get-tuple-element.57.refs_2_.refs_4_, ...), custom_call_target="tpu_custom_call" | custom-call | flops 134217728 | bytes 5636096 | tf_op jit(solution)/shard_map/late/pallas_call | solution.py:443
  27.9 0.7 %early.1 = (bf16[128,2048]{1,0:T(8,128)(2,1)S(1)}, bf16[128,2048]{1,0:T(8,128)(2,1)S(1)}) custom-call(bf16[128,1024]{1,0:T(8,128)(2,1)S(1)} %get-tuple-element.55.refs_0_.refs_2_, bf16[128,1024]{1,0:T(8,128)(2,1)S(1)} %get-tuple-element.56.refs_1_.refs_3_, bf16[128,1024]{1,0:T(8,128)(2,1)S(1)} %get-tuple-element.57.refs_2_.refs_4_, ...), custom_call_target="tpu_custom_call" | custom-call | flops 268435456 | bytes 6946816 | tf_op jit(solution)/shard_map/early/pallas_call | solution.py:443
  28.6 0.3 %collective-permute-done.15.refs_17_ = bf16[8,128,128]{2,1,0:T(8,128)(2,1)S(1)} collective-permute-done((bf16[8,128,128]{2,1,0:T(8,128)(2,1)S(1)}, bf16[8,128,128]{2,1,0:T(8,128)(2,1)S(1)}, u32[]{:S(2)}, u32[]{:S(2)}) %collective-permute-start.15) | collective-permute-done | bytes 262176 | tf_op jit(solution)/shard_map/ppermute | solution.py:549
  28.9 1.5 %last.1 = (bf16[128,2048]{1,0:T(8,128)(2,1)}, bf16[128,2048]{1,0:T(8,128)(2,1)}, bf16[128,2048]{1,0:T(8,128)(2,1)}, bf16[128,2048]{1,0:T(8,128)(2,1)}) custom-call(bf16[128,2048]{1,0:T(8,128)(2,1)S(1)} %get-tuple-element.86.refs_0_, bf16[128,2048]{1,0:T(8,128)(2,1)S(1)} %get-tuple-element.87.refs_1_, ...), custom_call_target="tpu_custom_call" | custom-call | flops 134217728 | bytes 8781824 | tf_op jit(solution)/shard_map/last/pallas_call | solution.py:443
  (12 shorter events, 0.1 us)
Async XLA Ops:
  2.5 2.4 %collective-permute-start = (bf16[2,8,128,128]{3,2,1,0:T(8,128)(2,1)S(1)}, bf16[2,8,128,128]{3,2,1,0:T(8,128)(2,1)S(1)}, u32[]{:S(2)}, u32[]{:S(2)}) collective-permute-start(bf16[2,8,128,128]{3,2,1,0:T(8,128)(2,1)S(1)} %get-tuple-element.73), channel_id=1, source_target_pairs={{0,1},{1,0},{2,3},{3,2},{4,5},{5,4},{6,7},{7,6},{8,9},{9,8},{10,11... | collective-permute-start | bytes 1572872 | tf_op jit(solution)/shard_map/ppermute | solution.py:478
  5.1 7.6 %collective-permute-start.1 = (bf16[2,128,128]{2,1,0:T(8,128)(2,1)S(1)}, bf16[2,128,128]{2,1,0:T(8,128)(2,1)S(1)}, u32[]{:S(2)}, u32[]{:S(2)}) collective-permute-start(bf16[2,128,128]{2,1,0:T(8,128)(2,1)S(1)} %get-tuple-element.75), channel_id=1, source_target_pairs={{0,6},{1,7},{2,4},{3,5},{4,2},{5,3},{6,0},{7,1},{8,14},{9,15},{10,... | collective-permute-start | bytes 196616 | tf_op jit(solution)/shard_map/ppermute | solution.py:511
  8.7 4.5 %collective-permute-start.2 = (bf16[2,128,128]{2,1,0:T(8,128)(2,1)S(1)}, bf16[2,128,128]{2,1,0:T(8,128)(2,1)S(1)}, u32[]{:S(2)}, u32[]{:S(2)}) collective-permute-start(bf16[2,128,128]{2,1,0:T(8,128)(2,1)S(1)} %get-tuple-element.76), channel_id=1, source_target_pairs={{0,2},{1,3},{2,0},{3,1},{4,6},{5,7},{6,4},{7,5},{8,10},{9,11},{10,... | collective-permute-start | bytes 196616 | tf_op jit(solution)/shard_map/ppermute | solution.py:511
  9.2 4.9 %collective-permute-start.3 = (bf16[2,128,128]{2,1,0:T(8,128)(2,1)S(1)}, bf16[2,128,128]{2,1,0:T(8,128)(2,1)S(1)}, u32[]{:S(2)}, u32[]{:S(2)}) collective-permute-start(bf16[2,128,128]{2,1,0:T(8,128)(2,1)S(1)} %get-tuple-element.77), channel_id=1, source_target_pairs={{0,4},{1,5},{2,6},{3,7},{4,0},{5,1},{6,2},{7,3},{8,12},{9,13},{10,... | collective-permute-start | bytes 196616 | tf_op jit(solution)/shard_map/ppermute | solution.py:511
  9.3 9.3 %collective-permute-start.8 = (bf16[2,128,128]{2,1,0:T(8,128)(2,1)S(1)}, bf16[2,128,128]{2,1,0:T(8,128)(2,1)S(1)}, u32[]{:S(2)}, u32[]{:S(2)}) collective-permute-start(bf16[2,128,128]{2,1,0:T(8,128)(2,1)S(1)} %get-tuple-element.89), channel_id=1, source_target_pairs={{0,6},{1,7},{2,4},{3,5},{4,2},{5,3},{6,0},{7,1},{8,14},{9,15},{10,... | collective-permute-start | bytes 196616 | tf_op jit(solution)/shard_map/ppermute | solution.py:511
  12.2 6.9 %collective-permute-start.9 = (bf16[2,128,128]{2,1,0:T(8,128)(2,1)S(1)}, bf16[2,128,128]{2,1,0:T(8,128)(2,1)S(1)}, u32[]{:S(2)}, u32[]{:S(2)}) collective-permute-start(bf16[2,128,128]{2,1,0:T(8,128)(2,1)S(1)} %get-tuple-element.90), channel_id=1, source_target_pairs={{0,2},{1,3},{2,0},{3,1},{4,6},{5,7},{6,4},{7,5},{8,10},{9,11},{10,... | collective-permute-start | bytes 196616 | tf_op jit(solution)/shard_map/ppermute | solution.py:511
  12.7 7.8 %collective-permute-start.10 = (bf16[2,128,128]{2,1,0:T(8,128)(2,1)S(1)}, bf16[2,128,128]{2,1,0:T(8,128)(2,1)S(1)}, u32[]{:S(2)}, u32[]{:S(2)}) collective-permute-start(bf16[2,128,128]{2,1,0:T(8,128)(2,1)S(1)} %get-tuple-element.91), channel_id=1, source_target_pairs={{0,4},{1,5},{2,6},{3,7},{4,0},{5,1},{6,2},{7,3},{8,12},{9,13},{10,... | collective-permute-start | bytes 196616 | tf_op jit(solution)/shard_map/ppermute | solution.py:511
  14.2 6.3 %collective-permute-start.11 = (bf16[2,128,128]{2,1,0:T(8,128)(2,1)S(1)}, bf16[2,128,128]{2,1,0:T(8,128)(2,1)S(1)}, u32[]{:S(2)}, u32[]{:S(2)}) collective-permute-start(bf16[2,128,128]{2,1,0:T(8,128)(2,1)S(1)} %totals.1), channel_id=1, source_target_pairs={{0,8},{1,9},{2,10},{3,11},{4,12},{5,13},{6,14},{7,15},{8,0},{9,1},... | collective-permute-start | bytes 196616 | tf_op jit(solution)/shard_map/ppermute | solution.py:535
  16.9 5.9 %collective-permute-start.4 = (bf16[2,128,128]{2,1,0:T(8,128)(2,1)S(1)}, bf16[2,128,128]{2,1,0:T(8,128)(2,1)S(1)}, u32[]{:S(2)}, u32[]{:S(2)}) collective-permute-start(bf16[2,128,128]{2,1,0:T(8,128)(2,1)S(1)} %get-tuple-element.79), channel_id=1, source_target_pairs={{0,6},{1,7},{2,4},{3,5},{4,2},{5,3},{6,0},{7,1},{8,14},{9,15},{10,... | collective-permute-start | bytes 196616 | tf_op jit(solution)/shard_map/ppermute | solution.py:511
  18.6 5.7 %collective-permute-start.5 = (bf16[2,128,128]{2,1,0:T(8,128)(2,1)S(1)}, bf16[2,128,128]{2,1,0:T(8,128)(2,1)S(1)}, u32[]{:S(2)}, u32[]{:S(2)}) collective-permute-start(bf16[2,128,128]{2,1,0:T(8,128)(2,1)S(1)} %get-tuple-element.80), channel_id=1, source_target_pairs={{0,2},{1,3},{2,0},{3,1},{4,6},{5,7},{6,4},{7,5},{8,10},{9,11},{10,... | collective-permute-start | bytes 196616 | tf_op jit(solution)/shard_map/ppermute | solution.py:511
  19.1 5.2 %collective-permute-start.6 = (bf16[2,128,128]{2,1,0:T(8,128)(2,1)S(1)}, bf16[2,128,128]{2,1,0:T(8,128)(2,1)S(1)}, u32[]{:S(2)}, u32[]{:S(2)}) collective-permute-start(bf16[2,128,128]{2,1,0:T(8,128)(2,1)S(1)} %get-tuple-element.81), channel_id=1, source_target_pairs={{0,4},{1,5},{2,6},{3,7},{4,0},{5,1},{6,2},{7,3},{8,12},{9,13},{10,... | collective-permute-start | bytes 196616 | tf_op jit(solution)/shard_map/ppermute | solution.py:511
  20.7 5.2 %collective-permute-start.12 = (bf16[2,128,128]{2,1,0:T(8,128)(2,1)S(1)}, bf16[2,128,128]{2,1,0:T(8,128)(2,1)S(1)}, u32[]{:S(2)}, u32[]{:S(2)}) collective-permute-start(bf16[2,128,128]{2,1,0:T(8,128)(2,1)S(1)} %get-tuple-element.93), channel_id=1, source_target_pairs={{0,6},{1,7},{2,4},{3,5},{4,2},{5,3},{6,0},{7,1},{8,14},{9,15},{10,... | collective-permute-start | bytes 196616 | tf_op jit(solution)/shard_map/ppermute | solution.py:511
  22.3 4.3 %collective-permute-start.13 = (bf16[2,128,128]{2,1,0:T(8,128)(2,1)S(1)}, bf16[2,128,128]{2,1,0:T(8,128)(2,1)S(1)}, u32[]{:S(2)}, u32[]{:S(2)}) collective-permute-start(bf16[2,128,128]{2,1,0:T(8,128)(2,1)S(1)} %get-tuple-element.94), channel_id=1, source_target_pairs={{0,2},{1,3},{2,0},{3,1},{4,6},{5,7},{6,4},{7,5},{8,10},{9,11},{10,... | collective-permute-start | bytes 196616 | tf_op jit(solution)/shard_map/ppermute | solution.py:511
  22.8 4.3 %collective-permute-start.14 = (bf16[2,128,128]{2,1,0:T(8,128)(2,1)S(1)}, bf16[2,128,128]{2,1,0:T(8,128)(2,1)S(1)}, u32[]{:S(2)}, u32[]{:S(2)}) collective-permute-start(bf16[2,128,128]{2,1,0:T(8,128)(2,1)S(1)} %get-tuple-element.95), channel_id=1, source_target_pairs={{0,4},{1,5},{2,6},{3,7},{4,0},{5,1},{6,2},{7,3},{8,12},{9,13},{10,... | collective-permute-start | bytes 196616 | tf_op jit(solution)/shard_map/ppermute | solution.py:511
  24.5 3.4 %collective-permute-start.7 = (bf16[8,128,128]{2,1,0:T(8,128)(2,1)S(1)}, bf16[8,128,128]{2,1,0:T(8,128)(2,1)S(1)}, u32[]{:S(2)}, u32[]{:S(2)}) collective-permute-start(bf16[8,128,128]{2,1,0:T(8,128)(2,1)S(1)} %get-tuple-element.85), channel_id=1, source_target_pairs={{0,1},{1,0},{2,3},{3,2},{4,5},{5,4},{6,7},{7,6},{8,9},{9,8},{10,11... | collective-permute-start | bytes 786440 | tf_op jit(solution)/shard_map/ppermute | solution.py:549
  27.3 1.6 %collective-permute-start.15 = (bf16[8,128,128]{2,1,0:T(8,128)(2,1)S(1)}, bf16[8,128,128]{2,1,0:T(8,128)(2,1)S(1)}, u32[]{:S(2)}, u32[]{:S(2)}) collective-permute-start(bf16[8,128,128]{2,1,0:T(8,128)(2,1)S(1)} %get-tuple-element.96), channel_id=1, source_target_pairs={{0,1},{1,0},{2,3},{3,2},{4,5},{5,4},{6,7},{7,6},{8,9},{9,8},{10,11... | collective-permute-start | bytes 786440 | tf_op jit(solution)/shard_map/ppermute | solution.py:549

commit v13 on v12

--- a/solution.py
+++ b/solution.py
@@ -146,10 +146,14 @@
     len_pass.wait()
 
 
+def slots():
+    pair = lax.rem(lax.axis_index("seq"), TEAM) // 2
+    return [pair ^ d for d in PARTNERS]
+
+
 def coefficients(starts, rows, n, coef_ref):
     me = lax.axis_index("seq")
     core = lax.rem(me, 2)
-    pair = lax.rem(me, TEAM) // 2
     base = me - lax.rem(me, TEAM)
     one = jnp.int32(1)
 
@@ -163,7 +167,7 @@
         return (a == b).astype(jnp.int32)
 
     team_low, team_high = both(base), both(base + TEAM)
-    pairs = [pair ^ d for d in PARTNERS]
+    pairs = slots()
     low = [both(base + 2 * p) for p in pairs]
     high = [both(base + 2 * p + 2) for p in pairs]
     middle = both(me - core + 1)
@@ -276,22 +280,31 @@
 
 def pair_kernel(split, coef_ref, keep_ref, got_ref, *out_refs):
     per = out_refs[0].shape[0]
-    pair = lax.rem(lax.axis_index("seq"), TEAM) // 2
+    both_ref = out_refs[1]
     for which in range(2):
         kind = kind_of(which, split)
         ca, cb = coef(coef_ref, KEEP_F + 2 * kind), coef(coef_ref, GOT_F + 2 * kind)
-        for d in range(PAIRS):
+        for d, pair in enumerate(slots()):
             for i in range(per):
-                h = (pair ^ PARTNERS[d]) * per + i
+                h = pair * per + i
                 both = keep_ref[kind, h].astype(F32) * ca + got_ref[kind, h].astype(F32) * cb
-                out_refs[which * PAIRS + d][i] = both.astype(BF16)
+                if d == 1:
+                    both_ref[which * per + i] = both.astype(BF16)
+                else:
+                    ref = out_refs[d] if which == 0 else out_refs[PAIRS + max(d - 1, 0)]
+                    ref[i] = both.astype(BF16)
+
+
+def sums_of(refs, which, i):
+    per = refs[0].shape[0]
+    return [ref[i + which * per * (ref.shape[0] > per)].astype(F32) for ref in refs]
 
 
 def totals_kernel(which, split, coef_ref, s0, s1, s2, s3, out_ref):
     row = TOT_F + PAIRS * kind_of(which, split)
     for i in range(out_ref.shape[0]):
-        parts = [s[i].astype(F32) * coef(coef_ref, row + d) for d, s in enumerate((s0, s1, s2, s3))]
-        out_ref[i] = sum(parts).astype(BF16)
+        parts = sums_of((s0, s1, s2, s3), which, i)
+        out_ref[i] = sum(part * coef(coef_ref, row + d) for d, part in enumerate(parts)).astype(BF16)
 
 
 def scan_kernel(which, split, enters, coef_ref, *refs):
@@ -299,7 +312,7 @@
     kind = kind_of(which, split)
     mix, enter = MIX_F + PAIRS * PAIRS * kind, ENTER_F + PAIRS * kind
     for i in range(out_refs[0].shape[0]):
-        parts = [s[i].astype(F32) for s in sums]
+        parts = sums_of(sums, which, i)
         for d, out_ref in enumerate(out_refs):
             terms = [
                 parts[s] * coef(coef_ref, mix + d * PAIRS + s) for s in range(PAIRS) if s != d
@@ -312,13 +325,13 @@
 def post_kernel(which, split, coef_ref, keep_ref, got_ref, *refs):
     mine_ref, theirs_ref = refs[-2:]
     per = refs[0].shape[0]
-    pair = lax.rem(lax.axis_index("seq"), TEAM) // 2
+    pairs = slots()
     kind = kind_of(which, split)
     m0, m1 = coef(coef_ref, MINE_F + 2 * kind), coef(coef_ref, MINE_F + 2 * kind + 1)
     t0, t1 = coef(coef_ref, THEIRS_F + 2 * kind), coef(coef_ref, THEIRS_F + 2 * kind + 1)
     for d in range(PAIRS):
         for i in range(per):
-            h = (pair ^ PARTNERS[d]) * per + i
+            h = pairs[d] * per + i
             came = refs[d][i].astype(F32)
             theirs_ref[h] = (came * t0 + keep_ref[kind, h].astype(F32) * t1).astype(BF16)
             mine_ref[h] = (came * m0 + got_ref[kind, h].astype(F32) * m1).astype(BF16)
@@ -501,18 +514,19 @@
     parts = call(
         functools.partial(pair_kernel, split),
         "pair",
-        [owned] * (2 * PAIRS),
+        [owned, shape(2 * per, HD, HD)] + [owned] * (2 * PAIRS - 3),
         (table, keep, got),
         [vmem] * 3,
     )
 
+    def send_to(d, x):
+        return lax.ppermute(x, "seq", [(i, i ^ (2 * PARTNERS[d])) for i in range(n)])
+
     def trade(parts):
-        return [parts[0]] + [
-            lax.ppermute(parts[d], "seq", [(i, i ^ (2 * PARTNERS[d])) for i in range(n)])
-            for d in range(1, PAIRS)
-        ]
-
-    sums = [trade(parts[:PAIRS]), trade(parts[PAIRS:])]
+        return [parts[0]] + [send_to(d, parts[d]) for d in range(1, PAIRS)]
+
+    sums = [trade(parts[:PAIRS])]
+    sums.append([parts[PAIRS], sums[0][1]] + [send_to(d, parts[PAIRS - 1 + d]) for d in range(2, PAIRS)])
 
     def edge(which):
         kernel = functools.partial(totals_kernel, which, split)

time: 30.6 us -> 32.3 us (1.056)
  waiting for transfers between devices: 2.45 us -> 4.63 us
  starting transfers between devices: 18.6 us -> 18.1 us
    ppermute x12 -> x11, waiting for transfers between devices: 2.11 us -> 4.29 us  [send_to(): return lax.ppermute(x, 'seq', [(i, i ^ 2 * PARTNERS[d]) for i in range(n)])]
    ppermute x12 -> x11, starting transfers between devices: 15.2 us -> 14.8 us  [send_to(): return lax.ppermute(x, 'seq', [(i, i ^ 2 * PARTNERS[d]) for i in range(n)])]
  transfers between devices with their start and end apart: 16 -> 15, of which waited for: 4 -> 7; matrix products, arithmetic and copies ran while one was open for 0% -> 0% of each run, Pallas kernels for 17% -> 16%
where the time goes in v13:
time: 32.3 us; the launch traced here: 32.1 us
  starting transfers between devices  18.1 us (56%)
  Pallas kernels  8.65 us (27%)
  waiting for transfers between devices  4.63 us (14%)
  between operations  0.75 us (2%)
    ppermute x11, starting transfers between devices, send_to(): return lax.ppermute(x, 'seq', [(i, i ^ 2 * PARTNERS[d]) for i in range(n)])  14.8 us
    pallas_call x12, Pallas kernels, call(): pl.pallas_call(kernel, in_specs=specs, out_specs=out_specs or [vmem] * le...  8.65 us
    ppermute x11, waiting for transfers between devices, send_to(): return lax.ppermute(x, 'seq', [(i, i ^ 2 * PARTNERS[d]) for i in range(n)])  4.29 us
    ppermute x1, starting transfers between devices, per_device(): enter = lax.ppermute(edge(0), 'seq', up + down)  2.65 us
  transfers between devices with their start and end apart: 15, of which 7 were waited for; matrix products, arithmetic and copies ran while one was open for 0% of the time, Pallas kernels for 16%

profile of v13, /device:TPU:0, one launch (start us, length us, event | category | flops | bytes accessed | tf_op | source)
XLA Modules:
  0.0 32.1 jit_solution(7749782852990200736)
XLA Ops:
  0.6 1.9 %send.1 = (s32[8]{0:T(128)S(1)}, bf16[2,8,128,128]{3,2,1,0:T(8,128)(2,1)S(1)}, bf16[128,1024]{1,0:T(8,128)(2,1)S(1)}, bf16[128,1024]{1,0:T(8,128)(2,1)S(1)}, bf1...) custom-call(s32[8]{0:T(128)} %len_hbm.1, ...), custom_call_target="tpu_custom_call" | custom-call | flops 67108864 | bytes 4325440 | tf_op jit(solution)/shard_map/send/pallas_call | solution.py:456
  2.5 0.5 %collective-permute-start = (bf16[2,8,128,128]{3,2,1,0:T(8,128)(2,1)S(1)}, bf16[2,8,128,128]{3,2,1,0:T(8,128)(2,1)S(1)}, u32[]{:S(2)}, u32[]{:S(2)}) collective-permute-start(bf16[2,8,128,128]{3,2,1,0:T(8,128)(2,1)S(1)} %get-tuple-element.72), channel_id=1, source_target_pairs={{0,1},{1,0},{2,3},{3,2},{4,5},{5,4},{6,7},{7,6},{8,9},{9,8},{10,11... | collective-permute-start | bytes 1572872 | tf_op jit(solution)/shard_map/ppermute | solution.py:491
  3.0 1.8 %keep.1 = (bf16[2,8,128,128]{3,2,1,0:T(8,128)(2,1)S(1)}, bf16[128,1024]{1,0:T(8,128)(2,1)S(1)}, bf16[128,1024]{1,0:T(8,128)(2,1)S(1)}, bf16[128,1024]{1,0:T(8,12...) custom-call(s32[8]{0:T(128)S(1)} %get-tuple-element.51.len_hbm, ...), custom_call_target="tpu_custom_call" | custom-call | flops 67108864 | bytes 4358176 | tf_op jit(solution)/shard_map/keep/pallas_call | solution.py:456
  4.8 0.2 pair.1
  5.1 3.6 %collective-permute-start.1 = (bf16[4,128,128]{2,1,0:T(8,128)(2,1)S(1)}, bf16[4,128,128]{2,1,0:T(8,128)(2,1)S(1)}, u32[]{:S(2)}, u32[]{:S(2)}) collective-permute-start(bf16[4,128,128]{2,1,0:T(8,128)(2,1)S(1)} %get-tuple-element.74), channel_id=1, source_target_pairs={{0,6},{1,7},{2,4},{3,5},{4,2},{5,3},{6,0},{7,1},{8,14},{9,15},{10,... | collective-permute-start | bytes 393224 | tf_op jit(solution)/shard_map/ppermute | solution.py:523
  8.7 0.5 %collective-permute-start.2 = (bf16[2,128,128]{2,1,0:T(8,128)(2,1)S(1)}, bf16[2,128,128]{2,1,0:T(8,128)(2,1)S(1)}, u32[]{:S(2)}, u32[]{:S(2)}) collective-permute-start(bf16[2,128,128]{2,1,0:T(8,128)(2,1)S(1)} %get-tuple-element.75), channel_id=1, source_target_pairs={{0,2},{1,3},{2,0},{3,1},{4,6},{5,7},{6,4},{7,5},{8,10},{9,11},{10,... | collective-permute-start | bytes 196616 | tf_op jit(solution)/shard_map/ppermute | solution.py:523
  9.2 0.1 collective-permute-start.3
  9.3 1.8 %collective-permute-start.8 = (bf16[2,128,128]{2,1,0:T(8,128)(2,1)S(1)}, bf16[2,128,128]{2,1,0:T(8,128)(2,1)S(1)}, u32[]{:S(2)}, u32[]{:S(2)}) collective-permute-start(bf16[2,128,128]{2,1,0:T(8,128)(2,1)S(1)} %get-tuple-element.88), channel_id=1, source_target_pairs={{0,2},{1,3},{2,0},{3,1},{4,6},{5,7},{6,4},{7,5},{8,10},{9,11},{10,... | collective-permute-start | bytes 196616 | tf_op jit(solution)/shard_map/ppermute | solution.py:523
  11.2 1.6 %collective-permute-start.9 = (bf16[2,128,128]{2,1,0:T(8,128)(2,1)S(1)}, bf16[2,128,128]{2,1,0:T(8,128)(2,1)S(1)}, u32[]{:S(2)}, u32[]{:S(2)}) collective-permute-start(bf16[2,128,128]{2,1,0:T(8,128)(2,1)S(1)} %get-tuple-element.89), channel_id=1, source_target_pairs={{0,4},{1,5},{2,6},{3,7},{4,0},{5,1},{6,2},{7,3},{8,12},{9,13},{10,... | collective-permute-start | bytes 196616 | tf_op jit(solution)/shard_map/ppermute | solution.py:523
  12.8 1.5 %collective-permute-done.2.refs_2_.s2 = bf16[2,128,128]{2,1,0:T(8,128)(2,1)S(1)} collective-permute-done((bf16[2,128,128]{2,1,0:T(8,128)(2,1)S(1)}, bf16[2,128,128]{2,1,0:T(8,128)(2,1)S(1)}, u32[]{:S(2)}, u32[]{:S(2)}) %collective-permute-start.2) | collective-permute-done | bytes 65568 | tf_op jit(solution)/shard_map/ppermute | solution.py:523
  14.3 0.6 %collective-permute-done.3.refs_3_.s3 = bf16[2,128,128]{2,1,0:T(8,128)(2,1)S(1)} collective-permute-done((bf16[2,128,128]{2,1,0:T(8,128)(2,1)S(1)}, bf16[2,128,128]{2,1,0:T(8,128)(2,1)S(1)}, u32[]{:S(2)}, u32[]{:S(2)}) %collective-permute-start.3) | collective-permute-done | bytes 65568 | tf_op jit(solution)/shard_map/ppermute | solution.py:523
  14.9 2.6 %collective-permute-start.10 = (bf16[2,128,128]{2,1,0:T(8,128)(2,1)S(1)}, bf16[2,128,128]{2,1,0:T(8,128)(2,1)S(1)}, u32[]{:S(2)}, u32[]{:S(2)}) collective-permute-start(bf16[2,128,128]{2,1,0:T(8,128)(2,1)S(1)} %totals.1), channel_id=1, source_target_pairs={{0,8},{1,9},{2,10},{3,11},{4,12},{5,13},{6,14},{7,15},{8,0},{9,1},... | collective-permute-start | bytes 196616 | tf_op jit(solution)/shard_map/ppermute | solution.py:549
  17.6 0.1 scan.2
  17.7 2.0 %collective-permute-start.4 = (bf16[2,128,128]{2,1,0:T(8,128)(2,1)S(1)}, bf16[2,128,128]{2,1,0:T(8,128)(2,1)S(1)}, u32[]{:S(2)}, u32[]{:S(2)}) collective-permute-start(bf16[2,128,128]{2,1,0:T(8,128)(2,1)S(1)} %get-tuple-element.78), channel_id=1, source_target_pairs={{0,6},{1,7},{2,4},{3,5},{4,2},{5,3},{6,0},{7,1},{8,14},{9,15},{10,... | collective-permute-start | bytes 196616 | tf_op jit(solution)/shard_map/ppermute | solution.py:523
  19.7 1.1 %collective-permute-start.5 = (bf16[2,128,128]{2,1,0:T(8,128)(2,1)S(1)}, bf16[2,128,128]{2,1,0:T(8,128)(2,1)S(1)}, u32[]{:S(2)}, u32[]{:S(2)}) collective-permute-start(bf16[2,128,128]{2,1,0:T(8,128)(2,1)S(1)} %get-tuple-element.79), channel_id=1, source_target_pairs={{0,2},{1,3},{2,0},{3,1},{4,6},{5,7},{6,4},{7,5},{8,10},{9,11},{10,... | collective-permute-start | bytes 196616 | tf_op jit(solution)/shard_map/ppermute | solution.py:523
  20.8 0.5 %collective-permute-start.6 = (bf16[2,128,128]{2,1,0:T(8,128)(2,1)S(1)}, bf16[2,128,128]{2,1,0:T(8,128)(2,1)S(1)}, u32[]{:S(2)}, u32[]{:S(2)}) collective-permute-start(bf16[2,128,128]{2,1,0:T(8,128)(2,1)S(1)} %get-tuple-element.80), channel_id=1, source_target_pairs={{0,4},{1,5},{2,6},{3,7},{4,0},{5,1},{6,2},{7,3},{8,12},{9,13},{10,... | collective-permute-start | bytes 196616 | tf_op jit(solution)/shard_map/ppermute | solution.py:523
  21.3 0.2 scan.3
  21.4 2.0 %collective-permute-start.11 = (bf16[2,128,128]{2,1,0:T(8,128)(2,1)S(1)}, bf16[2,128,128]{2,1,0:T(8,128)(2,1)S(1)}, u32[]{:S(2)}, u32[]{:S(2)}) collective-permute-start(bf16[2,128,128]{2,1,0:T(8,128)(2,1)S(1)} %get-tuple-element.91), channel_id=1, source_target_pairs={{0,6},{1,7},{2,4},{3,5},{4,2},{5,3},{6,0},{7,1},{8,14},{9,15},{10,... | collective-permute-start | bytes 196616 | tf_op jit(solution)/shard_map/ppermute | solution.py:523
  23.4 1.1 %collective-permute-start.12 = (bf16[2,128,128]{2,1,0:T(8,128)(2,1)S(1)}, bf16[2,128,128]{2,1,0:T(8,128)(2,1)S(1)}, u32[]{:S(2)}, u32[]{:S(2)}) collective-permute-start(bf16[2,128,128]{2,1,0:T(8,128)(2,1)S(1)} %get-tuple-element.92), channel_id=1, source_target_pairs={{0,2},{1,3},{2,0},{3,1},{4,6},{5,7},{6,4},{7,5},{8,10},{9,11},{10,... | collective-permute-start | bytes 196616 | tf_op jit(solution)/shard_map/ppermute | solution.py:523
  24.6 0.5 %collective-permute-start.13 = (bf16[2,128,128]{2,1,0:T(8,128)(2,1)S(1)}, bf16[2,128,128]{2,1,0:T(8,128)(2,1)S(1)}, u32[]{:S(2)}, u32[]{:S(2)}) collective-permute-start(bf16[2,128,128]{2,1,0:T(8,128)(2,1)S(1)} %get-tuple-element.93), channel_id=1, source_target_pairs={{0,4},{1,5},{2,6},{3,7},{4,0},{5,1},{6,2},{7,3},{8,12},{9,13},{10,... | collective-permute-start | bytes 196616 | tf_op jit(solution)/shard_map/ppermute | solution.py:523
  25.0 0.1 collective-permute-done.5.refs_2_
  25.1 0.1 collective-permute-done.6.refs_3_
  25.2 0.2 post.2
  25.5 0.1 collective-permute-start.7
  25.6 1.3 %local.1 = (bf16[16,128,128]{2,1,0:T(8,128)(2,1)S(1)}, bf16[16,128,128]{2,1,0:T(8,128)(2,1)S(1)}, bf16[16,128,128]{2,1,0:T(8,128)(2,1)S(1)}, bf16[16,128,128]{2,...) custom-call(s32[8]{0:T(128)S(1)} %get-tuple-element.51.len_hbm, ...), custom_call_target="tpu_custom_call" | custom-call | flops 134217728 | bytes 4784160 | tf_op jit(solution)/shard_map/local/pallas_call | solution.py:456
  26.9 0.8 %collective-permute-done.12.refs_2_ = bf16[2,128,128]{2,1,0:T(8,128)(2,1)S(1)} collective-permute-done((bf16[2,128,128]{2,1,0:T(8,128)(2,1)S(1)}, bf16[2,128,128]{2,1,0:T(8,128)(2,1)S(1)}, u32[]{:S(2)}, u32[]{:S(2)}) %collective-permute-start.12) | collective-permute-done | bytes 65568 | tf_op jit(solution)/shard_map/ppermute | solution.py:523
  27.7 1.1 %collective-permute-done.13.refs_3_ = bf16[2,128,128]{2,1,0:T(8,128)(2,1)S(1)} collective-permute-done((bf16[2,128,128]{2,1,0:T(8,128)(2,1)S(1)}, bf16[2,128,128]{2,1,0:T(8,128)(2,1)S(1)}, u32[]{:S(2)}, u32[]{:S(2)}) %collective-permute-start.13) | collective-permute-done | bytes 65568 | tf_op jit(solution)/shard_map/ppermute | solution.py:523
  28.8 0.2 post.3
  29.1 0.4 %late.1 = (bf16[128,1024]{1,0:T(8,128)(2,1)S(1)}, bf16[128,1024]{1,0:T(8,128)(2,1)S(1)}) custom-call(bf16[128,1024]{1,0:T(8,128)(2,1)S(1)} %get-tuple-element.54.refs_0_.refs_2_, bf16[128,1024]{1,0:T(8,128)(2,1)S(1)} %get-tuple-element.55.refs_1_.refs_3_, bf16[128,1024]{1,0:T(8,128)(2,1)S(1)} %get-tuple-element.56.refs_2_.refs_4_, ...), custom_call_target="tpu_custom_call" | custom-call | flops 134217728 | bytes 5636096 | tf_op jit(solution)/shard_map/late/pallas_call | solution.py:456
  29.6 0.7 %early.1 = (bf16[128,2048]{1,0:T(8,128)(2,1)S(1)}, bf16[128,2048]{1,0:T(8,128)(2,1)S(1)}) custom-call(bf16[128,1024]{1,0:T(8,128)(2,1)S(1)} %get-tuple-element.54.refs_0_.refs_2_, bf16[128,1024]{1,0:T(8,128)(2,1)S(1)} %get-tuple-element.55.refs_1_.refs_3_, bf16[128,1024]{1,0:T(8,128)(2,1)S(1)} %get-tuple-element.56.refs_2_.refs_4_, ...), custom_call_target="tpu_custom_call" | custom-call | flops 268435456 | bytes 6946816 | tf_op jit(solution)/shard_map/early/pallas_call | solution.py:456
  30.3 0.3 %collective-permute-done.14.refs_17_ = bf16[8,128,128]{2,1,0:T(8,128)(2,1)S(1)} collective-permute-done((bf16[8,128,128]{2,1,0:T(8,128)(2,1)S(1)}, bf16[8,128,128]{2,1,0:T(8,128)(2,1)S(1)}, u32[]{:S(2)}, u32[]{:S(2)}) %collective-permute-start.14) | collective-permute-done | bytes 262176 | tf_op jit(solution)/shard_map/ppermute | solution.py:563
  30.6 1.5 %last.1 = (bf16[128,2048]{1,0:T(8,128)(2,1)}, bf16[128,2048]{1,0:T(8,128)(2,1)}, bf16[128,2048]{1,0:T(8,128)(2,1)}, bf16[128,2048]{1,0:T(8,128)(2,1)}) custom-call(bf16[128,2048]{1,0:T(8,128)(2,1)S(1)} %get-tuple-element.85.refs_0_, bf16[128,2048]{1,0:T(8,128)(2,1)S(1)} %get-tuple-element.86.refs_1_, ...), custom_call_target="tpu_custom_call" | custom-call | flops 134217728 | bytes 8781824 | tf_op jit(solution)/shard_map/last/pallas_call | solution.py:456
  (10 shorter events, 0.1 us)
Async XLA Ops:
  2.5 2.4 %collective-permute-start = (bf16[2,8,128,128]{3,2,1,0:T(8,128)(2,1)S(1)}, bf16[2,8,128,128]{3,2,1,0:T(8,128)(2,1)S(1)}, u32[]{:S(2)}, u32[]{:S(2)}) collective-permute-start(bf16[2,8,128,128]{3,2,1,0:T(8,128)(2,1)S(1)} %get-tuple-element.72), channel_id=1, source_target_pairs={{0,1},{1,0},{2,3},{3,2},{4,5},{5,4},{6,7},{7,6},{8,9},{9,8},{10,11... | collective-permute-start | bytes 1572872 | tf_op jit(solution)/shard_map/ppermute | solution.py:491
  5.1 9.8 %collective-permute-start.1 = (bf16[4,128,128]{2,1,0:T(8,128)(2,1)S(1)}, bf16[4,128,128]{2,1,0:T(8,128)(2,1)S(1)}, u32[]{:S(2)}, u32[]{:S(2)}) collective-permute-start(bf16[4,128,128]{2,1,0:T(8,128)(2,1)S(1)} %get-tuple-element.74), channel_id=1, source_target_pairs={{0,6},{1,7},{2,4},{3,5},{4,2},{5,3},{6,0},{7,1},{8,14},{9,15},{10,... | collective-permute-start | bytes 393224 | tf_op jit(solution)/shard_map/ppermute | solution.py:523
  8.7 5.6 %collective-permute-start.2 = (bf16[2,128,128]{2,1,0:T(8,128)(2,1)S(1)}, bf16[2,128,128]{2,1,0:T(8,128)(2,1)S(1)}, u32[]{:S(2)}, u32[]{:S(2)}) collective-permute-start(bf16[2,128,128]{2,1,0:T(8,128)(2,1)S(1)} %get-tuple-element.75), channel_id=1, source_target_pairs={{0,2},{1,3},{2,0},{3,1},{4,6},{5,7},{6,4},{7,5},{8,10},{9,11},{10,... | collective-permute-start | bytes 196616 | tf_op jit(solution)/shard_map/ppermute | solution.py:523
  9.2 5.7 %collective-permute-start.3 = (bf16[2,128,128]{2,1,0:T(8,128)(2,1)S(1)}, bf16[2,128,128]{2,1,0:T(8,128)(2,1)S(1)}, u32[]{:S(2)}, u32[]{:S(2)}) collective-permute-start(bf16[2,128,128]{2,1,0:T(8,128)(2,1)S(1)} %get-tuple-element.76), channel_id=1, source_target_pairs={{0,4},{1,5},{2,6},{3,7},{4,0},{5,1},{6,2},{7,3},{8,12},{9,13},{10,... | collective-permute-start | bytes 196616 | tf_op jit(solution)/shard_map/ppermute | solution.py:523
  9.3 11.5 %collective-permute-start.8 = (bf16[2,128,128]{2,1,0:T(8,128)(2,1)S(1)}, bf16[2,128,128]{2,1,0:T(8,128)(2,1)S(1)}, u32[]{:S(2)}, u32[]{:S(2)}) collective-permute-start(bf16[2,128,128]{2,1,0:T(8,128)(2,1)S(1)} %get-tuple-element.88), channel_id=1, source_target_pairs={{0,2},{1,3},{2,0},{3,1},{4,6},{5,7},{6,4},{7,5},{8,10},{9,11},{10,... | collective-permute-start | bytes 196616 | tf_op jit(solution)/shard_map/ppermute | solution.py:523
  11.2 10.1 %collective-permute-start.9 = (bf16[2,128,128]{2,1,0:T(8,128)(2,1)S(1)}, bf16[2,128,128]{2,1,0:T(8,128)(2,1)S(1)}, u32[]{:S(2)}, u32[]{:S(2)}) collective-permute-start(bf16[2,128,128]{2,1,0:T(8,128)(2,1)S(1)} %get-tuple-element.89), channel_id=1, source_target_pairs={{0,4},{1,5},{2,6},{3,7},{4,0},{5,1},{6,2},{7,3},{8,12},{9,13},{10,... | collective-permute-start | bytes 196616 | tf_op jit(solution)/shard_map/ppermute | solution.py:523
  14.9 6.3 %collective-permute-start.10 = (bf16[2,128,128]{2,1,0:T(8,128)(2,1)S(1)}, bf16[2,128,128]{2,1,0:T(8,128)(2,1)S(1)}, u32[]{:S(2)}, u32[]{:S(2)}) collective-permute-start(bf16[2,128,128]{2,1,0:T(8,128)(2,1)S(1)} %totals.1), channel_id=1, source_target_pairs={{0,8},{1,9},{2,10},{3,11},{4,12},{5,13},{6,14},{7,15},{8,0},{9,1},... | collective-permute-start | bytes 196616 | tf_op jit(solution)/shard_map/ppermute | solution.py:549
  17.7 6.8 %collective-permute-start.4 = (bf16[2,128,128]{2,1,0:T(8,128)(2,1)S(1)}, bf16[2,128,128]{2,1,0:T(8,128)(2,1)S(1)}, u32[]{:S(2)}, u32[]{:S(2)}) collective-permute-start(bf16[2,128,128]{2,1,0:T(8,128)(2,1)S(1)} %get-tuple-element.78), channel_id=1, source_target_pairs={{0,6},{1,7},{2,4},{3,5},{4,2},{5,3},{6,0},{7,1},{8,14},{9,15},{10,... | collective-permute-start | bytes 196616 | tf_op jit(solution)/shard_map/ppermute | solution.py:523
  19.7 5.4 %collective-permute-start.5 = (bf16[2,128,128]{2,1,0:T(8,128)(2,1)S(1)}, bf16[2,128,128]{2,1,0:T(8,128)(2,1)S(1)}, u32[]{:S(2)}, u32[]{:S(2)}) collective-permute-start(bf16[2,128,128]{2,1,0:T(8,128)(2,1)S(1)} %get-tuple-element.79), channel_id=1, source_target_pairs={{0,2},{1,3},{2,0},{3,1},{4,6},{5,7},{6,4},{7,5},{8,10},{9,11},{10,... | collective-permute-start | bytes 196616 | tf_op jit(solution)/shard_map/ppermute | solution.py:523
  20.8 4.4 %collective-permute-start.6 = (bf16[2,128,128]{2,1,0:T(8,128)(2,1)S(1)}, bf16[2,128,128]{2,1,0:T(8,128)(2,1)S(1)}, u32[]{:S(2)}, u32[]{:S(2)}) collective-permute-start(bf16[2,128,128]{2,1,0:T(8,128)(2,1)S(1)} %get-tuple-element.80), channel_id=1, source_target_pairs={{0,4},{1,5},{2,6},{3,7},{4,0},{5,1},{6,2},{7,3},{8,12},{9,13},{10,... | collective-permute-start | bytes 196616 | tf_op jit(solution)/shard_map/ppermute | solution.py:523
  21.4 5.5 %collective-permute-start.11 = (bf16[2,128,128]{2,1,0:T(8,128)(2,1)S(1)}, bf16[2,128,128]{2,1,0:T(8,128)(2,1)S(1)}, u32[]{:S(2)}, u32[]{:S(2)}) collective-permute-start(bf16[2,128,128]{2,1,0:T(8,128)(2,1)S(1)} %get-tuple-element.91), channel_id=1, source_target_pairs={{0,6},{1,7},{2,4},{3,5},{4,2},{5,3},{6,0},{7,1},{8,14},{9,15},{10,... | collective-permute-start | bytes 196616 | tf_op jit(solution)/shard_map/ppermute | solution.py:523
  23.4 4.3 %collective-permute-start.12 = (bf16[2,128,128]{2,1,0:T(8,128)(2,1)S(1)}, bf16[2,128,128]{2,1,0:T(8,128)(2,1)S(1)}, u32[]{:S(2)}, u32[]{:S(2)}) collective-permute-start(bf16[2,128,128]{2,1,0:T(8,128)(2,1)S(1)} %get-tuple-element.92), channel_id=1, source_target_pairs={{0,2},{1,3},{2,0},{3,1},{4,6},{5,7},{6,4},{7,5},{8,10},{9,11},{10,... | collective-permute-start | bytes 196616 | tf_op jit(solution)/shard_map/ppermute | solution.py:523
  24.6 4.3 %collective-permute-start.13 = (bf16[2,128,128]{2,1,0:T(8,128)(2,1)S(1)}, bf16[2,128,128]{2,1,0:T(8,128)(2,1)S(1)}, u32[]{:S(2)}, u32[]{:S(2)}) collective-permute-start(bf16[2,128,128]{2,1,0:T(8,128)(2,1)S(1)} %get-tuple-element.93), channel_id=1, source_target_pairs={{0,4},{1,5},{2,6},{3,7},{4,0},{5,1},{6,2},{7,3},{8,12},{9,13},{10,... | collective-permute-start | bytes 196616 | tf_op jit(solution)/shard_map/ppermute | solution.py:523
  25.5 4.1 %collective-permute-start.7 = (bf16[8,128,128]{2,1,0:T(8,128)(2,1)S(1)}, bf16[8,128,128]{2,1,0:T(8,128)(2,1)S(1)}, u32[]{:S(2)}, u32[]{:S(2)}) collective-permute-start(bf16[8,128,128]{2,1,0:T(8,128)(2,1)S(1)} %get-tuple-element.84), channel_id=1, source_target_pairs={{0,1},{1,0},{2,3},{3,2},{4,5},{5,4},{6,7},{7,6},{8,9},{9,8},{10,11... | collective-permute-start | bytes 786440 | tf_op jit(solution)/shard_map/ppermute | solution.py:563
  29.0 1.6 %collective-permute-start.14 = (bf16[8,128,128]{2,1,0:T(8,128)(2,1)S(1)}, bf16[8,128,128]{2,1,0:T(8,128)(2,1)S(1)}, u32[]{:S(2)}, u32[]{:S(2)}) collective-permute-start(bf16[8,128,128]{2,1,0:T(8,128)(2,1)S(1)} %get-tuple-element.94), channel_id=1, source_target_pairs={{0,1},{1,0},{2,3},{3,2},{4,5},{5,4},{6,7},{7,6},{8,9},{9,8},{10,11... | collective-permute-start | bytes 786440 | tf_op jit(solution)/shard_map/ppermute | solution.py:563

commit v14 on v10

--- a/solution.py
+++ b/solution.py
@@ -394,7 +394,7 @@
     def shape(*dims, dtype=BF16):
         return jax.ShapeDtypeStruct(dims, dtype)
 
-    def call(kernel, name, outs, args, specs, out_specs=None, flops=0, scratch=(), room=8, aliases=None):
+    def call(kernel, name, outs, args, specs, out_specs=None, flops=0, scratch=(), aliases=None):
         moved = sum(a.size * a.dtype.itemsize for a in list(args) + list(outs))
         return pl.pallas_call(
             kernel,
@@ -403,11 +403,15 @@
             out_shape=list(outs),
             scratch_shapes=list(scratch),
             input_output_aliases=aliases or {},
-            compiler_params=pltpu.CompilerParams(vmem_limit_bytes=int(room * 1024 * 1024)),
+            compiler_params=pltpu.CompilerParams(vmem_limit_bytes=8 * 1024 * 1024),
             cost_estimate=pl.CostEstimate(flops=flops, bytes_accessed=moved, transcendentals=0),
             name=name,
         )(*args)
 
+    doc_lengths, queries, keys, values, grad_out = (
+        pltpu.with_memory_space_constraint(x, pltpu.HBM)
+        for x in (doc_lengths, queries, keys, values, grad_out)
+    )
     product = 2 * rows * HD * HD
     tokens, mats = shape(rows, width), shape(heads, rows, HD)
     lengths = [pltpu.SMEM(doc_lengths.shape, jnp.int32), pltpu.SemaphoreType.DMA(())]
@@ -424,9 +428,12 @@
         flops=heads * product,
         scratch=lengths[:1]
         + [pltpu.SemaphoreType.DMA((2, chunks)), pltpu.SemaphoreType.DMA((2,)), pltpu.SemaphoreType.DMA((2,))],
-        room=50.5,
     )
-    got = lax.ppermute(send, "seq", [(i, i ^ 1) for i in range(n)])
+
+    def swap(x):
+        return lax.ppermute(x, "seq", [(i, i ^ 1) for i in range(n)])
+
+    got = swap(send)
     keep, t_mine, table = call(
         functools.partial(keep_kernel, total, split),
         "keep",
@@ -455,7 +462,9 @@
 
     def trade(parts, devices):
         return [parts[0]] + [
-            lax.ppermute(parts[d], "seq", [(i, i ^ (2 * PARTNERS[d])) for i in devices])
+            lax.ppermute(
+                parts[d], "seq", [(i, i ^ (2 * PARTNERS[d]) if i in devices else i) for i in range(n)]
+            )
             for d in range(1, PAIRS)
         ]
 
@@ -491,18 +500,18 @@
     if split:
         sums = trade(pair(), odds)
         late_sums = trade(pair(masks), evens)
-        enter = lax.ppermute(edge(sums), "seq", [(i, (i ^ TEAM) - 1) for i in odds])
+        enter = lax.ppermute(edge(sums), "seq", [(i, (i ^ TEAM) - 1 if i % 2 else i + 1) for i in range(n)])
         mine, theirs = post(trade(scan(sums), odds))
-        early_states = (mine, lax.ppermute(theirs, "seq", [(i, i - 1) for i in odds]))
+        early_states = (mine, swap(theirs))
         *outs, _ = finish(False, early_states, ())
         mine, theirs = post(trade(scan(late_sums, enter), evens))
-        late_states = (lax.ppermute(theirs, "seq", [(i, i + 1) for i in evens]), mine)
+        late_states = (swap(theirs), mine)
     else:
         sums = trade(pair(), range(n))
         ups = [(i, i + TEAM) for i in odds if i + TEAM < n]
         enter = lax.ppermute(edge(sums), "seq", ups + [(i, i - TEAM) for i in evens if i >= TEAM])
         mine, theirs = post(trade(scan(sums, enter), range(n)))
-        other = lax.ppermute(theirs, "seq", [(i, i ^ 1) for i in range(n)])
+        other = swap(theirs)
         early_states, late_states = (mine, other), (other, mine)
         *outs, _ = finish(False, early_states, ())
     return tuple(finish(True, late_states, outs))

time: 47.1 us -> 44.8 us (0.951)
  starting transfers between devices: 29.1 us -> 24.8 us
  waiting for transfers between devices: 6.21 us -> 8.78 us
  local copies, waits for them, and re-layouts: 0.65 us -> 0 us
    ppermute x16, starting transfers between devices: 29.1 us -> 24.8 us  [the longest x12 24 us: trade(): lax.ppermute(parts[d], 'seq', [(i, i ^ 2 * PARTNERS[d] if i in devices el...]
    ppermute x16, waiting for transfers between devices: 6.21 us -> 8.78 us  [the longest x12 8.08 us: trade(): lax.ppermute(parts[d], 'seq', [(i, i ^ 2 * PARTNERS[d] if i in devices el...]
    unnamed x2 -> x0, local copies, waits for them, and re-layouts: 0.65 us -> none
  transfers between devices with their start and end apart: 16 -> 16, of which waited for: 4 -> 5; matrix products, arithmetic and copies ran while one was open for 0% -> 0% of each run, Pallas kernels for 13% -> 14%
where the time goes in v14:
time: 44.8 us; the launch traced here: 44.4 us
  starting transfers between devices  24.8 us (55%)
  Pallas kernels  9.87 us (22%)
  waiting for transfers between devices  8.78 us (20%)
  between operations  0.88 us (2%)
    ppermute x12, starting transfers between devices, trade(): lax.ppermute(parts[d], 'seq', [(i, i ^ 2 * PARTNERS[d] if i in devices el...  24 us
    pallas_call x12, Pallas kernels, call(): pl.pallas_call(kernel, in_specs=specs, out_specs=out_specs or [vmem] * le...  9.87 us
    ppermute x12, waiting for transfers between devices, trade(): lax.ppermute(parts[d], 'seq', [(i, i ^ 2 * PARTNERS[d] if i in devices el...  8.08 us
  transfers between devices with their start and end apart: 16, of which 5 were waited for; matrix products, arithmetic and copies ran while one was open for 0% of the time, Pallas kernels for 14%

profile of v14, /device:TPU:0, one launch (start us, length us, event | category | flops | bytes accessed | tf_op | source)
XLA Modules:
  0.0 44.4 jit_solution(4304494209392186453)
XLA Ops:
  0.6 2.1 %send.1 = (s32[8]{0:T(128)S(1)}, bf16[16,128,128]{2,1,0:T(8,128)(2,1)S(1)}, bf16[128,2048]{1,0:T(8,128)(2,1)S(1)}, bf16[128,2048]{1,0:T(8,128)(2,1)S(1)}, bf16[1...) custom-call(s32[8]{0:T(128)} %len_hbm.1, ...), custom_call_target="tpu_custom_call" | custom-call | flops 67108864 | bytes 5374016 | tf_op jit(solution)/shard_map/send/pallas_call | solution.py:399
  2.8 0.5 %collective-permute-start = (bf16[16,128,128]{2,1,0:T(8,128)(2,1)S(1)}, bf16[16,128,128]{2,1,0:T(8,128)(2,1)S(1)}, u32[]{:S(2)}, u32[]{:S(2)}) collective-permute-start(bf16[16,128,128]{2,1,0:T(8,128)(2,1)S(1)} %get-tuple-element.63), channel_id=1, source_target_pairs={{0,1},{1,0},{2,3},{3,2},{4,5},{5,4},{6,7},{7,6},{8,9},{9,8},{10,11... | collective-permute-start | bytes 1572872 | tf_op jit(solution)/shard_map/ppermute | solution.py:434
  3.3 0.8 %keep.1 = (bf16[16,128,128]{2,1,0:T(8,128)(2,1)S(1)}, bf16[16,128,128]{2,1,0:T(8,128)(2,1)S(1)}, f32[64,128]{1,0:T(8,128)S(1)}) custom-call(s32[8]{0:T(128)S(1)} %get-tuple-element.49.len_hbm, bf16[128,2048]{1,0:T(8,128)(2,1)S(1)} %get-tuple-element.46.q_ref.refs_0_, bf16[128,2048]{1,0:T(8,128)(2,1)S(1)} %get-tuple-element.47.k_ref.refs_1_, ...), custom_call_target="tpu_custom_call" | custom-call | flops 67108864 | bytes 3309600 | tf_op jit(solution)/shard_map/keep/pallas_call | solution.py:399
  4.1 0.7 %collective-permute-done.got_ref = bf16[16,128,128]{2,1,0:T(8,128)(2,1)S(1)} collective-permute-done((bf16[16,128,128]{2,1,0:T(8,128)(2,1)S(1)}, bf16[16,128,128]{2,1,0:T(8,128)(2,1)S(1)}, u32[]{:S(2)}, u32[]{:S(2)}) %collective-permute-start) | collective-permute-done | bytes 524320 | tf_op jit(solution)/shard_map/ppermute | solution.py:434
  4.8 0.2 pair.3
  5.0 0.7 %collective-permute-start.4 = (bf16[4,128,128]{2,1,0:T(8,128)(2,1)S(1)}, bf16[4,128,128]{2,1,0:T(8,128)(2,1)S(1)}, u32[]{:S(2)}, u32[]{:S(2)}) collective-permute-start(bf16[4,128,128]{2,1,0:T(8,128)(2,1)S(1)} %get-tuple-element.69), channel_id=1, source_target_pairs={{0,0},{1,7},{2,2},{3,5},{4,4},{5,3},{6,6},{7,1},{8,8},{9,15},{10,1... | collective-permute-start | bytes 393224 | tf_op jit(solution)/shard_map/ppermute | solution.py:465
  5.7 0.7 %collective-permute-start.5 = (bf16[4,128,128]{2,1,0:T(8,128)(2,1)S(1)}, bf16[4,128,128]{2,1,0:T(8,128)(2,1)S(1)}, u32[]{:S(2)}, u32[]{:S(2)}) collective-permute-start(bf16[4,128,128]{2,1,0:T(8,128)(2,1)S(1)} %get-tuple-element.70), channel_id=1, source_target_pairs={{0,0},{1,3},{2,2},{3,1},{4,4},{5,7},{6,6},{7,5},{8,8},{9,11},{10,1... | collective-permute-start | bytes 393224 | tf_op jit(solution)/shard_map/ppermute | solution.py:465
  6.4 0.7 %collective-permute-start.6 = (bf16[4,128,128]{2,1,0:T(8,128)(2,1)S(1)}, bf16[4,128,128]{2,1,0:T(8,128)(2,1)S(1)}, u32[]{:S(2)}, u32[]{:S(2)}) collective-permute-start(bf16[4,128,128]{2,1,0:T(8,128)(2,1)S(1)} %get-tuple-element.71), channel_id=1, source_target_pairs={{0,0},{1,5},{2,2},{3,7},{4,4},{5,1},{6,6},{7,3},{8,8},{9,13},{10,1... | collective-permute-start | bytes 393224 | tf_op jit(solution)/shard_map/ppermute | solution.py:465
  7.0 1.4 %local.1 = (bf16[16,128,128]{2,1,0:T(8,128)(2,1)S(1)}, bf16[16,128,128]{2,1,0:T(8,128)(2,1)S(1)}, bf16[16,128,128]{2,1,0:T(8,128)(2,1)S(1)}, bf16[16,128,128]{2,...) custom-call(s32[8]{0:T(128)S(1)} %get-tuple-element.49.len_hbm, ...), custom_call_target="tpu_custom_call" | custom-call | flops 134217728 | bytes 4784160 | tf_op jit(solution)/shard_map/local/pallas_call | solution.py:399
  8.4 0.2 pair.2
  8.6 5.8 %collective-permute-start.1 = (bf16[4,128,128]{2,1,0:T(8,128)(2,1)S(1)}, bf16[4,128,128]{2,1,0:T(8,128)(2,1)S(1)}, u32[]{:S(2)}, u32[]{:S(2)}) collective-permute-start(bf16[4,128,128]{2,1,0:T(8,128)(2,1)S(1)} %get-tuple-element.65), channel_id=1, source_target_pairs={{0,6},{1,1},{2,4},{3,3},{4,2},{5,5},{6,0},{7,7},{8,14},{9,9},{10,1... | collective-permute-start | bytes 393224 | tf_op jit(solution)/shard_map/ppermute | solution.py:465
  14.4 2.4 %collective-permute-start.2 = (bf16[4,128,128]{2,1,0:T(8,128)(2,1)S(1)}, bf16[4,128,128]{2,1,0:T(8,128)(2,1)S(1)}, u32[]{:S(2)}, u32[]{:S(2)}) collective-permute-start(bf16[4,128,128]{2,1,0:T(8,128)(2,1)S(1)} %get-tuple-element.66), channel_id=1, source_target_pairs={{0,2},{1,1},{2,0},{3,3},{4,6},{5,5},{6,4},{7,7},{8,10},{9,9},{10,8... | collective-permute-start | bytes 393224 | tf_op jit(solution)/shard_map/ppermute | solution.py:465
  16.9 2.0 %collective-permute-start.3 = (bf16[4,128,128]{2,1,0:T(8,128)(2,1)S(1)}, bf16[4,128,128]{2,1,0:T(8,128)(2,1)S(1)}, u32[]{:S(2)}, u32[]{:S(2)}) collective-permute-start(bf16[4,128,128]{2,1,0:T(8,128)(2,1)S(1)} %get-tuple-element.67), channel_id=1, source_target_pairs={{0,4},{1,1},{2,6},{3,3},{4,0},{5,5},{6,2},{7,7},{8,12},{9,9},{10,1... | collective-permute-start | bytes 393224 | tf_op jit(solution)/shard_map/ppermute | solution.py:465
  18.9 0.1 totals.1
  19.0 0.2 collective-permute-start.7
  19.2 0.2 scan.3
  19.4 0.7 %collective-permute-start.12 = (bf16[4,128,128]{2,1,0:T(8,128)(2,1)S(1)}, bf16[4,128,128]{2,1,0:T(8,128)(2,1)S(1)}, u32[]{:S(2)}, u32[]{:S(2)}) collective-permute-start(bf16[4,128,128]{2,1,0:T(8,128)(2,1)S(1)} %get-tuple-element.79), channel_id=1, source_target_pairs={{0,0},{1,7},{2,2},{3,5},{4,4},{5,3},{6,6},{7,1},{8,8},{9,15},{10,1... | collective-permute-start | bytes 393224 | tf_op jit(solution)/shard_map/ppermute | solution.py:465
  20.1 0.7 %collective-permute-start.13 = (bf16[4,128,128]{2,1,0:T(8,128)(2,1)S(1)}, bf16[4,128,128]{2,1,0:T(8,128)(2,1)S(1)}, u32[]{:S(2)}, u32[]{:S(2)}) collective-permute-start(bf16[4,128,128]{2,1,0:T(8,128)(2,1)S(1)} %get-tuple-element.80), channel_id=1, source_target_pairs={{0,0},{1,3},{2,2},{3,1},{4,4},{5,7},{6,6},{7,5},{8,8},{9,11},{10,1... | collective-permute-start | bytes 393224 | tf_op jit(solution)/shard_map/ppermute | solution.py:465
  20.8 0.5 %collective-permute-done.2.refs_2_ = bf16[4,128,128]{2,1,0:T(8,128)(2,1)S(1)} collective-permute-done((bf16[4,128,128]{2,1,0:T(8,128)(2,1)S(1)}, bf16[4,128,128]{2,1,0:T(8,128)(2,1)S(1)}, u32[]{:S(2)}, u32[]{:S(2)}) %collective-permute-start.2) | collective-permute-done | bytes 131104 | tf_op jit(solution)/shard_map/ppermute | solution.py:465
  21.3 0.7 %collective-permute-start.14 = (bf16[4,128,128]{2,1,0:T(8,128)(2,1)S(1)}, bf16[4,128,128]{2,1,0:T(8,128)(2,1)S(1)}, u32[]{:S(2)}, u32[]{:S(2)}) collective-permute-start(bf16[4,128,128]{2,1,0:T(8,128)(2,1)S(1)} %get-tuple-element.81), channel_id=1, source_target_pairs={{0,0},{1,5},{2,2},{3,7},{4,4},{5,1},{6,6},{7,3},{8,8},{9,13},{10,1... | collective-permute-start | bytes 393224 | tf_op jit(solution)/shard_map/ppermute | solution.py:465
  22.0 3.2 %collective-permute-done.3.refs_3_ = bf16[4,128,128]{2,1,0:T(8,128)(2,1)S(1)} collective-permute-done((bf16[4,128,128]{2,1,0:T(8,128)(2,1)S(1)}, bf16[4,128,128]{2,1,0:T(8,128)(2,1)S(1)}, u32[]{:S(2)}, u32[]{:S(2)}) %collective-permute-start.3) | collective-permute-done | bytes 131104 | tf_op jit(solution)/shard_map/ppermute | solution.py:465
  25.1 0.3 scan.2
  25.5 5.4 %collective-permute-start.8 = (bf16[4,128,128]{2,1,0:T(8,128)(2,1)S(1)}, bf16[4,128,128]{2,1,0:T(8,128)(2,1)S(1)}, u32[]{:S(2)}, u32[]{:S(2)}) collective-permute-start(bf16[4,128,128]{2,1,0:T(8,128)(2,1)S(1)} %get-tuple-element.73), channel_id=1, source_target_pairs={{0,6},{1,1},{2,4},{3,3},{4,2},{5,5},{6,0},{7,7},{8,14},{9,9},{10,1... | collective-permute-start | bytes 393224 | tf_op jit(solution)/shard_map/ppermute | solution.py:465
  30.9 2.4 %collective-permute-start.9 = (bf16[4,128,128]{2,1,0:T(8,128)(2,1)S(1)}, bf16[4,128,128]{2,1,0:T(8,128)(2,1)S(1)}, u32[]{:S(2)}, u32[]{:S(2)}) collective-permute-start(bf16[4,128,128]{2,1,0:T(8,128)(2,1)S(1)} %get-tuple-element.74), channel_id=1, source_target_pairs={{0,2},{1,1},{2,0},{3,3},{4,6},{5,5},{6,4},{7,7},{8,10},{9,9},{10,8... | collective-permute-start | bytes 393224 | tf_op jit(solution)/shard_map/ppermute | solution.py:465
  33.3 2.0 %collective-permute-start.10 = (bf16[4,128,128]{2,1,0:T(8,128)(2,1)S(1)}, bf16[4,128,128]{2,1,0:T(8,128)(2,1)S(1)}, u32[]{:S(2)}, u32[]{:S(2)}) collective-permute-start(bf16[4,128,128]{2,1,0:T(8,128)(2,1)S(1)} %get-tuple-element.75), channel_id=1, source_target_pairs={{0,4},{1,1},{2,6},{3,3},{4,0},{5,5},{6,2},{7,7},{8,12},{9,9},{10,1... | collective-permute-start | bytes 393224 | tf_op jit(solution)/shard_map/ppermute | solution.py:465
  35.3 0.4 post.3
  35.8 2.0 %collective-permute-done.9.refs_2_ = bf16[4,128,128]{2,1,0:T(8,128)(2,1)S(1)} collective-permute-done((bf16[4,128,128]{2,1,0:T(8,128)(2,1)S(1)}, bf16[4,128,128]{2,1,0:T(8,128)(2,1)S(1)}, u32[]{:S(2)}, u32[]{:S(2)}) %collective-permute-start.9) | collective-permute-done | bytes 131104 | tf_op jit(solution)/shard_map/ppermute | solution.py:465
  37.7 2.4 %collective-permute-done.10.refs_3_ = bf16[4,128,128]{2,1,0:T(8,128)(2,1)S(1)} collective-permute-done((bf16[4,128,128]{2,1,0:T(8,128)(2,1)S(1)}, bf16[4,128,128]{2,1,0:T(8,128)(2,1)S(1)}, u32[]{:S(2)}, u32[]{:S(2)}) %collective-permute-start.10) | collective-permute-done | bytes 131104 | tf_op jit(solution)/shard_map/ppermute | solution.py:465
  40.2 0.4 post.2
  40.5 0.1 collective-permute-start.11
  40.6 2.2 %early.1 = (bf16[128,2048]{1,0:T(8,128)(2,1)}, bf16[128,2048]{1,0:T(8,128)(2,1)}, bf16[128,2048]{1,0:T(8,128)(2,1)}, bf16[128,2048]{1,0:T(8,128)(2,1)}, f32[8,128]{1,0:T(8,128)}) custom-call(bf16[128,2048]{1,0:T(8,128)(2,1)S(1)} %get-tuple-element.46.q_ref.refs_0_, bf16[128,2048]{1,0:T(8,128)(2,1)S(1)} %get-tuple-element.47.k_ref.refs_1_, ...), custom_call_target="tpu_custom_call" | custom-call | flops 268435456 | bytes 8523776 | tf_op jit(solution)/shard_map/early/pallas_call | solution.py:399
  42.8 1.6 %late.1 = (bf16[128,2048]{1,0:T(8,128)(2,1)}, bf16[128,2048]{1,0:T(8,128)(2,1)}, bf16[128,2048]{1,0:T(8,128)(2,1)}, bf16[128,2048]{1,0:T(8,128)(2,1)}) custom-call(bf16[128,2048]{1,0:T(8,128)(2,1)S(1)} %get-tuple-element.46.q_ref.refs_0_, ...), custom_call_target="tpu_custom_call", output_to_operand_aliasing={{0}: (14, {}), {1}: (15, {}), {2}: (16, {}), {3}: (17, {})} | custom-call | flops 268435456 | bytes 10616832 | tf_op jit(solution)/shard_map/late/pallas_call | solution.py:399
  (12 shorter events, 0.1 us)
Async XLA Ops:
  2.8 2.1 %collective-permute-start = (bf16[16,128,128]{2,1,0:T(8,128)(2,1)S(1)}, bf16[16,128,128]{2,1,0:T(8,128)(2,1)S(1)}, u32[]{:S(2)}, u32[]{:S(2)}) collective-permute-start(bf16[16,128,128]{2,1,0:T(8,128)(2,1)S(1)} %get-tuple-element.63), channel_id=1, source_target_pairs={{0,1},{1,0},{2,3},{3,2},{4,5},{5,4},{6,7},{7,6},{8,9},{9,8},{10,11... | collective-permute-start | bytes 1572872 | tf_op jit(solution)/shard_map/ppermute | solution.py:434
  5.0 11.8 %collective-permute-start.4 = (bf16[4,128,128]{2,1,0:T(8,128)(2,1)S(1)}, bf16[4,128,128]{2,1,0:T(8,128)(2,1)S(1)}, u32[]{:S(2)}, u32[]{:S(2)}) collective-permute-start(bf16[4,128,128]{2,1,0:T(8,128)(2,1)S(1)} %get-tuple-element.69), channel_id=1, source_target_pairs={{0,0},{1,7},{2,2},{3,5},{4,4},{5,3},{6,6},{7,1},{8,8},{9,15},{10,1... | collective-permute-start | bytes 393224 | tf_op jit(solution)/shard_map/ppermute | solution.py:465
  5.7 13.2 %collective-permute-start.5 = (bf16[4,128,128]{2,1,0:T(8,128)(2,1)S(1)}, bf16[4,128,128]{2,1,0:T(8,128)(2,1)S(1)}, u32[]{:S(2)}, u32[]{:S(2)}) collective-permute-start(bf16[4,128,128]{2,1,0:T(8,128)(2,1)S(1)} %get-tuple-element.70), channel_id=1, source_target_pairs={{0,0},{1,3},{2,2},{3,1},{4,4},{5,7},{6,6},{7,5},{8,8},{9,11},{10,1... | collective-permute-start | bytes 393224 | tf_op jit(solution)/shard_map/ppermute | solution.py:465
  6.4 12.5 %collective-permute-start.6 = (bf16[4,128,128]{2,1,0:T(8,128)(2,1)S(1)}, bf16[4,128,128]{2,1,0:T(8,128)(2,1)S(1)}, u32[]{:S(2)}, u32[]{:S(2)}) collective-permute-start(bf16[4,128,128]{2,1,0:T(8,128)(2,1)S(1)} %get-tuple-element.71), channel_id=1, source_target_pairs={{0,0},{1,5},{2,2},{3,7},{4,4},{5,1},{6,6},{7,3},{8,8},{9,13},{10,1... | collective-permute-start | bytes 393224 | tf_op jit(solution)/shard_map/ppermute | solution.py:465
  8.6 11.5 %collective-permute-start.1 = (bf16[4,128,128]{2,1,0:T(8,128)(2,1)S(1)}, bf16[4,128,128]{2,1,0:T(8,128)(2,1)S(1)}, u32[]{:S(2)}, u32[]{:S(2)}) collective-permute-start(bf16[4,128,128]{2,1,0:T(8,128)(2,1)S(1)} %get-tuple-element.65), channel_id=1, source_target_pairs={{0,6},{1,1},{2,4},{3,3},{4,2},{5,5},{6,0},{7,7},{8,14},{9,9},{10,1... | collective-permute-start | bytes 393224 | tf_op jit(solution)/shard_map/ppermute | solution.py:465
  14.4 6.9 %collective-permute-start.2 = (bf16[4,128,128]{2,1,0:T(8,128)(2,1)S(1)}, bf16[4,128,128]{2,1,0:T(8,128)(2,1)S(1)}, u32[]{:S(2)}, u32[]{:S(2)}) collective-permute-start(bf16[4,128,128]{2,1,0:T(8,128)(2,1)S(1)} %get-tuple-element.66), channel_id=1, source_target_pairs={{0,2},{1,1},{2,0},{3,3},{4,6},{5,5},{6,4},{7,7},{8,10},{9,9},{10,8... | collective-permute-start | bytes 393224 | tf_op jit(solution)/shard_map/ppermute | solution.py:465
  16.9 8.3 %collective-permute-start.3 = (bf16[4,128,128]{2,1,0:T(8,128)(2,1)S(1)}, bf16[4,128,128]{2,1,0:T(8,128)(2,1)S(1)}, u32[]{:S(2)}, u32[]{:S(2)}) collective-permute-start(bf16[4,128,128]{2,1,0:T(8,128)(2,1)S(1)} %get-tuple-element.67), channel_id=1, source_target_pairs={{0,4},{1,1},{2,6},{3,3},{4,0},{5,5},{6,2},{7,7},{8,12},{9,9},{10,1... | collective-permute-start | bytes 393224 | tf_op jit(solution)/shard_map/ppermute | solution.py:465
  19.0 6.1 %collective-permute-start.7 = (bf16[4,128,128]{2,1,0:T(8,128)(2,1)S(1)}, bf16[4,128,128]{2,1,0:T(8,128)(2,1)S(1)}, u32[]{:S(2)}, u32[]{:S(2)}) collective-permute-start(bf16[4,128,128]{2,1,0:T(8,128)(2,1)S(1)} %totals.1), channel_id=1, source_target_pairs={{0,1},{1,8},{2,3},{3,10},{4,5},{5,12},{6,7},{7,14},{8,9},{9,0},{10... | collective-permute-start | bytes 393224 | tf_op jit(solution)/shard_map/ppermute | solution.py:503
  19.4 13.9 %collective-permute-start.12 = (bf16[4,128,128]{2,1,0:T(8,128)(2,1)S(1)}, bf16[4,128,128]{2,1,0:T(8,128)(2,1)S(1)}, u32[]{:S(2)}, u32[]{:S(2)}) collective-permute-start(bf16[4,128,128]{2,1,0:T(8,128)(2,1)S(1)} %get-tuple-element.79), channel_id=1, source_target_pairs={{0,0},{1,7},{2,2},{3,5},{4,4},{5,3},{6,6},{7,1},{8,8},{9,15},{10,1... | collective-permute-start | bytes 393224 | tf_op jit(solution)/shard_map/ppermute | solution.py:465
  20.1 15.2 %collective-permute-start.13 = (bf16[4,128,128]{2,1,0:T(8,128)(2,1)S(1)}, bf16[4,128,128]{2,1,0:T(8,128)(2,1)S(1)}, u32[]{:S(2)}, u32[]{:S(2)}) collective-permute-start(bf16[4,128,128]{2,1,0:T(8,128)(2,1)S(1)} %get-tuple-element.80), channel_id=1, source_target_pairs={{0,0},{1,3},{2,2},{3,1},{4,4},{5,7},{6,6},{7,5},{8,8},{9,11},{10,1... | collective-permute-start | bytes 393224 | tf_op jit(solution)/shard_map/ppermute | solution.py:465
  21.3 14.0 %collective-permute-start.14 = (bf16[4,128,128]{2,1,0:T(8,128)(2,1)S(1)}, bf16[4,128,128]{2,1,0:T(8,128)(2,1)S(1)}, u32[]{:S(2)}, u32[]{:S(2)}) collective-permute-start(bf16[4,128,128]{2,1,0:T(8,128)(2,1)S(1)} %get-tuple-element.81), channel_id=1, source_target_pairs={{0,0},{1,5},{2,2},{3,7},{4,4},{5,1},{6,6},{7,3},{8,8},{9,13},{10,1... | collective-permute-start | bytes 393224 | tf_op jit(solution)/shard_map/ppermute | solution.py:465
  25.5 10.3 %collective-permute-start.8 = (bf16[4,128,128]{2,1,0:T(8,128)(2,1)S(1)}, bf16[4,128,128]{2,1,0:T(8,128)(2,1)S(1)}, u32[]{:S(2)}, u32[]{:S(2)}) collective-permute-start(bf16[4,128,128]{2,1,0:T(8,128)(2,1)S(1)} %get-tuple-element.73), channel_id=1, source_target_pairs={{0,6},{1,1},{2,4},{3,3},{4,2},{5,5},{6,0},{7,7},{8,14},{9,9},{10,1... | collective-permute-start | bytes 393224 | tf_op jit(solution)/shard_map/ppermute | solution.py:465
  30.9 6.9 %collective-permute-start.9 = (bf16[4,128,128]{2,1,0:T(8,128)(2,1)S(1)}, bf16[4,128,128]{2,1,0:T(8,128)(2,1)S(1)}, u32[]{:S(2)}, u32[]{:S(2)}) collective-permute-start(bf16[4,128,128]{2,1,0:T(8,128)(2,1)S(1)} %get-tuple-element.74), channel_id=1, source_target_pairs={{0,2},{1,1},{2,0},{3,3},{4,6},{5,5},{6,4},{7,7},{8,10},{9,9},{10,8... | collective-permute-start | bytes 393224 | tf_op jit(solution)/shard_map/ppermute | solution.py:465
  33.3 6.9 %collective-permute-start.10 = (bf16[4,128,128]{2,1,0:T(8,128)(2,1)S(1)}, bf16[4,128,128]{2,1,0:T(8,128)(2,1)S(1)}, u32[]{:S(2)}, u32[]{:S(2)}) collective-permute-start(bf16[4,128,128]{2,1,0:T(8,128)(2,1)S(1)} %get-tuple-element.75), channel_id=1, source_target_pairs={{0,4},{1,1},{2,6},{3,3},{4,0},{5,5},{6,2},{7,7},{8,12},{9,9},{10,1... | collective-permute-start | bytes 393224 | tf_op jit(solution)/shard_map/ppermute | solution.py:465
  35.7 4.9 %collective-permute-start.15 = (bf16[16,128,128]{2,1,0:T(8,128)(2,1)S(1)}, bf16[16,128,128]{2,1,0:T(8,128)(2,1)S(1)}, u32[]{:S(2)}, u32[]{:S(2)}) collective-permute-start(bf16[16,128,128]{2,1,0:T(8,128)(2,1)S(1)} %get-tuple-element.83), channel_id=1, source_target_pairs={{0,1},{1,0},{2,3},{3,2},{4,5},{5,4},{6,7},{7,6},{8,9},{9,8},{10,11... | collective-permute-start | bytes 1572872 | tf_op jit(solution)/shard_map/ppermute | solution.py:434
  40.5 2.3 %collective-permute-start.11 = (bf16[16,128,128]{2,1,0:T(8,128)(2,1)S(1)}, bf16[16,128,128]{2,1,0:T(8,128)(2,1)S(1)}, u32[]{:S(2)}, u32[]{:S(2)}) collective-permute-start(bf16[16,128,128]{2,1,0:T(8,128)(2,1)S(1)} %get-tuple-element.76), channel_id=1, source_target_pairs={{0,1},{1,0},{2,3},{3,2},{4,5},{5,4},{6,7},{7,6},{8,9},{9,8},{10,11... | collective-permute-start | bytes 1572872 | tf_op jit(solution)/shard_map/ppermute | solution.py:434

commit v15 on v12

--- a/solution.py
+++ b/solution.py
@@ -234,8 +234,10 @@
     states_by_chunk(copies, chunks, q_ref, k_ref, v_ref, g_ref, kt_ref, qt_ref, out_ref, masks)
 
 
-def local_kernel(total, len_hbm, *refs):
-    halves, (w_ref, wt_ref, dw_ref, dwt_ref, sg_ref, mask_ref, len_ref, len_sem) = refs[:8], refs[8:]
+def local_kernel(total, split, len_hbm, *refs):
+    halves, (kt_ref, qt_ref, root_ref, s_ref) = refs[:8], refs[8:12]
+    w_ref, wt_ref, dw_ref, dwt_ref, sg_ref, mask_ref, *outs = refs[12:20]
+    len_ref, len_sem = refs[20:]
     len_copy = pltpu.make_async_copy(len_hbm, len_ref, len_sem)
     len_copy.start()
     len_copy.wait()
@@ -261,6 +263,14 @@
         dw = jnp.where(same, dot(g, v_ref[:, cols], (1, 1)), 0.0).astype(BF16)
         dw_ref[h] = dw
         dwt_ref[h] = dw.T
+    fixed = (*halves[:3], *halves[4:7], sg_ref, w_ref, wt_ref, dw_ref, dwt_ref, mask_ref, root_ref)
+
+    def run(kind):
+        for i in range(heads):
+            at = pl.ds(i * HD, HD)
+            outs[0][:, at], outs[1][:, at] = outputs_of(kind, fixed, 0, s_ref[i], kt_ref, qt_ref, i)
+
+    on_kind(0, split, run)
 
 
 def coef(coef_ref, row):
@@ -358,67 +368,52 @@
     return dk.astype(BF16), dv.astype(BF16)
 
 
-def early_kernel(split, *refs):
-    fixed, sides, outs = refs[:FIXED], refs[FIXED : FIXED + 6], refs[FIXED + 6 :]
-    heads = sides[2].shape[0]
+def half_of(kind, fixed, other, s_ref, kt_ref, qt_ref, bufs, outs, chunks, sems):
+    heads = s_ref.shape[0]
+    size = heads * HD // chunks
+    core = lax.rem(lax.axis_index("seq"), 2)
+    begin = (1 - core if other else core) * heads * HD
+    copies = []
+    for c in range(chunks):
+        for i in range(c * heads // chunks, (c + 1) * heads // chunks):
+            at = pl.ds(i * HD, HD)
+            bufs[0][:, at], bufs[1][:, at] = outputs_of(kind, fixed, other, s_ref[i], kt_ref, qt_ref, i)
+        to = pl.ds(pl.multiple_of(begin + c * size, HD), size)
+        for j in range(2):
+            copy = pltpu.make_async_copy(
+                bufs[j].at[:, pl.ds(c * size, size)], outs[2 * kind + j].at[:, to], sems.at[c, j]
+            )
+            copy.start()
+            copies.append(copy)
+    return copies
+
+
+def middle_kernel(split, chunks, *refs):
+    early, fixed, early_refs, late_refs = refs[:2], refs[2 : FIXED + 2], refs[FIXED + 2 :][:3], refs[FIXED + 5 :][:3]
+    outs, bufs, (own_sems, early_sems, late_sems) = refs[-11:-7], refs[-7:-3], refs[-3:]
+    width = early[0].shape[1]
+    mine = pl.ds(pl.multiple_of(lax.rem(lax.axis_index("seq"), 2) * width, HD), width)
 
     def run(kind):
-        for h in range(2 * heads):
-            kt_ref, qt_ref, s_ref = sides[h // heads * 3 :][:3]
-            at = pl.ds(h * HD, HD)
-            i = h % heads
-            outs[0][:, at], outs[1][:, at] = outputs_of(
-                kind, fixed, h // heads, s_ref[i], kt_ref, qt_ref, i
-            )
+        copies = []
+        for j in range(2):
+            copy = pltpu.make_async_copy(early[j], outs[2 * kind + j].at[:, mine], own_sems.at[j])
+            copy.start()
+            copies.append(copy)
+        copies += half_of(kind, fixed, 1, *early_refs, bufs[:2], outs, chunks, early_sems)
+        copies += half_of(1 - kind, fixed, 0, *late_refs, bufs[2:], outs, chunks, late_sems)
+        for copy in copies:
+            copy.wait()
 
     on_kind(0, split, run)
 
 
-def late_kernel(split, *refs):
-    fixed, (kt_ref, qt_ref, s_ref), outs = refs[:FIXED], refs[FIXED : FIXED + 3], refs[FIXED + 3 :]
+def last_kernel(split, chunks, *refs):
+    fixed, late_refs = refs[:FIXED], refs[FIXED : FIXED + 3]
+    outs, bufs, sems = refs[-7:-3], refs[-3:-1], refs[-1]
 
     def run(kind):
-        for i in range(s_ref.shape[0]):
-            at = pl.ds(i * HD, HD)
-            outs[0][:, at], outs[1][:, at] = outputs_of(kind, fixed, 0, s_ref[i], kt_ref, qt_ref, i)
-
-    on_kind(1, split, run)
-
-
-def last_kernel(split, chunks, *refs):
-    early, fixed, (kt_ref, qt_ref, s_ref), late = refs[:2], refs[2 : FIXED + 2], refs[FIXED + 2 :][:3], refs[FIXED + 5 :][:2]
-    outs, bufs, (sems, early_sems, late_sems) = refs[-9:-5], refs[-5:-3], refs[-3:]
-    heads = s_ref.shape[0]
-    width = heads * HD
-    core = lax.rem(lax.axis_index("seq"), 2)
-    mine, other = (pl.ds(pl.multiple_of(x * width, HD), width) for x in (core, 1 - core))
-    size = width // chunks
-
-    def run(kind):
-        early_outs, late_outs = (outs[2:], outs[:2]) if kind == 0 else (outs[:2], outs[2:])
-        copies = []
-        for i in range(2):
-            for j, to in enumerate((mine, other)):
-                copies.append(
-                    pltpu.make_async_copy(
-                        early[i].at[:, pl.ds(j * width, width)], early_outs[i].at[:, to], early_sems.at[i, j]
-                    )
-                )
-            copies.append(pltpu.make_async_copy(late[i], late_outs[i].at[:, mine], late_sems.at[i]))
-        for copy in copies:
-            copy.start()
-        for c in range(chunks):
-            for i in range(c * heads // chunks, (c + 1) * heads // chunks):
-                at = pl.ds(i * HD, HD)
-                bufs[0][:, at], bufs[1][:, at] = outputs_of(kind, fixed, 1, s_ref[i], kt_ref, qt_ref, i)
-            to = pl.ds(pl.multiple_of((1 - core) * width + c * size, HD), size)
-            for i in range(2):
-                copy = pltpu.make_async_copy(
-                    bufs[i].at[:, pl.ds(c * size, size)], late_outs[i].at[:, to], sems.at[i, c]
-                )
-                copy.start()
-                copies.append(copy)
-        for copy in copies:
+        for copy in half_of(kind, fixed, 1, *late_refs, bufs, outs, chunks, sems):
             copy.wait()
 
     on_kind(1, split, run)
@@ -438,7 +433,7 @@
     def shape(*dims, dtype=BF16):
         return jax.ShapeDtypeStruct(dims, dtype)
 
-    def call(kernel, name, outs, args, specs, out_specs=None, flops=0, scratch=()):
+    def call(kernel, name, outs, args, specs, out_specs=None, flops=0, scratch=(), aliases=None):
         moved = sum(a.size * a.dtype.itemsize for a in list(args) + list(outs))
         return pl.pallas_call(
             kernel,
@@ -446,6 +441,7 @@
             out_specs=out_specs or [vmem] * len(outs),
             out_shape=list(outs),
             scratch_shapes=list(scratch),
+            input_output_aliases=aliases or {},
             compiler_params=pltpu.CompilerParams(vmem_limit_bytes=8 * 1024 * 1024),
             cost_estimate=pl.CostEstimate(flops=flops, bytes_accessed=moved, transcendentals=0),
             name=name,
@@ -487,15 +483,6 @@
     )
     q_mine, k_mine, v_mine, g_mine, kt_mine, qt_mine = mines
     mats = shape(heads, rows, HD)
-    *local, masks = call(
-        functools.partial(local_kernel, total),
-        "local",
-        [mats] * 4 + [tokens, shape(2, rows, HD)],
-        (doc_lengths, *mines[:4], *others[:4]),
-        [hbm] + [vmem] * 8,
-        flops=2 * heads * product,
-        scratch=lengths,
-    )
     owned = shape(per, HD, HD)
     split = teams == 2
     parts = call(
@@ -536,47 +523,52 @@
         entering = scan(0) + scan(1, enter)
     else:
         entering = scan(0, lax.ppermute(edge(0), "seq", up)) + scan(1, lax.ppermute(edge(1), "seq", down))
-    mine, other = [], []
-    for which in range(2):
+    def post(which, *after):
         own, theirs = call(
             functools.partial(post_kernel, which, split),
             "post",
             [halves] * 2,
-            (table, keep, got, *entering[which * PAIRS :][:PAIRS], *[masks][:which]),
-            [vmem] * (3 + PAIRS + which),
+            (table, keep, got, *entering[which * PAIRS :][:PAIRS], *after),
+            [vmem] * (3 + PAIRS + len(after)),
         )
-        mine.append(own)
-        other.append(lax.ppermute(theirs, "seq", swap))
+        return own, lax.ppermute(theirs, "seq", swap)
+
+    early_mine, early_other = post(0)
+    *local, masks, early_0, early_1 = call(
+        functools.partial(local_kernel, total, split),
+        "local",
+        [mats] * 4 + [tokens, shape(2, rows, HD)] + [part] * 2,
+        (doc_lengths, *mines[:4], *others[:4], kt_mine, qt_mine, root, early_mine),
+        [hbm] + [vmem] * 12,
+        flops=2 * heads * product,
+        scratch=lengths,
+    )
+    late_mine, late_other = post(1, masks)
     w, wt, dw, dwt, scaled = local
     fixed = (*mines[:3], *others[:3], scaled, w, wt, dw, dwt, masks, root)
-    early = call(
-        functools.partial(early_kernel, split),
-        "early",
-        [tokens] * 2,
-        (*fixed, kt_mine, qt_mine, mine[0], kt_other, qt_other, other[0]),
-        [vmem] * (FIXED + 6),
+    chunks = 4
+    pieces = pltpu.SemaphoreType.DMA((chunks, 2))
+    outs = call(
+        functools.partial(middle_kernel, split, chunks),
+        "middle",
+        [tokens] * 4,
+        (early_0, early_1, *fixed, early_other, kt_other, qt_other, late_mine, kt_mine, qt_mine),
+        [vmem] * (FIXED + 8),
+        [hbm] * 4,
         flops=8 * half * product,
-    )
-    late = call(
-        functools.partial(late_kernel, split),
-        "late",
-        [part] * 2,
-        (*fixed, kt_mine, qt_mine, mine[1]),
-        [vmem] * (FIXED + 3),
-        flops=4 * half * product,
-    )
-    chunks = 4
+        scratch=[pltpu.VMEM(part.shape, BF16)] * 4 + [pltpu.SemaphoreType.DMA((2,)), pieces, pieces],
+    )
     return tuple(
         call(
             functools.partial(last_kernel, split, chunks),
             "last",
             [tokens] * 4,
-            (*early, *fixed, kt_other, qt_other, other[1], *late),
-            [vmem] * (FIXED + 7),
+            (*fixed, late_other, kt_other, qt_other, *outs),
+            [vmem] * (FIXED + 3) + [hbm] * 4,
             [hbm] * 4,
             flops=4 * half * product,
-            scratch=[pltpu.VMEM(part.shape, BF16)] * 2
-            + [pltpu.SemaphoreType.DMA((2, chunks)), pltpu.SemaphoreType.DMA((2, 2)), pltpu.SemaphoreType.DMA((2,))],
+            scratch=[pltpu.VMEM(part.shape, BF16)] * 2 + [pieces],
+            aliases={FIXED + 3 + i: i for i in range(4)},
         )
     )
 

time: 30.6 us -> 30.4 us (level)
  waiting for transfers between devices: 2.45 us -> 1.67 us
  Pallas kernels: 8.66 us -> 9.23 us
    pallas_call x12 -> x11, Pallas kernels: 8.66 us -> 9.23 us  [call(): pl.pallas_call(kernel, in_specs=specs, out_specs=out_specs or [vmem] * le...]
    ppermute x12, waiting for transfers between devices: 2.11 us -> 1.66 us  [trade(): lax.ppermute(parts[d], 'seq', [(i, i ^ 2 * PARTNERS[d]) for i in range(n)])]
    ppermute x2, waiting for transfers between devices: 0.34 us -> 0.01 us  [post(): return (own, lax.ppermute(theirs, 'seq', swap))]
  transfers between devices with their start and end apart: 16 -> 16, of which waited for: 4 -> 3; matrix products, arithmetic and copies ran while one was open for 0% -> 0% of each run, Pallas kernels for 17% -> 20%
where the time goes in v15:
time: 30.4 us; the launch traced here: 30.2 us
  starting transfers between devices  18.6 us (61%)
  Pallas kernels  9.23 us (30%)
  waiting for transfers between devices  1.67 us (5%)
  between operations  0.75 us (2%)
    ppermute x12, starting transfers between devices, trade(): lax.ppermute(parts[d], 'seq', [(i, i ^ 2 * PARTNERS[d]) for i in range(n)])  15.3 us
    pallas_call x11, Pallas kernels, call(): pl.pallas_call(kernel, in_specs=specs, out_specs=out_specs or [vmem] * le...  9.23 us
    ppermute x1, starting transfers between devices, per_device(): enter = lax.ppermute(edge(0), 'seq', up + down)  2.65 us
    ppermute x12, waiting for transfers between devices, trade(): lax.ppermute(parts[d], 'seq', [(i, i ^ 2 * PARTNERS[d]) for i in range(n)])  1.66 us
  transfers between devices with their start and end apart: 16, of which 3 were waited for; matrix products, arithmetic and copies ran while one was open for 0% of the time, Pallas kernels for 20%

profile of v15, /device:TPU:0, one launch (start us, length us, event | category | flops | bytes accessed | tf_op | source)
XLA Modules:
  0.0 30.2 jit_solution(3214032337925571828)
XLA Ops:
  0.6 1.9 %send.1 = (s32[8]{0:T(128)S(1)}, bf16[2,8,128,128]{3,2,1,0:T(8,128)(2,1)S(1)}, bf16[128,1024]{1,0:T(8,128)(2,1)S(1)}, bf16[128,1024]{1,0:T(8,128)(2,1)S(1)}, bf1...) custom-call(s32[8]{0:T(128)} %len_hbm.1, ...), custom_call_target="tpu_custom_call" | custom-call | flops 67108864 | bytes 4325440 | tf_op jit(solution)/shard_map/send/pallas_call | solution.py:438
  2.5 0.5 %collective-permute-start = (bf16[2,8,128,128]{3,2,1,0:T(8,128)(2,1)S(1)}, bf16[2,8,128,128]{3,2,1,0:T(8,128)(2,1)S(1)}, u32[]{:S(2)}, u32[]{:S(2)}) collective-permute-start(bf16[2,8,128,128]{3,2,1,0:T(8,128)(2,1)S(1)} %get-tuple-element.69), channel_id=1, source_target_pairs={{0,1},{1,0},{2,3},{3,2},{4,5},{5,4},{6,7},{7,6},{8,9},{9,8},{10,11... | collective-permute-start | bytes 1572872 | tf_op jit(solution)/shard_map/ppermute | solution.py:474
  3.0 1.8 %keep.1 = (bf16[2,8,128,128]{3,2,1,0:T(8,128)(2,1)S(1)}, bf16[128,1024]{1,0:T(8,128)(2,1)S(1)}, bf16[128,1024]{1,0:T(8,128)(2,1)S(1)}, bf16[128,1024]{1,0:T(8,12...) custom-call(s32[8]{0:T(128)S(1)} %get-tuple-element.54.len_hbm, ...), custom_call_target="tpu_custom_call" | custom-call | flops 67108864 | bytes 4358176 | tf_op jit(solution)/shard_map/keep/pallas_call | solution.py:438
  4.9 0.2 pair.1
  5.1 3.6 %collective-permute-start.1 = (bf16[2,128,128]{2,1,0:T(8,128)(2,1)S(1)}, bf16[2,128,128]{2,1,0:T(8,128)(2,1)S(1)}, u32[]{:S(2)}, u32[]{:S(2)}) collective-permute-start(bf16[2,128,128]{2,1,0:T(8,128)(2,1)S(1)} %get-tuple-element.71), channel_id=1, source_target_pairs={{0,6},{1,7},{2,4},{3,5},{4,2},{5,3},{6,0},{7,1},{8,14},{9,15},{10,... | collective-permute-start | bytes 196616 | tf_op jit(solution)/shard_map/ppermute | solution.py:498
  8.7 0.5 %collective-permute-start.2 = (bf16[2,128,128]{2,1,0:T(8,128)(2,1)S(1)}, bf16[2,128,128]{2,1,0:T(8,128)(2,1)S(1)}, u32[]{:S(2)}, u32[]{:S(2)}) collective-permute-start(bf16[2,128,128]{2,1,0:T(8,128)(2,1)S(1)} %get-tuple-element.72), channel_id=1, source_target_pairs={{0,2},{1,3},{2,0},{3,1},{4,6},{5,7},{6,4},{7,5},{8,10},{9,11},{10,... | collective-permute-start | bytes 196616 | tf_op jit(solution)/shard_map/ppermute | solution.py:498
  9.2 0.1 collective-permute-start.3
  9.4 2.8 %collective-permute-start.7 = (bf16[2,128,128]{2,1,0:T(8,128)(2,1)S(1)}, bf16[2,128,128]{2,1,0:T(8,128)(2,1)S(1)}, u32[]{:S(2)}, u32[]{:S(2)}) collective-permute-start(bf16[2,128,128]{2,1,0:T(8,128)(2,1)S(1)} %get-tuple-element.86), channel_id=1, source_target_pairs={{0,6},{1,7},{2,4},{3,5},{4,2},{5,3},{6,0},{7,1},{8,14},{9,15},{10,... | collective-permute-start | bytes 196616 | tf_op jit(solution)/shard_map/ppermute | solution.py:498
  12.2 0.5 %collective-permute-start.8 = (bf16[2,128,128]{2,1,0:T(8,128)(2,1)S(1)}, bf16[2,128,128]{2,1,0:T(8,128)(2,1)S(1)}, u32[]{:S(2)}, u32[]{:S(2)}) collective-permute-start(bf16[2,128,128]{2,1,0:T(8,128)(2,1)S(1)} %get-tuple-element.87), channel_id=1, source_target_pairs={{0,2},{1,3},{2,0},{3,1},{4,6},{5,7},{6,4},{7,5},{8,10},{9,11},{10,... | collective-permute-start | bytes 196616 | tf_op jit(solution)/shard_map/ppermute | solution.py:498
  12.7 0.0 collective-permute-done.1.refs_1_.s1
  12.7 0.5 %collective-permute-start.9 = (bf16[2,128,128]{2,1,0:T(8,128)(2,1)S(1)}, bf16[2,128,128]{2,1,0:T(8,128)(2,1)S(1)}, u32[]{:S(2)}, u32[]{:S(2)}) collective-permute-start(bf16[2,128,128]{2,1,0:T(8,128)(2,1)S(1)} %get-tuple-element.88), channel_id=1, source_target_pairs={{0,4},{1,5},{2,6},{3,7},{4,0},{5,1},{6,2},{7,3},{8,12},{9,13},{10,... | collective-permute-start | bytes 196616 | tf_op jit(solution)/shard_map/ppermute | solution.py:498
  13.2 0.9 %collective-permute-done.3.refs_3_.s3 = bf16[2,128,128]{2,1,0:T(8,128)(2,1)S(1)} collective-permute-done((bf16[2,128,128]{2,1,0:T(8,128)(2,1)S(1)}, bf16[2,128,128]{2,1,0:T(8,128)(2,1)S(1)}, u32[]{:S(2)}, u32[]{:S(2)}) %collective-permute-start.3) | collective-permute-done | bytes 65568 | tf_op jit(solution)/shard_map/ppermute | solution.py:498
  14.1 0.1 totals.1
  14.2 2.7 %collective-permute-start.10 = (bf16[2,128,128]{2,1,0:T(8,128)(2,1)S(1)}, bf16[2,128,128]{2,1,0:T(8,128)(2,1)S(1)}, u32[]{:S(2)}, u32[]{:S(2)}) collective-permute-start(bf16[2,128,128]{2,1,0:T(8,128)(2,1)S(1)} %totals.1), channel_id=1, source_target_pairs={{0,8},{1,9},{2,10},{3,11},{4,12},{5,13},{6,14},{7,15},{8,0},{9,1},... | collective-permute-start | bytes 196616 | tf_op jit(solution)/shard_map/ppermute | solution.py:522
  16.8 0.1 scan.2
  16.9 1.6 %collective-permute-start.4 = (bf16[2,128,128]{2,1,0:T(8,128)(2,1)S(1)}, bf16[2,128,128]{2,1,0:T(8,128)(2,1)S(1)}, u32[]{:S(2)}, u32[]{:S(2)}) collective-permute-start(bf16[2,128,128]{2,1,0:T(8,128)(2,1)S(1)} %get-tuple-element.75), channel_id=1, source_target_pairs={{0,6},{1,7},{2,4},{3,5},{4,2},{5,3},{6,0},{7,1},{8,14},{9,15},{10,... | collective-permute-start | bytes 196616 | tf_op jit(solution)/shard_map/ppermute | solution.py:498
  18.6 0.5 %collective-permute-start.5 = (bf16[2,128,128]{2,1,0:T(8,128)(2,1)S(1)}, bf16[2,128,128]{2,1,0:T(8,128)(2,1)S(1)}, u32[]{:S(2)}, u32[]{:S(2)}) collective-permute-start(bf16[2,128,128]{2,1,0:T(8,128)(2,1)S(1)} %get-tuple-element.76), channel_id=1, source_target_pairs={{0,2},{1,3},{2,0},{3,1},{4,6},{5,7},{6,4},{7,5},{8,10},{9,11},{10,... | collective-permute-start | bytes 196616 | tf_op jit(solution)/shard_map/ppermute | solution.py:498
  19.1 1.4 %collective-permute-start.6 = (bf16[2,128,128]{2,1,0:T(8,128)(2,1)S(1)}, bf16[2,128,128]{2,1,0:T(8,128)(2,1)S(1)}, u32[]{:S(2)}, u32[]{:S(2)}) collective-permute-start(bf16[2,128,128]{2,1,0:T(8,128)(2,1)S(1)} %get-tuple-element.77), channel_id=1, source_target_pairs={{0,4},{1,5},{2,6},{3,7},{4,0},{5,1},{6,2},{7,3},{8,12},{9,13},{10,... | collective-permute-start | bytes 196616 | tf_op jit(solution)/shard_map/ppermute | solution.py:498
  20.5 0.2 scan.3
  20.7 1.6 %collective-permute-start.11 = (bf16[2,128,128]{2,1,0:T(8,128)(2,1)S(1)}, bf16[2,128,128]{2,1,0:T(8,128)(2,1)S(1)}, u32[]{:S(2)}, u32[]{:S(2)}) collective-permute-start(bf16[2,128,128]{2,1,0:T(8,128)(2,1)S(1)} %get-tuple-element.90), channel_id=1, source_target_pairs={{0,6},{1,7},{2,4},{3,5},{4,2},{5,3},{6,0},{7,1},{8,14},{9,15},{10,... | collective-permute-start | bytes 196616 | tf_op jit(solution)/shard_map/ppermute | solution.py:498
  22.3 0.5 %collective-permute-start.12 = (bf16[2,128,128]{2,1,0:T(8,128)(2,1)S(1)}, bf16[2,128,128]{2,1,0:T(8,128)(2,1)S(1)}, u32[]{:S(2)}, u32[]{:S(2)}) collective-permute-start(bf16[2,128,128]{2,1,0:T(8,128)(2,1)S(1)} %get-tuple-element.91), channel_id=1, source_target_pairs={{0,2},{1,3},{2,0},{3,1},{4,6},{5,7},{6,4},{7,5},{8,10},{9,11},{10,... | collective-permute-start | bytes 196616 | tf_op jit(solution)/shard_map/ppermute | solution.py:498
  22.9 1.4 %collective-permute-start.13 = (bf16[2,128,128]{2,1,0:T(8,128)(2,1)S(1)}, bf16[2,128,128]{2,1,0:T(8,128)(2,1)S(1)}, u32[]{:S(2)}, u32[]{:S(2)}) collective-permute-start(bf16[2,128,128]{2,1,0:T(8,128)(2,1)S(1)} %get-tuple-element.92), channel_id=1, source_target_pairs={{0,4},{1,5},{2,6},{3,7},{4,0},{5,1},{6,2},{7,3},{8,12},{9,13},{10,... | collective-permute-start | bytes 196616 | tf_op jit(solution)/shard_map/ppermute | solution.py:498
  24.2 0.0 collective-permute-done.5.refs_2_
  24.3 0.2 post.2
  24.5 0.1 collective-permute-start.15
  24.6 1.8 %local.1 = (bf16[16,128,128]{2,1,0:T(8,128)(2,1)S(1)}, bf16[16,128,128]{2,1,0:T(8,128)(2,1)S(1)}, bf16[16,128,128]{2,1,0:T(8,128)(2,1)S(1)}, bf16[16,128,128]{2,...) custom-call(s32[8]{0:T(128)S(1)} %get-tuple-element.54.len_hbm, ...), custom_call_target="tpu_custom_call" | custom-call | flops 134217728 | bytes 6160416 | tf_op jit(solution)/shard_map/local/pallas_call | solution.py:438
  26.4 0.2 collective-permute-done.12.refs_2_
  26.6 0.5 %collective-permute-done.13.refs_3_ = bf16[2,128,128]{2,1,0:T(8,128)(2,1)S(1)} collective-permute-done((bf16[2,128,128]{2,1,0:T(8,128)(2,1)S(1)}, bf16[2,128,128]{2,1,0:T(8,128)(2,1)S(1)}, u32[]{:S(2)}, u32[]{:S(2)}) %collective-permute-start.13) | collective-permute-done | bytes 65568 | tf_op jit(solution)/shard_map/ppermute | solution.py:498
  27.1 0.2 post.3
  27.4 0.1 collective-permute-start.14
  27.5 1.6 %middle.1 = (bf16[128,2048]{1,0:T(8,128)(2,1)}, bf16[128,2048]{1,0:T(8,128)(2,1)}, bf16[128,2048]{1,0:T(8,128)(2,1)}, bf16[128,2048]{1,0:T(8,128)(2,1)}) custom-call(bf16[128,1024]{1,0:T(8,128)(2,1)S(1)} %get-tuple-element.96.refs_0_, bf16[128,1024]{1,0:T(8,128)(2,1)S(1)} %get-tuple-element.97.refs_1_, ...), custom_call_target="tpu_custom_call" | custom-call | flops 268435456 | bytes 8519680 | tf_op jit(solution)/shard_map/middle/pallas_call | solution.py:438
  29.0 1.2 %last.1 = (bf16[128,2048]{1,0:T(8,128)(2,1)}, bf16[128,2048]{1,0:T(8,128)(2,1)}, bf16[128,2048]{1,0:T(8,128)(2,1)}, bf16[128,2048]{1,0:T(8,128)(2,1)}) custom-call(bf16[128,1024]{1,0:T(8,128)(2,1)S(1)} %get-tuple-element.57.refs_0_.refs_2_, ...), custom_call_target="tpu_custom_call", output_to_operand_aliasing={{0}: (16, {}), {1}: (17, {}), {2}: (18, {}), {3}: (19, {})} | custom-call | flops 134217728 | bytes 9306112 | tf_op jit(solution)/shard_map/last/pallas_call | solution.py:438
  (11 shorter events, 0.0 us)
Async XLA Ops:
  2.5 2.4 %collective-permute-start = (bf16[2,8,128,128]{3,2,1,0:T(8,128)(2,1)S(1)}, bf16[2,8,128,128]{3,2,1,0:T(8,128)(2,1)S(1)}, u32[]{:S(2)}, u32[]{:S(2)}) collective-permute-start(bf16[2,8,128,128]{3,2,1,0:T(8,128)(2,1)S(1)} %get-tuple-element.69), channel_id=1, source_target_pairs={{0,1},{1,0},{2,3},{3,2},{4,5},{5,4},{6,7},{7,6},{8,9},{9,8},{10,11... | collective-permute-start | bytes 1572872 | tf_op jit(solution)/shard_map/ppermute | solution.py:474
  5.1 7.6 %collective-permute-start.1 = (bf16[2,128,128]{2,1,0:T(8,128)(2,1)S(1)}, bf16[2,128,128]{2,1,0:T(8,128)(2,1)S(1)}, u32[]{:S(2)}, u32[]{:S(2)}) collective-permute-start(bf16[2,128,128]{2,1,0:T(8,128)(2,1)S(1)} %get-tuple-element.71), channel_id=1, source_target_pairs={{0,6},{1,7},{2,4},{3,5},{4,2},{5,3},{6,0},{7,1},{8,14},{9,15},{10,... | collective-permute-start | bytes 196616 | tf_op jit(solution)/shard_map/ppermute | solution.py:498
  8.7 4.5 %collective-permute-start.2 = (bf16[2,128,128]{2,1,0:T(8,128)(2,1)S(1)}, bf16[2,128,128]{2,1,0:T(8,128)(2,1)S(1)}, u32[]{:S(2)}, u32[]{:S(2)}) collective-permute-start(bf16[2,128,128]{2,1,0:T(8,128)(2,1)S(1)} %get-tuple-element.72), channel_id=1, source_target_pairs={{0,2},{1,3},{2,0},{3,1},{4,6},{5,7},{6,4},{7,5},{8,10},{9,11},{10,... | collective-permute-start | bytes 196616 | tf_op jit(solution)/shard_map/ppermute | solution.py:498
  9.2 4.9 %collective-permute-start.3 = (bf16[2,128,128]{2,1,0:T(8,128)(2,1)S(1)}, bf16[2,128,128]{2,1,0:T(8,128)(2,1)S(1)}, u32[]{:S(2)}, u32[]{:S(2)}) collective-permute-start(bf16[2,128,128]{2,1,0:T(8,128)(2,1)S(1)} %get-tuple-element.73), channel_id=1, source_target_pairs={{0,4},{1,5},{2,6},{3,7},{4,0},{5,1},{6,2},{7,3},{8,12},{9,13},{10,... | collective-permute-start | bytes 196616 | tf_op jit(solution)/shard_map/ppermute | solution.py:498
  9.4 9.2 %collective-permute-start.7 = (bf16[2,128,128]{2,1,0:T(8,128)(2,1)S(1)}, bf16[2,128,128]{2,1,0:T(8,128)(2,1)S(1)}, u32[]{:S(2)}, u32[]{:S(2)}) collective-permute-start(bf16[2,128,128]{2,1,0:T(8,128)(2,1)S(1)} %get-tuple-element.86), channel_id=1, source_target_pairs={{0,6},{1,7},{2,4},{3,5},{4,2},{5,3},{6,0},{7,1},{8,14},{9,15},{10,... | collective-permute-start | bytes 196616 | tf_op jit(solution)/shard_map/ppermute | solution.py:498
  12.2 6.9 %collective-permute-start.8 = (bf16[2,128,128]{2,1,0:T(8,128)(2,1)S(1)}, bf16[2,128,128]{2,1,0:T(8,128)(2,1)S(1)}, u32[]{:S(2)}, u32[]{:S(2)}) collective-permute-start(bf16[2,128,128]{2,1,0:T(8,128)(2,1)S(1)} %get-tuple-element.87), channel_id=1, source_target_pairs={{0,2},{1,3},{2,0},{3,1},{4,6},{5,7},{6,4},{7,5},{8,10},{9,11},{10,... | collective-permute-start | bytes 196616 | tf_op jit(solution)/shard_map/ppermute | solution.py:498
  12.7 7.8 %collective-permute-start.9 = (bf16[2,128,128]{2,1,0:T(8,128)(2,1)S(1)}, bf16[2,128,128]{2,1,0:T(8,128)(2,1)S(1)}, u32[]{:S(2)}, u32[]{:S(2)}) collective-permute-start(bf16[2,128,128]{2,1,0:T(8,128)(2,1)S(1)} %get-tuple-element.88), channel_id=1, source_target_pairs={{0,4},{1,5},{2,6},{3,7},{4,0},{5,1},{6,2},{7,3},{8,12},{9,13},{10,... | collective-permute-start | bytes 196616 | tf_op jit(solution)/shard_map/ppermute | solution.py:498
  14.2 6.3 %collective-permute-start.10 = (bf16[2,128,128]{2,1,0:T(8,128)(2,1)S(1)}, bf16[2,128,128]{2,1,0:T(8,128)(2,1)S(1)}, u32[]{:S(2)}, u32[]{:S(2)}) collective-permute-start(bf16[2,128,128]{2,1,0:T(8,128)(2,1)S(1)} %totals.1), channel_id=1, source_target_pairs={{0,8},{1,9},{2,10},{3,11},{4,12},{5,13},{6,14},{7,15},{8,0},{9,1},... | collective-permute-start | bytes 196616 | tf_op jit(solution)/shard_map/ppermute | solution.py:522
  16.9 5.9 %collective-permute-start.4 = (bf16[2,128,128]{2,1,0:T(8,128)(2,1)S(1)}, bf16[2,128,128]{2,1,0:T(8,128)(2,1)S(1)}, u32[]{:S(2)}, u32[]{:S(2)}) collective-permute-start(bf16[2,128,128]{2,1,0:T(8,128)(2,1)S(1)} %get-tuple-element.75), channel_id=1, source_target_pairs={{0,6},{1,7},{2,4},{3,5},{4,2},{5,3},{6,0},{7,1},{8,14},{9,15},{10,... | collective-permute-start | bytes 196616 | tf_op jit(solution)/shard_map/ppermute | solution.py:498
  18.6 5.7 %collective-permute-start.5 = (bf16[2,128,128]{2,1,0:T(8,128)(2,1)S(1)}, bf16[2,128,128]{2,1,0:T(8,128)(2,1)S(1)}, u32[]{:S(2)}, u32[]{:S(2)}) collective-permute-start(bf16[2,128,128]{2,1,0:T(8,128)(2,1)S(1)} %get-tuple-element.76), channel_id=1, source_target_pairs={{0,2},{1,3},{2,0},{3,1},{4,6},{5,7},{6,4},{7,5},{8,10},{9,11},{10,... | collective-permute-start | bytes 196616 | tf_op jit(solution)/shard_map/ppermute | solution.py:498
  19.1 5.1 %collective-permute-start.6 = (bf16[2,128,128]{2,1,0:T(8,128)(2,1)S(1)}, bf16[2,128,128]{2,1,0:T(8,128)(2,1)S(1)}, u32[]{:S(2)}, u32[]{:S(2)}) collective-permute-start(bf16[2,128,128]{2,1,0:T(8,128)(2,1)S(1)} %get-tuple-element.77), channel_id=1, source_target_pairs={{0,4},{1,5},{2,6},{3,7},{4,0},{5,1},{6,2},{7,3},{8,12},{9,13},{10,... | collective-permute-start | bytes 196616 | tf_op jit(solution)/shard_map/ppermute | solution.py:498
  20.7 5.7 %collective-permute-start.11 = (bf16[2,128,128]{2,1,0:T(8,128)(2,1)S(1)}, bf16[2,128,128]{2,1,0:T(8,128)(2,1)S(1)}, u32[]{:S(2)}, u32[]{:S(2)}) collective-permute-start(bf16[2,128,128]{2,1,0:T(8,128)(2,1)S(1)} %get-tuple-element.90), channel_id=1, source_target_pairs={{0,6},{1,7},{2,4},{3,5},{4,2},{5,3},{6,0},{7,1},{8,14},{9,15},{10,... | collective-permute-start | bytes 196616 | tf_op jit(solution)/shard_map/ppermute | solution.py:498
  22.3 4.3 %collective-permute-start.12 = (bf16[2,128,128]{2,1,0:T(8,128)(2,1)S(1)}, bf16[2,128,128]{2,1,0:T(8,128)(2,1)S(1)}, u32[]{:S(2)}, u32[]{:S(2)}) collective-permute-start(bf16[2,128,128]{2,1,0:T(8,128)(2,1)S(1)} %get-tuple-element.91), channel_id=1, source_target_pairs={{0,2},{1,3},{2,0},{3,1},{4,6},{5,7},{6,4},{7,5},{8,10},{9,11},{10,... | collective-permute-start | bytes 196616 | tf_op jit(solution)/shard_map/ppermute | solution.py:498
  22.9 4.3 %collective-permute-start.13 = (bf16[2,128,128]{2,1,0:T(8,128)(2,1)S(1)}, bf16[2,128,128]{2,1,0:T(8,128)(2,1)S(1)}, u32[]{:S(2)}, u32[]{:S(2)}) collective-permute-start(bf16[2,128,128]{2,1,0:T(8,128)(2,1)S(1)} %get-tuple-element.92), channel_id=1, source_target_pairs={{0,4},{1,5},{2,6},{3,7},{4,0},{5,1},{6,2},{7,3},{8,12},{9,13},{10,... | collective-permute-start | bytes 196616 | tf_op jit(solution)/shard_map/ppermute | solution.py:498
  24.5 2.9 %collective-permute-start.15 = (bf16[8,128,128]{2,1,0:T(8,128)(2,1)S(1)}, bf16[8,128,128]{2,1,0:T(8,128)(2,1)S(1)}, u32[]{:S(2)}, u32[]{:S(2)}) collective-permute-start(bf16[8,128,128]{2,1,0:T(8,128)(2,1)S(1)} %get-tuple-element.98), channel_id=1, source_target_pairs={{0,1},{1,0},{2,3},{3,2},{4,5},{5,4},{6,7},{7,6},{8,9},{9,8},{10,11... | collective-permute-start | bytes 786440 | tf_op jit(solution)/shard_map/ppermute | solution.py:534
  27.4 1.7 %collective-permute-start.14 = (bf16[8,128,128]{2,1,0:T(8,128)(2,1)S(1)}, bf16[8,128,128]{2,1,0:T(8,128)(2,1)S(1)}, u32[]{:S(2)}, u32[]{:S(2)}) collective-permute-start(bf16[8,128,128]{2,1,0:T(8,128)(2,1)S(1)} %get-tuple-element.93), channel_id=1, source_target_pairs={{0,1},{1,0},{2,3},{3,2},{4,5},{5,4},{6,7},{7,6},{8,9},{9,8},{10,11... | collective-permute-start | bytes 786440 | tf_op jit(solution)/shard_map/ppermute | solution.py:534

commit v16 on v15

--- a/solution.py
+++ b/solution.py
@@ -10,6 +10,7 @@
 HD = 128
 PAIRS = 4
 PARTNERS = (0, 3, 1, 2)
+STEPS = (0, 6, 3, 5)
 TEAM = 2 * PAIRS
 F32 = jnp.float32
 BF16 = jnp.bfloat16
@@ -69,6 +70,11 @@
     tail = dot(kt, v * tail_rows, (1, 0))
     head = dot(qt, scaled * head_rows, (1, 0))
     return tail.astype(BF16), head.astype(BF16)
+
+
+def half_index():
+    me = lax.axis_index("seq")
+    return (me ^ (me >> 1) ^ (me >> 2) ^ (me >> 3)) & 1
 
 
 def bring(pairs, begin, chunks, sems):
@@ -129,7 +135,7 @@
     len_pass = pltpu.make_async_copy(len_hbm, len_out, len_sems.at[1])
     len_pass.start()
     pairs = ((k_hbm, k_ref), (q_hbm, q_ref), (v_hbm, v_ref), (g_hbm, g_ref))
-    copies = bring(pairs, (1 - lax.rem(me, 2)) * out_ref.shape[1], chunks, sems)
+    copies = bring(pairs, (1 - half_index()) * out_ref.shape[1], chunks, sems)
     len_copy.wait()
     starts = doc_starts(len_ref)
     first = me * rows
@@ -227,7 +233,7 @@
     len_copy = pltpu.make_async_copy(len_hbm, len_ref, len_sem)
     len_copy.start()
     pairs = ((k_hbm, k_ref), (q_hbm, q_ref), (v_hbm, v_ref), (g_hbm, g_ref))
-    copies = bring(pairs, lax.rem(lax.axis_index("seq"), 2) * out_ref.shape[1], chunks, sems)
+    copies = bring(pairs, half_index() * out_ref.shape[1], chunks, sems)
     len_copy.wait()
     coefficients(doc_starts(len_ref), rows, total // rows, coef_ref)
     masks = rows_ref[0], rows_ref[1], root_ref[...]
@@ -371,8 +377,7 @@
 def half_of(kind, fixed, other, s_ref, kt_ref, qt_ref, bufs, outs, chunks, sems):
     heads = s_ref.shape[0]
     size = heads * HD // chunks
-    core = lax.rem(lax.axis_index("seq"), 2)
-    begin = (1 - core if other else core) * heads * HD
+    begin = (1 - half_index() if other else half_index()) * heads * HD
     copies = []
     for c in range(chunks):
         for i in range(c * heads // chunks, (c + 1) * heads // chunks):
@@ -392,7 +397,7 @@
     early, fixed, early_refs, late_refs = refs[:2], refs[2 : FIXED + 2], refs[FIXED + 2 :][:3], refs[FIXED + 5 :][:3]
     outs, bufs, (own_sems, early_sems, late_sems) = refs[-11:-7], refs[-7:-3], refs[-3:]
     width = early[0].shape[1]
-    mine = pl.ds(pl.multiple_of(lax.rem(lax.axis_index("seq"), 2) * width, HD), width)
+    mine = pl.ds(pl.multiple_of(half_index() * width, HD), width)
 
     def run(kind):
         copies = []
@@ -495,7 +500,7 @@
 
     def trade(parts):
         return [parts[0]] + [
-            lax.ppermute(parts[d], "seq", [(i, i ^ (2 * PARTNERS[d])) for i in range(n)])
+            lax.ppermute(parts[d], "seq", [(i, i ^ STEPS[d]) for i in range(n)])
             for d in range(1, PAIRS)
         ]
 
@@ -516,13 +521,14 @@
             )
         )
 
-    up = [(i, i + TEAM) for i in range(n - TEAM)]
+    up = [(i, (i + TEAM) ^ 1) for i in range(n - TEAM)]
     down = [(j, i) for i, j in up]
     if split:
         enter = lax.ppermute(edge(0), "seq", up + down)
         entering = scan(0) + scan(1, enter)
     else:
         entering = scan(0, lax.ppermute(edge(0), "seq", up)) + scan(1, lax.ppermute(edge(1), "seq", down))
+
     def post(which, *after):
         own, theirs = call(
             functools.partial(post_kernel, which, split),

time: 30.4 us -> 29.3 us (0.964)
  starting transfers between devices: 18.6 us -> 17.6 us
    ppermute x12, starting transfers between devices: 15.3 us -> 13.9 us  [trade(): lax.ppermute(parts[d], 'seq', [(i, i ^ STEPS[d]) for i in range(n)])]
where the time goes in v16:
time: 29.3 us; the launch traced here: 29.2 us
  starting transfers between devices  17.6 us (60%)
  Pallas kernels  9.19 us (31%)
  waiting for transfers between devices  1.62 us (6%)
  between operations  0.73 us (2%)
    ppermute x12, starting transfers between devices, trade(): lax.ppermute(parts[d], 'seq', [(i, i ^ STEPS[d]) for i in range(n)])  13.9 us
    pallas_call x11, Pallas kernels, call(): pl.pallas_call(kernel, in_specs=specs, out_specs=out_specs or [vmem] * le...  9.19 us
    ppermute x1, starting transfers between devices, per_device(): enter = lax.ppermute(edge(0), 'seq', up + down)  2.84 us
    ppermute x12, waiting for transfers between devices, trade(): lax.ppermute(parts[d], 'seq', [(i, i ^ STEPS[d]) for i in range(n)])  1.61 us
  transfers between devices with their start and end apart: 16, of which 3 were waited for; matrix products, arithmetic and copies ran while one was open for 0% of the time, Pallas kernels for 20%

profile of v16, /device:TPU:0, one launch (start us, length us, event | category | flops | bytes accessed | tf_op | source)
XLA Modules:
  0.0 29.2 jit_solution(5165705618093036715)
XLA Ops:
  0.6 1.9 %send.1 = (s32[8]{0:T(128)S(1)}, bf16[2,8,128,128]{3,2,1,0:T(8,128)(2,1)S(1)}, bf16[128,1024]{1,0:T(8,128)(2,1)S(1)}, bf16[128,1024]{1,0:T(8,128)(2,1)S(1)}, bf1...) custom-call(s32[8]{0:T(128)} %len_hbm.1, ...), custom_call_target="tpu_custom_call" | custom-call | flops 67108864 | bytes 4325440 | tf_op jit(solution)/shard_map/send/pallas_call | solution.py:443
  2.5 0.5 %collective-permute-start = (bf16[2,8,128,128]{3,2,1,0:T(8,128)(2,1)S(1)}, bf16[2,8,128,128]{3,2,1,0:T(8,128)(2,1)S(1)}, u32[]{:S(2)}, u32[]{:S(2)}) collective-permute-start(bf16[2,8,128,128]{3,2,1,0:T(8,128)(2,1)S(1)} %get-tuple-element.69), channel_id=1, source_target_pairs={{0,1},{1,0},{2,3},{3,2},{4,5},{5,4},{6,7},{7,6},{8,9},{9,8},{10,11... | collective-permute-start | bytes 1572872 | tf_op jit(solution)/shard_map/ppermute | solution.py:479
  3.0 1.8 %keep.1 = (bf16[2,8,128,128]{3,2,1,0:T(8,128)(2,1)S(1)}, bf16[128,1024]{1,0:T(8,128)(2,1)S(1)}, bf16[128,1024]{1,0:T(8,128)(2,1)S(1)}, bf16[128,1024]{1,0:T(8,12...) custom-call(s32[8]{0:T(128)S(1)} %get-tuple-element.54.len_hbm, ...), custom_call_target="tpu_custom_call" | custom-call | flops 67108864 | bytes 4358176 | tf_op jit(solution)/shard_map/keep/pallas_call | solution.py:443
  4.9 0.2 pair.1
  5.1 3.6 %collective-permute-start.1 = (bf16[2,128,128]{2,1,0:T(8,128)(2,1)S(1)}, bf16[2,128,128]{2,1,0:T(8,128)(2,1)S(1)}, u32[]{:S(2)}, u32[]{:S(2)}) collective-permute-start(bf16[2,128,128]{2,1,0:T(8,128)(2,1)S(1)} %get-tuple-element.71), channel_id=1, source_target_pairs={{0,6},{1,7},{2,4},{3,5},{4,2},{5,3},{6,0},{7,1},{8,14},{9,15},{10,... | collective-permute-start | bytes 196616 | tf_op jit(solution)/shard_map/ppermute | solution.py:503
  8.7 0.3 %collective-permute-start.2 = (bf16[2,128,128]{2,1,0:T(8,128)(2,1)S(1)}, bf16[2,128,128]{2,1,0:T(8,128)(2,1)S(1)}, u32[]{:S(2)}, u32[]{:S(2)}) collective-permute-start(bf16[2,128,128]{2,1,0:T(8,128)(2,1)S(1)} %get-tuple-element.72), channel_id=1, source_target_pairs={{0,3},{1,2},{2,1},{3,0},{4,7},{5,6},{6,5},{7,4},{8,11},{9,10},{10,... | collective-permute-start | bytes 196616 | tf_op jit(solution)/shard_map/ppermute | solution.py:503
  9.0 0.1 collective-permute-start.3
  9.1 2.8 %collective-permute-start.7 = (bf16[2,128,128]{2,1,0:T(8,128)(2,1)S(1)}, bf16[2,128,128]{2,1,0:T(8,128)(2,1)S(1)}, u32[]{:S(2)}, u32[]{:S(2)}) collective-permute-start(bf16[2,128,128]{2,1,0:T(8,128)(2,1)S(1)} %get-tuple-element.86), channel_id=1, source_target_pairs={{0,6},{1,7},{2,4},{3,5},{4,2},{5,3},{6,0},{7,1},{8,14},{9,15},{10,... | collective-permute-start | bytes 196616 | tf_op jit(solution)/shard_map/ppermute | solution.py:503
  11.9 0.0 collective-permute-start.8
  11.9 0.5 %collective-permute-start.9 = (bf16[2,128,128]{2,1,0:T(8,128)(2,1)S(1)}, bf16[2,128,128]{2,1,0:T(8,128)(2,1)S(1)}, u32[]{:S(2)}, u32[]{:S(2)}) collective-permute-start(bf16[2,128,128]{2,1,0:T(8,128)(2,1)S(1)} %get-tuple-element.88), channel_id=1, source_target_pairs={{0,5},{1,4},{2,7},{3,6},{4,1},{5,0},{6,3},{7,2},{8,13},{9,12},{10,... | collective-permute-start | bytes 196616 | tf_op jit(solution)/shard_map/ppermute | solution.py:503
  12.4 0.4 %collective-permute-done.2.refs_2_.s2 = bf16[2,128,128]{2,1,0:T(8,128)(2,1)S(1)} collective-permute-done((bf16[2,128,128]{2,1,0:T(8,128)(2,1)S(1)}, bf16[2,128,128]{2,1,0:T(8,128)(2,1)S(1)}, u32[]{:S(2)}, u32[]{:S(2)}) %collective-permute-start.2) | collective-permute-done | bytes 65568 | tf_op jit(solution)/shard_map/ppermute | solution.py:503
  12.8 0.2 collective-permute-done.3.refs_3_.s3
  13.0 0.1 totals.1
  13.0 2.8 %collective-permute-start.10 = (bf16[2,128,128]{2,1,0:T(8,128)(2,1)S(1)}, bf16[2,128,128]{2,1,0:T(8,128)(2,1)S(1)}, u32[]{:S(2)}, u32[]{:S(2)}) collective-permute-start(bf16[2,128,128]{2,1,0:T(8,128)(2,1)S(1)} %totals.1), channel_id=1, source_target_pairs={{0,9},{1,8},{2,11},{3,10},{4,13},{5,12},{6,15},{7,14},{9,0},{8,1},... | collective-permute-start | bytes 196616 | tf_op jit(solution)/shard_map/ppermute | solution.py:527
  15.9 0.1 scan.2
  16.0 1.6 %collective-permute-start.4 = (bf16[2,128,128]{2,1,0:T(8,128)(2,1)S(1)}, bf16[2,128,128]{2,1,0:T(8,128)(2,1)S(1)}, u32[]{:S(2)}, u32[]{:S(2)}) collective-permute-start(bf16[2,128,128]{2,1,0:T(8,128)(2,1)S(1)} %get-tuple-element.75), channel_id=1, source_target_pairs={{0,6},{1,7},{2,4},{3,5},{4,2},{5,3},{6,0},{7,1},{8,14},{9,15},{10,... | collective-permute-start | bytes 196616 | tf_op jit(solution)/shard_map/ppermute | solution.py:503
  17.6 0.8 %collective-permute-start.5 = (bf16[2,128,128]{2,1,0:T(8,128)(2,1)S(1)}, bf16[2,128,128]{2,1,0:T(8,128)(2,1)S(1)}, u32[]{:S(2)}, u32[]{:S(2)}) collective-permute-start(bf16[2,128,128]{2,1,0:T(8,128)(2,1)S(1)} %get-tuple-element.76), channel_id=1, source_target_pairs={{0,3},{1,2},{2,1},{3,0},{4,7},{5,6},{6,5},{7,4},{8,11},{9,10},{10,... | collective-permute-start | bytes 196616 | tf_op jit(solution)/shard_map/ppermute | solution.py:503
  18.3 0.0 collective-permute-done.8.refs_2_
  18.3 1.0 %collective-permute-start.6 = (bf16[2,128,128]{2,1,0:T(8,128)(2,1)S(1)}, bf16[2,128,128]{2,1,0:T(8,128)(2,1)S(1)}, u32[]{:S(2)}, u32[]{:S(2)}) collective-permute-start(bf16[2,128,128]{2,1,0:T(8,128)(2,1)S(1)} %get-tuple-element.77), channel_id=1, source_target_pairs={{0,5},{1,4},{2,7},{3,6},{4,1},{5,0},{6,3},{7,2},{8,13},{9,12},{10,... | collective-permute-start | bytes 196616 | tf_op jit(solution)/shard_map/ppermute | solution.py:503
  19.3 0.2 scan.3
  19.5 1.9 %collective-permute-start.11 = (bf16[2,128,128]{2,1,0:T(8,128)(2,1)S(1)}, bf16[2,128,128]{2,1,0:T(8,128)(2,1)S(1)}, u32[]{:S(2)}, u32[]{:S(2)}) collective-permute-start(bf16[2,128,128]{2,1,0:T(8,128)(2,1)S(1)} %get-tuple-element.90), channel_id=1, source_target_pairs={{0,6},{1,7},{2,4},{3,5},{4,2},{5,3},{6,0},{7,1},{8,14},{9,15},{10,... | collective-permute-start | bytes 196616 | tf_op jit(solution)/shard_map/ppermute | solution.py:503
  21.4 0.2 collective-permute-start.12
  21.6 0.0 collective-permute-done.4.refs_1_
  21.6 1.2 %collective-permute-start.13 = (bf16[2,128,128]{2,1,0:T(8,128)(2,1)S(1)}, bf16[2,128,128]{2,1,0:T(8,128)(2,1)S(1)}, u32[]{:S(2)}, u32[]{:S(2)}) collective-permute-start(bf16[2,128,128]{2,1,0:T(8,128)(2,1)S(1)} %get-tuple-element.92), channel_id=1, source_target_pairs={{0,5},{1,4},{2,7},{3,6},{4,1},{5,0},{6,3},{7,2},{8,13},{9,12},{10,... | collective-permute-start | bytes 196616 | tf_op jit(solution)/shard_map/ppermute | solution.py:503
  22.8 0.2 post.2
  23.0 0.1 collective-permute-start.15
  23.2 1.8 %local.1 = (bf16[16,128,128]{2,1,0:T(8,128)(2,1)S(1)}, bf16[16,128,128]{2,1,0:T(8,128)(2,1)S(1)}, bf16[16,128,128]{2,1,0:T(8,128)(2,1)S(1)}, bf16[16,128,128]{2,...) custom-call(s32[8]{0:T(128)S(1)} %get-tuple-element.54.len_hbm, ...), custom_call_target="tpu_custom_call" | custom-call | flops 134217728 | bytes 6160416 | tf_op jit(solution)/shard_map/local/pallas_call | solution.py:443
  25.0 1.0 %collective-permute-done.12.refs_2_ = bf16[2,128,128]{2,1,0:T(8,128)(2,1)S(1)} collective-permute-done((bf16[2,128,128]{2,1,0:T(8,128)(2,1)S(1)}, bf16[2,128,128]{2,1,0:T(8,128)(2,1)S(1)}, u32[]{:S(2)}, u32[]{:S(2)}) %collective-permute-start.12) | collective-permute-done | bytes 65568 | tf_op jit(solution)/shard_map/ppermute | solution.py:503
  26.0 0.2 post.3
  26.2 0.2 collective-permute-start.14
  26.4 1.5 %middle.1 = (bf16[128,2048]{1,0:T(8,128)(2,1)}, bf16[128,2048]{1,0:T(8,128)(2,1)}, bf16[128,2048]{1,0:T(8,128)(2,1)}, bf16[128,2048]{1,0:T(8,128)(2,1)}) custom-call(bf16[128,1024]{1,0:T(8,128)(2,1)S(1)} %get-tuple-element.96.refs_0_, bf16[128,1024]{1,0:T(8,128)(2,1)S(1)} %get-tuple-element.97.refs_1_, ...), custom_call_target="tpu_custom_call" | custom-call | flops 268435456 | bytes 8519680 | tf_op jit(solution)/shard_map/middle/pallas_call | solution.py:443
  28.0 1.2 %last.1 = (bf16[128,2048]{1,0:T(8,128)(2,1)}, bf16[128,2048]{1,0:T(8,128)(2,1)}, bf16[128,2048]{1,0:T(8,128)(2,1)}, bf16[128,2048]{1,0:T(8,128)(2,1)}) custom-call(bf16[128,1024]{1,0:T(8,128)(2,1)S(1)} %get-tuple-element.57.refs_0_.refs_2_, ...), custom_call_target="tpu_custom_call", output_to_operand_aliasing={{0}: (16, {}), {1}: (17, {}), {2}: (18, {}), {3}: (19, {})} | custom-call | flops 134217728 | bytes 9306112 | tf_op jit(solution)/shard_map/last/pallas_call | solution.py:443
  (11 shorter events, 0.0 us)
Async XLA Ops:
  2.5 2.4 %collective-permute-start = (bf16[2,8,128,128]{3,2,1,0:T(8,128)(2,1)S(1)}, bf16[2,8,128,128]{3,2,1,0:T(8,128)(2,1)S(1)}, u32[]{:S(2)}, u32[]{:S(2)}) collective-permute-start(bf16[2,8,128,128]{3,2,1,0:T(8,128)(2,1)S(1)} %get-tuple-element.69), channel_id=1, source_target_pairs={{0,1},{1,0},{2,3},{3,2},{4,5},{5,4},{6,7},{7,6},{8,9},{9,8},{10,11... | collective-permute-start | bytes 1572872 | tf_op jit(solution)/shard_map/ppermute | solution.py:479
  5.1 6.9 %collective-permute-start.1 = (bf16[2,128,128]{2,1,0:T(8,128)(2,1)S(1)}, bf16[2,128,128]{2,1,0:T(8,128)(2,1)S(1)}, u32[]{:S(2)}, u32[]{:S(2)}) collective-permute-start(bf16[2,128,128]{2,1,0:T(8,128)(2,1)S(1)} %get-tuple-element.71), channel_id=1, source_target_pairs={{0,6},{1,7},{2,4},{3,5},{4,2},{5,3},{6,0},{7,1},{8,14},{9,15},{10,... | collective-permute-start | bytes 196616 | tf_op jit(solution)/shard_map/ppermute | solution.py:503
  8.7 4.1 %collective-permute-start.2 = (bf16[2,128,128]{2,1,0:T(8,128)(2,1)S(1)}, bf16[2,128,128]{2,1,0:T(8,128)(2,1)S(1)}, u32[]{:S(2)}, u32[]{:S(2)}) collective-permute-start(bf16[2,128,128]{2,1,0:T(8,128)(2,1)S(1)} %get-tuple-element.72), channel_id=1, source_target_pairs={{0,3},{1,2},{2,1},{3,0},{4,7},{5,6},{6,5},{7,4},{8,11},{9,10},{10,... | collective-permute-start | bytes 196616 | tf_op jit(solution)/shard_map/ppermute | solution.py:503
  9.0 4.0 %collective-permute-start.3 = (bf16[2,128,128]{2,1,0:T(8,128)(2,1)S(1)}, bf16[2,128,128]{2,1,0:T(8,128)(2,1)S(1)}, u32[]{:S(2)}, u32[]{:S(2)}) collective-permute-start(bf16[2,128,128]{2,1,0:T(8,128)(2,1)S(1)} %get-tuple-element.73), channel_id=1, source_target_pairs={{0,5},{1,4},{2,7},{3,6},{4,1},{5,0},{6,3},{7,2},{8,13},{9,12},{10,... | collective-permute-start | bytes 196616 | tf_op jit(solution)/shard_map/ppermute | solution.py:503
  9.1 8.5 %collective-permute-start.7 = (bf16[2,128,128]{2,1,0:T(8,128)(2,1)S(1)}, bf16[2,128,128]{2,1,0:T(8,128)(2,1)S(1)}, u32[]{:S(2)}, u32[]{:S(2)}) collective-permute-start(bf16[2,128,128]{2,1,0:T(8,128)(2,1)S(1)} %get-tuple-element.86), channel_id=1, source_target_pairs={{0,6},{1,7},{2,4},{3,5},{4,2},{5,3},{6,0},{7,1},{8,14},{9,15},{10,... | collective-permute-start | bytes 196616 | tf_op jit(solution)/shard_map/ppermute | solution.py:503
  11.9 6.4 %collective-permute-start.8 = (bf16[2,128,128]{2,1,0:T(8,128)(2,1)S(1)}, bf16[2,128,128]{2,1,0:T(8,128)(2,1)S(1)}, u32[]{:S(2)}, u32[]{:S(2)}) collective-permute-start(bf16[2,128,128]{2,1,0:T(8,128)(2,1)S(1)} %get-tuple-element.87), channel_id=1, source_target_pairs={{0,3},{1,2},{2,1},{3,0},{4,7},{5,6},{6,5},{7,4},{8,11},{9,10},{10,... | collective-permute-start | bytes 196616 | tf_op jit(solution)/shard_map/ppermute | solution.py:503
  11.9 7.4 %collective-permute-start.9 = (bf16[2,128,128]{2,1,0:T(8,128)(2,1)S(1)}, bf16[2,128,128]{2,1,0:T(8,128)(2,1)S(1)}, u32[]{:S(2)}, u32[]{:S(2)}) collective-permute-start(bf16[2,128,128]{2,1,0:T(8,128)(2,1)S(1)} %get-tuple-element.88), channel_id=1, source_target_pairs={{0,5},{1,4},{2,7},{3,6},{4,1},{5,0},{6,3},{7,2},{8,13},{9,12},{10,... | collective-permute-start | bytes 196616 | tf_op jit(solution)/shard_map/ppermute | solution.py:503
  13.0 6.3 %collective-permute-start.10 = (bf16[2,128,128]{2,1,0:T(8,128)(2,1)S(1)}, bf16[2,128,128]{2,1,0:T(8,128)(2,1)S(1)}, u32[]{:S(2)}, u32[]{:S(2)}) collective-permute-start(bf16[2,128,128]{2,1,0:T(8,128)(2,1)S(1)} %totals.1), channel_id=1, source_target_pairs={{0,9},{1,8},{2,11},{3,10},{4,13},{5,12},{6,15},{7,14},{9,0},{8,1},... | collective-permute-start | bytes 196616 | tf_op jit(solution)/shard_map/ppermute | solution.py:527
  16.0 5.6 %collective-permute-start.4 = (bf16[2,128,128]{2,1,0:T(8,128)(2,1)S(1)}, bf16[2,128,128]{2,1,0:T(8,128)(2,1)S(1)}, u32[]{:S(2)}, u32[]{:S(2)}) collective-permute-start(bf16[2,128,128]{2,1,0:T(8,128)(2,1)S(1)} %get-tuple-element.75), channel_id=1, source_target_pairs={{0,6},{1,7},{2,4},{3,5},{4,2},{5,3},{6,0},{7,1},{8,14},{9,15},{10,... | collective-permute-start | bytes 196616 | tf_op jit(solution)/shard_map/ppermute | solution.py:503
  17.6 5.2 %collective-permute-start.5 = (bf16[2,128,128]{2,1,0:T(8,128)(2,1)S(1)}, bf16[2,128,128]{2,1,0:T(8,128)(2,1)S(1)}, u32[]{:S(2)}, u32[]{:S(2)}) collective-permute-start(bf16[2,128,128]{2,1,0:T(8,128)(2,1)S(1)} %get-tuple-element.76), channel_id=1, source_target_pairs={{0,3},{1,2},{2,1},{3,0},{4,7},{5,6},{6,5},{7,4},{8,11},{9,10},{10,... | collective-permute-start | bytes 196616 | tf_op jit(solution)/shard_map/ppermute | solution.py:503
  18.3 4.4 %collective-permute-start.6 = (bf16[2,128,128]{2,1,0:T(8,128)(2,1)S(1)}, bf16[2,128,128]{2,1,0:T(8,128)(2,1)S(1)}, u32[]{:S(2)}, u32[]{:S(2)}) collective-permute-start(bf16[2,128,128]{2,1,0:T(8,128)(2,1)S(1)} %get-tuple-element.77), channel_id=1, source_target_pairs={{0,5},{1,4},{2,7},{3,6},{4,1},{5,0},{6,3},{7,2},{8,13},{9,12},{10,... | collective-permute-start | bytes 196616 | tf_op jit(solution)/shard_map/ppermute | solution.py:503
  19.5 5.5 %collective-permute-start.11 = (bf16[2,128,128]{2,1,0:T(8,128)(2,1)S(1)}, bf16[2,128,128]{2,1,0:T(8,128)(2,1)S(1)}, u32[]{:S(2)}, u32[]{:S(2)}) collective-permute-start(bf16[2,128,128]{2,1,0:T(8,128)(2,1)S(1)} %get-tuple-element.90), channel_id=1, source_target_pairs={{0,6},{1,7},{2,4},{3,5},{4,2},{5,3},{6,0},{7,1},{8,14},{9,15},{10,... | collective-permute-start | bytes 196616 | tf_op jit(solution)/shard_map/ppermute | solution.py:503
  21.4 4.6 %collective-permute-start.12 = (bf16[2,128,128]{2,1,0:T(8,128)(2,1)S(1)}, bf16[2,128,128]{2,1,0:T(8,128)(2,1)S(1)}, u32[]{:S(2)}, u32[]{:S(2)}) collective-permute-start(bf16[2,128,128]{2,1,0:T(8,128)(2,1)S(1)} %get-tuple-element.91), channel_id=1, source_target_pairs={{0,3},{1,2},{2,1},{3,0},{4,7},{5,6},{6,5},{7,4},{8,11},{9,10},{10,... | collective-permute-start | bytes 196616 | tf_op jit(solution)/shard_map/ppermute | solution.py:503
  21.6 4.4 %collective-permute-start.13 = (bf16[2,128,128]{2,1,0:T(8,128)(2,1)S(1)}, bf16[2,128,128]{2,1,0:T(8,128)(2,1)S(1)}, u32[]{:S(2)}, u32[]{:S(2)}) collective-permute-start(bf16[2,128,128]{2,1,0:T(8,128)(2,1)S(1)} %get-tuple-element.92), channel_id=1, source_target_pairs={{0,5},{1,4},{2,7},{3,6},{4,1},{5,0},{6,3},{7,2},{8,13},{9,12},{10,... | collective-permute-start | bytes 196616 | tf_op jit(solution)/shard_map/ppermute | solution.py:503
  23.0 3.4 %collective-permute-start.15 = (bf16[8,128,128]{2,1,0:T(8,128)(2,1)S(1)}, bf16[8,128,128]{2,1,0:T(8,128)(2,1)S(1)}, u32[]{:S(2)}, u32[]{:S(2)}) collective-permute-start(bf16[8,128,128]{2,1,0:T(8,128)(2,1)S(1)} %get-tuple-element.98), channel_id=1, source_target_pairs={{0,1},{1,0},{2,3},{3,2},{4,5},{5,4},{6,7},{7,6},{8,9},{9,8},{10,11... | collective-permute-start | bytes 786440 | tf_op jit(solution)/shard_map/ppermute | solution.py:540
  26.2 1.8 %collective-permute-start.14 = (bf16[8,128,128]{2,1,0:T(8,128)(2,1)S(1)}, bf16[8,128,128]{2,1,0:T(8,128)(2,1)S(1)}, u32[]{:S(2)}, u32[]{:S(2)}) collective-permute-start(bf16[8,128,128]{2,1,0:T(8,128)(2,1)S(1)} %get-tuple-element.93), channel_id=1, source_target_pairs={{0,1},{1,0},{2,3},{3,2},{4,5},{5,4},{6,7},{7,6},{8,9},{9,8},{10,11... | collective-permute-start | bytes 786440 | tf_op jit(solution)/shard_map/ppermute | solution.py:540

commit v17 on v16

--- a/solution.py
+++ b/solution.py
@@ -11,6 +11,7 @@
 PAIRS = 4
 PARTNERS = (0, 3, 1, 2)
 STEPS = (0, 6, 3, 5)
+EARLY_BACK = (0, 2, 1, 3)
 TEAM = 2 * PAIRS
 F32 = jnp.float32
 BF16 = jnp.bfloat16
@@ -325,17 +326,17 @@
             out_ref[i] = sum(terms).astype(BF16)
 
 
-def post_kernel(which, split, coef_ref, keep_ref, got_ref, *refs):
+def post_kernel(which, split, order, coef_ref, keep_ref, got_ref, *refs):
     mine_ref, theirs_ref = refs[-2:]
     per = refs[0].shape[0]
     pair = lax.rem(lax.axis_index("seq"), TEAM) // 2
     kind = kind_of(which, split)
     m0, m1 = coef(coef_ref, MINE_F + 2 * kind), coef(coef_ref, MINE_F + 2 * kind + 1)
     t0, t1 = coef(coef_ref, THEIRS_F + 2 * kind), coef(coef_ref, THEIRS_F + 2 * kind + 1)
-    for d in range(PAIRS):
+    for ref, d in zip(refs, order):
         for i in range(per):
             h = (pair ^ PARTNERS[d]) * per + i
-            came = refs[d][i].astype(F32)
+            came = ref[i].astype(F32)
             theirs_ref[h] = (came * t0 + keep_ref[kind, h].astype(F32) * t1).astype(BF16)
             mine_ref[h] = (came * m0 + got_ref[kind, h].astype(F32) * m1).astype(BF16)
 
@@ -374,39 +375,48 @@
     return dk.astype(BF16), dv.astype(BF16)
 
 
-def half_of(kind, fixed, other, s_ref, kt_ref, qt_ref, bufs, outs, chunks, sems):
+def write(refs, columns, kind, outs, to, sems):
+    copies = [
+        pltpu.make_async_copy(refs[j].at[:, columns], outs[2 * kind + j].at[:, to], sems.at[j])
+        for j in range(2)
+    ]
+    for copy in copies:
+        copy.start()
+    return copies
+
+
+def place(half, width):
+    return pl.ds(pl.multiple_of(half * width, HD), width)
+
+
+def half_of(kind, fixed, other, s_ref, kt_ref, qt_ref, bufs, chunks=1, send=None):
     heads = s_ref.shape[0]
     size = heads * HD // chunks
-    begin = (1 - half_index() if other else half_index()) * heads * HD
     copies = []
     for c in range(chunks):
         for i in range(c * heads // chunks, (c + 1) * heads // chunks):
             at = pl.ds(i * HD, HD)
             bufs[0][:, at], bufs[1][:, at] = outputs_of(kind, fixed, other, s_ref[i], kt_ref, qt_ref, i)
-        to = pl.ds(pl.multiple_of(begin + c * size, HD), size)
-        for j in range(2):
-            copy = pltpu.make_async_copy(
-                bufs[j].at[:, pl.ds(c * size, size)], outs[2 * kind + j].at[:, to], sems.at[c, j]
-            )
-            copy.start()
-            copies.append(copy)
+        if send:
+            copies += send(c, pl.ds(c * size, size))
     return copies
 
 
 def middle_kernel(split, chunks, *refs):
     early, fixed, early_refs, late_refs = refs[:2], refs[2 : FIXED + 2], refs[FIXED + 2 :][:3], refs[FIXED + 5 :][:3]
-    outs, bufs, (own_sems, early_sems, late_sems) = refs[-11:-7], refs[-7:-3], refs[-3:]
+    outs, late, bufs, (own_sems, sems) = refs[-10:-6], refs[-6:-4], refs[-4:-2], refs[-2:]
     width = early[0].shape[1]
-    mine = pl.ds(pl.multiple_of(half_index() * width, HD), width)
+    mine = half_index()
 
     def run(kind):
-        copies = []
-        for j in range(2):
-            copy = pltpu.make_async_copy(early[j], outs[2 * kind + j].at[:, mine], own_sems.at[j])
-            copy.start()
-            copies.append(copy)
-        copies += half_of(kind, fixed, 1, *early_refs, bufs[:2], outs, chunks, early_sems)
-        copies += half_of(1 - kind, fixed, 0, *late_refs, bufs[2:], outs, chunks, late_sems)
+        copies = write(early, pl.ds(0, width), kind, outs, place(mine, width), own_sems)
+
+        def send(c, at):
+            to = place((1 - mine) * chunks + c, width // chunks)
+            return write(bufs, at, kind, outs, to, sems.at[c])
+
+        copies += half_of(kind, fixed, 1, *early_refs, bufs, chunks, send)
+        half_of(1 - kind, fixed, 0, *late_refs, late)
         for copy in copies:
             copy.wait()
 
@@ -414,11 +424,20 @@
 
 
 def last_kernel(split, chunks, *refs):
-    fixed, late_refs = refs[:FIXED], refs[FIXED : FIXED + 3]
-    outs, bufs, sems = refs[-7:-3], refs[-3:-1], refs[-1]
+    fixed, late_refs, late = refs[:FIXED], refs[FIXED : FIXED + 3], refs[FIXED + 3 :][:2]
+    outs, bufs, (own_sems, sems) = refs[-8:-4], refs[-4:-2], refs[-2:]
+    width = late[0].shape[1]
+    mine = half_index()
 
     def run(kind):
-        for copy in half_of(kind, fixed, 1, *late_refs, bufs, outs, chunks, sems):
+        copies = write(late, pl.ds(0, width), kind, outs, place(mine, width), own_sems)
+
+        def send(c, at):
+            to = place((1 - mine) * chunks + c, width // chunks)
+            return write(bufs, at, kind, outs, to, sems.at[c])
+
+        copies += half_of(kind, fixed, 1, *late_refs, bufs, chunks, send)
+        for copy in copies:
             copy.wait()
 
     on_kind(1, split, run)
@@ -498,10 +517,10 @@
         [vmem] * 3,
     )
 
-    def trade(parts):
-        return [parts[0]] + [
-            lax.ppermute(parts[d], "seq", [(i, i ^ STEPS[d]) for i in range(n)])
-            for d in range(1, PAIRS)
+    def trade(parts, order=range(PAIRS)):
+        return [
+            lax.ppermute(parts[d], "seq", [(i, i ^ STEPS[d]) for i in range(n)]) if d else parts[0]
+            for d in order
         ]
 
     sums = [trade(parts[:PAIRS]), trade(parts[PAIRS:])]
@@ -511,35 +530,34 @@
         return call(kernel, "totals", [owned], (table, *sums[which]), [vmem] * 5)[0]
 
     def scan(which, *enter):
-        return trade(
-            call(
-                functools.partial(scan_kernel, which, split, bool(enter)),
-                "scan",
-                [owned] * PAIRS,
-                (table, *sums[which], *enter),
-                [vmem] * (5 + len(enter)),
-            )
+        return call(
+            functools.partial(scan_kernel, which, split, bool(enter)),
+            "scan",
+            [owned] * PAIRS,
+            (table, *sums[which], *enter),
+            [vmem] * (5 + len(enter)),
         )
 
     up = [(i, (i + TEAM) ^ 1) for i in range(n - TEAM)]
     down = [(j, i) for i, j in up]
     if split:
         enter = lax.ppermute(edge(0), "seq", up + down)
-        entering = scan(0) + scan(1, enter)
+        results = scan(0), scan(1, enter)
     else:
-        entering = scan(0, lax.ppermute(edge(0), "seq", up)) + scan(1, lax.ppermute(edge(1), "seq", down))
-
-    def post(which, *after):
+        forward, backward = lax.ppermute(edge(0), "seq", up), lax.ppermute(edge(1), "seq", down)
+        results = scan(0, forward), scan(1, backward)
+
+    def post(which, order, *after):
         own, theirs = call(
-            functools.partial(post_kernel, which, split),
+            functools.partial(post_kernel, which, split, order),
             "post",
             [halves] * 2,
-            (table, keep, got, *entering[which * PAIRS :][:PAIRS], *after),
+            (table, keep, got, *trade(results[which], order), *after),
             [vmem] * (3 + PAIRS + len(after)),
         )
         return own, lax.ppermute(theirs, "seq", swap)
 
-    early_mine, early_other = post(0)
+    early_mine, early_other = post(0, EARLY_BACK)
     *local, masks, early_0, early_1 = call(
         functools.partial(local_kernel, total, split),
         "local",
@@ -549,32 +567,36 @@
         flops=2 * heads * product,
         scratch=lengths,
     )
-    late_mine, late_other = post(1, masks)
+    late_mine, late_other = post(1, range(PAIRS), masks)
     w, wt, dw, dwt, scaled = local
     fixed = (*mines[:3], *others[:3], scaled, w, wt, dw, dwt, masks, root)
     chunks = 4
-    pieces = pltpu.SemaphoreType.DMA((chunks, 2))
-    outs = call(
+    scratch = [pltpu.VMEM(part.shape, BF16)] * 2 + [
+        pltpu.SemaphoreType.DMA((2,)),
+        pltpu.SemaphoreType.DMA((chunks, 2)),
+    ]
+    *outs, late_0, late_1 = call(
         functools.partial(middle_kernel, split, chunks),
         "middle",
-        [tokens] * 4,
+        [tokens] * 4 + [part] * 2,
         (early_0, early_1, *fixed, early_other, kt_other, qt_other, late_mine, kt_mine, qt_mine),
         [vmem] * (FIXED + 8),
-        [hbm] * 4,
+        [hbm] * 4 + [vmem] * 2,
         flops=8 * half * product,
-        scratch=[pltpu.VMEM(part.shape, BF16)] * 4 + [pltpu.SemaphoreType.DMA((2,)), pieces, pieces],
-    )
+        scratch=scratch,
+    )
+    given = (*fixed, late_other, kt_other, qt_other, late_0, late_1)
     return tuple(
         call(
             functools.partial(last_kernel, split, chunks),
             "last",
             [tokens] * 4,
-            (*fixed, late_other, kt_other, qt_other, *outs),
-            [vmem] * (FIXED + 3) + [hbm] * 4,
+            (*given, *outs),
+            [vmem] * len(given) + [hbm] * 4,
             [hbm] * 4,
             flops=4 * half * product,
-            scratch=[pltpu.VMEM(part.shape, BF16)] * 2 + [pieces],
-            aliases={FIXED + 3 + i: i for i in range(4)},
+            scratch=scratch,
+            aliases={len(given) + i: i for i in range(4)},
         )
     )
 

time: 29.3 us -> 30.1 us (1.027)
  waiting for transfers between devices: 1.62 us -> 2.95 us
    ppermute x12, waiting for transfers between devices: 1.61 us -> 2.87 us  [trade(): lax.ppermute(parts[d], 'seq', [(i, i ^ STEPS[d]) for i in range(n)])]
  transfers between devices with their start and end apart: 16 -> 16, of which waited for: 3 -> 6; matrix products, arithmetic and copies ran while one was open for 0% -> 0% of each run, Pallas kernels for 20% -> 19%
where the time goes in v17:
time: 30.1 us; the launch traced here: 30 us
  starting transfers between devices  17.3 us (57%)
  Pallas kernels  8.97 us (30%)
  waiting for transfers between devices  2.95 us (10%)
  between operations  0.71 us (2%)
    ppermute x12, starting transfers between devices, trade(): lax.ppermute(parts[d], 'seq', [(i, i ^ STEPS[d]) for i in range(n)])  13.6 us
    pallas_call x11, Pallas kernels, call(): pl.pallas_call(kernel, in_specs=specs, out_specs=out_specs or [vmem] * le...  8.97 us
    ppermute x12, waiting for transfers between devices, trade(): lax.ppermute(parts[d], 'seq', [(i, i ^ STEPS[d]) for i in range(n)])  2.87 us
    ppermute x1, starting transfers between devices, per_device(): enter = lax.ppermute(edge(0), 'seq', up + down)  2.85 us
  transfers between devices with their start and end apart: 16, of which 6 were waited for; matrix products, arithmetic and copies ran while one was open for 0% of the time, Pallas kernels for 19%

profile of v17, /device:TPU:0, one launch (start us, length us, event | category | flops | bytes accessed | tf_op | source)
XLA Modules:
  0.0 30.0 jit_solution(7362278651982154973)
XLA Ops:
  0.6 1.9 %send.1 = (s32[8]{0:T(128)S(1)}, bf16[2,8,128,128]{3,2,1,0:T(8,128)(2,1)S(1)}, bf16[128,1024]{1,0:T(8,128)(2,1)S(1)}, bf16[128,1024]{1,0:T(8,128)(2,1)S(1)}, bf1...) custom-call(s32[8]{0:T(128)} %len_hbm.1, ...), custom_call_target="tpu_custom_call" | custom-call | flops 67108864 | bytes 4325440 | tf_op jit(solution)/shard_map/send/pallas_call | solution.py:462
  2.5 0.5 %collective-permute-start = (bf16[2,8,128,128]{3,2,1,0:T(8,128)(2,1)S(1)}, bf16[2,8,128,128]{3,2,1,0:T(8,128)(2,1)S(1)}, u32[]{:S(2)}, u32[]{:S(2)}) collective-permute-start(bf16[2,8,128,128]{3,2,1,0:T(8,128)(2,1)S(1)} %get-tuple-element.71), channel_id=1, source_target_pairs={{0,1},{1,0},{2,3},{3,2},{4,5},{5,4},{6,7},{7,6},{8,9},{9,8},{10,11... | collective-permute-start | bytes 1572872 | tf_op jit(solution)/shard_map/ppermute | solution.py:498
  3.0 1.8 %keep.1 = (bf16[2,8,128,128]{3,2,1,0:T(8,128)(2,1)S(1)}, bf16[128,1024]{1,0:T(8,128)(2,1)S(1)}, bf16[128,1024]{1,0:T(8,128)(2,1)S(1)}, bf16[128,1024]{1,0:T(8,12...) custom-call(s32[8]{0:T(128)S(1)} %get-tuple-element.56.len_hbm, ...), custom_call_target="tpu_custom_call" | custom-call | flops 67108864 | bytes 4358176 | tf_op jit(solution)/shard_map/keep/pallas_call | solution.py:462
  4.9 0.2 pair.1
  5.1 3.6 %collective-permute-start.1 = (bf16[2,128,128]{2,1,0:T(8,128)(2,1)S(1)}, bf16[2,128,128]{2,1,0:T(8,128)(2,1)S(1)}, u32[]{:S(2)}, u32[]{:S(2)}) collective-permute-start(bf16[2,128,128]{2,1,0:T(8,128)(2,1)S(1)} %get-tuple-element.73), channel_id=1, source_target_pairs={{0,6},{1,7},{2,4},{3,5},{4,2},{5,3},{6,0},{7,1},{8,14},{9,15},{10,... | collective-permute-start | bytes 196616 | tf_op jit(solution)/shard_map/ppermute | solution.py:522
  8.7 0.3 collective-permute-start.2
  9.0 0.1 collective-permute-start.3
  9.1 2.8 %collective-permute-start.7 = (bf16[2,128,128]{2,1,0:T(8,128)(2,1)S(1)}, bf16[2,128,128]{2,1,0:T(8,128)(2,1)S(1)}, u32[]{:S(2)}, u32[]{:S(2)}) collective-permute-start(bf16[2,128,128]{2,1,0:T(8,128)(2,1)S(1)} %get-tuple-element.88), channel_id=1, source_target_pairs={{0,6},{1,7},{2,4},{3,5},{4,2},{5,3},{6,0},{7,1},{8,14},{9,15},{10,... | collective-permute-start | bytes 196616 | tf_op jit(solution)/shard_map/ppermute | solution.py:522
  11.9 0.5 %collective-permute-start.9 = (bf16[2,128,128]{2,1,0:T(8,128)(2,1)S(1)}, bf16[2,128,128]{2,1,0:T(8,128)(2,1)S(1)}, u32[]{:S(2)}, u32[]{:S(2)}) collective-permute-start(bf16[2,128,128]{2,1,0:T(8,128)(2,1)S(1)} %get-tuple-element.90), channel_id=1, source_target_pairs={{0,5},{1,4},{2,7},{3,6},{4,1},{5,0},{6,3},{7,2},{8,13},{9,12},{10,... | collective-permute-start | bytes 196616 | tf_op jit(solution)/shard_map/ppermute | solution.py:522
  12.4 0.4 %collective-permute-done.2.refs_2_.s2 = bf16[2,128,128]{2,1,0:T(8,128)(2,1)S(1)} collective-permute-done((bf16[2,128,128]{2,1,0:T(8,128)(2,1)S(1)}, bf16[2,128,128]{2,1,0:T(8,128)(2,1)S(1)}, u32[]{:S(2)}, u32[]{:S(2)}) %collective-permute-start.2) | collective-permute-done | bytes 65568 | tf_op jit(solution)/shard_map/ppermute | solution.py:522
  12.8 0.1 collective-permute-done.3.refs_3_.s3
  13.0 0.1 totals.1
  13.0 2.8 %collective-permute-start.10 = (bf16[2,128,128]{2,1,0:T(8,128)(2,1)S(1)}, bf16[2,128,128]{2,1,0:T(8,128)(2,1)S(1)}, u32[]{:S(2)}, u32[]{:S(2)}) collective-permute-start(bf16[2,128,128]{2,1,0:T(8,128)(2,1)S(1)} %totals.1), channel_id=1, source_target_pairs={{0,9},{1,8},{2,11},{3,10},{4,13},{5,12},{6,15},{7,14},{9,0},{8,1},... | collective-permute-start | bytes 196616 | tf_op jit(solution)/shard_map/ppermute | solution.py:544
  15.9 0.1 scan.2
  16.0 1.1 %collective-permute-start.4 = (bf16[2,128,128]{2,1,0:T(8,128)(2,1)S(1)}, bf16[2,128,128]{2,1,0:T(8,128)(2,1)S(1)}, u32[]{:S(2)}, u32[]{:S(2)}) collective-permute-start(bf16[2,128,128]{2,1,0:T(8,128)(2,1)S(1)} %get-tuple-element.77), channel_id=1, source_target_pairs={{0,3},{1,2},{2,1},{3,0},{4,7},{5,6},{6,5},{7,4},{8,11},{9,10},{10,... | collective-permute-start | bytes 196616 | tf_op jit(solution)/shard_map/ppermute | solution.py:522
  17.1 1.5 %collective-permute-start.5 = (bf16[2,128,128]{2,1,0:T(8,128)(2,1)S(1)}, bf16[2,128,128]{2,1,0:T(8,128)(2,1)S(1)}, u32[]{:S(2)}, u32[]{:S(2)}) collective-permute-start(bf16[2,128,128]{2,1,0:T(8,128)(2,1)S(1)} %get-tuple-element.78), channel_id=1, source_target_pairs={{0,6},{1,7},{2,4},{3,5},{4,2},{5,3},{6,0},{7,1},{8,14},{9,15},{10,... | collective-permute-start | bytes 196616 | tf_op jit(solution)/shard_map/ppermute | solution.py:522
  18.6 0.4 %collective-permute-start.6 = (bf16[2,128,128]{2,1,0:T(8,128)(2,1)S(1)}, bf16[2,128,128]{2,1,0:T(8,128)(2,1)S(1)}, u32[]{:S(2)}, u32[]{:S(2)}) collective-permute-start(bf16[2,128,128]{2,1,0:T(8,128)(2,1)S(1)} %get-tuple-element.79), channel_id=1, source_target_pairs={{0,5},{1,4},{2,7},{3,6},{4,1},{5,0},{6,3},{7,2},{8,13},{9,12},{10,... | collective-permute-start | bytes 196616 | tf_op jit(solution)/shard_map/ppermute | solution.py:522
  19.0 0.2 scan.3
  19.2 2.2 %collective-permute-start.11 = (bf16[2,128,128]{2,1,0:T(8,128)(2,1)S(1)}, bf16[2,128,128]{2,1,0:T(8,128)(2,1)S(1)}, u32[]{:S(2)}, u32[]{:S(2)}) collective-permute-start(bf16[2,128,128]{2,1,0:T(8,128)(2,1)S(1)} %get-tuple-element.92), channel_id=1, source_target_pairs={{0,6},{1,7},{2,4},{3,5},{4,2},{5,3},{6,0},{7,1},{8,14},{9,15},{10,... | collective-permute-start | bytes 196616 | tf_op jit(solution)/shard_map/ppermute | solution.py:522
  21.4 0.4 %collective-permute-start.12 = (bf16[2,128,128]{2,1,0:T(8,128)(2,1)S(1)}, bf16[2,128,128]{2,1,0:T(8,128)(2,1)S(1)}, u32[]{:S(2)}, u32[]{:S(2)}) collective-permute-start(bf16[2,128,128]{2,1,0:T(8,128)(2,1)S(1)} %get-tuple-element.93), channel_id=1, source_target_pairs={{0,3},{1,2},{2,1},{3,0},{4,7},{5,6},{6,5},{7,4},{8,11},{9,10},{10,... | collective-permute-start | bytes 196616 | tf_op jit(solution)/shard_map/ppermute | solution.py:522
  21.8 0.7 %collective-permute-start.13 = (bf16[2,128,128]{2,1,0:T(8,128)(2,1)S(1)}, bf16[2,128,128]{2,1,0:T(8,128)(2,1)S(1)}, u32[]{:S(2)}, u32[]{:S(2)}) collective-permute-start(bf16[2,128,128]{2,1,0:T(8,128)(2,1)S(1)} %get-tuple-element.94), channel_id=1, source_target_pairs={{0,5},{1,4},{2,7},{3,6},{4,1},{5,0},{6,3},{7,2},{8,13},{9,12},{10,... | collective-permute-start | bytes 196616 | tf_op jit(solution)/shard_map/ppermute | solution.py:522
  22.5 0.5 %collective-permute-done.5.refs_2_ = bf16[2,128,128]{2,1,0:T(8,128)(2,1)S(1)} collective-permute-done((bf16[2,128,128]{2,1,0:T(8,128)(2,1)S(1)}, bf16[2,128,128]{2,1,0:T(8,128)(2,1)S(1)}, u32[]{:S(2)}, u32[]{:S(2)}) %collective-permute-start.5) | collective-permute-done | bytes 65568 | tf_op jit(solution)/shard_map/ppermute | solution.py:522
  23.0 0.2 post.2
  23.2 0.2 collective-permute-start.15
  23.4 1.8 %local.1 = (bf16[16,128,128]{2,1,0:T(8,128)(2,1)S(1)}, bf16[16,128,128]{2,1,0:T(8,128)(2,1)S(1)}, bf16[16,128,128]{2,1,0:T(8,128)(2,1)S(1)}, bf16[16,128,128]{2,...) custom-call(s32[8]{0:T(128)S(1)} %get-tuple-element.56.len_hbm, ...), custom_call_target="tpu_custom_call" | custom-call | flops 134217728 | bytes 6160416 | tf_op jit(solution)/shard_map/local/pallas_call | solution.py:462
  25.2 0.5 %collective-permute-done.11.refs_1_ = bf16[2,128,128]{2,1,0:T(8,128)(2,1)S(1)} collective-permute-done((bf16[2,128,128]{2,1,0:T(8,128)(2,1)S(1)}, bf16[2,128,128]{2,1,0:T(8,128)(2,1)S(1)}, u32[]{:S(2)}, u32[]{:S(2)}) %collective-permute-start.11) | collective-permute-done | bytes 65568 | tf_op jit(solution)/shard_map/ppermute | solution.py:522
  25.7 1.3 %collective-permute-done.12.refs_2_ = bf16[2,128,128]{2,1,0:T(8,128)(2,1)S(1)} collective-permute-done((bf16[2,128,128]{2,1,0:T(8,128)(2,1)S(1)}, bf16[2,128,128]{2,1,0:T(8,128)(2,1)S(1)}, u32[]{:S(2)}, u32[]{:S(2)}) %collective-permute-start.12) | collective-permute-done | bytes 65568 | tf_op jit(solution)/shard_map/ppermute | solution.py:522
  27.0 0.2 post.3
  27.2 0.2 collective-permute-start.14
  27.4 1.3 %middle.1 = (bf16[128,2048]{1,0:T(8,128)(2,1)}, bf16[128,2048]{1,0:T(8,128)(2,1)}, bf16[128,2048]{1,0:T(8,128)(2,1)}, bf16[128,2048]{1,0:T(8,128)(2,1)}, bf16[12...) custom-call(bf16[128,1024]{1,0:T(8,128)(2,1)S(1)} %get-tuple-element.98.refs_0_, ...), custom_call_target="tpu_custom_call" | custom-call | flops 268435456 | bytes 9043968 | tf_op jit(solution)/shard_map/middle/pallas_call | solution.py:462
  28.7 0.1 collective-permute-done.14.refs_13_
  28.8 1.2 %last.1 = (bf16[128,2048]{1,0:T(8,128)(2,1)}, bf16[128,2048]{1,0:T(8,128)(2,1)}, bf16[128,2048]{1,0:T(8,128)(2,1)}, bf16[128,2048]{1,0:T(8,128)(2,1)}) custom-call(bf16[128,1024]{1,0:T(8,128)(2,1)S(1)} %get-tuple-element.59.refs_0_.refs_2_, ...), custom_call_target="tpu_custom_call", output_to_operand_aliasing={{0}: (18, {}), {1}: (19, {}), {2}: (20, {}), {3}: (21, {})} | custom-call | flops 134217728 | bytes 9830400 | tf_op jit(solution)/shard_map/last/pallas_call | solution.py:462
  (11 shorter events, 0.0 us)
Async XLA Ops:
  2.5 2.4 %collective-permute-start = (bf16[2,8,128,128]{3,2,1,0:T(8,128)(2,1)S(1)}, bf16[2,8,128,128]{3,2,1,0:T(8,128)(2,1)S(1)}, u32[]{:S(2)}, u32[]{:S(2)}) collective-permute-start(bf16[2,8,128,128]{3,2,1,0:T(8,128)(2,1)S(1)} %get-tuple-element.71), channel_id=1, source_target_pairs={{0,1},{1,0},{2,3},{3,2},{4,5},{5,4},{6,7},{7,6},{8,9},{9,8},{10,11... | collective-permute-start | bytes 1572872 | tf_op jit(solution)/shard_map/ppermute | solution.py:498
  5.1 6.9 %collective-permute-start.1 = (bf16[2,128,128]{2,1,0:T(8,128)(2,1)S(1)}, bf16[2,128,128]{2,1,0:T(8,128)(2,1)S(1)}, u32[]{:S(2)}, u32[]{:S(2)}) collective-permute-start(bf16[2,128,128]{2,1,0:T(8,128)(2,1)S(1)} %get-tuple-element.73), channel_id=1, source_target_pairs={{0,6},{1,7},{2,4},{3,5},{4,2},{5,3},{6,0},{7,1},{8,14},{9,15},{10,... | collective-permute-start | bytes 196616 | tf_op jit(solution)/shard_map/ppermute | solution.py:522
  8.7 4.1 %collective-permute-start.2 = (bf16[2,128,128]{2,1,0:T(8,128)(2,1)S(1)}, bf16[2,128,128]{2,1,0:T(8,128)(2,1)S(1)}, u32[]{:S(2)}, u32[]{:S(2)}) collective-permute-start(bf16[2,128,128]{2,1,0:T(8,128)(2,1)S(1)} %get-tuple-element.74), channel_id=1, source_target_pairs={{0,3},{1,2},{2,1},{3,0},{4,7},{5,6},{6,5},{7,4},{8,11},{9,10},{10,... | collective-permute-start | bytes 196616 | tf_op jit(solution)/shard_map/ppermute | solution.py:522
  9.0 4.0 %collective-permute-start.3 = (bf16[2,128,128]{2,1,0:T(8,128)(2,1)S(1)}, bf16[2,128,128]{2,1,0:T(8,128)(2,1)S(1)}, u32[]{:S(2)}, u32[]{:S(2)}) collective-permute-start(bf16[2,128,128]{2,1,0:T(8,128)(2,1)S(1)} %get-tuple-element.75), channel_id=1, source_target_pairs={{0,5},{1,4},{2,7},{3,6},{4,1},{5,0},{6,3},{7,2},{8,13},{9,12},{10,... | collective-permute-start | bytes 196616 | tf_op jit(solution)/shard_map/ppermute | solution.py:522
  9.1 8.0 %collective-permute-start.7 = (bf16[2,128,128]{2,1,0:T(8,128)(2,1)S(1)}, bf16[2,128,128]{2,1,0:T(8,128)(2,1)S(1)}, u32[]{:S(2)}, u32[]{:S(2)}) collective-permute-start(bf16[2,128,128]{2,1,0:T(8,128)(2,1)S(1)} %get-tuple-element.88), channel_id=1, source_target_pairs={{0,6},{1,7},{2,4},{3,5},{4,2},{5,3},{6,0},{7,1},{8,14},{9,15},{10,... | collective-permute-start | bytes 196616 | tf_op jit(solution)/shard_map/ppermute | solution.py:522
  11.9 6.7 %collective-permute-start.8 = (bf16[2,128,128]{2,1,0:T(8,128)(2,1)S(1)}, bf16[2,128,128]{2,1,0:T(8,128)(2,1)S(1)}, u32[]{:S(2)}, u32[]{:S(2)}) collective-permute-start(bf16[2,128,128]{2,1,0:T(8,128)(2,1)S(1)} %get-tuple-element.89), channel_id=1, source_target_pairs={{0,3},{1,2},{2,1},{3,0},{4,7},{5,6},{6,5},{7,4},{8,11},{9,10},{10,... | collective-permute-start | bytes 196616 | tf_op jit(solution)/shard_map/ppermute | solution.py:522
  11.9 7.1 %collective-permute-start.9 = (bf16[2,128,128]{2,1,0:T(8,128)(2,1)S(1)}, bf16[2,128,128]{2,1,0:T(8,128)(2,1)S(1)}, u32[]{:S(2)}, u32[]{:S(2)}) collective-permute-start(bf16[2,128,128]{2,1,0:T(8,128)(2,1)S(1)} %get-tuple-element.90), channel_id=1, source_target_pairs={{0,5},{1,4},{2,7},{3,6},{4,1},{5,0},{6,3},{7,2},{8,13},{9,12},{10,... | collective-permute-start | bytes 196616 | tf_op jit(solution)/shard_map/ppermute | solution.py:522
  13.0 6.0 %collective-permute-start.10 = (bf16[2,128,128]{2,1,0:T(8,128)(2,1)S(1)}, bf16[2,128,128]{2,1,0:T(8,128)(2,1)S(1)}, u32[]{:S(2)}, u32[]{:S(2)}) collective-permute-start(bf16[2,128,128]{2,1,0:T(8,128)(2,1)S(1)} %totals.1), channel_id=1, source_target_pairs={{0,9},{1,8},{2,11},{3,10},{4,13},{5,12},{6,15},{7,14},{9,0},{8,1},... | collective-permute-start | bytes 196616 | tf_op jit(solution)/shard_map/ppermute | solution.py:544
  16.0 5.8 %collective-permute-start.4 = (bf16[2,128,128]{2,1,0:T(8,128)(2,1)S(1)}, bf16[2,128,128]{2,1,0:T(8,128)(2,1)S(1)}, u32[]{:S(2)}, u32[]{:S(2)}) collective-permute-start(bf16[2,128,128]{2,1,0:T(8,128)(2,1)S(1)} %get-tuple-element.77), channel_id=1, source_target_pairs={{0,3},{1,2},{2,1},{3,0},{4,7},{5,6},{6,5},{7,4},{8,11},{9,10},{10,... | collective-permute-start | bytes 196616 | tf_op jit(solution)/shard_map/ppermute | solution.py:522
  17.1 5.9 %collective-permute-start.5 = (bf16[2,128,128]{2,1,0:T(8,128)(2,1)S(1)}, bf16[2,128,128]{2,1,0:T(8,128)(2,1)S(1)}, u32[]{:S(2)}, u32[]{:S(2)}) collective-permute-start(bf16[2,128,128]{2,1,0:T(8,128)(2,1)S(1)} %get-tuple-element.78), channel_id=1, source_target_pairs={{0,6},{1,7},{2,4},{3,5},{4,2},{5,3},{6,0},{7,1},{8,14},{9,15},{10,... | collective-permute-start | bytes 196616 | tf_op jit(solution)/shard_map/ppermute | solution.py:522
  18.6 4.4 %collective-permute-start.6 = (bf16[2,128,128]{2,1,0:T(8,128)(2,1)S(1)}, bf16[2,128,128]{2,1,0:T(8,128)(2,1)S(1)}, u32[]{:S(2)}, u32[]{:S(2)}) collective-permute-start(bf16[2,128,128]{2,1,0:T(8,128)(2,1)S(1)} %get-tuple-element.79), channel_id=1, source_target_pairs={{0,5},{1,4},{2,7},{3,6},{4,1},{5,0},{6,3},{7,2},{8,13},{9,12},{10,... | collective-permute-start | bytes 196616 | tf_op jit(solution)/shard_map/ppermute | solution.py:522
  19.2 6.5 %collective-permute-start.11 = (bf16[2,128,128]{2,1,0:T(8,128)(2,1)S(1)}, bf16[2,128,128]{2,1,0:T(8,128)(2,1)S(1)}, u32[]{:S(2)}, u32[]{:S(2)}) collective-permute-start(bf16[2,128,128]{2,1,0:T(8,128)(2,1)S(1)} %get-tuple-element.92), channel_id=1, source_target_pairs={{0,6},{1,7},{2,4},{3,5},{4,2},{5,3},{6,0},{7,1},{8,14},{9,15},{10,... | collective-permute-start | bytes 196616 | tf_op jit(solution)/shard_map/ppermute | solution.py:522
  21.4 5.6 %collective-permute-start.12 = (bf16[2,128,128]{2,1,0:T(8,128)(2,1)S(1)}, bf16[2,128,128]{2,1,0:T(8,128)(2,1)S(1)}, u32[]{:S(2)}, u32[]{:S(2)}) collective-permute-start(bf16[2,128,128]{2,1,0:T(8,128)(2,1)S(1)} %get-tuple-element.93), channel_id=1, source_target_pairs={{0,3},{1,2},{2,1},{3,0},{4,7},{5,6},{6,5},{7,4},{8,11},{9,10},{10,... | collective-permute-start | bytes 196616 | tf_op jit(solution)/shard_map/ppermute | solution.py:522
  21.8 5.2 %collective-permute-start.13 = (bf16[2,128,128]{2,1,0:T(8,128)(2,1)S(1)}, bf16[2,128,128]{2,1,0:T(8,128)(2,1)S(1)}, u32[]{:S(2)}, u32[]{:S(2)}) collective-permute-start(bf16[2,128,128]{2,1,0:T(8,128)(2,1)S(1)} %get-tuple-element.94), channel_id=1, source_target_pairs={{0,5},{1,4},{2,7},{3,6},{4,1},{5,0},{6,3},{7,2},{8,13},{9,12},{10,... | collective-permute-start | bytes 196616 | tf_op jit(solution)/shard_map/ppermute | solution.py:522
  23.2 4.2 %collective-permute-start.15 = (bf16[8,128,128]{2,1,0:T(8,128)(2,1)S(1)}, bf16[8,128,128]{2,1,0:T(8,128)(2,1)S(1)}, u32[]{:S(2)}, u32[]{:S(2)}) collective-permute-start(bf16[8,128,128]{2,1,0:T(8,128)(2,1)S(1)} %get-tuple-element.100), channel_id=1, source_target_pairs={{0,1},{1,0},{2,3},{3,2},{4,5},{5,4},{6,7},{7,6},{8,9},{9,8},{10,11... | collective-permute-start | bytes 786440 | tf_op jit(solution)/shard_map/ppermute | solution.py:558
  27.2 1.6 %collective-permute-start.14 = (bf16[8,128,128]{2,1,0:T(8,128)(2,1)S(1)}, bf16[8,128,128]{2,1,0:T(8,128)(2,1)S(1)}, u32[]{:S(2)}, u32[]{:S(2)}) collective-permute-start(bf16[8,128,128]{2,1,0:T(8,128)(2,1)S(1)} %get-tuple-element.95), channel_id=1, source_target_pairs={{0,1},{1,0},{2,3},{3,2},{4,5},{5,4},{6,7},{7,6},{8,9},{9,8},{10,11... | collective-permute-start | bytes 786440 | tf_op jit(solution)/shard_map/ppermute | solution.py:558

commit v18 on v17

--- a/solution.py
+++ b/solution.py
@@ -11,7 +11,7 @@
 PAIRS = 4
 PARTNERS = (0, 3, 1, 2)
 STEPS = (0, 6, 3, 5)
-EARLY_BACK = (0, 2, 1, 3)
+EARLY_BACK = (0, 1, 2, 3)
 TEAM = 2 * PAIRS
 F32 = jnp.float32
 BF16 = jnp.bfloat16

time: 30.1 us -> 29.1 us (0.967)
  waiting for transfers between devices: 2.95 us -> 1.63 us
    ppermute x12, waiting for transfers between devices: 2.87 us -> 1.59 us  [trade(): lax.ppermute(parts[d], 'seq', [(i, i ^ STEPS[d]) for i in range(n)])]
    ppermute x12, starting transfers between devices: 13.6 us -> 13.9 us  [trade(): lax.ppermute(parts[d], 'seq', [(i, i ^ STEPS[d]) for i in range(n)])]
  transfers between devices with their start and end apart: 16 -> 16, of which waited for: 6 -> 3; matrix products, arithmetic and copies ran while one was open for 0% -> 0% of each run, Pallas kernels for 19% -> 20%
where the time goes in v18:
time: 29.1 us; the launch traced here: 29 us
  starting transfers between devices  17.6 us (60%)
  Pallas kernels  8.98 us (31%)
  waiting for transfers between devices  1.63 us (6%)
  between operations  0.72 us (2%)
    ppermute x12, starting transfers between devices, trade(): lax.ppermute(parts[d], 'seq', [(i, i ^ STEPS[d]) for i in range(n)])  13.9 us
    pallas_call x11, Pallas kernels, call(): pl.pallas_call(kernel, in_specs=specs, out_specs=out_specs or [vmem] * le...  8.98 us
    ppermute x1, starting transfers between devices, per_device(): enter = lax.ppermute(edge(0), 'seq', up + down)  2.85 us
    ppermute x12, waiting for transfers between devices, trade(): lax.ppermute(parts[d], 'seq', [(i, i ^ STEPS[d]) for i in range(n)])  1.59 us
  transfers between devices with their start and end apart: 16, of which 3 were waited for; matrix products, arithmetic and copies ran while one was open for 0% of the time, Pallas kernels for 20%

profile of v18, /device:TPU:0, one launch (start us, length us, event | category | flops | bytes accessed | tf_op | source)
XLA Modules:
  0.0 29.0 jit_solution(5367401783569139882)
XLA Ops:
  0.6 1.9 %send.1 = (s32[8]{0:T(128)S(1)}, bf16[2,8,128,128]{3,2,1,0:T(8,128)(2,1)S(1)}, bf16[128,1024]{1,0:T(8,128)(2,1)S(1)}, bf16[128,1024]{1,0:T(8,128)(2,1)S(1)}, bf1...) custom-call(s32[8]{0:T(128)} %len_hbm.1, ...), custom_call_target="tpu_custom_call" | custom-call | flops 67108864 | bytes 4325440 | tf_op jit(solution)/shard_map/send/pallas_call | solution.py:462
  2.5 0.5 %collective-permute-start = (bf16[2,8,128,128]{3,2,1,0:T(8,128)(2,1)S(1)}, bf16[2,8,128,128]{3,2,1,0:T(8,128)(2,1)S(1)}, u32[]{:S(2)}, u32[]{:S(2)}) collective-permute-start(bf16[2,8,128,128]{3,2,1,0:T(8,128)(2,1)S(1)} %get-tuple-element.71), channel_id=1, source_target_pairs={{0,1},{1,0},{2,3},{3,2},{4,5},{5,4},{6,7},{7,6},{8,9},{9,8},{10,11... | collective-permute-start | bytes 1572872 | tf_op jit(solution)/shard_map/ppermute | solution.py:498
  3.0 1.8 %keep.1 = (bf16[2,8,128,128]{3,2,1,0:T(8,128)(2,1)S(1)}, bf16[128,1024]{1,0:T(8,128)(2,1)S(1)}, bf16[128,1024]{1,0:T(8,128)(2,1)S(1)}, bf16[128,1024]{1,0:T(8,12...) custom-call(s32[8]{0:T(128)S(1)} %get-tuple-element.56.len_hbm, ...), custom_call_target="tpu_custom_call" | custom-call | flops 67108864 | bytes 4358176 | tf_op jit(solution)/shard_map/keep/pallas_call | solution.py:462
  4.9 0.2 pair.1
  5.1 3.6 %collective-permute-start.1 = (bf16[2,128,128]{2,1,0:T(8,128)(2,1)S(1)}, bf16[2,128,128]{2,1,0:T(8,128)(2,1)S(1)}, u32[]{:S(2)}, u32[]{:S(2)}) collective-permute-start(bf16[2,128,128]{2,1,0:T(8,128)(2,1)S(1)} %get-tuple-element.73), channel_id=1, source_target_pairs={{0,6},{1,7},{2,4},{3,5},{4,2},{5,3},{6,0},{7,1},{8,14},{9,15},{10,... | collective-permute-start | bytes 196616 | tf_op jit(solution)/shard_map/ppermute | solution.py:522
  8.7 0.3 %collective-permute-start.2 = (bf16[2,128,128]{2,1,0:T(8,128)(2,1)S(1)}, bf16[2,128,128]{2,1,0:T(8,128)(2,1)S(1)}, u32[]{:S(2)}, u32[]{:S(2)}) collective-permute-start(bf16[2,128,128]{2,1,0:T(8,128)(2,1)S(1)} %get-tuple-element.74), channel_id=1, source_target_pairs={{0,3},{1,2},{2,1},{3,0},{4,7},{5,6},{6,5},{7,4},{8,11},{9,10},{10,... | collective-permute-start | bytes 196616 | tf_op jit(solution)/shard_map/ppermute | solution.py:522
  9.0 0.1 collective-permute-start.3
  9.1 2.8 %collective-permute-start.7 = (bf16[2,128,128]{2,1,0:T(8,128)(2,1)S(1)}, bf16[2,128,128]{2,1,0:T(8,128)(2,1)S(1)}, u32[]{:S(2)}, u32[]{:S(2)}) collective-permute-start(bf16[2,128,128]{2,1,0:T(8,128)(2,1)S(1)} %get-tuple-element.88), channel_id=1, source_target_pairs={{0,6},{1,7},{2,4},{3,5},{4,2},{5,3},{6,0},{7,1},{8,14},{9,15},{10,... | collective-permute-start | bytes 196616 | tf_op jit(solution)/shard_map/ppermute | solution.py:522
  11.9 0.0 collective-permute-start.8
  11.9 0.5 %collective-permute-start.9 = (bf16[2,128,128]{2,1,0:T(8,128)(2,1)S(1)}, bf16[2,128,128]{2,1,0:T(8,128)(2,1)S(1)}, u32[]{:S(2)}, u32[]{:S(2)}) collective-permute-start(bf16[2,128,128]{2,1,0:T(8,128)(2,1)S(1)} %get-tuple-element.90), channel_id=1, source_target_pairs={{0,5},{1,4},{2,7},{3,6},{4,1},{5,0},{6,3},{7,2},{8,13},{9,12},{10,... | collective-permute-start | bytes 196616 | tf_op jit(solution)/shard_map/ppermute | solution.py:522
  12.4 0.4 %collective-permute-done.2.refs_2_.s2 = bf16[2,128,128]{2,1,0:T(8,128)(2,1)S(1)} collective-permute-done((bf16[2,128,128]{2,1,0:T(8,128)(2,1)S(1)}, bf16[2,128,128]{2,1,0:T(8,128)(2,1)S(1)}, u32[]{:S(2)}, u32[]{:S(2)}) %collective-permute-start.2) | collective-permute-done | bytes 65568 | tf_op jit(solution)/shard_map/ppermute | solution.py:522
  12.8 0.1 collective-permute-done.3.refs_3_.s3
  13.0 0.1 totals.1
  13.0 2.8 %collective-permute-start.10 = (bf16[2,128,128]{2,1,0:T(8,128)(2,1)S(1)}, bf16[2,128,128]{2,1,0:T(8,128)(2,1)S(1)}, u32[]{:S(2)}, u32[]{:S(2)}) collective-permute-start(bf16[2,128,128]{2,1,0:T(8,128)(2,1)S(1)} %totals.1), channel_id=1, source_target_pairs={{0,9},{1,8},{2,11},{3,10},{4,13},{5,12},{6,15},{7,14},{9,0},{8,1},... | collective-permute-start | bytes 196616 | tf_op jit(solution)/shard_map/ppermute | solution.py:544
  15.9 0.1 scan.2
  16.0 1.6 %collective-permute-start.4 = (bf16[2,128,128]{2,1,0:T(8,128)(2,1)S(1)}, bf16[2,128,128]{2,1,0:T(8,128)(2,1)S(1)}, u32[]{:S(2)}, u32[]{:S(2)}) collective-permute-start(bf16[2,128,128]{2,1,0:T(8,128)(2,1)S(1)} %get-tuple-element.77), channel_id=1, source_target_pairs={{0,6},{1,7},{2,4},{3,5},{4,2},{5,3},{6,0},{7,1},{8,14},{9,15},{10,... | collective-permute-start | bytes 196616 | tf_op jit(solution)/shard_map/ppermute | solution.py:522
  17.6 0.8 %collective-permute-start.5 = (bf16[2,128,128]{2,1,0:T(8,128)(2,1)S(1)}, bf16[2,128,128]{2,1,0:T(8,128)(2,1)S(1)}, u32[]{:S(2)}, u32[]{:S(2)}) collective-permute-start(bf16[2,128,128]{2,1,0:T(8,128)(2,1)S(1)} %get-tuple-element.78), channel_id=1, source_target_pairs={{0,3},{1,2},{2,1},{3,0},{4,7},{5,6},{6,5},{7,4},{8,11},{9,10},{10,... | collective-permute-start | bytes 196616 | tf_op jit(solution)/shard_map/ppermute | solution.py:522
  18.3 1.0 %collective-permute-start.6 = (bf16[2,128,128]{2,1,0:T(8,128)(2,1)S(1)}, bf16[2,128,128]{2,1,0:T(8,128)(2,1)S(1)}, u32[]{:S(2)}, u32[]{:S(2)}) collective-permute-start(bf16[2,128,128]{2,1,0:T(8,128)(2,1)S(1)} %get-tuple-element.79), channel_id=1, source_target_pairs={{0,5},{1,4},{2,7},{3,6},{4,1},{5,0},{6,3},{7,2},{8,13},{9,12},{10,... | collective-permute-start | bytes 196616 | tf_op jit(solution)/shard_map/ppermute | solution.py:522
  19.3 0.2 scan.3
  19.5 1.9 %collective-permute-start.11 = (bf16[2,128,128]{2,1,0:T(8,128)(2,1)S(1)}, bf16[2,128,128]{2,1,0:T(8,128)(2,1)S(1)}, u32[]{:S(2)}, u32[]{:S(2)}) collective-permute-start(bf16[2,128,128]{2,1,0:T(8,128)(2,1)S(1)} %get-tuple-element.92), channel_id=1, source_target_pairs={{0,6},{1,7},{2,4},{3,5},{4,2},{5,3},{6,0},{7,1},{8,14},{9,15},{10,... | collective-permute-start | bytes 196616 | tf_op jit(solution)/shard_map/ppermute | solution.py:522
  21.4 0.2 collective-permute-start.12
  21.6 0.0 collective-permute-done.4.refs_1_
  21.6 1.2 %collective-permute-start.13 = (bf16[2,128,128]{2,1,0:T(8,128)(2,1)S(1)}, bf16[2,128,128]{2,1,0:T(8,128)(2,1)S(1)}, u32[]{:S(2)}, u32[]{:S(2)}) collective-permute-start(bf16[2,128,128]{2,1,0:T(8,128)(2,1)S(1)} %get-tuple-element.94), channel_id=1, source_target_pairs={{0,5},{1,4},{2,7},{3,6},{4,1},{5,0},{6,3},{7,2},{8,13},{9,12},{10,... | collective-permute-start | bytes 196616 | tf_op jit(solution)/shard_map/ppermute | solution.py:522
  22.8 0.2 post.2
  23.0 0.1 collective-permute-start.15
  23.2 1.8 %local.1 = (bf16[16,128,128]{2,1,0:T(8,128)(2,1)S(1)}, bf16[16,128,128]{2,1,0:T(8,128)(2,1)S(1)}, bf16[16,128,128]{2,1,0:T(8,128)(2,1)S(1)}, bf16[16,128,128]{2,...) custom-call(s32[8]{0:T(128)S(1)} %get-tuple-element.56.len_hbm, ...), custom_call_target="tpu_custom_call" | custom-call | flops 134217728 | bytes 6160416 | tf_op jit(solution)/shard_map/local/pallas_call | solution.py:462
  25.0 1.0 %collective-permute-done.12.refs_2_ = bf16[2,128,128]{2,1,0:T(8,128)(2,1)S(1)} collective-permute-done((bf16[2,128,128]{2,1,0:T(8,128)(2,1)S(1)}, bf16[2,128,128]{2,1,0:T(8,128)(2,1)S(1)}, u32[]{:S(2)}, u32[]{:S(2)}) %collective-permute-start.12) | collective-permute-done | bytes 65568 | tf_op jit(solution)/shard_map/ppermute | solution.py:522
  26.0 0.2 post.3
  26.2 0.2 collective-permute-start.14
  26.4 1.3 %middle.1 = (bf16[128,2048]{1,0:T(8,128)(2,1)}, bf16[128,2048]{1,0:T(8,128)(2,1)}, bf16[128,2048]{1,0:T(8,128)(2,1)}, bf16[128,2048]{1,0:T(8,128)(2,1)}, bf16[12...) custom-call(bf16[128,1024]{1,0:T(8,128)(2,1)S(1)} %get-tuple-element.98.refs_0_, ...), custom_call_target="tpu_custom_call" | custom-call | flops 268435456 | bytes 9043968 | tf_op jit(solution)/shard_map/middle/pallas_call | solution.py:462
  27.8 0.0 collective-permute-done.14.refs_13_
  27.8 1.2 %last.1 = (bf16[128,2048]{1,0:T(8,128)(2,1)}, bf16[128,2048]{1,0:T(8,128)(2,1)}, bf16[128,2048]{1,0:T(8,128)(2,1)}, bf16[128,2048]{1,0:T(8,128)(2,1)}) custom-call(bf16[128,1024]{1,0:T(8,128)(2,1)S(1)} %get-tuple-element.59.refs_0_.refs_2_, ...), custom_call_target="tpu_custom_call", output_to_operand_aliasing={{0}: (18, {}), {1}: (19, {}), {2}: (20, {}), {3}: (21, {})} | custom-call | flops 134217728 | bytes 9830400 | tf_op jit(solution)/shard_map/last/pallas_call | solution.py:462
  (11 shorter events, 0.0 us)
Async XLA Ops:
  2.5 2.4 %collective-permute-start = (bf16[2,8,128,128]{3,2,1,0:T(8,128)(2,1)S(1)}, bf16[2,8,128,128]{3,2,1,0:T(8,128)(2,1)S(1)}, u32[]{:S(2)}, u32[]{:S(2)}) collective-permute-start(bf16[2,8,128,128]{3,2,1,0:T(8,128)(2,1)S(1)} %get-tuple-element.71), channel_id=1, source_target_pairs={{0,1},{1,0},{2,3},{3,2},{4,5},{5,4},{6,7},{7,6},{8,9},{9,8},{10,11... | collective-permute-start | bytes 1572872 | tf_op jit(solution)/shard_map/ppermute | solution.py:498
  5.1 6.9 %collective-permute-start.1 = (bf16[2,128,128]{2,1,0:T(8,128)(2,1)S(1)}, bf16[2,128,128]{2,1,0:T(8,128)(2,1)S(1)}, u32[]{:S(2)}, u32[]{:S(2)}) collective-permute-start(bf16[2,128,128]{2,1,0:T(8,128)(2,1)S(1)} %get-tuple-element.73), channel_id=1, source_target_pairs={{0,6},{1,7},{2,4},{3,5},{4,2},{5,3},{6,0},{7,1},{8,14},{9,15},{10,... | collective-permute-start | bytes 196616 | tf_op jit(solution)/shard_map/ppermute | solution.py:522
  8.7 4.1 %collective-permute-start.2 = (bf16[2,128,128]{2,1,0:T(8,128)(2,1)S(1)}, bf16[2,128,128]{2,1,0:T(8,128)(2,1)S(1)}, u32[]{:S(2)}, u32[]{:S(2)}) collective-permute-start(bf16[2,128,128]{2,1,0:T(8,128)(2,1)S(1)} %get-tuple-element.74), channel_id=1, source_target_pairs={{0,3},{1,2},{2,1},{3,0},{4,7},{5,6},{6,5},{7,4},{8,11},{9,10},{10,... | collective-permute-start | bytes 196616 | tf_op jit(solution)/shard_map/ppermute | solution.py:522
  9.0 4.0 %collective-permute-start.3 = (bf16[2,128,128]{2,1,0:T(8,128)(2,1)S(1)}, bf16[2,128,128]{2,1,0:T(8,128)(2,1)S(1)}, u32[]{:S(2)}, u32[]{:S(2)}) collective-permute-start(bf16[2,128,128]{2,1,0:T(8,128)(2,1)S(1)} %get-tuple-element.75), channel_id=1, source_target_pairs={{0,5},{1,4},{2,7},{3,6},{4,1},{5,0},{6,3},{7,2},{8,13},{9,12},{10,... | collective-permute-start | bytes 196616 | tf_op jit(solution)/shard_map/ppermute | solution.py:522
  9.1 8.5 %collective-permute-start.7 = (bf16[2,128,128]{2,1,0:T(8,128)(2,1)S(1)}, bf16[2,128,128]{2,1,0:T(8,128)(2,1)S(1)}, u32[]{:S(2)}, u32[]{:S(2)}) collective-permute-start(bf16[2,128,128]{2,1,0:T(8,128)(2,1)S(1)} %get-tuple-element.88), channel_id=1, source_target_pairs={{0,6},{1,7},{2,4},{3,5},{4,2},{5,3},{6,0},{7,1},{8,14},{9,15},{10,... | collective-permute-start | bytes 196616 | tf_op jit(solution)/shard_map/ppermute | solution.py:522
  11.9 6.4 %collective-permute-start.8 = (bf16[2,128,128]{2,1,0:T(8,128)(2,1)S(1)}, bf16[2,128,128]{2,1,0:T(8,128)(2,1)S(1)}, u32[]{:S(2)}, u32[]{:S(2)}) collective-permute-start(bf16[2,128,128]{2,1,0:T(8,128)(2,1)S(1)} %get-tuple-element.89), channel_id=1, source_target_pairs={{0,3},{1,2},{2,1},{3,0},{4,7},{5,6},{6,5},{7,4},{8,11},{9,10},{10,... | collective-permute-start | bytes 196616 | tf_op jit(solution)/shard_map/ppermute | solution.py:522
  11.9 7.4 %collective-permute-start.9 = (bf16[2,128,128]{2,1,0:T(8,128)(2,1)S(1)}, bf16[2,128,128]{2,1,0:T(8,128)(2,1)S(1)}, u32[]{:S(2)}, u32[]{:S(2)}) collective-permute-start(bf16[2,128,128]{2,1,0:T(8,128)(2,1)S(1)} %get-tuple-element.90), channel_id=1, source_target_pairs={{0,5},{1,4},{2,7},{3,6},{4,1},{5,0},{6,3},{7,2},{8,13},{9,12},{10,... | collective-permute-start | bytes 196616 | tf_op jit(solution)/shard_map/ppermute | solution.py:522
  13.0 6.3 %collective-permute-start.10 = (bf16[2,128,128]{2,1,0:T(8,128)(2,1)S(1)}, bf16[2,128,128]{2,1,0:T(8,128)(2,1)S(1)}, u32[]{:S(2)}, u32[]{:S(2)}) collective-permute-start(bf16[2,128,128]{2,1,0:T(8,128)(2,1)S(1)} %totals.1), channel_id=1, source_target_pairs={{0,9},{1,8},{2,11},{3,10},{4,13},{5,12},{6,15},{7,14},{9,0},{8,1},... | collective-permute-start | bytes 196616 | tf_op jit(solution)/shard_map/ppermute | solution.py:544
  16.0 5.6 %collective-permute-start.4 = (bf16[2,128,128]{2,1,0:T(8,128)(2,1)S(1)}, bf16[2,128,128]{2,1,0:T(8,128)(2,1)S(1)}, u32[]{:S(2)}, u32[]{:S(2)}) collective-permute-start(bf16[2,128,128]{2,1,0:T(8,128)(2,1)S(1)} %get-tuple-element.77), channel_id=1, source_target_pairs={{0,6},{1,7},{2,4},{3,5},{4,2},{5,3},{6,0},{7,1},{8,14},{9,15},{10,... | collective-permute-start | bytes 196616 | tf_op jit(solution)/shard_map/ppermute | solution.py:522
  17.6 5.2 %collective-permute-start.5 = (bf16[2,128,128]{2,1,0:T(8,128)(2,1)S(1)}, bf16[2,128,128]{2,1,0:T(8,128)(2,1)S(1)}, u32[]{:S(2)}, u32[]{:S(2)}) collective-permute-start(bf16[2,128,128]{2,1,0:T(8,128)(2,1)S(1)} %get-tuple-element.78), channel_id=1, source_target_pairs={{0,3},{1,2},{2,1},{3,0},{4,7},{5,6},{6,5},{7,4},{8,11},{9,10},{10,... | collective-permute-start | bytes 196616 | tf_op jit(solution)/shard_map/ppermute | solution.py:522
  18.3 4.4 %collective-permute-start.6 = (bf16[2,128,128]{2,1,0:T(8,128)(2,1)S(1)}, bf16[2,128,128]{2,1,0:T(8,128)(2,1)S(1)}, u32[]{:S(2)}, u32[]{:S(2)}) collective-permute-start(bf16[2,128,128]{2,1,0:T(8,128)(2,1)S(1)} %get-tuple-element.79), channel_id=1, source_target_pairs={{0,5},{1,4},{2,7},{3,6},{4,1},{5,0},{6,3},{7,2},{8,13},{9,12},{10,... | collective-permute-start | bytes 196616 | tf_op jit(solution)/shard_map/ppermute | solution.py:522
  19.5 5.5 %collective-permute-start.11 = (bf16[2,128,128]{2,1,0:T(8,128)(2,1)S(1)}, bf16[2,128,128]{2,1,0:T(8,128)(2,1)S(1)}, u32[]{:S(2)}, u32[]{:S(2)}) collective-permute-start(bf16[2,128,128]{2,1,0:T(8,128)(2,1)S(1)} %get-tuple-element.92), channel_id=1, source_target_pairs={{0,6},{1,7},{2,4},{3,5},{4,2},{5,3},{6,0},{7,1},{8,14},{9,15},{10,... | collective-permute-start | bytes 196616 | tf_op jit(solution)/shard_map/ppermute | solution.py:522
  21.4 4.6 %collective-permute-start.12 = (bf16[2,128,128]{2,1,0:T(8,128)(2,1)S(1)}, bf16[2,128,128]{2,1,0:T(8,128)(2,1)S(1)}, u32[]{:S(2)}, u32[]{:S(2)}) collective-permute-start(bf16[2,128,128]{2,1,0:T(8,128)(2,1)S(1)} %get-tuple-element.93), channel_id=1, source_target_pairs={{0,3},{1,2},{2,1},{3,0},{4,7},{5,6},{6,5},{7,4},{8,11},{9,10},{10,... | collective-permute-start | bytes 196616 | tf_op jit(solution)/shard_map/ppermute | solution.py:522
  21.6 4.4 %collective-permute-start.13 = (bf16[2,128,128]{2,1,0:T(8,128)(2,1)S(1)}, bf16[2,128,128]{2,1,0:T(8,128)(2,1)S(1)}, u32[]{:S(2)}, u32[]{:S(2)}) collective-permute-start(bf16[2,128,128]{2,1,0:T(8,128)(2,1)S(1)} %get-tuple-element.94), channel_id=1, source_target_pairs={{0,5},{1,4},{2,7},{3,6},{4,1},{5,0},{6,3},{7,2},{8,13},{9,12},{10,... | collective-permute-start | bytes 196616 | tf_op jit(solution)/shard_map/ppermute | solution.py:522
  23.0 3.4 %collective-permute-start.15 = (bf16[8,128,128]{2,1,0:T(8,128)(2,1)S(1)}, bf16[8,128,128]{2,1,0:T(8,128)(2,1)S(1)}, u32[]{:S(2)}, u32[]{:S(2)}) collective-permute-start(bf16[8,128,128]{2,1,0:T(8,128)(2,1)S(1)} %get-tuple-element.100), channel_id=1, source_target_pairs={{0,1},{1,0},{2,3},{3,2},{4,5},{5,4},{6,7},{7,6},{8,9},{9,8},{10,11... | collective-permute-start | bytes 786440 | tf_op jit(solution)/shard_map/ppermute | solution.py:558
  26.2 1.6 %collective-permute-start.14 = (bf16[8,128,128]{2,1,0:T(8,128)(2,1)S(1)}, bf16[8,128,128]{2,1,0:T(8,128)(2,1)S(1)}, u32[]{:S(2)}, u32[]{:S(2)}) collective-permute-start(bf16[8,128,128]{2,1,0:T(8,128)(2,1)S(1)} %get-tuple-element.95), channel_id=1, source_target_pairs={{0,1},{1,0},{2,3},{3,2},{4,5},{5,4},{6,7},{7,6},{8,9},{9,8},{10,11... | collective-permute-start | bytes 786440 | tf_op jit(solution)/shard_map/ppermute | solution.py:558

commit v19 on v18

--- a/solution.py
+++ b/solution.py
@@ -9,8 +9,8 @@
 
 HD = 128
 PAIRS = 4
-PARTNERS = (0, 3, 1, 2)
-STEPS = (0, 6, 3, 5)
+PARTNERS = (0, 1, 3, 2)
+STEPS = (0, 3, 6, 5)
 EARLY_BACK = (0, 1, 2, 3)
 TEAM = 2 * PAIRS
 F32 = jnp.float32

time: 29.1 us -> 30.6 us (1.052)
  waiting for transfers between devices: 1.63 us -> 3.63 us
  starting transfers between devices: 17.6 us -> 17.1 us
    ppermute x12, waiting for transfers between devices: 1.59 us -> 3.47 us  [trade(): lax.ppermute(parts[d], 'seq', [(i, i ^ STEPS[d]) for i in range(n)])]
    ppermute x1, starting transfers between devices: 2.85 us -> 2.31 us  [per_device(): enter = lax.ppermute(edge(0), 'seq', up + down)]
  transfers between devices with their start and end apart: 16 -> 16, of which waited for: 3 -> 5; matrix products, arithmetic and copies ran while one was open for 0% -> 0% of each run, Pallas kernels for 20% -> 19%
where the time goes in v19:
time: 30.6 us; the launch traced here: 30.5 us
  starting transfers between devices  17.1 us (56%)
  Pallas kernels  9 us (29%)
  waiting for transfers between devices  3.63 us (12%)
  between operations  0.75 us (2%)
    ppermute x12, starting transfers between devices, trade(): lax.ppermute(parts[d], 'seq', [(i, i ^ STEPS[d]) for i in range(n)])  14 us
    pallas_call x11, Pallas kernels, call(): pl.pallas_call(kernel, in_specs=specs, out_specs=out_specs or [vmem] * le...  9 us
    ppermute x12, waiting for transfers between devices, trade(): lax.ppermute(parts[d], 'seq', [(i, i ^ STEPS[d]) for i in range(n)])  3.47 us
    ppermute x1, starting transfers between devices, per_device(): enter = lax.ppermute(edge(0), 'seq', up + down)  2.31 us
  transfers between devices with their start and end apart: 16, of which 5 were waited for; matrix products, arithmetic and copies ran while one was open for 0% of the time, Pallas kernels for 19%

profile of v19, /device:TPU:0, one launch (start us, length us, event | category | flops | bytes accessed | tf_op | source)
XLA Modules:
  0.0 30.5 jit_solution(3163269081174525683)
XLA Ops:
  0.6 1.9 %send.1 = (s32[8]{0:T(128)S(1)}, bf16[2,8,128,128]{3,2,1,0:T(8,128)(2,1)S(1)}, bf16[128,1024]{1,0:T(8,128)(2,1)S(1)}, bf16[128,1024]{1,0:T(8,128)(2,1)S(1)}, bf1...) custom-call(s32[8]{0:T(128)} %len_hbm.1, ...), custom_call_target="tpu_custom_call" | custom-call | flops 67108864 | bytes 4325440 | tf_op jit(solution)/shard_map/send/pallas_call | solution.py:462
  2.5 0.5 %collective-permute-start = (bf16[2,8,128,128]{3,2,1,0:T(8,128)(2,1)S(1)}, bf16[2,8,128,128]{3,2,1,0:T(8,128)(2,1)S(1)}, u32[]{:S(2)}, u32[]{:S(2)}) collective-permute-start(bf16[2,8,128,128]{3,2,1,0:T(8,128)(2,1)S(1)} %get-tuple-element.71), channel_id=1, source_target_pairs={{0,1},{1,0},{2,3},{3,2},{4,5},{5,4},{6,7},{7,6},{8,9},{9,8},{10,11... | collective-permute-start | bytes 1572872 | tf_op jit(solution)/shard_map/ppermute | solution.py:498
  3.0 1.8 %keep.1 = (bf16[2,8,128,128]{3,2,1,0:T(8,128)(2,1)S(1)}, bf16[128,1024]{1,0:T(8,128)(2,1)S(1)}, bf16[128,1024]{1,0:T(8,128)(2,1)S(1)}, bf16[128,1024]{1,0:T(8,12...) custom-call(s32[8]{0:T(128)S(1)} %get-tuple-element.56.len_hbm, ...), custom_call_target="tpu_custom_call" | custom-call | flops 67108864 | bytes 4358176 | tf_op jit(solution)/shard_map/keep/pallas_call | solution.py:462
  4.8 0.0 collective-permute-done.got_ref
  4.9 0.2 pair.1
  5.1 2.7 %collective-permute-start.1 = (bf16[2,128,128]{2,1,0:T(8,128)(2,1)S(1)}, bf16[2,128,128]{2,1,0:T(8,128)(2,1)S(1)}, u32[]{:S(2)}, u32[]{:S(2)}) collective-permute-start(bf16[2,128,128]{2,1,0:T(8,128)(2,1)S(1)} %get-tuple-element.73), channel_id=1, source_target_pairs={{0,3},{1,2},{2,1},{3,0},{4,7},{5,6},{6,5},{7,4},{8,11},{9,10},{10,... | collective-permute-start | bytes 196616 | tf_op jit(solution)/shard_map/ppermute | solution.py:522
  7.8 1.5 %collective-permute-start.2 = (bf16[2,128,128]{2,1,0:T(8,128)(2,1)S(1)}, bf16[2,128,128]{2,1,0:T(8,128)(2,1)S(1)}, u32[]{:S(2)}, u32[]{:S(2)}) collective-permute-start(bf16[2,128,128]{2,1,0:T(8,128)(2,1)S(1)} %get-tuple-element.74), channel_id=1, source_target_pairs={{0,6},{1,7},{2,4},{3,5},{4,2},{5,3},{6,0},{7,1},{8,14},{9,15},{10,... | collective-permute-start | bytes 196616 | tf_op jit(solution)/shard_map/ppermute | solution.py:522
  9.3 0.0 collective-permute-start.3
  9.3 1.7 %collective-permute-start.7 = (bf16[2,128,128]{2,1,0:T(8,128)(2,1)S(1)}, bf16[2,128,128]{2,1,0:T(8,128)(2,1)S(1)}, u32[]{:S(2)}, u32[]{:S(2)}) collective-permute-start(bf16[2,128,128]{2,1,0:T(8,128)(2,1)S(1)} %get-tuple-element.88), channel_id=1, source_target_pairs={{0,3},{1,2},{2,1},{3,0},{4,7},{5,6},{6,5},{7,4},{8,11},{9,10},{10,... | collective-permute-start | bytes 196616 | tf_op jit(solution)/shard_map/ppermute | solution.py:522
  11.0 1.5 %collective-permute-start.8 = (bf16[2,128,128]{2,1,0:T(8,128)(2,1)S(1)}, bf16[2,128,128]{2,1,0:T(8,128)(2,1)S(1)}, u32[]{:S(2)}, u32[]{:S(2)}) collective-permute-start(bf16[2,128,128]{2,1,0:T(8,128)(2,1)S(1)} %get-tuple-element.89), channel_id=1, source_target_pairs={{0,6},{1,7},{2,4},{3,5},{4,2},{5,3},{6,0},{7,1},{8,14},{9,15},{10,... | collective-permute-start | bytes 196616 | tf_op jit(solution)/shard_map/ppermute | solution.py:522
  12.5 0.0 collective-permute-done.1.refs_1_.s1
  12.5 0.5 %collective-permute-done.2.refs_2_.s2 = bf16[2,128,128]{2,1,0:T(8,128)(2,1)S(1)} collective-permute-done((bf16[2,128,128]{2,1,0:T(8,128)(2,1)S(1)}, bf16[2,128,128]{2,1,0:T(8,128)(2,1)S(1)}, u32[]{:S(2)}, u32[]{:S(2)}) %collective-permute-start.2) | collective-permute-done | bytes 65568 | tf_op jit(solution)/shard_map/ppermute | solution.py:522
  13.0 0.6 %collective-permute-done.3.refs_3_.s3 = bf16[2,128,128]{2,1,0:T(8,128)(2,1)S(1)} collective-permute-done((bf16[2,128,128]{2,1,0:T(8,128)(2,1)S(1)}, bf16[2,128,128]{2,1,0:T(8,128)(2,1)S(1)}, u32[]{:S(2)}, u32[]{:S(2)}) %collective-permute-start.3) | collective-permute-done | bytes 65568 | tf_op jit(solution)/shard_map/ppermute | solution.py:522
  13.6 0.1 totals.1
  13.7 2.3 %collective-permute-start.10 = (bf16[2,128,128]{2,1,0:T(8,128)(2,1)S(1)}, bf16[2,128,128]{2,1,0:T(8,128)(2,1)S(1)}, u32[]{:S(2)}, u32[]{:S(2)}) collective-permute-start(bf16[2,128,128]{2,1,0:T(8,128)(2,1)S(1)} %totals.1), channel_id=1, source_target_pairs={{0,9},{1,8},{2,11},{3,10},{4,13},{5,12},{6,15},{7,14},{9,0},{8,1},... | collective-permute-start | bytes 196616 | tf_op jit(solution)/shard_map/ppermute | solution.py:544
  16.0 0.1 scan.2
  16.1 1.6 %collective-permute-start.4 = (bf16[2,128,128]{2,1,0:T(8,128)(2,1)S(1)}, bf16[2,128,128]{2,1,0:T(8,128)(2,1)S(1)}, u32[]{:S(2)}, u32[]{:S(2)}) collective-permute-start(bf16[2,128,128]{2,1,0:T(8,128)(2,1)S(1)} %get-tuple-element.77), channel_id=1, source_target_pairs={{0,3},{1,2},{2,1},{3,0},{4,7},{5,6},{6,5},{7,4},{8,11},{9,10},{10,... | collective-permute-start | bytes 196616 | tf_op jit(solution)/shard_map/ppermute | solution.py:522
  17.8 1.5 %collective-permute-start.5 = (bf16[2,128,128]{2,1,0:T(8,128)(2,1)S(1)}, bf16[2,128,128]{2,1,0:T(8,128)(2,1)S(1)}, u32[]{:S(2)}, u32[]{:S(2)}) collective-permute-start(bf16[2,128,128]{2,1,0:T(8,128)(2,1)S(1)} %get-tuple-element.78), channel_id=1, source_target_pairs={{0,6},{1,7},{2,4},{3,5},{4,2},{5,3},{6,0},{7,1},{8,14},{9,15},{10,... | collective-permute-start | bytes 196616 | tf_op jit(solution)/shard_map/ppermute | solution.py:522
  19.3 0.2 scan.3
  19.5 2.2 %collective-permute-start.11 = (bf16[2,128,128]{2,1,0:T(8,128)(2,1)S(1)}, bf16[2,128,128]{2,1,0:T(8,128)(2,1)S(1)}, u32[]{:S(2)}, u32[]{:S(2)}) collective-permute-start(bf16[2,128,128]{2,1,0:T(8,128)(2,1)S(1)} %get-tuple-element.92), channel_id=1, source_target_pairs={{0,3},{1,2},{2,1},{3,0},{4,7},{5,6},{6,5},{7,4},{8,11},{9,10},{10,... | collective-permute-start | bytes 196616 | tf_op jit(solution)/shard_map/ppermute | solution.py:522
  21.7 1.1 %collective-permute-start.12 = (bf16[2,128,128]{2,1,0:T(8,128)(2,1)S(1)}, bf16[2,128,128]{2,1,0:T(8,128)(2,1)S(1)}, u32[]{:S(2)}, u32[]{:S(2)}) collective-permute-start(bf16[2,128,128]{2,1,0:T(8,128)(2,1)S(1)} %get-tuple-element.93), channel_id=1, source_target_pairs={{0,6},{1,7},{2,4},{3,5},{4,2},{5,3},{6,0},{7,1},{8,14},{9,15},{10,... | collective-permute-start | bytes 196616 | tf_op jit(solution)/shard_map/ppermute | solution.py:522
  22.7 0.2 collective-permute-start.13
  22.9 0.7 %collective-permute-done.5.refs_2_ = bf16[2,128,128]{2,1,0:T(8,128)(2,1)S(1)} collective-permute-done((bf16[2,128,128]{2,1,0:T(8,128)(2,1)S(1)}, bf16[2,128,128]{2,1,0:T(8,128)(2,1)S(1)}, u32[]{:S(2)}, u32[]{:S(2)}) %collective-permute-start.5) | collective-permute-done | bytes 65568 | tf_op jit(solution)/shard_map/ppermute | solution.py:522
  23.6 0.2 post.2
  23.9 0.1 collective-permute-start.15
  24.0 1.8 %local.1 = (bf16[16,128,128]{2,1,0:T(8,128)(2,1)S(1)}, bf16[16,128,128]{2,1,0:T(8,128)(2,1)S(1)}, bf16[16,128,128]{2,1,0:T(8,128)(2,1)S(1)}, bf16[16,128,128]{2,...) custom-call(s32[8]{0:T(128)S(1)} %get-tuple-element.56.len_hbm, ...), custom_call_target="tpu_custom_call" | custom-call | flops 134217728 | bytes 6160416 | tf_op jit(solution)/shard_map/local/pallas_call | solution.py:462
  25.8 1.6 %collective-permute-done.12.refs_2_ = bf16[2,128,128]{2,1,0:T(8,128)(2,1)S(1)} collective-permute-done((bf16[2,128,128]{2,1,0:T(8,128)(2,1)S(1)}, bf16[2,128,128]{2,1,0:T(8,128)(2,1)S(1)}, u32[]{:S(2)}, u32[]{:S(2)}) %collective-permute-start.12) | collective-permute-done | bytes 65568 | tf_op jit(solution)/shard_map/ppermute | solution.py:522
  27.5 0.2 post.3
  27.7 0.1 collective-permute-start.14
  27.8 1.4 %middle.1 = (bf16[128,2048]{1,0:T(8,128)(2,1)}, bf16[128,2048]{1,0:T(8,128)(2,1)}, bf16[128,2048]{1,0:T(8,128)(2,1)}, bf16[128,2048]{1,0:T(8,128)(2,1)}, bf16[12...) custom-call(bf16[128,1024]{1,0:T(8,128)(2,1)S(1)} %get-tuple-element.98.refs_0_, ...), custom_call_target="tpu_custom_call" | custom-call | flops 268435456 | bytes 9043968 | tf_op jit(solution)/shard_map/middle/pallas_call | solution.py:462
  29.2 0.1 collective-permute-done.14.refs_13_
  29.3 1.2 %last.1 = (bf16[128,2048]{1,0:T(8,128)(2,1)}, bf16[128,2048]{1,0:T(8,128)(2,1)}, bf16[128,2048]{1,0:T(8,128)(2,1)}, bf16[128,2048]{1,0:T(8,128)(2,1)}) custom-call(bf16[128,1024]{1,0:T(8,128)(2,1)S(1)} %get-tuple-element.59.refs_0_.refs_2_, ...), custom_call_target="tpu_custom_call", output_to_operand_aliasing={{0}: (18, {}), {1}: (19, {}), {2}: (20, {}), {3}: (21, {})} | custom-call | flops 134217728 | bytes 9830400 | tf_op jit(solution)/shard_map/last/pallas_call | solution.py:462
  (11 shorter events, 0.0 us)
Async XLA Ops:
  2.5 2.4 %collective-permute-start = (bf16[2,8,128,128]{3,2,1,0:T(8,128)(2,1)S(1)}, bf16[2,8,128,128]{3,2,1,0:T(8,128)(2,1)S(1)}, u32[]{:S(2)}, u32[]{:S(2)}) collective-permute-start(bf16[2,8,128,128]{3,2,1,0:T(8,128)(2,1)S(1)} %get-tuple-element.71), channel_id=1, source_target_pairs={{0,1},{1,0},{2,3},{3,2},{4,5},{5,4},{6,7},{7,6},{8,9},{9,8},{10,11... | collective-permute-start | bytes 1572872 | tf_op jit(solution)/shard_map/ppermute | solution.py:498
  5.1 7.4 %collective-permute-start.1 = (bf16[2,128,128]{2,1,0:T(8,128)(2,1)S(1)}, bf16[2,128,128]{2,1,0:T(8,128)(2,1)S(1)}, u32[]{:S(2)}, u32[]{:S(2)}) collective-permute-start(bf16[2,128,128]{2,1,0:T(8,128)(2,1)S(1)} %get-tuple-element.73), channel_id=1, source_target_pairs={{0,3},{1,2},{2,1},{3,0},{4,7},{5,6},{6,5},{7,4},{8,11},{9,10},{10,... | collective-permute-start | bytes 196616 | tf_op jit(solution)/shard_map/ppermute | solution.py:522
  7.8 5.2 %collective-permute-start.2 = (bf16[2,128,128]{2,1,0:T(8,128)(2,1)S(1)}, bf16[2,128,128]{2,1,0:T(8,128)(2,1)S(1)}, u32[]{:S(2)}, u32[]{:S(2)}) collective-permute-start(bf16[2,128,128]{2,1,0:T(8,128)(2,1)S(1)} %get-tuple-element.74), channel_id=1, source_target_pairs={{0,6},{1,7},{2,4},{3,5},{4,2},{5,3},{6,0},{7,1},{8,14},{9,15},{10,... | collective-permute-start | bytes 196616 | tf_op jit(solution)/shard_map/ppermute | solution.py:522
  9.3 4.3 %collective-permute-start.3 = (bf16[2,128,128]{2,1,0:T(8,128)(2,1)S(1)}, bf16[2,128,128]{2,1,0:T(8,128)(2,1)S(1)}, u32[]{:S(2)}, u32[]{:S(2)}) collective-permute-start(bf16[2,128,128]{2,1,0:T(8,128)(2,1)S(1)} %get-tuple-element.75), channel_id=1, source_target_pairs={{0,5},{1,4},{2,7},{3,6},{4,1},{5,0},{6,3},{7,2},{8,13},{9,12},{10,... | collective-permute-start | bytes 196616 | tf_op jit(solution)/shard_map/ppermute | solution.py:522
  9.3 8.5 %collective-permute-start.7 = (bf16[2,128,128]{2,1,0:T(8,128)(2,1)S(1)}, bf16[2,128,128]{2,1,0:T(8,128)(2,1)S(1)}, u32[]{:S(2)}, u32[]{:S(2)}) collective-permute-start(bf16[2,128,128]{2,1,0:T(8,128)(2,1)S(1)} %get-tuple-element.88), channel_id=1, source_target_pairs={{0,3},{1,2},{2,1},{3,0},{4,7},{5,6},{6,5},{7,4},{8,11},{9,10},{10,... | collective-permute-start | bytes 196616 | tf_op jit(solution)/shard_map/ppermute | solution.py:522
  11.0 8.3 %collective-permute-start.8 = (bf16[2,128,128]{2,1,0:T(8,128)(2,1)S(1)}, bf16[2,128,128]{2,1,0:T(8,128)(2,1)S(1)}, u32[]{:S(2)}, u32[]{:S(2)}) collective-permute-start(bf16[2,128,128]{2,1,0:T(8,128)(2,1)S(1)} %get-tuple-element.89), channel_id=1, source_target_pairs={{0,6},{1,7},{2,4},{3,5},{4,2},{5,3},{6,0},{7,1},{8,14},{9,15},{10,... | collective-permute-start | bytes 196616 | tf_op jit(solution)/shard_map/ppermute | solution.py:522
  12.5 6.8 %collective-permute-start.9 = (bf16[2,128,128]{2,1,0:T(8,128)(2,1)S(1)}, bf16[2,128,128]{2,1,0:T(8,128)(2,1)S(1)}, u32[]{:S(2)}, u32[]{:S(2)}) collective-permute-start(bf16[2,128,128]{2,1,0:T(8,128)(2,1)S(1)} %get-tuple-element.90), channel_id=1, source_target_pairs={{0,5},{1,4},{2,7},{3,6},{4,1},{5,0},{6,3},{7,2},{8,13},{9,12},{10,... | collective-permute-start | bytes 196616 | tf_op jit(solution)/shard_map/ppermute | solution.py:522
  13.7 5.6 %collective-permute-start.10 = (bf16[2,128,128]{2,1,0:T(8,128)(2,1)S(1)}, bf16[2,128,128]{2,1,0:T(8,128)(2,1)S(1)}, u32[]{:S(2)}, u32[]{:S(2)}) collective-permute-start(bf16[2,128,128]{2,1,0:T(8,128)(2,1)S(1)} %totals.1), channel_id=1, source_target_pairs={{0,9},{1,8},{2,11},{3,10},{4,13},{5,12},{6,15},{7,14},{9,0},{8,1},... | collective-permute-start | bytes 196616 | tf_op jit(solution)/shard_map/ppermute | solution.py:544
  16.1 6.6 %collective-permute-start.4 = (bf16[2,128,128]{2,1,0:T(8,128)(2,1)S(1)}, bf16[2,128,128]{2,1,0:T(8,128)(2,1)S(1)}, u32[]{:S(2)}, u32[]{:S(2)}) collective-permute-start(bf16[2,128,128]{2,1,0:T(8,128)(2,1)S(1)} %get-tuple-element.77), channel_id=1, source_target_pairs={{0,3},{1,2},{2,1},{3,0},{4,7},{5,6},{6,5},{7,4},{8,11},{9,10},{10,... | collective-permute-start | bytes 196616 | tf_op jit(solution)/shard_map/ppermute | solution.py:522
  17.8 5.9 %collective-permute-start.5 = (bf16[2,128,128]{2,1,0:T(8,128)(2,1)S(1)}, bf16[2,128,128]{2,1,0:T(8,128)(2,1)S(1)}, u32[]{:S(2)}, u32[]{:S(2)}) collective-permute-start(bf16[2,128,128]{2,1,0:T(8,128)(2,1)S(1)} %get-tuple-element.78), channel_id=1, source_target_pairs={{0,6},{1,7},{2,4},{3,5},{4,2},{5,3},{6,0},{7,1},{8,14},{9,15},{10,... | collective-permute-start | bytes 196616 | tf_op jit(solution)/shard_map/ppermute | solution.py:522
  19.3 4.4 %collective-permute-start.6 = (bf16[2,128,128]{2,1,0:T(8,128)(2,1)S(1)}, bf16[2,128,128]{2,1,0:T(8,128)(2,1)S(1)}, u32[]{:S(2)}, u32[]{:S(2)}) collective-permute-start(bf16[2,128,128]{2,1,0:T(8,128)(2,1)S(1)} %get-tuple-element.79), channel_id=1, source_target_pairs={{0,5},{1,4},{2,7},{3,6},{4,1},{5,0},{6,3},{7,2},{8,13},{9,12},{10,... | collective-permute-start | bytes 196616 | tf_op jit(solution)/shard_map/ppermute | solution.py:522
  19.5 6.4 %collective-permute-start.11 = (bf16[2,128,128]{2,1,0:T(8,128)(2,1)S(1)}, bf16[2,128,128]{2,1,0:T(8,128)(2,1)S(1)}, u32[]{:S(2)}, u32[]{:S(2)}) collective-permute-start(bf16[2,128,128]{2,1,0:T(8,128)(2,1)S(1)} %get-tuple-element.92), channel_id=1, source_target_pairs={{0,3},{1,2},{2,1},{3,0},{4,7},{5,6},{6,5},{7,4},{8,11},{9,10},{10,... | collective-permute-start | bytes 196616 | tf_op jit(solution)/shard_map/ppermute | solution.py:522
  21.7 5.8 %collective-permute-start.12 = (bf16[2,128,128]{2,1,0:T(8,128)(2,1)S(1)}, bf16[2,128,128]{2,1,0:T(8,128)(2,1)S(1)}, u32[]{:S(2)}, u32[]{:S(2)}) collective-permute-start(bf16[2,128,128]{2,1,0:T(8,128)(2,1)S(1)} %get-tuple-element.93), channel_id=1, source_target_pairs={{0,6},{1,7},{2,4},{3,5},{4,2},{5,3},{6,0},{7,1},{8,14},{9,15},{10,... | collective-permute-start | bytes 196616 | tf_op jit(solution)/shard_map/ppermute | solution.py:522
  22.7 4.7 %collective-permute-start.13 = (bf16[2,128,128]{2,1,0:T(8,128)(2,1)S(1)}, bf16[2,128,128]{2,1,0:T(8,128)(2,1)S(1)}, u32[]{:S(2)}, u32[]{:S(2)}) collective-permute-start(bf16[2,128,128]{2,1,0:T(8,128)(2,1)S(1)} %get-tuple-element.94), channel_id=1, source_target_pairs={{0,5},{1,4},{2,7},{3,6},{4,1},{5,0},{6,3},{7,2},{8,13},{9,12},{10,... | collective-permute-start | bytes 196616 | tf_op jit(solution)/shard_map/ppermute | solution.py:522
  23.9 3.9 %collective-permute-start.15 = (bf16[8,128,128]{2,1,0:T(8,128)(2,1)S(1)}, bf16[8,128,128]{2,1,0:T(8,128)(2,1)S(1)}, u32[]{:S(2)}, u32[]{:S(2)}) collective-permute-start(bf16[8,128,128]{2,1,0:T(8,128)(2,1)S(1)} %get-tuple-element.100), channel_id=1, source_target_pairs={{0,1},{1,0},{2,3},{3,2},{4,5},{5,4},{6,7},{7,6},{8,9},{9,8},{10,11... | collective-permute-start | bytes 786440 | tf_op jit(solution)/shard_map/ppermute | solution.py:558
  27.7 1.6 %collective-permute-start.14 = (bf16[8,128,128]{2,1,0:T(8,128)(2,1)S(1)}, bf16[8,128,128]{2,1,0:T(8,128)(2,1)S(1)}, u32[]{:S(2)}, u32[]{:S(2)}) collective-permute-start(bf16[8,128,128]{2,1,0:T(8,128)(2,1)S(1)} %get-tuple-element.95), channel_id=1, source_target_pairs={{0,1},{1,0},{2,3},{3,2},{4,5},{5,4},{6,7},{7,6},{8,9},{9,8},{10,11... | collective-permute-start | bytes 786440 | tf_op jit(solution)/shard_map/ppermute | solution.py:558

commit v20 on v18

--- a/solution.py
+++ b/solution.py
@@ -11,7 +11,7 @@
 PAIRS = 4
 PARTNERS = (0, 3, 1, 2)
 STEPS = (0, 6, 3, 5)
-EARLY_BACK = (0, 1, 2, 3)
+LATE = (0, 1, 3, 2)
 TEAM = 2 * PAIRS
 F32 = jnp.float32
 BF16 = jnp.bfloat16
@@ -311,8 +311,8 @@
         out_ref[i] = sum(parts).astype(BF16)
 
 
-def scan_kernel(which, split, enters, coef_ref, *refs):
-    sums, out_refs = refs[:PAIRS], refs[-PAIRS:]
+def scan_kernel(which, split, enters, order, coef_ref, *refs):
+    sums, out_refs = [refs[order.index(d)] for d in range(PAIRS)], refs[-PAIRS:]
     kind = kind_of(which, split)
     mix, enter = MIX_F + PAIRS * PAIRS * kind, ENTER_F + PAIRS * kind
     for i in range(out_refs[0].shape[0]):
@@ -517,13 +517,15 @@
         [vmem] * 3,
     )
 
-    def trade(parts, order=range(PAIRS)):
+    orders = tuple(range(PAIRS)), LATE
+
+    def trade(parts, order):
         return [
             lax.ppermute(parts[d], "seq", [(i, i ^ STEPS[d]) for i in range(n)]) if d else parts[0]
             for d in order
         ]
 
-    sums = [trade(parts[:PAIRS]), trade(parts[PAIRS:])]
+    sums = [trade(parts[w * PAIRS :][:PAIRS], orders[w]) for w in range(2)]
 
     def edge(which):
         kernel = functools.partial(totals_kernel, which, split)
@@ -531,7 +533,7 @@
 
     def scan(which, *enter):
         return call(
-            functools.partial(scan_kernel, which, split, bool(enter)),
+            functools.partial(scan_kernel, which, split, bool(enter), orders[which]),
             "scan",
             [owned] * PAIRS,
             (table, *sums[which], *enter),
@@ -547,17 +549,17 @@
         forward, backward = lax.ppermute(edge(0), "seq", up), lax.ppermute(edge(1), "seq", down)
         results = scan(0, forward), scan(1, backward)
 
-    def post(which, order, *after):
+    def post(which, *after):
         own, theirs = call(
-            functools.partial(post_kernel, which, split, order),
+            functools.partial(post_kernel, which, split, orders[which]),
             "post",
             [halves] * 2,
-            (table, keep, got, *trade(results[which], order), *after),
+            (table, keep, got, *trade(results[which], orders[which]), *after),
             [vmem] * (3 + PAIRS + len(after)),
         )
         return own, lax.ppermute(theirs, "seq", swap)
 
-    early_mine, early_other = post(0, EARLY_BACK)
+    early_mine, early_other = post(0)
     *local, masks, early_0, early_1 = call(
         functools.partial(local_kernel, total, split),
         "local",
@@ -567,7 +569,7 @@
         flops=2 * heads * product,
         scratch=lengths,
     )
-    late_mine, late_other = post(1, range(PAIRS), masks)
+    late_mine, late_other = post(1, masks)
     w, wt, dw, dwt, scaled = local
     fixed = (*mines[:3], *others[:3], scaled, w, wt, dw, dwt, masks, root)
     chunks = 4

time: 29.1 us -> 29.6 us (1.017)
  starting transfers between devices: 17.6 us -> 17.9 us
    ppermute x2, starting transfers between devices: 0.37 us -> 0.76 us  [post(): return (own, lax.ppermute(theirs, 'seq', swap))]
  transfers between devices with their start and end apart: 16 -> 16, of which waited for: 3 -> 4; matrix products, arithmetic and copies ran while one was open for 0% -> 0% of each run, Pallas kernels for 20% -> 20%
where the time goes in v20:
time: 29.6 us; the launch traced here: 29.4 us
  starting transfers between devices  17.9 us (60%)
  Pallas kernels  9 us (30%)
  waiting for transfers between devices  1.75 us (6%)
  between operations  0.73 us (2%)
    ppermute x12, starting transfers between devices, trade(): lax.ppermute(parts[d], 'seq', [(i, i ^ STEPS[d]) for i in range(n)])  13.8 us
    pallas_call x11, Pallas kernels, call(): pl.pallas_call(kernel, in_specs=specs, out_specs=out_specs or [vmem] * le...  9 us
    ppermute x1, starting transfers between devices, per_device(): enter = lax.ppermute(edge(0), 'seq', up + down)  2.85 us
    ppermute x12, waiting for transfers between devices, trade(): lax.ppermute(parts[d], 'seq', [(i, i ^ STEPS[d]) for i in range(n)])  1.74 us
    ppermute x2, starting transfers between devices, post(): return (own, lax.ppermute(theirs, 'seq', swap))  0.76 us
  transfers between devices with their start and end apart: 16, of which 4 were waited for; matrix products, arithmetic and copies ran while one was open for 0% of the time, Pallas kernels for 20%

profile of v20, /device:TPU:0, one launch (start us, length us, event | category | flops | bytes accessed | tf_op | source)
XLA Modules:
  0.0 29.4 jit_solution(10154716328989913737)
XLA Ops:
  0.6 1.9 %send.1 = (s32[8]{0:T(128)S(1)}, bf16[2,8,128,128]{3,2,1,0:T(8,128)(2,1)S(1)}, bf16[128,1024]{1,0:T(8,128)(2,1)S(1)}, bf16[128,1024]{1,0:T(8,128)(2,1)S(1)}, bf1...) custom-call(s32[8]{0:T(128)} %len_hbm.1, ...), custom_call_target="tpu_custom_call" | custom-call | flops 67108864 | bytes 4325440 | tf_op jit(solution)/shard_map/send/pallas_call | solution.py:462
  2.5 0.5 %collective-permute-start = (bf16[2,8,128,128]{3,2,1,0:T(8,128)(2,1)S(1)}, bf16[2,8,128,128]{3,2,1,0:T(8,128)(2,1)S(1)}, u32[]{:S(2)}, u32[]{:S(2)}) collective-permute-start(bf16[2,8,128,128]{3,2,1,0:T(8,128)(2,1)S(1)} %get-tuple-element.71), channel_id=1, source_target_pairs={{0,1},{1,0},{2,3},{3,2},{4,5},{5,4},{6,7},{7,6},{8,9},{9,8},{10,11... | collective-permute-start | bytes 1572872 | tf_op jit(solution)/shard_map/ppermute | solution.py:498
  3.0 1.8 %keep.1 = (bf16[2,8,128,128]{3,2,1,0:T(8,128)(2,1)S(1)}, bf16[128,1024]{1,0:T(8,128)(2,1)S(1)}, bf16[128,1024]{1,0:T(8,128)(2,1)S(1)}, bf16[128,1024]{1,0:T(8,12...) custom-call(s32[8]{0:T(128)S(1)} %get-tuple-element.56.len_hbm, ...), custom_call_target="tpu_custom_call" | custom-call | flops 67108864 | bytes 4358176 | tf_op jit(solution)/shard_map/keep/pallas_call | solution.py:462
  4.9 0.2 pair.1
  5.1 3.6 %collective-permute-start.1 = (bf16[2,128,128]{2,1,0:T(8,128)(2,1)S(1)}, bf16[2,128,128]{2,1,0:T(8,128)(2,1)S(1)}, u32[]{:S(2)}, u32[]{:S(2)}) collective-permute-start(bf16[2,128,128]{2,1,0:T(8,128)(2,1)S(1)} %get-tuple-element.73), channel_id=1, source_target_pairs={{0,6},{1,7},{2,4},{3,5},{4,2},{5,3},{6,0},{7,1},{8,14},{9,15},{10,... | collective-permute-start | bytes 196616 | tf_op jit(solution)/shard_map/ppermute | solution.py:524
  8.7 0.3 %collective-permute-start.2 = (bf16[2,128,128]{2,1,0:T(8,128)(2,1)S(1)}, bf16[2,128,128]{2,1,0:T(8,128)(2,1)S(1)}, u32[]{:S(2)}, u32[]{:S(2)}) collective-permute-start(bf16[2,128,128]{2,1,0:T(8,128)(2,1)S(1)} %get-tuple-element.74), channel_id=1, source_target_pairs={{0,3},{1,2},{2,1},{3,0},{4,7},{5,6},{6,5},{7,4},{8,11},{9,10},{10,... | collective-permute-start | bytes 196616 | tf_op jit(solution)/shard_map/ppermute | solution.py:524
  9.0 0.1 collective-permute-start.3
  9.1 2.8 %collective-permute-start.7 = (bf16[2,128,128]{2,1,0:T(8,128)(2,1)S(1)}, bf16[2,128,128]{2,1,0:T(8,128)(2,1)S(1)}, u32[]{:S(2)}, u32[]{:S(2)}) collective-permute-start(bf16[2,128,128]{2,1,0:T(8,128)(2,1)S(1)} %get-tuple-element.88), channel_id=1, source_target_pairs={{0,6},{1,7},{2,4},{3,5},{4,2},{5,3},{6,0},{7,1},{8,14},{9,15},{10,... | collective-permute-start | bytes 196616 | tf_op jit(solution)/shard_map/ppermute | solution.py:524
  11.9 0.0 collective-permute-done.1.refs_1_.s1
  11.9 0.4 %collective-permute-start.9 = (bf16[2,128,128]{2,1,0:T(8,128)(2,1)S(1)}, bf16[2,128,128]{2,1,0:T(8,128)(2,1)S(1)}, u32[]{:S(2)}, u32[]{:S(2)}) collective-permute-start(bf16[2,128,128]{2,1,0:T(8,128)(2,1)S(1)} %get-tuple-element.90), channel_id=1, source_target_pairs={{0,3},{1,2},{2,1},{3,0},{4,7},{5,6},{6,5},{7,4},{8,11},{9,10},{10,... | collective-permute-start | bytes 196616 | tf_op jit(solution)/shard_map/ppermute | solution.py:524
  12.3 0.5 %collective-permute-done.2.refs_2_.s2 = bf16[2,128,128]{2,1,0:T(8,128)(2,1)S(1)} collective-permute-done((bf16[2,128,128]{2,1,0:T(8,128)(2,1)S(1)}, bf16[2,128,128]{2,1,0:T(8,128)(2,1)S(1)}, u32[]{:S(2)}, u32[]{:S(2)}) %collective-permute-start.2) | collective-permute-done | bytes 65568 | tf_op jit(solution)/shard_map/ppermute | solution.py:524
  12.8 0.1 collective-permute-done.3.refs_3_.s3
  13.0 0.1 totals.1
  13.0 2.8 %collective-permute-start.10 = (bf16[2,128,128]{2,1,0:T(8,128)(2,1)S(1)}, bf16[2,128,128]{2,1,0:T(8,128)(2,1)S(1)}, u32[]{:S(2)}, u32[]{:S(2)}) collective-permute-start(bf16[2,128,128]{2,1,0:T(8,128)(2,1)S(1)} %totals.1), channel_id=1, source_target_pairs={{0,9},{1,8},{2,11},{3,10},{4,13},{5,12},{6,15},{7,14},{9,0},{8,1},... | collective-permute-start | bytes 196616 | tf_op jit(solution)/shard_map/ppermute | solution.py:546
  15.9 0.1 scan.2
  16.0 1.6 %collective-permute-start.4 = (bf16[2,128,128]{2,1,0:T(8,128)(2,1)S(1)}, bf16[2,128,128]{2,1,0:T(8,128)(2,1)S(1)}, u32[]{:S(2)}, u32[]{:S(2)}) collective-permute-start(bf16[2,128,128]{2,1,0:T(8,128)(2,1)S(1)} %get-tuple-element.77), channel_id=1, source_target_pairs={{0,6},{1,7},{2,4},{3,5},{4,2},{5,3},{6,0},{7,1},{8,14},{9,15},{10,... | collective-permute-start | bytes 196616 | tf_op jit(solution)/shard_map/ppermute | solution.py:524
  17.6 0.0 collective-permute-done.7.refs_1_
  17.6 0.7 %collective-permute-start.5 = (bf16[2,128,128]{2,1,0:T(8,128)(2,1)S(1)}, bf16[2,128,128]{2,1,0:T(8,128)(2,1)S(1)}, u32[]{:S(2)}, u32[]{:S(2)}) collective-permute-start(bf16[2,128,128]{2,1,0:T(8,128)(2,1)S(1)} %get-tuple-element.78), channel_id=1, source_target_pairs={{0,3},{1,2},{2,1},{3,0},{4,7},{5,6},{6,5},{7,4},{8,11},{9,10},{10,... | collective-permute-start | bytes 196616 | tf_op jit(solution)/shard_map/ppermute | solution.py:524
  18.3 1.0 %collective-permute-start.6 = (bf16[2,128,128]{2,1,0:T(8,128)(2,1)S(1)}, bf16[2,128,128]{2,1,0:T(8,128)(2,1)S(1)}, u32[]{:S(2)}, u32[]{:S(2)}) collective-permute-start(bf16[2,128,128]{2,1,0:T(8,128)(2,1)S(1)} %get-tuple-element.79), channel_id=1, source_target_pairs={{0,5},{1,4},{2,7},{3,6},{4,1},{5,0},{6,3},{7,2},{8,13},{9,12},{10,... | collective-permute-start | bytes 196616 | tf_op jit(solution)/shard_map/ppermute | solution.py:524
  19.3 0.2 scan.3
  19.5 1.9 %collective-permute-start.11 = (bf16[2,128,128]{2,1,0:T(8,128)(2,1)S(1)}, bf16[2,128,128]{2,1,0:T(8,128)(2,1)S(1)}, u32[]{:S(2)}, u32[]{:S(2)}) collective-permute-start(bf16[2,128,128]{2,1,0:T(8,128)(2,1)S(1)} %get-tuple-element.92), channel_id=1, source_target_pairs={{0,6},{1,7},{2,4},{3,5},{4,2},{5,3},{6,0},{7,1},{8,14},{9,15},{10,... | collective-permute-start | bytes 196616 | tf_op jit(solution)/shard_map/ppermute | solution.py:524
  21.4 1.0 %collective-permute-start.12 = (bf16[2,128,128]{2,1,0:T(8,128)(2,1)S(1)}, bf16[2,128,128]{2,1,0:T(8,128)(2,1)S(1)}, u32[]{:S(2)}, u32[]{:S(2)}) collective-permute-start(bf16[2,128,128]{2,1,0:T(8,128)(2,1)S(1)} %get-tuple-element.93), channel_id=1, source_target_pairs={{0,5},{1,4},{2,7},{3,6},{4,1},{5,0},{6,3},{7,2},{8,13},{9,12},{10,... | collective-permute-start | bytes 196616 | tf_op jit(solution)/shard_map/ppermute | solution.py:524
  22.4 0.4 %collective-permute-start.13 = (bf16[2,128,128]{2,1,0:T(8,128)(2,1)S(1)}, bf16[2,128,128]{2,1,0:T(8,128)(2,1)S(1)}, u32[]{:S(2)}, u32[]{:S(2)}) collective-permute-start(bf16[2,128,128]{2,1,0:T(8,128)(2,1)S(1)} %get-tuple-element.94), channel_id=1, source_target_pairs={{0,3},{1,2},{2,1},{3,0},{4,7},{5,6},{6,5},{7,4},{8,11},{9,10},{10,... | collective-permute-start | bytes 196616 | tf_op jit(solution)/shard_map/ppermute | solution.py:524
  22.7 0.2 post.2
  23.0 0.4 %collective-permute-start.15 = (bf16[8,128,128]{2,1,0:T(8,128)(2,1)S(1)}, bf16[8,128,128]{2,1,0:T(8,128)(2,1)S(1)}, u32[]{:S(2)}, u32[]{:S(2)}) collective-permute-start(bf16[8,128,128]{2,1,0:T(8,128)(2,1)S(1)} %get-tuple-element.100), channel_id=1, source_target_pairs={{0,1},{1,0},{2,3},{3,2},{4,5},{5,4},{6,7},{7,6},{8,9},{9,8},{10,11... | collective-permute-start | bytes 786440 | tf_op jit(solution)/shard_map/ppermute | solution.py:560
  23.4 1.8 %local.1 = (bf16[16,128,128]{2,1,0:T(8,128)(2,1)S(1)}, bf16[16,128,128]{2,1,0:T(8,128)(2,1)S(1)}, bf16[16,128,128]{2,1,0:T(8,128)(2,1)S(1)}, bf16[16,128,128]{2,...) custom-call(s32[8]{0:T(128)S(1)} %get-tuple-element.56.len_hbm, ...), custom_call_target="tpu_custom_call" | custom-call | flops 134217728 | bytes 6160416 | tf_op jit(solution)/shard_map/local/pallas_call | solution.py:462
  25.2 0.7 %collective-permute-done.12.refs_2_ = bf16[2,128,128]{2,1,0:T(8,128)(2,1)S(1)} collective-permute-done((bf16[2,128,128]{2,1,0:T(8,128)(2,1)S(1)}, bf16[2,128,128]{2,1,0:T(8,128)(2,1)S(1)}, u32[]{:S(2)}, u32[]{:S(2)}) %collective-permute-start.12) | collective-permute-done | bytes 65568 | tf_op jit(solution)/shard_map/ppermute | solution.py:524
  25.9 0.4 %collective-permute-done.13.refs_3_ = bf16[2,128,128]{2,1,0:T(8,128)(2,1)S(1)} collective-permute-done((bf16[2,128,128]{2,1,0:T(8,128)(2,1)S(1)}, bf16[2,128,128]{2,1,0:T(8,128)(2,1)S(1)}, u32[]{:S(2)}, u32[]{:S(2)}) %collective-permute-start.13) | collective-permute-done | bytes 65568 | tf_op jit(solution)/shard_map/ppermute | solution.py:524
  26.3 0.2 post.3
  26.5 0.3 %collective-permute-start.14 = (bf16[8,128,128]{2,1,0:T(8,128)(2,1)S(1)}, bf16[8,128,128]{2,1,0:T(8,128)(2,1)S(1)}, u32[]{:S(2)}, u32[]{:S(2)}) collective-permute-start(bf16[8,128,128]{2,1,0:T(8,128)(2,1)S(1)} %get-tuple-element.95), channel_id=1, source_target_pairs={{0,1},{1,0},{2,3},{3,2},{4,5},{5,4},{6,7},{7,6},{8,9},{9,8},{10,11... | collective-permute-start | bytes 786440 | tf_op jit(solution)/shard_map/ppermute | solution.py:560
  26.9 1.3 %middle.1 = (bf16[128,2048]{1,0:T(8,128)(2,1)}, bf16[128,2048]{1,0:T(8,128)(2,1)}, bf16[128,2048]{1,0:T(8,128)(2,1)}, bf16[128,2048]{1,0:T(8,128)(2,1)}, bf16[12...) custom-call(bf16[128,1024]{1,0:T(8,128)(2,1)S(1)} %get-tuple-element.98.refs_0_, ...), custom_call_target="tpu_custom_call" | custom-call | flops 268435456 | bytes 9043968 | tf_op jit(solution)/shard_map/middle/pallas_call | solution.py:462
  28.2 1.2 %last.1 = (bf16[128,2048]{1,0:T(8,128)(2,1)}, bf16[128,2048]{1,0:T(8,128)(2,1)}, bf16[128,2048]{1,0:T(8,128)(2,1)}, bf16[128,2048]{1,0:T(8,128)(2,1)}) custom-call(bf16[128,1024]{1,0:T(8,128)(2,1)S(1)} %get-tuple-element.59.refs_0_.refs_2_, ...), custom_call_target="tpu_custom_call", output_to_operand_aliasing={{0}: (18, {}), {1}: (19, {}), {2}: (20, {}), {3}: (21, {})} | custom-call | flops 134217728 | bytes 9830400 | tf_op jit(solution)/shard_map/last/pallas_call | solution.py:462
  (11 shorter events, 0.0 us)
Async XLA Ops:
  2.5 2.4 %collective-permute-start = (bf16[2,8,128,128]{3,2,1,0:T(8,128)(2,1)S(1)}, bf16[2,8,128,128]{3,2,1,0:T(8,128)(2,1)S(1)}, u32[]{:S(2)}, u32[]{:S(2)}) collective-permute-start(bf16[2,8,128,128]{3,2,1,0:T(8,128)(2,1)S(1)} %get-tuple-element.71), channel_id=1, source_target_pairs={{0,1},{1,0},{2,3},{3,2},{4,5},{5,4},{6,7},{7,6},{8,9},{9,8},{10,11... | collective-permute-start | bytes 1572872 | tf_op jit(solution)/shard_map/ppermute | solution.py:498
  5.1 6.9 %collective-permute-start.1 = (bf16[2,128,128]{2,1,0:T(8,128)(2,1)S(1)}, bf16[2,128,128]{2,1,0:T(8,128)(2,1)S(1)}, u32[]{:S(2)}, u32[]{:S(2)}) collective-permute-start(bf16[2,128,128]{2,1,0:T(8,128)(2,1)S(1)} %get-tuple-element.73), channel_id=1, source_target_pairs={{0,6},{1,7},{2,4},{3,5},{4,2},{5,3},{6,0},{7,1},{8,14},{9,15},{10,... | collective-permute-start | bytes 196616 | tf_op jit(solution)/shard_map/ppermute | solution.py:524
  8.7 4.1 %collective-permute-start.2 = (bf16[2,128,128]{2,1,0:T(8,128)(2,1)S(1)}, bf16[2,128,128]{2,1,0:T(8,128)(2,1)S(1)}, u32[]{:S(2)}, u32[]{:S(2)}) collective-permute-start(bf16[2,128,128]{2,1,0:T(8,128)(2,1)S(1)} %get-tuple-element.74), channel_id=1, source_target_pairs={{0,3},{1,2},{2,1},{3,0},{4,7},{5,6},{6,5},{7,4},{8,11},{9,10},{10,... | collective-permute-start | bytes 196616 | tf_op jit(solution)/shard_map/ppermute | solution.py:524
  9.0 4.0 %collective-permute-start.3 = (bf16[2,128,128]{2,1,0:T(8,128)(2,1)S(1)}, bf16[2,128,128]{2,1,0:T(8,128)(2,1)S(1)}, u32[]{:S(2)}, u32[]{:S(2)}) collective-permute-start(bf16[2,128,128]{2,1,0:T(8,128)(2,1)S(1)} %get-tuple-element.75), channel_id=1, source_target_pairs={{0,5},{1,4},{2,7},{3,6},{4,1},{5,0},{6,3},{7,2},{8,13},{9,12},{10,... | collective-permute-start | bytes 196616 | tf_op jit(solution)/shard_map/ppermute | solution.py:524
  9.1 8.5 %collective-permute-start.7 = (bf16[2,128,128]{2,1,0:T(8,128)(2,1)S(1)}, bf16[2,128,128]{2,1,0:T(8,128)(2,1)S(1)}, u32[]{:S(2)}, u32[]{:S(2)}) collective-permute-start(bf16[2,128,128]{2,1,0:T(8,128)(2,1)S(1)} %get-tuple-element.88), channel_id=1, source_target_pairs={{0,6},{1,7},{2,4},{3,5},{4,2},{5,3},{6,0},{7,1},{8,14},{9,15},{10,... | collective-permute-start | bytes 196616 | tf_op jit(solution)/shard_map/ppermute | solution.py:524
  11.9 6.4 %collective-permute-start.8 = (bf16[2,128,128]{2,1,0:T(8,128)(2,1)S(1)}, bf16[2,128,128]{2,1,0:T(8,128)(2,1)S(1)}, u32[]{:S(2)}, u32[]{:S(2)}) collective-permute-start(bf16[2,128,128]{2,1,0:T(8,128)(2,1)S(1)} %get-tuple-element.89), channel_id=1, source_target_pairs={{0,5},{1,4},{2,7},{3,6},{4,1},{5,0},{6,3},{7,2},{8,13},{9,12},{10,... | collective-permute-start | bytes 196616 | tf_op jit(solution)/shard_map/ppermute | solution.py:524
  11.9 7.4 %collective-permute-start.9 = (bf16[2,128,128]{2,1,0:T(8,128)(2,1)S(1)}, bf16[2,128,128]{2,1,0:T(8,128)(2,1)S(1)}, u32[]{:S(2)}, u32[]{:S(2)}) collective-permute-start(bf16[2,128,128]{2,1,0:T(8,128)(2,1)S(1)} %get-tuple-element.90), channel_id=1, source_target_pairs={{0,3},{1,2},{2,1},{3,0},{4,7},{5,6},{6,5},{7,4},{8,11},{9,10},{10,... | collective-permute-start | bytes 196616 | tf_op jit(solution)/shard_map/ppermute | solution.py:524
  13.0 6.3 %collective-permute-start.10 = (bf16[2,128,128]{2,1,0:T(8,128)(2,1)S(1)}, bf16[2,128,128]{2,1,0:T(8,128)(2,1)S(1)}, u32[]{:S(2)}, u32[]{:S(2)}) collective-permute-start(bf16[2,128,128]{2,1,0:T(8,128)(2,1)S(1)} %totals.1), channel_id=1, source_target_pairs={{0,9},{1,8},{2,11},{3,10},{4,13},{5,12},{6,15},{7,14},{9,0},{8,1},... | collective-permute-start | bytes 196616 | tf_op jit(solution)/shard_map/ppermute | solution.py:546
  16.0 6.4 %collective-permute-start.4 = (bf16[2,128,128]{2,1,0:T(8,128)(2,1)S(1)}, bf16[2,128,128]{2,1,0:T(8,128)(2,1)S(1)}, u32[]{:S(2)}, u32[]{:S(2)}) collective-permute-start(bf16[2,128,128]{2,1,0:T(8,128)(2,1)S(1)} %get-tuple-element.77), channel_id=1, source_target_pairs={{0,6},{1,7},{2,4},{3,5},{4,2},{5,3},{6,0},{7,1},{8,14},{9,15},{10,... | collective-permute-start | bytes 196616 | tf_op jit(solution)/shard_map/ppermute | solution.py:524
  17.6 5.2 %collective-permute-start.5 = (bf16[2,128,128]{2,1,0:T(8,128)(2,1)S(1)}, bf16[2,128,128]{2,1,0:T(8,128)(2,1)S(1)}, u32[]{:S(2)}, u32[]{:S(2)}) collective-permute-start(bf16[2,128,128]{2,1,0:T(8,128)(2,1)S(1)} %get-tuple-element.78), channel_id=1, source_target_pairs={{0,3},{1,2},{2,1},{3,0},{4,7},{5,6},{6,5},{7,4},{8,11},{9,10},{10,... | collective-permute-start | bytes 196616 | tf_op jit(solution)/shard_map/ppermute | solution.py:524
  18.3 4.4 %collective-permute-start.6 = (bf16[2,128,128]{2,1,0:T(8,128)(2,1)S(1)}, bf16[2,128,128]{2,1,0:T(8,128)(2,1)S(1)}, u32[]{:S(2)}, u32[]{:S(2)}) collective-permute-start(bf16[2,128,128]{2,1,0:T(8,128)(2,1)S(1)} %get-tuple-element.79), channel_id=1, source_target_pairs={{0,5},{1,4},{2,7},{3,6},{4,1},{5,0},{6,3},{7,2},{8,13},{9,12},{10,... | collective-permute-start | bytes 196616 | tf_op jit(solution)/shard_map/ppermute | solution.py:524
  19.5 5.7 %collective-permute-start.11 = (bf16[2,128,128]{2,1,0:T(8,128)(2,1)S(1)}, bf16[2,128,128]{2,1,0:T(8,128)(2,1)S(1)}, u32[]{:S(2)}, u32[]{:S(2)}) collective-permute-start(bf16[2,128,128]{2,1,0:T(8,128)(2,1)S(1)} %get-tuple-element.92), channel_id=1, source_target_pairs={{0,6},{1,7},{2,4},{3,5},{4,2},{5,3},{6,0},{7,1},{8,14},{9,15},{10,... | collective-permute-start | bytes 196616 | tf_op jit(solution)/shard_map/ppermute | solution.py:524
  21.4 4.5 %collective-permute-start.12 = (bf16[2,128,128]{2,1,0:T(8,128)(2,1)S(1)}, bf16[2,128,128]{2,1,0:T(8,128)(2,1)S(1)}, u32[]{:S(2)}, u32[]{:S(2)}) collective-permute-start(bf16[2,128,128]{2,1,0:T(8,128)(2,1)S(1)} %get-tuple-element.93), channel_id=1, source_target_pairs={{0,5},{1,4},{2,7},{3,6},{4,1},{5,0},{6,3},{7,2},{8,13},{9,12},{10,... | collective-permute-start | bytes 196616 | tf_op jit(solution)/shard_map/ppermute | solution.py:524
  22.4 4.0 %collective-permute-start.13 = (bf16[2,128,128]{2,1,0:T(8,128)(2,1)S(1)}, bf16[2,128,128]{2,1,0:T(8,128)(2,1)S(1)}, u32[]{:S(2)}, u32[]{:S(2)}) collective-permute-start(bf16[2,128,128]{2,1,0:T(8,128)(2,1)S(1)} %get-tuple-element.94), channel_id=1, source_target_pairs={{0,3},{1,2},{2,1},{3,0},{4,7},{5,6},{6,5},{7,4},{8,11},{9,10},{10,... | collective-permute-start | bytes 196616 | tf_op jit(solution)/shard_map/ppermute | solution.py:524
  23.0 3.9 %collective-permute-start.15 = (bf16[8,128,128]{2,1,0:T(8,128)(2,1)S(1)}, bf16[8,128,128]{2,1,0:T(8,128)(2,1)S(1)}, u32[]{:S(2)}, u32[]{:S(2)}) collective-permute-start(bf16[8,128,128]{2,1,0:T(8,128)(2,1)S(1)} %get-tuple-element.100), channel_id=1, source_target_pairs={{0,1},{1,0},{2,3},{3,2},{4,5},{5,4},{6,7},{7,6},{8,9},{9,8},{10,11... | collective-permute-start | bytes 786440 | tf_op jit(solution)/shard_map/ppermute | solution.py:560
  26.5 1.7 %collective-permute-start.14 = (bf16[8,128,128]{2,1,0:T(8,128)(2,1)S(1)}, bf16[8,128,128]{2,1,0:T(8,128)(2,1)S(1)}, u32[]{:S(2)}, u32[]{:S(2)}) collective-permute-start(bf16[8,128,128]{2,1,0:T(8,128)(2,1)S(1)} %get-tuple-element.95), channel_id=1, source_target_pairs={{0,1},{1,0},{2,3},{3,2},{4,5},{5,4},{6,7},{7,6},{8,9},{9,8},{10,11... | collective-permute-start | bytes 786440 | tf_op jit(solution)/shard_map/ppermute | solution.py:560

commit v21 on v18

--- a/solution.py
+++ b/solution.py
@@ -11,7 +11,6 @@
 PAIRS = 4
 PARTNERS = (0, 3, 1, 2)
 STEPS = (0, 6, 3, 5)
-EARLY_BACK = (0, 1, 2, 3)
 TEAM = 2 * PAIRS
 F32 = jnp.float32
 BF16 = jnp.bfloat16
@@ -479,7 +478,7 @@
         pltpu.with_memory_space_constraint(x, pltpu.HBM)
         for x in (doc_lengths, queries, keys, values, grad_out)
     )
-    chunks = 2
+    chunks = 4
     doc_lengths, send, *others = call(
         functools.partial(send_kernel, total, chunks),
         "send",
@@ -557,7 +556,7 @@
         )
         return own, lax.ppermute(theirs, "seq", swap)
 
-    early_mine, early_other = post(0, EARLY_BACK)
+    early_mine, early_other = post(0, range(PAIRS))
     *local, masks, early_0, early_1 = call(
         functools.partial(local_kernel, total, split),
         "local",

time: 29.1 us -> 30.3 us (1.041)
  Pallas kernels: 8.98 us -> 10.1 us
    pallas_call x11, Pallas kernels: 8.98 us -> 10.1 us  [call(): pl.pallas_call(kernel, in_specs=specs, out_specs=out_specs or [vmem] * le...]
  transfers between devices with their start and end apart: 16 -> 16, of which waited for: 3 -> 3; matrix products, arithmetic and copies ran while one was open for 0% -> 0% of each run, Pallas kernels for 20% -> 21%
where the time goes in v21:
time: 30.3 us; the launch traced here: 30.1 us
  starting transfers between devices  17.6 us (58%)
  Pallas kernels  10.1 us (33%)
  waiting for transfers between devices  1.63 us (5%)
  between operations  0.72 us (2%)
    ppermute x12, starting transfers between devices, trade(): lax.ppermute(parts[d], 'seq', [(i, i ^ STEPS[d]) for i in range(n)])  13.8 us
    pallas_call x11, Pallas kernels, call(): pl.pallas_call(kernel, in_specs=specs, out_specs=out_specs or [vmem] * le...  10.1 us
    ppermute x1, starting transfers between devices, per_device(): enter = lax.ppermute(edge(0), 'seq', up + down)  2.85 us
    ppermute x12, waiting for transfers between devices, trade(): lax.ppermute(parts[d], 'seq', [(i, i ^ STEPS[d]) for i in range(n)])  1.58 us
  transfers between devices with their start and end apart: 16, of which 3 were waited for; matrix products, arithmetic and copies ran while one was open for 0% of the time, Pallas kernels for 21%

profile of v21, /device:TPU:0, one launch (start us, length us, event | category | flops | bytes accessed | tf_op | source)
XLA Modules:
  0.0 30.1 jit_solution(7721646309974011191)
XLA Ops:
  0.6 2.4 %send.1 = (s32[8]{0:T(128)S(1)}, bf16[2,8,128,128]{3,2,1,0:T(8,128)(2,1)S(1)}, bf16[128,1024]{1,0:T(8,128)(2,1)S(1)}, bf16[128,1024]{1,0:T(8,128)(2,1)S(1)}, bf1...) custom-call(s32[8]{0:T(128)} %len_hbm.1, ...), custom_call_target="tpu_custom_call" | custom-call | flops 67108864 | bytes 4325440 | tf_op jit(solution)/shard_map/send/pallas_call | solution.py:461
  3.1 0.5 %collective-permute-start = (bf16[2,8,128,128]{3,2,1,0:T(8,128)(2,1)S(1)}, bf16[2,8,128,128]{3,2,1,0:T(8,128)(2,1)S(1)}, u32[]{:S(2)}, u32[]{:S(2)}) collective-permute-start(bf16[2,8,128,128]{3,2,1,0:T(8,128)(2,1)S(1)} %get-tuple-element.71), channel_id=1, source_target_pairs={{0,1},{1,0},{2,3},{3,2},{4,5},{5,4},{6,7},{7,6},{8,9},{9,8},{10,11... | collective-permute-start | bytes 1572872 | tf_op jit(solution)/shard_map/ppermute | solution.py:497
  3.6 2.3 %keep.1 = (bf16[2,8,128,128]{3,2,1,0:T(8,128)(2,1)S(1)}, bf16[128,1024]{1,0:T(8,128)(2,1)S(1)}, bf16[128,1024]{1,0:T(8,128)(2,1)S(1)}, bf16[128,1024]{1,0:T(8,12...) custom-call(s32[8]{0:T(128)S(1)} %get-tuple-element.56.len_hbm, ...), custom_call_target="tpu_custom_call" | custom-call | flops 67108864 | bytes 4358176 | tf_op jit(solution)/shard_map/keep/pallas_call | solution.py:461
  5.9 0.2 pair.1
  6.2 3.6 %collective-permute-start.1 = (bf16[2,128,128]{2,1,0:T(8,128)(2,1)S(1)}, bf16[2,128,128]{2,1,0:T(8,128)(2,1)S(1)}, u32[]{:S(2)}, u32[]{:S(2)}) collective-permute-start(bf16[2,128,128]{2,1,0:T(8,128)(2,1)S(1)} %get-tuple-element.73), channel_id=1, source_target_pairs={{0,6},{1,7},{2,4},{3,5},{4,2},{5,3},{6,0},{7,1},{8,14},{9,15},{10,... | collective-permute-start | bytes 196616 | tf_op jit(solution)/shard_map/ppermute | solution.py:521
  9.8 0.3 collective-permute-start.2
  10.1 0.1 collective-permute-start.3
  10.2 2.8 %collective-permute-start.7 = (bf16[2,128,128]{2,1,0:T(8,128)(2,1)S(1)}, bf16[2,128,128]{2,1,0:T(8,128)(2,1)S(1)}, u32[]{:S(2)}, u32[]{:S(2)}) collective-permute-start(bf16[2,128,128]{2,1,0:T(8,128)(2,1)S(1)} %get-tuple-element.88), channel_id=1, source_target_pairs={{0,6},{1,7},{2,4},{3,5},{4,2},{5,3},{6,0},{7,1},{8,14},{9,15},{10,... | collective-permute-start | bytes 196616 | tf_op jit(solution)/shard_map/ppermute | solution.py:521
  13.0 0.0 collective-permute-start.8
  13.0 0.5 %collective-permute-start.9 = (bf16[2,128,128]{2,1,0:T(8,128)(2,1)S(1)}, bf16[2,128,128]{2,1,0:T(8,128)(2,1)S(1)}, u32[]{:S(2)}, u32[]{:S(2)}) collective-permute-start(bf16[2,128,128]{2,1,0:T(8,128)(2,1)S(1)} %get-tuple-element.90), channel_id=1, source_target_pairs={{0,5},{1,4},{2,7},{3,6},{4,1},{5,0},{6,3},{7,2},{8,13},{9,12},{10,... | collective-permute-start | bytes 196616 | tf_op jit(solution)/shard_map/ppermute | solution.py:521
  13.5 0.4 %collective-permute-done.2.refs_2_.s2 = bf16[2,128,128]{2,1,0:T(8,128)(2,1)S(1)} collective-permute-done((bf16[2,128,128]{2,1,0:T(8,128)(2,1)S(1)}, bf16[2,128,128]{2,1,0:T(8,128)(2,1)S(1)}, u32[]{:S(2)}, u32[]{:S(2)}) %collective-permute-start.2) | collective-permute-done | bytes 65568 | tf_op jit(solution)/shard_map/ppermute | solution.py:521
  13.9 0.1 collective-permute-done.3.refs_3_.s3
  14.0 0.1 totals.1
  14.1 2.8 %collective-permute-start.10 = (bf16[2,128,128]{2,1,0:T(8,128)(2,1)S(1)}, bf16[2,128,128]{2,1,0:T(8,128)(2,1)S(1)}, u32[]{:S(2)}, u32[]{:S(2)}) collective-permute-start(bf16[2,128,128]{2,1,0:T(8,128)(2,1)S(1)} %totals.1), channel_id=1, source_target_pairs={{0,9},{1,8},{2,11},{3,10},{4,13},{5,12},{6,15},{7,14},{9,0},{8,1},... | collective-permute-start | bytes 196616 | tf_op jit(solution)/shard_map/ppermute | solution.py:543
  17.0 0.1 scan.2
  17.1 1.6 %collective-permute-start.4 = (bf16[2,128,128]{2,1,0:T(8,128)(2,1)S(1)}, bf16[2,128,128]{2,1,0:T(8,128)(2,1)S(1)}, u32[]{:S(2)}, u32[]{:S(2)}) collective-permute-start(bf16[2,128,128]{2,1,0:T(8,128)(2,1)S(1)} %get-tuple-element.77), channel_id=1, source_target_pairs={{0,6},{1,7},{2,4},{3,5},{4,2},{5,3},{6,0},{7,1},{8,14},{9,15},{10,... | collective-permute-start | bytes 196616 | tf_op jit(solution)/shard_map/ppermute | solution.py:521
  18.6 0.8 %collective-permute-start.5 = (bf16[2,128,128]{2,1,0:T(8,128)(2,1)S(1)}, bf16[2,128,128]{2,1,0:T(8,128)(2,1)S(1)}, u32[]{:S(2)}, u32[]{:S(2)}) collective-permute-start(bf16[2,128,128]{2,1,0:T(8,128)(2,1)S(1)} %get-tuple-element.78), channel_id=1, source_target_pairs={{0,3},{1,2},{2,1},{3,0},{4,7},{5,6},{6,5},{7,4},{8,11},{9,10},{10,... | collective-permute-start | bytes 196616 | tf_op jit(solution)/shard_map/ppermute | solution.py:521
  19.4 0.9 %collective-permute-start.6 = (bf16[2,128,128]{2,1,0:T(8,128)(2,1)S(1)}, bf16[2,128,128]{2,1,0:T(8,128)(2,1)S(1)}, u32[]{:S(2)}, u32[]{:S(2)}) collective-permute-start(bf16[2,128,128]{2,1,0:T(8,128)(2,1)S(1)} %get-tuple-element.79), channel_id=1, source_target_pairs={{0,5},{1,4},{2,7},{3,6},{4,1},{5,0},{6,3},{7,2},{8,13},{9,12},{10,... | collective-permute-start | bytes 196616 | tf_op jit(solution)/shard_map/ppermute | solution.py:521
  20.4 0.2 scan.3
  20.5 2.0 %collective-permute-start.11 = (bf16[2,128,128]{2,1,0:T(8,128)(2,1)S(1)}, bf16[2,128,128]{2,1,0:T(8,128)(2,1)S(1)}, u32[]{:S(2)}, u32[]{:S(2)}) collective-permute-start(bf16[2,128,128]{2,1,0:T(8,128)(2,1)S(1)} %get-tuple-element.92), channel_id=1, source_target_pairs={{0,6},{1,7},{2,4},{3,5},{4,2},{5,3},{6,0},{7,1},{8,14},{9,15},{10,... | collective-permute-start | bytes 196616 | tf_op jit(solution)/shard_map/ppermute | solution.py:521
  22.5 0.2 collective-permute-start.12
  22.7 0.0 collective-permute-done.4.refs_1_
  22.7 1.1 %collective-permute-start.13 = (bf16[2,128,128]{2,1,0:T(8,128)(2,1)S(1)}, bf16[2,128,128]{2,1,0:T(8,128)(2,1)S(1)}, u32[]{:S(2)}, u32[]{:S(2)}) collective-permute-start(bf16[2,128,128]{2,1,0:T(8,128)(2,1)S(1)} %get-tuple-element.94), channel_id=1, source_target_pairs={{0,5},{1,4},{2,7},{3,6},{4,1},{5,0},{6,3},{7,2},{8,13},{9,12},{10,... | collective-permute-start | bytes 196616 | tf_op jit(solution)/shard_map/ppermute | solution.py:521
  23.8 0.2 post.2
  24.1 0.2 collective-permute-start.15
  24.3 1.8 %local.1 = (bf16[16,128,128]{2,1,0:T(8,128)(2,1)S(1)}, bf16[16,128,128]{2,1,0:T(8,128)(2,1)S(1)}, bf16[16,128,128]{2,1,0:T(8,128)(2,1)S(1)}, bf16[16,128,128]{2,...) custom-call(s32[8]{0:T(128)S(1)} %get-tuple-element.56.len_hbm, ...), custom_call_target="tpu_custom_call" | custom-call | flops 134217728 | bytes 6160416 | tf_op jit(solution)/shard_map/local/pallas_call | solution.py:461
  26.1 1.0 %collective-permute-done.12.refs_2_ = bf16[2,128,128]{2,1,0:T(8,128)(2,1)S(1)} collective-permute-done((bf16[2,128,128]{2,1,0:T(8,128)(2,1)S(1)}, bf16[2,128,128]{2,1,0:T(8,128)(2,1)S(1)}, u32[]{:S(2)}, u32[]{:S(2)}) %collective-permute-start.12) | collective-permute-done | bytes 65568 | tf_op jit(solution)/shard_map/ppermute | solution.py:521
  27.1 0.2 post.3
  27.3 0.2 collective-permute-start.14
  27.5 1.3 %middle.1 = (bf16[128,2048]{1,0:T(8,128)(2,1)}, bf16[128,2048]{1,0:T(8,128)(2,1)}, bf16[128,2048]{1,0:T(8,128)(2,1)}, bf16[128,2048]{1,0:T(8,128)(2,1)}, bf16[12...) custom-call(bf16[128,1024]{1,0:T(8,128)(2,1)S(1)} %get-tuple-element.98.refs_0_, ...), custom_call_target="tpu_custom_call" | custom-call | flops 268435456 | bytes 9043968 | tf_op jit(solution)/shard_map/middle/pallas_call | solution.py:461
  28.9 0.0 collective-permute-done.14.refs_13_
  28.9 1.2 %last.1 = (bf16[128,2048]{1,0:T(8,128)(2,1)}, bf16[128,2048]{1,0:T(8,128)(2,1)}, bf16[128,2048]{1,0:T(8,128)(2,1)}, bf16[128,2048]{1,0:T(8,128)(2,1)}) custom-call(bf16[128,1024]{1,0:T(8,128)(2,1)S(1)} %get-tuple-element.59.refs_0_.refs_2_, ...), custom_call_target="tpu_custom_call", output_to_operand_aliasing={{0}: (18, {}), {1}: (19, {}), {2}: (20, {}), {3}: (21, {})} | custom-call | flops 134217728 | bytes 9830400 | tf_op jit(solution)/shard_map/last/pallas_call | solution.py:461
  (11 shorter events, 0.0 us)
Async XLA Ops:
  3.1 2.9 %collective-permute-start = (bf16[2,8,128,128]{3,2,1,0:T(8,128)(2,1)S(1)}, bf16[2,8,128,128]{3,2,1,0:T(8,128)(2,1)S(1)}, u32[]{:S(2)}, u32[]{:S(2)}) collective-permute-start(bf16[2,8,128,128]{3,2,1,0:T(8,128)(2,1)S(1)} %get-tuple-element.71), channel_id=1, source_target_pairs={{0,1},{1,0},{2,3},{3,2},{4,5},{5,4},{6,7},{7,6},{8,9},{9,8},{10,11... | collective-permute-start | bytes 1572872 | tf_op jit(solution)/shard_map/ppermute | solution.py:497
  6.2 6.9 %collective-permute-start.1 = (bf16[2,128,128]{2,1,0:T(8,128)(2,1)S(1)}, bf16[2,128,128]{2,1,0:T(8,128)(2,1)S(1)}, u32[]{:S(2)}, u32[]{:S(2)}) collective-permute-start(bf16[2,128,128]{2,1,0:T(8,128)(2,1)S(1)} %get-tuple-element.73), channel_id=1, source_target_pairs={{0,6},{1,7},{2,4},{3,5},{4,2},{5,3},{6,0},{7,1},{8,14},{9,15},{10,... | collective-permute-start | bytes 196616 | tf_op jit(solution)/shard_map/ppermute | solution.py:521
  9.8 4.1 %collective-permute-start.2 = (bf16[2,128,128]{2,1,0:T(8,128)(2,1)S(1)}, bf16[2,128,128]{2,1,0:T(8,128)(2,1)S(1)}, u32[]{:S(2)}, u32[]{:S(2)}) collective-permute-start(bf16[2,128,128]{2,1,0:T(8,128)(2,1)S(1)} %get-tuple-element.74), channel_id=1, source_target_pairs={{0,3},{1,2},{2,1},{3,0},{4,7},{5,6},{6,5},{7,4},{8,11},{9,10},{10,... | collective-permute-start | bytes 196616 | tf_op jit(solution)/shard_map/ppermute | solution.py:521
  10.1 4.0 %collective-permute-start.3 = (bf16[2,128,128]{2,1,0:T(8,128)(2,1)S(1)}, bf16[2,128,128]{2,1,0:T(8,128)(2,1)S(1)}, u32[]{:S(2)}, u32[]{:S(2)}) collective-permute-start(bf16[2,128,128]{2,1,0:T(8,128)(2,1)S(1)} %get-tuple-element.75), channel_id=1, source_target_pairs={{0,5},{1,4},{2,7},{3,6},{4,1},{5,0},{6,3},{7,2},{8,13},{9,12},{10,... | collective-permute-start | bytes 196616 | tf_op jit(solution)/shard_map/ppermute | solution.py:521
  10.2 8.5 %collective-permute-start.7 = (bf16[2,128,128]{2,1,0:T(8,128)(2,1)S(1)}, bf16[2,128,128]{2,1,0:T(8,128)(2,1)S(1)}, u32[]{:S(2)}, u32[]{:S(2)}) collective-permute-start(bf16[2,128,128]{2,1,0:T(8,128)(2,1)S(1)} %get-tuple-element.88), channel_id=1, source_target_pairs={{0,6},{1,7},{2,4},{3,5},{4,2},{5,3},{6,0},{7,1},{8,14},{9,15},{10,... | collective-permute-start | bytes 196616 | tf_op jit(solution)/shard_map/ppermute | solution.py:521
  13.0 6.4 %collective-permute-start.8 = (bf16[2,128,128]{2,1,0:T(8,128)(2,1)S(1)}, bf16[2,128,128]{2,1,0:T(8,128)(2,1)S(1)}, u32[]{:S(2)}, u32[]{:S(2)}) collective-permute-start(bf16[2,128,128]{2,1,0:T(8,128)(2,1)S(1)} %get-tuple-element.89), channel_id=1, source_target_pairs={{0,3},{1,2},{2,1},{3,0},{4,7},{5,6},{6,5},{7,4},{8,11},{9,10},{10,... | collective-permute-start | bytes 196616 | tf_op jit(solution)/shard_map/ppermute | solution.py:521
  13.0 7.3 %collective-permute-start.9 = (bf16[2,128,128]{2,1,0:T(8,128)(2,1)S(1)}, bf16[2,128,128]{2,1,0:T(8,128)(2,1)S(1)}, u32[]{:S(2)}, u32[]{:S(2)}) collective-permute-start(bf16[2,128,128]{2,1,0:T(8,128)(2,1)S(1)} %get-tuple-element.90), channel_id=1, source_target_pairs={{0,5},{1,4},{2,7},{3,6},{4,1},{5,0},{6,3},{7,2},{8,13},{9,12},{10,... | collective-permute-start | bytes 196616 | tf_op jit(solution)/shard_map/ppermute | solution.py:521
  14.1 6.3 %collective-permute-start.10 = (bf16[2,128,128]{2,1,0:T(8,128)(2,1)S(1)}, bf16[2,128,128]{2,1,0:T(8,128)(2,1)S(1)}, u32[]{:S(2)}, u32[]{:S(2)}) collective-permute-start(bf16[2,128,128]{2,1,0:T(8,128)(2,1)S(1)} %totals.1), channel_id=1, source_target_pairs={{0,9},{1,8},{2,11},{3,10},{4,13},{5,12},{6,15},{7,14},{9,0},{8,1},... | collective-permute-start | bytes 196616 | tf_op jit(solution)/shard_map/ppermute | solution.py:543
  17.1 5.6 %collective-permute-start.4 = (bf16[2,128,128]{2,1,0:T(8,128)(2,1)S(1)}, bf16[2,128,128]{2,1,0:T(8,128)(2,1)S(1)}, u32[]{:S(2)}, u32[]{:S(2)}) collective-permute-start(bf16[2,128,128]{2,1,0:T(8,128)(2,1)S(1)} %get-tuple-element.77), channel_id=1, source_target_pairs={{0,6},{1,7},{2,4},{3,5},{4,2},{5,3},{6,0},{7,1},{8,14},{9,15},{10,... | collective-permute-start | bytes 196616 | tf_op jit(solution)/shard_map/ppermute | solution.py:521
  18.6 5.2 %collective-permute-start.5 = (bf16[2,128,128]{2,1,0:T(8,128)(2,1)S(1)}, bf16[2,128,128]{2,1,0:T(8,128)(2,1)S(1)}, u32[]{:S(2)}, u32[]{:S(2)}) collective-permute-start(bf16[2,128,128]{2,1,0:T(8,128)(2,1)S(1)} %get-tuple-element.78), channel_id=1, source_target_pairs={{0,3},{1,2},{2,1},{3,0},{4,7},{5,6},{6,5},{7,4},{8,11},{9,10},{10,... | collective-permute-start | bytes 196616 | tf_op jit(solution)/shard_map/ppermute | solution.py:521
  19.4 4.4 %collective-permute-start.6 = (bf16[2,128,128]{2,1,0:T(8,128)(2,1)S(1)}, bf16[2,128,128]{2,1,0:T(8,128)(2,1)S(1)}, u32[]{:S(2)}, u32[]{:S(2)}) collective-permute-start(bf16[2,128,128]{2,1,0:T(8,128)(2,1)S(1)} %get-tuple-element.79), channel_id=1, source_target_pairs={{0,5},{1,4},{2,7},{3,6},{4,1},{5,0},{6,3},{7,2},{8,13},{9,12},{10,... | collective-permute-start | bytes 196616 | tf_op jit(solution)/shard_map/ppermute | solution.py:521
  20.5 5.5 %collective-permute-start.11 = (bf16[2,128,128]{2,1,0:T(8,128)(2,1)S(1)}, bf16[2,128,128]{2,1,0:T(8,128)(2,1)S(1)}, u32[]{:S(2)}, u32[]{:S(2)}) collective-permute-start(bf16[2,128,128]{2,1,0:T(8,128)(2,1)S(1)} %get-tuple-element.92), channel_id=1, source_target_pairs={{0,6},{1,7},{2,4},{3,5},{4,2},{5,3},{6,0},{7,1},{8,14},{9,15},{10,... | collective-permute-start | bytes 196616 | tf_op jit(solution)/shard_map/ppermute | solution.py:521
  22.5 4.6 %collective-permute-start.12 = (bf16[2,128,128]{2,1,0:T(8,128)(2,1)S(1)}, bf16[2,128,128]{2,1,0:T(8,128)(2,1)S(1)}, u32[]{:S(2)}, u32[]{:S(2)}) collective-permute-start(bf16[2,128,128]{2,1,0:T(8,128)(2,1)S(1)} %get-tuple-element.93), channel_id=1, source_target_pairs={{0,3},{1,2},{2,1},{3,0},{4,7},{5,6},{6,5},{7,4},{8,11},{9,10},{10,... | collective-permute-start | bytes 196616 | tf_op jit(solution)/shard_map/ppermute | solution.py:521
  22.7 4.4 %collective-permute-start.13 = (bf16[2,128,128]{2,1,0:T(8,128)(2,1)S(1)}, bf16[2,128,128]{2,1,0:T(8,128)(2,1)S(1)}, u32[]{:S(2)}, u32[]{:S(2)}) collective-permute-start(bf16[2,128,128]{2,1,0:T(8,128)(2,1)S(1)} %get-tuple-element.94), channel_id=1, source_target_pairs={{0,5},{1,4},{2,7},{3,6},{4,1},{5,0},{6,3},{7,2},{8,13},{9,12},{10,... | collective-permute-start | bytes 196616 | tf_op jit(solution)/shard_map/ppermute | solution.py:521
  24.1 3.5 %collective-permute-start.15 = (bf16[8,128,128]{2,1,0:T(8,128)(2,1)S(1)}, bf16[8,128,128]{2,1,0:T(8,128)(2,1)S(1)}, u32[]{:S(2)}, u32[]{:S(2)}) collective-permute-start(bf16[8,128,128]{2,1,0:T(8,128)(2,1)S(1)} %get-tuple-element.100), channel_id=1, source_target_pairs={{0,1},{1,0},{2,3},{3,2},{4,5},{5,4},{6,7},{7,6},{8,9},{9,8},{10,11... | collective-permute-start | bytes 786440 | tf_op jit(solution)/shard_map/ppermute | solution.py:557
  27.3 1.6 %collective-permute-start.14 = (bf16[8,128,128]{2,1,0:T(8,128)(2,1)S(1)}, bf16[8,128,128]{2,1,0:T(8,128)(2,1)S(1)}, u32[]{:S(2)}, u32[]{:S(2)}) collective-permute-start(bf16[8,128,128]{2,1,0:T(8,128)(2,1)S(1)} %get-tuple-element.95), channel_id=1, source_target_pairs={{0,1},{1,0},{2,3},{3,2},{4,5},{5,4},{6,7},{7,6},{8,9},{9,8},{10,11... | collective-permute-start | bytes 786440 | tf_op jit(solution)/shard_map/ppermute | solution.py:557

commit v22 on v21

--- a/solution.py
+++ b/solution.py
@@ -65,50 +65,38 @@
     return lax.dot_general(a, b, ((contract[:1], contract[1:]), ((), ())), preferred_element_type=F32)
 
 
-def states_of(kt, qt, v, g, tail_rows, head_rows, inv_root):
-    scaled = (g.astype(F32) * inv_root).astype(BF16)
-    tail = dot(kt, v * tail_rows, (1, 0))
-    head = dot(qt, scaled * head_rows, (1, 0))
-    return tail.astype(BF16), head.astype(BF16)
-
-
 def half_index():
     me = lax.axis_index("seq")
     return (me ^ (me >> 1) ^ (me >> 2) ^ (me >> 3)) & 1
 
 
-def bring(pairs, begin, chunks, sems):
-    width = pairs[0][1].shape[1]
-    size = width // chunks
+def bring(pairs, half, sems):
     copies = []
-    for c in range(chunks):
-        at = pl.ds(pl.multiple_of(begin * HD + c * size, HD), size)
-        for i, (src, dst) in enumerate(pairs):
-            copy = pltpu.make_async_copy(src.at[:, at], dst.at[:, pl.ds(c * size, size)], sems.at[i, c])
-            copy.start()
-            copies.append(copy)
+    for i, (src, dst) in enumerate(pairs):
+        width = dst.shape[1]
+        at = pl.ds(pl.multiple_of(half * width, HD), width)
+        copies.append(pltpu.make_async_copy(src.at[:, at], dst, sems.at[i]))
+        copies[-1].start()
     return copies
 
 
-def states_by_chunk(copies, chunks, q_ref, k_ref, v_ref, g_ref, kt_ref, qt_ref, out_ref, masks):
-    per = out_ref.shape[1] // chunks
-    for c in range(chunks):
-        for i, (ref, t_ref) in enumerate(((k_ref, kt_ref), (q_ref, qt_ref))):
-            copies[4 * c + i].wait()
-            for h in range(c * per, (c + 1) * per):
-                t_ref[h] = ref[:, pl.ds(h * HD, HD)].T
-        for copy in copies[4 * c + 2 : 4 * c + 4]:
-            copy.wait()
-        for h in range(c * per, (c + 1) * per):
-            cols = pl.ds(h * HD, HD)
-            tail, head = states_of(kt_ref[h], qt_ref[h], v_ref[:, cols], g_ref[:, cols], *masks)
-            out_ref[0, h] = tail
-            out_ref[1, h] = head
+def states_of(copies, k_ref, q_ref, v_ref, g_ref, kt_ref, qt_ref, out_ref, tail_rows, head_rows, inv_root):
+    columns = [pl.ds(h * HD, HD) for h in range(out_ref.shape[1])]
+    for copy, ref, t_ref in zip(copies, (k_ref, q_ref), (kt_ref, qt_ref)):
+        copy.wait()
+        for h, cols in enumerate(columns):
+            t_ref[h] = ref[:, cols].T
+    copies[2].wait()
+    for h, cols in enumerate(columns):
+        out_ref[0, h] = dot(kt_ref[h], v_ref[:, cols] * tail_rows, (1, 0)).astype(BF16)
+    copies[3].wait()
+    for h, cols in enumerate(columns):
+        scaled = (g_ref[:, cols].astype(F32) * inv_root).astype(BF16)
+        out_ref[1, h] = dot(qt_ref[h], scaled * head_rows, (1, 0)).astype(BF16)
 
 
 def send_kernel(
     total,
-    chunks,
     len_hbm,
     q_hbm,
     k_hbm,
@@ -135,7 +123,7 @@
     len_pass = pltpu.make_async_copy(len_hbm, len_out, len_sems.at[1])
     len_pass.start()
     pairs = ((k_hbm, k_ref), (q_hbm, q_ref), (v_hbm, v_ref), (g_hbm, g_ref))
-    copies = bring(pairs, (1 - half_index()) * out_ref.shape[1], chunks, sems)
+    copies = bring(pairs, 1 - half_index(), sems)
     len_copy.wait()
     starts = doc_starts(len_ref)
     first = me * rows
@@ -146,8 +134,8 @@
     rows_ref[0] = tail_rows
     rows_ref[1] = head_rows
     root_ref[...] = inv_root
-    states_by_chunk(
-        copies, chunks, q_ref, k_ref, v_ref, g_ref, kt_ref, qt_ref, out_ref, (tail_rows, head_rows, inv_root)
+    states_of(
+        copies, k_ref, q_ref, v_ref, g_ref, kt_ref, qt_ref, out_ref, tail_rows, head_rows, inv_root
     )
     len_pass.wait()
 
@@ -209,7 +197,6 @@
 
 def keep_kernel(
     total,
-    chunks,
     len_hbm,
     q_hbm,
     k_hbm,
@@ -233,11 +220,11 @@
     len_copy = pltpu.make_async_copy(len_hbm, len_ref, len_sem)
     len_copy.start()
     pairs = ((k_hbm, k_ref), (q_hbm, q_ref), (v_hbm, v_ref), (g_hbm, g_ref))
-    copies = bring(pairs, half_index() * out_ref.shape[1], chunks, sems)
+    copies = bring(pairs, half_index(), sems)
     len_copy.wait()
     coefficients(doc_starts(len_ref), rows, total // rows, coef_ref)
     masks = rows_ref[0], rows_ref[1], root_ref[...]
-    states_by_chunk(copies, chunks, q_ref, k_ref, v_ref, g_ref, kt_ref, qt_ref, out_ref, masks)
+    states_of(copies, k_ref, q_ref, v_ref, g_ref, kt_ref, qt_ref, out_ref, *masks)
 
 
 def local_kernel(total, split, len_hbm, *refs):
@@ -478,9 +465,8 @@
         pltpu.with_memory_space_constraint(x, pltpu.HBM)
         for x in (doc_lengths, queries, keys, values, grad_out)
     )
-    chunks = 4
     doc_lengths, send, *others = call(
-        functools.partial(send_kernel, total, chunks),
+        functools.partial(send_kernel, total),
         "send",
         [shape(*doc_lengths.shape, dtype=jnp.int32), states]
         + [part] * 4
@@ -490,19 +476,19 @@
         [hbm] * 5,
         [hbm] + [vmem] * 9,
         flops=2 * half * product,
-        scratch=lengths[:1] + [pltpu.SemaphoreType.DMA((4, chunks)), pltpu.SemaphoreType.DMA((2,))],
+        scratch=lengths[:1] + [pltpu.SemaphoreType.DMA((4,)), pltpu.SemaphoreType.DMA((2,))],
     )
     q_other, k_other, v_other, g_other, kt_other, qt_other, row_masks, root = others
     swap = [(i, i ^ 1) for i in range(n)]
     got = lax.ppermute(send, "seq", swap)
     keep, *mines, table = call(
-        functools.partial(keep_kernel, total, chunks),
+        functools.partial(keep_kernel, total),
         "keep",
         [states] + [part] * 4 + [halves] * 2 + [shape(COEFS, HD, dtype=F32)],
         (doc_lengths, *arrays, row_masks, root),
         [hbm] * 5 + [vmem] * 2,
         flops=2 * half * product,
-        scratch=lengths[:1] + [pltpu.SemaphoreType.DMA((4, chunks))] + lengths[1:],
+        scratch=lengths[:1] + [pltpu.SemaphoreType.DMA((4,))] + lengths[1:],
     )
     q_mine, k_mine, v_mine, g_mine, kt_mine, qt_mine = mines
     mats = shape(heads, rows, HD)
@@ -569,7 +555,7 @@
     late_mine, late_other = post(1, range(PAIRS), masks)
     w, wt, dw, dwt, scaled = local
     fixed = (*mines[:3], *others[:3], scaled, w, wt, dw, dwt, masks, root)
-    chunks = 4
+    chunks = 2
     scratch = [pltpu.VMEM(part.shape, BF16)] * 2 + [
         pltpu.SemaphoreType.DMA((2,)),
         pltpu.SemaphoreType.DMA((chunks, 2)),

time: 30.3 us -> 29 us (0.957)
  Pallas kernels: 10.1 us -> 8.77 us
    pallas_call x11, Pallas kernels: 10.1 us -> 8.77 us  [call(): pl.pallas_call(kernel, in_specs=specs, out_specs=out_specs or [vmem] * le...]
  transfers between devices with their start and end apart: 16 -> 16, of which waited for: 3 -> 4; matrix products, arithmetic and copies ran while one was open for 0% -> 0% of each run, Pallas kernels for 21% -> 20%
where the time goes in v22:
time: 29 us; the launch traced here: 28.8 us
  starting transfers between devices  17.9 us (62%)
  Pallas kernels  8.77 us (30%)
  waiting for transfers between devices  1.47 us (5%)
  between operations  0.73 us (3%)
    ppermute x12, starting transfers between devices, trade(): lax.ppermute(parts[d], 'seq', [(i, i ^ STEPS[d]) for i in range(n)])  13.8 us
    pallas_call x11, Pallas kernels, call(): pl.pallas_call(kernel, in_specs=specs, out_specs=out_specs or [vmem] * le...  8.77 us
    ppermute x1, starting transfers between devices, per_device(): enter = lax.ppermute(edge(0), 'seq', up + down)  2.83 us
    ppermute x12, waiting for transfers between devices, trade(): lax.ppermute(parts[d], 'seq', [(i, i ^ STEPS[d]) for i in range(n)])  1.46 us
    ppermute x2, starting transfers between devices, post(): return (own, lax.ppermute(theirs, 'seq', swap))  0.68 us
  transfers between devices with their start and end apart: 16, of which 4 were waited for; matrix products, arithmetic and copies ran while one was open for 0% of the time, Pallas kernels for 20%

profile of v22, /device:TPU:0, one launch (start us, length us, event | category | flops | bytes accessed | tf_op | source)
XLA Modules:
  0.0 28.8 jit_solution(16004426948627642389)
XLA Ops:
  0.6 1.7 %send.1 = (s32[8]{0:T(128)S(1)}, bf16[2,8,128,128]{3,2,1,0:T(8,128)(2,1)S(1)}, bf16[128,1024]{1,0:T(8,128)(2,1)S(1)}, bf16[128,1024]{1,0:T(8,128)(2,1)S(1)}, bf1...) custom-call(s32[8]{0:T(128)} %len_hbm.1, ...), custom_call_target="tpu_custom_call" | custom-call | flops 67108864 | bytes 4325440 | tf_op jit(solution)/shard_map/send/pallas_call | solution.py:448
  2.4 0.5 %collective-permute-start = (bf16[2,8,128,128]{3,2,1,0:T(8,128)(2,1)S(1)}, bf16[2,8,128,128]{3,2,1,0:T(8,128)(2,1)S(1)}, u32[]{:S(2)}, u32[]{:S(2)}) collective-permute-start(bf16[2,8,128,128]{3,2,1,0:T(8,128)(2,1)S(1)} %get-tuple-element.71), channel_id=1, source_target_pairs={{0,1},{1,0},{2,3},{3,2},{4,5},{5,4},{6,7},{7,6},{8,9},{9,8},{10,11... | collective-permute-start | bytes 1572872 | tf_op jit(solution)/shard_map/ppermute | solution.py:483
  2.9 1.7 %keep.1 = (bf16[2,8,128,128]{3,2,1,0:T(8,128)(2,1)S(1)}, bf16[128,1024]{1,0:T(8,128)(2,1)S(1)}, bf16[128,1024]{1,0:T(8,128)(2,1)S(1)}, bf16[128,1024]{1,0:T(8,12...) custom-call(s32[8]{0:T(128)S(1)} %get-tuple-element.56.len_hbm, ...), custom_call_target="tpu_custom_call" | custom-call | flops 67108864 | bytes 4358176 | tf_op jit(solution)/shard_map/keep/pallas_call | solution.py:448
  4.6 0.0 collective-permute-done.got_ref
  4.6 0.2 pair.1
  4.8 3.8 %collective-permute-start.1 = (bf16[2,128,128]{2,1,0:T(8,128)(2,1)S(1)}, bf16[2,128,128]{2,1,0:T(8,128)(2,1)S(1)}, u32[]{:S(2)}, u32[]{:S(2)}) collective-permute-start(bf16[2,128,128]{2,1,0:T(8,128)(2,1)S(1)} %get-tuple-element.73), channel_id=1, source_target_pairs={{0,6},{1,7},{2,4},{3,5},{4,2},{5,3},{6,0},{7,1},{8,14},{9,15},{10,... | collective-permute-start | bytes 196616 | tf_op jit(solution)/shard_map/ppermute | solution.py:507
  8.6 0.2 collective-permute-start.2
  8.7 0.2 collective-permute-start.3
  8.9 2.8 %collective-permute-start.7 = (bf16[2,128,128]{2,1,0:T(8,128)(2,1)S(1)}, bf16[2,128,128]{2,1,0:T(8,128)(2,1)S(1)}, u32[]{:S(2)}, u32[]{:S(2)}) collective-permute-start(bf16[2,128,128]{2,1,0:T(8,128)(2,1)S(1)} %get-tuple-element.88), channel_id=1, source_target_pairs={{0,6},{1,7},{2,4},{3,5},{4,2},{5,3},{6,0},{7,1},{8,14},{9,15},{10,... | collective-permute-start | bytes 196616 | tf_op jit(solution)/shard_map/ppermute | solution.py:507
  11.8 0.4 %collective-permute-start.9 = (bf16[2,128,128]{2,1,0:T(8,128)(2,1)S(1)}, bf16[2,128,128]{2,1,0:T(8,128)(2,1)S(1)}, u32[]{:S(2)}, u32[]{:S(2)}) collective-permute-start(bf16[2,128,128]{2,1,0:T(8,128)(2,1)S(1)} %get-tuple-element.90), channel_id=1, source_target_pairs={{0,5},{1,4},{2,7},{3,6},{4,1},{5,0},{6,3},{7,2},{8,13},{9,12},{10,... | collective-permute-start | bytes 196616 | tf_op jit(solution)/shard_map/ppermute | solution.py:507
  12.2 0.6 %collective-permute-done.2.refs_2_.s2 = bf16[2,128,128]{2,1,0:T(8,128)(2,1)S(1)} collective-permute-done((bf16[2,128,128]{2,1,0:T(8,128)(2,1)S(1)}, bf16[2,128,128]{2,1,0:T(8,128)(2,1)S(1)}, u32[]{:S(2)}, u32[]{:S(2)}) %collective-permute-start.2) | collective-permute-done | bytes 65568 | tf_op jit(solution)/shard_map/ppermute | solution.py:507
  12.7 0.1 totals.1
  12.8 2.8 %collective-permute-start.10 = (bf16[2,128,128]{2,1,0:T(8,128)(2,1)S(1)}, bf16[2,128,128]{2,1,0:T(8,128)(2,1)S(1)}, u32[]{:S(2)}, u32[]{:S(2)}) collective-permute-start(bf16[2,128,128]{2,1,0:T(8,128)(2,1)S(1)} %totals.1), channel_id=1, source_target_pairs={{0,9},{1,8},{2,11},{3,10},{4,13},{5,12},{6,15},{7,14},{9,0},{8,1},... | collective-permute-start | bytes 196616 | tf_op jit(solution)/shard_map/ppermute | solution.py:529
  15.6 0.1 scan.2
  15.7 1.5 %collective-permute-start.4 = (bf16[2,128,128]{2,1,0:T(8,128)(2,1)S(1)}, bf16[2,128,128]{2,1,0:T(8,128)(2,1)S(1)}, u32[]{:S(2)}, u32[]{:S(2)}) collective-permute-start(bf16[2,128,128]{2,1,0:T(8,128)(2,1)S(1)} %get-tuple-element.77), channel_id=1, source_target_pairs={{0,6},{1,7},{2,4},{3,5},{4,2},{5,3},{6,0},{7,1},{8,14},{9,15},{10,... | collective-permute-start | bytes 196616 | tf_op jit(solution)/shard_map/ppermute | solution.py:507
  17.3 0.8 %collective-permute-start.5 = (bf16[2,128,128]{2,1,0:T(8,128)(2,1)S(1)}, bf16[2,128,128]{2,1,0:T(8,128)(2,1)S(1)}, u32[]{:S(2)}, u32[]{:S(2)}) collective-permute-start(bf16[2,128,128]{2,1,0:T(8,128)(2,1)S(1)} %get-tuple-element.78), channel_id=1, source_target_pairs={{0,3},{1,2},{2,1},{3,0},{4,7},{5,6},{6,5},{7,4},{8,11},{9,10},{10,... | collective-permute-start | bytes 196616 | tf_op jit(solution)/shard_map/ppermute | solution.py:507
  18.1 0.9 %collective-permute-start.6 = (bf16[2,128,128]{2,1,0:T(8,128)(2,1)S(1)}, bf16[2,128,128]{2,1,0:T(8,128)(2,1)S(1)}, u32[]{:S(2)}, u32[]{:S(2)}) collective-permute-start(bf16[2,128,128]{2,1,0:T(8,128)(2,1)S(1)} %get-tuple-element.79), channel_id=1, source_target_pairs={{0,5},{1,4},{2,7},{3,6},{4,1},{5,0},{6,3},{7,2},{8,13},{9,12},{10,... | collective-permute-start | bytes 196616 | tf_op jit(solution)/shard_map/ppermute | solution.py:507
  19.0 0.2 scan.3
  19.2 1.8 %collective-permute-start.11 = (bf16[2,128,128]{2,1,0:T(8,128)(2,1)S(1)}, bf16[2,128,128]{2,1,0:T(8,128)(2,1)S(1)}, u32[]{:S(2)}, u32[]{:S(2)}) collective-permute-start(bf16[2,128,128]{2,1,0:T(8,128)(2,1)S(1)} %get-tuple-element.92), channel_id=1, source_target_pairs={{0,6},{1,7},{2,4},{3,5},{4,2},{5,3},{6,0},{7,1},{8,14},{9,15},{10,... | collective-permute-start | bytes 196616 | tf_op jit(solution)/shard_map/ppermute | solution.py:507
  21.0 0.4 %collective-permute-start.12 = (bf16[2,128,128]{2,1,0:T(8,128)(2,1)S(1)}, bf16[2,128,128]{2,1,0:T(8,128)(2,1)S(1)}, u32[]{:S(2)}, u32[]{:S(2)}) collective-permute-start(bf16[2,128,128]{2,1,0:T(8,128)(2,1)S(1)} %get-tuple-element.93), channel_id=1, source_target_pairs={{0,3},{1,2},{2,1},{3,0},{4,7},{5,6},{6,5},{7,4},{8,11},{9,10},{10,... | collective-permute-start | bytes 196616 | tf_op jit(solution)/shard_map/ppermute | solution.py:507
  21.4 0.1 collective-permute-done.4.refs_1_
  21.4 1.0 %collective-permute-start.13 = (bf16[2,128,128]{2,1,0:T(8,128)(2,1)S(1)}, bf16[2,128,128]{2,1,0:T(8,128)(2,1)S(1)}, u32[]{:S(2)}, u32[]{:S(2)}) collective-permute-start(bf16[2,128,128]{2,1,0:T(8,128)(2,1)S(1)} %get-tuple-element.94), channel_id=1, source_target_pairs={{0,5},{1,4},{2,7},{3,6},{4,1},{5,0},{6,3},{7,2},{8,13},{9,12},{10,... | collective-permute-start | bytes 196616 | tf_op jit(solution)/shard_map/ppermute | solution.py:507
  22.5 0.0 collective-permute-done.5.refs_2_
  22.5 0.2 post.2
  22.7 0.3 collective-permute-start.15
  23.0 1.8 %local.1 = (bf16[16,128,128]{2,1,0:T(8,128)(2,1)S(1)}, bf16[16,128,128]{2,1,0:T(8,128)(2,1)S(1)}, bf16[16,128,128]{2,1,0:T(8,128)(2,1)S(1)}, bf16[16,128,128]{2,...) custom-call(s32[8]{0:T(128)S(1)} %get-tuple-element.56.len_hbm, ...), custom_call_target="tpu_custom_call" | custom-call | flops 134217728 | bytes 6160416 | tf_op jit(solution)/shard_map/local/pallas_call | solution.py:448
  24.8 0.7 %collective-permute-done.12.refs_2_ = bf16[2,128,128]{2,1,0:T(8,128)(2,1)S(1)} collective-permute-done((bf16[2,128,128]{2,1,0:T(8,128)(2,1)S(1)}, bf16[2,128,128]{2,1,0:T(8,128)(2,1)S(1)}, u32[]{:S(2)}, u32[]{:S(2)}) %collective-permute-start.12) | collective-permute-done | bytes 65568 | tf_op jit(solution)/shard_map/ppermute | solution.py:507
  25.6 0.1 collective-permute-done.13.refs_3_
  25.6 0.2 post.3
  25.9 0.4 %collective-permute-start.14 = (bf16[8,128,128]{2,1,0:T(8,128)(2,1)S(1)}, bf16[8,128,128]{2,1,0:T(8,128)(2,1)S(1)}, u32[]{:S(2)}, u32[]{:S(2)}) collective-permute-start(bf16[8,128,128]{2,1,0:T(8,128)(2,1)S(1)} %get-tuple-element.95), channel_id=1, source_target_pairs={{0,1},{1,0},{2,3},{3,2},{4,5},{5,4},{6,7},{7,6},{8,9},{9,8},{10,11... | collective-permute-start | bytes 786440 | tf_op jit(solution)/shard_map/ppermute | solution.py:543
  26.3 1.4 %middle.1 = (bf16[128,2048]{1,0:T(8,128)(2,1)}, bf16[128,2048]{1,0:T(8,128)(2,1)}, bf16[128,2048]{1,0:T(8,128)(2,1)}, bf16[128,2048]{1,0:T(8,128)(2,1)}, bf16[12...) custom-call(bf16[128,1024]{1,0:T(8,128)(2,1)S(1)} %get-tuple-element.98.refs_0_, ...), custom_call_target="tpu_custom_call" | custom-call | flops 268435456 | bytes 9043968 | tf_op jit(solution)/shard_map/middle/pallas_call | solution.py:448
  27.6 1.2 %last.1 = (bf16[128,2048]{1,0:T(8,128)(2,1)}, bf16[128,2048]{1,0:T(8,128)(2,1)}, bf16[128,2048]{1,0:T(8,128)(2,1)}, bf16[128,2048]{1,0:T(8,128)(2,1)}) custom-call(bf16[128,1024]{1,0:T(8,128)(2,1)S(1)} %get-tuple-element.59.refs_0_.refs_2_, ...), custom_call_target="tpu_custom_call", output_to_operand_aliasing={{0}: (18, {}), {1}: (19, {}), {2}: (20, {}), {3}: (21, {})} | custom-call | flops 134217728 | bytes 9830400 | tf_op jit(solution)/shard_map/last/pallas_call | solution.py:448
  (11 shorter events, 0.0 us)
Async XLA Ops:
  2.4 2.2 %collective-permute-start = (bf16[2,8,128,128]{3,2,1,0:T(8,128)(2,1)S(1)}, bf16[2,8,128,128]{3,2,1,0:T(8,128)(2,1)S(1)}, u32[]{:S(2)}, u32[]{:S(2)}) collective-permute-start(bf16[2,8,128,128]{3,2,1,0:T(8,128)(2,1)S(1)} %get-tuple-element.71), channel_id=1, source_target_pairs={{0,1},{1,0},{2,3},{3,2},{4,5},{5,4},{6,7},{7,6},{8,9},{9,8},{10,11... | collective-permute-start | bytes 1572872 | tf_op jit(solution)/shard_map/ppermute | solution.py:483
  4.8 7.0 %collective-permute-start.1 = (bf16[2,128,128]{2,1,0:T(8,128)(2,1)S(1)}, bf16[2,128,128]{2,1,0:T(8,128)(2,1)S(1)}, u32[]{:S(2)}, u32[]{:S(2)}) collective-permute-start(bf16[2,128,128]{2,1,0:T(8,128)(2,1)S(1)} %get-tuple-element.73), channel_id=1, source_target_pairs={{0,6},{1,7},{2,4},{3,5},{4,2},{5,3},{6,0},{7,1},{8,14},{9,15},{10,... | collective-permute-start | bytes 196616 | tf_op jit(solution)/shard_map/ppermute | solution.py:507
  8.6 4.2 %collective-permute-start.2 = (bf16[2,128,128]{2,1,0:T(8,128)(2,1)S(1)}, bf16[2,128,128]{2,1,0:T(8,128)(2,1)S(1)}, u32[]{:S(2)}, u32[]{:S(2)}) collective-permute-start(bf16[2,128,128]{2,1,0:T(8,128)(2,1)S(1)} %get-tuple-element.74), channel_id=1, source_target_pairs={{0,3},{1,2},{2,1},{3,0},{4,7},{5,6},{6,5},{7,4},{8,11},{9,10},{10,... | collective-permute-start | bytes 196616 | tf_op jit(solution)/shard_map/ppermute | solution.py:507
  8.7 4.0 %collective-permute-start.3 = (bf16[2,128,128]{2,1,0:T(8,128)(2,1)S(1)}, bf16[2,128,128]{2,1,0:T(8,128)(2,1)S(1)}, u32[]{:S(2)}, u32[]{:S(2)}) collective-permute-start(bf16[2,128,128]{2,1,0:T(8,128)(2,1)S(1)} %get-tuple-element.75), channel_id=1, source_target_pairs={{0,5},{1,4},{2,7},{3,6},{4,1},{5,0},{6,3},{7,2},{8,13},{9,12},{10,... | collective-permute-start | bytes 196616 | tf_op jit(solution)/shard_map/ppermute | solution.py:507
  8.9 8.3 %collective-permute-start.7 = (bf16[2,128,128]{2,1,0:T(8,128)(2,1)S(1)}, bf16[2,128,128]{2,1,0:T(8,128)(2,1)S(1)}, u32[]{:S(2)}, u32[]{:S(2)}) collective-permute-start(bf16[2,128,128]{2,1,0:T(8,128)(2,1)S(1)} %get-tuple-element.88), channel_id=1, source_target_pairs={{0,6},{1,7},{2,4},{3,5},{4,2},{5,3},{6,0},{7,1},{8,14},{9,15},{10,... | collective-permute-start | bytes 196616 | tf_op jit(solution)/shard_map/ppermute | solution.py:507
  11.8 6.3 %collective-permute-start.8 = (bf16[2,128,128]{2,1,0:T(8,128)(2,1)S(1)}, bf16[2,128,128]{2,1,0:T(8,128)(2,1)S(1)}, u32[]{:S(2)}, u32[]{:S(2)}) collective-permute-start(bf16[2,128,128]{2,1,0:T(8,128)(2,1)S(1)} %get-tuple-element.89), channel_id=1, source_target_pairs={{0,3},{1,2},{2,1},{3,0},{4,7},{5,6},{6,5},{7,4},{8,11},{9,10},{10,... | collective-permute-start | bytes 196616 | tf_op jit(solution)/shard_map/ppermute | solution.py:507
  11.8 7.2 %collective-permute-start.9 = (bf16[2,128,128]{2,1,0:T(8,128)(2,1)S(1)}, bf16[2,128,128]{2,1,0:T(8,128)(2,1)S(1)}, u32[]{:S(2)}, u32[]{:S(2)}) collective-permute-start(bf16[2,128,128]{2,1,0:T(8,128)(2,1)S(1)} %get-tuple-element.90), channel_id=1, source_target_pairs={{0,5},{1,4},{2,7},{3,6},{4,1},{5,0},{6,3},{7,2},{8,13},{9,12},{10,... | collective-permute-start | bytes 196616 | tf_op jit(solution)/shard_map/ppermute | solution.py:507
  12.8 6.2 %collective-permute-start.10 = (bf16[2,128,128]{2,1,0:T(8,128)(2,1)S(1)}, bf16[2,128,128]{2,1,0:T(8,128)(2,1)S(1)}, u32[]{:S(2)}, u32[]{:S(2)}) collective-permute-start(bf16[2,128,128]{2,1,0:T(8,128)(2,1)S(1)} %totals.1), channel_id=1, source_target_pairs={{0,9},{1,8},{2,11},{3,10},{4,13},{5,12},{6,15},{7,14},{9,0},{8,1},... | collective-permute-start | bytes 196616 | tf_op jit(solution)/shard_map/ppermute | solution.py:529
  15.7 5.7 %collective-permute-start.4 = (bf16[2,128,128]{2,1,0:T(8,128)(2,1)S(1)}, bf16[2,128,128]{2,1,0:T(8,128)(2,1)S(1)}, u32[]{:S(2)}, u32[]{:S(2)}) collective-permute-start(bf16[2,128,128]{2,1,0:T(8,128)(2,1)S(1)} %get-tuple-element.77), channel_id=1, source_target_pairs={{0,6},{1,7},{2,4},{3,5},{4,2},{5,3},{6,0},{7,1},{8,14},{9,15},{10,... | collective-permute-start | bytes 196616 | tf_op jit(solution)/shard_map/ppermute | solution.py:507
  17.3 5.2 %collective-permute-start.5 = (bf16[2,128,128]{2,1,0:T(8,128)(2,1)S(1)}, bf16[2,128,128]{2,1,0:T(8,128)(2,1)S(1)}, u32[]{:S(2)}, u32[]{:S(2)}) collective-permute-start(bf16[2,128,128]{2,1,0:T(8,128)(2,1)S(1)} %get-tuple-element.78), channel_id=1, source_target_pairs={{0,3},{1,2},{2,1},{3,0},{4,7},{5,6},{6,5},{7,4},{8,11},{9,10},{10,... | collective-permute-start | bytes 196616 | tf_op jit(solution)/shard_map/ppermute | solution.py:507
  18.1 4.4 %collective-permute-start.6 = (bf16[2,128,128]{2,1,0:T(8,128)(2,1)S(1)}, bf16[2,128,128]{2,1,0:T(8,128)(2,1)S(1)}, u32[]{:S(2)}, u32[]{:S(2)}) collective-permute-start(bf16[2,128,128]{2,1,0:T(8,128)(2,1)S(1)} %get-tuple-element.79), channel_id=1, source_target_pairs={{0,5},{1,4},{2,7},{3,6},{4,1},{5,0},{6,3},{7,2},{8,13},{9,12},{10,... | collective-permute-start | bytes 196616 | tf_op jit(solution)/shard_map/ppermute | solution.py:507
  19.2 5.6 %collective-permute-start.11 = (bf16[2,128,128]{2,1,0:T(8,128)(2,1)S(1)}, bf16[2,128,128]{2,1,0:T(8,128)(2,1)S(1)}, u32[]{:S(2)}, u32[]{:S(2)}) collective-permute-start(bf16[2,128,128]{2,1,0:T(8,128)(2,1)S(1)} %get-tuple-element.92), channel_id=1, source_target_pairs={{0,6},{1,7},{2,4},{3,5},{4,2},{5,3},{6,0},{7,1},{8,14},{9,15},{10,... | collective-permute-start | bytes 196616 | tf_op jit(solution)/shard_map/ppermute | solution.py:507
  21.0 4.5 %collective-permute-start.12 = (bf16[2,128,128]{2,1,0:T(8,128)(2,1)S(1)}, bf16[2,128,128]{2,1,0:T(8,128)(2,1)S(1)}, u32[]{:S(2)}, u32[]{:S(2)}) collective-permute-start(bf16[2,128,128]{2,1,0:T(8,128)(2,1)S(1)} %get-tuple-element.93), channel_id=1, source_target_pairs={{0,3},{1,2},{2,1},{3,0},{4,7},{5,6},{6,5},{7,4},{8,11},{9,10},{10,... | collective-permute-start | bytes 196616 | tf_op jit(solution)/shard_map/ppermute | solution.py:507
  21.4 4.2 %collective-permute-start.13 = (bf16[2,128,128]{2,1,0:T(8,128)(2,1)S(1)}, bf16[2,128,128]{2,1,0:T(8,128)(2,1)S(1)}, u32[]{:S(2)}, u32[]{:S(2)}) collective-permute-start(bf16[2,128,128]{2,1,0:T(8,128)(2,1)S(1)} %get-tuple-element.94), channel_id=1, source_target_pairs={{0,5},{1,4},{2,7},{3,6},{4,1},{5,0},{6,3},{7,2},{8,13},{9,12},{10,... | collective-permute-start | bytes 196616 | tf_op jit(solution)/shard_map/ppermute | solution.py:507
  22.7 3.5 %collective-permute-start.15 = (bf16[8,128,128]{2,1,0:T(8,128)(2,1)S(1)}, bf16[8,128,128]{2,1,0:T(8,128)(2,1)S(1)}, u32[]{:S(2)}, u32[]{:S(2)}) collective-permute-start(bf16[8,128,128]{2,1,0:T(8,128)(2,1)S(1)} %get-tuple-element.100), channel_id=1, source_target_pairs={{0,1},{1,0},{2,3},{3,2},{4,5},{5,4},{6,7},{7,6},{8,9},{9,8},{10,11... | collective-permute-start | bytes 786440 | tf_op jit(solution)/shard_map/ppermute | solution.py:543
  25.9 1.8 %collective-permute-start.14 = (bf16[8,128,128]{2,1,0:T(8,128)(2,1)S(1)}, bf16[8,128,128]{2,1,0:T(8,128)(2,1)S(1)}, u32[]{:S(2)}, u32[]{:S(2)}) collective-permute-start(bf16[8,128,128]{2,1,0:T(8,128)(2,1)S(1)} %get-tuple-element.95), channel_id=1, source_target_pairs={{0,1},{1,0},{2,3},{3,2},{4,5},{5,4},{6,7},{7,6},{8,9},{9,8},{10,11... | collective-permute-start | bytes 786440 | tf_op jit(solution)/shard_map/ppermute | solution.py:543

commit v23 on v22

--- a/solution.py
+++ b/solution.py
@@ -277,17 +277,21 @@
     return upper if which == 0 else 1 - upper
 
 
+def flag(coef_ref, row):
+    return jnp.broadcast_to(coef(coef_ref, row), (HD, HD)).astype(BF16)
+
+
 def pair_kernel(split, coef_ref, keep_ref, got_ref, *out_refs):
     per = out_refs[0].shape[0]
     pair = lax.rem(lax.axis_index("seq"), TEAM) // 2
     for which in range(2):
         kind = kind_of(which, split)
-        ca, cb = coef(coef_ref, KEEP_F + 2 * kind), coef(coef_ref, GOT_F + 2 * kind)
+        ca, cb = flag(coef_ref, KEEP_F + 2 * kind), flag(coef_ref, GOT_F + 2 * kind)
         for d in range(PAIRS):
             for i in range(per):
                 h = (pair ^ PARTNERS[d]) * per + i
-                both = keep_ref[kind, h].astype(F32) * ca + got_ref[kind, h].astype(F32) * cb
-                out_refs[which * PAIRS + d][i] = both.astype(BF16)
+                both = keep_ref[kind, h] * ca + got_ref[kind, h] * cb
+                out_refs[which * PAIRS + d][i] = both
 
 
 def totals_kernel(which, split, coef_ref, s0, s1, s2, s3, out_ref):
@@ -317,14 +321,14 @@
     per = refs[0].shape[0]
     pair = lax.rem(lax.axis_index("seq"), TEAM) // 2
     kind = kind_of(which, split)
-    m0, m1 = coef(coef_ref, MINE_F + 2 * kind), coef(coef_ref, MINE_F + 2 * kind + 1)
-    t0, t1 = coef(coef_ref, THEIRS_F + 2 * kind), coef(coef_ref, THEIRS_F + 2 * kind + 1)
+    m0, m1 = flag(coef_ref, MINE_F + 2 * kind), flag(coef_ref, MINE_F + 2 * kind + 1)
+    t0, t1 = flag(coef_ref, THEIRS_F + 2 * kind), flag(coef_ref, THEIRS_F + 2 * kind + 1)
     for ref, d in zip(refs, order):
         for i in range(per):
             h = (pair ^ PARTNERS[d]) * per + i
-            came = ref[i].astype(F32)
-            theirs_ref[h] = (came * t0 + keep_ref[kind, h].astype(F32) * t1).astype(BF16)
-            mine_ref[h] = (came * m0 + got_ref[kind, h].astype(F32) * m1).astype(BF16)
+            came = ref[i]
+            theirs_ref[h] = came * t0 + keep_ref[kind, h] * t1
+            mine_ref[h] = came * m0 + got_ref[kind, h] * m1
 
 
 def on_kind(which, split, run):

time: 29 us -> 28.8 us (level)
  transfers between devices with their start and end apart: 16 -> 16, of which waited for: 4 -> 4; matrix products, arithmetic and copies ran while one was open for 0% -> 0% of each run, Pallas kernels for 20% -> 19%
where the time goes in v23:
time: 28.8 us; the launch traced here: 28.7 us
  starting transfers between devices  17.9 us (62%)
  Pallas kernels  8.51 us (30%)
  waiting for transfers between devices  1.56 us (5%)
  between operations  0.73 us (3%)
    ppermute x12, starting transfers between devices, trade(): lax.ppermute(parts[d], 'seq', [(i, i ^ STEPS[d]) for i in range(n)])  13.8 us
    pallas_call x11, Pallas kernels, call(): pl.pallas_call(kernel, in_specs=specs, out_specs=out_specs or [vmem] * le...  8.51 us
    ppermute x1, starting transfers between devices, per_device(): enter = lax.ppermute(edge(0), 'seq', up + down)  2.83 us
    ppermute x12, waiting for transfers between devices, trade(): lax.ppermute(parts[d], 'seq', [(i, i ^ STEPS[d]) for i in range(n)])  1.55 us
    ppermute x2, starting transfers between devices, post(): return (own, lax.ppermute(theirs, 'seq', swap))  0.69 us
  transfers between devices with their start and end apart: 16, of which 4 were waited for; matrix products, arithmetic and copies ran while one was open for 0% of the time, Pallas kernels for 19%

profile of v23, /device:TPU:0, one launch (start us, length us, event | category | flops | bytes accessed | tf_op | source)
XLA Modules:
  0.0 28.7 jit_solution(8902940143570786762)
XLA Ops:
  0.6 1.7 %send.1 = (s32[8]{0:T(128)S(1)}, bf16[2,8,128,128]{3,2,1,0:T(8,128)(2,1)S(1)}, bf16[128,1024]{1,0:T(8,128)(2,1)S(1)}, bf16[128,1024]{1,0:T(8,128)(2,1)S(1)}, bf1...) custom-call(s32[8]{0:T(128)} %len_hbm.1, ...), custom_call_target="tpu_custom_call" | custom-call | flops 67108864 | bytes 4325440 | tf_op jit(solution)/shard_map/send/pallas_call | solution.py:452
  2.4 0.5 %collective-permute-start = (bf16[2,8,128,128]{3,2,1,0:T(8,128)(2,1)S(1)}, bf16[2,8,128,128]{3,2,1,0:T(8,128)(2,1)S(1)}, u32[]{:S(2)}, u32[]{:S(2)}) collective-permute-start(bf16[2,8,128,128]{3,2,1,0:T(8,128)(2,1)S(1)} %get-tuple-element.71), channel_id=1, source_target_pairs={{0,1},{1,0},{2,3},{3,2},{4,5},{5,4},{6,7},{7,6},{8,9},{9,8},{10,11... | collective-permute-start | bytes 1572872 | tf_op jit(solution)/shard_map/ppermute | solution.py:487
  2.9 1.7 %keep.1 = (bf16[2,8,128,128]{3,2,1,0:T(8,128)(2,1)S(1)}, bf16[128,1024]{1,0:T(8,128)(2,1)S(1)}, bf16[128,1024]{1,0:T(8,128)(2,1)S(1)}, bf16[128,1024]{1,0:T(8,12...) custom-call(s32[8]{0:T(128)S(1)} %get-tuple-element.56.len_hbm, ...), custom_call_target="tpu_custom_call" | custom-call | flops 67108864 | bytes 4358176 | tf_op jit(solution)/shard_map/keep/pallas_call | solution.py:452
  4.6 0.1 pair.1
  4.7 3.8 %collective-permute-start.1 = (bf16[2,128,128]{2,1,0:T(8,128)(2,1)S(1)}, bf16[2,128,128]{2,1,0:T(8,128)(2,1)S(1)}, u32[]{:S(2)}, u32[]{:S(2)}) collective-permute-start(bf16[2,128,128]{2,1,0:T(8,128)(2,1)S(1)} %get-tuple-element.73), channel_id=1, source_target_pairs={{0,6},{1,7},{2,4},{3,5},{4,2},{5,3},{6,0},{7,1},{8,14},{9,15},{10,... | collective-permute-start | bytes 196616 | tf_op jit(solution)/shard_map/ppermute | solution.py:511
  8.5 0.2 collective-permute-start.2
  8.7 0.2 collective-permute-start.3
  8.9 2.8 %collective-permute-start.7 = (bf16[2,128,128]{2,1,0:T(8,128)(2,1)S(1)}, bf16[2,128,128]{2,1,0:T(8,128)(2,1)S(1)}, u32[]{:S(2)}, u32[]{:S(2)}) collective-permute-start(bf16[2,128,128]{2,1,0:T(8,128)(2,1)S(1)} %get-tuple-element.88), channel_id=1, source_target_pairs={{0,6},{1,7},{2,4},{3,5},{4,2},{5,3},{6,0},{7,1},{8,14},{9,15},{10,... | collective-permute-start | bytes 196616 | tf_op jit(solution)/shard_map/ppermute | solution.py:511
  11.7 0.0 collective-permute-start.8
  11.7 0.4 %collective-permute-start.9 = (bf16[2,128,128]{2,1,0:T(8,128)(2,1)S(1)}, bf16[2,128,128]{2,1,0:T(8,128)(2,1)S(1)}, u32[]{:S(2)}, u32[]{:S(2)}) collective-permute-start(bf16[2,128,128]{2,1,0:T(8,128)(2,1)S(1)} %get-tuple-element.90), channel_id=1, source_target_pairs={{0,5},{1,4},{2,7},{3,6},{4,1},{5,0},{6,3},{7,2},{8,13},{9,12},{10,... | collective-permute-start | bytes 196616 | tf_op jit(solution)/shard_map/ppermute | solution.py:511
  12.1 0.6 %collective-permute-done.2.refs_2_.s2 = bf16[2,128,128]{2,1,0:T(8,128)(2,1)S(1)} collective-permute-done((bf16[2,128,128]{2,1,0:T(8,128)(2,1)S(1)}, bf16[2,128,128]{2,1,0:T(8,128)(2,1)S(1)}, u32[]{:S(2)}, u32[]{:S(2)}) %collective-permute-start.2) | collective-permute-done | bytes 65568 | tf_op jit(solution)/shard_map/ppermute | solution.py:511
  12.7 0.1 totals.1
  12.7 2.8 %collective-permute-start.10 = (bf16[2,128,128]{2,1,0:T(8,128)(2,1)S(1)}, bf16[2,128,128]{2,1,0:T(8,128)(2,1)S(1)}, u32[]{:S(2)}, u32[]{:S(2)}) collective-permute-start(bf16[2,128,128]{2,1,0:T(8,128)(2,1)S(1)} %totals.1), channel_id=1, source_target_pairs={{0,9},{1,8},{2,11},{3,10},{4,13},{5,12},{6,15},{7,14},{9,0},{8,1},... | collective-permute-start | bytes 196616 | tf_op jit(solution)/shard_map/ppermute | solution.py:533
  15.6 0.1 scan.2
  15.7 1.5 %collective-permute-start.4 = (bf16[2,128,128]{2,1,0:T(8,128)(2,1)S(1)}, bf16[2,128,128]{2,1,0:T(8,128)(2,1)S(1)}, u32[]{:S(2)}, u32[]{:S(2)}) collective-permute-start(bf16[2,128,128]{2,1,0:T(8,128)(2,1)S(1)} %get-tuple-element.77), channel_id=1, source_target_pairs={{0,6},{1,7},{2,4},{3,5},{4,2},{5,3},{6,0},{7,1},{8,14},{9,15},{10,... | collective-permute-start | bytes 196616 | tf_op jit(solution)/shard_map/ppermute | solution.py:511
  17.2 0.8 %collective-permute-start.5 = (bf16[2,128,128]{2,1,0:T(8,128)(2,1)S(1)}, bf16[2,128,128]{2,1,0:T(8,128)(2,1)S(1)}, u32[]{:S(2)}, u32[]{:S(2)}) collective-permute-start(bf16[2,128,128]{2,1,0:T(8,128)(2,1)S(1)} %get-tuple-element.78), channel_id=1, source_target_pairs={{0,3},{1,2},{2,1},{3,0},{4,7},{5,6},{6,5},{7,4},{8,11},{9,10},{10,... | collective-permute-start | bytes 196616 | tf_op jit(solution)/shard_map/ppermute | solution.py:511
  18.0 0.9 %collective-permute-start.6 = (bf16[2,128,128]{2,1,0:T(8,128)(2,1)S(1)}, bf16[2,128,128]{2,1,0:T(8,128)(2,1)S(1)}, u32[]{:S(2)}, u32[]{:S(2)}) collective-permute-start(bf16[2,128,128]{2,1,0:T(8,128)(2,1)S(1)} %get-tuple-element.79), channel_id=1, source_target_pairs={{0,5},{1,4},{2,7},{3,6},{4,1},{5,0},{6,3},{7,2},{8,13},{9,12},{10,... | collective-permute-start | bytes 196616 | tf_op jit(solution)/shard_map/ppermute | solution.py:511
  19.0 0.2 scan.3
  19.1 1.8 %collective-permute-start.11 = (bf16[2,128,128]{2,1,0:T(8,128)(2,1)S(1)}, bf16[2,128,128]{2,1,0:T(8,128)(2,1)S(1)}, u32[]{:S(2)}, u32[]{:S(2)}) collective-permute-start(bf16[2,128,128]{2,1,0:T(8,128)(2,1)S(1)} %get-tuple-element.92), channel_id=1, source_target_pairs={{0,6},{1,7},{2,4},{3,5},{4,2},{5,3},{6,0},{7,1},{8,14},{9,15},{10,... | collective-permute-start | bytes 196616 | tf_op jit(solution)/shard_map/ppermute | solution.py:511
  21.0 0.4 %collective-permute-start.12 = (bf16[2,128,128]{2,1,0:T(8,128)(2,1)S(1)}, bf16[2,128,128]{2,1,0:T(8,128)(2,1)S(1)}, u32[]{:S(2)}, u32[]{:S(2)}) collective-permute-start(bf16[2,128,128]{2,1,0:T(8,128)(2,1)S(1)} %get-tuple-element.93), channel_id=1, source_target_pairs={{0,3},{1,2},{2,1},{3,0},{4,7},{5,6},{6,5},{7,4},{8,11},{9,10},{10,... | collective-permute-start | bytes 196616 | tf_op jit(solution)/shard_map/ppermute | solution.py:511
  21.3 0.1 collective-permute-done.4.refs_1_
  21.4 1.0 %collective-permute-start.13 = (bf16[2,128,128]{2,1,0:T(8,128)(2,1)S(1)}, bf16[2,128,128]{2,1,0:T(8,128)(2,1)S(1)}, u32[]{:S(2)}, u32[]{:S(2)}) collective-permute-start(bf16[2,128,128]{2,1,0:T(8,128)(2,1)S(1)} %get-tuple-element.94), channel_id=1, source_target_pairs={{0,5},{1,4},{2,7},{3,6},{4,1},{5,0},{6,3},{7,2},{8,13},{9,12},{10,... | collective-permute-start | bytes 196616 | tf_op jit(solution)/shard_map/ppermute | solution.py:511
  22.4 0.0 collective-permute-done.5.refs_2_
  22.4 0.1 post.2
  22.6 0.3 collective-permute-start.15
  22.9 1.8 %local.1 = (bf16[16,128,128]{2,1,0:T(8,128)(2,1)S(1)}, bf16[16,128,128]{2,1,0:T(8,128)(2,1)S(1)}, bf16[16,128,128]{2,1,0:T(8,128)(2,1)S(1)}, bf16[16,128,128]{2,...) custom-call(s32[8]{0:T(128)S(1)} %get-tuple-element.56.len_hbm, ...), custom_call_target="tpu_custom_call" | custom-call | flops 134217728 | bytes 6160416 | tf_op jit(solution)/shard_map/local/pallas_call | solution.py:452
  24.7 0.8 %collective-permute-done.12.refs_2_ = bf16[2,128,128]{2,1,0:T(8,128)(2,1)S(1)} collective-permute-done((bf16[2,128,128]{2,1,0:T(8,128)(2,1)S(1)}, bf16[2,128,128]{2,1,0:T(8,128)(2,1)S(1)}, u32[]{:S(2)}, u32[]{:S(2)}) %collective-permute-start.12) | collective-permute-done | bytes 65568 | tf_op jit(solution)/shard_map/ppermute | solution.py:511
  25.5 0.1 collective-permute-done.13.refs_3_
  25.6 0.1 post.3
  25.7 0.4 %collective-permute-start.14 = (bf16[8,128,128]{2,1,0:T(8,128)(2,1)S(1)}, bf16[8,128,128]{2,1,0:T(8,128)(2,1)S(1)}, u32[]{:S(2)}, u32[]{:S(2)}) collective-permute-start(bf16[8,128,128]{2,1,0:T(8,128)(2,1)S(1)} %get-tuple-element.95), channel_id=1, source_target_pairs={{0,1},{1,0},{2,3},{3,2},{4,5},{5,4},{6,7},{7,6},{8,9},{9,8},{10,11... | collective-permute-start | bytes 786440 | tf_op jit(solution)/shard_map/ppermute | solution.py:547
  26.1 1.3 %middle.1 = (bf16[128,2048]{1,0:T(8,128)(2,1)}, bf16[128,2048]{1,0:T(8,128)(2,1)}, bf16[128,2048]{1,0:T(8,128)(2,1)}, bf16[128,2048]{1,0:T(8,128)(2,1)}, bf16[12...) custom-call(bf16[128,1024]{1,0:T(8,128)(2,1)S(1)} %get-tuple-element.98.refs_0_, ...), custom_call_target="tpu_custom_call" | custom-call | flops 268435456 | bytes 9043968 | tf_op jit(solution)/shard_map/middle/pallas_call | solution.py:452
  27.5 1.2 %last.1 = (bf16[128,2048]{1,0:T(8,128)(2,1)}, bf16[128,2048]{1,0:T(8,128)(2,1)}, bf16[128,2048]{1,0:T(8,128)(2,1)}, bf16[128,2048]{1,0:T(8,128)(2,1)}) custom-call(bf16[128,1024]{1,0:T(8,128)(2,1)S(1)} %get-tuple-element.59.refs_0_.refs_2_, ...), custom_call_target="tpu_custom_call", output_to_operand_aliasing={{0}: (18, {}), {1}: (19, {}), {2}: (20, {}), {3}: (21, {})} | custom-call | flops 134217728 | bytes 9830400 | tf_op jit(solution)/shard_map/last/pallas_call | solution.py:452
  (11 shorter events, 0.0 us)
Async XLA Ops:
  2.4 2.2 %collective-permute-start = (bf16[2,8,128,128]{3,2,1,0:T(8,128)(2,1)S(1)}, bf16[2,8,128,128]{3,2,1,0:T(8,128)(2,1)S(1)}, u32[]{:S(2)}, u32[]{:S(2)}) collective-permute-start(bf16[2,8,128,128]{3,2,1,0:T(8,128)(2,1)S(1)} %get-tuple-element.71), channel_id=1, source_target_pairs={{0,1},{1,0},{2,3},{3,2},{4,5},{5,4},{6,7},{7,6},{8,9},{9,8},{10,11... | collective-permute-start | bytes 1572872 | tf_op jit(solution)/shard_map/ppermute | solution.py:487
  4.7 7.0 %collective-permute-start.1 = (bf16[2,128,128]{2,1,0:T(8,128)(2,1)S(1)}, bf16[2,128,128]{2,1,0:T(8,128)(2,1)S(1)}, u32[]{:S(2)}, u32[]{:S(2)}) collective-permute-start(bf16[2,128,128]{2,1,0:T(8,128)(2,1)S(1)} %get-tuple-element.73), channel_id=1, source_target_pairs={{0,6},{1,7},{2,4},{3,5},{4,2},{5,3},{6,0},{7,1},{8,14},{9,15},{10,... | collective-permute-start | bytes 196616 | tf_op jit(solution)/shard_map/ppermute | solution.py:511
  8.5 4.2 %collective-permute-start.2 = (bf16[2,128,128]{2,1,0:T(8,128)(2,1)S(1)}, bf16[2,128,128]{2,1,0:T(8,128)(2,1)S(1)}, u32[]{:S(2)}, u32[]{:S(2)}) collective-permute-start(bf16[2,128,128]{2,1,0:T(8,128)(2,1)S(1)} %get-tuple-element.74), channel_id=1, source_target_pairs={{0,3},{1,2},{2,1},{3,0},{4,7},{5,6},{6,5},{7,4},{8,11},{9,10},{10,... | collective-permute-start | bytes 196616 | tf_op jit(solution)/shard_map/ppermute | solution.py:511
  8.7 4.0 %collective-permute-start.3 = (bf16[2,128,128]{2,1,0:T(8,128)(2,1)S(1)}, bf16[2,128,128]{2,1,0:T(8,128)(2,1)S(1)}, u32[]{:S(2)}, u32[]{:S(2)}) collective-permute-start(bf16[2,128,128]{2,1,0:T(8,128)(2,1)S(1)} %get-tuple-element.75), channel_id=1, source_target_pairs={{0,5},{1,4},{2,7},{3,6},{4,1},{5,0},{6,3},{7,2},{8,13},{9,12},{10,... | collective-permute-start | bytes 196616 | tf_op jit(solution)/shard_map/ppermute | solution.py:511
  8.9 8.3 %collective-permute-start.7 = (bf16[2,128,128]{2,1,0:T(8,128)(2,1)S(1)}, bf16[2,128,128]{2,1,0:T(8,128)(2,1)S(1)}, u32[]{:S(2)}, u32[]{:S(2)}) collective-permute-start(bf16[2,128,128]{2,1,0:T(8,128)(2,1)S(1)} %get-tuple-element.88), channel_id=1, source_target_pairs={{0,6},{1,7},{2,4},{3,5},{4,2},{5,3},{6,0},{7,1},{8,14},{9,15},{10,... | collective-permute-start | bytes 196616 | tf_op jit(solution)/shard_map/ppermute | solution.py:511
  11.7 6.3 %collective-permute-start.8 = (bf16[2,128,128]{2,1,0:T(8,128)(2,1)S(1)}, bf16[2,128,128]{2,1,0:T(8,128)(2,1)S(1)}, u32[]{:S(2)}, u32[]{:S(2)}) collective-permute-start(bf16[2,128,128]{2,1,0:T(8,128)(2,1)S(1)} %get-tuple-element.89), channel_id=1, source_target_pairs={{0,3},{1,2},{2,1},{3,0},{4,7},{5,6},{6,5},{7,4},{8,11},{9,10},{10,... | collective-permute-start | bytes 196616 | tf_op jit(solution)/shard_map/ppermute | solution.py:511
  11.7 7.2 %collective-permute-start.9 = (bf16[2,128,128]{2,1,0:T(8,128)(2,1)S(1)}, bf16[2,128,128]{2,1,0:T(8,128)(2,1)S(1)}, u32[]{:S(2)}, u32[]{:S(2)}) collective-permute-start(bf16[2,128,128]{2,1,0:T(8,128)(2,1)S(1)} %get-tuple-element.90), channel_id=1, source_target_pairs={{0,5},{1,4},{2,7},{3,6},{4,1},{5,0},{6,3},{7,2},{8,13},{9,12},{10,... | collective-permute-start | bytes 196616 | tf_op jit(solution)/shard_map/ppermute | solution.py:511
  12.7 6.2 %collective-permute-start.10 = (bf16[2,128,128]{2,1,0:T(8,128)(2,1)S(1)}, bf16[2,128,128]{2,1,0:T(8,128)(2,1)S(1)}, u32[]{:S(2)}, u32[]{:S(2)}) collective-permute-start(bf16[2,128,128]{2,1,0:T(8,128)(2,1)S(1)} %totals.1), channel_id=1, source_target_pairs={{0,9},{1,8},{2,11},{3,10},{4,13},{5,12},{6,15},{7,14},{9,0},{8,1},... | collective-permute-start | bytes 196616 | tf_op jit(solution)/shard_map/ppermute | solution.py:533
  15.7 5.7 %collective-permute-start.4 = (bf16[2,128,128]{2,1,0:T(8,128)(2,1)S(1)}, bf16[2,128,128]{2,1,0:T(8,128)(2,1)S(1)}, u32[]{:S(2)}, u32[]{:S(2)}) collective-permute-start(bf16[2,128,128]{2,1,0:T(8,128)(2,1)S(1)} %get-tuple-element.77), channel_id=1, source_target_pairs={{0,6},{1,7},{2,4},{3,5},{4,2},{5,3},{6,0},{7,1},{8,14},{9,15},{10,... | collective-permute-start | bytes 196616 | tf_op jit(solution)/shard_map/ppermute | solution.py:511
  17.2 5.2 %collective-permute-start.5 = (bf16[2,128,128]{2,1,0:T(8,128)(2,1)S(1)}, bf16[2,128,128]{2,1,0:T(8,128)(2,1)S(1)}, u32[]{:S(2)}, u32[]{:S(2)}) collective-permute-start(bf16[2,128,128]{2,1,0:T(8,128)(2,1)S(1)} %get-tuple-element.78), channel_id=1, source_target_pairs={{0,3},{1,2},{2,1},{3,0},{4,7},{5,6},{6,5},{7,4},{8,11},{9,10},{10,... | collective-permute-start | bytes 196616 | tf_op jit(solution)/shard_map/ppermute | solution.py:511
  18.0 4.4 %collective-permute-start.6 = (bf16[2,128,128]{2,1,0:T(8,128)(2,1)S(1)}, bf16[2,128,128]{2,1,0:T(8,128)(2,1)S(1)}, u32[]{:S(2)}, u32[]{:S(2)}) collective-permute-start(bf16[2,128,128]{2,1,0:T(8,128)(2,1)S(1)} %get-tuple-element.79), channel_id=1, source_target_pairs={{0,5},{1,4},{2,7},{3,6},{4,1},{5,0},{6,3},{7,2},{8,13},{9,12},{10,... | collective-permute-start | bytes 196616 | tf_op jit(solution)/shard_map/ppermute | solution.py:511
  19.1 5.5 %collective-permute-start.11 = (bf16[2,128,128]{2,1,0:T(8,128)(2,1)S(1)}, bf16[2,128,128]{2,1,0:T(8,128)(2,1)S(1)}, u32[]{:S(2)}, u32[]{:S(2)}) collective-permute-start(bf16[2,128,128]{2,1,0:T(8,128)(2,1)S(1)} %get-tuple-element.92), channel_id=1, source_target_pairs={{0,6},{1,7},{2,4},{3,5},{4,2},{5,3},{6,0},{7,1},{8,14},{9,15},{10,... | collective-permute-start | bytes 196616 | tf_op jit(solution)/shard_map/ppermute | solution.py:511
  21.0 4.5 %collective-permute-start.12 = (bf16[2,128,128]{2,1,0:T(8,128)(2,1)S(1)}, bf16[2,128,128]{2,1,0:T(8,128)(2,1)S(1)}, u32[]{:S(2)}, u32[]{:S(2)}) collective-permute-start(bf16[2,128,128]{2,1,0:T(8,128)(2,1)S(1)} %get-tuple-element.93), channel_id=1, source_target_pairs={{0,3},{1,2},{2,1},{3,0},{4,7},{5,6},{6,5},{7,4},{8,11},{9,10},{10,... | collective-permute-start | bytes 196616 | tf_op jit(solution)/shard_map/ppermute | solution.py:511
  21.4 4.2 %collective-permute-start.13 = (bf16[2,128,128]{2,1,0:T(8,128)(2,1)S(1)}, bf16[2,128,128]{2,1,0:T(8,128)(2,1)S(1)}, u32[]{:S(2)}, u32[]{:S(2)}) collective-permute-start(bf16[2,128,128]{2,1,0:T(8,128)(2,1)S(1)} %get-tuple-element.94), channel_id=1, source_target_pairs={{0,5},{1,4},{2,7},{3,6},{4,1},{5,0},{6,3},{7,2},{8,13},{9,12},{10,... | collective-permute-start | bytes 196616 | tf_op jit(solution)/shard_map/ppermute | solution.py:511
  22.6 3.5 %collective-permute-start.15 = (bf16[8,128,128]{2,1,0:T(8,128)(2,1)S(1)}, bf16[8,128,128]{2,1,0:T(8,128)(2,1)S(1)}, u32[]{:S(2)}, u32[]{:S(2)}) collective-permute-start(bf16[8,128,128]{2,1,0:T(8,128)(2,1)S(1)} %get-tuple-element.100), channel_id=1, source_target_pairs={{0,1},{1,0},{2,3},{3,2},{4,5},{5,4},{6,7},{7,6},{8,9},{9,8},{10,11... | collective-permute-start | bytes 786440 | tf_op jit(solution)/shard_map/ppermute | solution.py:547
  25.7 1.8 %collective-permute-start.14 = (bf16[8,128,128]{2,1,0:T(8,128)(2,1)S(1)}, bf16[8,128,128]{2,1,0:T(8,128)(2,1)S(1)}, u32[]{:S(2)}, u32[]{:S(2)}) collective-permute-start(bf16[8,128,128]{2,1,0:T(8,128)(2,1)S(1)} %get-tuple-element.95), channel_id=1, source_target_pairs={{0,1},{1,0},{2,3},{3,2},{4,5},{5,4},{6,7},{7,6},{8,9},{9,8},{10,11... | collective-permute-start | bytes 786440 | tf_op jit(solution)/shard_map/ppermute | solution.py:547

commit v24 on v23

--- a/solution.py
+++ b/solution.py
@@ -10,7 +10,7 @@
 HD = 128
 PAIRS = 4
 PARTNERS = (0, 3, 1, 2)
-STEPS = (0, 6, 3, 5)
+STEPS = (0, 7, 3, 4)
 TEAM = 2 * PAIRS
 F32 = jnp.float32
 BF16 = jnp.bfloat16
@@ -67,7 +67,7 @@
 
 def half_index():
     me = lax.axis_index("seq")
-    return (me ^ (me >> 1) ^ (me >> 2) ^ (me >> 3)) & 1
+    return (me ^ (me >> 1) ^ (me >> 3)) & 1
 
 
 def bring(pairs, half, sems):

time: 28.8 us -> 30.1 us (1.045)
  waiting for transfers between devices: 1.56 us -> 2.59 us
    ppermute x12, starting transfers between devices: 13.8 us -> 15.2 us  [trade(): lax.ppermute(parts[d], 'seq', [(i, i ^ STEPS[d]) for i in range(n)])]
    ppermute x12, waiting for transfers between devices: 1.55 us -> 2.44 us  [trade(): lax.ppermute(parts[d], 'seq', [(i, i ^ STEPS[d]) for i in range(n)])]
    ppermute x1, starting transfers between devices: 2.83 us -> 2.15 us  [per_device(): enter = lax.ppermute(edge(0), 'seq', up + down)]
    ppermute x2, starting transfers between devices: 0.69 us -> 0.29 us  [post(): return (own, lax.ppermute(theirs, 'seq', swap))]
  transfers between devices with their start and end apart: 16 -> 16, of which waited for: 4 -> 5; matrix products, arithmetic and copies ran while one was open for 0% -> 0% of each run, Pallas kernels for 19% -> 18%
where the time goes in v24:
time: 30.1 us; the launch traced here: 30 us
  starting transfers between devices  18.1 us (60%)
  Pallas kernels  8.51 us (28%)
  waiting for transfers between devices  2.59 us (9%)
  between operations  0.73 us (2%)
    ppermute x12, starting transfers between devices, trade(): lax.ppermute(parts[d], 'seq', [(i, i ^ STEPS[d]) for i in range(n)])  15.2 us
    pallas_call x11, Pallas kernels, call(): pl.pallas_call(kernel, in_specs=specs, out_specs=out_specs or [vmem] * le...  8.51 us
    ppermute x12, waiting for transfers between devices, trade(): lax.ppermute(parts[d], 'seq', [(i, i ^ STEPS[d]) for i in range(n)])  2.44 us
    ppermute x1, starting transfers between devices, per_device(): enter = lax.ppermute(edge(0), 'seq', up + down)  2.15 us
  transfers between devices with their start and end apart: 16, of which 5 were waited for; matrix products, arithmetic and copies ran while one was open for 0% of the time, Pallas kernels for 18%

profile of v24, /device:TPU:0, one launch (start us, length us, event | category | flops | bytes accessed | tf_op | source)
XLA Modules:
  0.0 30.0 jit_solution(1534734003093648616)
XLA Ops:
  0.6 1.7 %send.1 = (s32[8]{0:T(128)S(1)}, bf16[2,8,128,128]{3,2,1,0:T(8,128)(2,1)S(1)}, bf16[128,1024]{1,0:T(8,128)(2,1)S(1)}, bf16[128,1024]{1,0:T(8,128)(2,1)S(1)}, bf1...) custom-call(s32[8]{0:T(128)} %len_hbm.1, ...), custom_call_target="tpu_custom_call" | custom-call | flops 67108864 | bytes 4325440 | tf_op jit(solution)/shard_map/send/pallas_call | solution.py:452
  2.4 0.5 %collective-permute-start = (bf16[2,8,128,128]{3,2,1,0:T(8,128)(2,1)S(1)}, bf16[2,8,128,128]{3,2,1,0:T(8,128)(2,1)S(1)}, u32[]{:S(2)}, u32[]{:S(2)}) collective-permute-start(bf16[2,8,128,128]{3,2,1,0:T(8,128)(2,1)S(1)} %get-tuple-element.71), channel_id=1, source_target_pairs={{0,1},{1,0},{2,3},{3,2},{4,5},{5,4},{6,7},{7,6},{8,9},{9,8},{10,11... | collective-permute-start | bytes 1572872 | tf_op jit(solution)/shard_map/ppermute | solution.py:487
  2.9 1.7 %keep.1 = (bf16[2,8,128,128]{3,2,1,0:T(8,128)(2,1)S(1)}, bf16[128,1024]{1,0:T(8,128)(2,1)S(1)}, bf16[128,1024]{1,0:T(8,128)(2,1)S(1)}, bf16[128,1024]{1,0:T(8,12...) custom-call(s32[8]{0:T(128)S(1)} %get-tuple-element.56.len_hbm, ...), custom_call_target="tpu_custom_call" | custom-call | flops 67108864 | bytes 4358176 | tf_op jit(solution)/shard_map/keep/pallas_call | solution.py:452
  4.6 0.1 pair.1
  4.7 3.7 %collective-permute-start.1 = (bf16[2,128,128]{2,1,0:T(8,128)(2,1)S(1)}, bf16[2,128,128]{2,1,0:T(8,128)(2,1)S(1)}, u32[]{:S(2)}, u32[]{:S(2)}) collective-permute-start(bf16[2,128,128]{2,1,0:T(8,128)(2,1)S(1)} %get-tuple-element.73), channel_id=1, source_target_pairs={{0,7},{1,6},{2,5},{3,4},{4,3},{5,2},{6,1},{7,0},{8,15},{9,14},{10,... | collective-permute-start | bytes 196616 | tf_op jit(solution)/shard_map/ppermute | solution.py:511
  8.5 0.3 collective-permute-start.2
  8.7 0.4 %collective-permute-start.3 = (bf16[2,128,128]{2,1,0:T(8,128)(2,1)S(1)}, bf16[2,128,128]{2,1,0:T(8,128)(2,1)S(1)}, u32[]{:S(2)}, u32[]{:S(2)}) collective-permute-start(bf16[2,128,128]{2,1,0:T(8,128)(2,1)S(1)} %get-tuple-element.75), channel_id=1, source_target_pairs={{0,4},{1,5},{2,6},{3,7},{4,0},{5,1},{6,2},{7,3},{8,12},{9,13},{10,... | collective-permute-start | bytes 196616 | tf_op jit(solution)/shard_map/ppermute | solution.py:511
  9.1 2.3 %collective-permute-start.7 = (bf16[2,128,128]{2,1,0:T(8,128)(2,1)S(1)}, bf16[2,128,128]{2,1,0:T(8,128)(2,1)S(1)}, u32[]{:S(2)}, u32[]{:S(2)}) collective-permute-start(bf16[2,128,128]{2,1,0:T(8,128)(2,1)S(1)} %get-tuple-element.88), channel_id=1, source_target_pairs={{0,7},{1,6},{2,5},{3,4},{4,3},{5,2},{6,1},{7,0},{8,15},{9,14},{10,... | collective-permute-start | bytes 196616 | tf_op jit(solution)/shard_map/ppermute | solution.py:511
  11.4 0.6 %collective-permute-start.8 = (bf16[2,128,128]{2,1,0:T(8,128)(2,1)S(1)}, bf16[2,128,128]{2,1,0:T(8,128)(2,1)S(1)}, u32[]{:S(2)}, u32[]{:S(2)}) collective-permute-start(bf16[2,128,128]{2,1,0:T(8,128)(2,1)S(1)} %get-tuple-element.89), channel_id=1, source_target_pairs={{0,3},{1,2},{2,1},{3,0},{4,7},{5,6},{6,5},{7,4},{8,11},{9,10},{10,... | collective-permute-start | bytes 196616 | tf_op jit(solution)/shard_map/ppermute | solution.py:511
  12.0 0.5 %collective-permute-start.9 = (bf16[2,128,128]{2,1,0:T(8,128)(2,1)S(1)}, bf16[2,128,128]{2,1,0:T(8,128)(2,1)S(1)}, u32[]{:S(2)}, u32[]{:S(2)}) collective-permute-start(bf16[2,128,128]{2,1,0:T(8,128)(2,1)S(1)} %get-tuple-element.90), channel_id=1, source_target_pairs={{0,4},{1,5},{2,6},{3,7},{4,0},{5,1},{6,2},{7,3},{8,12},{9,13},{10,... | collective-permute-start | bytes 196616 | tf_op jit(solution)/shard_map/ppermute | solution.py:511
  12.5 0.1 collective-permute-done.2.refs_2_.s2
  12.6 0.5 %collective-permute-done.3.refs_3_.s3 = bf16[2,128,128]{2,1,0:T(8,128)(2,1)S(1)} collective-permute-done((bf16[2,128,128]{2,1,0:T(8,128)(2,1)S(1)}, bf16[2,128,128]{2,1,0:T(8,128)(2,1)S(1)}, u32[]{:S(2)}, u32[]{:S(2)}) %collective-permute-start.3) | collective-permute-done | bytes 65568 | tf_op jit(solution)/shard_map/ppermute | solution.py:511
  13.1 0.1 totals.1
  13.1 2.2 %collective-permute-start.10 = (bf16[2,128,128]{2,1,0:T(8,128)(2,1)S(1)}, bf16[2,128,128]{2,1,0:T(8,128)(2,1)S(1)}, u32[]{:S(2)}, u32[]{:S(2)}) collective-permute-start(bf16[2,128,128]{2,1,0:T(8,128)(2,1)S(1)} %totals.1), channel_id=1, source_target_pairs={{0,9},{1,8},{2,11},{3,10},{4,13},{5,12},{6,15},{7,14},{9,0},{8,1},... | collective-permute-start | bytes 196616 | tf_op jit(solution)/shard_map/ppermute | solution.py:533
  15.3 0.1 scan.2
  15.4 2.2 %collective-permute-start.4 = (bf16[2,128,128]{2,1,0:T(8,128)(2,1)S(1)}, bf16[2,128,128]{2,1,0:T(8,128)(2,1)S(1)}, u32[]{:S(2)}, u32[]{:S(2)}) collective-permute-start(bf16[2,128,128]{2,1,0:T(8,128)(2,1)S(1)} %get-tuple-element.77), channel_id=1, source_target_pairs={{0,7},{1,6},{2,5},{3,4},{4,3},{5,2},{6,1},{7,0},{8,15},{9,14},{10,... | collective-permute-start | bytes 196616 | tf_op jit(solution)/shard_map/ppermute | solution.py:511
  17.6 0.5 %collective-permute-start.5 = (bf16[2,128,128]{2,1,0:T(8,128)(2,1)S(1)}, bf16[2,128,128]{2,1,0:T(8,128)(2,1)S(1)}, u32[]{:S(2)}, u32[]{:S(2)}) collective-permute-start(bf16[2,128,128]{2,1,0:T(8,128)(2,1)S(1)} %get-tuple-element.78), channel_id=1, source_target_pairs={{0,3},{1,2},{2,1},{3,0},{4,7},{5,6},{6,5},{7,4},{8,11},{9,10},{10,... | collective-permute-start | bytes 196616 | tf_op jit(solution)/shard_map/ppermute | solution.py:511
  18.1 1.3 %collective-permute-start.6 = (bf16[2,128,128]{2,1,0:T(8,128)(2,1)S(1)}, bf16[2,128,128]{2,1,0:T(8,128)(2,1)S(1)}, u32[]{:S(2)}, u32[]{:S(2)}) collective-permute-start(bf16[2,128,128]{2,1,0:T(8,128)(2,1)S(1)} %get-tuple-element.79), channel_id=1, source_target_pairs={{0,4},{1,5},{2,6},{3,7},{4,0},{5,1},{6,2},{7,3},{8,12},{9,13},{10,... | collective-permute-start | bytes 196616 | tf_op jit(solution)/shard_map/ppermute | solution.py:511
  19.3 0.2 scan.3
  19.5 2.2 %collective-permute-start.11 = (bf16[2,128,128]{2,1,0:T(8,128)(2,1)S(1)}, bf16[2,128,128]{2,1,0:T(8,128)(2,1)S(1)}, u32[]{:S(2)}, u32[]{:S(2)}) collective-permute-start(bf16[2,128,128]{2,1,0:T(8,128)(2,1)S(1)} %get-tuple-element.92), channel_id=1, source_target_pairs={{0,7},{1,6},{2,5},{3,4},{4,3},{5,2},{6,1},{7,0},{8,15},{9,14},{10,... | collective-permute-start | bytes 196616 | tf_op jit(solution)/shard_map/ppermute | solution.py:511
  21.7 0.1 collective-permute-start.12
  21.8 1.3 %collective-permute-start.13 = (bf16[2,128,128]{2,1,0:T(8,128)(2,1)S(1)}, bf16[2,128,128]{2,1,0:T(8,128)(2,1)S(1)}, u32[]{:S(2)}, u32[]{:S(2)}) collective-permute-start(bf16[2,128,128]{2,1,0:T(8,128)(2,1)S(1)} %get-tuple-element.94), channel_id=1, source_target_pairs={{0,4},{1,5},{2,6},{3,7},{4,0},{5,1},{6,2},{7,3},{8,12},{9,13},{10,... | collective-permute-start | bytes 196616 | tf_op jit(solution)/shard_map/ppermute | solution.py:511
  23.1 0.1 post.2
  23.2 0.2 collective-permute-start.15
  23.4 1.8 %local.1 = (bf16[16,128,128]{2,1,0:T(8,128)(2,1)S(1)}, bf16[16,128,128]{2,1,0:T(8,128)(2,1)S(1)}, bf16[16,128,128]{2,1,0:T(8,128)(2,1)S(1)}, bf16[16,128,128]{2,...) custom-call(s32[8]{0:T(128)S(1)} %get-tuple-element.56.len_hbm, ...), custom_call_target="tpu_custom_call" | custom-call | flops 134217728 | bytes 6160416 | tf_op jit(solution)/shard_map/local/pallas_call | solution.py:452
  25.2 1.1 %collective-permute-done.12.refs_2_ = bf16[2,128,128]{2,1,0:T(8,128)(2,1)S(1)} collective-permute-done((bf16[2,128,128]{2,1,0:T(8,128)(2,1)S(1)}, bf16[2,128,128]{2,1,0:T(8,128)(2,1)S(1)}, u32[]{:S(2)}, u32[]{:S(2)}) %collective-permute-start.12) | collective-permute-done | bytes 65568 | tf_op jit(solution)/shard_map/ppermute | solution.py:511
  26.4 0.7 %collective-permute-done.13.refs_3_ = bf16[2,128,128]{2,1,0:T(8,128)(2,1)S(1)} collective-permute-done((bf16[2,128,128]{2,1,0:T(8,128)(2,1)S(1)}, bf16[2,128,128]{2,1,0:T(8,128)(2,1)S(1)}, u32[]{:S(2)}, u32[]{:S(2)}) %collective-permute-start.13) | collective-permute-done | bytes 65568 | tf_op jit(solution)/shard_map/ppermute | solution.py:511
  27.0 0.1 post.3
  27.2 0.1 collective-permute-start.14
  27.3 1.4 %middle.1 = (bf16[128,2048]{1,0:T(8,128)(2,1)}, bf16[128,2048]{1,0:T(8,128)(2,1)}, bf16[128,2048]{1,0:T(8,128)(2,1)}, bf16[128,2048]{1,0:T(8,128)(2,1)}, bf16[12...) custom-call(bf16[128,1024]{1,0:T(8,128)(2,1)S(1)} %get-tuple-element.98.refs_0_, ...), custom_call_target="tpu_custom_call" | custom-call | flops 268435456 | bytes 9043968 | tf_op jit(solution)/shard_map/middle/pallas_call | solution.py:452
  28.6 0.1 collective-permute-done.14.refs_13_
  28.8 1.2 %last.1 = (bf16[128,2048]{1,0:T(8,128)(2,1)}, bf16[128,2048]{1,0:T(8,128)(2,1)}, bf16[128,2048]{1,0:T(8,128)(2,1)}, bf16[128,2048]{1,0:T(8,128)(2,1)}) custom-call(bf16[128,1024]{1,0:T(8,128)(2,1)S(1)} %get-tuple-element.59.refs_0_.refs_2_, ...), custom_call_target="tpu_custom_call", output_to_operand_aliasing={{0}: (18, {}), {1}: (19, {}), {2}: (20, {}), {3}: (21, {})} | custom-call | flops 134217728 | bytes 9830400 | tf_op jit(solution)/shard_map/last/pallas_call | solution.py:452
  (11 shorter events, 0.0 us)
Async XLA Ops:
  2.4 2.2 %collective-permute-start = (bf16[2,8,128,128]{3,2,1,0:T(8,128)(2,1)S(1)}, bf16[2,8,128,128]{3,2,1,0:T(8,128)(2,1)S(1)}, u32[]{:S(2)}, u32[]{:S(2)}) collective-permute-start(bf16[2,8,128,128]{3,2,1,0:T(8,128)(2,1)S(1)} %get-tuple-element.71), channel_id=1, source_target_pairs={{0,1},{1,0},{2,3},{3,2},{4,5},{5,4},{6,7},{7,6},{8,9},{9,8},{10,11... | collective-permute-start | bytes 1572872 | tf_op jit(solution)/shard_map/ppermute | solution.py:487
  4.7 7.2 %collective-permute-start.1 = (bf16[2,128,128]{2,1,0:T(8,128)(2,1)S(1)}, bf16[2,128,128]{2,1,0:T(8,128)(2,1)S(1)}, u32[]{:S(2)}, u32[]{:S(2)}) collective-permute-start(bf16[2,128,128]{2,1,0:T(8,128)(2,1)S(1)} %get-tuple-element.73), channel_id=1, source_target_pairs={{0,7},{1,6},{2,5},{3,4},{4,3},{5,2},{6,1},{7,0},{8,15},{9,14},{10,... | collective-permute-start | bytes 196616 | tf_op jit(solution)/shard_map/ppermute | solution.py:511
  8.5 4.1 %collective-permute-start.2 = (bf16[2,128,128]{2,1,0:T(8,128)(2,1)S(1)}, bf16[2,128,128]{2,1,0:T(8,128)(2,1)S(1)}, u32[]{:S(2)}, u32[]{:S(2)}) collective-permute-start(bf16[2,128,128]{2,1,0:T(8,128)(2,1)S(1)} %get-tuple-element.74), channel_id=1, source_target_pairs={{0,3},{1,2},{2,1},{3,0},{4,7},{5,6},{6,5},{7,4},{8,11},{9,10},{10,... | collective-permute-start | bytes 196616 | tf_op jit(solution)/shard_map/ppermute | solution.py:511
  8.7 4.3 %collective-permute-start.3 = (bf16[2,128,128]{2,1,0:T(8,128)(2,1)S(1)}, bf16[2,128,128]{2,1,0:T(8,128)(2,1)S(1)}, u32[]{:S(2)}, u32[]{:S(2)}) collective-permute-start(bf16[2,128,128]{2,1,0:T(8,128)(2,1)S(1)} %get-tuple-element.75), channel_id=1, source_target_pairs={{0,4},{1,5},{2,6},{3,7},{4,0},{5,1},{6,2},{7,3},{8,12},{9,13},{10,... | collective-permute-start | bytes 196616 | tf_op jit(solution)/shard_map/ppermute | solution.py:511
  9.1 8.5 %collective-permute-start.7 = (bf16[2,128,128]{2,1,0:T(8,128)(2,1)S(1)}, bf16[2,128,128]{2,1,0:T(8,128)(2,1)S(1)}, u32[]{:S(2)}, u32[]{:S(2)}) collective-permute-start(bf16[2,128,128]{2,1,0:T(8,128)(2,1)S(1)} %get-tuple-element.88), channel_id=1, source_target_pairs={{0,7},{1,6},{2,5},{3,4},{4,3},{5,2},{6,1},{7,0},{8,15},{9,14},{10,... | collective-permute-start | bytes 196616 | tf_op jit(solution)/shard_map/ppermute | solution.py:511
  11.4 6.7 %collective-permute-start.8 = (bf16[2,128,128]{2,1,0:T(8,128)(2,1)S(1)}, bf16[2,128,128]{2,1,0:T(8,128)(2,1)S(1)}, u32[]{:S(2)}, u32[]{:S(2)}) collective-permute-start(bf16[2,128,128]{2,1,0:T(8,128)(2,1)S(1)} %get-tuple-element.89), channel_id=1, source_target_pairs={{0,3},{1,2},{2,1},{3,0},{4,7},{5,6},{6,5},{7,4},{8,11},{9,10},{10,... | collective-permute-start | bytes 196616 | tf_op jit(solution)/shard_map/ppermute | solution.py:511
  12.0 7.4 %collective-permute-start.9 = (bf16[2,128,128]{2,1,0:T(8,128)(2,1)S(1)}, bf16[2,128,128]{2,1,0:T(8,128)(2,1)S(1)}, u32[]{:S(2)}, u32[]{:S(2)}) collective-permute-start(bf16[2,128,128]{2,1,0:T(8,128)(2,1)S(1)} %get-tuple-element.90), channel_id=1, source_target_pairs={{0,4},{1,5},{2,6},{3,7},{4,0},{5,1},{6,2},{7,3},{8,12},{9,13},{10,... | collective-permute-start | bytes 196616 | tf_op jit(solution)/shard_map/ppermute | solution.py:511
  13.1 6.2 %collective-permute-start.10 = (bf16[2,128,128]{2,1,0:T(8,128)(2,1)S(1)}, bf16[2,128,128]{2,1,0:T(8,128)(2,1)S(1)}, u32[]{:S(2)}, u32[]{:S(2)}) collective-permute-start(bf16[2,128,128]{2,1,0:T(8,128)(2,1)S(1)} %totals.1), channel_id=1, source_target_pairs={{0,9},{1,8},{2,11},{3,10},{4,13},{5,12},{6,15},{7,14},{9,0},{8,1},... | collective-permute-start | bytes 196616 | tf_op jit(solution)/shard_map/ppermute | solution.py:533
  15.4 6.4 %collective-permute-start.4 = (bf16[2,128,128]{2,1,0:T(8,128)(2,1)S(1)}, bf16[2,128,128]{2,1,0:T(8,128)(2,1)S(1)}, u32[]{:S(2)}, u32[]{:S(2)}) collective-permute-start(bf16[2,128,128]{2,1,0:T(8,128)(2,1)S(1)} %get-tuple-element.77), channel_id=1, source_target_pairs={{0,7},{1,6},{2,5},{3,4},{4,3},{5,2},{6,1},{7,0},{8,15},{9,14},{10,... | collective-permute-start | bytes 196616 | tf_op jit(solution)/shard_map/ppermute | solution.py:511
  17.6 5.5 %collective-permute-start.5 = (bf16[2,128,128]{2,1,0:T(8,128)(2,1)S(1)}, bf16[2,128,128]{2,1,0:T(8,128)(2,1)S(1)}, u32[]{:S(2)}, u32[]{:S(2)}) collective-permute-start(bf16[2,128,128]{2,1,0:T(8,128)(2,1)S(1)} %get-tuple-element.78), channel_id=1, source_target_pairs={{0,3},{1,2},{2,1},{3,0},{4,7},{5,6},{6,5},{7,4},{8,11},{9,10},{10,... | collective-permute-start | bytes 196616 | tf_op jit(solution)/shard_map/ppermute | solution.py:511
  18.1 5.0 %collective-permute-start.6 = (bf16[2,128,128]{2,1,0:T(8,128)(2,1)S(1)}, bf16[2,128,128]{2,1,0:T(8,128)(2,1)S(1)}, u32[]{:S(2)}, u32[]{:S(2)}) collective-permute-start(bf16[2,128,128]{2,1,0:T(8,128)(2,1)S(1)} %get-tuple-element.79), channel_id=1, source_target_pairs={{0,4},{1,5},{2,6},{3,7},{4,0},{5,1},{6,2},{7,3},{8,12},{9,13},{10,... | collective-permute-start | bytes 196616 | tf_op jit(solution)/shard_map/ppermute | solution.py:511
  19.5 5.7 %collective-permute-start.11 = (bf16[2,128,128]{2,1,0:T(8,128)(2,1)S(1)}, bf16[2,128,128]{2,1,0:T(8,128)(2,1)S(1)}, u32[]{:S(2)}, u32[]{:S(2)}) collective-permute-start(bf16[2,128,128]{2,1,0:T(8,128)(2,1)S(1)} %get-tuple-element.92), channel_id=1, source_target_pairs={{0,7},{1,6},{2,5},{3,4},{4,3},{5,2},{6,1},{7,0},{8,15},{9,14},{10,... | collective-permute-start | bytes 196616 | tf_op jit(solution)/shard_map/ppermute | solution.py:511
  21.7 4.6 %collective-permute-start.12 = (bf16[2,128,128]{2,1,0:T(8,128)(2,1)S(1)}, bf16[2,128,128]{2,1,0:T(8,128)(2,1)S(1)}, u32[]{:S(2)}, u32[]{:S(2)}) collective-permute-start(bf16[2,128,128]{2,1,0:T(8,128)(2,1)S(1)} %get-tuple-element.93), channel_id=1, source_target_pairs={{0,3},{1,2},{2,1},{3,0},{4,7},{5,6},{6,5},{7,4},{8,11},{9,10},{10,... | collective-permute-start | bytes 196616 | tf_op jit(solution)/shard_map/ppermute | solution.py:511
  21.8 5.3 %collective-permute-start.13 = (bf16[2,128,128]{2,1,0:T(8,128)(2,1)S(1)}, bf16[2,128,128]{2,1,0:T(8,128)(2,1)S(1)}, u32[]{:S(2)}, u32[]{:S(2)}) collective-permute-start(bf16[2,128,128]{2,1,0:T(8,128)(2,1)S(1)} %get-tuple-element.94), channel_id=1, source_target_pairs={{0,4},{1,5},{2,6},{3,7},{4,0},{5,1},{6,2},{7,3},{8,12},{9,13},{10,... | collective-permute-start | bytes 196616 | tf_op jit(solution)/shard_map/ppermute | solution.py:511
  23.2 4.0 %collective-permute-start.15 = (bf16[8,128,128]{2,1,0:T(8,128)(2,1)S(1)}, bf16[8,128,128]{2,1,0:T(8,128)(2,1)S(1)}, u32[]{:S(2)}, u32[]{:S(2)}) collective-permute-start(bf16[8,128,128]{2,1,0:T(8,128)(2,1)S(1)} %get-tuple-element.100), channel_id=1, source_target_pairs={{0,1},{1,0},{2,3},{3,2},{4,5},{5,4},{6,7},{7,6},{8,9},{9,8},{10,11... | collective-permute-start | bytes 786440 | tf_op jit(solution)/shard_map/ppermute | solution.py:547
  27.2 1.6 %collective-permute-start.14 = (bf16[8,128,128]{2,1,0:T(8,128)(2,1)S(1)}, bf16[8,128,128]{2,1,0:T(8,128)(2,1)S(1)}, u32[]{:S(2)}, u32[]{:S(2)}) collective-permute-start(bf16[8,128,128]{2,1,0:T(8,128)(2,1)S(1)} %get-tuple-element.95), channel_id=1, source_target_pairs={{0,1},{1,0},{2,3},{3,2},{4,5},{5,4},{6,7},{7,6},{8,9},{9,8},{10,11... | collective-permute-start | bytes 786440 | tf_op jit(solution)/shard_map/ppermute | solution.py:547

commit v25 on v23

--- a/solution.py
+++ b/solution.py
@@ -70,13 +70,15 @@
     return (me ^ (me >> 1) ^ (me >> 2) ^ (me >> 3)) & 1
 
 
-def bring(pairs, half, sems):
+def bring(pairs, half, sems, len_copy):
     copies = []
     for i, (src, dst) in enumerate(pairs):
         width = dst.shape[1]
         at = pl.ds(pl.multiple_of(half * width, HD), width)
         copies.append(pltpu.make_async_copy(src.at[:, at], dst, sems.at[i]))
         copies[-1].start()
+        if i == 0:
+            len_copy.start()
     return copies
 
 
@@ -119,11 +121,10 @@
     rows = q_ref.shape[0]
     me = lax.axis_index("seq")
     len_copy = pltpu.make_async_copy(len_hbm, len_ref, len_sems.at[0])
-    len_copy.start()
     len_pass = pltpu.make_async_copy(len_hbm, len_out, len_sems.at[1])
+    pairs = ((k_hbm, k_ref), (q_hbm, q_ref), (v_hbm, v_ref), (g_hbm, g_ref))
+    copies = bring(pairs, 1 - half_index(), sems, len_copy)
     len_pass.start()
-    pairs = ((k_hbm, k_ref), (q_hbm, q_ref), (v_hbm, v_ref), (g_hbm, g_ref))
-    copies = bring(pairs, 1 - half_index(), sems)
     len_copy.wait()
     starts = doc_starts(len_ref)
     first = me * rows
@@ -218,9 +219,8 @@
 ):
     rows = q_ref.shape[0]
     len_copy = pltpu.make_async_copy(len_hbm, len_ref, len_sem)
-    len_copy.start()
     pairs = ((k_hbm, k_ref), (q_hbm, q_ref), (v_hbm, v_ref), (g_hbm, g_ref))
-    copies = bring(pairs, half_index(), sems)
+    copies = bring(pairs, half_index(), sems, len_copy)
     len_copy.wait()
     coefficients(doc_starts(len_ref), rows, total // rows, coef_ref)
     masks = rows_ref[0], rows_ref[1], root_ref[...]

time: 28.8 us -> 28.8 us (level)
  no operation moved by 1% of the time
where the time goes in v25:
time: 28.8 us; the launch traced here: 28.7 us
  starting transfers between devices  17.9 us (62%)
  Pallas kernels  8.5 us (30%)
  waiting for transfers between devices  1.55 us (5%)
  between operations  0.73 us (3%)
    ppermute x12, starting transfers between devices, trade(): lax.ppermute(parts[d], 'seq', [(i, i ^ STEPS[d]) for i in range(n)])  13.8 us
    pallas_call x11, Pallas kernels, call(): pl.pallas_call(kernel, in_specs=specs, out_specs=out_specs or [vmem] * le...  8.5 us
    ppermute x1, starting transfers between devices, per_device(): enter = lax.ppermute(edge(0), 'seq', up + down)  2.83 us
    ppermute x12, waiting for transfers between devices, trade(): lax.ppermute(parts[d], 'seq', [(i, i ^ STEPS[d]) for i in range(n)])  1.54 us
    ppermute x2, starting transfers between devices, post(): return (own, lax.ppermute(theirs, 'seq', swap))  0.69 us
  transfers between devices with their start and end apart: 16, of which 4 were waited for; matrix products, arithmetic and copies ran while one was open for 0% of the time, Pallas kernels for 19%

profile of v25, /device:TPU:0, one launch (start us, length us, event | category | flops | bytes accessed | tf_op | source)
XLA Modules:
  0.0 28.7 jit_solution(9023983706885449359)
XLA Ops:
  0.6 1.7 %send.1 = (s32[8]{0:T(128)S(1)}, bf16[2,8,128,128]{3,2,1,0:T(8,128)(2,1)S(1)}, bf16[128,1024]{1,0:T(8,128)(2,1)S(1)}, bf16[128,1024]{1,0:T(8,128)(2,1)S(1)}, bf1...) custom-call(s32[8]{0:T(128)} %len_hbm.1, ...), custom_call_target="tpu_custom_call" | custom-call | flops 67108864 | bytes 4325440 | tf_op jit(solution)/shard_map/send/pallas_call | solution.py:452
  2.4 0.5 %collective-permute-start = (bf16[2,8,128,128]{3,2,1,0:T(8,128)(2,1)S(1)}, bf16[2,8,128,128]{3,2,1,0:T(8,128)(2,1)S(1)}, u32[]{:S(2)}, u32[]{:S(2)}) collective-permute-start(bf16[2,8,128,128]{3,2,1,0:T(8,128)(2,1)S(1)} %get-tuple-element.71), channel_id=1, source_target_pairs={{0,1},{1,0},{2,3},{3,2},{4,5},{5,4},{6,7},{7,6},{8,9},{9,8},{10,11... | collective-permute-start | bytes 1572872 | tf_op jit(solution)/shard_map/ppermute | solution.py:487
  2.9 1.7 %keep.1 = (bf16[2,8,128,128]{3,2,1,0:T(8,128)(2,1)S(1)}, bf16[128,1024]{1,0:T(8,128)(2,1)S(1)}, bf16[128,1024]{1,0:T(8,128)(2,1)S(1)}, bf16[128,1024]{1,0:T(8,12...) custom-call(s32[8]{0:T(128)S(1)} %get-tuple-element.56.len_hbm, ...), custom_call_target="tpu_custom_call" | custom-call | flops 67108864 | bytes 4358176 | tf_op jit(solution)/shard_map/keep/pallas_call | solution.py:452
  4.6 0.1 pair.1
  4.7 3.8 %collective-permute-start.1 = (bf16[2,128,128]{2,1,0:T(8,128)(2,1)S(1)}, bf16[2,128,128]{2,1,0:T(8,128)(2,1)S(1)}, u32[]{:S(2)}, u32[]{:S(2)}) collective-permute-start(bf16[2,128,128]{2,1,0:T(8,128)(2,1)S(1)} %get-tuple-element.73), channel_id=1, source_target_pairs={{0,6},{1,7},{2,4},{3,5},{4,2},{5,3},{6,0},{7,1},{8,14},{9,15},{10,... | collective-permute-start | bytes 196616 | tf_op jit(solution)/shard_map/ppermute | solution.py:511
  8.5 0.2 collective-permute-start.2
  8.7 0.2 collective-permute-start.3
  8.9 2.8 %collective-permute-start.7 = (bf16[2,128,128]{2,1,0:T(8,128)(2,1)S(1)}, bf16[2,128,128]{2,1,0:T(8,128)(2,1)S(1)}, u32[]{:S(2)}, u32[]{:S(2)}) collective-permute-start(bf16[2,128,128]{2,1,0:T(8,128)(2,1)S(1)} %get-tuple-element.88), channel_id=1, source_target_pairs={{0,6},{1,7},{2,4},{3,5},{4,2},{5,3},{6,0},{7,1},{8,14},{9,15},{10,... | collective-permute-start | bytes 196616 | tf_op jit(solution)/shard_map/ppermute | solution.py:511
  11.7 0.4 %collective-permute-start.9 = (bf16[2,128,128]{2,1,0:T(8,128)(2,1)S(1)}, bf16[2,128,128]{2,1,0:T(8,128)(2,1)S(1)}, u32[]{:S(2)}, u32[]{:S(2)}) collective-permute-start(bf16[2,128,128]{2,1,0:T(8,128)(2,1)S(1)} %get-tuple-element.90), channel_id=1, source_target_pairs={{0,5},{1,4},{2,7},{3,6},{4,1},{5,0},{6,3},{7,2},{8,13},{9,12},{10,... | collective-permute-start | bytes 196616 | tf_op jit(solution)/shard_map/ppermute | solution.py:511
  12.1 0.6 %collective-permute-done.2.refs_2_.s2 = bf16[2,128,128]{2,1,0:T(8,128)(2,1)S(1)} collective-permute-done((bf16[2,128,128]{2,1,0:T(8,128)(2,1)S(1)}, bf16[2,128,128]{2,1,0:T(8,128)(2,1)S(1)}, u32[]{:S(2)}, u32[]{:S(2)}) %collective-permute-start.2) | collective-permute-done | bytes 65568 | tf_op jit(solution)/shard_map/ppermute | solution.py:511
  12.7 0.1 totals.1
  12.7 2.8 %collective-permute-start.10 = (bf16[2,128,128]{2,1,0:T(8,128)(2,1)S(1)}, bf16[2,128,128]{2,1,0:T(8,128)(2,1)S(1)}, u32[]{:S(2)}, u32[]{:S(2)}) collective-permute-start(bf16[2,128,128]{2,1,0:T(8,128)(2,1)S(1)} %totals.1), channel_id=1, source_target_pairs={{0,9},{1,8},{2,11},{3,10},{4,13},{5,12},{6,15},{7,14},{9,0},{8,1},... | collective-permute-start | bytes 196616 | tf_op jit(solution)/shard_map/ppermute | solution.py:533
  15.6 0.1 scan.2
  15.7 1.5 %collective-permute-start.4 = (bf16[2,128,128]{2,1,0:T(8,128)(2,1)S(1)}, bf16[2,128,128]{2,1,0:T(8,128)(2,1)S(1)}, u32[]{:S(2)}, u32[]{:S(2)}) collective-permute-start(bf16[2,128,128]{2,1,0:T(8,128)(2,1)S(1)} %get-tuple-element.77), channel_id=1, source_target_pairs={{0,6},{1,7},{2,4},{3,5},{4,2},{5,3},{6,0},{7,1},{8,14},{9,15},{10,... | collective-permute-start | bytes 196616 | tf_op jit(solution)/shard_map/ppermute | solution.py:511
  17.2 0.8 %collective-permute-start.5 = (bf16[2,128,128]{2,1,0:T(8,128)(2,1)S(1)}, bf16[2,128,128]{2,1,0:T(8,128)(2,1)S(1)}, u32[]{:S(2)}, u32[]{:S(2)}) collective-permute-start(bf16[2,128,128]{2,1,0:T(8,128)(2,1)S(1)} %get-tuple-element.78), channel_id=1, source_target_pairs={{0,3},{1,2},{2,1},{3,0},{4,7},{5,6},{6,5},{7,4},{8,11},{9,10},{10,... | collective-permute-start | bytes 196616 | tf_op jit(solution)/shard_map/ppermute | solution.py:511
  18.0 0.0 collective-permute-done.8.refs_2_
  18.0 0.9 %collective-permute-start.6 = (bf16[2,128,128]{2,1,0:T(8,128)(2,1)S(1)}, bf16[2,128,128]{2,1,0:T(8,128)(2,1)S(1)}, u32[]{:S(2)}, u32[]{:S(2)}) collective-permute-start(bf16[2,128,128]{2,1,0:T(8,128)(2,1)S(1)} %get-tuple-element.79), channel_id=1, source_target_pairs={{0,5},{1,4},{2,7},{3,6},{4,1},{5,0},{6,3},{7,2},{8,13},{9,12},{10,... | collective-permute-start | bytes 196616 | tf_op jit(solution)/shard_map/ppermute | solution.py:511
  19.0 0.2 scan.3
  19.1 1.8 %collective-permute-start.11 = (bf16[2,128,128]{2,1,0:T(8,128)(2,1)S(1)}, bf16[2,128,128]{2,1,0:T(8,128)(2,1)S(1)}, u32[]{:S(2)}, u32[]{:S(2)}) collective-permute-start(bf16[2,128,128]{2,1,0:T(8,128)(2,1)S(1)} %get-tuple-element.92), channel_id=1, source_target_pairs={{0,6},{1,7},{2,4},{3,5},{4,2},{5,3},{6,0},{7,1},{8,14},{9,15},{10,... | collective-permute-start | bytes 196616 | tf_op jit(solution)/shard_map/ppermute | solution.py:511
  21.0 0.3 %collective-permute-start.12 = (bf16[2,128,128]{2,1,0:T(8,128)(2,1)S(1)}, bf16[2,128,128]{2,1,0:T(8,128)(2,1)S(1)}, u32[]{:S(2)}, u32[]{:S(2)}) collective-permute-start(bf16[2,128,128]{2,1,0:T(8,128)(2,1)S(1)} %get-tuple-element.93), channel_id=1, source_target_pairs={{0,3},{1,2},{2,1},{3,0},{4,7},{5,6},{6,5},{7,4},{8,11},{9,10},{10,... | collective-permute-start | bytes 196616 | tf_op jit(solution)/shard_map/ppermute | solution.py:511
  21.3 0.1 collective-permute-done.4.refs_1_
  21.4 1.1 %collective-permute-start.13 = (bf16[2,128,128]{2,1,0:T(8,128)(2,1)S(1)}, bf16[2,128,128]{2,1,0:T(8,128)(2,1)S(1)}, u32[]{:S(2)}, u32[]{:S(2)}) collective-permute-start(bf16[2,128,128]{2,1,0:T(8,128)(2,1)S(1)} %get-tuple-element.94), channel_id=1, source_target_pairs={{0,5},{1,4},{2,7},{3,6},{4,1},{5,0},{6,3},{7,2},{8,13},{9,12},{10,... | collective-permute-start | bytes 196616 | tf_op jit(solution)/shard_map/ppermute | solution.py:511
  22.4 0.0 collective-permute-done.5.refs_2_
  22.4 0.1 post.2
  22.6 0.3 collective-permute-start.15
  22.9 1.8 %local.1 = (bf16[16,128,128]{2,1,0:T(8,128)(2,1)S(1)}, bf16[16,128,128]{2,1,0:T(8,128)(2,1)S(1)}, bf16[16,128,128]{2,1,0:T(8,128)(2,1)S(1)}, bf16[16,128,128]{2,...) custom-call(s32[8]{0:T(128)S(1)} %get-tuple-element.56.len_hbm, ...), custom_call_target="tpu_custom_call" | custom-call | flops 134217728 | bytes 6160416 | tf_op jit(solution)/shard_map/local/pallas_call | solution.py:452
  24.7 0.8 %collective-permute-done.12.refs_2_ = bf16[2,128,128]{2,1,0:T(8,128)(2,1)S(1)} collective-permute-done((bf16[2,128,128]{2,1,0:T(8,128)(2,1)S(1)}, bf16[2,128,128]{2,1,0:T(8,128)(2,1)S(1)}, u32[]{:S(2)}, u32[]{:S(2)}) %collective-permute-start.12) | collective-permute-done | bytes 65568 | tf_op jit(solution)/shard_map/ppermute | solution.py:511
  25.5 0.1 collective-permute-done.13.refs_3_
  25.6 0.1 post.3
  25.7 0.4 %collective-permute-start.14 = (bf16[8,128,128]{2,1,0:T(8,128)(2,1)S(1)}, bf16[8,128,128]{2,1,0:T(8,128)(2,1)S(1)}, u32[]{:S(2)}, u32[]{:S(2)}) collective-permute-start(bf16[8,128,128]{2,1,0:T(8,128)(2,1)S(1)} %get-tuple-element.95), channel_id=1, source_target_pairs={{0,1},{1,0},{2,3},{3,2},{4,5},{5,4},{6,7},{7,6},{8,9},{9,8},{10,11... | collective-permute-start | bytes 786440 | tf_op jit(solution)/shard_map/ppermute | solution.py:547
  26.1 1.3 %middle.1 = (bf16[128,2048]{1,0:T(8,128)(2,1)}, bf16[128,2048]{1,0:T(8,128)(2,1)}, bf16[128,2048]{1,0:T(8,128)(2,1)}, bf16[128,2048]{1,0:T(8,128)(2,1)}, bf16[12...) custom-call(bf16[128,1024]{1,0:T(8,128)(2,1)S(1)} %get-tuple-element.98.refs_0_, ...), custom_call_target="tpu_custom_call" | custom-call | flops 268435456 | bytes 9043968 | tf_op jit(solution)/shard_map/middle/pallas_call | solution.py:452
  27.5 1.2 %last.1 = (bf16[128,2048]{1,0:T(8,128)(2,1)}, bf16[128,2048]{1,0:T(8,128)(2,1)}, bf16[128,2048]{1,0:T(8,128)(2,1)}, bf16[128,2048]{1,0:T(8,128)(2,1)}) custom-call(bf16[128,1024]{1,0:T(8,128)(2,1)S(1)} %get-tuple-element.59.refs_0_.refs_2_, ...), custom_call_target="tpu_custom_call", output_to_operand_aliasing={{0}: (18, {}), {1}: (19, {}), {2}: (20, {}), {3}: (21, {})} | custom-call | flops 134217728 | bytes 9830400 | tf_op jit(solution)/shard_map/last/pallas_call | solution.py:452
  (11 shorter events, 0.0 us)
Async XLA Ops:
  2.4 2.2 %collective-permute-start = (bf16[2,8,128,128]{3,2,1,0:T(8,128)(2,1)S(1)}, bf16[2,8,128,128]{3,2,1,0:T(8,128)(2,1)S(1)}, u32[]{:S(2)}, u32[]{:S(2)}) collective-permute-start(bf16[2,8,128,128]{3,2,1,0:T(8,128)(2,1)S(1)} %get-tuple-element.71), channel_id=1, source_target_pairs={{0,1},{1,0},{2,3},{3,2},{4,5},{5,4},{6,7},{7,6},{8,9},{9,8},{10,11... | collective-permute-start | bytes 1572872 | tf_op jit(solution)/shard_map/ppermute | solution.py:487
  4.7 7.0 %collective-permute-start.1 = (bf16[2,128,128]{2,1,0:T(8,128)(2,1)S(1)}, bf16[2,128,128]{2,1,0:T(8,128)(2,1)S(1)}, u32[]{:S(2)}, u32[]{:S(2)}) collective-permute-start(bf16[2,128,128]{2,1,0:T(8,128)(2,1)S(1)} %get-tuple-element.73), channel_id=1, source_target_pairs={{0,6},{1,7},{2,4},{3,5},{4,2},{5,3},{6,0},{7,1},{8,14},{9,15},{10,... | collective-permute-start | bytes 196616 | tf_op jit(solution)/shard_map/ppermute | solution.py:511
  8.5 4.2 %collective-permute-start.2 = (bf16[2,128,128]{2,1,0:T(8,128)(2,1)S(1)}, bf16[2,128,128]{2,1,0:T(8,128)(2,1)S(1)}, u32[]{:S(2)}, u32[]{:S(2)}) collective-permute-start(bf16[2,128,128]{2,1,0:T(8,128)(2,1)S(1)} %get-tuple-element.74), channel_id=1, source_target_pairs={{0,3},{1,2},{2,1},{3,0},{4,7},{5,6},{6,5},{7,4},{8,11},{9,10},{10,... | collective-permute-start | bytes 196616 | tf_op jit(solution)/shard_map/ppermute | solution.py:511
  8.7 4.0 %collective-permute-start.3 = (bf16[2,128,128]{2,1,0:T(8,128)(2,1)S(1)}, bf16[2,128,128]{2,1,0:T(8,128)(2,1)S(1)}, u32[]{:S(2)}, u32[]{:S(2)}) collective-permute-start(bf16[2,128,128]{2,1,0:T(8,128)(2,1)S(1)} %get-tuple-element.75), channel_id=1, source_target_pairs={{0,5},{1,4},{2,7},{3,6},{4,1},{5,0},{6,3},{7,2},{8,13},{9,12},{10,... | collective-permute-start | bytes 196616 | tf_op jit(solution)/shard_map/ppermute | solution.py:511
  8.9 8.4 %collective-permute-start.7 = (bf16[2,128,128]{2,1,0:T(8,128)(2,1)S(1)}, bf16[2,128,128]{2,1,0:T(8,128)(2,1)S(1)}, u32[]{:S(2)}, u32[]{:S(2)}) collective-permute-start(bf16[2,128,128]{2,1,0:T(8,128)(2,1)S(1)} %get-tuple-element.88), channel_id=1, source_target_pairs={{0,6},{1,7},{2,4},{3,5},{4,2},{5,3},{6,0},{7,1},{8,14},{9,15},{10,... | collective-permute-start | bytes 196616 | tf_op jit(solution)/shard_map/ppermute | solution.py:511
  11.7 6.3 %collective-permute-start.8 = (bf16[2,128,128]{2,1,0:T(8,128)(2,1)S(1)}, bf16[2,128,128]{2,1,0:T(8,128)(2,1)S(1)}, u32[]{:S(2)}, u32[]{:S(2)}) collective-permute-start(bf16[2,128,128]{2,1,0:T(8,128)(2,1)S(1)} %get-tuple-element.89), channel_id=1, source_target_pairs={{0,3},{1,2},{2,1},{3,0},{4,7},{5,6},{6,5},{7,4},{8,11},{9,10},{10,... | collective-permute-start | bytes 196616 | tf_op jit(solution)/shard_map/ppermute | solution.py:511
  11.7 7.2 %collective-permute-start.9 = (bf16[2,128,128]{2,1,0:T(8,128)(2,1)S(1)}, bf16[2,128,128]{2,1,0:T(8,128)(2,1)S(1)}, u32[]{:S(2)}, u32[]{:S(2)}) collective-permute-start(bf16[2,128,128]{2,1,0:T(8,128)(2,1)S(1)} %get-tuple-element.90), channel_id=1, source_target_pairs={{0,5},{1,4},{2,7},{3,6},{4,1},{5,0},{6,3},{7,2},{8,13},{9,12},{10,... | collective-permute-start | bytes 196616 | tf_op jit(solution)/shard_map/ppermute | solution.py:511
  12.7 6.2 %collective-permute-start.10 = (bf16[2,128,128]{2,1,0:T(8,128)(2,1)S(1)}, bf16[2,128,128]{2,1,0:T(8,128)(2,1)S(1)}, u32[]{:S(2)}, u32[]{:S(2)}) collective-permute-start(bf16[2,128,128]{2,1,0:T(8,128)(2,1)S(1)} %totals.1), channel_id=1, source_target_pairs={{0,9},{1,8},{2,11},{3,10},{4,13},{5,12},{6,15},{7,14},{9,0},{8,1},... | collective-permute-start | bytes 196616 | tf_op jit(solution)/shard_map/ppermute | solution.py:533
  15.7 5.7 %collective-permute-start.4 = (bf16[2,128,128]{2,1,0:T(8,128)(2,1)S(1)}, bf16[2,128,128]{2,1,0:T(8,128)(2,1)S(1)}, u32[]{:S(2)}, u32[]{:S(2)}) collective-permute-start(bf16[2,128,128]{2,1,0:T(8,128)(2,1)S(1)} %get-tuple-element.77), channel_id=1, source_target_pairs={{0,6},{1,7},{2,4},{3,5},{4,2},{5,3},{6,0},{7,1},{8,14},{9,15},{10,... | collective-permute-start | bytes 196616 | tf_op jit(solution)/shard_map/ppermute | solution.py:511
  17.2 5.2 %collective-permute-start.5 = (bf16[2,128,128]{2,1,0:T(8,128)(2,1)S(1)}, bf16[2,128,128]{2,1,0:T(8,128)(2,1)S(1)}, u32[]{:S(2)}, u32[]{:S(2)}) collective-permute-start(bf16[2,128,128]{2,1,0:T(8,128)(2,1)S(1)} %get-tuple-element.78), channel_id=1, source_target_pairs={{0,3},{1,2},{2,1},{3,0},{4,7},{5,6},{6,5},{7,4},{8,11},{9,10},{10,... | collective-permute-start | bytes 196616 | tf_op jit(solution)/shard_map/ppermute | solution.py:511
  18.0 4.4 %collective-permute-start.6 = (bf16[2,128,128]{2,1,0:T(8,128)(2,1)S(1)}, bf16[2,128,128]{2,1,0:T(8,128)(2,1)S(1)}, u32[]{:S(2)}, u32[]{:S(2)}) collective-permute-start(bf16[2,128,128]{2,1,0:T(8,128)(2,1)S(1)} %get-tuple-element.79), channel_id=1, source_target_pairs={{0,5},{1,4},{2,7},{3,6},{4,1},{5,0},{6,3},{7,2},{8,13},{9,12},{10,... | collective-permute-start | bytes 196616 | tf_op jit(solution)/shard_map/ppermute | solution.py:511
  19.1 5.5 %collective-permute-start.11 = (bf16[2,128,128]{2,1,0:T(8,128)(2,1)S(1)}, bf16[2,128,128]{2,1,0:T(8,128)(2,1)S(1)}, u32[]{:S(2)}, u32[]{:S(2)}) collective-permute-start(bf16[2,128,128]{2,1,0:T(8,128)(2,1)S(1)} %get-tuple-element.92), channel_id=1, source_target_pairs={{0,6},{1,7},{2,4},{3,5},{4,2},{5,3},{6,0},{7,1},{8,14},{9,15},{10,... | collective-permute-start | bytes 196616 | tf_op jit(solution)/shard_map/ppermute | solution.py:511
  21.0 4.5 %collective-permute-start.12 = (bf16[2,128,128]{2,1,0:T(8,128)(2,1)S(1)}, bf16[2,128,128]{2,1,0:T(8,128)(2,1)S(1)}, u32[]{:S(2)}, u32[]{:S(2)}) collective-permute-start(bf16[2,128,128]{2,1,0:T(8,128)(2,1)S(1)} %get-tuple-element.93), channel_id=1, source_target_pairs={{0,3},{1,2},{2,1},{3,0},{4,7},{5,6},{6,5},{7,4},{8,11},{9,10},{10,... | collective-permute-start | bytes 196616 | tf_op jit(solution)/shard_map/ppermute | solution.py:511
  21.4 4.2 %collective-permute-start.13 = (bf16[2,128,128]{2,1,0:T(8,128)(2,1)S(1)}, bf16[2,128,128]{2,1,0:T(8,128)(2,1)S(1)}, u32[]{:S(2)}, u32[]{:S(2)}) collective-permute-start(bf16[2,128,128]{2,1,0:T(8,128)(2,1)S(1)} %get-tuple-element.94), channel_id=1, source_target_pairs={{0,5},{1,4},{2,7},{3,6},{4,1},{5,0},{6,3},{7,2},{8,13},{9,12},{10,... | collective-permute-start | bytes 196616 | tf_op jit(solution)/shard_map/ppermute | solution.py:511
  22.6 3.5 %collective-permute-start.15 = (bf16[8,128,128]{2,1,0:T(8,128)(2,1)S(1)}, bf16[8,128,128]{2,1,0:T(8,128)(2,1)S(1)}, u32[]{:S(2)}, u32[]{:S(2)}) collective-permute-start(bf16[8,128,128]{2,1,0:T(8,128)(2,1)S(1)} %get-tuple-element.100), channel_id=1, source_target_pairs={{0,1},{1,0},{2,3},{3,2},{4,5},{5,4},{6,7},{7,6},{8,9},{9,8},{10,11... | collective-permute-start | bytes 786440 | tf_op jit(solution)/shard_map/ppermute | solution.py:547
  25.7 1.8 %collective-permute-start.14 = (bf16[8,128,128]{2,1,0:T(8,128)(2,1)S(1)}, bf16[8,128,128]{2,1,0:T(8,128)(2,1)S(1)}, u32[]{:S(2)}, u32[]{:S(2)}) collective-permute-start(bf16[8,128,128]{2,1,0:T(8,128)(2,1)S(1)} %get-tuple-element.95), channel_id=1, source_target_pairs={{0,1},{1,0},{2,3},{3,2},{4,5},{5,4},{6,7},{7,6},{8,9},{9,8},{10,11... | collective-permute-start | bytes 786440 | tf_op jit(solution)/shard_map/ppermute | solution.py:547

commit v26 on v25

--- a/solution.py
+++ b/solution.py
@@ -260,8 +260,8 @@
 
     def run(kind):
         for i in range(heads):
-            at = pl.ds(i * HD, HD)
-            outs[0][:, at], outs[1][:, at] = outputs_of(kind, fixed, 0, s_ref[i], kt_ref, qt_ref, i)
+            for j in range(2):
+                outs[j][:, pl.ds(i * HD, HD)] = output_of(kind, j, fixed, 0, s_ref[i], kt_ref, qt_ref, i)
 
     on_kind(0, split, run)
 
@@ -343,69 +343,59 @@
 FIXED = 13
 
 
-def outputs_of(kind, fixed_refs, other, state, kt_ref, qt_ref, i):
+def output_of(kind, j, fixed_refs, other, state, kt_ref, qt_ref, i):
     q_ref, k_ref, v_ref = fixed_refs[3 * other :][:3]
     g_ref, w_ref, wt_ref, dw_ref, dwt_ref, mask_ref, root_ref = fixed_refs[6:]
     cols = pl.ds(i * HD, HD)
-    q, k, v = q_ref[:, cols], k_ref[:, cols], v_ref[:, cols]
     h = other * (q_ref.shape[1] // HD) + i
-    g = g_ref[:, pl.ds(h * HD, HD)]
+    scaled = pl.ds(h * HD, HD)
+    mask = mask_ref[kind]
 
     def wide(a, b):
         return jnp.concatenate([a, b], axis=1)
 
-    if kind == 0:
-        prefix = mask_ref[0]
-        o = dot(wide(w_ref[h], q * prefix), jnp.concatenate([v, state], axis=0), (1, 0))
-        dq = dot(wide(dw_ref[h], g * prefix), wide(kt_ref[i], state), (1, 1))
-        return (o * root_ref[...]).astype(BF16), dq.astype(BF16)
-    suffix = mask_ref[1]
-    dk = dot(wide(dwt_ref[h], v * suffix), wide(qt_ref[i], state), (1, 1))
-    dv = dot(wide(wt_ref[h], k * suffix), jnp.concatenate([g, state], axis=0), (1, 0))
-    return dk.astype(BF16), dv.astype(BF16)
-
-
-def write(refs, columns, kind, outs, to, sems):
-    copies = [
-        pltpu.make_async_copy(refs[j].at[:, columns], outs[2 * kind + j].at[:, to], sems.at[j])
-        for j in range(2)
-    ]
-    for copy in copies:
-        copy.start()
+    def tall(a, b):
+        return jnp.concatenate([a, b], axis=0)
+
+    if (kind, j) == (0, 0):
+        o = dot(wide(w_ref[h], q_ref[:, cols] * mask), tall(v_ref[:, cols], state), (1, 0))
+        return (o * root_ref[...]).astype(BF16)
+    if (kind, j) == (0, 1):
+        out = dot(wide(dw_ref[h], g_ref[:, scaled] * mask), wide(kt_ref[i], state), (1, 1))
+    elif (kind, j) == (1, 0):
+        out = dot(wide(dwt_ref[h], v_ref[:, cols] * mask), wide(qt_ref[i], state), (1, 1))
+    else:
+        out = dot(wide(wt_ref[h], k_ref[:, cols] * mask), tall(g_ref[:, scaled], state), (1, 0))
+    return out.astype(BF16)
+
+
+def write(ref, out, half, sem):
+    width = ref.shape[1]
+    to = pl.ds(pl.multiple_of(half * width, HD), width)
+    copy = pltpu.make_async_copy(ref, out.at[:, to], sem)
+    copy.start()
+    return copy
+
+
+def half_of(kind, fixed, other, s_ref, kt_ref, qt_ref, bufs, outs=None, sems=None):
+    copies = []
+    half = 1 - half_index() if other else half_index()
+    for j in range(2):
+        for i in range(s_ref.shape[0]):
+            at = pl.ds(i * HD, HD)
+            bufs[j][:, at] = output_of(kind, j, fixed, other, s_ref[i], kt_ref, qt_ref, i)
+        if outs:
+            copies.append(write(bufs[j], outs[2 * kind + j], half, sems.at[j]))
     return copies
 
 
-def place(half, width):
-    return pl.ds(pl.multiple_of(half * width, HD), width)
-
-
-def half_of(kind, fixed, other, s_ref, kt_ref, qt_ref, bufs, chunks=1, send=None):
-    heads = s_ref.shape[0]
-    size = heads * HD // chunks
-    copies = []
-    for c in range(chunks):
-        for i in range(c * heads // chunks, (c + 1) * heads // chunks):
-            at = pl.ds(i * HD, HD)
-            bufs[0][:, at], bufs[1][:, at] = outputs_of(kind, fixed, other, s_ref[i], kt_ref, qt_ref, i)
-        if send:
-            copies += send(c, pl.ds(c * size, size))
-    return copies
-
-
-def middle_kernel(split, chunks, *refs):
+def middle_kernel(split, *refs):
     early, fixed, early_refs, late_refs = refs[:2], refs[2 : FIXED + 2], refs[FIXED + 2 :][:3], refs[FIXED + 5 :][:3]
     outs, late, bufs, (own_sems, sems) = refs[-10:-6], refs[-6:-4], refs[-4:-2], refs[-2:]
-    width = early[0].shape[1]
-    mine = half_index()
 
     def run(kind):
-        copies = write(early, pl.ds(0, width), kind, outs, place(mine, width), own_sems)
-
-        def send(c, at):
-            to = place((1 - mine) * chunks + c, width // chunks)
-            return write(bufs, at, kind, outs, to, sems.at[c])
-
-        copies += half_of(kind, fixed, 1, *early_refs, bufs, chunks, send)
+        copies = [write(early[j], outs[2 * kind + j], half_index(), own_sems.at[j]) for j in range(2)]
+        copies += half_of(kind, fixed, 1, *early_refs, bufs, outs, sems)
         half_of(1 - kind, fixed, 0, *late_refs, late)
         for copy in copies:
             copy.wait()
@@ -413,20 +403,13 @@
     on_kind(0, split, run)
 
 
-def last_kernel(split, chunks, *refs):
+def last_kernel(split, *refs):
     fixed, late_refs, late = refs[:FIXED], refs[FIXED : FIXED + 3], refs[FIXED + 3 :][:2]
     outs, bufs, (own_sems, sems) = refs[-8:-4], refs[-4:-2], refs[-2:]
-    width = late[0].shape[1]
-    mine = half_index()
 
     def run(kind):
-        copies = write(late, pl.ds(0, width), kind, outs, place(mine, width), own_sems)
-
-        def send(c, at):
-            to = place((1 - mine) * chunks + c, width // chunks)
-            return write(bufs, at, kind, outs, to, sems.at[c])
-
-        copies += half_of(kind, fixed, 1, *late_refs, bufs, chunks, send)
+        copies = [write(late[j], outs[2 * kind + j], half_index(), own_sems.at[j]) for j in range(2)]
+        copies += half_of(kind, fixed, 1, *late_refs, bufs, outs, sems)
         for copy in copies:
             copy.wait()
 
@@ -559,13 +542,12 @@
     late_mine, late_other = post(1, range(PAIRS), masks)
     w, wt, dw, dwt, scaled = local
     fixed = (*mines[:3], *others[:3], scaled, w, wt, dw, dwt, masks, root)
-    chunks = 2
     scratch = [pltpu.VMEM(part.shape, BF16)] * 2 + [
         pltpu.SemaphoreType.DMA((2,)),
-        pltpu.SemaphoreType.DMA((chunks, 2)),
+        pltpu.SemaphoreType.DMA((2,)),
     ]
     *outs, late_0, late_1 = call(
-        functools.partial(middle_kernel, split, chunks),
+        functools.partial(middle_kernel, split),
         "middle",
         [tokens] * 4 + [part] * 2,
         (early_0, early_1, *fixed, early_other, kt_other, qt_other, late_mine, kt_mine, qt_mine),
@@ -577,7 +559,7 @@
     given = (*fixed, late_other, kt_other, qt_other, late_0, late_1)
     return tuple(
         call(
-            functools.partial(last_kernel, split, chunks),
+            functools.partial(last_kernel, split),
             "last",
             [tokens] * 4,
             (*given, *outs),

time: 28.8 us -> 29.2 us (1.014)
  Pallas kernels: 8.5 us -> 8.93 us
    pallas_call x11, Pallas kernels: 8.5 us -> 8.93 us  [call(): pl.pallas_call(kernel, in_specs=specs, out_specs=out_specs or [vmem] * le...]
  transfers between devices with their start and end apart: 16 -> 16, of which waited for: 4 -> 4; matrix products, arithmetic and copies ran while one was open for 0% -> 0% of each run, Pallas kernels for 19% -> 20%
where the time goes in v26:
time: 29.2 us; the launch traced here: 29.1 us
  starting transfers between devices  17.9 us (61%)
  Pallas kernels  8.93 us (31%)
  waiting for transfers between devices  1.54 us (5%)
  between operations  0.73 us (2%)
    ppermute x12, starting transfers between devices, trade(): lax.ppermute(parts[d], 'seq', [(i, i ^ STEPS[d]) for i in range(n)])  13.8 us
    pallas_call x11, Pallas kernels, call(): pl.pallas_call(kernel, in_specs=specs, out_specs=out_specs or [vmem] * le...  8.93 us
    ppermute x1, starting transfers between devices, per_device(): enter = lax.ppermute(edge(0), 'seq', up + down)  2.83 us
    ppermute x12, waiting for transfers between devices, trade(): lax.ppermute(parts[d], 'seq', [(i, i ^ STEPS[d]) for i in range(n)])  1.53 us
    ppermute x2, starting transfers between devices, post(): return (own, lax.ppermute(theirs, 'seq', swap))  0.69 us
  transfers between devices with their start and end apart: 16, of which 4 were waited for; matrix products, arithmetic and copies ran while one was open for 0% of the time, Pallas kernels for 20%

profile of v26, /device:TPU:0, one launch (start us, length us, event | category | flops | bytes accessed | tf_op | source)
XLA Modules:
  0.0 29.1 jit_solution(5690897129865505292)
XLA Ops:
  0.6 1.7 %send.1 = (s32[8]{0:T(128)S(1)}, bf16[2,8,128,128]{3,2,1,0:T(8,128)(2,1)S(1)}, bf16[128,1024]{1,0:T(8,128)(2,1)S(1)}, bf16[128,1024]{1,0:T(8,128)(2,1)S(1)}, bf1...) custom-call(s32[8]{0:T(128)} %len_hbm.1, ...), custom_call_target="tpu_custom_call" | custom-call | flops 67108864 | bytes 4325440 | tf_op jit(solution)/shard_map/send/pallas_call | solution.py:435
  2.4 0.5 %collective-permute-start = (bf16[2,8,128,128]{3,2,1,0:T(8,128)(2,1)S(1)}, bf16[2,8,128,128]{3,2,1,0:T(8,128)(2,1)S(1)}, u32[]{:S(2)}, u32[]{:S(2)}) collective-permute-start(bf16[2,8,128,128]{3,2,1,0:T(8,128)(2,1)S(1)} %get-tuple-element.71), channel_id=1, source_target_pairs={{0,1},{1,0},{2,3},{3,2},{4,5},{5,4},{6,7},{7,6},{8,9},{9,8},{10,11... | collective-permute-start | bytes 1572872 | tf_op jit(solution)/shard_map/ppermute | solution.py:470
  2.9 1.7 %keep.1 = (bf16[2,8,128,128]{3,2,1,0:T(8,128)(2,1)S(1)}, bf16[128,1024]{1,0:T(8,128)(2,1)S(1)}, bf16[128,1024]{1,0:T(8,128)(2,1)S(1)}, bf16[128,1024]{1,0:T(8,12...) custom-call(s32[8]{0:T(128)S(1)} %get-tuple-element.56.len_hbm, ...), custom_call_target="tpu_custom_call" | custom-call | flops 67108864 | bytes 4358176 | tf_op jit(solution)/shard_map/keep/pallas_call | solution.py:435
  4.6 0.0 collective-permute-done.got_ref
  4.6 0.1 pair.1
  4.7 3.8 %collective-permute-start.1 = (bf16[2,128,128]{2,1,0:T(8,128)(2,1)S(1)}, bf16[2,128,128]{2,1,0:T(8,128)(2,1)S(1)}, u32[]{:S(2)}, u32[]{:S(2)}) collective-permute-start(bf16[2,128,128]{2,1,0:T(8,128)(2,1)S(1)} %get-tuple-element.73), channel_id=1, source_target_pairs={{0,6},{1,7},{2,4},{3,5},{4,2},{5,3},{6,0},{7,1},{8,14},{9,15},{10,... | collective-permute-start | bytes 196616 | tf_op jit(solution)/shard_map/ppermute | solution.py:494
  8.5 0.2 collective-permute-start.2
  8.7 0.2 collective-permute-start.3
  8.9 2.8 %collective-permute-start.7 = (bf16[2,128,128]{2,1,0:T(8,128)(2,1)S(1)}, bf16[2,128,128]{2,1,0:T(8,128)(2,1)S(1)}, u32[]{:S(2)}, u32[]{:S(2)}) collective-permute-start(bf16[2,128,128]{2,1,0:T(8,128)(2,1)S(1)} %get-tuple-element.88), channel_id=1, source_target_pairs={{0,6},{1,7},{2,4},{3,5},{4,2},{5,3},{6,0},{7,1},{8,14},{9,15},{10,... | collective-permute-start | bytes 196616 | tf_op jit(solution)/shard_map/ppermute | solution.py:494
  11.7 0.4 %collective-permute-start.9 = (bf16[2,128,128]{2,1,0:T(8,128)(2,1)S(1)}, bf16[2,128,128]{2,1,0:T(8,128)(2,1)S(1)}, u32[]{:S(2)}, u32[]{:S(2)}) collective-permute-start(bf16[2,128,128]{2,1,0:T(8,128)(2,1)S(1)} %get-tuple-element.90), channel_id=1, source_target_pairs={{0,5},{1,4},{2,7},{3,6},{4,1},{5,0},{6,3},{7,2},{8,13},{9,12},{10,... | collective-permute-start | bytes 196616 | tf_op jit(solution)/shard_map/ppermute | solution.py:494
  12.1 0.6 %collective-permute-done.2.refs_2_.s2 = bf16[2,128,128]{2,1,0:T(8,128)(2,1)S(1)} collective-permute-done((bf16[2,128,128]{2,1,0:T(8,128)(2,1)S(1)}, bf16[2,128,128]{2,1,0:T(8,128)(2,1)S(1)}, u32[]{:S(2)}, u32[]{:S(2)}) %collective-permute-start.2) | collective-permute-done | bytes 65568 | tf_op jit(solution)/shard_map/ppermute | solution.py:494
  12.7 0.1 totals.1
  12.7 2.8 %collective-permute-start.10 = (bf16[2,128,128]{2,1,0:T(8,128)(2,1)S(1)}, bf16[2,128,128]{2,1,0:T(8,128)(2,1)S(1)}, u32[]{:S(2)}, u32[]{:S(2)}) collective-permute-start(bf16[2,128,128]{2,1,0:T(8,128)(2,1)S(1)} %totals.1), channel_id=1, source_target_pairs={{0,9},{1,8},{2,11},{3,10},{4,13},{5,12},{6,15},{7,14},{9,0},{8,1},... | collective-permute-start | bytes 196616 | tf_op jit(solution)/shard_map/ppermute | solution.py:516
  15.6 0.1 scan.2
  15.7 1.5 %collective-permute-start.4 = (bf16[2,128,128]{2,1,0:T(8,128)(2,1)S(1)}, bf16[2,128,128]{2,1,0:T(8,128)(2,1)S(1)}, u32[]{:S(2)}, u32[]{:S(2)}) collective-permute-start(bf16[2,128,128]{2,1,0:T(8,128)(2,1)S(1)} %get-tuple-element.77), channel_id=1, source_target_pairs={{0,6},{1,7},{2,4},{3,5},{4,2},{5,3},{6,0},{7,1},{8,14},{9,15},{10,... | collective-permute-start | bytes 196616 | tf_op jit(solution)/shard_map/ppermute | solution.py:494
  17.2 0.8 %collective-permute-start.5 = (bf16[2,128,128]{2,1,0:T(8,128)(2,1)S(1)}, bf16[2,128,128]{2,1,0:T(8,128)(2,1)S(1)}, u32[]{:S(2)}, u32[]{:S(2)}) collective-permute-start(bf16[2,128,128]{2,1,0:T(8,128)(2,1)S(1)} %get-tuple-element.78), channel_id=1, source_target_pairs={{0,3},{1,2},{2,1},{3,0},{4,7},{5,6},{6,5},{7,4},{8,11},{9,10},{10,... | collective-permute-start | bytes 196616 | tf_op jit(solution)/shard_map/ppermute | solution.py:494
  18.0 0.9 %collective-permute-start.6 = (bf16[2,128,128]{2,1,0:T(8,128)(2,1)S(1)}, bf16[2,128,128]{2,1,0:T(8,128)(2,1)S(1)}, u32[]{:S(2)}, u32[]{:S(2)}) collective-permute-start(bf16[2,128,128]{2,1,0:T(8,128)(2,1)S(1)} %get-tuple-element.79), channel_id=1, source_target_pairs={{0,5},{1,4},{2,7},{3,6},{4,1},{5,0},{6,3},{7,2},{8,13},{9,12},{10,... | collective-permute-start | bytes 196616 | tf_op jit(solution)/shard_map/ppermute | solution.py:494
  19.0 0.2 scan.3
  19.1 1.8 %collective-permute-start.11 = (bf16[2,128,128]{2,1,0:T(8,128)(2,1)S(1)}, bf16[2,128,128]{2,1,0:T(8,128)(2,1)S(1)}, u32[]{:S(2)}, u32[]{:S(2)}) collective-permute-start(bf16[2,128,128]{2,1,0:T(8,128)(2,1)S(1)} %get-tuple-element.92), channel_id=1, source_target_pairs={{0,6},{1,7},{2,4},{3,5},{4,2},{5,3},{6,0},{7,1},{8,14},{9,15},{10,... | collective-permute-start | bytes 196616 | tf_op jit(solution)/shard_map/ppermute | solution.py:494
  21.0 0.3 %collective-permute-start.12 = (bf16[2,128,128]{2,1,0:T(8,128)(2,1)S(1)}, bf16[2,128,128]{2,1,0:T(8,128)(2,1)S(1)}, u32[]{:S(2)}, u32[]{:S(2)}) collective-permute-start(bf16[2,128,128]{2,1,0:T(8,128)(2,1)S(1)} %get-tuple-element.93), channel_id=1, source_target_pairs={{0,3},{1,2},{2,1},{3,0},{4,7},{5,6},{6,5},{7,4},{8,11},{9,10},{10,... | collective-permute-start | bytes 196616 | tf_op jit(solution)/shard_map/ppermute | solution.py:494
  21.3 0.1 collective-permute-done.4.refs_1_
  21.4 1.1 %collective-permute-start.13 = (bf16[2,128,128]{2,1,0:T(8,128)(2,1)S(1)}, bf16[2,128,128]{2,1,0:T(8,128)(2,1)S(1)}, u32[]{:S(2)}, u32[]{:S(2)}) collective-permute-start(bf16[2,128,128]{2,1,0:T(8,128)(2,1)S(1)} %get-tuple-element.94), channel_id=1, source_target_pairs={{0,5},{1,4},{2,7},{3,6},{4,1},{5,0},{6,3},{7,2},{8,13},{9,12},{10,... | collective-permute-start | bytes 196616 | tf_op jit(solution)/shard_map/ppermute | solution.py:494
  22.4 0.0 collective-permute-done.5.refs_2_
  22.4 0.1 post.2
  22.6 0.3 collective-permute-start.15
  22.9 1.8 %local.1 = (bf16[16,128,128]{2,1,0:T(8,128)(2,1)S(1)}, bf16[16,128,128]{2,1,0:T(8,128)(2,1)S(1)}, bf16[16,128,128]{2,1,0:T(8,128)(2,1)S(1)}, bf16[16,128,128]{2,...) custom-call(s32[8]{0:T(128)S(1)} %get-tuple-element.56.len_hbm, ...), custom_call_target="tpu_custom_call" | custom-call | flops 134217728 | bytes 6160416 | tf_op jit(solution)/shard_map/local/pallas_call | solution.py:435
  24.7 0.8 %collective-permute-done.12.refs_2_ = bf16[2,128,128]{2,1,0:T(8,128)(2,1)S(1)} collective-permute-done((bf16[2,128,128]{2,1,0:T(8,128)(2,1)S(1)}, bf16[2,128,128]{2,1,0:T(8,128)(2,1)S(1)}, u32[]{:S(2)}, u32[]{:S(2)}) %collective-permute-start.12) | collective-permute-done | bytes 65568 | tf_op jit(solution)/shard_map/ppermute | solution.py:494
  25.5 0.1 collective-permute-done.13.refs_3_
  25.6 0.1 post.3
  25.7 0.4 %collective-permute-start.14 = (bf16[8,128,128]{2,1,0:T(8,128)(2,1)S(1)}, bf16[8,128,128]{2,1,0:T(8,128)(2,1)S(1)}, u32[]{:S(2)}, u32[]{:S(2)}) collective-permute-start(bf16[8,128,128]{2,1,0:T(8,128)(2,1)S(1)} %get-tuple-element.95), channel_id=1, source_target_pairs={{0,1},{1,0},{2,3},{3,2},{4,5},{5,4},{6,7},{7,6},{8,9},{9,8},{10,11... | collective-permute-start | bytes 786440 | tf_op jit(solution)/shard_map/ppermute | solution.py:530
  26.1 1.6 %middle.1 = (bf16[128,2048]{1,0:T(8,128)(2,1)}, bf16[128,2048]{1,0:T(8,128)(2,1)}, bf16[128,2048]{1,0:T(8,128)(2,1)}, bf16[128,2048]{1,0:T(8,128)(2,1)}, bf16[12...) custom-call(bf16[128,1024]{1,0:T(8,128)(2,1)S(1)} %get-tuple-element.98.refs_0_, ...), custom_call_target="tpu_custom_call" | custom-call | flops 268435456 | bytes 9043968 | tf_op jit(solution)/shard_map/middle/pallas_call | solution.py:435
  27.7 1.4 %last.1 = (bf16[128,2048]{1,0:T(8,128)(2,1)}, bf16[128,2048]{1,0:T(8,128)(2,1)}, bf16[128,2048]{1,0:T(8,128)(2,1)}, bf16[128,2048]{1,0:T(8,128)(2,1)}) custom-call(bf16[128,1024]{1,0:T(8,128)(2,1)S(1)} %get-tuple-element.59.refs_0_.refs_2_, ...), custom_call_target="tpu_custom_call", output_to_operand_aliasing={{0}: (18, {}), {1}: (19, {}), {2}: (20, {}), {3}: (21, {})} | custom-call | flops 134217728 | bytes 9830400 | tf_op jit(solution)/shard_map/last/pallas_call | solution.py:435
  (11 shorter events, 0.0 us)
Async XLA Ops:
  2.4 2.2 %collective-permute-start = (bf16[2,8,128,128]{3,2,1,0:T(8,128)(2,1)S(1)}, bf16[2,8,128,128]{3,2,1,0:T(8,128)(2,1)S(1)}, u32[]{:S(2)}, u32[]{:S(2)}) collective-permute-start(bf16[2,8,128,128]{3,2,1,0:T(8,128)(2,1)S(1)} %get-tuple-element.71), channel_id=1, source_target_pairs={{0,1},{1,0},{2,3},{3,2},{4,5},{5,4},{6,7},{7,6},{8,9},{9,8},{10,11... | collective-permute-start | bytes 1572872 | tf_op jit(solution)/shard_map/ppermute | solution.py:470
  4.7 7.0 %collective-permute-start.1 = (bf16[2,128,128]{2,1,0:T(8,128)(2,1)S(1)}, bf16[2,128,128]{2,1,0:T(8,128)(2,1)S(1)}, u32[]{:S(2)}, u32[]{:S(2)}) collective-permute-start(bf16[2,128,128]{2,1,0:T(8,128)(2,1)S(1)} %get-tuple-element.73), channel_id=1, source_target_pairs={{0,6},{1,7},{2,4},{3,5},{4,2},{5,3},{6,0},{7,1},{8,14},{9,15},{10,... | collective-permute-start | bytes 196616 | tf_op jit(solution)/shard_map/ppermute | solution.py:494
  8.5 4.2 %collective-permute-start.2 = (bf16[2,128,128]{2,1,0:T(8,128)(2,1)S(1)}, bf16[2,128,128]{2,1,0:T(8,128)(2,1)S(1)}, u32[]{:S(2)}, u32[]{:S(2)}) collective-permute-start(bf16[2,128,128]{2,1,0:T(8,128)(2,1)S(1)} %get-tuple-element.74), channel_id=1, source_target_pairs={{0,3},{1,2},{2,1},{3,0},{4,7},{5,6},{6,5},{7,4},{8,11},{9,10},{10,... | collective-permute-start | bytes 196616 | tf_op jit(solution)/shard_map/ppermute | solution.py:494
  8.7 4.0 %collective-permute-start.3 = (bf16[2,128,128]{2,1,0:T(8,128)(2,1)S(1)}, bf16[2,128,128]{2,1,0:T(8,128)(2,1)S(1)}, u32[]{:S(2)}, u32[]{:S(2)}) collective-permute-start(bf16[2,128,128]{2,1,0:T(8,128)(2,1)S(1)} %get-tuple-element.75), channel_id=1, source_target_pairs={{0,5},{1,4},{2,7},{3,6},{4,1},{5,0},{6,3},{7,2},{8,13},{9,12},{10,... | collective-permute-start | bytes 196616 | tf_op jit(solution)/shard_map/ppermute | solution.py:494
  8.9 8.4 %collective-permute-start.7 = (bf16[2,128,128]{2,1,0:T(8,128)(2,1)S(1)}, bf16[2,128,128]{2,1,0:T(8,128)(2,1)S(1)}, u32[]{:S(2)}, u32[]{:S(2)}) collective-permute-start(bf16[2,128,128]{2,1,0:T(8,128)(2,1)S(1)} %get-tuple-element.88), channel_id=1, source_target_pairs={{0,6},{1,7},{2,4},{3,5},{4,2},{5,3},{6,0},{7,1},{8,14},{9,15},{10,... | collective-permute-start | bytes 196616 | tf_op jit(solution)/shard_map/ppermute | solution.py:494
  11.7 6.3 %collective-permute-start.8 = (bf16[2,128,128]{2,1,0:T(8,128)(2,1)S(1)}, bf16[2,128,128]{2,1,0:T(8,128)(2,1)S(1)}, u32[]{:S(2)}, u32[]{:S(2)}) collective-permute-start(bf16[2,128,128]{2,1,0:T(8,128)(2,1)S(1)} %get-tuple-element.89), channel_id=1, source_target_pairs={{0,3},{1,2},{2,1},{3,0},{4,7},{5,6},{6,5},{7,4},{8,11},{9,10},{10,... | collective-permute-start | bytes 196616 | tf_op jit(solution)/shard_map/ppermute | solution.py:494
  11.7 7.2 %collective-permute-start.9 = (bf16[2,128,128]{2,1,0:T(8,128)(2,1)S(1)}, bf16[2,128,128]{2,1,0:T(8,128)(2,1)S(1)}, u32[]{:S(2)}, u32[]{:S(2)}) collective-permute-start(bf16[2,128,128]{2,1,0:T(8,128)(2,1)S(1)} %get-tuple-element.90), channel_id=1, source_target_pairs={{0,5},{1,4},{2,7},{3,6},{4,1},{5,0},{6,3},{7,2},{8,13},{9,12},{10,... | collective-permute-start | bytes 196616 | tf_op jit(solution)/shard_map/ppermute | solution.py:494
  12.7 6.2 %collective-permute-start.10 = (bf16[2,128,128]{2,1,0:T(8,128)(2,1)S(1)}, bf16[2,128,128]{2,1,0:T(8,128)(2,1)S(1)}, u32[]{:S(2)}, u32[]{:S(2)}) collective-permute-start(bf16[2,128,128]{2,1,0:T(8,128)(2,1)S(1)} %totals.1), channel_id=1, source_target_pairs={{0,9},{1,8},{2,11},{3,10},{4,13},{5,12},{6,15},{7,14},{9,0},{8,1},... | collective-permute-start | bytes 196616 | tf_op jit(solution)/shard_map/ppermute | solution.py:516
  15.7 5.7 %collective-permute-start.4 = (bf16[2,128,128]{2,1,0:T(8,128)(2,1)S(1)}, bf16[2,128,128]{2,1,0:T(8,128)(2,1)S(1)}, u32[]{:S(2)}, u32[]{:S(2)}) collective-permute-start(bf16[2,128,128]{2,1,0:T(8,128)(2,1)S(1)} %get-tuple-element.77), channel_id=1, source_target_pairs={{0,6},{1,7},{2,4},{3,5},{4,2},{5,3},{6,0},{7,1},{8,14},{9,15},{10,... | collective-permute-start | bytes 196616 | tf_op jit(solution)/shard_map/ppermute | solution.py:494
  17.2 5.2 %collective-permute-start.5 = (bf16[2,128,128]{2,1,0:T(8,128)(2,1)S(1)}, bf16[2,128,128]{2,1,0:T(8,128)(2,1)S(1)}, u32[]{:S(2)}, u32[]{:S(2)}) collective-permute-start(bf16[2,128,128]{2,1,0:T(8,128)(2,1)S(1)} %get-tuple-element.78), channel_id=1, source_target_pairs={{0,3},{1,2},{2,1},{3,0},{4,7},{5,6},{6,5},{7,4},{8,11},{9,10},{10,... | collective-permute-start | bytes 196616 | tf_op jit(solution)/shard_map/ppermute | solution.py:494
  18.0 4.4 %collective-permute-start.6 = (bf16[2,128,128]{2,1,0:T(8,128)(2,1)S(1)}, bf16[2,128,128]{2,1,0:T(8,128)(2,1)S(1)}, u32[]{:S(2)}, u32[]{:S(2)}) collective-permute-start(bf16[2,128,128]{2,1,0:T(8,128)(2,1)S(1)} %get-tuple-element.79), channel_id=1, source_target_pairs={{0,5},{1,4},{2,7},{3,6},{4,1},{5,0},{6,3},{7,2},{8,13},{9,12},{10,... | collective-permute-start | bytes 196616 | tf_op jit(solution)/shard_map/ppermute | solution.py:494
  19.1 5.5 %collective-permute-start.11 = (bf16[2,128,128]{2,1,0:T(8,128)(2,1)S(1)}, bf16[2,128,128]{2,1,0:T(8,128)(2,1)S(1)}, u32[]{:S(2)}, u32[]{:S(2)}) collective-permute-start(bf16[2,128,128]{2,1,0:T(8,128)(2,1)S(1)} %get-tuple-element.92), channel_id=1, source_target_pairs={{0,6},{1,7},{2,4},{3,5},{4,2},{5,3},{6,0},{7,1},{8,14},{9,15},{10,... | collective-permute-start | bytes 196616 | tf_op jit(solution)/shard_map/ppermute | solution.py:494
  21.0 4.5 %collective-permute-start.12 = (bf16[2,128,128]{2,1,0:T(8,128)(2,1)S(1)}, bf16[2,128,128]{2,1,0:T(8,128)(2,1)S(1)}, u32[]{:S(2)}, u32[]{:S(2)}) collective-permute-start(bf16[2,128,128]{2,1,0:T(8,128)(2,1)S(1)} %get-tuple-element.93), channel_id=1, source_target_pairs={{0,3},{1,2},{2,1},{3,0},{4,7},{5,6},{6,5},{7,4},{8,11},{9,10},{10,... | collective-permute-start | bytes 196616 | tf_op jit(solution)/shard_map/ppermute | solution.py:494
  21.4 4.2 %collective-permute-start.13 = (bf16[2,128,128]{2,1,0:T(8,128)(2,1)S(1)}, bf16[2,128,128]{2,1,0:T(8,128)(2,1)S(1)}, u32[]{:S(2)}, u32[]{:S(2)}) collective-permute-start(bf16[2,128,128]{2,1,0:T(8,128)(2,1)S(1)} %get-tuple-element.94), channel_id=1, source_target_pairs={{0,5},{1,4},{2,7},{3,6},{4,1},{5,0},{6,3},{7,2},{8,13},{9,12},{10,... | collective-permute-start | bytes 196616 | tf_op jit(solution)/shard_map/ppermute | solution.py:494
  22.6 3.5 %collective-permute-start.15 = (bf16[8,128,128]{2,1,0:T(8,128)(2,1)S(1)}, bf16[8,128,128]{2,1,0:T(8,128)(2,1)S(1)}, u32[]{:S(2)}, u32[]{:S(2)}) collective-permute-start(bf16[8,128,128]{2,1,0:T(8,128)(2,1)S(1)} %get-tuple-element.100), channel_id=1, source_target_pairs={{0,1},{1,0},{2,3},{3,2},{4,5},{5,4},{6,7},{7,6},{8,9},{9,8},{10,11... | collective-permute-start | bytes 786440 | tf_op jit(solution)/shard_map/ppermute | solution.py:530
  25.7 2.0 %collective-permute-start.14 = (bf16[8,128,128]{2,1,0:T(8,128)(2,1)S(1)}, bf16[8,128,128]{2,1,0:T(8,128)(2,1)S(1)}, u32[]{:S(2)}, u32[]{:S(2)}) collective-permute-start(bf16[8,128,128]{2,1,0:T(8,128)(2,1)S(1)} %get-tuple-element.95), channel_id=1, source_target_pairs={{0,1},{1,0},{2,3},{3,2},{4,5},{5,4},{6,7},{7,6},{8,9},{9,8},{10,11... | collective-permute-start | bytes 786440 | tf_op jit(solution)/shard_map/ppermute | solution.py:530

commit v27 on v25

--- a/solution.py
+++ b/solution.py
@@ -89,11 +89,10 @@
         for h, cols in enumerate(columns):
             t_ref[h] = ref[:, cols].T
     copies[2].wait()
-    for h, cols in enumerate(columns):
-        out_ref[0, h] = dot(kt_ref[h], v_ref[:, cols] * tail_rows, (1, 0)).astype(BF16)
     copies[3].wait()
     for h, cols in enumerate(columns):
         scaled = (g_ref[:, cols].astype(F32) * inv_root).astype(BF16)
+        out_ref[0, h] = dot(kt_ref[h], v_ref[:, cols] * tail_rows, (1, 0)).astype(BF16)
         out_ref[1, h] = dot(qt_ref[h], scaled * head_rows, (1, 0)).astype(BF16)
 
 

time: 28.8 us -> 28.7 us (level)
  waiting for transfers between devices: 1.55 us -> 2.36 us
  starting transfers between devices: 17.9 us -> 17.3 us
  Pallas kernels: 8.5 us -> 8.2 us
    ppermute x12, waiting for transfers between devices: 1.54 us -> 2.31 us  [trade(): lax.ppermute(parts[d], 'seq', [(i, i ^ STEPS[d]) for i in range(n)])]
    pallas_call x11, Pallas kernels: 8.5 us -> 8.2 us  [call(): pl.pallas_call(kernel, in_specs=specs, out_specs=out_specs or [vmem] * le...]
  transfers between devices with their start and end apart: 16 -> 16, of which waited for: 4 -> 5; matrix products, arithmetic and copies ran while one was open for 0% -> 0% of each run, Pallas kernels for 19% -> 19%
where the time goes in v27:
time: 28.7 us; the launch traced here: 28.5 us
  starting transfers between devices  17.3 us (60%)
  Pallas kernels  8.2 us (29%)
  waiting for transfers between devices  2.36 us (8%)
  between operations  0.72 us (3%)
    ppermute x12, starting transfers between devices, trade(): lax.ppermute(parts[d], 'seq', [(i, i ^ STEPS[d]) for i in range(n)])  13.6 us
    pallas_call x11, Pallas kernels, call(): pl.pallas_call(kernel, in_specs=specs, out_specs=out_specs or [vmem] * le...  8.2 us
    ppermute x1, starting transfers between devices, per_device(): enter = lax.ppermute(edge(0), 'seq', up + down)  2.69 us
    ppermute x12, waiting for transfers between devices, trade(): lax.ppermute(parts[d], 'seq', [(i, i ^ STEPS[d]) for i in range(n)])  2.31 us
  transfers between devices with their start and end apart: 16, of which 5 were waited for; matrix products, arithmetic and copies ran while one was open for 0% of the time, Pallas kernels for 19%

profile of v27, /device:TPU:0, one launch (start us, length us, event | category | flops | bytes accessed | tf_op | source)
XLA Modules:
  0.0 28.5 jit_solution(16693344125026566792)
XLA Ops:
  0.6 1.6 %send.1 = (s32[8]{0:T(128)S(1)}, bf16[2,8,128,128]{3,2,1,0:T(8,128)(2,1)S(1)}, bf16[128,1024]{1,0:T(8,128)(2,1)S(1)}, bf16[128,1024]{1,0:T(8,128)(2,1)S(1)}, bf1...) custom-call(s32[8]{0:T(128)} %len_hbm.1, ...), custom_call_target="tpu_custom_call" | custom-call | flops 67108864 | bytes 4325440 | tf_op jit(solution)/shard_map/send/pallas_call | solution.py:451
  2.2 0.5 %collective-permute-start = (bf16[2,8,128,128]{3,2,1,0:T(8,128)(2,1)S(1)}, bf16[2,8,128,128]{3,2,1,0:T(8,128)(2,1)S(1)}, u32[]{:S(2)}, u32[]{:S(2)}) collective-permute-start(bf16[2,8,128,128]{3,2,1,0:T(8,128)(2,1)S(1)} %get-tuple-element.71), channel_id=1, source_target_pairs={{0,1},{1,0},{2,3},{3,2},{4,5},{5,4},{6,7},{7,6},{8,9},{9,8},{10,11... | collective-permute-start | bytes 1572872 | tf_op jit(solution)/shard_map/ppermute | solution.py:486
  2.7 1.6 %keep.1 = (bf16[2,8,128,128]{3,2,1,0:T(8,128)(2,1)S(1)}, bf16[128,1024]{1,0:T(8,128)(2,1)S(1)}, bf16[128,1024]{1,0:T(8,128)(2,1)S(1)}, bf16[128,1024]{1,0:T(8,12...) custom-call(s32[8]{0:T(128)S(1)} %get-tuple-element.56.len_hbm, ...), custom_call_target="tpu_custom_call" | custom-call | flops 67108864 | bytes 4358176 | tf_op jit(solution)/shard_map/keep/pallas_call | solution.py:451
  4.3 0.1 pair.1
  4.5 3.9 %collective-permute-start.1 = (bf16[2,128,128]{2,1,0:T(8,128)(2,1)S(1)}, bf16[2,128,128]{2,1,0:T(8,128)(2,1)S(1)}, u32[]{:S(2)}, u32[]{:S(2)}) collective-permute-start(bf16[2,128,128]{2,1,0:T(8,128)(2,1)S(1)} %get-tuple-element.73), channel_id=1, source_target_pairs={{0,6},{1,7},{2,4},{3,5},{4,2},{5,3},{6,0},{7,1},{8,14},{9,15},{10,... | collective-permute-start | bytes 196616 | tf_op jit(solution)/shard_map/ppermute | solution.py:510
  8.4 0.0 collective-permute-start.2
  8.4 0.3 %collective-permute-start.3 = (bf16[2,128,128]{2,1,0:T(8,128)(2,1)S(1)}, bf16[2,128,128]{2,1,0:T(8,128)(2,1)S(1)}, u32[]{:S(2)}, u32[]{:S(2)}) collective-permute-start(bf16[2,128,128]{2,1,0:T(8,128)(2,1)S(1)} %get-tuple-element.75), channel_id=1, source_target_pairs={{0,5},{1,4},{2,7},{3,6},{4,1},{5,0},{6,3},{7,2},{8,13},{9,12},{10,... | collective-permute-start | bytes 196616 | tf_op jit(solution)/shard_map/ppermute | solution.py:510
  8.7 2.8 %collective-permute-start.7 = (bf16[2,128,128]{2,1,0:T(8,128)(2,1)S(1)}, bf16[2,128,128]{2,1,0:T(8,128)(2,1)S(1)}, u32[]{:S(2)}, u32[]{:S(2)}) collective-permute-start(bf16[2,128,128]{2,1,0:T(8,128)(2,1)S(1)} %get-tuple-element.88), channel_id=1, source_target_pairs={{0,6},{1,7},{2,4},{3,5},{4,2},{5,3},{6,0},{7,1},{8,14},{9,15},{10,... | collective-permute-start | bytes 196616 | tf_op jit(solution)/shard_map/ppermute | solution.py:510
  11.6 0.4 %collective-permute-start.9 = (bf16[2,128,128]{2,1,0:T(8,128)(2,1)S(1)}, bf16[2,128,128]{2,1,0:T(8,128)(2,1)S(1)}, u32[]{:S(2)}, u32[]{:S(2)}) collective-permute-start(bf16[2,128,128]{2,1,0:T(8,128)(2,1)S(1)} %get-tuple-element.90), channel_id=1, source_target_pairs={{0,5},{1,4},{2,7},{3,6},{4,1},{5,0},{6,3},{7,2},{8,13},{9,12},{10,... | collective-permute-start | bytes 196616 | tf_op jit(solution)/shard_map/ppermute | solution.py:510
  11.9 0.7 %collective-permute-done.2.refs_2_.s2 = bf16[2,128,128]{2,1,0:T(8,128)(2,1)S(1)} collective-permute-done((bf16[2,128,128]{2,1,0:T(8,128)(2,1)S(1)}, bf16[2,128,128]{2,1,0:T(8,128)(2,1)S(1)}, u32[]{:S(2)}, u32[]{:S(2)}) %collective-permute-start.2) | collective-permute-done | bytes 65568 | tf_op jit(solution)/shard_map/ppermute | solution.py:510
  12.7 0.1 totals.1
  12.7 2.7 %collective-permute-start.10 = (bf16[2,128,128]{2,1,0:T(8,128)(2,1)S(1)}, bf16[2,128,128]{2,1,0:T(8,128)(2,1)S(1)}, u32[]{:S(2)}, u32[]{:S(2)}) collective-permute-start(bf16[2,128,128]{2,1,0:T(8,128)(2,1)S(1)} %totals.1), channel_id=1, source_target_pairs={{0,9},{1,8},{2,11},{3,10},{4,13},{5,12},{6,15},{7,14},{9,0},{8,1},... | collective-permute-start | bytes 196616 | tf_op jit(solution)/shard_map/ppermute | solution.py:532
  15.4 0.1 scan.2
  15.5 1.5 %collective-permute-start.4 = (bf16[2,128,128]{2,1,0:T(8,128)(2,1)S(1)}, bf16[2,128,128]{2,1,0:T(8,128)(2,1)S(1)}, u32[]{:S(2)}, u32[]{:S(2)}) collective-permute-start(bf16[2,128,128]{2,1,0:T(8,128)(2,1)S(1)} %get-tuple-element.77), channel_id=1, source_target_pairs={{0,6},{1,7},{2,4},{3,5},{4,2},{5,3},{6,0},{7,1},{8,14},{9,15},{10,... | collective-permute-start | bytes 196616 | tf_op jit(solution)/shard_map/ppermute | solution.py:510
  17.1 0.6 %collective-permute-start.5 = (bf16[2,128,128]{2,1,0:T(8,128)(2,1)S(1)}, bf16[2,128,128]{2,1,0:T(8,128)(2,1)S(1)}, u32[]{:S(2)}, u32[]{:S(2)}) collective-permute-start(bf16[2,128,128]{2,1,0:T(8,128)(2,1)S(1)} %get-tuple-element.78), channel_id=1, source_target_pairs={{0,3},{1,2},{2,1},{3,0},{4,7},{5,6},{6,5},{7,4},{8,11},{9,10},{10,... | collective-permute-start | bytes 196616 | tf_op jit(solution)/shard_map/ppermute | solution.py:510
  17.7 1.1 %collective-permute-start.6 = (bf16[2,128,128]{2,1,0:T(8,128)(2,1)S(1)}, bf16[2,128,128]{2,1,0:T(8,128)(2,1)S(1)}, u32[]{:S(2)}, u32[]{:S(2)}) collective-permute-start(bf16[2,128,128]{2,1,0:T(8,128)(2,1)S(1)} %get-tuple-element.79), channel_id=1, source_target_pairs={{0,5},{1,4},{2,7},{3,6},{4,1},{5,0},{6,3},{7,2},{8,13},{9,12},{10,... | collective-permute-start | bytes 196616 | tf_op jit(solution)/shard_map/ppermute | solution.py:510
  18.8 0.2 scan.3
  19.0 1.8 %collective-permute-start.11 = (bf16[2,128,128]{2,1,0:T(8,128)(2,1)S(1)}, bf16[2,128,128]{2,1,0:T(8,128)(2,1)S(1)}, u32[]{:S(2)}, u32[]{:S(2)}) collective-permute-start(bf16[2,128,128]{2,1,0:T(8,128)(2,1)S(1)} %get-tuple-element.92), channel_id=1, source_target_pairs={{0,6},{1,7},{2,4},{3,5},{4,2},{5,3},{6,0},{7,1},{8,14},{9,15},{10,... | collective-permute-start | bytes 196616 | tf_op jit(solution)/shard_map/ppermute | solution.py:510
  20.8 0.1 collective-permute-start.12
  20.9 0.4 %collective-permute-done.4.refs_1_ = bf16[2,128,128]{2,1,0:T(8,128)(2,1)S(1)} collective-permute-done((bf16[2,128,128]{2,1,0:T(8,128)(2,1)S(1)}, bf16[2,128,128]{2,1,0:T(8,128)(2,1)S(1)}, u32[]{:S(2)}, u32[]{:S(2)}) %collective-permute-start.4) | collective-permute-done | bytes 65568 | tf_op jit(solution)/shard_map/ppermute | solution.py:510
  21.3 1.0 %collective-permute-start.13 = (bf16[2,128,128]{2,1,0:T(8,128)(2,1)S(1)}, bf16[2,128,128]{2,1,0:T(8,128)(2,1)S(1)}, u32[]{:S(2)}, u32[]{:S(2)}) collective-permute-start(bf16[2,128,128]{2,1,0:T(8,128)(2,1)S(1)} %get-tuple-element.94), channel_id=1, source_target_pairs={{0,5},{1,4},{2,7},{3,6},{4,1},{5,0},{6,3},{7,2},{8,13},{9,12},{10,... | collective-permute-start | bytes 196616 | tf_op jit(solution)/shard_map/ppermute | solution.py:510
  22.3 0.1 collective-permute-done.5.refs_2_
  22.4 0.1 post.2
  22.5 0.2 collective-permute-start.15
  22.7 1.8 %local.1 = (bf16[16,128,128]{2,1,0:T(8,128)(2,1)S(1)}, bf16[16,128,128]{2,1,0:T(8,128)(2,1)S(1)}, bf16[16,128,128]{2,1,0:T(8,128)(2,1)S(1)}, bf16[16,128,128]{2,...) custom-call(s32[8]{0:T(128)S(1)} %get-tuple-element.56.len_hbm, ...), custom_call_target="tpu_custom_call" | custom-call | flops 134217728 | bytes 6160416 | tf_op jit(solution)/shard_map/local/pallas_call | solution.py:451
  24.5 0.9 %collective-permute-done.12.refs_2_ = bf16[2,128,128]{2,1,0:T(8,128)(2,1)S(1)} collective-permute-done((bf16[2,128,128]{2,1,0:T(8,128)(2,1)S(1)}, bf16[2,128,128]{2,1,0:T(8,128)(2,1)S(1)}, u32[]{:S(2)}, u32[]{:S(2)}) %collective-permute-start.12) | collective-permute-done | bytes 65568 | tf_op jit(solution)/shard_map/ppermute | solution.py:510
  25.4 0.2 collective-permute-done.13.refs_3_
  25.6 0.1 post.3
  25.8 0.2 collective-permute-start.14
  26.0 1.3 %middle.1 = (bf16[128,2048]{1,0:T(8,128)(2,1)}, bf16[128,2048]{1,0:T(8,128)(2,1)}, bf16[128,2048]{1,0:T(8,128)(2,1)}, bf16[128,2048]{1,0:T(8,128)(2,1)}, bf16[12...) custom-call(bf16[128,1024]{1,0:T(8,128)(2,1)S(1)} %get-tuple-element.98.refs_0_, ...), custom_call_target="tpu_custom_call" | custom-call | flops 268435456 | bytes 9043968 | tf_op jit(solution)/shard_map/middle/pallas_call | solution.py:451
  27.3 0.0 collective-permute-done.14.refs_13_
  27.4 1.2 %last.1 = (bf16[128,2048]{1,0:T(8,128)(2,1)}, bf16[128,2048]{1,0:T(8,128)(2,1)}, bf16[128,2048]{1,0:T(8,128)(2,1)}, bf16[128,2048]{1,0:T(8,128)(2,1)}) custom-call(bf16[128,1024]{1,0:T(8,128)(2,1)S(1)} %get-tuple-element.59.refs_0_.refs_2_, ...), custom_call_target="tpu_custom_call", output_to_operand_aliasing={{0}: (18, {}), {1}: (19, {}), {2}: (20, {}), {3}: (21, {})} | custom-call | flops 134217728 | bytes 9830400 | tf_op jit(solution)/shard_map/last/pallas_call | solution.py:451
  (11 shorter events, 0.0 us)
Async XLA Ops:
  2.2 2.1 %collective-permute-start = (bf16[2,8,128,128]{3,2,1,0:T(8,128)(2,1)S(1)}, bf16[2,8,128,128]{3,2,1,0:T(8,128)(2,1)S(1)}, u32[]{:S(2)}, u32[]{:S(2)}) collective-permute-start(bf16[2,8,128,128]{3,2,1,0:T(8,128)(2,1)S(1)} %get-tuple-element.71), channel_id=1, source_target_pairs={{0,1},{1,0},{2,3},{3,2},{4,5},{5,4},{6,7},{7,6},{8,9},{9,8},{10,11... | collective-permute-start | bytes 1572872 | tf_op jit(solution)/shard_map/ppermute | solution.py:486
  4.5 7.1 %collective-permute-start.1 = (bf16[2,128,128]{2,1,0:T(8,128)(2,1)S(1)}, bf16[2,128,128]{2,1,0:T(8,128)(2,1)S(1)}, u32[]{:S(2)}, u32[]{:S(2)}) collective-permute-start(bf16[2,128,128]{2,1,0:T(8,128)(2,1)S(1)} %get-tuple-element.73), channel_id=1, source_target_pairs={{0,6},{1,7},{2,4},{3,5},{4,2},{5,3},{6,0},{7,1},{8,14},{9,15},{10,... | collective-permute-start | bytes 196616 | tf_op jit(solution)/shard_map/ppermute | solution.py:510
  8.4 4.3 %collective-permute-start.2 = (bf16[2,128,128]{2,1,0:T(8,128)(2,1)S(1)}, bf16[2,128,128]{2,1,0:T(8,128)(2,1)S(1)}, u32[]{:S(2)}, u32[]{:S(2)}) collective-permute-start(bf16[2,128,128]{2,1,0:T(8,128)(2,1)S(1)} %get-tuple-element.74), channel_id=1, source_target_pairs={{0,3},{1,2},{2,1},{3,0},{4,7},{5,6},{6,5},{7,4},{8,11},{9,10},{10,... | collective-permute-start | bytes 196616 | tf_op jit(solution)/shard_map/ppermute | solution.py:510
  8.4 4.3 %collective-permute-start.3 = (bf16[2,128,128]{2,1,0:T(8,128)(2,1)S(1)}, bf16[2,128,128]{2,1,0:T(8,128)(2,1)S(1)}, u32[]{:S(2)}, u32[]{:S(2)}) collective-permute-start(bf16[2,128,128]{2,1,0:T(8,128)(2,1)S(1)} %get-tuple-element.75), channel_id=1, source_target_pairs={{0,5},{1,4},{2,7},{3,6},{4,1},{5,0},{6,3},{7,2},{8,13},{9,12},{10,... | collective-permute-start | bytes 196616 | tf_op jit(solution)/shard_map/ppermute | solution.py:510
  8.7 8.4 %collective-permute-start.7 = (bf16[2,128,128]{2,1,0:T(8,128)(2,1)S(1)}, bf16[2,128,128]{2,1,0:T(8,128)(2,1)S(1)}, u32[]{:S(2)}, u32[]{:S(2)}) collective-permute-start(bf16[2,128,128]{2,1,0:T(8,128)(2,1)S(1)} %get-tuple-element.88), channel_id=1, source_target_pairs={{0,6},{1,7},{2,4},{3,5},{4,2},{5,3},{6,0},{7,1},{8,14},{9,15},{10,... | collective-permute-start | bytes 196616 | tf_op jit(solution)/shard_map/ppermute | solution.py:510
  11.6 6.1 %collective-permute-start.8 = (bf16[2,128,128]{2,1,0:T(8,128)(2,1)S(1)}, bf16[2,128,128]{2,1,0:T(8,128)(2,1)S(1)}, u32[]{:S(2)}, u32[]{:S(2)}) collective-permute-start(bf16[2,128,128]{2,1,0:T(8,128)(2,1)S(1)} %get-tuple-element.89), channel_id=1, source_target_pairs={{0,3},{1,2},{2,1},{3,0},{4,7},{5,6},{6,5},{7,4},{8,11},{9,10},{10,... | collective-permute-start | bytes 196616 | tf_op jit(solution)/shard_map/ppermute | solution.py:510
  11.6 7.2 %collective-permute-start.9 = (bf16[2,128,128]{2,1,0:T(8,128)(2,1)S(1)}, bf16[2,128,128]{2,1,0:T(8,128)(2,1)S(1)}, u32[]{:S(2)}, u32[]{:S(2)}) collective-permute-start(bf16[2,128,128]{2,1,0:T(8,128)(2,1)S(1)} %get-tuple-element.90), channel_id=1, source_target_pairs={{0,5},{1,4},{2,7},{3,6},{4,1},{5,0},{6,3},{7,2},{8,13},{9,12},{10,... | collective-permute-start | bytes 196616 | tf_op jit(solution)/shard_map/ppermute | solution.py:510
  12.7 6.1 %collective-permute-start.10 = (bf16[2,128,128]{2,1,0:T(8,128)(2,1)S(1)}, bf16[2,128,128]{2,1,0:T(8,128)(2,1)S(1)}, u32[]{:S(2)}, u32[]{:S(2)}) collective-permute-start(bf16[2,128,128]{2,1,0:T(8,128)(2,1)S(1)} %totals.1), channel_id=1, source_target_pairs={{0,9},{1,8},{2,11},{3,10},{4,13},{5,12},{6,15},{7,14},{9,0},{8,1},... | collective-permute-start | bytes 196616 | tf_op jit(solution)/shard_map/ppermute | solution.py:532
  15.5 5.8 %collective-permute-start.4 = (bf16[2,128,128]{2,1,0:T(8,128)(2,1)S(1)}, bf16[2,128,128]{2,1,0:T(8,128)(2,1)S(1)}, u32[]{:S(2)}, u32[]{:S(2)}) collective-permute-start(bf16[2,128,128]{2,1,0:T(8,128)(2,1)S(1)} %get-tuple-element.77), channel_id=1, source_target_pairs={{0,6},{1,7},{2,4},{3,5},{4,2},{5,3},{6,0},{7,1},{8,14},{9,15},{10,... | collective-permute-start | bytes 196616 | tf_op jit(solution)/shard_map/ppermute | solution.py:510
  17.1 5.3 %collective-permute-start.5 = (bf16[2,128,128]{2,1,0:T(8,128)(2,1)S(1)}, bf16[2,128,128]{2,1,0:T(8,128)(2,1)S(1)}, u32[]{:S(2)}, u32[]{:S(2)}) collective-permute-start(bf16[2,128,128]{2,1,0:T(8,128)(2,1)S(1)} %get-tuple-element.78), channel_id=1, source_target_pairs={{0,3},{1,2},{2,1},{3,0},{4,7},{5,6},{6,5},{7,4},{8,11},{9,10},{10,... | collective-permute-start | bytes 196616 | tf_op jit(solution)/shard_map/ppermute | solution.py:510
  17.7 4.7 %collective-permute-start.6 = (bf16[2,128,128]{2,1,0:T(8,128)(2,1)S(1)}, bf16[2,128,128]{2,1,0:T(8,128)(2,1)S(1)}, u32[]{:S(2)}, u32[]{:S(2)}) collective-permute-start(bf16[2,128,128]{2,1,0:T(8,128)(2,1)S(1)} %get-tuple-element.79), channel_id=1, source_target_pairs={{0,5},{1,4},{2,7},{3,6},{4,1},{5,0},{6,3},{7,2},{8,13},{9,12},{10,... | collective-permute-start | bytes 196616 | tf_op jit(solution)/shard_map/ppermute | solution.py:510
  19.0 5.5 %collective-permute-start.11 = (bf16[2,128,128]{2,1,0:T(8,128)(2,1)S(1)}, bf16[2,128,128]{2,1,0:T(8,128)(2,1)S(1)}, u32[]{:S(2)}, u32[]{:S(2)}) collective-permute-start(bf16[2,128,128]{2,1,0:T(8,128)(2,1)S(1)} %get-tuple-element.92), channel_id=1, source_target_pairs={{0,6},{1,7},{2,4},{3,5},{4,2},{5,3},{6,0},{7,1},{8,14},{9,15},{10,... | collective-permute-start | bytes 196616 | tf_op jit(solution)/shard_map/ppermute | solution.py:510
  20.8 4.6 %collective-permute-start.12 = (bf16[2,128,128]{2,1,0:T(8,128)(2,1)S(1)}, bf16[2,128,128]{2,1,0:T(8,128)(2,1)S(1)}, u32[]{:S(2)}, u32[]{:S(2)}) collective-permute-start(bf16[2,128,128]{2,1,0:T(8,128)(2,1)S(1)} %get-tuple-element.93), channel_id=1, source_target_pairs={{0,3},{1,2},{2,1},{3,0},{4,7},{5,6},{6,5},{7,4},{8,11},{9,10},{10,... | collective-permute-start | bytes 196616 | tf_op jit(solution)/shard_map/ppermute | solution.py:510
  21.3 4.3 %collective-permute-start.13 = (bf16[2,128,128]{2,1,0:T(8,128)(2,1)S(1)}, bf16[2,128,128]{2,1,0:T(8,128)(2,1)S(1)}, u32[]{:S(2)}, u32[]{:S(2)}) collective-permute-start(bf16[2,128,128]{2,1,0:T(8,128)(2,1)S(1)} %get-tuple-element.94), channel_id=1, source_target_pairs={{0,5},{1,4},{2,7},{3,6},{4,1},{5,0},{6,3},{7,2},{8,13},{9,12},{10,... | collective-permute-start | bytes 196616 | tf_op jit(solution)/shard_map/ppermute | solution.py:510
  22.5 3.4 %collective-permute-start.15 = (bf16[8,128,128]{2,1,0:T(8,128)(2,1)S(1)}, bf16[8,128,128]{2,1,0:T(8,128)(2,1)S(1)}, u32[]{:S(2)}, u32[]{:S(2)}) collective-permute-start(bf16[8,128,128]{2,1,0:T(8,128)(2,1)S(1)} %get-tuple-element.100), channel_id=1, source_target_pairs={{0,1},{1,0},{2,3},{3,2},{4,5},{5,4},{6,7},{7,6},{8,9},{9,8},{10,11... | collective-permute-start | bytes 786440 | tf_op jit(solution)/shard_map/ppermute | solution.py:546
  25.8 1.6 %collective-permute-start.14 = (bf16[8,128,128]{2,1,0:T(8,128)(2,1)S(1)}, bf16[8,128,128]{2,1,0:T(8,128)(2,1)S(1)}, u32[]{:S(2)}, u32[]{:S(2)}) collective-permute-start(bf16[8,128,128]{2,1,0:T(8,128)(2,1)S(1)} %get-tuple-element.95), channel_id=1, source_target_pairs={{0,1},{1,0},{2,3},{3,2},{4,5},{5,4},{6,7},{7,6},{8,9},{9,8},{10,11... | collective-permute-start | bytes 786440 | tf_op jit(solution)/shard_map/ppermute | solution.py:546

commit v28 on v27

--- a/solution.py
+++ b/solution.py
@@ -84,10 +84,11 @@
 
 def states_of(copies, k_ref, q_ref, v_ref, g_ref, kt_ref, qt_ref, out_ref, tail_rows, head_rows, inv_root):
     columns = [pl.ds(h * HD, HD) for h in range(out_ref.shape[1])]
-    for copy, ref, t_ref in zip(copies, (k_ref, q_ref), (kt_ref, qt_ref)):
-        copy.wait()
-        for h, cols in enumerate(columns):
-            t_ref[h] = ref[:, cols].T
+    copies[0].wait()
+    copies[1].wait()
+    for h, cols in enumerate(columns):
+        kt_ref[h] = k_ref[:, cols].T
+        qt_ref[h] = q_ref[:, cols].T
     copies[2].wait()
     copies[3].wait()
     for h, cols in enumerate(columns):

time: 28.7 us -> 29 us (1.010)
  starting transfers between devices: 17.3 us -> 17.7 us
    ppermute x2, starting transfers between devices: 0.42 us -> 1 us  [post(): return (own, lax.ppermute(theirs, 'seq', swap))]
  transfers between devices with their start and end apart: 16 -> 16, of which waited for: 5 -> 4; matrix products, arithmetic and copies ran while one was open for 0% -> 0% of each run, Pallas kernels for 19% -> 18%
where the time goes in v28:
time: 29 us; the launch traced here: 28.9 us
  starting transfers between devices  17.7 us (61%)
  Pallas kernels  8.28 us (29%)
  waiting for transfers between devices  2.15 us (7%)
  between operations  0.73 us (3%)
    ppermute x12, starting transfers between devices, trade(): lax.ppermute(parts[d], 'seq', [(i, i ^ STEPS[d]) for i in range(n)])  13.5 us
    pallas_call x11, Pallas kernels, call(): pl.pallas_call(kernel, in_specs=specs, out_specs=out_specs or [vmem] * le...  8.28 us
    ppermute x1, starting transfers between devices, per_device(): enter = lax.ppermute(edge(0), 'seq', up + down)  2.7 us
    ppermute x12, waiting for transfers between devices, trade(): lax.ppermute(parts[d], 'seq', [(i, i ^ STEPS[d]) for i in range(n)])  2.14 us
    ppermute x2, starting transfers between devices, post(): return (own, lax.ppermute(theirs, 'seq', swap))  1 us
  transfers between devices with their start and end apart: 16, of which 4 were waited for; matrix products, arithmetic and copies ran while one was open for 0% of the time, Pallas kernels for 18%

profile of v28, /device:TPU:0, one launch (start us, length us, event | category | flops | bytes accessed | tf_op | source)
XLA Modules:
  0.0 28.9 jit_solution(5910892340100665047)
XLA Ops:
  0.6 1.6 %send.1 = (s32[8]{0:T(128)S(1)}, bf16[2,8,128,128]{3,2,1,0:T(8,128)(2,1)S(1)}, bf16[128,1024]{1,0:T(8,128)(2,1)S(1)}, bf16[128,1024]{1,0:T(8,128)(2,1)S(1)}, bf1...) custom-call(s32[8]{0:T(128)} %len_hbm.1, ...), custom_call_target="tpu_custom_call" | custom-call | flops 67108864 | bytes 4325440 | tf_op jit(solution)/shard_map/send/pallas_call | solution.py:452
  2.2 0.5 %collective-permute-start = (bf16[2,8,128,128]{3,2,1,0:T(8,128)(2,1)S(1)}, bf16[2,8,128,128]{3,2,1,0:T(8,128)(2,1)S(1)}, u32[]{:S(2)}, u32[]{:S(2)}) collective-permute-start(bf16[2,8,128,128]{3,2,1,0:T(8,128)(2,1)S(1)} %get-tuple-element.71), channel_id=1, source_target_pairs={{0,1},{1,0},{2,3},{3,2},{4,5},{5,4},{6,7},{7,6},{8,9},{9,8},{10,11... | collective-permute-start | bytes 1572872 | tf_op jit(solution)/shard_map/ppermute | solution.py:487
  2.8 1.6 %keep.1 = (bf16[2,8,128,128]{3,2,1,0:T(8,128)(2,1)S(1)}, bf16[128,1024]{1,0:T(8,128)(2,1)S(1)}, bf16[128,1024]{1,0:T(8,128)(2,1)S(1)}, bf16[128,1024]{1,0:T(8,12...) custom-call(s32[8]{0:T(128)S(1)} %get-tuple-element.56.len_hbm, ...), custom_call_target="tpu_custom_call" | custom-call | flops 67108864 | bytes 4358176 | tf_op jit(solution)/shard_map/keep/pallas_call | solution.py:452
  4.3 0.0 collective-permute-done.got_ref
  4.4 0.1 pair.1
  4.5 3.9 %collective-permute-start.1 = (bf16[2,128,128]{2,1,0:T(8,128)(2,1)S(1)}, bf16[2,128,128]{2,1,0:T(8,128)(2,1)S(1)}, u32[]{:S(2)}, u32[]{:S(2)}) collective-permute-start(bf16[2,128,128]{2,1,0:T(8,128)(2,1)S(1)} %get-tuple-element.73), channel_id=1, source_target_pairs={{0,6},{1,7},{2,4},{3,5},{4,2},{5,3},{6,0},{7,1},{8,14},{9,15},{10,... | collective-permute-start | bytes 196616 | tf_op jit(solution)/shard_map/ppermute | solution.py:511
  8.4 0.1 collective-permute-start.2
  8.4 0.3 %collective-permute-start.3 = (bf16[2,128,128]{2,1,0:T(8,128)(2,1)S(1)}, bf16[2,128,128]{2,1,0:T(8,128)(2,1)S(1)}, u32[]{:S(2)}, u32[]{:S(2)}) collective-permute-start(bf16[2,128,128]{2,1,0:T(8,128)(2,1)S(1)} %get-tuple-element.75), channel_id=1, source_target_pairs={{0,5},{1,4},{2,7},{3,6},{4,1},{5,0},{6,3},{7,2},{8,13},{9,12},{10,... | collective-permute-start | bytes 196616 | tf_op jit(solution)/shard_map/ppermute | solution.py:511
  8.8 2.8 %collective-permute-start.7 = (bf16[2,128,128]{2,1,0:T(8,128)(2,1)S(1)}, bf16[2,128,128]{2,1,0:T(8,128)(2,1)S(1)}, u32[]{:S(2)}, u32[]{:S(2)}) collective-permute-start(bf16[2,128,128]{2,1,0:T(8,128)(2,1)S(1)} %get-tuple-element.88), channel_id=1, source_target_pairs={{0,6},{1,7},{2,4},{3,5},{4,2},{5,3},{6,0},{7,1},{8,14},{9,15},{10,... | collective-permute-start | bytes 196616 | tf_op jit(solution)/shard_map/ppermute | solution.py:511
  11.6 0.0 collective-permute-start.8
  11.6 0.4 %collective-permute-start.9 = (bf16[2,128,128]{2,1,0:T(8,128)(2,1)S(1)}, bf16[2,128,128]{2,1,0:T(8,128)(2,1)S(1)}, u32[]{:S(2)}, u32[]{:S(2)}) collective-permute-start(bf16[2,128,128]{2,1,0:T(8,128)(2,1)S(1)} %get-tuple-element.90), channel_id=1, source_target_pairs={{0,5},{1,4},{2,7},{3,6},{4,1},{5,0},{6,3},{7,2},{8,13},{9,12},{10,... | collective-permute-start | bytes 196616 | tf_op jit(solution)/shard_map/ppermute | solution.py:511
  12.0 0.7 %collective-permute-done.2.refs_2_.s2 = bf16[2,128,128]{2,1,0:T(8,128)(2,1)S(1)} collective-permute-done((bf16[2,128,128]{2,1,0:T(8,128)(2,1)S(1)}, bf16[2,128,128]{2,1,0:T(8,128)(2,1)S(1)}, u32[]{:S(2)}, u32[]{:S(2)}) %collective-permute-start.2) | collective-permute-done | bytes 65568 | tf_op jit(solution)/shard_map/ppermute | solution.py:511
  12.7 0.1 totals.1
  12.7 2.7 %collective-permute-start.10 = (bf16[2,128,128]{2,1,0:T(8,128)(2,1)S(1)}, bf16[2,128,128]{2,1,0:T(8,128)(2,1)S(1)}, u32[]{:S(2)}, u32[]{:S(2)}) collective-permute-start(bf16[2,128,128]{2,1,0:T(8,128)(2,1)S(1)} %totals.1), channel_id=1, source_target_pairs={{0,9},{1,8},{2,11},{3,10},{4,13},{5,12},{6,15},{7,14},{9,0},{8,1},... | collective-permute-start | bytes 196616 | tf_op jit(solution)/shard_map/ppermute | solution.py:533
  15.4 0.1 scan.2
  15.5 1.5 %collective-permute-start.4 = (bf16[2,128,128]{2,1,0:T(8,128)(2,1)S(1)}, bf16[2,128,128]{2,1,0:T(8,128)(2,1)S(1)}, u32[]{:S(2)}, u32[]{:S(2)}) collective-permute-start(bf16[2,128,128]{2,1,0:T(8,128)(2,1)S(1)} %get-tuple-element.77), channel_id=1, source_target_pairs={{0,6},{1,7},{2,4},{3,5},{4,2},{5,3},{6,0},{7,1},{8,14},{9,15},{10,... | collective-permute-start | bytes 196616 | tf_op jit(solution)/shard_map/ppermute | solution.py:511
  17.1 0.7 %collective-permute-start.5 = (bf16[2,128,128]{2,1,0:T(8,128)(2,1)S(1)}, bf16[2,128,128]{2,1,0:T(8,128)(2,1)S(1)}, u32[]{:S(2)}, u32[]{:S(2)}) collective-permute-start(bf16[2,128,128]{2,1,0:T(8,128)(2,1)S(1)} %get-tuple-element.78), channel_id=1, source_target_pairs={{0,3},{1,2},{2,1},{3,0},{4,7},{5,6},{6,5},{7,4},{8,11},{9,10},{10,... | collective-permute-start | bytes 196616 | tf_op jit(solution)/shard_map/ppermute | solution.py:511
  17.7 1.1 %collective-permute-start.6 = (bf16[2,128,128]{2,1,0:T(8,128)(2,1)S(1)}, bf16[2,128,128]{2,1,0:T(8,128)(2,1)S(1)}, u32[]{:S(2)}, u32[]{:S(2)}) collective-permute-start(bf16[2,128,128]{2,1,0:T(8,128)(2,1)S(1)} %get-tuple-element.79), channel_id=1, source_target_pairs={{0,5},{1,4},{2,7},{3,6},{4,1},{5,0},{6,3},{7,2},{8,13},{9,12},{10,... | collective-permute-start | bytes 196616 | tf_op jit(solution)/shard_map/ppermute | solution.py:511
  18.8 0.2 scan.3
  19.0 1.5 %collective-permute-start.11 = (bf16[2,128,128]{2,1,0:T(8,128)(2,1)S(1)}, bf16[2,128,128]{2,1,0:T(8,128)(2,1)S(1)}, u32[]{:S(2)}, u32[]{:S(2)}) collective-permute-start(bf16[2,128,128]{2,1,0:T(8,128)(2,1)S(1)} %get-tuple-element.92), channel_id=1, source_target_pairs={{0,6},{1,7},{2,4},{3,5},{4,2},{5,3},{6,0},{7,1},{8,14},{9,15},{10,... | collective-permute-start | bytes 196616 | tf_op jit(solution)/shard_map/ppermute | solution.py:511
  20.5 0.5 %collective-permute-start.12 = (bf16[2,128,128]{2,1,0:T(8,128)(2,1)S(1)}, bf16[2,128,128]{2,1,0:T(8,128)(2,1)S(1)}, u32[]{:S(2)}, u32[]{:S(2)}) collective-permute-start(bf16[2,128,128]{2,1,0:T(8,128)(2,1)S(1)} %get-tuple-element.93), channel_id=1, source_target_pairs={{0,3},{1,2},{2,1},{3,0},{4,7},{5,6},{6,5},{7,4},{8,11},{9,10},{10,... | collective-permute-start | bytes 196616 | tf_op jit(solution)/shard_map/ppermute | solution.py:511
  21.1 0.5 %collective-permute-done.4.refs_1_ = bf16[2,128,128]{2,1,0:T(8,128)(2,1)S(1)} collective-permute-done((bf16[2,128,128]{2,1,0:T(8,128)(2,1)S(1)}, bf16[2,128,128]{2,1,0:T(8,128)(2,1)S(1)}, u32[]{:S(2)}, u32[]{:S(2)}) %collective-permute-start.4) | collective-permute-done | bytes 65568 | tf_op jit(solution)/shard_map/ppermute | solution.py:511
  21.6 0.7 %collective-permute-start.13 = (bf16[2,128,128]{2,1,0:T(8,128)(2,1)S(1)}, bf16[2,128,128]{2,1,0:T(8,128)(2,1)S(1)}, u32[]{:S(2)}, u32[]{:S(2)}) collective-permute-start(bf16[2,128,128]{2,1,0:T(8,128)(2,1)S(1)} %get-tuple-element.94), channel_id=1, source_target_pairs={{0,5},{1,4},{2,7},{3,6},{4,1},{5,0},{6,3},{7,2},{8,13},{9,12},{10,... | collective-permute-start | bytes 196616 | tf_op jit(solution)/shard_map/ppermute | solution.py:511
  22.3 0.1 post.2
  22.4 0.7 %collective-permute-start.15 = (bf16[8,128,128]{2,1,0:T(8,128)(2,1)S(1)}, bf16[8,128,128]{2,1,0:T(8,128)(2,1)S(1)}, u32[]{:S(2)}, u32[]{:S(2)}) collective-permute-start(bf16[8,128,128]{2,1,0:T(8,128)(2,1)S(1)} %get-tuple-element.100), channel_id=1, source_target_pairs={{0,1},{1,0},{2,3},{3,2},{4,5},{5,4},{6,7},{7,6},{8,9},{9,8},{10,11... | collective-permute-start | bytes 786440 | tf_op jit(solution)/shard_map/ppermute | solution.py:547
  23.2 1.8 %local.1 = (bf16[16,128,128]{2,1,0:T(8,128)(2,1)S(1)}, bf16[16,128,128]{2,1,0:T(8,128)(2,1)S(1)}, bf16[16,128,128]{2,1,0:T(8,128)(2,1)S(1)}, bf16[16,128,128]{2,...) custom-call(s32[8]{0:T(128)S(1)} %get-tuple-element.56.len_hbm, ...), custom_call_target="tpu_custom_call" | custom-call | flops 134217728 | bytes 6160416 | tf_op jit(solution)/shard_map/local/pallas_call | solution.py:452
  25.0 0.6 %collective-permute-done.12.refs_2_ = bf16[2,128,128]{2,1,0:T(8,128)(2,1)S(1)} collective-permute-done((bf16[2,128,128]{2,1,0:T(8,128)(2,1)S(1)}, bf16[2,128,128]{2,1,0:T(8,128)(2,1)S(1)}, u32[]{:S(2)}, u32[]{:S(2)}) %collective-permute-start.12) | collective-permute-done | bytes 65568 | tf_op jit(solution)/shard_map/ppermute | solution.py:511
  25.6 0.3 %collective-permute-done.13.refs_3_ = bf16[2,128,128]{2,1,0:T(8,128)(2,1)S(1)} collective-permute-done((bf16[2,128,128]{2,1,0:T(8,128)(2,1)S(1)}, bf16[2,128,128]{2,1,0:T(8,128)(2,1)S(1)}, u32[]{:S(2)}, u32[]{:S(2)}) %collective-permute-start.13) | collective-permute-done | bytes 65568 | tf_op jit(solution)/shard_map/ppermute | solution.py:511
  25.9 0.1 post.3
  26.0 0.3 collective-permute-start.14
  26.3 1.3 %middle.1 = (bf16[128,2048]{1,0:T(8,128)(2,1)}, bf16[128,2048]{1,0:T(8,128)(2,1)}, bf16[128,2048]{1,0:T(8,128)(2,1)}, bf16[128,2048]{1,0:T(8,128)(2,1)}, bf16[12...) custom-call(bf16[128,1024]{1,0:T(8,128)(2,1)S(1)} %get-tuple-element.98.refs_0_, ...), custom_call_target="tpu_custom_call" | custom-call | flops 268435456 | bytes 9043968 | tf_op jit(solution)/shard_map/middle/pallas_call | solution.py:452
  27.7 1.2 %last.1 = (bf16[128,2048]{1,0:T(8,128)(2,1)}, bf16[128,2048]{1,0:T(8,128)(2,1)}, bf16[128,2048]{1,0:T(8,128)(2,1)}, bf16[128,2048]{1,0:T(8,128)(2,1)}) custom-call(bf16[128,1024]{1,0:T(8,128)(2,1)S(1)} %get-tuple-element.59.refs_0_.refs_2_, ...), custom_call_target="tpu_custom_call", output_to_operand_aliasing={{0}: (18, {}), {1}: (19, {}), {2}: (20, {}), {3}: (21, {})} | custom-call | flops 134217728 | bytes 9830400 | tf_op jit(solution)/shard_map/last/pallas_call | solution.py:452
  (11 shorter events, 0.0 us)
Async XLA Ops:
  2.2 2.1 %collective-permute-start = (bf16[2,8,128,128]{3,2,1,0:T(8,128)(2,1)S(1)}, bf16[2,8,128,128]{3,2,1,0:T(8,128)(2,1)S(1)}, u32[]{:S(2)}, u32[]{:S(2)}) collective-permute-start(bf16[2,8,128,128]{3,2,1,0:T(8,128)(2,1)S(1)} %get-tuple-element.71), channel_id=1, source_target_pairs={{0,1},{1,0},{2,3},{3,2},{4,5},{5,4},{6,7},{7,6},{8,9},{9,8},{10,11... | collective-permute-start | bytes 1572872 | tf_op jit(solution)/shard_map/ppermute | solution.py:487
  4.5 7.1 %collective-permute-start.1 = (bf16[2,128,128]{2,1,0:T(8,128)(2,1)S(1)}, bf16[2,128,128]{2,1,0:T(8,128)(2,1)S(1)}, u32[]{:S(2)}, u32[]{:S(2)}) collective-permute-start(bf16[2,128,128]{2,1,0:T(8,128)(2,1)S(1)} %get-tuple-element.73), channel_id=1, source_target_pairs={{0,6},{1,7},{2,4},{3,5},{4,2},{5,3},{6,0},{7,1},{8,14},{9,15},{10,... | collective-permute-start | bytes 196616 | tf_op jit(solution)/shard_map/ppermute | solution.py:511
  8.4 4.3 %collective-permute-start.2 = (bf16[2,128,128]{2,1,0:T(8,128)(2,1)S(1)}, bf16[2,128,128]{2,1,0:T(8,128)(2,1)S(1)}, u32[]{:S(2)}, u32[]{:S(2)}) collective-permute-start(bf16[2,128,128]{2,1,0:T(8,128)(2,1)S(1)} %get-tuple-element.74), channel_id=1, source_target_pairs={{0,3},{1,2},{2,1},{3,0},{4,7},{5,6},{6,5},{7,4},{8,11},{9,10},{10,... | collective-permute-start | bytes 196616 | tf_op jit(solution)/shard_map/ppermute | solution.py:511
  8.4 4.2 %collective-permute-start.3 = (bf16[2,128,128]{2,1,0:T(8,128)(2,1)S(1)}, bf16[2,128,128]{2,1,0:T(8,128)(2,1)S(1)}, u32[]{:S(2)}, u32[]{:S(2)}) collective-permute-start(bf16[2,128,128]{2,1,0:T(8,128)(2,1)S(1)} %get-tuple-element.75), channel_id=1, source_target_pairs={{0,5},{1,4},{2,7},{3,6},{4,1},{5,0},{6,3},{7,2},{8,13},{9,12},{10,... | collective-permute-start | bytes 196616 | tf_op jit(solution)/shard_map/ppermute | solution.py:511
  8.8 8.3 %collective-permute-start.7 = (bf16[2,128,128]{2,1,0:T(8,128)(2,1)S(1)}, bf16[2,128,128]{2,1,0:T(8,128)(2,1)S(1)}, u32[]{:S(2)}, u32[]{:S(2)}) collective-permute-start(bf16[2,128,128]{2,1,0:T(8,128)(2,1)S(1)} %get-tuple-element.88), channel_id=1, source_target_pairs={{0,6},{1,7},{2,4},{3,5},{4,2},{5,3},{6,0},{7,1},{8,14},{9,15},{10,... | collective-permute-start | bytes 196616 | tf_op jit(solution)/shard_map/ppermute | solution.py:511
  11.6 6.1 %collective-permute-start.8 = (bf16[2,128,128]{2,1,0:T(8,128)(2,1)S(1)}, bf16[2,128,128]{2,1,0:T(8,128)(2,1)S(1)}, u32[]{:S(2)}, u32[]{:S(2)}) collective-permute-start(bf16[2,128,128]{2,1,0:T(8,128)(2,1)S(1)} %get-tuple-element.89), channel_id=1, source_target_pairs={{0,3},{1,2},{2,1},{3,0},{4,7},{5,6},{6,5},{7,4},{8,11},{9,10},{10,... | collective-permute-start | bytes 196616 | tf_op jit(solution)/shard_map/ppermute | solution.py:511
  11.6 7.2 %collective-permute-start.9 = (bf16[2,128,128]{2,1,0:T(8,128)(2,1)S(1)}, bf16[2,128,128]{2,1,0:T(8,128)(2,1)S(1)}, u32[]{:S(2)}, u32[]{:S(2)}) collective-permute-start(bf16[2,128,128]{2,1,0:T(8,128)(2,1)S(1)} %get-tuple-element.90), channel_id=1, source_target_pairs={{0,5},{1,4},{2,7},{3,6},{4,1},{5,0},{6,3},{7,2},{8,13},{9,12},{10,... | collective-permute-start | bytes 196616 | tf_op jit(solution)/shard_map/ppermute | solution.py:511
  12.7 6.1 %collective-permute-start.10 = (bf16[2,128,128]{2,1,0:T(8,128)(2,1)S(1)}, bf16[2,128,128]{2,1,0:T(8,128)(2,1)S(1)}, u32[]{:S(2)}, u32[]{:S(2)}) collective-permute-start(bf16[2,128,128]{2,1,0:T(8,128)(2,1)S(1)} %totals.1), channel_id=1, source_target_pairs={{0,9},{1,8},{2,11},{3,10},{4,13},{5,12},{6,15},{7,14},{9,0},{8,1},... | collective-permute-start | bytes 196616 | tf_op jit(solution)/shard_map/ppermute | solution.py:533
  15.5 6.0 %collective-permute-start.4 = (bf16[2,128,128]{2,1,0:T(8,128)(2,1)S(1)}, bf16[2,128,128]{2,1,0:T(8,128)(2,1)S(1)}, u32[]{:S(2)}, u32[]{:S(2)}) collective-permute-start(bf16[2,128,128]{2,1,0:T(8,128)(2,1)S(1)} %get-tuple-element.77), channel_id=1, source_target_pairs={{0,6},{1,7},{2,4},{3,5},{4,2},{5,3},{6,0},{7,1},{8,14},{9,15},{10,... | collective-permute-start | bytes 196616 | tf_op jit(solution)/shard_map/ppermute | solution.py:511
  17.1 5.2 %collective-permute-start.5 = (bf16[2,128,128]{2,1,0:T(8,128)(2,1)S(1)}, bf16[2,128,128]{2,1,0:T(8,128)(2,1)S(1)}, u32[]{:S(2)}, u32[]{:S(2)}) collective-permute-start(bf16[2,128,128]{2,1,0:T(8,128)(2,1)S(1)} %get-tuple-element.78), channel_id=1, source_target_pairs={{0,3},{1,2},{2,1},{3,0},{4,7},{5,6},{6,5},{7,4},{8,11},{9,10},{10,... | collective-permute-start | bytes 196616 | tf_op jit(solution)/shard_map/ppermute | solution.py:511
  17.7 4.5 %collective-permute-start.6 = (bf16[2,128,128]{2,1,0:T(8,128)(2,1)S(1)}, bf16[2,128,128]{2,1,0:T(8,128)(2,1)S(1)}, u32[]{:S(2)}, u32[]{:S(2)}) collective-permute-start(bf16[2,128,128]{2,1,0:T(8,128)(2,1)S(1)} %get-tuple-element.79), channel_id=1, source_target_pairs={{0,5},{1,4},{2,7},{3,6},{4,1},{5,0},{6,3},{7,2},{8,13},{9,12},{10,... | collective-permute-start | bytes 196616 | tf_op jit(solution)/shard_map/ppermute | solution.py:511
  19.0 6.0 %collective-permute-start.11 = (bf16[2,128,128]{2,1,0:T(8,128)(2,1)S(1)}, bf16[2,128,128]{2,1,0:T(8,128)(2,1)S(1)}, u32[]{:S(2)}, u32[]{:S(2)}) collective-permute-start(bf16[2,128,128]{2,1,0:T(8,128)(2,1)S(1)} %get-tuple-element.92), channel_id=1, source_target_pairs={{0,6},{1,7},{2,4},{3,5},{4,2},{5,3},{6,0},{7,1},{8,14},{9,15},{10,... | collective-permute-start | bytes 196616 | tf_op jit(solution)/shard_map/ppermute | solution.py:511
  20.5 5.1 %collective-permute-start.12 = (bf16[2,128,128]{2,1,0:T(8,128)(2,1)S(1)}, bf16[2,128,128]{2,1,0:T(8,128)(2,1)S(1)}, u32[]{:S(2)}, u32[]{:S(2)}) collective-permute-start(bf16[2,128,128]{2,1,0:T(8,128)(2,1)S(1)} %get-tuple-element.93), channel_id=1, source_target_pairs={{0,3},{1,2},{2,1},{3,0},{4,7},{5,6},{6,5},{7,4},{8,11},{9,10},{10,... | collective-permute-start | bytes 196616 | tf_op jit(solution)/shard_map/ppermute | solution.py:511
  21.6 4.3 %collective-permute-start.13 = (bf16[2,128,128]{2,1,0:T(8,128)(2,1)S(1)}, bf16[2,128,128]{2,1,0:T(8,128)(2,1)S(1)}, u32[]{:S(2)}, u32[]{:S(2)}) collective-permute-start(bf16[2,128,128]{2,1,0:T(8,128)(2,1)S(1)} %get-tuple-element.94), channel_id=1, source_target_pairs={{0,5},{1,4},{2,7},{3,6},{4,1},{5,0},{6,3},{7,2},{8,13},{9,12},{10,... | collective-permute-start | bytes 196616 | tf_op jit(solution)/shard_map/ppermute | solution.py:511
  22.4 3.9 %collective-permute-start.15 = (bf16[8,128,128]{2,1,0:T(8,128)(2,1)S(1)}, bf16[8,128,128]{2,1,0:T(8,128)(2,1)S(1)}, u32[]{:S(2)}, u32[]{:S(2)}) collective-permute-start(bf16[8,128,128]{2,1,0:T(8,128)(2,1)S(1)} %get-tuple-element.100), channel_id=1, source_target_pairs={{0,1},{1,0},{2,3},{3,2},{4,5},{5,4},{6,7},{7,6},{8,9},{9,8},{10,11... | collective-permute-start | bytes 786440 | tf_op jit(solution)/shard_map/ppermute | solution.py:547
  26.0 1.6 %collective-permute-start.14 = (bf16[8,128,128]{2,1,0:T(8,128)(2,1)S(1)}, bf16[8,128,128]{2,1,0:T(8,128)(2,1)S(1)}, u32[]{:S(2)}, u32[]{:S(2)}) collective-permute-start(bf16[8,128,128]{2,1,0:T(8,128)(2,1)S(1)} %get-tuple-element.95), channel_id=1, source_target_pairs={{0,1},{1,0},{2,3},{3,2},{4,5},{5,4},{6,7},{7,6},{8,9},{9,8},{10,11... | collective-permute-start | bytes 786440 | tf_op jit(solution)/shard_map/ppermute | solution.py:547
